TPU v7x, 32 devices: a whole 2x2x4 slice. The times are simulated.
32 devices in a mesh: row: 4 (over x, core), col: 8 (over z, y).
Axes of the slice: x: 2, y: 2, z: 4, core: 2. Of those that a mesh axis runs over, the one named last changes fastest.
Arguments:
- features: bfloat16 [32, 256, 256], P('row', 'col'), may hold values from -16 to 16
- expand_weight: bfloat16 [2, 256, 1024], replicated, may hold values from -0.375 to 0.375
- expand_bias: float32 [2, 1024], replicated, may hold values from -3 to 3
- depth_weight: float32 [2, 3, 3, 1024], replicated, may hold values from -2 to 2
- depth_bias: float32 [2, 1024], replicated, may hold values from -3 to 3
- project_weight: bfloat16 [2, 1024, 256], replicated, may hold values from -0.1875 to 0.1875
- project_bias: float32 [2, 256], replicated, may hold values from -3 to 3
- qkv_weight: bfloat16 [2, 256, 768], replicated, may hold values from -0.375 to 0.375
- aggregate_depth: float32 [2, 5, 5, 768], replicated, may hold values from -1.25 to 1.25
- aggregate_group: bfloat16 [2, 24, 32, 32], replicated, may hold values from -1 to 1
- output_weight: bfloat16 [2, 512, 256], replicated, may hold values from -0.25 to 0.25
- output_bias: float32 [2, 256], replicated, may hold values from -3 to 3
- head_weight: bfloat16 [3, 3, 4, 256], replicated, may hold values from -0.125 to 0.125
- head_bias: float32 [4], replicated, may hold values from -3 to 3
Outputs:
- final_map: bfloat16 [32, 256, 256], P('row', 'col')
- boxes: float32 [4, 32, 256], P(None, 'row', 'col')
All inputs are finite; a program needn't handle non-finite values.
Results may differ from a plain program's by a relative error of at most 0.009.
Values may be sent and summed in bfloat16 or wider, within the bound.
No kernel may reach another device: no remote copies, remote signals or barrier semaphores. Data moves between devices by JAX's collectives and lax.ppermute only.
A program may use at most 64 MiB of HBM per device.

v0:
```python
import jax
import jax.numpy as jnp
from jax import lax
from jax.sharding import PartitionSpec as P

SECTIONS = 2


def with_halo(cells, sides, width):
    for axis, dim in sides:
        count = lax.axis_size(axis)
        ends = count - 1
        head = lax.slice_in_dim(cells, 0, width, axis=dim)
        tail = lax.slice_in_dim(cells, cells.shape[dim] - width, cells.shape[dim], axis=dim)
        cells = jnp.concatenate(
            [
                lax.ppermute(tail, axis, [(i, (i + 1) % count) for i in range(ends)]),
                cells,
                lax.ppermute(head, axis, [((i + 1) % count, i) for i in range(ends)]),
            ],
            axis=dim,
        )
    return cells


def hard_swish(value):
    return value * jnp.minimum(jnp.maximum(value + 3.0, 0.0), 6.0) / 6.0


def depthwise(padded, weight, rows, cols):
    ksize = weight.shape[0]
    total = jnp.zeros((rows, cols, padded.shape[2]), jnp.float32)
    for offset_r in range(ksize):
        for offset_c in range(ksize):
            total = (
                total
                + padded[offset_r : offset_r + rows, offset_c : offset_c + cols, :].astype(
                    jnp.float32
                )
                * weight[offset_r, offset_c]
            )
    return total


def dense(values, weight):
    return lax.dot_general(
        values, weight, (((values.ndim - 1,), (0,)), ((), ())), preferred_element_type=jnp.float32
    )


def heads_of(padded_qkv, agg_depth, agg_group, rows, cols, heads, head_dim):
    center = padded_qkv[2 : 2 + rows, 2 : 2 + cols, :]
    spread = depthwise(padded_qkv, agg_depth, rows, cols).astype(jnp.bfloat16)
    grouped = jnp.einsum(
        "rcgd,gde->rcge",
        spread.reshape(rows, cols, 3 * heads, head_dim),
        agg_group,
        preferred_element_type=jnp.float32,
    ).astype(jnp.bfloat16)
    return jnp.concatenate(
        [
            center.reshape(rows, cols, heads, 3, head_dim),
            grouped.reshape(rows, cols, heads, 3, head_dim),
        ],
        axis=2,
    )


def local(
    features,
    expand_weight,
    expand_bias,
    depth_weight,
    depth_bias,
    project_weight,
    project_bias,
    qkv_weight,
    aggregate_depth,
    aggregate_group,
    output_weight,
    output_bias,
    head_weight,
    head_bias,
):
    rows, cols, width = features.shape
    head_dim = aggregate_group.shape[2]
    heads = width // head_dim
    current = features
    for section in range(SECTIONS):
        hidden = hard_swish(dense(current, expand_weight[section]) + expand_bias[section]).astype(
            jnp.bfloat16
        )
        hidden = with_halo(hidden, (("row", 0), ("col", 1)), 1)
        spread = hard_swish(
            depthwise(hidden, depth_weight[section], rows, cols) + depth_bias[section]
        ).astype(jnp.bfloat16)
        mixed = (current + dense(spread, project_weight[section]) + project_bias[section]).astype(
            jnp.bfloat16
        )
        local_qkv = dense(mixed, qkv_weight[section]).astype(jnp.bfloat16)
        padded_qkv = with_halo(local_qkv, (("row", 0), ("col", 1)), 2)
        both = heads_of(
            padded_qkv,
            aggregate_depth[section],
            aggregate_group[section],
            rows,
            cols,
            heads,
            head_dim,
        )
        queries = jax.nn.relu(both[:, :, :, 0, :]).astype(jnp.float32)
        keys = jax.nn.relu(both[:, :, :, 1, :]).astype(jnp.float32)
        values = both[:, :, :, 2, :].astype(jnp.float32)
        kv_local = jnp.einsum("rchd,rche->hde", keys, values, precision=lax.Precision.HIGHEST)
        key_local = jnp.sum(keys, axis=(0, 1))
        kv_all, key_all = lax.psum((kv_local, key_local), ("row", "col"))
        numer = jnp.einsum("rchd,hde->rche", queries, kv_all, precision=lax.Precision.HIGHEST)
        denom = jnp.einsum("rchd,hd->rch", queries, key_all, precision=lax.Precision.HIGHEST)
        attended = (
            (numer / (denom[..., None] + 1e-06)).astype(jnp.bfloat16).reshape(rows, cols, 2 * width)
        )
        current = (mixed + dense(attended, output_weight[section]) + output_bias[section]).astype(
            jnp.bfloat16
        )
    padded = with_halo(current, (("row", 0), ("col", 1)), 1)
    boxes = jnp.zeros((4, rows, cols), jnp.float32)
    for offset_r in range(3):
        for offset_c in range(3):
            window = padded[offset_r : offset_r + rows, offset_c : offset_c + cols, :]
            boxes = boxes + lax.dot_general(
                head_weight[offset_r, offset_c],
                window,
                (((1,), (2,)), ((), ())),
                preferred_element_type=jnp.float32,
            )
    boxes = boxes + head_bias[:, None, None]
    return (current, boxes)


def solution(mesh):
    return jax.shard_map(
        local,
        mesh=mesh,
        in_specs=(
            P("row", "col", None),
            P(),
            P(),
            P(),
            P(),
            P(),
            P(),
            P(),
            P(),
            P(),
            P(),
            P(),
            P(),
            P(),
        ),
        out_specs=(P("row", "col", None), P(None, "row", "col")),
        check_vma=False,
    )
```

profile of v0, /device:TPU:0, one launch (start us, length us, event | category | flops | bytes accessed | tf_op | source)
XLA Modules:
  0.0 489.6 jit_solution(8197895957033972068)
XLA Ops:
  17.8 3.4 collective-permute-start.2
  23.3 3.8 collective-permute-done.3
  30.1 3.4 collective-permute-start.4
  38.9 4.3 collective-permute-start.6
  46.5 2.5 collective-permute-done.7
  49.5 3.0 add_convert_fusion.1
  58.8 42.3 %psum.29 = f32[16,32]{1,0:T(8,128)S(1)} all-reduce(f32[16,32]{1,0:T(8,128)S(1)} %convert_reduce_fusion.1), channel_id=1, replica_groups=mesh['row'=4,'col'=8] {'row','col'}, use_global_device_ids=true, to_apply=%region_2.3 | all-reduce | flops 512 | bytes 4096 | tf_op jit(solution)/shard_map/psum | solution.py:116
  101.1 5.4 %fusion.26 = f32[16,1,8,32]{3,1,2,0:T(1,128)S(1)} fusion(f32[16,32,1,1]{1,2,3,0:T(1,128)S(1)} %bitcast.210, bf16[8,32,16,3,32]{4,1,0,2,3:T(8,128)(2,1)} %copy-done.1), kind=kOutput, calls=%fused_computation.60 | convolution fusion | flops 2097152 | bytes 1067008 | tf_op jit(solution)/shard_map/rchd,hd->rch/dot_general | solution.py:118
  106.6 124.8 %all-reduce.3.cloned.1.call-done = f32[16,32,32]{1,2,0:T(8,128)} async-done(((f32[16,32,32]{1,2,0:T(8,128)}), f32[16,32,32]{1,2,0:T(8,128)}) %all-reduce.3.cloned.1.call-update) | async-done | bytes 65552 | tf_op jit(solution)/shard_map/psum | solution.py:116
  231.4 6.1 %fusion.1 = bf16[8,32,16,32]{1,3,0,2:T(8,128)(2,1)S(1)} fusion(f32[8,32,16]{1,0,2:T(8,128)S(1)} %add_bitcast_fusion.1, bf16[8,32,16,3,32]{4,1,0,2,3:T(8,128)(2,1)} %copy-done.1, f32[16,32,32]{1,2,0:T(8,128)} %all-reduce.3.cloned.1.call-done), kind=kOutput, calls=%fused_computation.3 | convolution fusion | flops 51118080 | bytes 1589248 | tf_op jit(solution)/shard_map/rchd,hde->rche/dot_general | solution.py:117
  243.9 3.5 collective-permute-done.9
  247.4 3.4 collective-permute-start.10
  252.4 4.2 collective-permute-done.11
  258.9 3.4 collective-permute-start.12
  266.5 4.2 collective-permute-start.14
  274.2 2.4 collective-permute-done.15
  276.9 3.0 add_convert_fusion
  286.2 40.8 %psum.31 = f32[16,32]{1,0:T(8,128)S(1)} all-reduce(f32[16,32]{1,0:T(8,128)S(1)} %convert_reduce_fusion), channel_id=1, replica_groups=mesh['row'=4,'col'=8] {'row','col'}, use_global_device_ids=true, to_apply=%region_5.6 | all-reduce | flops 512 | bytes 4096 | tf_op jit(solution)/shard_map/psum | solution.py:116
  326.9 5.4 %fusion.29 = f32[16,1,8,32]{3,1,2,0:T(1,128)S(1)} fusion(f32[16,32,1,1]{1,2,3,0:T(1,128)S(1)} %bitcast.211, bf16[8,32,16,3,32]{4,1,0,2,3:T(8,128)(2,1)} %copy-done.3), kind=kOutput, calls=%fused_computation.61 | convolution fusion | flops 2097152 | bytes 1067008 | tf_op jit(solution)/shard_map/rchd,hd->rch/dot_general | solution.py:118
  332.4 125.0 %all-reduce.5.cloned.1.call-done = f32[16,32,32]{1,2,0:T(8,128)} async-done(((f32[16,32,32]{1,2,0:T(8,128)}), f32[16,32,32]{1,2,0:T(8,128)}) %all-reduce.5.cloned.1.call-update) | async-done | bytes 65552 | tf_op jit(solution)/shard_map/psum | solution.py:116
  457.4 6.1 %fusion = bf16[8,32,16,32]{1,3,0,2:T(8,128)(2,1)S(1)} fusion(f32[8,32,16]{1,0,2:T(8,128)S(1)} %add_bitcast_fusion, bf16[8,32,16,3,32]{4,1,0,2,3:T(8,128)(2,1)} %copy-done.3, f32[16,32,32]{1,2,0:T(8,128)} %all-reduce.5.cloned.1.call-done), kind=kOutput, calls=%fused_computation.1 | convolution fusion | flops 51118080 | bytes 1589248 | tf_op jit(solution)/shard_map/rchd,hde->rche/dot_general | solution.py:117
  468.6 3.3 collective-permute-done.17
  471.9 3.4 collective-permute-start.18
  477.0 3.9 collective-permute-done.19
  (191 shorter events, 63.3 us)
Async XLA Ops:
  7.2 224.2 %all-reduce.3.cloned.1.call-start = ((), (), s32[]{:S(2)}) async-start(), calls=%async_computation | async-start | bytes 524288 | tf_op jit(solution)/shard_map/psum | solution.py:116
  10.1 6.4 %collective-permute-start = (bf16[1,32,1024]{2,1,0:T(8,128)(2,1)S(1)}, bf16[1,32,1024]{2,1,0:T(8,128)(2,1)S(1)}, u32[]{:S(2)}, u32[]{:S(2)}) collective-permute-start(bf16[1,32,1024]{2,1,0:T(8,128)(2,1)S(1)} %get-tuple-element.74), channel_id=1, source_target_pairs={{0,8},{8,16},{16,24},{1,9},{9,17},{17,25},{2,10},{10,18},{18,26},{... | collective-permute-start | bytes 196616 | tf_op jit(solution)/shard_map/ppermute | solution.py:17
  12.5 5.3 %collective-permute-start.1 = (bf16[1,32,1024]{2,1,0:T(8,128)(2,1)S(1)}, bf16[1,32,1024]{2,1,0:T(8,128)(2,1)S(1)}, u32[]{:S(2)}, u32[]{:S(2)}) collective-permute-start(bf16[1,32,1024]{2,1,0:T(8,128)(2,1)S(1)} %get-tuple-element.75), channel_id=1, source_target_pairs={{8,0},{16,8},{24,16},{9,1},{17,9},{25,17},{10,2},{18,10},{26,18},{... | collective-permute-start | bytes 196616 | tf_op jit(solution)/shard_map/ppermute | solution.py:19
  17.8 5.5 %collective-permute-start.2 = (bf16[10,1,1024]{2,1,0:T(2,128)(2,1)S(1)}, bf16[10,1,1024]{2,1,0:T(2,128)(2,1)S(1)}, u32[]{:S(2)}, u32[]{:S(2)}) collective-permute-start(bf16[10,1,1024]{2,1,0:T(2,128)(2,1)S(1)} %get-tuple-element.62), channel_id=1, source_target_pairs={{0,1},{1,2},{2,3},{3,4},{4,5},{5,6},{6,7},{8,9},{9,10},{10,11},{11... | collective-permute-start | bytes 61448 | tf_op jit(solution)/shard_map/ppermute | solution.py:17
  21.3 5.9 %collective-permute-start.3 = (bf16[10,1,1024]{2,1,0:T(2,128)(2,1)S(1)}, bf16[10,1,1024]{2,1,0:T(2,128)(2,1)S(1)}, u32[]{:S(2)}, u32[]{:S(2)}) collective-permute-start(bf16[10,1,1024]{2,1,0:T(2,128)(2,1)S(1)} %get-tuple-element.63), channel_id=1, source_target_pairs={{1,0},{2,1},{3,2},{4,3},{5,4},{6,5},{7,6},{9,8},{10,9},{11,10},{12... | collective-permute-start | bytes 61448 | tf_op jit(solution)/shard_map/ppermute | solution.py:19
  30.1 6.9 %collective-permute-start.4 = (bf16[2,32,768]{2,1,0:T(8,128)(2,1)}, bf16[2,32,768]{2,1,0:T(8,128)(2,1)S(1)}, u32[]{:S(2)}, u32[]{:S(2)}) collective-permute-start(bf16[2,32,768]{2,1,0:T(8,128)(2,1)} %get-tuple-element.78), channel_id=1, source_target_pairs={{0,8},{8,16},{16,24},{1,9},{9,17},{17,25},{2,10},{10,18},{18,26},{... | collective-permute-start | bytes 294920 | tf_op jit(solution)/shard_map/ppermute | solution.py:17
  33.5 5.3 %collective-permute-start.5 = (bf16[2,32,768]{2,1,0:T(8,128)(2,1)}, bf16[2,32,768]{2,1,0:T(8,128)(2,1)S(1)}, u32[]{:S(2)}, u32[]{:S(2)}) collective-permute-start(bf16[2,32,768]{2,1,0:T(8,128)(2,1)} %get-tuple-element.79), channel_id=1, source_target_pairs={{8,0},{16,8},{24,16},{9,1},{17,9},{25,17},{10,2},{18,10},{26,18},{... | collective-permute-start | bytes 294920 | tf_op jit(solution)/shard_map/ppermute | solution.py:19
  38.9 7.7 %collective-permute-start.6 = (bf16[12,2,768]{2,1,0:T(2,128)(2,1)S(1)}, bf16[12,2,768]{2,1,0:T(2,128)(2,1)S(1)}, u32[]{:S(2)}, u32[]{:S(2)}) collective-permute-start(bf16[12,2,768]{2,1,0:T(2,128)(2,1)S(1)} %get-tuple-element.70), channel_id=1, source_target_pairs={{0,1},{1,2},{2,3},{3,4},{4,5},{5,6},{6,7},{8,9},{9,10},{10,11},{11... | collective-permute-start | bytes 110600 | tf_op jit(solution)/shard_map/ppermute | solution.py:17
  43.2 5.9 %collective-permute-start.7 = (bf16[12,2,768]{2,1,0:T(2,128)(2,1)S(1)}, bf16[12,2,768]{2,1,0:T(2,128)(2,1)S(1)}, u32[]{:S(2)}, u32[]{:S(2)}) collective-permute-start(bf16[12,2,768]{2,1,0:T(2,128)(2,1)S(1)} %get-tuple-element.71), channel_id=1, source_target_pairs={{1,0},{2,1},{3,2},{4,3},{5,4},{6,5},{7,6},{9,8},{10,9},{11,10},{12... | collective-permute-start | bytes 110600 | tf_op jit(solution)/shard_map/ppermute | solution.py:19
  106.5 350.8 %all-reduce.5.cloned.1.call-start = ((), (), s32[]{:S(2)}) async-start(), calls=%async_computation.1 | async-start | bytes 524288 | tf_op jit(solution)/shard_map/psum | solution.py:116
  241.2 2.7 collective-permute-start.8
  242.5 4.8 collective-permute-start.9
  247.4 5.0 %collective-permute-start.10 = (bf16[10,1,1024]{2,1,0:T(2,128)(2,1)S(1)}, bf16[10,1,1024]{2,1,0:T(2,128)(2,1)S(1)}, u32[]{:S(2)}, u32[]{:S(2)}) collective-permute-start(bf16[10,1,1024]{2,1,0:T(2,128)(2,1)S(1)} %get-tuple-element.58), channel_id=1, source_target_pairs={{0,1},{1,2},{2,3},{3,4},{4,5},{5,6},{6,7},{8,9},{9,10},{10,11},{11... | collective-permute-start | bytes 61448 | tf_op jit(solution)/shard_map/ppermute | solution.py:17
  250.8 5.9 %collective-permute-start.11 = (bf16[10,1,1024]{2,1,0:T(2,128)(2,1)S(1)}, bf16[10,1,1024]{2,1,0:T(2,128)(2,1)S(1)}, u32[]{:S(2)}, u32[]{:S(2)}) collective-permute-start(bf16[10,1,1024]{2,1,0:T(2,128)(2,1)S(1)} %get-tuple-element.59), channel_id=1, source_target_pairs={{1,0},{2,1},{3,2},{4,3},{5,4},{6,5},{7,6},{9,8},{10,9},{11,10},{12... | collective-permute-start | bytes 61448 | tf_op jit(solution)/shard_map/ppermute | solution.py:19
  258.9 6.4 %collective-permute-start.12 = (bf16[2,32,768]{2,1,0:T(8,128)(2,1)S(1)}, bf16[2,32,768]{2,1,0:T(8,128)(2,1)S(1)}, u32[]{:S(2)}, u32[]{:S(2)}) collective-permute-start(bf16[2,32,768]{2,1,0:T(8,128)(2,1)S(1)} %get-tuple-element.76), channel_id=1, source_target_pairs={{0,8},{8,16},{16,24},{1,9},{9,17},{17,25},{2,10},{10,18},{18,26},{... | collective-permute-start | bytes 294920 | tf_op jit(solution)/shard_map/ppermute | solution.py:17
  262.3 4.1 collective-permute-start.13
  266.5 7.7 %collective-permute-start.14 = (bf16[12,2,768]{2,1,0:T(2,128)(2,1)S(1)}, bf16[12,2,768]{2,1,0:T(2,128)(2,1)S(1)}, u32[]{:S(2)}, u32[]{:S(2)}) collective-permute-start(bf16[12,2,768]{2,1,0:T(2,128)(2,1)S(1)} %get-tuple-element.66), channel_id=1, source_target_pairs={{0,1},{1,2},{2,3},{3,4},{4,5},{5,6},{6,7},{8,9},{9,10},{10,11},{11... | collective-permute-start | bytes 110600 | tf_op jit(solution)/shard_map/ppermute | solution.py:17
  270.8 5.9 %collective-permute-start.15 = (bf16[12,2,768]{2,1,0:T(2,128)(2,1)S(1)}, bf16[12,2,768]{2,1,0:T(2,128)(2,1)S(1)}, u32[]{:S(2)}, u32[]{:S(2)}) collective-permute-start(bf16[12,2,768]{2,1,0:T(2,128)(2,1)S(1)} %get-tuple-element.67), channel_id=1, source_target_pairs={{1,0},{2,1},{3,2},{4,3},{5,4},{6,5},{7,6},{9,8},{10,9},{11,10},{12... | collective-permute-start | bytes 110600 | tf_op jit(solution)/shard_map/ppermute | solution.py:19
  465.5 16.4 %copy-start.46 = (f32[4]{0:T(128)S(1)}, f32[4]{0:T(128)}, u32[]{:S(2)}) copy-start(f32[4]{0:T(128)} %param.27) | copy-start | bytes 52
  465.8 17.0 %copy-start.4 = (bf16[8,32,256]{2,1,0:T(8,128)(2,1)}, bf16[8,32,256]{2,1,0:T(8,128)(2,1)S(1)}, u32[]{:S(2)}) copy-start(bf16[8,32,256]{2,1,0:T(8,128)(2,1)S(1)} %fusion.9) | copy-start | bytes 393220
  465.8 2.8 collective-permute-start.16
  467.1 4.8 collective-permute-start.17
  471.9 5.0 %collective-permute-start.18 = (bf16[10,1,256]{2,1,0:T(2,128)(2,1)S(1)}, bf16[10,1,256]{2,1,0:T(2,128)(2,1)S(1)}, u32[]{:S(2)}, u32[]{:S(2)}) collective-permute-start(bf16[10,1,256]{2,1,0:T(2,128)(2,1)S(1)} %get-tuple-element.82), channel_id=1, source_target_pairs={{0,1},{1,2},{2,3},{3,4},{4,5},{5,6},{6,7},{8,9},{9,10},{10,11},{11... | collective-permute-start | bytes 15368 | tf_op jit(solution)/shard_map/ppermute | solution.py:17
  475.3 5.6 %collective-permute-start.19 = (bf16[10,1,256]{2,1,0:T(2,128)(2,1)S(1)}, bf16[10,1,256]{2,1,0:T(2,128)(2,1)S(1)}, u32[]{:S(2)}, u32[]{:S(2)}) collective-permute-start(bf16[10,1,256]{2,1,0:T(2,128)(2,1)S(1)} %get-tuple-element.83), channel_id=1, source_target_pairs={{1,0},{2,1},{3,2},{4,3},{5,4},{6,5},{7,6},{9,8},{10,9},{11,10},{12... | collective-permute-start | bytes 15368 | tf_op jit(solution)/shard_map/ppermute | solution.py:19
  (45 other events, 202.9 us)
Sparse Core Ops, SparseCore 0:
  106.7 124.7 all-reduce.2
  332.5 124.8 all-reduce.4
where the time goes:
time: 491 us; the launch traced here: 490 us
  waiting for transfers between devices  278 us (57%)
  blocking collectives  83.1 us (17%)
  starting transfers between devices  43.7 us (9%)
  matrix products  35 us (7%)
  local copies, waits for them, and re-layouts  26.6 us (5%)
  between operations  15.2 us (3%)
  other arithmetic  8.23 us (2%)
    psum x2, waiting for transfers between devices, local(): kv_all, key_all = lax.psum((kv_local, key_local), ('row', 'col'))  250 us
    psum x2, blocking collectives, local(): kv_all, key_all = lax.psum((kv_local, key_local), ('row', 'col'))  83.1 us
    ppermute x10, starting transfers between devices, with_halo(): lax.ppermute(tail, axis, [(i, (i + 1) % count) for i in range(ends)])  30.5 us
    ppermute x10, waiting for transfers between devices, with_halo(): lax.ppermute(head, axis, [((i + 1) % count, i) for i in range(ends)])  27.8 us
    ppermute x10, starting transfers between devices, with_halo(): lax.ppermute(head, axis, [((i + 1) % count, i) for i in range(ends)])  13.1 us
    dot_general x2, matrix products, local(): jnp.einsum('rchd,hde->rche', queries, kv_all, precision=lax.Precision.HIG...  12.2 us
    dot_general x2, matrix products, local(): jnp.einsum('rchd,hd->rch', queries, key_all, precision=lax.Precision.HIGH...  10.8 us
    unnamed x98, local copies, waits for them, and re-layouts  10 us
  transfers between devices with their start and end apart: 22, of which 13 were waited for; matrix products, arithmetic and copies ran while one was open for 2% of the time, Pallas kernels for 0%

commit v1 on v0

--- a/solution.py
+++ b/solution.py
@@ -21,6 +21,44 @@
             axis=dim,
         )
     return cells
+
+
+def digits(size, most):
+    radices = []
+    while size > 1:
+        radix = next((r for r in range(min(most, size), 1, -1) if size % r == 0), size)
+        radices.append(radix)
+        size //= radix
+    return radices
+
+
+def sum_by_permutes(value):
+    for axis in ("row", "col"):
+        count = lax.axis_size(axis)
+        stride = 1
+        for radix in digits(count, 4):
+            total = value
+            for step in range(1, radix):
+                pairs = []
+                for i in range(count):
+                    digit = (i // stride) % radix
+                    pairs.append((i, i + ((digit + step) % radix - digit) * stride))
+                total = total + lax.ppermute(value, axis, pairs)
+            value = total
+            stride *= radix
+    return value
+
+
+def sum_by_all_to_all(value):
+    axes = ("row", "col")
+    count = lax.axis_size("row") * lax.axis_size("col")
+    rows = value.shape[0]
+    share = -(-rows // count)
+    value = jnp.pad(value, ((0, share * count - rows), (0, 0)))
+    pieces = lax.all_to_all(value.reshape(count, share, -1), axes, 0, 0, tiled=True)
+    total = jnp.sum(pieces, axis=0, keepdims=True)
+    spread = jnp.broadcast_to(total, pieces.shape)
+    return lax.all_to_all(spread, axes, 0, 0, tiled=True).reshape(share * count, -1)[:rows]
 
 
 def hard_swish(value):
@@ -113,7 +151,11 @@
         values = both[:, :, :, 2, :].astype(jnp.float32)
         kv_local = jnp.einsum("rchd,rche->hde", keys, values, precision=lax.Precision.HIGHEST)
         key_local = jnp.sum(keys, axis=(0, 1))
-        kv_all, key_all = lax.psum((kv_local, key_local), ("row", "col"))
+        packed = jnp.concatenate([kv_local.reshape(-1, 128), key_local.reshape(-1, 128)], axis=0)
+        packed = sum_by_permutes(packed) if section == 0 else sum_by_all_to_all(packed)
+        cut = kv_local.size // 128
+        kv_all = packed[:cut].reshape(kv_local.shape)
+        key_all = packed[cut:].reshape(key_local.shape)
         numer = jnp.einsum("rchd,hde->rche", queries, kv_all, precision=lax.Precision.HIGHEST)
         denom = jnp.einsum("rchd,hd->rch", queries, key_all, precision=lax.Precision.HIGHEST)
         attended = (

time: 491 us -> 186 us (0.38)
  waiting for transfers between devices: 278 us -> 37.7 us
  blocking collectives: 83.1 us -> 22.5 us
  between operations: 15.2 us -> 1.86 us
  starting transfers between devices: 43.7 us -> 53.8 us
    psum x2 -> x0, waiting for transfers between devices: 250 us -> none  [local(): kv_all, key_all = lax.psum((kv_local, key_local), ('row', 'col'))]
    psum x2 -> x0, blocking collectives: 83.1 us -> none  [local(): kv_all, key_all = lax.psum((kv_local, key_local), ('row', 'col'))]
    all_to_all x0 -> x2, blocking collectives: none -> 22.5 us  [the longest x1 12.5 us: sum_by_all_to_all(): lax.all_to_all(value.reshape(count, share, -1), axes, 0, 0, tiled=True)]
    ppermute x0 -> x7, waiting for transfers between devices: none -> 11 us  [sum_by_permutes(): total = total + lax.ppermute(value, axis, pairs)]
    ppermute x0 -> x7, starting transfers between devices: none -> 10.1 us  [sum_by_permutes(): total = total + lax.ppermute(value, axis, pairs)]
    unnamed x98 -> x95, local copies, waits for them, and re-layouts: 10 us -> 10 us
  transfers between devices with their start and end apart: 22 -> 27, of which waited for: 13 -> 17; matrix products, arithmetic and copies ran while one was open for 2% -> 6% of each run, Pallas kernels for 0% -> 0%
where the time goes in v1:
time: 186 us; the launch traced here: 185 us
  starting transfers between devices  53.8 us (29%)
  waiting for transfers between devices  37.7 us (20%)
  matrix products  33.6 us (18%)
  local copies, waits for them, and re-layouts  26.9 us (14%)
  blocking collectives  22.5 us (12%)
  other arithmetic  8.34 us (4%)
  between operations  1.86 us (1%)
    ppermute x10, starting transfers between devices, with_halo(): lax.ppermute(tail, axis, [(i, (i + 1) % count) for i in range(ends)])  30.6 us
    ppermute x10, waiting for transfers between devices, with_halo(): lax.ppermute(head, axis, [((i + 1) % count, i) for i in range(ends)])  26.5 us
    ppermute x10, starting transfers between devices, with_halo(): lax.ppermute(head, axis, [((i + 1) % count, i) for i in range(ends)])  13.1 us
    all_to_all x1, blocking collectives, sum_by_all_to_all(): lax.all_to_all(value.reshape(count, share, -1), axes, 0, 0, tiled=True)  12.5 us
    dot_general x2, matrix products, local(): jnp.einsum('rchd,hde->rche', queries, kv_all, precision=lax.Precision.HIG...  12.3 us
    ppermute x7, waiting for transfers between devices, sum_by_permutes(): total = total + lax.ppermute(value, axis, pairs)  11 us
    dot_general x2, matrix products, local(): jnp.einsum('rchd,hd->rch', queries, key_all, precision=lax.Precision.HIGH...  10.8 us
    ppermute x7, starting transfers between devices, sum_by_permutes(): total = total + lax.ppermute(value, axis, pairs)  10.1 us
  transfers between devices with their start and end apart: 27, of which 17 were waited for; matrix products, arithmetic and copies ran while one was open for 6% of the time, Pallas kernels for 0%

profile of v1, /device:TPU:0, one launch (start us, length us, event | category | flops | bytes accessed | tf_op | source)
XLA Modules:
  0.0 184.7 jit_solution(15131613970399048423)
XLA Ops:
  11.2 3.4 %collective-permute-start.2 = (bf16[10,1,1024]{2,1,0:T(2,128)(2,1)S(1)}, bf16[10,1,1024]{2,1,0:T(2,128)(2,1)S(1)}, u32[]{:S(2)}, u32[]{:S(2)}) collective-permute-start(bf16[10,1,1024]{2,1,0:T(2,128)(2,1)S(1)} %get-tuple-element.62), channel_id=1, source_target_pairs={{0,1},{1,2},{2,3},{3,4},{4,5},{5,6},{6,7},{8,9},{9,10},{10,11},{11... | collective-permute-start | bytes 61448 | tf_op jit(solution)/shard_map/ppermute | solution.py:17
  16.7 3.8 %collective-permute-done.3 = bf16[10,1,1024]{2,1,0:T(2,128)(2,1)S(1)} collective-permute-done((bf16[10,1,1024]{2,1,0:T(2,128)(2,1)S(1)}, bf16[10,1,1024]{2,1,0:T(2,128)(2,1)S(1)}, u32[]{:S(2)}, u32[]{:S(2)}) %collective-permute-start.3) | collective-permute-done | bytes 20512 | tf_op jit(solution)/shard_map/ppermute | solution.py:19
  23.5 3.4 %collective-permute-start.4 = (bf16[2,32,768]{2,1,0:T(8,128)(2,1)}, bf16[2,32,768]{2,1,0:T(8,128)(2,1)S(1)}, u32[]{:S(2)}, u32[]{:S(2)}) collective-permute-start(bf16[2,32,768]{2,1,0:T(8,128)(2,1)} %get-tuple-element.78), channel_id=1, source_target_pairs={{0,8},{8,16},{16,24},{1,9},{9,17},{17,25},{2,10},{10,18},{18,26},{... | collective-permute-start | bytes 294920 | tf_op jit(solution)/shard_map/ppermute | solution.py:17
  31.6 4.3 %collective-permute-start.6 = (bf16[12,2,768]{2,1,0:T(2,128)(2,1)S(1)}, bf16[12,2,768]{2,1,0:T(2,128)(2,1)S(1)}, u32[]{:S(2)}, u32[]{:S(2)}) collective-permute-start(bf16[12,2,768]{2,1,0:T(2,128)(2,1)S(1)} %get-tuple-element.70), channel_id=1, source_target_pairs={{0,1},{1,2},{2,3},{3,4},{4,5},{5,6},{6,7},{8,9},{9,10},{10,11},{11... | collective-permute-start | bytes 110600 | tf_op jit(solution)/shard_map/ppermute | solution.py:17
  39.3 2.5 %collective-permute-done.7 = bf16[12,2,768]{2,1,0:T(2,128)(2,1)S(1)} collective-permute-done((bf16[12,2,768]{2,1,0:T(2,128)(2,1)S(1)}, bf16[12,2,768]{2,1,0:T(2,128)(2,1)S(1)}, u32[]{:S(2)}, u32[]{:S(2)}) %collective-permute-start.7) | collective-permute-done | bytes 36896 | tf_op jit(solution)/shard_map/ppermute | solution.py:19
  42.3 3.0 %add_convert_fusion.1 = bf16[8,32,768]{2,1,0:T(8,128)(2,1)S(1)} fusion(bf16[8,32,768]{2,1,0:T(8,128)(2,1)S(1)} %convolution_convert_fusion.3, bf16[2,32,768]{2,1,0:T(8,128)(2,1)S(1)} %collective-permute-done.5, bf16[2,32,768]{2,1,0:T(8,128)(2,1)S(1)} %collective-permute-done.4, bf16[12,34,768]{2,1,0:T(8,128)(2,1)S(1)} %get-tuple-element.69, ...), kind=kLoop, calls=%fused_computation.63 | loop fusion | flops 15532032 | bytes 8924160 | tf_op jit(solution)/shard_map/convert_element_type | solution.py:91
  51.1 3.4 %collective-permute-start.9 = (f32[132,128]{1,0:T(8,128)S(1)}, f32[132,128]{1,0:T(8,128)S(1)}, u32[]{:S(2)}, u32[]{:S(2)}) collective-permute-start(f32[132,128]{1,0:T(8,128)S(1)} %constant_dynamic-update-slice_fusion), channel_id=1, source_target_pairs={{0,16},{8,24},{16,0},{24,8},{1,17},{9,25},{17,1},{25,9},{2,18},{10... | collective-permute-start | bytes 202760 | tf_op jit(solution)/shard_map/ppermute | solution.py:46
  54.6 3.6 %collective-permute-done.9 = f32[132,128]{1,0:T(8,128)S(1)} collective-permute-done((f32[132,128]{1,0:T(8,128)S(1)}, f32[132,128]{1,0:T(8,128)S(1)}, u32[]{:S(2)}, u32[]{:S(2)}) %collective-permute-start.9) | collective-permute-done | bytes 67616 | tf_op jit(solution)/shard_map/ppermute | solution.py:46
  58.6 2.6 %collective-permute-start.13 = (f32[132,128]{1,0:T(8,128)S(1)}, f32[132,128]{1,0:T(8,128)S(1)}, u32[]{:S(2)}, u32[]{:S(2)}) collective-permute-start(f32[132,128]{1,0:T(8,128)S(1)} %add_add_fusion.1), channel_id=1, source_target_pairs={{0,3},{1,0},{2,1},{3,2},{4,7},{5,4},{6,5},{7,6},{8,11},{9,8},{10,9... | collective-permute-start | bytes 202760 | tf_op jit(solution)/shard_map/ppermute | solution.py:46
  66.9 2.9 %collective-permute-start.14 = (f32[132,128]{1,0:T(8,128)S(1)}, f32[132,128]{1,0:T(8,128)S(1)}, u32[]{:S(2)}, u32[]{:S(2)}) collective-permute-start(f32[132,128]{1,0:T(8,128)S(1)} %add_add_fusion), channel_id=1, source_target_pairs={{0,4},{1,5},{2,6},{3,7},{4,0},{5,1},{6,2},{7,3},{8,12},{9,13},{10,... | collective-permute-start | bytes 202760 | tf_op jit(solution)/shard_map/ppermute | solution.py:46
  72.3 5.4 %fusion.26 = f32[16,1,8,32]{3,1,2,0:T(1,128)S(1)} fusion(f32[16,32,1,1]{1,2,3,0:T(1,128)S(1)} %bitcast.206, bf16[8,32,16,3,32]{4,1,0,2,3:T(8,128)(2,1)} %copy-done.1), kind=kOutput, calls=%fused_computation.60 | convolution fusion | flops 2097152 | bytes 1067008 | tf_op jit(solution)/shard_map/rchd,hd->rch/dot_general | solution.py:160
  77.8 6.1 %fusion.1 = bf16[8,32,16,32]{1,3,0,2:T(8,128)(2,1)S(1)} fusion(f32[8,32,16]{1,0,2:T(8,128)S(1)} %add_bitcast_fusion.1, bf16[8,32,16,3,32]{4,1,0,2,3:T(8,128)(2,1)} %copy-done.1, f32[16,32,32]{2,1,0:T(8,128)S(1)} %reshape.85), kind=kOutput, calls=%fused_computation.3 | convolution fusion | flops 51118080 | bytes 1392640 | tf_op jit(solution)/shard_map/rchd,hde->rche/dot_general | solution.py:159
  90.3 3.0 %collective-permute-done.16 = bf16[1,32,1024]{2,1,0:T(8,128)(2,1)S(1)} collective-permute-done((bf16[1,32,1024]{2,1,0:T(8,128)(2,1)S(1)}, bf16[1,32,1024]{2,1,0:T(8,128)(2,1)S(1)}, u32[]{:S(2)}, u32[]{:S(2)}) %collective-permute-start.16) | collective-permute-done | bytes 65568 | tf_op jit(solution)/shard_map/ppermute | solution.py:19
  97.5 4.9 %collective-permute-done.18 = bf16[10,1,1024]{2,1,0:T(2,128)(2,1)S(1)} collective-permute-done((bf16[10,1,1024]{2,1,0:T(2,128)(2,1)S(1)}, bf16[10,1,1024]{2,1,0:T(2,128)(2,1)S(1)}, u32[]{:S(2)}, u32[]{:S(2)}) %collective-permute-start.18) | collective-permute-done | bytes 20512 | tf_op jit(solution)/shard_map/ppermute | solution.py:19
  104.6 3.7 %collective-permute-start.19 = (bf16[2,32,768]{2,1,0:T(8,128)(2,1)S(1)}, bf16[2,32,768]{2,1,0:T(8,128)(2,1)S(1)}, u32[]{:S(2)}, u32[]{:S(2)}) collective-permute-start(bf16[2,32,768]{2,1,0:T(8,128)(2,1)S(1)} %get-tuple-element.76), channel_id=1, source_target_pairs={{0,8},{8,16},{16,24},{1,9},{9,17},{17,25},{2,10},{10,18},{18,26},{... | collective-permute-start | bytes 294920 | tf_op jit(solution)/shard_map/ppermute | solution.py:17
  112.2 4.8 %collective-permute-start.21 = (bf16[12,2,768]{2,1,0:T(2,128)(2,1)S(1)}, bf16[12,2,768]{2,1,0:T(2,128)(2,1)S(1)}, u32[]{:S(2)}, u32[]{:S(2)}) collective-permute-start(bf16[12,2,768]{2,1,0:T(2,128)(2,1)S(1)} %get-tuple-element.66), channel_id=1, source_target_pairs={{0,1},{1,2},{2,3},{3,4},{4,5},{5,6},{6,7},{8,9},{9,10},{10,11},{11... | collective-permute-start | bytes 110600 | tf_op jit(solution)/shard_map/ppermute | solution.py:17
  120.4 2.4 %collective-permute-done.22 = bf16[12,2,768]{2,1,0:T(2,128)(2,1)S(1)} collective-permute-done((bf16[12,2,768]{2,1,0:T(2,128)(2,1)S(1)}, bf16[12,2,768]{2,1,0:T(2,128)(2,1)S(1)}, u32[]{:S(2)}, u32[]{:S(2)}) %collective-permute-start.22) | collective-permute-done | bytes 36896 | tf_op jit(solution)/shard_map/ppermute | solution.py:19
  123.2 3.0 %add_convert_fusion = bf16[8,32,768]{2,1,0:T(8,128)(2,1)S(1)} fusion(bf16[8,32,768]{2,1,0:T(8,128)(2,1)S(1)} %convolution_convert_fusion.2, bf16[2,32,768]{2,1,0:T(8,128)(2,1)S(1)} %collective-permute-done.20, bf16[2,32,768]{2,1,0:T(8,128)(2,1)S(1)} %collective-permute-done.19, bf16[12,34,768]{2,1,0:T(8,128)(2,1)S(1)} %get-tuple-element.65, ...), kind=kLoop, calls=%fused_computation.62 | loop fusion | flops 15532032 | bytes 8924160 | tf_op jit(solution)/shard_map/convert_element_type | solution.py:91
  132.0 12.5 %all_to_all.10 = f32[32,5,128]{2,1,0:T(8,128)S(1)} all-to-all(f32[32,5,128]{2,1,0:T(8,128)S(1)} %reshape.93), channel_id=1, replica_groups=mesh['row'=4,'col'=8] {'row','col'}, dimensions={0} | all-to-all | bytes 163840 | tf_op jit(solution)/shard_map/all_to_all | solution.py:58
  144.5 10.0 %all_to_all.11 = f32[32,5,128]{2,1,0:T(8,128)S(1)} all-to-all(f32[32,5,128]{2,1,0:T(8,128)S(1)} %broadcast_in_dim.2), channel_id=1, replica_groups=mesh['row'=4,'col'=8] {'row','col'}, dimensions={0} | all-to-all | bytes 163840 | tf_op jit(solution)/shard_map/all_to_all | solution.py:61
  154.6 5.4 %fusion.29 = f32[16,1,8,32]{3,1,2,0:T(1,128)S(1)} fusion(f32[16,32,1,1]{1,2,3,0:T(1,128)S(1)} %bitcast.207, bf16[8,32,16,3,32]{4,1,0,2,3:T(8,128)(2,1)} %copy-done.3), kind=kOutput, calls=%fused_computation.61 | convolution fusion | flops 2097152 | bytes 1067008 | tf_op jit(solution)/shard_map/rchd,hd->rch/dot_general | solution.py:160
  160.2 6.1 %fusion = bf16[8,32,16,32]{1,3,0,2:T(8,128)(2,1)S(1)} fusion(f32[8,32,16]{1,0,2:T(8,128)S(1)} %add_bitcast_fusion, bf16[8,32,16,3,32]{4,1,0,2,3:T(8,128)(2,1)} %copy-done.3, f32[16,32,32]{2,1,0:T(8,128)S(1)} %reshape.95), kind=kOutput, calls=%fused_computation.1 | convolution fusion | flops 51118080 | bytes 1392640 | tf_op jit(solution)/shard_map/rchd,hde->rche/dot_general | solution.py:159
  174.4 2.8 %collective-permute-start.25 = (bf16[10,1,256]{2,1,0:T(2,128)(2,1)S(1)}, bf16[10,1,256]{2,1,0:T(2,128)(2,1)S(1)}, u32[]{:S(2)}, u32[]{:S(2)}) collective-permute-start(bf16[10,1,256]{2,1,0:T(2,128)(2,1)S(1)} %get-tuple-element.82), channel_id=1, source_target_pairs={{0,1},{1,2},{2,3},{3,4},{4,5},{5,6},{6,7},{8,9},{9,10},{10,11},{11... | collective-permute-start | bytes 15368 | tf_op jit(solution)/shard_map/ppermute | solution.py:17
  178.9 3.9 %collective-permute-done.26 = bf16[10,1,256]{2,1,0:T(2,128)(2,1)S(1)} collective-permute-done((bf16[10,1,256]{2,1,0:T(2,128)(2,1)S(1)}, bf16[10,1,256]{2,1,0:T(2,128)(2,1)S(1)}, u32[]{:S(2)}, u32[]{:S(2)}) %collective-permute-start.26) | collective-permute-done | bytes 5152 | tf_op jit(solution)/shard_map/ppermute | solution.py:19
  (217 shorter events, 75.8 us)
Async XLA Ops:
  3.5 5.8 %collective-permute-start = (bf16[1,32,1024]{2,1,0:T(8,128)(2,1)S(1)}, bf16[1,32,1024]{2,1,0:T(8,128)(2,1)S(1)}, u32[]{:S(2)}, u32[]{:S(2)}) collective-permute-start(bf16[1,32,1024]{2,1,0:T(8,128)(2,1)S(1)} %get-tuple-element.74), channel_id=1, source_target_pairs={{0,8},{8,16},{16,24},{1,9},{9,17},{17,25},{2,10},{10,18},{18,26},{... | collective-permute-start | bytes 196616 | tf_op jit(solution)/shard_map/ppermute | solution.py:17
  5.9 5.3 %collective-permute-start.1 = (bf16[1,32,1024]{2,1,0:T(8,128)(2,1)S(1)}, bf16[1,32,1024]{2,1,0:T(8,128)(2,1)S(1)}, u32[]{:S(2)}, u32[]{:S(2)}) collective-permute-start(bf16[1,32,1024]{2,1,0:T(8,128)(2,1)S(1)} %get-tuple-element.75), channel_id=1, source_target_pairs={{8,0},{16,8},{24,16},{9,1},{17,9},{25,17},{10,2},{18,10},{26,18},{... | collective-permute-start | bytes 196616 | tf_op jit(solution)/shard_map/ppermute | solution.py:19
  11.2 5.5 %collective-permute-start.2 = (bf16[10,1,1024]{2,1,0:T(2,128)(2,1)S(1)}, bf16[10,1,1024]{2,1,0:T(2,128)(2,1)S(1)}, u32[]{:S(2)}, u32[]{:S(2)}) collective-permute-start(bf16[10,1,1024]{2,1,0:T(2,128)(2,1)S(1)} %get-tuple-element.62), channel_id=1, source_target_pairs={{0,1},{1,2},{2,3},{3,4},{4,5},{5,6},{6,7},{8,9},{9,10},{10,11},{11... | collective-permute-start | bytes 61448 | tf_op jit(solution)/shard_map/ppermute | solution.py:17
  14.7 5.9 %collective-permute-start.3 = (bf16[10,1,1024]{2,1,0:T(2,128)(2,1)S(1)}, bf16[10,1,1024]{2,1,0:T(2,128)(2,1)S(1)}, u32[]{:S(2)}, u32[]{:S(2)}) collective-permute-start(bf16[10,1,1024]{2,1,0:T(2,128)(2,1)S(1)} %get-tuple-element.63), channel_id=1, source_target_pairs={{1,0},{2,1},{3,2},{4,3},{5,4},{6,5},{7,6},{9,8},{10,9},{11,10},{12... | collective-permute-start | bytes 61448 | tf_op jit(solution)/shard_map/ppermute | solution.py:19
  23.5 6.9 %collective-permute-start.4 = (bf16[2,32,768]{2,1,0:T(8,128)(2,1)}, bf16[2,32,768]{2,1,0:T(8,128)(2,1)S(1)}, u32[]{:S(2)}, u32[]{:S(2)}) collective-permute-start(bf16[2,32,768]{2,1,0:T(8,128)(2,1)} %get-tuple-element.78), channel_id=1, source_target_pairs={{0,8},{8,16},{16,24},{1,9},{9,17},{17,25},{2,10},{10,18},{18,26},{... | collective-permute-start | bytes 294920 | tf_op jit(solution)/shard_map/ppermute | solution.py:17
  26.9 4.6 %collective-permute-start.5 = (bf16[2,32,768]{2,1,0:T(8,128)(2,1)}, bf16[2,32,768]{2,1,0:T(8,128)(2,1)S(1)}, u32[]{:S(2)}, u32[]{:S(2)}) collective-permute-start(bf16[2,32,768]{2,1,0:T(8,128)(2,1)} %get-tuple-element.79), channel_id=1, source_target_pairs={{8,0},{16,8},{24,16},{9,1},{17,9},{25,17},{10,2},{18,10},{26,18},{... | collective-permute-start | bytes 294920 | tf_op jit(solution)/shard_map/ppermute | solution.py:19
  31.6 7.7 %collective-permute-start.6 = (bf16[12,2,768]{2,1,0:T(2,128)(2,1)S(1)}, bf16[12,2,768]{2,1,0:T(2,128)(2,1)S(1)}, u32[]{:S(2)}, u32[]{:S(2)}) collective-permute-start(bf16[12,2,768]{2,1,0:T(2,128)(2,1)S(1)} %get-tuple-element.70), channel_id=1, source_target_pairs={{0,1},{1,2},{2,3},{3,4},{4,5},{5,6},{6,7},{8,9},{9,10},{10,11},{11... | collective-permute-start | bytes 110600 | tf_op jit(solution)/shard_map/ppermute | solution.py:17
  35.9 5.9 %collective-permute-start.7 = (bf16[12,2,768]{2,1,0:T(2,128)(2,1)S(1)}, bf16[12,2,768]{2,1,0:T(2,128)(2,1)S(1)}, u32[]{:S(2)}, u32[]{:S(2)}) collective-permute-start(bf16[12,2,768]{2,1,0:T(2,128)(2,1)S(1)} %get-tuple-element.71), channel_id=1, source_target_pairs={{1,0},{2,1},{3,2},{4,3},{5,4},{6,5},{7,6},{9,8},{10,9},{11,10},{12... | collective-permute-start | bytes 110600 | tf_op jit(solution)/shard_map/ppermute | solution.py:19
  51.1 7.0 %collective-permute-start.9 = (f32[132,128]{1,0:T(8,128)S(1)}, f32[132,128]{1,0:T(8,128)S(1)}, u32[]{:S(2)}, u32[]{:S(2)}) collective-permute-start(f32[132,128]{1,0:T(8,128)S(1)} %constant_dynamic-update-slice_fusion), channel_id=1, source_target_pairs={{0,16},{8,24},{16,0},{24,8},{1,17},{9,25},{17,1},{25,9},{2,18},{10... | collective-permute-start | bytes 202760 | tf_op jit(solution)/shard_map/ppermute | solution.py:46
  54.5 4.1 %collective-permute-start.8 = (f32[132,128]{1,0:T(8,128)S(1)}, f32[132,128]{1,0:T(8,128)S(1)}, u32[]{:S(2)}, u32[]{:S(2)}) collective-permute-start(f32[132,128]{1,0:T(8,128)S(1)} %constant_dynamic-update-slice_fusion), channel_id=1, source_target_pairs={{0,8},{8,16},{16,24},{24,0},{1,9},{9,17},{17,25},{25,1},{2,10},{10... | collective-permute-start | bytes 202760 | tf_op jit(solution)/shard_map/ppermute | solution.py:46
  58.6 4.5 %collective-permute-start.13 = (f32[132,128]{1,0:T(8,128)S(1)}, f32[132,128]{1,0:T(8,128)S(1)}, u32[]{:S(2)}, u32[]{:S(2)}) collective-permute-start(f32[132,128]{1,0:T(8,128)S(1)} %add_add_fusion.1), channel_id=1, source_target_pairs={{0,3},{1,0},{2,1},{3,2},{4,7},{5,4},{6,5},{7,6},{8,11},{9,8},{10,9... | collective-permute-start | bytes 202760 | tf_op jit(solution)/shard_map/ppermute | solution.py:46
  61.2 4.3 %collective-permute-start.12 = (f32[132,128]{1,0:T(8,128)S(1)}, f32[132,128]{1,0:T(8,128)S(1)}, u32[]{:S(2)}, u32[]{:S(2)}) collective-permute-start(f32[132,128]{1,0:T(8,128)S(1)} %add_add_fusion.1), channel_id=1, source_target_pairs={{0,2},{1,3},{2,0},{3,1},{4,6},{5,7},{6,4},{7,5},{8,10},{9,11},{10,... | collective-permute-start | bytes 202760 | tf_op jit(solution)/shard_map/ppermute | solution.py:46
  61.7 5.2 %collective-permute-start.11 = (f32[132,128]{1,0:T(8,128)S(1)}, f32[132,128]{1,0:T(8,128)S(1)}, u32[]{:S(2)}, u32[]{:S(2)}) collective-permute-start(f32[132,128]{1,0:T(8,128)S(1)} %add_add_fusion.1), channel_id=1, source_target_pairs={{0,1},{1,2},{2,3},{3,0},{4,5},{5,6},{6,7},{7,4},{8,9},{9,10},{10,1... | collective-permute-start | bytes 202760 | tf_op jit(solution)/shard_map/ppermute | solution.py:46
  66.9 5.3 %collective-permute-start.14 = (f32[132,128]{1,0:T(8,128)S(1)}, f32[132,128]{1,0:T(8,128)S(1)}, u32[]{:S(2)}, u32[]{:S(2)}) collective-permute-start(f32[132,128]{1,0:T(8,128)S(1)} %add_add_fusion), channel_id=1, source_target_pairs={{0,4},{1,5},{2,6},{3,7},{4,0},{5,1},{6,2},{7,3},{8,12},{9,13},{10,... | collective-permute-start | bytes 202760 | tf_op jit(solution)/shard_map/ppermute | solution.py:46
  89.0 4.4 %collective-permute-start.16 = (bf16[1,32,1024]{2,1,0:T(8,128)(2,1)S(1)}, bf16[1,32,1024]{2,1,0:T(8,128)(2,1)S(1)}, u32[]{:S(2)}, u32[]{:S(2)}) collective-permute-start(bf16[1,32,1024]{2,1,0:T(8,128)(2,1)S(1)} %get-tuple-element.73), channel_id=1, source_target_pairs={{8,0},{16,8},{24,16},{9,1},{17,9},{25,17},{10,2},{18,10},{26,18},{... | collective-permute-start | bytes 196616 | tf_op jit(solution)/shard_map/ppermute | solution.py:19
  93.4 4.1 %collective-permute-start.17 = (bf16[10,1,1024]{2,1,0:T(2,128)(2,1)S(1)}, bf16[10,1,1024]{2,1,0:T(2,128)(2,1)S(1)}, u32[]{:S(2)}, u32[]{:S(2)}) collective-permute-start(bf16[10,1,1024]{2,1,0:T(2,128)(2,1)S(1)} %get-tuple-element.58), channel_id=1, source_target_pairs={{0,1},{1,2},{2,3},{3,4},{4,5},{5,6},{6,7},{8,9},{9,10},{10,11},{11... | collective-permute-start | bytes 61448 | tf_op jit(solution)/shard_map/ppermute | solution.py:17
  95.9 6.5 %collective-permute-start.18 = (bf16[10,1,1024]{2,1,0:T(2,128)(2,1)S(1)}, bf16[10,1,1024]{2,1,0:T(2,128)(2,1)S(1)}, u32[]{:S(2)}, u32[]{:S(2)}) collective-permute-start(bf16[10,1,1024]{2,1,0:T(2,128)(2,1)S(1)} %get-tuple-element.59), channel_id=1, source_target_pairs={{1,0},{2,1},{3,2},{4,3},{5,4},{6,5},{7,6},{9,8},{10,9},{11,10},{12... | collective-permute-start | bytes 61448 | tf_op jit(solution)/shard_map/ppermute | solution.py:19
  104.6 6.7 %collective-permute-start.19 = (bf16[2,32,768]{2,1,0:T(8,128)(2,1)S(1)}, bf16[2,32,768]{2,1,0:T(8,128)(2,1)S(1)}, u32[]{:S(2)}, u32[]{:S(2)}) collective-permute-start(bf16[2,32,768]{2,1,0:T(8,128)(2,1)S(1)} %get-tuple-element.76), channel_id=1, source_target_pairs={{0,8},{8,16},{16,24},{1,9},{9,17},{17,25},{2,10},{10,18},{18,26},{... | collective-permute-start | bytes 294920 | tf_op jit(solution)/shard_map/ppermute | solution.py:17
  108.3 3.8 %collective-permute-start.20 = (bf16[2,32,768]{2,1,0:T(8,128)(2,1)S(1)}, bf16[2,32,768]{2,1,0:T(8,128)(2,1)S(1)}, u32[]{:S(2)}, u32[]{:S(2)}) collective-permute-start(bf16[2,32,768]{2,1,0:T(8,128)(2,1)S(1)} %get-tuple-element.77), channel_id=1, source_target_pairs={{8,0},{16,8},{24,16},{9,1},{17,9},{25,17},{10,2},{18,10},{26,18},{... | collective-permute-start | bytes 294920 | tf_op jit(solution)/shard_map/ppermute | solution.py:19
  112.2 8.2 %collective-permute-start.21 = (bf16[12,2,768]{2,1,0:T(2,128)(2,1)S(1)}, bf16[12,2,768]{2,1,0:T(2,128)(2,1)S(1)}, u32[]{:S(2)}, u32[]{:S(2)}) collective-permute-start(bf16[12,2,768]{2,1,0:T(2,128)(2,1)S(1)} %get-tuple-element.66), channel_id=1, source_target_pairs={{0,1},{1,2},{2,3},{3,4},{4,5},{5,6},{6,7},{8,9},{9,10},{10,11},{11... | collective-permute-start | bytes 110600 | tf_op jit(solution)/shard_map/ppermute | solution.py:17
  117.0 5.9 %collective-permute-start.22 = (bf16[12,2,768]{2,1,0:T(2,128)(2,1)S(1)}, bf16[12,2,768]{2,1,0:T(2,128)(2,1)S(1)}, u32[]{:S(2)}, u32[]{:S(2)}) collective-permute-start(bf16[12,2,768]{2,1,0:T(2,128)(2,1)S(1)} %get-tuple-element.67), channel_id=1, source_target_pairs={{1,0},{2,1},{3,2},{4,3},{5,4},{6,5},{7,6},{9,8},{10,9},{11,10},{12... | collective-permute-start | bytes 110600 | tf_op jit(solution)/shard_map/ppermute | solution.py:19
  170.7 3.6 %collective-permute-start.24 = (bf16[1,32,256]{2,1,0:T(8,128)(2,1)S(1)}, bf16[1,32,256]{2,1,0:T(8,128)(2,1)S(1)}, u32[]{:S(2)}, u32[]{:S(2)}) collective-permute-start(bf16[1,32,256]{2,1,0:T(8,128)(2,1)S(1)} %get-tuple-element.87), channel_id=1, source_target_pairs={{8,0},{16,8},{24,16},{9,1},{17,9},{25,17},{10,2},{18,10},{26,18},{... | collective-permute-start | bytes 49160 | tf_op jit(solution)/shard_map/ppermute | solution.py:19
  174.4 4.5 %collective-permute-start.25 = (bf16[10,1,256]{2,1,0:T(2,128)(2,1)S(1)}, bf16[10,1,256]{2,1,0:T(2,128)(2,1)S(1)}, u32[]{:S(2)}, u32[]{:S(2)}) collective-permute-start(bf16[10,1,256]{2,1,0:T(2,128)(2,1)S(1)} %get-tuple-element.82), channel_id=1, source_target_pairs={{0,1},{1,2},{2,3},{3,4},{4,5},{5,6},{6,7},{8,9},{9,10},{10,11},{11... | collective-permute-start | bytes 15368 | tf_op jit(solution)/shard_map/ppermute | solution.py:17
  177.2 5.6 %collective-permute-start.26 = (bf16[10,1,256]{2,1,0:T(2,128)(2,1)S(1)}, bf16[10,1,256]{2,1,0:T(2,128)(2,1)S(1)}, u32[]{:S(2)}, u32[]{:S(2)}) collective-permute-start(bf16[10,1,256]{2,1,0:T(2,128)(2,1)S(1)} %get-tuple-element.83), channel_id=1, source_target_pairs={{1,0},{2,1},{3,2},{4,3},{5,4},{6,5},{7,6},{9,8},{10,9},{11,10},{12... | collective-permute-start | bytes 15368 | tf_op jit(solution)/shard_map/ppermute | solution.py:19
  (48 other events, 249.2 us)

commit v2 on v1

v2 whole, which is shorter than its diff:
```python
import functools

import jax
import jax.numpy as jnp
from jax import lax
from jax.experimental import pallas as pl
from jax.experimental.pallas import tpu as pltpu
from jax.sharding import PartitionSpec as P

SECTIONS = 2
LANES = 128
SIDE = 8
REACH = 7
PAYLOAD_ROWS = 144
F32 = jnp.float32
BF16 = jnp.bfloat16


def hard_swish(value):
    return value * jnp.minimum(jnp.maximum(value * (1.0 / 6.0) + 0.5, 0.0), 1.0)


def clear_outside(ref, halo, cols):
    rows = ref.shape[0]
    row, col = lax.axis_index("row"), lax.axis_index("col")

    @pl.when(row == 0)
    def _():
        ref[0:halo] = jnp.zeros((halo,) + ref.shape[1:], ref.dtype)

    @pl.when(row == lax.axis_size("row") - 1)
    def _():
        ref[rows - halo : rows] = jnp.zeros((halo,) + ref.shape[1:], ref.dtype)

    @pl.when(col == 0)
    def _():
        ref[:, cols + SIDE : cols + 2 * SIDE, :] = jnp.zeros((rows, SIDE, ref.shape[2]), ref.dtype)

    @pl.when(col == lax.axis_size("col") - 1)
    def _():
        ref[:, cols : cols + SIDE, :] = jnp.zeros((rows, SIDE, ref.shape[2]), ref.dtype)


def flat(value):
    return value.reshape(-1, value.shape[-1])


def same_head(head_dim):
    across = lax.broadcasted_iota(jnp.int32, (LANES, LANES), 0) // head_dim
    along = lax.broadcasted_iota(jnp.int32, (LANES, LANES), 1) // head_dim
    return across == along


def front(x_ref, weights, outs, scratch, halo, tile, head_dim):
    expand, expand_bias, depth, depth_bias, project, project_bias, qkv_weight, agg, group = weights
    mixed_out, query_out, payload_out = outs
    hidden, spread, total, mixed, qkv, scaled = scratch
    rows, width, channels = x_ref.shape
    tile_rows, tile_cols = tile
    inner = rows - 2
    chunk = hidden.shape[2]
    x = flat(x_ref[...])

    def expanded(step, carry):
        at = pl.multiple_of(step * chunk, chunk)
        value = jnp.dot(x, expand[0, :, pl.ds(at, chunk)], preferred_element_type=F32)
        value = hard_swish(value + expand_bias[:, pl.ds(at, chunk)])
        hidden[...] = value.reshape(rows, width, chunk)
        clear_outside(hidden, halo, tile_cols)

        def one_row(r, carry):
            for lane in range(0, chunk, LANES):
                here = pl.ds(pl.multiple_of(at + lane, LANES), LANES)
                above, level, below = (hidden[r + a, :, lane : lane + LANES] for a in range(3))
                parts = [
                    above * depth[0, 0, b : b + 1, here]
                    + level * depth[0, 1, b : b + 1, here]
                    + below * depth[0, 2, b : b + 1, here]
                    for b in range(3)
                ]
                value = parts[1] + pltpu.roll(parts[0], 1, 0) + pltpu.roll(parts[2], width - 1, 0)
                value = hard_swish(value + depth_bias[:, here])
                spread[r, :, lane : lane + LANES] = value.astype(BF16)
            return carry

        lax.fori_loop(0, inner, one_row, 0)
        product = jnp.dot(
            flat(spread[...]), project[0, pl.ds(at, chunk), :], preferred_element_type=F32
        )

        @pl.when(step == 0)
        def _():
            total[...] = product

        @pl.when(step > 0)
        def _():
            total[...] += product

        return carry

    lax.fori_loop(0, expand.shape[2] // chunk, expanded, 0)
    value = total[...] + project_bias[...] + flat(x_ref[1 : rows - 1]).astype(F32)
    mixed[...] = value.astype(BF16).reshape(inner, width, channels)
    mixed_out[...] = mixed[2 : inner - 2]
    value = jnp.dot(flat(mixed[...]), qkv_weight[...], preferred_element_type=F32)
    qkv[...] = value.reshape(inner, width, 3 * channels)
    around = halo - 1
    clear_outside(qkv, around, tile_cols)

    def aggregated(kind, first, count):
        def one_row(r, carry):
            for lane in range(0, channels, LANES):
                here = slice(kind * channels + lane, kind * channels + lane + LANES)
                value = None
                for b in range(5):
                    part = None
                    for a in range(5):
                        term = qkv[first + r + a, :, here] * agg[5 * a + b : 5 * a + b + 1, here]
                        part = term if part is None else part + term
                    if b != 2:
                        part = pltpu.roll(part, (2 - b) % width, 0)
                    value = part if value is None else value + part
                scaled[r, :, lane : lane + LANES] = value.astype(BF16)
            return carry

        lax.fori_loop(0, count, one_row, 0)
        value = jnp.dot(flat(scaled[0:count]), group[kind], preferred_element_type=F32)
        return value.reshape(count, width, channels)

    outer = inner - 4
    query_out[:, :, 0:channels] = jnp.maximum(qkv[2 : inner - 2, :, 0:channels], 0.0).astype(BF16)
    query_out[:, :, channels : 2 * channels] = jnp.maximum(
        aggregated(0, 0, outer), 0.0
    ).astype(BF16)

    def own(value):
        return flat(value[:, 0:tile_cols, :])

    mine = slice(around, around + tile_rows)
    keys = [own(qkv[mine, :, channels : 2 * channels]), own(aggregated(1, around - 2, tile_rows))]
    values = [
        own(qkv[mine, :, 2 * channels : 3 * channels]),
        own(aggregated(2, around - 2, tile_rows)),
    ]
    same = same_head(head_dim)
    summary = jnp.zeros((LANES, LANES), F32)
    payload_out[LANES:PAYLOAD_ROWS, :] = jnp.zeros((PAYLOAD_ROWS - LANES, LANES), F32)
    index = 0
    for key, value in zip(keys, values):
        key = jnp.maximum(key, 0.0)
        sums = jnp.sum(key, axis=0, keepdims=True)
        key, value = key.astype(BF16), value.astype(BF16)
        for lane in range(0, channels, LANES):
            here = slice(lane, lane + LANES)
            product = lax.dot_general(
                key[:, here], value[:, here], (((0,), (0,)), ((), ())), preferred_element_type=F32
            )
            product = jnp.where(same, product, 0.0)
            if index:
                product = pltpu.roll(product, index * head_dim, 1)
            summary = summary + product
            payload_out[LANES + index : LANES + index + 1, :] = sums[:, here]
            index += 1
    payload_out[0:LANES, :] = summary


def attend(mixed_ref, query_ref, payload_ref, weight, bias, head_dim):
    query = flat(query_ref[...])
    same = same_head(head_dim)
    square = (LANES, LANES)
    diagonal = lax.broadcasted_iota(jnp.int32, square, 0) == lax.broadcasted_iota(
        jnp.int32, square, 1
    )
    ones = jnp.where(same, 1.0, 0.0).astype(BF16)
    packed = payload_ref[0:LANES, :]
    total = flat(mixed_ref[...]).astype(F32) + bias[...]
    for index in range(query.shape[1] // LANES):
        summary = packed if index == 0 else pltpu.roll(packed, LANES - index * head_dim, 1)
        summary = jnp.where(same, summary, 0.0).astype(BF16)
        sums = payload_ref[LANES + index : LANES + index + 1, :]
        sums = jnp.where(diagonal, sums, 0.0).astype(BF16)
        sums = jnp.dot(sums, ones, preferred_element_type=F32).astype(BF16)
        part = query[:, index * LANES : (index + 1) * LANES]
        numer = jnp.dot(part, summary, preferred_element_type=F32)
        denom = jnp.dot(part, sums, preferred_element_type=F32)
        attended = (numer / (denom + 1e-6)).astype(BF16)
        total = total + jnp.dot(
            attended, weight[0, index * LANES : (index + 1) * LANES, :], preferred_element_type=F32
        )
    return total


def first_kernel(tile, head_dim, own, top, bottom, right, left, *refs):
    weights, outs, scratch = refs[:9], refs[9:12], refs[12:]
    x_ref = scratch[0]
    rows, cols = tile
    x_ref[0:REACH, 0:cols, :] = top[...]
    x_ref[REACH : REACH + rows, 0:cols, :] = own[...]
    x_ref[REACH + rows :, 0:cols, :] = bottom[...]
    x_ref[:, cols : cols + 2 * SIDE, :] = jnp.concatenate([right[...], left[...]], axis=1)
    front(x_ref, weights, outs, scratch[1:], REACH, tile, head_dim)


def second_kernel(tile, head_dim, mixed, query, payload, out_weight, out_bias, *refs):
    weights, outs, scratch = refs[:9], refs[9:12], refs[12:]
    x_ref = scratch[0]
    value = attend(mixed, query, payload, out_weight, out_bias, head_dim)
    x_ref[...] = value.astype(BF16).reshape(x_ref.shape)
    front(x_ref, weights, outs, scratch[1:], REACH - 3, tile, head_dim)


def last_kernel(
    tile, head_dim, mixed, query, payload, out_weight, out_bias, head_weight, head_bias,
    map_out, boxes_out, x_ref,
):
    rows, cols = tile
    width = cols + 2 * SIDE
    value = attend(mixed, query, payload, out_weight, out_bias, head_dim)
    x_ref[...] = value.astype(BF16).reshape(x_ref.shape)
    clear_outside(x_ref, 1, cols)
    map_out[...] = x_ref[1 : 1 + rows, 0:cols, :]
    total = None
    for a in range(3):
        part = lax.dot_general(
            flat(x_ref[a : a + rows]), head_weight[a], (((1,), (1,)), ((), ())),
            preferred_element_type=F32,
        )
        total = part if total is None else total + part
    total = total.reshape(rows, width, LANES)
    lane = lax.broadcasted_iota(jnp.int32, (width, LANES), 1) // 4
    shifted = [
        jnp.where(
            lane == 0,
            pltpu.roll(total[r], 1, 0),
            jnp.where(lane == 2, pltpu.roll(total[r], width - 1, 0), total[r]),
        )
        for r in range(rows)
    ]
    shifted = jnp.concatenate(shifted, axis=0)
    across = lax.broadcasted_iota(jnp.int32, (8, LANES), 0)
    along = lax.broadcasted_iota(jnp.int32, (8, LANES), 1)
    fold = jnp.where((along % 4 == across) & (along < 12), 1.0, 0.0)
    boxes = lax.dot_general(
        fold, shifted, (((1,), (1,)), ((), ())), precision=lax.Precision.HIGHEST,
        preferred_element_type=F32,
    )
    boxes = boxes[0:4] + head_bias[...]
    for r in range(rows):
        boxes_out[:, r, :] = boxes[:, r * width : r * width + cols]


def section_spec(array, section):
    block = (1,) + array.shape[1:]
    return pl.BlockSpec(block, lambda step: (section,) + (0,) * (array.ndim - 1))


def whole_spec():
    return pl.BlockSpec(memory_space=pltpu.VMEM)


def digits(size, most):
    radices = []
    while size > 1:
        radix = next((r for r in range(min(most, size), 1, -1) if size % r == 0), size)
        radices.append(radix)
        size //= radix
    return radices


def sum_by_permutes(value):
    for axis in ("row", "col"):
        count = lax.axis_size(axis)
        stride = 1
        for radix in digits(count, 4):
            total = value
            sent = value.astype(BF16)
            for step in range(1, radix):
                pairs = []
                for i in range(count):
                    digit = (i // stride) % radix
                    pairs.append((i, i + ((digit + step) % radix - digit) * stride))
                total = total + lax.ppermute(sent, axis, pairs).astype(F32)
            value = total
            stride *= radix
    return value


def shift(value, axis, step):
    count = lax.axis_size(axis)
    pairs = [(i, i + step) for i in range(count) if 0 <= i + step < count]
    return lax.ppermute(value, axis, pairs)


def local(
    features,
    expand_weight,
    expand_bias,
    depth_weight,
    depth_bias,
    project_weight,
    project_bias,
    qkv_weight,
    aggregate_depth,
    aggregate_group,
    output_weight,
    output_bias,
    head_weight,
    head_bias,
):
    rows, cols, channels = features.shape
    head_dim = aggregate_group.shape[2]
    heads = channels // head_dim
    width = cols + 2 * SIDE
    tile = (rows, cols)
    wide = expand_weight.shape[2]

    top = shift(features[rows - REACH :], "row", 1)
    bottom = shift(features[:REACH], "row", -1)
    column = jnp.concatenate([top[:, -SIDE:], features[:, -SIDE:], bottom[:, -SIDE:]], axis=0)
    left = shift(column, "col", 1)
    column = jnp.concatenate([top[:, :SIDE], features[:, :SIDE], bottom[:, :SIDE]], axis=0)
    right = shift(column, "col", -1)

    def by_kind(array, axis):
        shape = array.shape[:axis] + (heads, 3, head_dim) + array.shape[axis + 1 :]
        return jnp.swapaxes(array.reshape(shape), axis, axis + 1).reshape(array.shape)

    qkv_weight = by_kind(qkv_weight, 2)
    aggregate_depth = by_kind(aggregate_depth, 3).reshape(SECTIONS, 25, 3 * channels)
    group = aggregate_group.reshape(SECTIONS, heads, 3, head_dim, head_dim).swapaxes(1, 2)
    group = (
        group[:, :, :, :, None, :] * jnp.eye(heads, dtype=BF16)[None, None, :, None, :, None]
    ).reshape(SECTIONS, 3, channels, channels)
    head_weight = jnp.pad(
        head_weight.reshape(3, 12, channels), ((0, 0), (0, LANES - 12), (0, 0))
    )

    def weights_of(section):
        arrays = [
            expand_weight, expand_bias[section : section + 1], depth_weight,
            depth_bias[section : section + 1], project_weight, project_bias[section : section + 1],
            qkv_weight[section], aggregate_depth[section], group[section],
        ]
        specs = [whole_spec()] * 9
        for index in (0, 2, 4):
            specs[index] = section_spec(arrays[index], section)
        return arrays, specs

    def outs_of(count):
        return [
            jax.ShapeDtypeStruct((count, width, channels), BF16),
            jax.ShapeDtypeStruct((count, width, 2 * channels), BF16),
            jax.ShapeDtypeStruct((PAYLOAD_ROWS, LANES), F32),
        ]

    def scratch_of(count):
        return [
            pltpu.VMEM((count, width, channels), BF16),
            pltpu.VMEM((count, width, 256), F32),
            pltpu.VMEM((count - 2, width, 256), BF16),
            pltpu.VMEM(((count - 2) * width, channels), F32),
            pltpu.VMEM((count - 2, width, channels), BF16),
            pltpu.VMEM((count - 2, width, 3 * channels), F32),
            pltpu.VMEM((count - 6, width, channels), BF16),
        ]

    params = pltpu.CompilerParams(vmem_limit_bytes=40 * 2**20)
    first_rows = rows + 2 * REACH
    arrays, specs = weights_of(0)
    mixed, query, payload = pl.pallas_call(
        functools.partial(first_kernel, tile, head_dim),
        out_shape=outs_of(first_rows - 6),
        grid=(1,),
        in_specs=[whole_spec()] * 5 + specs,
        out_specs=[whole_spec()] * 3,
        scratch_shapes=scratch_of(first_rows),
        compiler_params=params,
        name="first",
    )(features, top, bottom, right, left, *arrays)
    payload = sum_by_permutes(payload)

    second_rows = first_rows - 6
    arrays, specs = weights_of(1)
    mixed, query, payload = pl.pallas_call(
        functools.partial(second_kernel, tile, head_dim),
        out_shape=outs_of(second_rows - 6),
        grid=(1,),
        in_specs=[whole_spec()] * 3 + [section_spec(output_weight, 0), whole_spec()] + specs,
        out_specs=[whole_spec()] * 3,
        scratch_shapes=scratch_of(second_rows),
        compiler_params=params,
        name="second",
    )(mixed, query, payload, output_weight, output_bias[0:1], *arrays)
    payload = sum_by_permutes(payload)

    return pl.pallas_call(
        functools.partial(last_kernel, tile, head_dim),
        out_shape=[
            jax.ShapeDtypeStruct((rows, cols, channels), BF16),
            jax.ShapeDtypeStruct((4, rows, cols), F32),
        ],
        grid=(1,),
        in_specs=[whole_spec()] * 3 + [section_spec(output_weight, 1)] + [whole_spec()] * 3,
        out_specs=[whole_spec()] * 2,
        scratch_shapes=[pltpu.VMEM((rows + 2, width, channels), BF16)],
        compiler_params=params,
        name="last",
    )(
        mixed, query, payload, output_weight, output_bias[1:2], head_weight, head_bias.reshape(4, 1)
    )


def solution(mesh):
    return jax.shard_map(
        local,
        mesh=mesh,
        in_specs=(P("row", "col", None),) + (P(),) * 13,
        out_specs=(P("row", "col", None), P(None, "row", "col")),
        check_vma=False,
    )
```

time: 186 us -> 110 us (0.59)
  matrix products: 33.6 us -> 0 us
  Pallas kernels: 0 us -> 29 us
  waiting for transfers between devices: 37.7 us -> 13.3 us
  starting transfers between devices: 53.8 us -> 31 us
  blocking collectives: 22.5 us -> 0 us
  other arithmetic: 8.34 us -> 5.05 us
  local copies, waits for them, and re-layouts: 26.9 us -> 29.5 us
    dot_general x25 -> x0, matrix products: 33.6 us -> none  [the longest x2 12.3 us: local(): jnp.einsum('rchd,hde->rche', queries, kv_all, precision=lax.Precision.HIG...]
    pallas_call x0 -> x3, Pallas kernels: none -> 29 us  [the longest x1 14.5 us: local(): pl.pallas_call(functools.partial(first_kernel, tile, head_dim), out_shape...]
    ppermute x27 -> x18, waiting for transfers between devices: 37.7 us -> 13.3 us  [the longest x14 13.3 us: sum_by_permutes(): total = total + lax.ppermute(sent, axis, pairs).astype(F32)]
    ppermute x27 -> x18, starting transfers between devices: 53.8 us -> 31 us  [the longest x14 21.1 us: sum_by_permutes(): total = total + lax.ppermute(sent, axis, pairs).astype(F32)]
    all_to_all x2 -> x0, blocking collectives: 22.5 us -> none  [the longest x1 12.5 us: sum_by_all_to_all(): lax.all_to_all(value.reshape(count, share, -1), axes, 0, 0, tiled=True)]
    squeeze x1 -> x6, local copies, waits for them, and re-layouts: 0.68 us -> 9.94 us  [the longest x2 4.73 us: weights_of(): group[section]]
    reshape x16 -> x3, local copies, waits for them, and re-layouts: 8.18 us -> 0.67 us  [the longest x1 0.56 us: by_kind(): array.reshape(shape)]
    slice x21 -> x14, local copies, waits for them, and re-layouts: 5.09 us -> 11.7 us  [the longest x3 4.54 us: weights_of(): aggregate_depth[section]]
  transfers between devices with their start and end apart: 27 -> 18, of which waited for: 17 -> 10; matrix products, arithmetic and copies ran while one was open for 6% -> 23% of each run, Pallas kernels for 0% -> 0%
where the time goes in v2:
time: 110 us; the launch traced here: 109 us
  starting transfers between devices  31 us (28%)
  local copies, waits for them, and re-layouts  29.5 us (27%)
  Pallas kernels  29 us (26%)
  waiting for transfers between devices  13.3 us (12%)
  other arithmetic  5.05 us (5%)
    ppermute x14, starting transfers between devices, sum_by_permutes(): total = total + lax.ppermute(sent, axis, pairs).astype(F32)  21.1 us
    pallas_call x1, Pallas kernels, local(): pl.pallas_call(functools.partial(first_kernel, tile, head_dim), out_shape...  14.5 us
    ppermute x14, waiting for transfers between devices, sum_by_permutes(): total = total + lax.ppermute(sent, axis, pairs).astype(F32)  13.3 us
    pallas_call x1, Pallas kernels, local(): pl.pallas_call(functools.partial(second_kernel, tile, head_dim), out_shap...  11.8 us
    ppermute x4, starting transfers between devices, shift(): return lax.ppermute(value, axis, pairs)  9.82 us
    unnamed x44, local copies, waits for them, and re-layouts  7.13 us
    squeeze x2, local copies, waits for them, and re-layouts, weights_of(): group[section]  4.73 us
    slice x3, local copies, waits for them, and re-layouts, weights_of(): aggregate_depth[section]  4.54 us
  transfers between devices with their start and end apart: 18, of which 10 were waited for; matrix products, arithmetic and copies ran while one was open for 23% of the time, Pallas kernels for 0%

profile of v2, /device:TPU:0, one launch (start us, length us, event | category | flops | bytes accessed | tf_op | source)
XLA Modules:
  0.0 108.7 jit_solution(4972909486731536080)
XLA Ops:
  1.6 2.4 %collective-permute-start = (bf16[7,32,256]{2,1,0:T(8,128)(2,1)S(1)}, bf16[7,32,256]{2,1,0:T(8,128)(2,1)S(1)}, u32[]{:S(2)}, u32[]{:S(2)}) collective-permute-start(bf16[7,32,256]{2,1,0:T(8,128)(2,1)S(1)} %get-tuple-element.27), channel_id=1, source_target_pairs={{0,8},{8,16},{16,24},{1,9},{9,17},{17,25},{2,10},{10,18},{18,26},{... | collective-permute-start | bytes 344072 | tf_op jit(solution)/shard_map/ppermute | solution.py:291
  6.1 2.1 %broadcast_multiply_fusion = bf16[2,3,8,32,8,32]{5,4,3,2,1,0:T(8,128)(2,1)S(1)} fusion(bf16[8,8]{1,0:T(8,128)(2,1)S(1)} %fusion.2, bf16[2,3,8,32,32]{4,3,1,2,0:T(8,128)(2,1)} %bitcast.24), kind=kLoop, calls=%fused_computation | loop fusion | flops 1572864 | bytes 884864 | tf_op jit(solution)/shard_map/mul | solution.py:332
  8.2 2.0 %fusion.5 = (bf16[1,3,8,32,8,32]{5,4,3,2,1,0:T(8,128)(2,1)}, bf16[1,3,8,32,8,32]{5,4,3,2,1,0:T(8,128)(2,1)}) fusion(bf16[2,3,8,32,8,32]{5,4,3,2,1,0:T(8,128)(2,1)S(1)} %broadcast_multiply_fusion), kind=kLoop, calls=%fused_computation.15 | loop fusion | bytes 1572864 | tf_op jit(solution)/shard_map/slice | solution.py:342
  13.6 4.9 %collective-permute-start.3 = (bf16[22,8,256]{2,1,0:T(8,128)(2,1)}, bf16[22,8,256]{2,1,0:T(8,128)(2,1)}, u32[]{:S(2)}, u32[]{:S(2)}) collective-permute-start(bf16[22,8,256]{2,1,0:T(8,128)(2,1)} %pad_maximum_fusion.1), channel_id=1, source_target_pairs={{0,1},{1,2},{2,3},{3,4},{4,5},{5,6},{6,7},{8,9},{9,10},{10,11},{11... | collective-permute-start | bytes 270344 | tf_op jit(solution)/shard_map/ppermute | solution.py:291
  20.5 2.4 %squeeze.20.refs_8_ = bf16[3,256,256]{2,1,0:T(8,128)(2,1)S(1)} reshape(bf16[1,3,8,32,8,32]{5,4,3,2,1,0:T(8,128)(2,1)} %get-tuple-element.19) | data formatting | bytes 786432 | tf_op jit(solution)/shard_map/squeeze | solution.py:342
  24.8 1.7 %copy.24 = f32[1,5,5,3,8,32]{5,4,3,2,1,0:T(8,128)} copy(f32[1,5,5,3,8,32]{5,3,4,0,2,1:T(4,128)} %get-tuple-element.21) | data formatting | bytes 153600 | tf_op jit(solution)/shard_map/slice | solution.py:342
  28.7 14.5 %first.1 = (bf16[16,48,256]{2,1,0:T(8,128)(2,1)S(1)}, bf16[16,48,512]{2,1,0:T(8,128)(2,1)S(1)}, f32[144,128]{1,0:T(8,128)S(1)}) custom-call(bf16[8,32,256]{2,1,0:T(8,128)(2,1)S(1)} %copy-done.3, bf16[7,32,256]{2,1,0:T(8,128)(2,1)S(1)} %collective-permute-done.top, bf16[7,32,256]{2,1,0:T(8,128)(2,1)S(1)} %collective-permute-done.1.bottom, ...), custom_call_target="tpu_custom_call" | custom-call | tf_op jit(solution)/shard_map/first/pallas_call | solution.py:370
  44.1 2.1 %collective-permute-start.4 = (bf16[144,128]{1,0:T(8,128)(2,1)S(1)}, bf16[144,128]{1,0:T(8,128)(2,1)S(1)}, u32[]{:S(2)}, u32[]{:S(2)}) collective-permute-start(bf16[144,128]{1,0:T(8,128)(2,1)S(1)} %convert_element_type.70), channel_id=1, source_target_pairs={{0,8},{8,16},{16,24},{24,0},{1,9},{9,17},{17,25},{25,1},{2,10},{10... | collective-permute-start | bytes 110600 | tf_op jit(solution)/shard_map/ppermute | solution.py:282
  46.1 2.0 %collective-permute-start.5 = (bf16[144,128]{1,0:T(8,128)(2,1)S(1)}, bf16[144,128]{1,0:T(8,128)(2,1)S(1)}, u32[]{:S(2)}, u32[]{:S(2)}) collective-permute-start(bf16[144,128]{1,0:T(8,128)(2,1)S(1)} %convert_element_type.70), channel_id=1, source_target_pairs={{0,16},{8,24},{16,0},{24,8},{1,17},{9,25},{17,1},{25,9},{2,18},{10... | collective-permute-start | bytes 110600 | tf_op jit(solution)/shard_map/ppermute | solution.py:282
  51.2 2.6 %collective-permute-start.7 = (bf16[144,128]{1,0:T(8,128)(2,1)S(1)}, bf16[144,128]{1,0:T(8,128)(2,1)S(1)}, u32[]{:S(2)}, u32[]{:S(2)}) collective-permute-start(bf16[144,128]{1,0:T(8,128)(2,1)S(1)} %fusion), channel_id=1, source_target_pairs={{0,1},{1,2},{2,3},{3,0},{4,5},{5,6},{6,7},{7,4},{8,9},{9,10},{10,1... | collective-permute-start | bytes 110600 | tf_op jit(solution)/shard_map/ppermute | solution.py:282
  54.8 2.3 %collective-permute-start.9 = (bf16[144,128]{1,0:T(8,128)(2,1)S(1)}, bf16[144,128]{1,0:T(8,128)(2,1)S(1)}, u32[]{:S(2)}, u32[]{:S(2)}) collective-permute-start(bf16[144,128]{1,0:T(8,128)(2,1)S(1)} %fusion), channel_id=1, source_target_pairs={{0,3},{1,0},{2,1},{3,2},{4,7},{5,4},{6,5},{7,6},{8,11},{9,8},{10,9... | collective-permute-start | bytes 110600 | tf_op jit(solution)/shard_map/ppermute | solution.py:282
  59.4 3.3 %collective-permute-start.10 = (bf16[144,128]{1,0:T(8,128)(2,1)}, bf16[144,128]{1,0:T(8,128)(2,1)}, u32[]{:S(2)}, u32[]{:S(2)}) collective-permute-start(bf16[144,128]{1,0:T(8,128)(2,1)} %get-tuple-element.16), channel_id=1, source_target_pairs={{0,4},{1,5},{2,6},{3,7},{4,0},{5,1},{6,2},{7,3},{8,12},{9,13},{10,... | collective-permute-start | bytes 110600 | tf_op jit(solution)/shard_map/ppermute | solution.py:282
  62.7 2.4 %squeeze.23.refs_8_ = bf16[3,256,256]{2,1,0:T(8,128)(2,1)S(1)} reshape(bf16[1,3,8,32,8,32]{5,4,3,2,1,0:T(8,128)(2,1)} %get-tuple-element.18) | data formatting | bytes 786432 | tf_op jit(solution)/shard_map/squeeze | solution.py:342
  65.1 1.8 %copy.28 = bf16[1,256,3,8,32]{1,4,3,2,0:T(8,128)(2,1)} copy(bf16[1,256,3,8,32]{1,4,2,3,0:T(8,128)(2,1)} %get-tuple-element.22) | data formatting | bytes 786432 | tf_op jit(solution)/shard_map/slice | solution.py:342
  68.0 1.8 %copy.29 = f32[1,5,5,3,8,32]{5,4,3,2,1,0:T(8,128)} copy(f32[1,5,5,3,8,32]{5,3,4,0,2,1:T(4,128)} %get-tuple-element.20) | data formatting | bytes 153600 | tf_op jit(solution)/shard_map/slice | solution.py:342
  69.8 1.8 %squeeze.22.refs_7_ = f32[25,768]{1,0:T(8,128)} reshape(f32[1,5,5,3,8,32]{5,4,3,2,1,0:T(8,128)} %copy.29) | data formatting | bytes 153600 | tf_op jit(solution)/shard_map/squeeze | solution.py:342
  75.5 11.8 %second.1 = (bf16[10,48,256]{2,1,0:T(8,128)(2,1)S(1)}, bf16[10,48,512]{2,1,0:T(8,128)(2,1)S(1)}, f32[144,128]{1,0:T(8,128)S(1)}) custom-call(bf16[16,48,256]{2,1,0:T(8,128)(2,1)S(1)} %copy-done.9, bf16[16,48,512]{2,1,0:T(8,128)(2,1)S(1)} %copy-done.5, f32[144,128]{1,0:T(8,128)S(1)} %convert_add_fusion.3.payload, bf16[2,512,256]{2,1,0:T(8,128)(2,1)S(1)} %copy-done.2, ...), custom_call_target="tpu_custom_call" | custom-call | tf_op jit(solution)/shard_map/second/pallas_call | solution.py:384
  88.5 1.4 %collective-permute-start.13 = (bf16[144,128]{1,0:T(8,128)(2,1)S(1)}, bf16[144,128]{1,0:T(8,128)(2,1)S(1)}, u32[]{:S(2)}, u32[]{:S(2)}) collective-permute-start(bf16[144,128]{1,0:T(8,128)(2,1)S(1)} %convert_element_type.80), channel_id=1, source_target_pairs={{0,24},{8,0},{16,8},{24,16},{1,25},{9,1},{17,9},{25,17},{2,26},{10... | collective-permute-start | bytes 110600 | tf_op jit(solution)/shard_map/ppermute | solution.py:282
  91.7 1.5 %collective-permute-start.14 = (bf16[144,128]{1,0:T(8,128)(2,1)S(1)}, bf16[144,128]{1,0:T(8,128)(2,1)S(1)}, u32[]{:S(2)}, u32[]{:S(2)}) collective-permute-start(bf16[144,128]{1,0:T(8,128)(2,1)S(1)} %fusion.1), channel_id=1, source_target_pairs={{0,1},{1,2},{2,3},{3,0},{4,5},{5,6},{6,7},{7,4},{8,9},{9,10},{10,1... | collective-permute-start | bytes 110600 | tf_op jit(solution)/shard_map/ppermute | solution.py:282
  93.3 1.6 %collective-permute-start.15 = (bf16[144,128]{1,0:T(8,128)(2,1)S(1)}, bf16[144,128]{1,0:T(8,128)(2,1)S(1)}, u32[]{:S(2)}, u32[]{:S(2)}) collective-permute-start(bf16[144,128]{1,0:T(8,128)(2,1)S(1)} %fusion.1), channel_id=1, source_target_pairs={{0,2},{1,3},{2,0},{3,1},{4,6},{5,7},{6,4},{7,5},{8,10},{9,11},{10,... | collective-permute-start | bytes 110600 | tf_op jit(solution)/shard_map/ppermute | solution.py:282
  95.3 1.8 %collective-permute-done.14 = bf16[144,128]{1,0:T(8,128)(2,1)S(1)} collective-permute-done((bf16[144,128]{1,0:T(8,128)(2,1)S(1)}, bf16[144,128]{1,0:T(8,128)(2,1)S(1)}, u32[]{:S(2)}, u32[]{:S(2)}) %collective-permute-start.14) | collective-permute-done | bytes 36896 | tf_op jit(solution)/shard_map/ppermute | solution.py:282
  97.3 1.5 %collective-permute-done.16 = bf16[144,128]{1,0:T(8,128)(2,1)S(1)} collective-permute-done((bf16[144,128]{1,0:T(8,128)(2,1)S(1)}, bf16[144,128]{1,0:T(8,128)(2,1)S(1)}, u32[]{:S(2)}, u32[]{:S(2)}) %collective-permute-start.16) | collective-permute-done | bytes 36896 | tf_op jit(solution)/shard_map/ppermute | solution.py:282
  99.5 4.6 %collective-permute-done.17 = bf16[144,128]{1,0:T(8,128)(2,1)S(1)} collective-permute-done((bf16[144,128]{1,0:T(8,128)(2,1)S(1)}, bf16[144,128]{1,0:T(8,128)(2,1)S(1)}, u32[]{:S(2)}, u32[]{:S(2)}) %collective-permute-start.17) | collective-permute-done | bytes 36896 | tf_op jit(solution)/shard_map/ppermute | solution.py:282
  106.1 2.7 %last.1 = (bf16[8,32,256]{2,1,0:T(8,128)(2,1)}, f32[4,8,32]{2,1,0:T(8,128)}) custom-call(bf16[10,48,256]{2,1,0:T(8,128)(2,1)S(1)} %copy-done.12, bf16[10,48,512]{2,1,0:T(8,128)(2,1)S(1)} %copy-done.7, f32[144,128]{1,0:T(8,128)S(1)} %convert_add_fusion.payload, bf16[2,512,256]{2,1,0:T(8,128)(2,1)S(1)} %copy-done.2, f32[1,256]{1,0:T(1,128)S(1)} %get-tuple-element.36.out_bias, ...), custom_call_target="tpu_custom_call" | custom-call | tf_op jit(solution)/shard_map/last/pallas_call | solution.py:396
  (95 shorter events, 31.0 us)
Async XLA Ops:
  1.6 11.3 %collective-permute-start = (bf16[7,32,256]{2,1,0:T(8,128)(2,1)S(1)}, bf16[7,32,256]{2,1,0:T(8,128)(2,1)S(1)}, u32[]{:S(2)}, u32[]{:S(2)}) collective-permute-start(bf16[7,32,256]{2,1,0:T(8,128)(2,1)S(1)} %get-tuple-element.27), channel_id=1, source_target_pairs={{0,8},{8,16},{16,24},{1,9},{9,17},{17,25},{2,10},{10,18},{18,26},{... | collective-permute-start | bytes 344072 | tf_op jit(solution)/shard_map/ppermute | solution.py:291
  4.0 9.0 %collective-permute-start.1 = (bf16[7,32,256]{2,1,0:T(8,128)(2,1)S(1)}, bf16[7,32,256]{2,1,0:T(8,128)(2,1)S(1)}, u32[]{:S(2)}, u32[]{:S(2)}) collective-permute-start(bf16[7,32,256]{2,1,0:T(8,128)(2,1)S(1)} %get-tuple-element.26), channel_id=1, source_target_pairs={{8,0},{16,8},{24,16},{9,1},{17,9},{25,17},{10,2},{18,10},{26,18},{... | collective-permute-start | bytes 344072 | tf_op jit(solution)/shard_map/ppermute | solution.py:291
  12.9 15.7 %copy-start.3 = (bf16[8,32,256]{2,1,0:T(8,128)(2,1)S(1)}, bf16[8,32,256]{2,1,0:T(8,128)(2,1)}, u32[]{:S(2)}) copy-start(bf16[8,32,256]{2,1,0:T(8,128)(2,1)} %own.1) | copy-start | bytes 393220
  13.6 15.0 %collective-permute-start.3 = (bf16[22,8,256]{2,1,0:T(8,128)(2,1)}, bf16[22,8,256]{2,1,0:T(8,128)(2,1)}, u32[]{:S(2)}, u32[]{:S(2)}) collective-permute-start(bf16[22,8,256]{2,1,0:T(8,128)(2,1)} %pad_maximum_fusion.1), channel_id=1, source_target_pairs={{0,1},{1,2},{2,3},{3,4},{4,5},{5,6},{6,7},{8,9},{9,10},{10,11},{11... | collective-permute-start | bytes 270344 | tf_op jit(solution)/shard_map/ppermute | solution.py:291
  19.2 9.5 %collective-permute-start.2 = (bf16[22,8,256]{2,1,0:T(8,128)(2,1)}, bf16[22,8,256]{2,1,0:T(8,128)(2,1)}, u32[]{:S(2)}, u32[]{:S(2)}) collective-permute-start(bf16[22,8,256]{2,1,0:T(8,128)(2,1)} %pad_maximum_fusion), channel_id=1, source_target_pairs={{1,0},{2,1},{3,2},{4,3},{5,4},{6,5},{7,6},{9,8},{10,9},{11,10},{12... | collective-permute-start | bytes 270344 | tf_op jit(solution)/shard_map/ppermute | solution.py:291
  23.6 39.0 %copy-start.19 = (f32[2,256]{1,0:T(2,128)S(1)}, f32[2,256]{1,0:T(2,128)}, u32[]{:S(2)}) copy-start(f32[2,256]{1,0:T(2,128)} %param.25) | copy-start | bytes 6148
  44.1 18.6 %copy-start.8 = (bf16[16,48,256]{2,1,0:T(8,128)(2,1)}, bf16[16,48,256]{2,1,0:T(8,128)(2,1)S(1)}, u32[]{:S(2)}) copy-start(bf16[16,48,256]{2,1,0:T(8,128)(2,1)S(1)} %get-tuple-element.8.mixed) | copy-start | bytes 1179652
  44.1 28.4 %copy-start.2 = (bf16[2,512,256]{2,1,0:T(8,128)(2,1)S(1)}, bf16[2,512,256]{2,1,0:T(8,128)(2,1)}, u32[]{:S(2)}) copy-start(bf16[2,512,256]{2,1,0:T(8,128)(2,1)} %out_weight.3) | copy-start | bytes 1572868
  44.1 5.5 %collective-permute-start.4 = (bf16[144,128]{1,0:T(8,128)(2,1)S(1)}, bf16[144,128]{1,0:T(8,128)(2,1)S(1)}, u32[]{:S(2)}, u32[]{:S(2)}) collective-permute-start(bf16[144,128]{1,0:T(8,128)(2,1)S(1)} %convert_element_type.70), channel_id=1, source_target_pairs={{0,8},{8,16},{16,24},{24,0},{1,9},{9,17},{17,25},{25,1},{2,10},{10... | collective-permute-start | bytes 110600 | tf_op jit(solution)/shard_map/ppermute | solution.py:282
  46.1 4.0 %collective-permute-start.5 = (bf16[144,128]{1,0:T(8,128)(2,1)S(1)}, bf16[144,128]{1,0:T(8,128)(2,1)S(1)}, u32[]{:S(2)}, u32[]{:S(2)}) collective-permute-start(bf16[144,128]{1,0:T(8,128)(2,1)S(1)} %convert_element_type.70), channel_id=1, source_target_pairs={{0,16},{8,24},{16,0},{24,8},{1,17},{9,25},{17,1},{25,9},{2,18},{10... | collective-permute-start | bytes 110600 | tf_op jit(solution)/shard_map/ppermute | solution.py:282
  48.1 3.0 %collective-permute-start.6 = (bf16[144,128]{1,0:T(8,128)(2,1)S(1)}, bf16[144,128]{1,0:T(8,128)(2,1)S(1)}, u32[]{:S(2)}, u32[]{:S(2)}) collective-permute-start(bf16[144,128]{1,0:T(8,128)(2,1)S(1)} %convert_element_type.70), channel_id=1, source_target_pairs={{0,24},{8,0},{16,8},{24,16},{1,25},{9,1},{17,9},{25,17},{2,26},{10... | collective-permute-start | bytes 110600 | tf_op jit(solution)/shard_map/ppermute | solution.py:282
  51.2 5.9 %collective-permute-start.7 = (bf16[144,128]{1,0:T(8,128)(2,1)S(1)}, bf16[144,128]{1,0:T(8,128)(2,1)S(1)}, u32[]{:S(2)}, u32[]{:S(2)}) collective-permute-start(bf16[144,128]{1,0:T(8,128)(2,1)S(1)} %fusion), channel_id=1, source_target_pairs={{0,1},{1,2},{2,3},{3,0},{4,5},{5,6},{6,7},{7,4},{8,9},{9,10},{10,1... | collective-permute-start | bytes 110600 | tf_op jit(solution)/shard_map/ppermute | solution.py:282
  53.8 4.0 %collective-permute-start.8 = (bf16[144,128]{1,0:T(8,128)(2,1)S(1)}, bf16[144,128]{1,0:T(8,128)(2,1)S(1)}, u32[]{:S(2)}, u32[]{:S(2)}) collective-permute-start(bf16[144,128]{1,0:T(8,128)(2,1)S(1)} %fusion), channel_id=1, source_target_pairs={{0,2},{1,3},{2,0},{3,1},{4,6},{5,7},{6,4},{7,5},{8,10},{9,11},{10,... | collective-permute-start | bytes 110600 | tf_op jit(solution)/shard_map/ppermute | solution.py:282
  54.8 4.0 %collective-permute-start.9 = (bf16[144,128]{1,0:T(8,128)(2,1)S(1)}, bf16[144,128]{1,0:T(8,128)(2,1)S(1)}, u32[]{:S(2)}, u32[]{:S(2)}) collective-permute-start(bf16[144,128]{1,0:T(8,128)(2,1)S(1)} %fusion), channel_id=1, source_target_pairs={{0,3},{1,0},{2,1},{3,2},{4,7},{5,4},{6,5},{7,6},{8,11},{9,8},{10,9... | collective-permute-start | bytes 110600 | tf_op jit(solution)/shard_map/ppermute | solution.py:282
  59.4 12.1 %collective-permute-start.10 = (bf16[144,128]{1,0:T(8,128)(2,1)}, bf16[144,128]{1,0:T(8,128)(2,1)}, u32[]{:S(2)}, u32[]{:S(2)}) collective-permute-start(bf16[144,128]{1,0:T(8,128)(2,1)} %get-tuple-element.16), channel_id=1, source_target_pairs={{0,4},{1,5},{2,6},{3,7},{4,0},{5,1},{6,2},{7,3},{8,12},{9,13},{10,... | collective-permute-start | bytes 110600 | tf_op jit(solution)/shard_map/ppermute | solution.py:282
  69.8 29.6 %copy-start.15 = (bf16[3,3,4,256]{3,2,1,0:T(4,128)(2,1)S(1)}, bf16[3,3,4,256]{3,2,1,0:T(4,128)(2,1)}, u32[]{:S(2)}) copy-start(bf16[3,3,4,256]{3,2,1,0:T(4,128)(2,1)} %param.26) | copy-start | bytes 55300
  69.8 29.6 %copy-start.20 = (f32[4]{0:T(128)S(1)}, f32[4]{0:T(128)}, u32[]{:S(2)}) copy-start(f32[4]{0:T(128)} %param.27) | copy-start | bytes 52
  87.3 3.4 %collective-permute-start.11 = (bf16[144,128]{1,0:T(8,128)(2,1)S(1)}, bf16[144,128]{1,0:T(8,128)(2,1)S(1)}, u32[]{:S(2)}, u32[]{:S(2)}) collective-permute-start(bf16[144,128]{1,0:T(8,128)(2,1)S(1)} %convert_element_type.80), channel_id=1, source_target_pairs={{0,8},{8,16},{16,24},{24,0},{1,9},{9,17},{17,25},{25,1},{2,10},{10... | collective-permute-start | bytes 110600 | tf_op jit(solution)/shard_map/ppermute | solution.py:282
  87.4 4.3 %collective-permute-start.12 = (bf16[144,128]{1,0:T(8,128)(2,1)S(1)}, bf16[144,128]{1,0:T(8,128)(2,1)S(1)}, u32[]{:S(2)}, u32[]{:S(2)}) collective-permute-start(bf16[144,128]{1,0:T(8,128)(2,1)S(1)} %convert_element_type.80), channel_id=1, source_target_pairs={{0,16},{8,24},{16,0},{24,8},{1,17},{9,25},{17,1},{25,9},{2,18},{10... | collective-permute-start | bytes 110600 | tf_op jit(solution)/shard_map/ppermute | solution.py:282
  88.5 3.2 %collective-permute-start.13 = (bf16[144,128]{1,0:T(8,128)(2,1)S(1)}, bf16[144,128]{1,0:T(8,128)(2,1)S(1)}, u32[]{:S(2)}, u32[]{:S(2)}) collective-permute-start(bf16[144,128]{1,0:T(8,128)(2,1)S(1)} %convert_element_type.80), channel_id=1, source_target_pairs={{0,24},{8,0},{16,8},{24,16},{1,25},{9,1},{17,9},{25,17},{2,26},{10... | collective-permute-start | bytes 110600 | tf_op jit(solution)/shard_map/ppermute | solution.py:282
  91.7 5.3 %collective-permute-start.14 = (bf16[144,128]{1,0:T(8,128)(2,1)S(1)}, bf16[144,128]{1,0:T(8,128)(2,1)S(1)}, u32[]{:S(2)}, u32[]{:S(2)}) collective-permute-start(bf16[144,128]{1,0:T(8,128)(2,1)S(1)} %fusion.1), channel_id=1, source_target_pairs={{0,1},{1,2},{2,3},{3,0},{4,5},{5,6},{6,7},{7,4},{8,9},{9,10},{10,1... | collective-permute-start | bytes 110600 | tf_op jit(solution)/shard_map/ppermute | solution.py:282
  93.3 4.0 %collective-permute-start.15 = (bf16[144,128]{1,0:T(8,128)(2,1)S(1)}, bf16[144,128]{1,0:T(8,128)(2,1)S(1)}, u32[]{:S(2)}, u32[]{:S(2)}) collective-permute-start(bf16[144,128]{1,0:T(8,128)(2,1)S(1)} %fusion.1), channel_id=1, source_target_pairs={{0,2},{1,3},{2,0},{3,1},{4,6},{5,7},{6,4},{7,5},{8,10},{9,11},{10,... | collective-permute-start | bytes 110600 | tf_op jit(solution)/shard_map/ppermute | solution.py:282
  94.8 4.0 %collective-permute-start.16 = (bf16[144,128]{1,0:T(8,128)(2,1)S(1)}, bf16[144,128]{1,0:T(8,128)(2,1)S(1)}, u32[]{:S(2)}, u32[]{:S(2)}) collective-permute-start(bf16[144,128]{1,0:T(8,128)(2,1)S(1)} %fusion.1), channel_id=1, source_target_pairs={{0,3},{1,0},{2,1},{3,2},{4,7},{5,4},{6,5},{7,6},{8,11},{9,8},{10,9... | collective-permute-start | bytes 110600 | tf_op jit(solution)/shard_map/ppermute | solution.py:282
  98.9 5.2 %collective-permute-start.17 = (bf16[144,128]{1,0:T(8,128)(2,1)S(1)}, bf16[144,128]{1,0:T(8,128)(2,1)S(1)}, u32[]{:S(2)}, u32[]{:S(2)}) collective-permute-start(bf16[144,128]{1,0:T(8,128)(2,1)S(1)} %get-tuple-element.14), channel_id=1, source_target_pairs={{0,4},{1,5},{2,6},{3,7},{4,0},{5,1},{6,2},{7,3},{8,12},{9,13},{10,... | collective-permute-start | bytes 110600 | tf_op jit(solution)/shard_map/ppermute | solution.py:282
  (15 other events, 79.4 us)

commit v3 on v2

--- a/solution.py
+++ b/solution.py
@@ -11,7 +11,7 @@
 LANES = 128
 SIDE = 8
 REACH = 7
-PAYLOAD_ROWS = 144
+KEY_ROWS = 16
 F32 = jnp.float32
 BF16 = jnp.bfloat16
 
@@ -51,7 +51,7 @@
     return across == along
 
 
-def front(x_ref, weights, outs, scratch, halo, tile, head_dim):
+def front(x_ref, weights, outs, scratch, halo, tile, head_dim, section):
     expand, expand_bias, depth, depth_bias, project, project_bias, qkv_weight, agg, group = weights
     mixed_out, query_out, payload_out = outs
     hidden, spread, total, mixed, qkv, scaled = scratch
@@ -64,7 +64,7 @@
     def expanded(step, carry):
         at = pl.multiple_of(step * chunk, chunk)
         value = jnp.dot(x, expand[0, :, pl.ds(at, chunk)], preferred_element_type=F32)
-        value = hard_swish(value + expand_bias[:, pl.ds(at, chunk)])
+        value = hard_swish(value + expand_bias[section : section + 1, pl.ds(at, chunk)])
         hidden[...] = value.reshape(rows, width, chunk)
         clear_outside(hidden, halo, tile_cols)
 
@@ -73,13 +73,13 @@
                 here = pl.ds(pl.multiple_of(at + lane, LANES), LANES)
                 above, level, below = (hidden[r + a, :, lane : lane + LANES] for a in range(3))
                 parts = [
-                    above * depth[0, 0, b : b + 1, here]
-                    + level * depth[0, 1, b : b + 1, here]
-                    + below * depth[0, 2, b : b + 1, here]
+                    above * depth[0, b, section : section + 1, here]
+                    + level * depth[1, b, section : section + 1, here]
+                    + below * depth[2, b, section : section + 1, here]
                     for b in range(3)
                 ]
                 value = parts[1] + pltpu.roll(parts[0], 1, 0) + pltpu.roll(parts[2], width - 1, 0)
-                value = hard_swish(value + depth_bias[:, here])
+                value = hard_swish(value + depth_bias[section : section + 1, here])
                 spread[r, :, lane : lane + LANES] = value.astype(BF16)
             return carry
 
@@ -99,10 +99,10 @@
         return carry
 
     lax.fori_loop(0, expand.shape[2] // chunk, expanded, 0)
-    value = total[...] + project_bias[...] + flat(x_ref[1 : rows - 1]).astype(F32)
+    value = total[...] + project_bias[section : section + 1, :] + flat(x_ref[1 : rows - 1]).astype(F32)
     mixed[...] = value.astype(BF16).reshape(inner, width, channels)
     mixed_out[...] = mixed[2 : inner - 2]
-    value = jnp.dot(flat(mixed[...]), qkv_weight[...], preferred_element_type=F32)
+    value = jnp.dot(flat(mixed[...]), qkv_weight[section], preferred_element_type=F32)
     qkv[...] = value.reshape(inner, width, 3 * channels)
     around = halo - 1
     clear_outside(qkv, around, tile_cols)
@@ -115,7 +115,7 @@
                 for b in range(5):
                     part = None
                     for a in range(5):
-                        term = qkv[first + r + a, :, here] * agg[5 * a + b : 5 * a + b + 1, here]
+                        term = qkv[first + r + a, :, here] * agg[tap(section, a, b), here]
                         part = term if part is None else part + term
                     if b != 2:
                         part = pltpu.roll(part, (2 - b) % width, 0)
@@ -124,7 +124,7 @@
             return carry
 
         lax.fori_loop(0, count, one_row, 0)
-        value = jnp.dot(flat(scaled[0:count]), group[kind], preferred_element_type=F32)
+        value = jnp.dot(flat(scaled[0:count]), group[section, kind], preferred_element_type=F32)
         return value.reshape(count, width, channels)
 
     outer = inner - 4
@@ -144,7 +144,7 @@
     ]
     same = same_head(head_dim)
     summary = jnp.zeros((LANES, LANES), F32)
-    payload_out[LANES:PAYLOAD_ROWS, :] = jnp.zeros((PAYLOAD_ROWS - LANES, LANES), F32)
+    key_sums = []
     index = 0
     for key, value in zip(keys, values):
         key = jnp.maximum(key, 0.0)
@@ -159,12 +159,19 @@
             if index:
                 product = pltpu.roll(product, index * head_dim, 1)
             summary = summary + product
-            payload_out[LANES + index : LANES + index + 1, :] = sums[:, here]
+            key_sums.append(sums[:, here])
             index += 1
-    payload_out[0:LANES, :] = summary
-
-
-def attend(mixed_ref, query_ref, payload_ref, weight, bias, head_dim):
+    key_sums = jnp.concatenate(
+        key_sums + [jnp.zeros((KEY_ROWS - index, LANES), F32)], axis=0
+    )
+    payload_out[0:LANES, :] = summary.astype(BF16)
+    payload_out[LANES : LANES + KEY_ROWS, :] = key_sums.astype(BF16)
+    rest = payload_out.shape[0] - LANES - KEY_ROWS
+    if rest:
+        payload_out[LANES + KEY_ROWS :, :] = jnp.zeros((rest, LANES), BF16)
+
+
+def attend(mixed_ref, query_ref, payload_ref, weight, bias, head_dim, section):
     query = flat(query_ref[...])
     same = same_head(head_dim)
     square = (LANES, LANES)
@@ -172,12 +179,15 @@
         jnp.int32, square, 1
     )
     ones = jnp.where(same, 1.0, 0.0).astype(BF16)
-    packed = payload_ref[0:LANES, :]
-    total = flat(mixed_ref[...]).astype(F32) + bias[...]
+    payload = payload_ref[0].astype(F32)
+    for part in range(1, payload_ref.shape[0]):
+        payload = payload + payload_ref[part].astype(F32)
+    packed = payload[0:LANES]
+    total = flat(mixed_ref[...]).astype(F32) + bias[section : section + 1, :]
     for index in range(query.shape[1] // LANES):
         summary = packed if index == 0 else pltpu.roll(packed, LANES - index * head_dim, 1)
         summary = jnp.where(same, summary, 0.0).astype(BF16)
-        sums = payload_ref[LANES + index : LANES + index + 1, :]
+        sums = payload[LANES + index : LANES + index + 1]
         sums = jnp.where(diagonal, sums, 0.0).astype(BF16)
         sums = jnp.dot(sums, ones, preferred_element_type=F32).astype(BF16)
         part = query[:, index * LANES : (index + 1) * LANES]
@@ -190,6 +200,57 @@
     return total
 
 
+def tap(section, a, b):
+    at = 32 * section + 5 * a + b
+    return slice(at, at + 1)
+
+
+def prepare_kernel(head_dim, qkv, agg, group, head, qkv_out, agg_out, group_out, head_out, taps):
+    sections, channels, wide = qkv.shape
+    half = 3 * LANES
+    heads = LANES // head_dim
+    src = lax.broadcasted_iota(jnp.int32, (half, LANES), 0)
+    dst = lax.broadcasted_iota(jnp.int32, (half, LANES), 1)
+    first = (dst // head_dim) * 3 * head_dim + dst % head_dim
+    picks = [jnp.where(src == first + k * head_dim, 1.0, 0.0).astype(BF16) for k in range(3)]
+    taps[...] = jnp.zeros(taps.shape, F32)
+    for section in range(sections):
+        for a in range(5):
+            for b in range(5):
+                taps[tap(section, a, b), :] = agg[a, b, section : section + 1, :]
+    rest = taps[...]
+    high = rest.astype(BF16)
+    rest = rest - high.astype(F32)
+    middle = rest.astype(BF16)
+    low = (rest - middle.astype(F32)).astype(BF16)
+    split = jnp.concatenate([high, middle, low], axis=0)
+    count = taps.shape[0]
+    weights = qkv[...].reshape(sections * channels, wide)
+    for part in range(wide // half):
+        here = slice(part * half, (part + 1) * half)
+        for kind in range(3):
+            to = kind * channels + part * LANES
+            there = slice(to, to + LANES)
+            value = jnp.dot(weights[:, here], picks[kind], preferred_element_type=F32)
+            qkv_out[:, :, there] = value.astype(BF16).reshape(sections, channels, LANES)
+            value = jnp.dot(split[:, here], picks[kind], preferred_element_type=F32)
+            agg_out[:, there] = value[:count] + value[count : 2 * count] + value[2 * count :]
+    row = lax.broadcasted_iota(jnp.int32, (head_dim, channels), 0)
+    lane = lax.broadcasted_iota(jnp.int32, (head_dim, channels), 1)
+    spread = jnp.where(lane % head_dim == row, 1.0, 0.0).astype(BF16)
+    across = lax.broadcasted_iota(jnp.int32, (channels, channels), 0) // head_dim
+    along = lax.broadcasted_iota(jnp.int32, (channels, channels), 1) // head_dim
+    for section in range(sections):
+        for kind in range(3):
+            tall = [group[section, 3 * h + kind] for h in range(channels // head_dim)]
+            value = jnp.dot(jnp.concatenate(tall, axis=0), spread, preferred_element_type=F32)
+            group_out[section, kind] = jnp.where(across == along, value, 0.0).astype(BF16)
+    head_out[...] = jnp.zeros(head_out.shape, BF16)
+    for a in range(3):
+        rows = [head[a, b] for b in range(3)] + [jnp.zeros((4, channels), BF16)]
+        head_out[a, 0:16, :] = jnp.concatenate(rows, axis=0)
+
+
 def first_kernel(tile, head_dim, own, top, bottom, right, left, *refs):
     weights, outs, scratch = refs[:9], refs[9:12], refs[12:]
     x_ref = scratch[0]
@@ -198,15 +259,15 @@
     x_ref[REACH : REACH + rows, 0:cols, :] = own[...]
     x_ref[REACH + rows :, 0:cols, :] = bottom[...]
     x_ref[:, cols : cols + 2 * SIDE, :] = jnp.concatenate([right[...], left[...]], axis=1)
-    front(x_ref, weights, outs, scratch[1:], REACH, tile, head_dim)
+    front(x_ref, weights, outs, scratch[1:], REACH, tile, head_dim, 0)
 
 
 def second_kernel(tile, head_dim, mixed, query, payload, out_weight, out_bias, *refs):
     weights, outs, scratch = refs[:9], refs[9:12], refs[12:]
     x_ref = scratch[0]
-    value = attend(mixed, query, payload, out_weight, out_bias, head_dim)
+    value = attend(mixed, query, payload, out_weight, out_bias, head_dim, 0)
     x_ref[...] = value.astype(BF16).reshape(x_ref.shape)
-    front(x_ref, weights, outs, scratch[1:], REACH - 3, tile, head_dim)
+    front(x_ref, weights, outs, scratch[1:], REACH - 3, tile, head_dim, 1)
 
 
 def last_kernel(
@@ -215,7 +276,7 @@
 ):
     rows, cols = tile
     width = cols + 2 * SIDE
-    value = attend(mixed, query, payload, out_weight, out_bias, head_dim)
+    value = attend(mixed, query, payload, out_weight, out_bias, head_dim, 1)
     x_ref[...] = value.astype(BF16).reshape(x_ref.shape)
     clear_outside(x_ref, 1, cols)
     map_out[...] = x_ref[1 : 1 + rows, 0:cols, :]
@@ -267,22 +328,29 @@
     return radices
 
 
-def sum_by_permutes(value):
-    for axis in ("row", "col"):
-        count = lax.axis_size(axis)
-        stride = 1
-        for radix in digits(count, 4):
-            total = value
-            sent = value.astype(BF16)
-            for step in range(1, radix):
-                pairs = []
-                for i in range(count):
-                    digit = (i // stride) % radix
-                    pairs.append((i, i + ((digit + step) % radix - digit) * stride))
-                total = total + lax.ppermute(sent, axis, pairs).astype(F32)
-            value = total
-            stride *= radix
-    return value
+def exchanged(pieces, axis):
+    return lax.all_to_all(pieces, axis, 0, 0, tiled=True)
+
+
+def copies(value, axis):
+    return jnp.broadcast_to(value[None], (lax.axis_size(axis),) + value.shape)
+
+
+def added(pieces):
+    return jnp.sum(pieces.astype(F32), axis=0).astype(BF16)
+
+
+def sum_whole(payload):
+    payload = added(exchanged(copies(payload, "row"), "row"))
+    return exchanged(copies(payload, "col"), "col")
+
+
+def sum_in_shares(payload):
+    count = lax.axis_size("row")
+    pieces = exchanged(payload.reshape(count, -1, LANES), "row")
+    pieces = exchanged(copies(added(pieces), "col"), "col")
+    pieces = exchanged(copies(added(pieces), "row"), "row")
+    return pieces.reshape(1, -1, LANES)
 
 
 def shift(value, axis, step):
@@ -321,36 +389,43 @@
     column = jnp.concatenate([top[:, :SIDE], features[:, :SIDE], bottom[:, :SIDE]], axis=0)
     right = shift(column, "col", -1)
 
-    def by_kind(array, axis):
-        shape = array.shape[:axis] + (heads, 3, head_dim) + array.shape[axis + 1 :]
-        return jnp.swapaxes(array.reshape(shape), axis, axis + 1).reshape(array.shape)
-
-    qkv_weight = by_kind(qkv_weight, 2)
-    aggregate_depth = by_kind(aggregate_depth, 3).reshape(SECTIONS, 25, 3 * channels)
-    group = aggregate_group.reshape(SECTIONS, heads, 3, head_dim, head_dim).swapaxes(1, 2)
-    group = (
-        group[:, :, :, :, None, :] * jnp.eye(heads, dtype=BF16)[None, None, :, None, :, None]
-    ).reshape(SECTIONS, 3, channels, channels)
-    head_weight = jnp.pad(
-        head_weight.reshape(3, 12, channels), ((0, 0), (0, LANES - 12), (0, 0))
-    )
+    aggregate_depth = aggregate_depth.transpose(1, 2, 0, 3)
+    depth_weight = depth_weight.transpose(1, 2, 0, 3)
+    params = pltpu.CompilerParams(vmem_limit_bytes=24 * 2**20)
+    qkv_weight, taps, group, head_weight = pl.pallas_call(
+        functools.partial(prepare_kernel, head_dim),
+        out_shape=[
+            jax.ShapeDtypeStruct(qkv_weight.shape, BF16),
+            jax.ShapeDtypeStruct((32 * SECTIONS, 3 * channels), F32),
+            jax.ShapeDtypeStruct((SECTIONS, 3, channels, channels), BF16),
+            jax.ShapeDtypeStruct((3, LANES, channels), BF16),
+        ],
+        grid=(1,),
+        in_specs=[whole_spec()] * 4,
+        out_specs=[whole_spec()] * 4,
+        scratch_shapes=[pltpu.VMEM((32 * SECTIONS, 3 * channels), F32)],
+        compiler_params=params,
+        cost_estimate=pl.CostEstimate(
+            flops=2 * 10**9, bytes_accessed=4 * 10**6, transcendentals=0
+        ),
+        name="prepare",
+    )(qkv_weight, aggregate_depth, aggregate_group, head_weight)
 
     def weights_of(section):
         arrays = [
-            expand_weight, expand_bias[section : section + 1], depth_weight,
-            depth_bias[section : section + 1], project_weight, project_bias[section : section + 1],
-            qkv_weight[section], aggregate_depth[section], group[section],
+            expand_weight, expand_bias, depth_weight, depth_bias, project_weight, project_bias,
+            qkv_weight, taps, group,
         ]
         specs = [whole_spec()] * 9
-        for index in (0, 2, 4):
+        for index in (0, 4):
             specs[index] = section_spec(arrays[index], section)
         return arrays, specs
 
-    def outs_of(count):
+    def outs_of(count, payload_rows):
         return [
             jax.ShapeDtypeStruct((count, width, channels), BF16),
             jax.ShapeDtypeStruct((count, width, 2 * channels), BF16),
-            jax.ShapeDtypeStruct((PAYLOAD_ROWS, LANES), F32),
+            jax.ShapeDtypeStruct((payload_rows, LANES), BF16),
         ]
 
     def scratch_of(count):
@@ -364,12 +439,13 @@
             pltpu.VMEM((count - 6, width, channels), BF16),
         ]
 
-    params = pltpu.CompilerParams(vmem_limit_bytes=40 * 2**20)
+    shares = lax.axis_size("row")
+    share_rows = -(-(LANES + KEY_ROWS) // (16 * shares)) * 16
     first_rows = rows + 2 * REACH
     arrays, specs = weights_of(0)
     mixed, query, payload = pl.pallas_call(
         functools.partial(first_kernel, tile, head_dim),
-        out_shape=outs_of(first_rows - 6),
+        out_shape=outs_of(first_rows - 6, LANES + KEY_ROWS),
         grid=(1,),
         in_specs=[whole_spec()] * 5 + specs,
         out_specs=[whole_spec()] * 3,
@@ -377,21 +453,21 @@
         compiler_params=params,
         name="first",
     )(features, top, bottom, right, left, *arrays)
-    payload = sum_by_permutes(payload)
+    payload = sum_whole(payload)
 
     second_rows = first_rows - 6
     arrays, specs = weights_of(1)
     mixed, query, payload = pl.pallas_call(
         functools.partial(second_kernel, tile, head_dim),
-        out_shape=outs_of(second_rows - 6),
+        out_shape=outs_of(second_rows - 6, share_rows * shares),
         grid=(1,),
         in_specs=[whole_spec()] * 3 + [section_spec(output_weight, 0), whole_spec()] + specs,
         out_specs=[whole_spec()] * 3,
         scratch_shapes=scratch_of(second_rows),
         compiler_params=params,
         name="second",
-    )(mixed, query, payload, output_weight, output_bias[0:1], *arrays)
-    payload = sum_by_permutes(payload)
+    )(mixed, query, payload, output_weight, output_bias, *arrays)
+    payload = sum_in_shares(payload)
 
     return pl.pallas_call(
         functools.partial(last_kernel, tile, head_dim),
@@ -406,7 +482,7 @@
         compiler_params=params,
         name="last",
     )(
-        mixed, query, payload, output_weight, output_bias[1:2], head_weight, head_bias.reshape(4, 1)
+        mixed, query, payload, output_weight, output_bias, head_weight, head_bias.reshape(4, 1)
     )
 
 

time: 110 us -> 107 us (0.973)
  blocking collectives: 0 us -> 41.8 us
  starting transfers between devices: 31 us -> 11.8 us
  local copies, waits for them, and re-layouts: 29.5 us -> 12.1 us
  other arithmetic: 5.05 us -> 0.99 us
  waiting for transfers between devices: 13.3 us -> 10 us
    all_to_all x0 -> x4, blocking collectives: none -> 41.8 us  [exchanged(): return lax.all_to_all(pieces, axis, 0, 0, tiled=True)]
    ppermute x14 -> x0, starting transfers between devices: 21.1 us -> none  [sum_by_permutes(): total = total + lax.ppermute(sent, axis, pairs).astype(F32)]
    ppermute x14 -> x0, waiting for transfers between devices: 13.3 us -> none  [sum_by_permutes(): total = total + lax.ppermute(sent, axis, pairs).astype(F32)]
    squeeze x6 -> x0, local copies, waits for them, and re-layouts: 9.94 us -> none  [the longest x2 4.73 us: weights_of(): group[section]]
    slice x10 -> x0, local copies, waits for them, and re-layouts: 9.93 us -> none  [the longest x3 4.54 us: weights_of(): aggregate_depth[section]]
    ppermute x4, waiting for transfers between devices: 0.01 us -> 6.75 us  [shift(): return lax.ppermute(value, axis, pairs)]
    all_to_all x0 -> x1, starting transfers between devices: none -> 3.27 us  [exchanged(): return lax.all_to_all(pieces, axis, 0, 0, tiled=True)]
    all_to_all x0 -> x1, waiting for transfers between devices: none -> 3.25 us  [exchanged(): return lax.all_to_all(pieces, axis, 0, 0, tiled=True)]
  transfers between devices with their start and end apart: 18 -> 5, of which waited for: 10 -> 3; matrix products, arithmetic and copies ran while one was open for 23% -> 0% of each run, Pallas kernels for 0% -> 1%
where the time goes in v3:
time: 107 us; the launch traced here: 106 us
  blocking collectives  41.8 us (39%)
  Pallas kernels  28.9 us (27%)
  local copies, waits for them, and re-layouts  12.1 us (11%)
  starting transfers between devices  11.8 us (11%)
  waiting for transfers between devices  10 us (9%)
    all_to_all x4, blocking collectives, exchanged(): return lax.all_to_all(pieces, axis, 0, 0, tiled=True)  41.8 us
    pallas_call x1, Pallas kernels, local(): pl.pallas_call(functools.partial(first_kernel, tile, head_dim), out_shape...  13.4 us
    pallas_call x1, Pallas kernels, local(): pl.pallas_call(functools.partial(second_kernel, tile, head_dim), out_shap...  11.7 us
    unnamed x56, local copies, waits for them, and re-layouts  10.2 us
    ppermute x4, starting transfers between devices, shift(): return lax.ppermute(value, axis, pairs)  8.51 us
    ppermute x4, waiting for transfers between devices, shift(): return lax.ppermute(value, axis, pairs)  6.75 us
    all_to_all x1, starting transfers between devices, exchanged(): return lax.all_to_all(pieces, axis, 0, 0, tiled=True)  3.27 us
    all_to_all x1, waiting for transfers between devices, exchanged(): return lax.all_to_all(pieces, axis, 0, 0, tiled=True)  3.25 us
  transfers between devices with their start and end apart: 5, of which 3 were waited for; matrix products, arithmetic and copies ran while one was open for 0% of the time, Pallas kernels for 1%

profile of v3, /device:TPU:0, one launch (start us, length us, event | category | flops | bytes accessed | tf_op | source)
XLA Modules:
  0.0 106.5 jit_solution(17006471876410084957)
XLA Ops:
  0.6 1.0 fusion.1
  1.7 2.4 %collective-permute-start = (bf16[7,32,256]{2,1,0:T(8,128)(2,1)S(1)}, bf16[7,32,256]{2,1,0:T(8,128)(2,1)S(1)}, u32[]{:S(2)}, u32[]{:S(2)}) collective-permute-start(bf16[7,32,256]{2,1,0:T(8,128)(2,1)S(1)} %get-tuple-element.25), channel_id=1, source_target_pairs={{0,8},{8,16},{16,24},{1,9},{9,17},{17,25},{2,10},{10,18},{18,26},{... | collective-permute-start | bytes 344072 | tf_op jit(solution)/shard_map/ppermute | solution.py:359
  4.1 1.3 %collective-permute-start.1 = (bf16[7,32,256]{2,1,0:T(8,128)(2,1)S(1)}, bf16[7,32,256]{2,1,0:T(8,128)(2,1)S(1)}, u32[]{:S(2)}, u32[]{:S(2)}) collective-permute-start(bf16[7,32,256]{2,1,0:T(8,128)(2,1)S(1)} %get-tuple-element.24), channel_id=1, source_target_pairs={{8,0},{16,8},{24,16},{9,1},{17,9},{25,17},{10,2},{18,10},{26,18},{... | collective-permute-start | bytes 344072 | tf_op jit(solution)/shard_map/ppermute | solution.py:359
  5.4 4.0 %collective-permute-done.1.bottom = bf16[7,32,256]{2,1,0:T(8,128)(2,1)S(1)} collective-permute-done((bf16[7,32,256]{2,1,0:T(8,128)(2,1)S(1)}, bf16[7,32,256]{2,1,0:T(8,128)(2,1)S(1)}, u32[]{:S(2)}, u32[]{:S(2)}) %collective-permute-start.1) | collective-permute-done | bytes 114720 | tf_op jit(solution)/shard_map/ppermute | solution.py:359
  9.4 3.6 %collective-permute-start.3 = (bf16[22,8,256]{2,1,0:T(8,128)(2,1)S(1)}, bf16[22,8,256]{2,1,0:T(8,128)(2,1)S(1)}, u32[]{:S(2)}, u32[]{:S(2)}) collective-permute-start(bf16[22,8,256]{2,1,0:T(8,128)(2,1)S(1)} %pad_maximum_fusion.1), channel_id=1, source_target_pairs={{0,1},{1,2},{2,3},{3,4},{4,5},{5,6},{6,7},{8,9},{9,10},{10,11},{11... | collective-permute-start | bytes 270344 | tf_op jit(solution)/shard_map/ppermute | solution.py:359
  13.0 1.3 %collective-permute-start.2 = (bf16[22,8,256]{2,1,0:T(8,128)(2,1)S(1)}, bf16[22,8,256]{2,1,0:T(8,128)(2,1)S(1)}, u32[]{:S(2)}, u32[]{:S(2)}) collective-permute-start(bf16[22,8,256]{2,1,0:T(8,128)(2,1)S(1)} %pad_maximum_fusion), channel_id=1, source_target_pairs={{1,0},{2,1},{3,2},{4,3},{5,4},{6,5},{7,6},{9,8},{10,9},{11,10},{12... | collective-permute-start | bytes 270344 | tf_op jit(solution)/shard_map/ppermute | solution.py:359
  14.4 1.0 copy-done.24
  15.4 1.2 %prepare.1 = (bf16[2,256,768]{2,1,0:T(8,128)(2,1)S(1)}, f32[64,768]{1,0:T(8,128)S(1)}, bf16[2,3,256,256]{3,2,1,0:T(8,128)(2,1)S(1)}, bf16[3,128,256]{2,1,0:T(8,128)(2,1)S(1)}) custom-call(bf16[2,256,768]{2,1,0:T(8,128)(2,1)S(1)} %copy-done.23, f32[5,5,2,768]{3,2,1,0:T(2,128)S(1)} %bitcast.9, bf16[2,24,32,32]{3,2,1,0:T(8,128)(2,1)S(1)} %copy-done.24, ...), custom_call_target="tpu_custom_call" | custom-call | flops 2000000000 | bytes 4000000 | tf_op jit(solution)/shard_map/prepare/pallas_call | solution.py:395
  16.7 2.8 %collective-permute-done.2.right = bf16[22,8,256]{2,1,0:T(8,128)(2,1)S(1)} collective-permute-done((bf16[22,8,256]{2,1,0:T(8,128)(2,1)S(1)}, bf16[22,8,256]{2,1,0:T(8,128)(2,1)S(1)}, u32[]{:S(2)}, u32[]{:S(2)}) %collective-permute-start.2) | collective-permute-done | bytes 90144 | tf_op jit(solution)/shard_map/ppermute | solution.py:359
  20.1 13.4 %first.1 = (bf16[16,48,256]{2,1,0:T(8,128)(2,1)S(1)}, bf16[16,48,512]{2,1,0:T(8,128)(2,1)S(1)}, bf16[144,128]{1,0:T(8,128)(2,1)S(1)}) custom-call(bf16[8,32,256]{2,1,0:T(8,128)(2,1)S(1)} %copy-done.5, bf16[7,32,256]{2,1,0:T(8,128)(2,1)S(1)} %collective-permute-done.top, bf16[7,32,256]{2,1,0:T(8,128)(2,1)S(1)} %collective-permute-done.1.bottom, ...), custom_call_target="tpu_custom_call" | custom-call | tf_op jit(solution)/shard_map/first/pallas_call | solution.py:446
  33.5 0.9 copy-done.8
  35.2 9.2 %all_to_all.25 = bf16[4,144,128]{2,1,0:T(8,128)(2,1)} all-to-all(bf16[4,144,128]{2,1,0:T(8,128)(2,1)S(1)} %broadcast_in_dim.8), channel_id=1, replica_groups=mesh['row'=4,'col'=8] {'row'}, dimensions={0} | all-to-all | bytes 294912 | tf_op jit(solution)/shard_map/all_to_all | solution.py:332
  44.5 0.9 reduce_sum.36
  45.4 16.1 %all_to_all.26.payload = bf16[8,144,128]{2,1,0:T(8,128)(2,1)S(1)} all-to-all(bf16[8,144,128]{2,1,0:T(8,128)(2,1)S(1)} %broadcast_in_dim.9), channel_id=1, replica_groups=mesh['row'=4,'col'=8] {'col'}, dimensions={0} | all-to-all | bytes 589824 | tf_op jit(solution)/shard_map/all_to_all | solution.py:332
  62.2 0.9 copy-done.7
  63.2 1.1 %copy-done.9 = bf16[16,48,512]{2,1,0:T(8,128)(2,1)S(1)} copy-done((bf16[16,48,512]{2,1,0:T(8,128)(2,1)S(1)}, bf16[16,48,512]{2,1,0:T(8,128)(2,1)}, u32[]{:S(2)}) %copy-start.9) | copy-done | bytes 786456
  64.3 1.0 copy-done.13
  65.3 11.7 %second.1 = (bf16[10,48,256]{2,1,0:T(8,128)(2,1)S(1)}, bf16[10,48,512]{2,1,0:T(8,128)(2,1)S(1)}, bf16[192,128]{1,0:T(8,128)(2,1)S(1)}) custom-call(bf16[16,48,256]{2,1,0:T(8,128)(2,1)S(1)} %copy-done.13, bf16[16,48,512]{2,1,0:T(8,128)(2,1)S(1)} %copy-done.9, bf16[8,144,128]{2,1,0:T(8,128)(2,1)S(1)} %all_to_all.26.payload, ...), custom_call_target="tpu_custom_call" | custom-call | tf_op jit(solution)/shard_map/second/pallas_call | solution.py:460
  78.5 6.5 %all_to_all.27 = bf16[4,48,128]{2,1,0:T(8,128)(2,1)S(1)} all-to-all(bf16[4,48,128]{2,1,0:T(8,128)(2,1)S(1)} %bitcast.8), channel_id=1, replica_groups=mesh['row'=4,'col'=8] {'row'}, dimensions={0} | all-to-all | bytes 98304 | tf_op jit(solution)/shard_map/all_to_all | solution.py:332
  85.0 9.9 %all_to_all.28 = bf16[8,48,128]{2,1,0:T(8,128)(2,1)S(1)} all-to-all(bf16[8,48,128]{2,1,0:T(8,128)(2,1)S(1)} %broadcast_in_dim.10), channel_id=1, replica_groups=mesh['row'=4,'col'=8] {'col'}, dimensions={0} | all-to-all | bytes 196608 | tf_op jit(solution)/shard_map/all_to_all | solution.py:332
  95.6 3.3 %all-to-all-start.4 = ((bf16[4,48,128]{2,1,0:T(8,128)(2,1)}), bf16[4,48,128]{2,1,0:T(8,128)(2,1)S(1)}, u32[]{:S(2)}, u32[]{:S(2)}) async-start(bf16[4,48,128]{2,1,0:T(8,128)(2,1)} %broadcast_in_dim.11), calls=%async_computation.4 | async-start | bytes 98304 | tf_op jit(solution)/shard_map/all_to_all | solution.py:332
  99.6 3.2 %all-to-all-done.4 = bf16[4,48,128]{2,1,0:T(8,128)(2,1)S(1)} async-done(((bf16[4,48,128]{2,1,0:T(8,128)(2,1)}), bf16[4,48,128]{2,1,0:T(8,128)(2,1)S(1)}, u32[]{:S(2)}, u32[]{:S(2)}) %all-to-all-start.4) | async-done | bytes 49184 | tf_op jit(solution)/shard_map/all_to_all | solution.py:332
  102.9 0.9 copy-done.18
  103.8 2.7 %last.1 = (bf16[8,32,256]{2,1,0:T(8,128)(2,1)}, f32[4,8,32]{2,1,0:T(8,128)}) custom-call(bf16[10,48,256]{2,1,0:T(8,128)(2,1)S(1)} %copy-done.16, bf16[10,48,512]{2,1,0:T(8,128)(2,1)S(1)} %copy-done.11, bf16[1,192,128]{2,1,0:T(8,128)(2,1)S(1)} %bitcast.7, bf16[2,512,256]{2,1,0:T(8,128)(2,1)S(1)} %copy-done.4, f32[2,256]{1,0:T(2,128)S(1)} %copy-done.22, ...), custom_call_target="tpu_custom_call" | custom-call | tf_op jit(solution)/shard_map/last/pallas_call | solution.py:472
  (64 shorter events, 5.2 us)
Async XLA Ops:
  0.6 4.7 %copy-start.5 = (bf16[8,32,256]{2,1,0:T(8,128)(2,1)S(1)}, bf16[8,32,256]{2,1,0:T(8,128)(2,1)}, u32[]{:S(2)}) copy-start(bf16[8,32,256]{2,1,0:T(8,128)(2,1)} %own.1) | copy-start | bytes 393220
  0.6 13.7 %copy-start.23 = (bf16[2,256,768]{2,1,0:T(8,128)(2,1)S(1)}, bf16[2,256,768]{2,1,0:T(8,128)(2,1)}, u32[]{:S(2)}) copy-start(bf16[2,256,768]{2,1,0:T(8,128)(2,1)} %qkv.1) | copy-start | bytes 2359300
  1.7 3.7 %collective-permute-start = (bf16[7,32,256]{2,1,0:T(8,128)(2,1)S(1)}, bf16[7,32,256]{2,1,0:T(8,128)(2,1)S(1)}, u32[]{:S(2)}, u32[]{:S(2)}) collective-permute-start(bf16[7,32,256]{2,1,0:T(8,128)(2,1)S(1)} %get-tuple-element.25), channel_id=1, source_target_pairs={{0,8},{8,16},{16,24},{1,9},{9,17},{17,25},{2,10},{10,18},{18,26},{... | collective-permute-start | bytes 344072 | tf_op jit(solution)/shard_map/ppermute | solution.py:359
  4.1 5.3 %collective-permute-start.1 = (bf16[7,32,256]{2,1,0:T(8,128)(2,1)S(1)}, bf16[7,32,256]{2,1,0:T(8,128)(2,1)S(1)}, u32[]{:S(2)}, u32[]{:S(2)}) collective-permute-start(bf16[7,32,256]{2,1,0:T(8,128)(2,1)S(1)} %get-tuple-element.24), channel_id=1, source_target_pairs={{8,0},{16,8},{24,16},{9,1},{17,9},{25,17},{10,2},{18,10},{26,18},{... | collective-permute-start | bytes 344072 | tf_op jit(solution)/shard_map/ppermute | solution.py:359
  9.4 4.9 %copy-start.25 = (f32[2,5,5,768]{3,0,2,1:T(2,128)S(1)}, f32[2,5,5,768]{3,0,2,1:T(2,128)}, u32[]{:S(2)}) copy-start(f32[2,5,5,768]{3,0,2,1:T(2,128)} %param.22) | copy-start | bytes 460804
  9.4 7.2 %collective-permute-start.3 = (bf16[22,8,256]{2,1,0:T(8,128)(2,1)S(1)}, bf16[22,8,256]{2,1,0:T(8,128)(2,1)S(1)}, u32[]{:S(2)}, u32[]{:S(2)}) collective-permute-start(bf16[22,8,256]{2,1,0:T(8,128)(2,1)S(1)} %pad_maximum_fusion.1), channel_id=1, source_target_pairs={{0,1},{1,2},{2,3},{3,4},{4,5},{5,6},{6,7},{8,9},{9,10},{10,11},{11... | collective-permute-start | bytes 270344 | tf_op jit(solution)/shard_map/ppermute | solution.py:359
  13.0 1.4 %copy-start.26 = (bf16[3,3,4,256]{3,2,1,0:T(4,128)(2,1)S(1)}, bf16[3,3,4,256]{3,2,1,0:T(4,128)(2,1)}, u32[]{:S(2)}) copy-start(bf16[3,3,4,256]{3,2,1,0:T(4,128)(2,1)} %head.1) | copy-start | bytes 55300
  13.0 6.4 %collective-permute-start.2 = (bf16[22,8,256]{2,1,0:T(8,128)(2,1)S(1)}, bf16[22,8,256]{2,1,0:T(8,128)(2,1)S(1)}, u32[]{:S(2)}, u32[]{:S(2)}) collective-permute-start(bf16[22,8,256]{2,1,0:T(8,128)(2,1)S(1)} %pad_maximum_fusion), channel_id=1, source_target_pairs={{1,0},{2,1},{3,2},{4,3},{5,4},{6,5},{7,6},{9,8},{10,9},{11,10},{12... | collective-permute-start | bytes 270344 | tf_op jit(solution)/shard_map/ppermute | solution.py:359
  14.3 1.0 copy-start.24
  15.3 4.1 %copy-start = (bf16[2,256,1024]{2,1,0:T(8,128)(2,1)S(1)}, bf16[2,256,1024]{2,1,0:T(8,128)(2,1)}, u32[]{:S(2)}) copy-start(bf16[2,256,1024]{2,1,0:T(8,128)(2,1)} %refs_0_.3) | copy-start | bytes 3145732
  15.3 4.1 %copy-start.1 = (bf16[2,1024,256]{2,1,0:T(8,128)(2,1)S(1)}, bf16[2,1024,256]{2,1,0:T(8,128)(2,1)}, u32[]{:S(2)}) copy-start(bf16[2,1024,256]{2,1,0:T(8,128)(2,1)} %refs_4_.3) | copy-start | bytes 3145732
  15.4 4.1 %copy-start.14 = (f32[2,3,3,1024]{3,0,2,1:T(2,128)S(1)}, f32[2,3,3,1024]{3,0,2,1:T(2,128)}, u32[]{:S(2)}) copy-start(f32[2,3,3,1024]{3,0,2,1:T(2,128)} %param.17) | copy-start | bytes 221188
  15.4 4.1 %copy-start.19 = (f32[2,1024]{1,0:T(2,128)S(1)}, f32[2,1024]{1,0:T(2,128)}, u32[]{:S(2)}) copy-start(f32[2,1024]{1,0:T(2,128)} %refs_1_.3) | copy-start | bytes 24580
  15.4 4.1 %copy-start.20 = (f32[2,1024]{1,0:T(2,128)S(1)}, f32[2,1024]{1,0:T(2,128)}, u32[]{:S(2)}) copy-start(f32[2,1024]{1,0:T(2,128)} %refs_3_.3) | copy-start | bytes 24580
  16.6 16.9 %copy-start.2 = (bf16[2,3,256,256]{3,2,1,0:T(8,128)(2,1)}, bf16[2,3,256,256]{3,2,1,0:T(8,128)(2,1)S(1)}, u32[]{:S(2)}) copy-start(bf16[2,3,256,256]{3,2,1,0:T(8,128)(2,1)S(1)} %get-tuple-element.14.refs_8_) | copy-start | bytes 2359300
  16.6 16.9 %copy-start.6 = (f32[64,768]{1,0:T(8,128)}, f32[64,768]{1,0:T(8,128)S(1)}, u32[]{:S(2)}) copy-start(f32[64,768]{1,0:T(8,128)S(1)} %get-tuple-element.13.refs_7_) | copy-start | bytes 589828
  16.6 16.9 %copy-start.17 = (bf16[3,128,256]{2,1,0:T(8,128)(2,1)}, bf16[3,128,256]{2,1,0:T(8,128)(2,1)S(1)}, u32[]{:S(2)}) copy-start(bf16[3,128,256]{2,1,0:T(8,128)(2,1)S(1)} %get-tuple-element.21.head_weight) | copy-start | bytes 589828
  35.2 26.3 %copy-start.4 = (bf16[2,512,256]{2,1,0:T(8,128)(2,1)S(1)}, bf16[2,512,256]{2,1,0:T(8,128)(2,1)}, u32[]{:S(2)}) copy-start(bf16[2,512,256]{2,1,0:T(8,128)(2,1)} %out_weight.3) | copy-start | bytes 1572868
  45.4 16.2 %copy-start.3 = (bf16[2,3,256,256]{3,2,1,0:T(8,128)(2,1)S(1)}, bf16[2,3,256,256]{3,2,1,0:T(8,128)(2,1)}, u32[]{:S(2)}) copy-start(bf16[2,3,256,256]{3,2,1,0:T(8,128)(2,1)} %copy-done.2) | copy-start | bytes 2359300
  63.2 1.1 %copy-start.9 = (bf16[16,48,512]{2,1,0:T(8,128)(2,1)S(1)}, bf16[16,48,512]{2,1,0:T(8,128)(2,1)}, u32[]{:S(2)}) copy-start(bf16[16,48,512]{2,1,0:T(8,128)(2,1)} %copy-done.8) | copy-start | bytes 2359300
  64.3 1.0 copy-start.13
  78.5 24.4 %copy-start.11 = (bf16[10,48,512]{2,1,0:T(8,128)(2,1)S(1)}, bf16[10,48,512]{2,1,0:T(8,128)(2,1)}, u32[]{:S(2)}) copy-start(bf16[10,48,512]{2,1,0:T(8,128)(2,1)} %copy-done.10) | copy-start | bytes 1474564
  85.0 17.9 %copy-start.16 = (bf16[10,48,256]{2,1,0:T(8,128)(2,1)S(1)}, bf16[10,48,256]{2,1,0:T(8,128)(2,1)}, u32[]{:S(2)}) copy-start(bf16[10,48,256]{2,1,0:T(8,128)(2,1)} %copy-done.15) | copy-start | bytes 737284
  95.6 7.3 %all-to-all-start.4 = ((bf16[4,48,128]{2,1,0:T(8,128)(2,1)}), bf16[4,48,128]{2,1,0:T(8,128)(2,1)S(1)}, u32[]{:S(2)}, u32[]{:S(2)}) async-start(bf16[4,48,128]{2,1,0:T(8,128)(2,1)} %broadcast_in_dim.11), calls=%async_computation.4 | async-start | bytes 98304 | tf_op jit(solution)/shard_map/all_to_all | solution.py:332
  (9 other events, 7.1 us)

commit v4 on v3

v4 whole, which is shorter than its diff:
```python
import functools

import jax
import jax.numpy as jnp
from jax import lax
from jax.experimental import pallas as pl
from jax.experimental.pallas import tpu as pltpu
from jax.sharding import PartitionSpec as P

SECTIONS = 2
LANES = 128
SIDE = 8
REACH = 7
KEY_ROWS = 16
F32 = jnp.float32
BF16 = jnp.bfloat16


def hard_swish(value):
    return value * jnp.minimum(jnp.maximum(value * (1.0 / 6.0) + 0.5, 0.0), 1.0)


def clear_outside(ref, halo, cols):
    rows = ref.shape[0]
    row, col = lax.axis_index("row"), lax.axis_index("col")

    @pl.when(row == 0)
    def _():
        ref[0:halo] = jnp.zeros((halo,) + ref.shape[1:], ref.dtype)

    @pl.when(row == lax.axis_size("row") - 1)
    def _():
        ref[rows - halo : rows] = jnp.zeros((halo,) + ref.shape[1:], ref.dtype)

    @pl.when(col == 0)
    def _():
        ref[:, cols + SIDE : cols + 2 * SIDE, :] = jnp.zeros((rows, SIDE, ref.shape[2]), ref.dtype)

    @pl.when(col == lax.axis_size("col") - 1)
    def _():
        ref[:, cols : cols + SIDE, :] = jnp.zeros((rows, SIDE, ref.shape[2]), ref.dtype)


def grouped_loop(count, most, body):
    size = next(n for n in range(min(most, count), 0, -1) if count % n == 0)

    def group(index, carry):
        for r in range(size):
            body(index * size + r)
        return carry

    lax.fori_loop(0, count // size, group, 0)


def flat(value):
    return value.reshape(-1, value.shape[-1])


def same_head(head_dim):
    across = lax.broadcasted_iota(jnp.int32, (LANES, LANES), 0) // head_dim
    along = lax.broadcasted_iota(jnp.int32, (LANES, LANES), 1) // head_dim
    return across == along


def front(x_ref, weights, outs, scratch, halo, tile, head_dim, section):
    expand, expand_bias, depth, depth_bias, project, project_bias = weights[:6]
    mixed_out, query_out, payload_out = outs
    hidden, spread, total, mixed, qkv, scaled, query, qkv_weight, agg, group, sems = scratch
    loads = [
        pltpu.make_async_copy(weights[6].at[section], qkv_weight, sems.at[0]),
        pltpu.make_async_copy(weights[7].at[section], agg, sems.at[1]),
        pltpu.make_async_copy(weights[8].at[section], group, sems.at[2]),
    ]
    for load in loads:
        load.start()
    rows, width, channels = x_ref.shape
    tile_rows, tile_cols = tile
    inner = rows - 2
    chunk = hidden.shape[2]
    x = flat(x_ref[...])

    def expanded(step, carry):
        at = pl.multiple_of(step * chunk, chunk)
        value = jnp.dot(x, expand[section, :, pl.ds(at, chunk)], preferred_element_type=F32)
        value = hard_swish(value + expand_bias[section : section + 1, pl.ds(at, chunk)])
        hidden[...] = value.reshape(rows, width, chunk)
        clear_outside(hidden, halo, tile_cols)

        def one_row(r):
            for lane in range(0, chunk, LANES):
                here = pl.ds(pl.multiple_of(at + lane, LANES), LANES)
                above, level, below = (hidden[r + a, :, lane : lane + LANES] for a in range(3))
                parts = [
                    above * depth[0, b, section : section + 1, here]
                    + level * depth[1, b, section : section + 1, here]
                    + below * depth[2, b, section : section + 1, here]
                    for b in range(3)
                ]
                value = parts[1] + pltpu.roll(parts[0], 1, 0) + pltpu.roll(parts[2], width - 1, 0)
                value = hard_swish(value + depth_bias[section : section + 1, here])
                spread[r, :, lane : lane + LANES] = value.astype(BF16)

        grouped_loop(inner, 7, one_row)
        product = jnp.dot(
            flat(spread[...]), project[section, pl.ds(at, chunk), :], preferred_element_type=F32
        )

        @pl.when(step == 0)
        def _():
            total[...] = product

        @pl.when(step > 0)
        def _():
            total[...] += product

        return carry

    lax.fori_loop(0, expand.shape[2] // chunk, expanded, 0)
    value = total[...] + project_bias[section : section + 1, :] + flat(x_ref[1 : rows - 1]).astype(F32)
    mixed[...] = value.astype(BF16).reshape(inner, width, channels)
    outer = inner - 4
    stores = [
        pltpu.make_async_copy(mixed.at[pl.ds(2, outer)], mixed_out, sems.at[3]),
        pltpu.make_async_copy(query, query_out, sems.at[4]),
    ]
    stores[0].start()
    for load in loads:
        load.wait()
    value = jnp.dot(flat(mixed[...]), qkv_weight[...], preferred_element_type=F32)
    qkv[...] = value.reshape(inner, width, 3 * channels)
    around = halo - 1
    clear_outside(qkv, around, tile_cols)

    def aggregated(kind, first, count):
        def one_row(r):
            for lane in range(0, channels, LANES):
                here = slice(kind * channels + lane, kind * channels + lane + LANES)
                value = None
                for b in range(5):
                    part = None
                    for a in range(5):
                        term = qkv[first + r + a, :, here] * agg[5 * a + b : 5 * a + b + 1, here]
                        part = term if part is None else part + term
                    if b != 2:
                        part = pltpu.roll(part, (2 - b) % width, 0)
                    value = part if value is None else value + part
                scaled[r, :, lane : lane + LANES] = value.astype(BF16)

        grouped_loop(count, 5, one_row)
        value = jnp.dot(flat(scaled[0:count]), group[kind], preferred_element_type=F32)
        return value.reshape(count, width, channels)

    query[:, :, 0:channels] = jnp.maximum(qkv[2 : inner - 2, :, 0:channels], 0.0).astype(BF16)
    query[:, :, channels : 2 * channels] = jnp.maximum(
        aggregated(0, 0, outer), 0.0
    ).astype(BF16)

    stores[1].start()

    def own(value):
        return flat(value[:, 0:tile_cols, :])

    mine = slice(around, around + tile_rows)
    keys = [own(qkv[mine, :, channels : 2 * channels]), own(aggregated(1, around - 2, tile_rows))]
    values = [
        own(qkv[mine, :, 2 * channels : 3 * channels]),
        own(aggregated(2, around - 2, tile_rows)),
    ]
    same = same_head(head_dim)
    summary = jnp.zeros((LANES, LANES), F32)
    key_sums = []
    index = 0
    for key, value in zip(keys, values):
        key = jnp.maximum(key, 0.0)
        sums = jnp.sum(key, axis=0, keepdims=True)
        key, value = key.astype(BF16), value.astype(BF16)
        for lane in range(0, channels, LANES):
            here = slice(lane, lane + LANES)
            product = lax.dot_general(
                key[:, here], value[:, here], (((0,), (0,)), ((), ())), preferred_element_type=F32
            )
            product = jnp.where(same, product, 0.0)
            if index:
                product = pltpu.roll(product, index * head_dim, 1)
            summary = summary + product
            key_sums.append(sums[:, here])
            index += 1
    key_sums = jnp.concatenate(
        key_sums + [jnp.zeros((KEY_ROWS - index, LANES), F32)], axis=0
    )
    payload_out[0:LANES, :] = summary.astype(BF16)
    payload_out[LANES : LANES + KEY_ROWS, :] = key_sums.astype(BF16)
    for store in stores:
        store.wait()


def attend(
    mixed_in, query_in, payloads, weight, bias, mixed_ref, query_ref, sems, head_dim, section
):
    loads = [
        pltpu.make_async_copy(query_in, query_ref, sems.at[0]),
        pltpu.make_async_copy(mixed_in, mixed_ref, sems.at[1]),
    ]
    for load in loads:
        load.start()
    same = same_head(head_dim)
    square = (LANES, LANES)
    diagonal = lax.broadcasted_iota(jnp.int32, square, 0) == lax.broadcasted_iota(
        jnp.int32, square, 1
    )
    ones = jnp.where(same, 1.0, 0.0).astype(BF16)
    payload = payloads[0][...].astype(F32)
    for part in payloads[1:]:
        payload = payload + part[...].astype(F32)
    packed = payload[0:LANES]
    for load in loads:
        load.wait()
    query = flat(query_ref[...])
    total = flat(mixed_ref[...]).astype(F32) + bias[section : section + 1, :]
    for index in range(query.shape[1] // LANES):
        summary = packed if index == 0 else pltpu.roll(packed, LANES - index * head_dim, 1)
        summary = jnp.where(same, summary, 0.0).astype(BF16)
        sums = payload[LANES + index : LANES + index + 1]
        sums = jnp.where(diagonal, sums, 0.0).astype(BF16)
        sums = jnp.dot(sums, ones, preferred_element_type=F32).astype(BF16)
        part = query[:, index * LANES : (index + 1) * LANES]
        numer = jnp.dot(part, summary, preferred_element_type=F32)
        denom = jnp.dot(part, sums, preferred_element_type=F32)
        attended = (numer / (denom + 1e-6)).astype(BF16)
        total = total + jnp.dot(
            attended, weight[section, index * LANES : (index + 1) * LANES, :], preferred_element_type=F32
        )
    return total


def tap(section, a, b):
    at = 32 * section + 5 * a + b
    return slice(at, at + 1)


def prepare_kernel(head_dim, qkv, agg, group, head, *refs):
    outs, made, taps, sems = refs[:4], refs[4:8], refs[8], refs[9]
    qkv_out, agg_out, group_out, head_out = made
    sections, channels, wide = qkv.shape
    half = 3 * LANES
    heads = LANES // head_dim
    src = lax.broadcasted_iota(jnp.int32, (half, LANES), 0)
    dst = lax.broadcasted_iota(jnp.int32, (half, LANES), 1)
    first = (dst // head_dim) * 3 * head_dim + dst % head_dim
    picks = [jnp.where(src == first + k * head_dim, 1.0, 0.0).astype(BF16) for k in range(3)]
    taps[...] = jnp.zeros(taps.shape, F32)
    for section in range(sections):
        for a in range(5):
            for b in range(5):
                taps[tap(section, a, b), :] = agg[a, b, section : section + 1, :]
    rest = taps[...]
    high = rest.astype(BF16)
    rest = rest - high.astype(F32)
    middle = rest.astype(BF16)
    low = (rest - middle.astype(F32)).astype(BF16)
    split = jnp.concatenate([high, middle, low], axis=0)
    count = taps.shape[0]
    weights = qkv[...].reshape(sections * channels, wide)
    for part in range(wide // half):
        here = slice(part * half, (part + 1) * half)
        for kind in range(3):
            to = kind * channels + part * LANES
            there = slice(to, to + LANES)
            value = jnp.dot(weights[:, here], picks[kind], preferred_element_type=F32)
            qkv_out[:, :, there] = value.astype(BF16).reshape(sections, channels, LANES)
            value = jnp.dot(split[:, here], picks[kind], preferred_element_type=F32)
            value = value[:count] + value[count : 2 * count] + value[2 * count :]
            agg_out[:, :, there] = value.reshape(sections, -1, LANES)
    row = lax.broadcasted_iota(jnp.int32, (head_dim, channels), 0)
    lane = lax.broadcasted_iota(jnp.int32, (head_dim, channels), 1)
    spread = jnp.where(lane % head_dim == row, 1.0, 0.0).astype(BF16)
    across = lax.broadcasted_iota(jnp.int32, (channels, channels), 0) // head_dim
    along = lax.broadcasted_iota(jnp.int32, (channels, channels), 1) // head_dim
    for section in range(sections):
        for kind in range(3):
            tall = [group[section, 3 * h + kind] for h in range(channels // head_dim)]
            value = jnp.dot(jnp.concatenate(tall, axis=0), spread, preferred_element_type=F32)
            group_out[section, kind] = jnp.where(across == along, value, 0.0).astype(BF16)
    head_out[...] = jnp.zeros(head_out.shape, BF16)
    for a in range(3):
        rows = [head[a, b] for b in range(3)] + [jnp.zeros((4, channels), BF16)]
        head_out[a, 0:16, :] = jnp.concatenate(rows, axis=0)
    stores = [pltpu.make_async_copy(made[i], outs[i], sems.at[i]) for i in range(4)]
    for store in stores:
        store.start()
    for store in stores:
        store.wait()


def first_kernel(tile, head_dim, own, halos, *refs):
    weights, outs, scratch = refs[:9], refs[9:12], refs[12:]
    x_ref = scratch[0]
    rows, cols = tile
    x_ref[REACH : REACH + rows, 0:cols, :] = own[...]
    for step, at, count in ((-1, 0, REACH), (0, REACH, rows), (1, REACH + rows, REACH)):
        if step:
            x_ref[at : at + count, 0:cols, :] = halos[step, 0][...]
        sides = [halos[step, 1][...], halos[step, -1][...]]
        x_ref[at : at + count, cols : cols + 2 * SIDE, :] = jnp.concatenate(sides, axis=1)
    front(x_ref, weights, outs, scratch[1:], REACH, tile, head_dim, 0)


def second_kernel(tile, head_dim, mixed, query, payload, other, out_weight, out_bias, *refs):
    weights, outs, scratch = refs[:9], refs[9:12], refs[12:]
    x_ref, mixed_ref, query_ref, sems = scratch[:4]
    value = attend(
        mixed, query, (payload, other), out_weight, out_bias, mixed_ref, query_ref, sems, head_dim, 0
    )
    x_ref[...] = value.astype(BF16).reshape(x_ref.shape)
    front(x_ref, weights, outs, scratch[4:], REACH - 3, tile, head_dim, 1)


def last_kernel(
    tile, head_dim, mixed, query, payload, other, out_weight, out_bias, head_weight, head_bias,
    map_out, boxes_out, x_ref, mixed_ref, query_ref, sems,
):
    rows, cols = tile
    width = cols + 2 * SIDE
    value = attend(
        mixed, query, (payload, other), out_weight, out_bias, mixed_ref, query_ref, sems, head_dim, 1
    )
    x_ref[...] = value.astype(BF16).reshape(x_ref.shape)
    clear_outside(x_ref, 1, cols)
    map_out[...] = x_ref[1 : 1 + rows, 0:cols, :]
    total = None
    for a in range(3):
        part = lax.dot_general(
            flat(x_ref[a : a + rows]), head_weight[a], (((1,), (1,)), ((), ())),
            preferred_element_type=F32,
        )
        total = part if total is None else total + part
    total = total.reshape(rows, width, LANES)
    lane = lax.broadcasted_iota(jnp.int32, (width, LANES), 1) // 4
    shifted = [
        jnp.where(
            lane == 0,
            pltpu.roll(total[r], 1, 0),
            jnp.where(lane == 2, pltpu.roll(total[r], width - 1, 0), total[r]),
        )
        for r in range(rows)
    ]
    shifted = jnp.concatenate(shifted, axis=0)
    across = lax.broadcasted_iota(jnp.int32, (8, LANES), 0)
    along = lax.broadcasted_iota(jnp.int32, (8, LANES), 1)
    fold = jnp.where((along % 4 == across) & (along < 12), 1.0, 0.0)
    boxes = lax.dot_general(
        fold, shifted, (((1,), (1,)), ((), ())), precision=lax.Precision.HIGHEST,
        preferred_element_type=F32,
    )
    boxes = boxes[0:4] + head_bias[...]
    for r in range(rows):
        boxes_out[:, r, :] = boxes[:, r * width : r * width + cols]


def near():
    return pl.BlockSpec(memory_space=pltpu.VMEM)


def far():
    return pl.BlockSpec(memory_space=pltpu.HBM)


def digits(size, most):
    radices = []
    while size > 1:
        radix = next((r for r in range(min(most, size), 1, -1) if size % r == 0), size)
        radices.append(radix)
        size //= radix
    return radices


def partner(i, stride, radix, step):
    digit = (i // stride) % radix
    other = digit ^ step if radix & (radix - 1) == 0 else (digit + step) % radix
    return i + (other - digit) * stride


def sum_by_permutes(value):
    rounds = []
    for axis in ("row", "col"):
        stride = 1
        for radix in digits(lax.axis_size(axis), 4):
            rounds.append((axis, stride, radix))
            stride *= radix
    for axis, stride, radix in rounds:
        count = lax.axis_size(axis)
        others = [
            lax.ppermute(value, axis, [(i, partner(i, stride, radix, k)) for i in range(count)])
            for k in range(1, radix)
        ]
        if (axis, stride, radix) == rounds[-1] and radix == 2:
            return value, others[0]
        total = value.astype(F32)
        for other in others:
            total = total + other.astype(F32)
        value = total.astype(BF16)
    return value, jnp.zeros_like(value)


def digits(size, most):
    radices = []
    while size > 1:
        radix = next((r for r in range(min(most, size), 1, -1) if size % r == 0), size)
        radices.append(radix)
        size //= radix
    return radices


def from_neighbour(value, row_step, col_step):
    rows, cols = lax.axis_size("row"), lax.axis_size("col")
    pairs = [
        ((r + row_step) * cols + c + col_step, r * cols + c)
        for r in range(rows)
        for c in range(cols)
        if 0 <= r + row_step < rows and 0 <= c + col_step < cols
    ]
    return lax.ppermute(value, ("row", "col"), pairs)


def local(
    features,
    expand_weight,
    expand_bias,
    depth_weight,
    depth_bias,
    project_weight,
    project_bias,
    qkv_weight,
    aggregate_depth,
    aggregate_group,
    output_weight,
    output_bias,
    head_weight,
    head_bias,
):
    rows, cols, channels = features.shape
    head_dim = aggregate_group.shape[2]
    heads = channels // head_dim
    width = cols + 2 * SIDE
    tile = (rows, cols)
    wide = expand_weight.shape[2]

    row_part = {-1: slice(rows - REACH, rows), 0: slice(0, rows), 1: slice(0, REACH)}
    col_part = {-1: slice(cols - SIDE, cols), 0: slice(0, cols), 1: slice(0, SIDE)}
    halos = {
        (r, c): from_neighbour(features[row_part[r], col_part[c]], r, c)
        for r in (-1, 0, 1)
        for c in (-1, 0, 1)
        if r or c
    }

    aggregate_depth = aggregate_depth.transpose(1, 2, 0, 3)
    depth_weight = depth_weight.transpose(1, 2, 0, 3)
    params = pltpu.CompilerParams(vmem_limit_bytes=24 * 2**20)
    made = [
        jax.ShapeDtypeStruct(qkv_weight.shape, BF16),
        jax.ShapeDtypeStruct((SECTIONS, 32, 3 * channels), F32),
        jax.ShapeDtypeStruct((SECTIONS, 3, channels, channels), BF16),
        jax.ShapeDtypeStruct((3, LANES, channels), BF16),
    ]
    qkv_weight, taps, group, head_weight = pl.pallas_call(
        functools.partial(prepare_kernel, head_dim),
        out_shape=made,
        grid=(1,),
        in_specs=[near()] * 4,
        out_specs=[far()] * 4,
        scratch_shapes=[pltpu.VMEM(array.shape, array.dtype) for array in made]
        + [pltpu.VMEM((32 * SECTIONS, 3 * channels), F32), pltpu.SemaphoreType.DMA((4,))],
        compiler_params=params,
        cost_estimate=pl.CostEstimate(
            flops=2 * 10**9, bytes_accessed=4 * 10**6, transcendentals=0
        ),
        name="prepare",
    )(qkv_weight, aggregate_depth, aggregate_group, head_weight)

    weights = [
        expand_weight, expand_bias, depth_weight, depth_bias, project_weight, project_bias,
        qkv_weight, taps, group,
    ]
    weight_specs = [near()] * 6 + [far()] * 3

    def outs_of(count):
        return [
            jax.ShapeDtypeStruct((count, width, channels), BF16),
            jax.ShapeDtypeStruct((count, width, 2 * channels), BF16),
            jax.ShapeDtypeStruct((LANES + KEY_ROWS, LANES), BF16),
        ]

    def front_scratch(count):
        return [
            pltpu.VMEM((count, width, 256), F32),
            pltpu.VMEM((count - 2, width, 256), BF16),
            pltpu.VMEM(((count - 2) * width, channels), F32),
            pltpu.VMEM((count - 2, width, channels), BF16),
            pltpu.VMEM((count - 2, width, 3 * channels), F32),
            pltpu.VMEM((count - 6, width, channels), BF16),
            pltpu.VMEM((count - 6, width, 2 * channels), BF16),
            pltpu.VMEM(qkv_weight.shape[1:], BF16),
            pltpu.VMEM(taps.shape[1:], F32),
            pltpu.VMEM(group.shape[1:], BF16),
            pltpu.SemaphoreType.DMA((5,)),
        ]

    def attend_scratch(count):
        return [
            pltpu.VMEM((count, width, channels), BF16),
            pltpu.VMEM((count, width, channels), BF16),
            pltpu.VMEM((count, width, 2 * channels), BF16),
            pltpu.SemaphoreType.DMA((2,)),
        ]

    first_rows = rows + 2 * REACH
    names = list(halos)

    def first_body(own, *refs):
        parts = dict(zip(names, refs[: len(names)]))
        first_kernel(tile, head_dim, own, parts, *refs[len(names) :])

    mixed, query, payload = pl.pallas_call(
        first_body,
        out_shape=outs_of(first_rows - 6),
        grid=(1,),
        in_specs=[near()] * (1 + len(names)) + weight_specs,
        out_specs=[far(), far(), near()],
        scratch_shapes=[pltpu.VMEM((first_rows, width, channels), BF16)]
        + front_scratch(first_rows),
        compiler_params=params,
        name="first",
    )(features, *halos.values(), *weights)
    payload, other = sum_by_permutes(payload)

    second_rows = first_rows - 6
    mixed, query, payload = pl.pallas_call(
        functools.partial(second_kernel, tile, head_dim),
        out_shape=outs_of(second_rows - 6),
        grid=(1,),
        in_specs=[far()] * 2 + [near()] * 4 + weight_specs,
        out_specs=[far(), far(), near()],
        scratch_shapes=attend_scratch(second_rows) + front_scratch(second_rows),
        compiler_params=params,
        name="second",
    )(mixed, query, payload, other, output_weight, output_bias, *weights)
    payload, other = sum_by_permutes(payload)

    return pl.pallas_call(
        functools.partial(last_kernel, tile, head_dim),
        out_shape=[
            jax.ShapeDtypeStruct((rows, cols, channels), BF16),
            jax.ShapeDtypeStruct((4, rows, cols), F32),
        ],
        grid=(1,),
        in_specs=[far()] * 2 + [near()] * 6,
        out_specs=[near()] * 2,
        scratch_shapes=attend_scratch(rows + 2),
        compiler_params=params,
        name="last",
    )(
        mixed, query, payload, other, output_weight, output_bias, head_weight,
        head_bias.reshape(4, 1),
    )


def solution(mesh):
    return jax.shard_map(
        local,
        mesh=mesh,
        in_specs=(P("row", "col", None),) + (P(),) * 13,
        out_specs=(P("row", "col", None), P(None, "row", "col")),
        check_vma=False,
    )
```

time: 107 us -> 97.5 us (0.911)
  blocking collectives: 41.8 us -> 0 us
  starting transfers between devices: 11.8 us -> 40 us
  waiting for transfers between devices: 10 us -> 21.8 us
  local copies, waits for them, and re-layouts: 12.1 us -> 2.82 us
  Pallas kernels: 28.9 us -> 31.3 us
    all_to_all x4 -> x0, blocking collectives: 41.8 us -> none  [exchanged(): return lax.all_to_all(pieces, axis, 0, 0, tiled=True)]
    ppermute x4 -> x22, starting transfers between devices: 8.51 us -> 40 us  [the longest x8 22.3 us: from_neighbour(): return lax.ppermute(value, ('row', 'col'), pairs)]
    ppermute x4 -> x22, waiting for transfers between devices: 6.75 us -> 21.8 us  [the longest x14 20.4 us: sum_by_permutes(): lax.ppermute(value, axis, [(i, partner(i, stride, radix, k)) for i in ran...]
    unnamed x56 -> x28, local copies, waits for them, and re-layouts: 10.2 us -> 1.82 us
    all_to_all x1 -> x0, starting transfers between devices: 3.27 us -> none  [exchanged(): return lax.all_to_all(pieces, axis, 0, 0, tiled=True)]
    all_to_all x1 -> x0, waiting for transfers between devices: 3.25 us -> none  [exchanged(): return lax.all_to_all(pieces, axis, 0, 0, tiled=True)]
  transfers between devices with their start and end apart: 5 -> 22, of which waited for: 3 -> 12; matrix products, arithmetic and copies ran while one was open for 0% -> 0% of each run, Pallas kernels for 1% -> 2%
where the time goes in v4:
time: 97.5 us; the launch traced here: 97.1 us
  starting transfers between devices  40 us (41%)
  Pallas kernels  31.3 us (32%)
  waiting for transfers between devices  21.8 us (22%)
  local copies, waits for them, and re-layouts  2.82 us (3%)
  between operations  1.11 us (1%)
    ppermute x8, starting transfers between devices, from_neighbour(): return lax.ppermute(value, ('row', 'col'), pairs)  22.3 us
    ppermute x14, waiting for transfers between devices, sum_by_permutes(): lax.ppermute(value, axis, [(i, partner(i, stride, radix, k)) for i in ran...  20.4 us
    ppermute x14, starting transfers between devices, sum_by_permutes(): lax.ppermute(value, axis, [(i, partner(i, stride, radix, k)) for i in ran...  17.6 us
    pallas_call x1, Pallas kernels, local(): pl.pallas_call(first_body, out_shape=outs_of(first_rows - 6), grid=(1,),...  13.4 us
    pallas_call x1, Pallas kernels, local(): pl.pallas_call(functools.partial(second_kernel, tile, head_dim), out_shap...  12.7 us
    pallas_call x1, Pallas kernels, local(): pl.pallas_call(functools.partial(last_kernel, tile, head_dim), out_shape=...  3.33 us
  transfers between devices with their start and end apart: 22, of which 12 were waited for; matrix products, arithmetic and copies ran while one was open for 0% of the time, Pallas kernels for 2%

profile of v4, /device:TPU:0, one launch (start us, length us, event | category | flops | bytes accessed | tf_op | source)
XLA Modules:
  0.0 97.1 jit_solution(17899183460672986844)
XLA Ops:
  1.5 4.3 %collective-permute-start = (bf16[7,8,256]{2,1,0:T(8,128)(2,1)S(1)}, bf16[7,8,256]{2,1,0:T(8,128)(2,1)S(1)}, u32[]{:S(2)}, u32[]{:S(2)}) collective-permute-start(bf16[7,8,256]{2,1,0:T(8,128)(2,1)S(1)} %get-tuple-element.25), channel_id=1, source_target_pairs={{0,9},{1,10},{2,11},{3,12},{4,13},{5,14},{6,15},{8,17},{9,18},{10,... | collective-permute-start | bytes 86024 | tf_op jit(solution)/shard_map/ppermute | solution.py:422
  7.2 1.4 %collective-permute-start.7 = (bf16[7,8,256]{2,1,0:T(8,128)(2,1)S(1)}, bf16[7,8,256]{2,1,0:T(8,128)(2,1)S(1)}, u32[]{:S(2)}, u32[]{:S(2)}) collective-permute-start(bf16[7,8,256]{2,1,0:T(8,128)(2,1)S(1)} %get-tuple-element.22), channel_id=1, source_target_pairs={{9,0},{10,1},{11,2},{12,3},{13,4},{14,5},{15,6},{17,8},{18,9},{19,... | collective-permute-start | bytes 86024 | tf_op jit(solution)/shard_map/ppermute | solution.py:422
  8.7 7.7 %collective-permute-start.1 = (bf16[7,32,256]{2,1,0:T(8,128)(2,1)S(1)}, bf16[7,32,256]{2,1,0:T(8,128)(2,1)S(1)}, u32[]{:S(2)}, u32[]{:S(2)}) collective-permute-start(bf16[7,32,256]{2,1,0:T(8,128)(2,1)S(1)} %get-tuple-element.27), channel_id=1, source_target_pairs={{0,8},{1,9},{2,10},{3,11},{4,12},{5,13},{6,14},{7,15},{8,16},{9,17... | collective-permute-start | bytes 344072 | tf_op jit(solution)/shard_map/ppermute | solution.py:422
  16.5 1.3 %collective-permute-start.6 = (bf16[7,32,256]{2,1,0:T(8,128)(2,1)S(1)}, bf16[7,32,256]{2,1,0:T(8,128)(2,1)S(1)}, u32[]{:S(2)}, u32[]{:S(2)}) collective-permute-start(bf16[7,32,256]{2,1,0:T(8,128)(2,1)S(1)} %get-tuple-element.26), channel_id=1, source_target_pairs={{8,0},{9,1},{10,2},{11,3},{12,4},{13,5},{14,6},{15,7},{16,8},{17,9... | collective-permute-start | bytes 344072 | tf_op jit(solution)/shard_map/ppermute | solution.py:422
  17.8 5.0 %collective-permute-start.3 = (bf16[8,8,256]{2,1,0:T(8,128)(2,1)S(1)}, bf16[8,8,256]{2,1,0:T(8,128)(2,1)S(1)}, u32[]{:S(2)}, u32[]{:S(2)}) collective-permute-start(bf16[8,8,256]{2,1,0:T(8,128)(2,1)S(1)} %get-tuple-element.29), channel_id=1, source_target_pairs={{0,1},{1,2},{2,3},{3,4},{4,5},{5,6},{6,7},{8,9},{9,10},{10,11},{11... | collective-permute-start | bytes 98312 | tf_op jit(solution)/shard_map/ppermute | solution.py:422
  22.8 1.3 %collective-permute-start.4 = (bf16[8,8,256]{2,1,0:T(8,128)(2,1)S(1)}, bf16[8,8,256]{2,1,0:T(8,128)(2,1)S(1)}, u32[]{:S(2)}, u32[]{:S(2)}) collective-permute-start(bf16[8,8,256]{2,1,0:T(8,128)(2,1)S(1)} %get-tuple-element.28), channel_id=1, source_target_pairs={{1,0},{2,1},{3,2},{4,3},{5,4},{6,5},{7,6},{9,8},{10,9},{11,10},{12... | collective-permute-start | bytes 98312 | tf_op jit(solution)/shard_map/ppermute | solution.py:422
  25.2 1.9 %prepare.1 = (bf16[2,256,768]{2,1,0:T(8,128)(2,1)S(1)}, f32[2,32,768]{2,1,0:T(8,128)S(1)}, bf16[2,3,256,256]{3,2,1,0:T(8,128)(2,1)S(1)}, bf16[3,128,256]{2,1,0:T(8,128)(2,1)S(1)}) custom-call(bf16[2,256,768]{2,1,0:T(8,128)(2,1)S(1)} %copy-done.9, f32[5,5,2,768]{3,2,1,0:T(2,128)S(1)} %bitcast.5, bf16[2,24,32,32]{3,2,1,0:T(8,128)(2,1)S(1)} %copy-done.10, ...), custom_call_target="tpu_custom_call" | custom-call | flops 2000000000 | bytes 4000000 | tf_op jit(solution)/shard_map/prepare/pallas_call | solution.py:466
  27.2 1.4 %collective-permute-done.4.refs_4_ = bf16[8,8,256]{2,1,0:T(8,128)(2,1)S(1)} collective-permute-done((bf16[8,8,256]{2,1,0:T(8,128)(2,1)S(1)}, bf16[8,8,256]{2,1,0:T(8,128)(2,1)S(1)}, u32[]{:S(2)}, u32[]{:S(2)}) %collective-permute-start.4) | collective-permute-done | bytes 32800 | tf_op jit(solution)/shard_map/ppermute | solution.py:422
  29.3 13.4 %first.1 = (bf16[16,48,256]{2,1,0:T(8,128)(2,1)S(1)}, bf16[16,48,512]{2,1,0:T(8,128)(2,1)S(1)}, bf16[144,128]{1,0:T(8,128)(2,1)S(1)}) custom-call(bf16[8,32,256]{2,1,0:T(8,128)(2,1)S(1)} %copy-done.2, bf16[7,8,256]{2,1,0:T(8,128)(2,1)S(1)} %collective-permute-done.refs_0_, bf16[7,32,256]{2,1,0:T(8,128)(2,1)S(1)} %collective-permute-done.1.refs_1_, ...), custom_call_target="tpu_custom_call" | custom-call | tf_op jit(solution)/shard_map/first/pallas_call | solution.py:524
  42.6 1.7 %collective-permute-start.10 = (bf16[144,128]{1,0:T(8,128)(2,1)S(1)}, bf16[144,128]{1,0:T(8,128)(2,1)S(1)}, u32[]{:S(2)}, u32[]{:S(2)}) collective-permute-start(bf16[144,128]{1,0:T(8,128)(2,1)S(1)} %get-tuple-element.17), channel_id=1, source_target_pairs={{0,24},{8,16},{16,8},{24,0},{1,25},{9,17},{17,9},{25,1},{2,26},{10... | collective-permute-start | bytes 110600 | tf_op jit(solution)/shard_map/ppermute | solution.py:393
  44.3 2.7 %collective-permute-start.8 = (bf16[144,128]{1,0:T(8,128)(2,1)S(1)}, bf16[144,128]{1,0:T(8,128)(2,1)S(1)}, u32[]{:S(2)}, u32[]{:S(2)}) collective-permute-start(bf16[144,128]{1,0:T(8,128)(2,1)S(1)} %get-tuple-element.17), channel_id=1, source_target_pairs={{0,8},{8,0},{16,24},{24,16},{1,9},{9,1},{17,25},{25,17},{2,10},{10... | collective-permute-start | bytes 110600 | tf_op jit(solution)/shard_map/ppermute | solution.py:393
  47.9 3.1 %collective-permute-done.9 = bf16[144,128]{1,0:T(8,128)(2,1)S(1)} collective-permute-done((bf16[144,128]{1,0:T(8,128)(2,1)S(1)}, bf16[144,128]{1,0:T(8,128)(2,1)S(1)}, u32[]{:S(2)}, u32[]{:S(2)}) %collective-permute-start.9) | collective-permute-done | bytes 36896 | tf_op jit(solution)/shard_map/ppermute | solution.py:393
  51.0 2.9 %collective-permute-start.11 = (bf16[144,128]{1,0:T(8,128)(2,1)S(1)}, bf16[144,128]{1,0:T(8,128)(2,1)S(1)}, u32[]{:S(2)}, u32[]{:S(2)}) collective-permute-start(bf16[144,128]{1,0:T(8,128)(2,1)S(1)} %add_convert_fusion.3), channel_id=1, source_target_pairs={{0,1},{1,0},{2,3},{3,2},{4,5},{5,4},{6,7},{7,6},{8,9},{9,8},{10,11... | collective-permute-start | bytes 110600 | tf_op jit(solution)/shard_map/ppermute | solution.py:393
  54.0 1.6 %collective-permute-start.12 = (bf16[144,128]{1,0:T(8,128)(2,1)S(1)}, bf16[144,128]{1,0:T(8,128)(2,1)S(1)}, u32[]{:S(2)}, u32[]{:S(2)}) collective-permute-start(bf16[144,128]{1,0:T(8,128)(2,1)S(1)} %add_convert_fusion.3), channel_id=1, source_target_pairs={{0,2},{1,3},{2,0},{3,1},{4,6},{5,7},{6,4},{7,5},{8,10},{9,11},{10,... | collective-permute-start | bytes 110600 | tf_op jit(solution)/shard_map/ppermute | solution.py:393
  55.9 2.0 %collective-permute-done.12 = bf16[144,128]{1,0:T(8,128)(2,1)S(1)} collective-permute-done((bf16[144,128]{1,0:T(8,128)(2,1)S(1)}, bf16[144,128]{1,0:T(8,128)(2,1)S(1)}, u32[]{:S(2)}, u32[]{:S(2)}) %collective-permute-start.12) | collective-permute-done | bytes 36896 | tf_op jit(solution)/shard_map/ppermute | solution.py:393
  57.9 2.5 %collective-permute-done.13 = bf16[144,128]{1,0:T(8,128)(2,1)S(1)} collective-permute-done((bf16[144,128]{1,0:T(8,128)(2,1)S(1)}, bf16[144,128]{1,0:T(8,128)(2,1)S(1)}, u32[]{:S(2)}, u32[]{:S(2)}) %collective-permute-start.13) | collective-permute-done | bytes 36896 | tf_op jit(solution)/shard_map/ppermute | solution.py:393
  61.5 4.1 %collective-permute-done.14.other = bf16[144,128]{1,0:T(8,128)(2,1)S(1)} collective-permute-done((bf16[144,128]{1,0:T(8,128)(2,1)S(1)}, bf16[144,128]{1,0:T(8,128)(2,1)S(1)}, u32[]{:S(2)}, u32[]{:S(2)}) %collective-permute-start.14) | collective-permute-done | bytes 36896 | tf_op jit(solution)/shard_map/ppermute | solution.py:393
  65.6 12.7 %second.1 = (bf16[10,48,256]{2,1,0:T(8,128)(2,1)S(1)}, bf16[10,48,512]{2,1,0:T(8,128)(2,1)S(1)}, bf16[144,128]{1,0:T(8,128)(2,1)S(1)}) custom-call(bf16[16,48,256]{2,1,0:T(8,128)(2,1)S(1)} %get-tuple-element.15.mixed, bf16[16,48,512]{2,1,0:T(8,128)(2,1)S(1)} %get-tuple-element.16.query, bf16[144,128]{1,0:T(8,128)(2,1)S(1)} %add_convert_fusion.2.payload, ...), custom_call_target="tpu_custom_call" | custom-call | tf_op jit(solution)/shard_map/second/pallas_call | solution.py:538
  78.6 1.7 %collective-permute-start.17 = (bf16[144,128]{1,0:T(8,128)(2,1)S(1)}, bf16[144,128]{1,0:T(8,128)(2,1)S(1)}, u32[]{:S(2)}, u32[]{:S(2)}) collective-permute-start(bf16[144,128]{1,0:T(8,128)(2,1)S(1)} %get-tuple-element.20), channel_id=1, source_target_pairs={{0,24},{8,16},{16,8},{24,0},{1,25},{9,17},{17,9},{25,1},{2,26},{10... | collective-permute-start | bytes 110600 | tf_op jit(solution)/shard_map/ppermute | solution.py:393
  80.3 2.4 %collective-permute-done.16 = bf16[144,128]{1,0:T(8,128)(2,1)S(1)} collective-permute-done((bf16[144,128]{1,0:T(8,128)(2,1)S(1)}, bf16[144,128]{1,0:T(8,128)(2,1)S(1)}, u32[]{:S(2)}, u32[]{:S(2)}) %collective-permute-start.16) | collective-permute-done | bytes 36896 | tf_op jit(solution)/shard_map/ppermute | solution.py:393
  83.6 2.7 %collective-permute-start.20 = (bf16[144,128]{1,0:T(8,128)(2,1)S(1)}, bf16[144,128]{1,0:T(8,128)(2,1)S(1)}, u32[]{:S(2)}, u32[]{:S(2)}) collective-permute-start(bf16[144,128]{1,0:T(8,128)(2,1)S(1)} %add_convert_fusion.1), channel_id=1, source_target_pairs={{0,3},{1,2},{2,1},{3,0},{4,7},{5,6},{6,5},{7,4},{8,11},{9,10},{10,... | collective-permute-start | bytes 110600 | tf_op jit(solution)/shard_map/ppermute | solution.py:393
  88.7 2.1 %collective-permute-start.21 = (bf16[144,128]{1,0:T(8,128)(2,1)S(1)}, bf16[144,128]{1,0:T(8,128)(2,1)S(1)}, u32[]{:S(2)}, u32[]{:S(2)}) collective-permute-start(bf16[144,128]{1,0:T(8,128)(2,1)S(1)} %add_convert_fusion.payload), channel_id=1, source_target_pairs={{0,4},{1,5},{2,6},{3,7},{4,0},{5,1},{6,2},{7,3},{8,12},{9,13},{10,... | collective-permute-start | bytes 110600 | tf_op jit(solution)/shard_map/ppermute | solution.py:393
  90.9 2.7 %collective-permute-done.21.other = bf16[144,128]{1,0:T(8,128)(2,1)S(1)} collective-permute-done((bf16[144,128]{1,0:T(8,128)(2,1)S(1)}, bf16[144,128]{1,0:T(8,128)(2,1)S(1)}, u32[]{:S(2)}, u32[]{:S(2)}) %collective-permute-start.21) | collective-permute-done | bytes 36896 | tf_op jit(solution)/shard_map/ppermute | solution.py:393
  93.6 3.3 %last.1 = (bf16[8,32,256]{2,1,0:T(8,128)(2,1)}, f32[4,8,32]{2,1,0:T(8,128)}) custom-call(bf16[10,48,256]{2,1,0:T(8,128)(2,1)S(1)} %get-tuple-element.18.mixed, bf16[10,48,512]{2,1,0:T(8,128)(2,1)S(1)} %get-tuple-element.19.query, bf16[144,128]{1,0:T(8,128)(2,1)S(1)} %add_convert_fusion.payload, bf16[144,128]{1,0:T(8,128)(2,1)S(1)} %collective-permute-done.21.other, ...), custom_call_target="tpu_custom_call" | custom-call | tf_op jit(solution)/shard_map/last/pallas_call | solution.py:550
  (60 shorter events, 9.9 us)
Async XLA Ops:
  0.6 23.4 %copy-start.10 = (bf16[2,24,32,32]{3,2,1,0:T(8,128)(2,1)S(1)}, bf16[2,24,32,32]{3,2,1,0:T(8,128)(2,1)}, u32[]{:S(2)}) copy-start(bf16[2,24,32,32]{3,2,1,0:T(8,128)(2,1)} %group.1) | copy-start | bytes 294916
  1.5 14.9 %collective-permute-start = (bf16[7,8,256]{2,1,0:T(8,128)(2,1)S(1)}, bf16[7,8,256]{2,1,0:T(8,128)(2,1)S(1)}, u32[]{:S(2)}, u32[]{:S(2)}) collective-permute-start(bf16[7,8,256]{2,1,0:T(8,128)(2,1)S(1)} %get-tuple-element.25), channel_id=1, source_target_pairs={{0,9},{1,10},{2,11},{3,12},{4,13},{5,14},{6,15},{8,17},{9,18},{10,... | collective-permute-start | bytes 86024 | tf_op jit(solution)/shard_map/ppermute | solution.py:422
  5.9 11.9 %collective-permute-start.2 = (bf16[7,8,256]{2,1,0:T(8,128)(2,1)S(1)}, bf16[7,8,256]{2,1,0:T(8,128)(2,1)S(1)}, u32[]{:S(2)}, u32[]{:S(2)}) collective-permute-start(bf16[7,8,256]{2,1,0:T(8,128)(2,1)S(1)} %get-tuple-element.24), channel_id=1, source_target_pairs={{1,8},{2,9},{3,10},{4,11},{5,12},{6,13},{7,14},{9,16},{10,17},{11,... | collective-permute-start | bytes 86024 | tf_op jit(solution)/shard_map/ppermute | solution.py:422
  6.5 16.2 %collective-permute-start.5 = (bf16[7,8,256]{2,1,0:T(8,128)(2,1)S(1)}, bf16[7,8,256]{2,1,0:T(8,128)(2,1)S(1)}, u32[]{:S(2)}, u32[]{:S(2)}) collective-permute-start(bf16[7,8,256]{2,1,0:T(8,128)(2,1)S(1)} %get-tuple-element.23), channel_id=1, source_target_pairs={{8,1},{9,2},{10,3},{11,4},{12,5},{13,6},{14,7},{16,9},{17,10},{18,... | collective-permute-start | bytes 86024 | tf_op jit(solution)/shard_map/ppermute | solution.py:422
  7.2 19.9 %collective-permute-start.7 = (bf16[7,8,256]{2,1,0:T(8,128)(2,1)S(1)}, bf16[7,8,256]{2,1,0:T(8,128)(2,1)S(1)}, u32[]{:S(2)}, u32[]{:S(2)}) collective-permute-start(bf16[7,8,256]{2,1,0:T(8,128)(2,1)S(1)} %get-tuple-element.22), channel_id=1, source_target_pairs={{9,0},{10,1},{11,2},{12,3},{13,4},{14,5},{15,6},{17,8},{18,9},{19,... | collective-permute-start | bytes 86024 | tf_op jit(solution)/shard_map/ppermute | solution.py:422
  8.7 19.9 %collective-permute-start.1 = (bf16[7,32,256]{2,1,0:T(8,128)(2,1)S(1)}, bf16[7,32,256]{2,1,0:T(8,128)(2,1)S(1)}, u32[]{:S(2)}, u32[]{:S(2)}) collective-permute-start(bf16[7,32,256]{2,1,0:T(8,128)(2,1)S(1)} %get-tuple-element.27), channel_id=1, source_target_pairs={{0,8},{1,9},{2,10},{3,11},{4,12},{5,13},{6,14},{7,15},{8,16},{9,17... | collective-permute-start | bytes 344072 | tf_op jit(solution)/shard_map/ppermute | solution.py:422
  16.5 12.1 %collective-permute-start.6 = (bf16[7,32,256]{2,1,0:T(8,128)(2,1)S(1)}, bf16[7,32,256]{2,1,0:T(8,128)(2,1)S(1)}, u32[]{:S(2)}, u32[]{:S(2)}) collective-permute-start(bf16[7,32,256]{2,1,0:T(8,128)(2,1)S(1)} %get-tuple-element.26), channel_id=1, source_target_pairs={{8,0},{9,1},{10,2},{11,3},{12,4},{13,5},{14,6},{15,7},{16,8},{17,9... | collective-permute-start | bytes 344072 | tf_op jit(solution)/shard_map/ppermute | solution.py:422
  17.8 9.4 %collective-permute-start.3 = (bf16[8,8,256]{2,1,0:T(8,128)(2,1)S(1)}, bf16[8,8,256]{2,1,0:T(8,128)(2,1)S(1)}, u32[]{:S(2)}, u32[]{:S(2)}) collective-permute-start(bf16[8,8,256]{2,1,0:T(8,128)(2,1)S(1)} %get-tuple-element.29), channel_id=1, source_target_pairs={{0,1},{1,2},{2,3},{3,4},{4,5},{5,6},{6,7},{8,9},{9,10},{10,11},{11... | collective-permute-start | bytes 98312 | tf_op jit(solution)/shard_map/ppermute | solution.py:422
  22.8 5.8 %collective-permute-start.4 = (bf16[8,8,256]{2,1,0:T(8,128)(2,1)S(1)}, bf16[8,8,256]{2,1,0:T(8,128)(2,1)S(1)}, u32[]{:S(2)}, u32[]{:S(2)}) collective-permute-start(bf16[8,8,256]{2,1,0:T(8,128)(2,1)S(1)} %get-tuple-element.28), channel_id=1, source_target_pairs={{1,0},{2,1},{3,2},{4,3},{5,4},{6,5},{7,6},{9,8},{10,9},{11,10},{12... | collective-permute-start | bytes 98312 | tf_op jit(solution)/shard_map/ppermute | solution.py:422
  29.3 36.4 %copy-start.3 = (bf16[2,512,256]{2,1,0:T(8,128)(2,1)S(1)}, bf16[2,512,256]{2,1,0:T(8,128)(2,1)}, u32[]{:S(2)}) copy-start(bf16[2,512,256]{2,1,0:T(8,128)(2,1)} %out_weight.3) | copy-start | bytes 1572868
  42.6 4.5 %collective-permute-start.10 = (bf16[144,128]{1,0:T(8,128)(2,1)S(1)}, bf16[144,128]{1,0:T(8,128)(2,1)S(1)}, u32[]{:S(2)}, u32[]{:S(2)}) collective-permute-start(bf16[144,128]{1,0:T(8,128)(2,1)S(1)} %get-tuple-element.17), channel_id=1, source_target_pairs={{0,24},{8,16},{16,8},{24,0},{1,25},{9,17},{17,9},{25,1},{2,26},{10... | collective-permute-start | bytes 110600 | tf_op jit(solution)/shard_map/ppermute | solution.py:393
  44.3 3.6 %collective-permute-start.8 = (bf16[144,128]{1,0:T(8,128)(2,1)S(1)}, bf16[144,128]{1,0:T(8,128)(2,1)S(1)}, u32[]{:S(2)}, u32[]{:S(2)}) collective-permute-start(bf16[144,128]{1,0:T(8,128)(2,1)S(1)} %get-tuple-element.17), channel_id=1, source_target_pairs={{0,8},{8,0},{16,24},{24,16},{1,9},{9,1},{17,25},{25,17},{2,10},{10... | collective-permute-start | bytes 110600 | tf_op jit(solution)/shard_map/ppermute | solution.py:393
  47.1 4.0 %collective-permute-start.9 = (bf16[144,128]{1,0:T(8,128)(2,1)S(1)}, bf16[144,128]{1,0:T(8,128)(2,1)S(1)}, u32[]{:S(2)}, u32[]{:S(2)}) collective-permute-start(bf16[144,128]{1,0:T(8,128)(2,1)S(1)} %get-tuple-element.17), channel_id=1, source_target_pairs={{0,16},{8,24},{16,0},{24,8},{1,17},{9,25},{17,1},{25,9},{2,18},{10... | collective-permute-start | bytes 110600 | tf_op jit(solution)/shard_map/ppermute | solution.py:393
  51.0 4.9 %collective-permute-start.11 = (bf16[144,128]{1,0:T(8,128)(2,1)S(1)}, bf16[144,128]{1,0:T(8,128)(2,1)S(1)}, u32[]{:S(2)}, u32[]{:S(2)}) collective-permute-start(bf16[144,128]{1,0:T(8,128)(2,1)S(1)} %add_convert_fusion.3), channel_id=1, source_target_pairs={{0,1},{1,0},{2,3},{3,2},{4,5},{5,4},{6,7},{7,6},{8,9},{9,8},{10,11... | collective-permute-start | bytes 110600 | tf_op jit(solution)/shard_map/ppermute | solution.py:393
  54.0 4.0 %collective-permute-start.12 = (bf16[144,128]{1,0:T(8,128)(2,1)S(1)}, bf16[144,128]{1,0:T(8,128)(2,1)S(1)}, u32[]{:S(2)}, u32[]{:S(2)}) collective-permute-start(bf16[144,128]{1,0:T(8,128)(2,1)S(1)} %add_convert_fusion.3), channel_id=1, source_target_pairs={{0,2},{1,3},{2,0},{3,1},{4,6},{5,7},{6,4},{7,5},{8,10},{9,11},{10,... | collective-permute-start | bytes 110600 | tf_op jit(solution)/shard_map/ppermute | solution.py:393
  55.5 4.9 %collective-permute-start.13 = (bf16[144,128]{1,0:T(8,128)(2,1)S(1)}, bf16[144,128]{1,0:T(8,128)(2,1)S(1)}, u32[]{:S(2)}, u32[]{:S(2)}) collective-permute-start(bf16[144,128]{1,0:T(8,128)(2,1)S(1)} %add_convert_fusion.3), channel_id=1, source_target_pairs={{0,3},{1,2},{2,1},{3,0},{4,7},{5,6},{6,5},{7,4},{8,11},{9,10},{10,... | collective-permute-start | bytes 110600 | tf_op jit(solution)/shard_map/ppermute | solution.py:393
  60.4 5.2 %collective-permute-start.14 = (bf16[144,128]{1,0:T(8,128)(2,1)S(1)}, bf16[144,128]{1,0:T(8,128)(2,1)S(1)}, u32[]{:S(2)}, u32[]{:S(2)}) collective-permute-start(bf16[144,128]{1,0:T(8,128)(2,1)S(1)} %add_convert_fusion.2.payload), channel_id=1, source_target_pairs={{0,4},{1,5},{2,6},{3,7},{4,0},{5,1},{6,2},{7,3},{8,12},{9,13},{10,... | collective-permute-start | bytes 110600 | tf_op jit(solution)/shard_map/ppermute | solution.py:393
  78.4 1.9 %collective-permute-start.15 = (bf16[144,128]{1,0:T(8,128)(2,1)S(1)}, bf16[144,128]{1,0:T(8,128)(2,1)S(1)}, u32[]{:S(2)}, u32[]{:S(2)}) collective-permute-start(bf16[144,128]{1,0:T(8,128)(2,1)S(1)} %get-tuple-element.20), channel_id=1, source_target_pairs={{0,8},{8,0},{16,24},{24,16},{1,9},{9,1},{17,25},{25,17},{2,10},{10... | collective-permute-start | bytes 110600 | tf_op jit(solution)/shard_map/ppermute | solution.py:393
  78.4 4.3 %collective-permute-start.16 = (bf16[144,128]{1,0:T(8,128)(2,1)S(1)}, bf16[144,128]{1,0:T(8,128)(2,1)S(1)}, u32[]{:S(2)}, u32[]{:S(2)}) collective-permute-start(bf16[144,128]{1,0:T(8,128)(2,1)S(1)} %get-tuple-element.20), channel_id=1, source_target_pairs={{0,16},{8,24},{16,0},{24,8},{1,17},{9,25},{17,1},{25,9},{2,18},{10... | collective-permute-start | bytes 110600 | tf_op jit(solution)/shard_map/ppermute | solution.py:393
  78.6 4.2 %collective-permute-start.17 = (bf16[144,128]{1,0:T(8,128)(2,1)S(1)}, bf16[144,128]{1,0:T(8,128)(2,1)S(1)}, u32[]{:S(2)}, u32[]{:S(2)}) collective-permute-start(bf16[144,128]{1,0:T(8,128)(2,1)S(1)} %get-tuple-element.20), channel_id=1, source_target_pairs={{0,24},{8,16},{16,8},{24,0},{1,25},{9,17},{17,9},{25,1},{2,26},{10... | collective-permute-start | bytes 110600 | tf_op jit(solution)/shard_map/ppermute | solution.py:393
  82.8 4.0 %collective-permute-start.18 = (bf16[144,128]{1,0:T(8,128)(2,1)S(1)}, bf16[144,128]{1,0:T(8,128)(2,1)S(1)}, u32[]{:S(2)}, u32[]{:S(2)}) collective-permute-start(bf16[144,128]{1,0:T(8,128)(2,1)S(1)} %add_convert_fusion.1), channel_id=1, source_target_pairs={{0,1},{1,0},{2,3},{3,2},{4,5},{5,4},{6,7},{7,6},{8,9},{9,8},{10,11... | collective-permute-start | bytes 110600 | tf_op jit(solution)/shard_map/ppermute | solution.py:393
  83.2 4.2 %collective-permute-start.19 = (bf16[144,128]{1,0:T(8,128)(2,1)S(1)}, bf16[144,128]{1,0:T(8,128)(2,1)S(1)}, u32[]{:S(2)}, u32[]{:S(2)}) collective-permute-start(bf16[144,128]{1,0:T(8,128)(2,1)S(1)} %add_convert_fusion.1), channel_id=1, source_target_pairs={{0,2},{1,3},{2,0},{3,1},{4,6},{5,7},{6,4},{7,5},{8,10},{9,11},{10,... | collective-permute-start | bytes 110600 | tf_op jit(solution)/shard_map/ppermute | solution.py:393
  83.6 5.1 %collective-permute-start.20 = (bf16[144,128]{1,0:T(8,128)(2,1)S(1)}, bf16[144,128]{1,0:T(8,128)(2,1)S(1)}, u32[]{:S(2)}, u32[]{:S(2)}) collective-permute-start(bf16[144,128]{1,0:T(8,128)(2,1)S(1)} %add_convert_fusion.1), channel_id=1, source_target_pairs={{0,3},{1,2},{2,1},{3,0},{4,7},{5,6},{6,5},{7,4},{8,11},{9,10},{10,... | collective-permute-start | bytes 110600 | tf_op jit(solution)/shard_map/ppermute | solution.py:393
  88.7 4.9 %collective-permute-start.21 = (bf16[144,128]{1,0:T(8,128)(2,1)S(1)}, bf16[144,128]{1,0:T(8,128)(2,1)S(1)}, u32[]{:S(2)}, u32[]{:S(2)}) collective-permute-start(bf16[144,128]{1,0:T(8,128)(2,1)S(1)} %add_convert_fusion.payload), channel_id=1, source_target_pairs={{0,4},{1,5},{2,6},{3,7},{4,0},{5,1},{6,2},{7,3},{8,12},{9,13},{10,... | collective-permute-start | bytes 110600 | tf_op jit(solution)/shard_map/ppermute | solution.py:393
  (12 other events, 66.3 us)

commit v5 on v4

--- a/solution.py
+++ b/solution.py
@@ -292,16 +292,25 @@
         store.wait()
 
 
-def first_kernel(tile, head_dim, own, halos, *refs):
+def first_kernel(tile, head_dim, own, row_0, row_1, col_0, col_1, *refs):
     weights, outs, scratch = refs[:9], refs[9:12], refs[12:]
     x_ref = scratch[0]
     rows, cols = tile
     x_ref[REACH : REACH + rows, 0:cols, :] = own[...]
-    for step, at, count in ((-1, 0, REACH), (0, REACH, rows), (1, REACH + rows, REACH)):
-        if step:
-            x_ref[at : at + count, 0:cols, :] = halos[step, 0][...]
-        sides = [halos[step, 1][...], halos[step, -1][...]]
-        x_ref[at : at + count, cols : cols + 2 * SIDE, :] = jnp.concatenate(sides, axis=1)
+    below = REACH + rows
+    even = lax.axis_index("row") % 2 == 0
+    x_ref[pl.ds(jnp.where(even, below, 0), REACH), 0:cols, :] = row_0[...]
+    x_ref[pl.ds(jnp.where(even, 0, below), REACH), 0:cols, :] = row_1[...]
+    even = lax.axis_index("col") % 2 == 0
+
+    @pl.when(even)
+    def _():
+        x_ref[:, cols : cols + 2 * SIDE, :] = jnp.concatenate([col_0[...], col_1[...]], axis=1)
+
+    @pl.when(jnp.logical_not(even))
+    def _():
+        x_ref[:, cols : cols + 2 * SIDE, :] = jnp.concatenate([col_1[...], col_0[...]], axis=1)
+
     front(x_ref, weights, outs, scratch[1:], REACH, tile, head_dim, 0)
 
 
@@ -411,15 +420,12 @@
     return radices
 
 
-def from_neighbour(value, row_step, col_step):
-    rows, cols = lax.axis_size("row"), lax.axis_size("col")
-    pairs = [
-        ((r + row_step) * cols + c + col_step, r * cols + c)
-        for r in range(rows)
-        for c in range(cols)
-        if 0 <= r + row_step < rows and 0 <= c + col_step < cols
-    ]
-    return lax.ppermute(value, ("row", "col"), pairs)
+def pair_exchange(value, axis, first):
+    count = lax.axis_size(axis)
+    pairs = []
+    for i in range(first, count - 1, 2):
+        pairs += [(i, i + 1), (i + 1, i)]
+    return lax.ppermute(value, axis, pairs)
 
 
 def local(
@@ -445,14 +451,21 @@
     tile = (rows, cols)
     wide = expand_weight.shape[2]
 
-    row_part = {-1: slice(rows - REACH, rows), 0: slice(0, rows), 1: slice(0, REACH)}
-    col_part = {-1: slice(cols - SIDE, cols), 0: slice(0, cols), 1: slice(0, SIDE)}
-    halos = {
-        (r, c): from_neighbour(features[row_part[r], col_part[c]], r, c)
-        for r in (-1, 0, 1)
-        for c in (-1, 0, 1)
-        if r or c
-    }
+    def edges(value, dim, size, odd):
+        far = value.shape[dim] - size
+        return [
+            lax.dynamic_slice_in_dim(value, jnp.where(odd == at, far, 0), size, dim) for at in (0, 1)
+        ]
+
+    odd_row = lax.axis_index("row") % 2
+    odd_col = lax.axis_index("col") % 2
+    low, high = edges(features, 0, REACH, odd_row)
+    row_halos = [pair_exchange(low, "row", 0), pair_exchange(high, "row", 1)]
+    below = jnp.where(odd_row == 0, row_halos[0], row_halos[1])
+    above = jnp.where(odd_row == 0, row_halos[1], row_halos[0])
+    tall = jnp.concatenate([above, features, below], axis=0)
+    low, high = edges(tall, 1, SIDE, odd_col)
+    col_halos = [pair_exchange(low, "col", 0), pair_exchange(high, "col", 1)]
 
     aggregate_depth = aggregate_depth.transpose(1, 2, 0, 3)
     depth_weight = depth_weight.transpose(1, 2, 0, 3)
@@ -515,23 +528,17 @@
         ]
 
     first_rows = rows + 2 * REACH
-    names = list(halos)
-
-    def first_body(own, *refs):
-        parts = dict(zip(names, refs[: len(names)]))
-        first_kernel(tile, head_dim, own, parts, *refs[len(names) :])
-
     mixed, query, payload = pl.pallas_call(
-        first_body,
+        functools.partial(first_kernel, tile, head_dim),
         out_shape=outs_of(first_rows - 6),
         grid=(1,),
-        in_specs=[near()] * (1 + len(names)) + weight_specs,
+        in_specs=[near()] * 5 + weight_specs,
         out_specs=[far(), far(), near()],
         scratch_shapes=[pltpu.VMEM((first_rows, width, channels), BF16)]
         + front_scratch(first_rows),
         compiler_params=params,
         name="first",
-    )(features, *halos.values(), *weights)
+    )(features, *row_halos, *col_halos, *weights)
     payload, other = sum_by_permutes(payload)
 
     second_rows = first_rows - 6

time: 97.5 us -> 82 us (0.84)
  starting transfers between devices: 40 us -> 29 us
  waiting for transfers between devices: 21.8 us -> 17.8 us
    ppermute x8 -> x4, starting transfers between devices: 22.3 us -> 4.43 us  [pair_exchange(): return lax.ppermute(value, axis, pairs)]
    ppermute x14, starting transfers between devices: 17.6 us -> 24.6 us  [sum_by_permutes(): lax.ppermute(value, axis, [(i, partner(i, stride, radix, k)) for i in ran...]
    ppermute x14, waiting for transfers between devices: 20.4 us -> 17.5 us  [sum_by_permutes(): lax.ppermute(value, axis, [(i, partner(i, stride, radix, k)) for i in ran...]
    ppermute x8 -> x4, waiting for transfers between devices: 1.41 us -> 0.27 us  [pair_exchange(): return lax.ppermute(value, axis, pairs)]
    dynamic_slice x0 -> x2, local copies, waits for them, and re-layouts: none -> 1.03 us  [edges(): lax.dynamic_slice_in_dim(value, jnp.where(odd == at, far, 0), size, dim)]
  transfers between devices with their start and end apart: 22 -> 18, of which waited for: 12 -> 12; matrix products, arithmetic and copies ran while one was open for 0% -> 0% of each run, Pallas kernels for 2% -> 2%
where the time goes in v5:
time: 82 us; the launch traced here: 81.8 us
  Pallas kernels  31.3 us (38%)
  starting transfers between devices  29 us (35%)
  waiting for transfers between devices  17.8 us (22%)
  local copies, waits for them, and re-layouts  2.42 us (3%)
  between operations  1.1 us (1%)
    ppermute x14, starting transfers between devices, sum_by_permutes(): lax.ppermute(value, axis, [(i, partner(i, stride, radix, k)) for i in ran...  24.6 us
    ppermute x14, waiting for transfers between devices, sum_by_permutes(): lax.ppermute(value, axis, [(i, partner(i, stride, radix, k)) for i in ran...  17.5 us
    pallas_call x1, Pallas kernels, local(): pl.pallas_call(functools.partial(first_kernel, tile, head_dim), out_shape...  13.4 us
    pallas_call x1, Pallas kernels, local(): pl.pallas_call(functools.partial(second_kernel, tile, head_dim), out_shap...  12.7 us
    ppermute x4, starting transfers between devices, pair_exchange(): return lax.ppermute(value, axis, pairs)  4.43 us
    pallas_call x1, Pallas kernels, local(): pl.pallas_call(functools.partial(last_kernel, tile, head_dim), out_shape=...  3.33 us
    pallas_call x1, Pallas kernels, local(): pl.pallas_call(functools.partial(prepare_kernel, head_dim), out_shape=mad...  1.89 us
  transfers between devices with their start and end apart: 18, of which 12 were waited for; matrix products, arithmetic and copies ran while one was open for 0% of the time, Pallas kernels for 2%

profile of v5, /device:TPU:0, one launch (start us, length us, event | category | flops | bytes accessed | tf_op | source)
XLA Modules:
  0.0 81.8 jit_solution(7768199569147040497)
XLA Ops:
  0.6 1.0 %constant_dynamic-slice_fusion.2 = (bf16[7,32,256]{2,1,0:T(8,128)(2,1)S(1)}, bf16[7,32,256]{2,1,0:T(8,128)(2,1)S(1)}) fusion(bf16[8,32,256]{2,1,0:T(8,128)(2,1)} %own.1, s32[]{:T(128)S(6)} %select_n.42, s32[]{:T(128)S(6)} %select_n.41), kind=kLoop, calls=%fused_computation.9 | loop fusion | bytes 458760 | tf_op jit(solution)/shard_map/dynamic_slice | solution.py:457
  3.9 2.6 %collective-permute-start.2 = (bf16[22,8,256]{2,1,0:T(8,128)(2,1)S(1)}, bf16[22,8,256]{2,1,0:T(8,128)(2,1)S(1)}, u32[]{:S(2)}, u32[]{:S(2)}) collective-permute-start(bf16[22,8,256]{2,1,0:T(8,128)(2,1)S(1)} %get-tuple-element.23), channel_id=1, source_target_pairs={{0,1},{1,0},{2,3},{3,2},{4,5},{5,4},{6,7},{7,6},{8,9},{9,8},{10,11... | collective-permute-start | bytes 270344 | tf_op jit(solution)/shard_map/ppermute | solution.py:428
  7.2 1.9 %prepare.1 = (bf16[2,256,768]{2,1,0:T(8,128)(2,1)S(1)}, f32[2,32,768]{2,1,0:T(8,128)S(1)}, bf16[2,3,256,256]{3,2,1,0:T(8,128)(2,1)S(1)}, bf16[3,128,256]{2,1,0:T(8,128)(2,1)S(1)}) custom-call(bf16[2,256,768]{2,1,0:T(8,128)(2,1)S(1)} %copy-done.9, f32[5,5,2,768]{3,2,1,0:T(2,128)S(1)} %bitcast.5, bf16[2,24,32,32]{3,2,1,0:T(8,128)(2,1)S(1)} %copy-done.10, ...), custom_call_target="tpu_custom_call" | custom-call | flops 2000000000 | bytes 4000000 | tf_op jit(solution)/shard_map/prepare/pallas_call | solution.py:479
  9.8 13.4 %first.1 = (bf16[16,48,256]{2,1,0:T(8,128)(2,1)S(1)}, bf16[16,48,512]{2,1,0:T(8,128)(2,1)S(1)}, bf16[144,128]{1,0:T(8,128)(2,1)S(1)}) custom-call(bf16[8,32,256]{2,1,0:T(8,128)(2,1)S(1)} %copy-done.3, bf16[7,32,256]{2,1,0:T(8,128)(2,1)S(1)} %collective-permute-done.row_0, bf16[7,32,256]{2,1,0:T(8,128)(2,1)S(1)} %collective-permute-done.1.row_1, ...), custom_call_target="tpu_custom_call" | custom-call | tf_op jit(solution)/shard_map/first/pallas_call | solution.py:531
  23.2 4.7 %collective-permute-start.4 = (bf16[144,128]{1,0:T(8,128)(2,1)S(1)}, bf16[144,128]{1,0:T(8,128)(2,1)S(1)}, u32[]{:S(2)}, u32[]{:S(2)}) collective-permute-start(bf16[144,128]{1,0:T(8,128)(2,1)S(1)} %get-tuple-element.17), channel_id=1, source_target_pairs={{0,8},{8,0},{16,24},{24,16},{1,9},{9,1},{17,25},{25,17},{2,10},{10... | collective-permute-start | bytes 110600 | tf_op jit(solution)/shard_map/ppermute | solution.py:402
  28.0 1.7 %collective-permute-start.5 = (bf16[144,128]{1,0:T(8,128)(2,1)S(1)}, bf16[144,128]{1,0:T(8,128)(2,1)S(1)}, u32[]{:S(2)}, u32[]{:S(2)}) collective-permute-start(bf16[144,128]{1,0:T(8,128)(2,1)S(1)} %get-tuple-element.17), channel_id=1, source_target_pairs={{0,16},{8,24},{16,0},{24,8},{1,17},{9,25},{17,1},{25,9},{2,18},{10... | collective-permute-start | bytes 110600 | tf_op jit(solution)/shard_map/ppermute | solution.py:402
  29.7 2.2 %collective-permute-done.5 = bf16[144,128]{1,0:T(8,128)(2,1)S(1)} collective-permute-done((bf16[144,128]{1,0:T(8,128)(2,1)S(1)}, bf16[144,128]{1,0:T(8,128)(2,1)S(1)}, u32[]{:S(2)}, u32[]{:S(2)}) %collective-permute-start.5) | collective-permute-done | bytes 36896 | tf_op jit(solution)/shard_map/ppermute | solution.py:402
  31.9 1.2 %collective-permute-done.6 = bf16[144,128]{1,0:T(8,128)(2,1)S(1)} collective-permute-done((bf16[144,128]{1,0:T(8,128)(2,1)S(1)}, bf16[144,128]{1,0:T(8,128)(2,1)S(1)}, u32[]{:S(2)}, u32[]{:S(2)}) %collective-permute-start.6) | collective-permute-done | bytes 36896 | tf_op jit(solution)/shard_map/ppermute | solution.py:402
  33.1 4.8 %collective-permute-start.7 = (bf16[144,128]{1,0:T(8,128)(2,1)S(1)}, bf16[144,128]{1,0:T(8,128)(2,1)S(1)}, u32[]{:S(2)}, u32[]{:S(2)}) collective-permute-start(bf16[144,128]{1,0:T(8,128)(2,1)S(1)} %add_convert_fusion.3), channel_id=1, source_target_pairs={{0,1},{1,0},{2,3},{3,2},{4,5},{5,4},{6,7},{7,6},{8,9},{9,8},{10,11... | collective-permute-start | bytes 110600 | tf_op jit(solution)/shard_map/ppermute | solution.py:402
  37.9 1.6 %collective-permute-start.8 = (bf16[144,128]{1,0:T(8,128)(2,1)S(1)}, bf16[144,128]{1,0:T(8,128)(2,1)S(1)}, u32[]{:S(2)}, u32[]{:S(2)}) collective-permute-start(bf16[144,128]{1,0:T(8,128)(2,1)S(1)} %add_convert_fusion.3), channel_id=1, source_target_pairs={{0,2},{1,3},{2,0},{3,1},{4,6},{5,7},{6,4},{7,5},{8,10},{9,11},{10,... | collective-permute-start | bytes 110600 | tf_op jit(solution)/shard_map/ppermute | solution.py:402
  40.5 1.4 %collective-permute-done.8 = bf16[144,128]{1,0:T(8,128)(2,1)S(1)} collective-permute-done((bf16[144,128]{1,0:T(8,128)(2,1)S(1)}, bf16[144,128]{1,0:T(8,128)(2,1)S(1)}, u32[]{:S(2)}, u32[]{:S(2)}) %collective-permute-start.8) | collective-permute-done | bytes 36896 | tf_op jit(solution)/shard_map/ppermute | solution.py:402
  41.9 2.5 %collective-permute-done.9 = bf16[144,128]{1,0:T(8,128)(2,1)S(1)} collective-permute-done((bf16[144,128]{1,0:T(8,128)(2,1)S(1)}, bf16[144,128]{1,0:T(8,128)(2,1)S(1)}, u32[]{:S(2)}, u32[]{:S(2)}) %collective-permute-start.9) | collective-permute-done | bytes 36896 | tf_op jit(solution)/shard_map/ppermute | solution.py:402
  44.4 2.2 %collective-permute-start.10 = (bf16[144,128]{1,0:T(8,128)(2,1)S(1)}, bf16[144,128]{1,0:T(8,128)(2,1)S(1)}, u32[]{:S(2)}, u32[]{:S(2)}) collective-permute-start(bf16[144,128]{1,0:T(8,128)(2,1)S(1)} %add_convert_fusion.2.payload), channel_id=1, source_target_pairs={{0,4},{1,5},{2,6},{3,7},{4,0},{5,1},{6,2},{7,3},{8,12},{9,13},{10,... | collective-permute-start | bytes 110600 | tf_op jit(solution)/shard_map/ppermute | solution.py:402
  46.6 3.0 %collective-permute-done.10.other = bf16[144,128]{1,0:T(8,128)(2,1)S(1)} collective-permute-done((bf16[144,128]{1,0:T(8,128)(2,1)S(1)}, bf16[144,128]{1,0:T(8,128)(2,1)S(1)}, u32[]{:S(2)}, u32[]{:S(2)}) %collective-permute-start.10) | collective-permute-done | bytes 36896 | tf_op jit(solution)/shard_map/ppermute | solution.py:402
  49.6 12.7 %second.1 = (bf16[10,48,256]{2,1,0:T(8,128)(2,1)S(1)}, bf16[10,48,512]{2,1,0:T(8,128)(2,1)S(1)}, bf16[144,128]{1,0:T(8,128)(2,1)S(1)}) custom-call(bf16[16,48,256]{2,1,0:T(8,128)(2,1)S(1)} %get-tuple-element.15.mixed, bf16[16,48,512]{2,1,0:T(8,128)(2,1)S(1)} %get-tuple-element.16.query, bf16[144,128]{1,0:T(8,128)(2,1)S(1)} %add_convert_fusion.2.payload, ...), custom_call_target="tpu_custom_call" | custom-call | tf_op jit(solution)/shard_map/second/pallas_call | solution.py:545
  63.2 1.0 %collective-permute-start.13 = (bf16[144,128]{1,0:T(8,128)(2,1)S(1)}, bf16[144,128]{1,0:T(8,128)(2,1)S(1)}, u32[]{:S(2)}, u32[]{:S(2)}) collective-permute-start(bf16[144,128]{1,0:T(8,128)(2,1)S(1)} %get-tuple-element.20), channel_id=1, source_target_pairs={{0,24},{8,16},{16,8},{24,0},{1,25},{9,17},{17,9},{25,1},{2,26},{10... | collective-permute-start | bytes 110600 | tf_op jit(solution)/shard_map/ppermute | solution.py:402
  64.3 2.4 %collective-permute-done.12 = bf16[144,128]{1,0:T(8,128)(2,1)S(1)} collective-permute-done((bf16[144,128]{1,0:T(8,128)(2,1)S(1)}, bf16[144,128]{1,0:T(8,128)(2,1)S(1)}, u32[]{:S(2)}, u32[]{:S(2)}) %collective-permute-start.12) | collective-permute-done | bytes 36896 | tf_op jit(solution)/shard_map/ppermute | solution.py:402
  67.0 1.3 %collective-permute-start.14 = (bf16[144,128]{1,0:T(8,128)(2,1)S(1)}, bf16[144,128]{1,0:T(8,128)(2,1)S(1)}, u32[]{:S(2)}, u32[]{:S(2)}) collective-permute-start(bf16[144,128]{1,0:T(8,128)(2,1)S(1)} %add_convert_fusion.1), channel_id=1, source_target_pairs={{0,1},{1,0},{2,3},{3,2},{4,5},{5,4},{6,7},{7,6},{8,9},{9,8},{10,11... | collective-permute-start | bytes 110600 | tf_op jit(solution)/shard_map/ppermute | solution.py:402
  68.4 2.2 %collective-permute-start.16 = (bf16[144,128]{1,0:T(8,128)(2,1)S(1)}, bf16[144,128]{1,0:T(8,128)(2,1)S(1)}, u32[]{:S(2)}, u32[]{:S(2)}) collective-permute-start(bf16[144,128]{1,0:T(8,128)(2,1)S(1)} %add_convert_fusion.1), channel_id=1, source_target_pairs={{0,3},{1,2},{2,1},{3,0},{4,7},{5,6},{6,5},{7,4},{8,11},{9,10},{10,... | collective-permute-start | bytes 110600 | tf_op jit(solution)/shard_map/ppermute | solution.py:402
  71.1 1.2 %collective-permute-done.15 = bf16[144,128]{1,0:T(8,128)(2,1)S(1)} collective-permute-done((bf16[144,128]{1,0:T(8,128)(2,1)S(1)}, bf16[144,128]{1,0:T(8,128)(2,1)S(1)}, u32[]{:S(2)}, u32[]{:S(2)}) %collective-permute-start.15) | collective-permute-done | bytes 36896 | tf_op jit(solution)/shard_map/ppermute | solution.py:402
  72.3 1.0 %collective-permute-done.16 = bf16[144,128]{1,0:T(8,128)(2,1)S(1)} collective-permute-done((bf16[144,128]{1,0:T(8,128)(2,1)S(1)}, bf16[144,128]{1,0:T(8,128)(2,1)S(1)}, u32[]{:S(2)}, u32[]{:S(2)}) %collective-permute-start.16) | collective-permute-done | bytes 36896 | tf_op jit(solution)/shard_map/ppermute | solution.py:402
  73.3 3.0 %collective-permute-start.17 = (bf16[144,128]{1,0:T(8,128)(2,1)S(1)}, bf16[144,128]{1,0:T(8,128)(2,1)S(1)}, u32[]{:S(2)}, u32[]{:S(2)}) collective-permute-start(bf16[144,128]{1,0:T(8,128)(2,1)S(1)} %add_convert_fusion.payload), channel_id=1, source_target_pairs={{0,4},{1,5},{2,6},{3,7},{4,0},{5,1},{6,2},{7,3},{8,12},{9,13},{10,... | collective-permute-start | bytes 110600 | tf_op jit(solution)/shard_map/ppermute | solution.py:402
  76.4 1.8 %collective-permute-done.17.other = bf16[144,128]{1,0:T(8,128)(2,1)S(1)} collective-permute-done((bf16[144,128]{1,0:T(8,128)(2,1)S(1)}, bf16[144,128]{1,0:T(8,128)(2,1)S(1)}, u32[]{:S(2)}, u32[]{:S(2)}) %collective-permute-start.17) | collective-permute-done | bytes 36896 | tf_op jit(solution)/shard_map/ppermute | solution.py:402
  78.3 3.3 %last.1 = (bf16[8,32,256]{2,1,0:T(8,128)(2,1)}, f32[4,8,32]{2,1,0:T(8,128)}) custom-call(bf16[10,48,256]{2,1,0:T(8,128)(2,1)S(1)} %get-tuple-element.18.mixed, bf16[10,48,512]{2,1,0:T(8,128)(2,1)S(1)} %get-tuple-element.19.query, bf16[144,128]{1,0:T(8,128)(2,1)S(1)} %add_convert_fusion.payload, bf16[144,128]{1,0:T(8,128)(2,1)S(1)} %collective-permute-done.17.other, ...), custom_call_target="tpu_custom_call" | custom-call | tf_op jit(solution)/shard_map/last/pallas_call | solution.py:557
  (53 shorter events, 6.5 us)
Async XLA Ops:
  1.6 1.5 %collective-permute-start = (bf16[7,32,256]{2,1,0:T(8,128)(2,1)S(1)}, bf16[7,32,256]{2,1,0:T(8,128)(2,1)S(1)}, u32[]{:S(2)}, u32[]{:S(2)}) collective-permute-start(bf16[7,32,256]{2,1,0:T(8,128)(2,1)S(1)} %get-tuple-element.27), channel_id=1, source_target_pairs={{0,8},{8,0},{16,24},{24,16},{1,9},{9,1},{17,25},{25,17},{2,10},{10... | collective-permute-start | bytes 344072 | tf_op jit(solution)/shard_map/ppermute | solution.py:428
  2.2 1.0 %collective-permute-start.1 = (bf16[7,32,256]{2,1,0:T(8,128)(2,1)S(1)}, bf16[7,32,256]{2,1,0:T(8,128)(2,1)S(1)}, u32[]{:S(2)}, u32[]{:S(2)}) collective-permute-start(bf16[7,32,256]{2,1,0:T(8,128)(2,1)S(1)} %get-tuple-element.26), channel_id=1, source_target_pairs={{8,16},{16,8},{9,17},{17,9},{10,18},{18,10},{11,19},{19,11},{12,20... | collective-permute-start | bytes 344072 | tf_op jit(solution)/shard_map/ppermute | solution.py:428
  2.9 4.3 %copy-start.9 = (bf16[2,256,768]{2,1,0:T(8,128)(2,1)S(1)}, bf16[2,256,768]{2,1,0:T(8,128)(2,1)}, u32[]{:S(2)}) copy-start(bf16[2,256,768]{2,1,0:T(8,128)(2,1)} %qkv.1) | copy-start | bytes 2359300
  3.8 3.4 %copy-start.10 = (bf16[2,24,32,32]{3,2,1,0:T(8,128)(2,1)S(1)}, bf16[2,24,32,32]{3,2,1,0:T(8,128)(2,1)}, u32[]{:S(2)}) copy-start(bf16[2,24,32,32]{3,2,1,0:T(8,128)(2,1)} %group.1) | copy-start | bytes 294916
  3.8 3.4 %copy-start.11 = (f32[2,5,5,768]{3,0,2,1:T(2,128)S(1)}, f32[2,5,5,768]{3,0,2,1:T(2,128)}, u32[]{:S(2)}) copy-start(f32[2,5,5,768]{3,0,2,1:T(2,128)} %param.22) | copy-start | bytes 460804
  3.8 3.4 %copy-start.12 = (bf16[3,3,4,256]{3,2,1,0:T(4,128)(2,1)S(1)}, bf16[3,3,4,256]{3,2,1,0:T(4,128)(2,1)}, u32[]{:S(2)}) copy-start(bf16[3,3,4,256]{3,2,1,0:T(4,128)(2,1)} %head.1) | copy-start | bytes 55300
  3.9 5.3 %collective-permute-start.2 = (bf16[22,8,256]{2,1,0:T(8,128)(2,1)S(1)}, bf16[22,8,256]{2,1,0:T(8,128)(2,1)S(1)}, u32[]{:S(2)}, u32[]{:S(2)}) collective-permute-start(bf16[22,8,256]{2,1,0:T(8,128)(2,1)S(1)} %get-tuple-element.23), channel_id=1, source_target_pairs={{0,1},{1,0},{2,3},{3,2},{4,5},{5,4},{6,7},{7,6},{8,9},{9,8},{10,11... | collective-permute-start | bytes 270344 | tf_op jit(solution)/shard_map/ppermute | solution.py:428
  6.5 2.7 %collective-permute-start.3 = (bf16[22,8,256]{2,1,0:T(8,128)(2,1)S(1)}, bf16[22,8,256]{2,1,0:T(8,128)(2,1)S(1)}, u32[]{:S(2)}, u32[]{:S(2)}) collective-permute-start(bf16[22,8,256]{2,1,0:T(8,128)(2,1)S(1)} %get-tuple-element.22), channel_id=1, source_target_pairs={{1,2},{2,1},{3,4},{4,3},{5,6},{6,5},{9,10},{10,9},{11,12},{12,11},... | collective-permute-start | bytes 270344 | tf_op jit(solution)/shard_map/ppermute | solution.py:428
  9.8 39.8 %copy-start.2 = (bf16[2,512,256]{2,1,0:T(8,128)(2,1)S(1)}, bf16[2,512,256]{2,1,0:T(8,128)(2,1)}, u32[]{:S(2)}) copy-start(bf16[2,512,256]{2,1,0:T(8,128)(2,1)} %out_weight.3) | copy-start | bytes 1572868
  23.2 6.5 %collective-permute-start.4 = (bf16[144,128]{1,0:T(8,128)(2,1)S(1)}, bf16[144,128]{1,0:T(8,128)(2,1)S(1)}, u32[]{:S(2)}, u32[]{:S(2)}) collective-permute-start(bf16[144,128]{1,0:T(8,128)(2,1)S(1)} %get-tuple-element.17), channel_id=1, source_target_pairs={{0,8},{8,0},{16,24},{24,16},{1,9},{9,1},{17,25},{25,17},{2,10},{10... | collective-permute-start | bytes 110600 | tf_op jit(solution)/shard_map/ppermute | solution.py:402
  28.0 4.0 %collective-permute-start.5 = (bf16[144,128]{1,0:T(8,128)(2,1)S(1)}, bf16[144,128]{1,0:T(8,128)(2,1)S(1)}, u32[]{:S(2)}, u32[]{:S(2)}) collective-permute-start(bf16[144,128]{1,0:T(8,128)(2,1)S(1)} %get-tuple-element.17), channel_id=1, source_target_pairs={{0,16},{8,24},{16,0},{24,8},{1,17},{9,25},{17,1},{25,9},{2,18},{10... | collective-permute-start | bytes 110600 | tf_op jit(solution)/shard_map/ppermute | solution.py:402
  29.7 3.4 %collective-permute-start.6 = (bf16[144,128]{1,0:T(8,128)(2,1)S(1)}, bf16[144,128]{1,0:T(8,128)(2,1)S(1)}, u32[]{:S(2)}, u32[]{:S(2)}) collective-permute-start(bf16[144,128]{1,0:T(8,128)(2,1)S(1)} %get-tuple-element.17), channel_id=1, source_target_pairs={{0,24},{8,16},{16,8},{24,0},{1,25},{9,17},{17,9},{25,1},{2,26},{10... | collective-permute-start | bytes 110600 | tf_op jit(solution)/shard_map/ppermute | solution.py:402
  33.1 7.3 %collective-permute-start.7 = (bf16[144,128]{1,0:T(8,128)(2,1)S(1)}, bf16[144,128]{1,0:T(8,128)(2,1)S(1)}, u32[]{:S(2)}, u32[]{:S(2)}) collective-permute-start(bf16[144,128]{1,0:T(8,128)(2,1)S(1)} %add_convert_fusion.3), channel_id=1, source_target_pairs={{0,1},{1,0},{2,3},{3,2},{4,5},{5,4},{6,7},{7,6},{8,9},{9,8},{10,11... | collective-permute-start | bytes 110600 | tf_op jit(solution)/shard_map/ppermute | solution.py:402
  37.9 4.0 %collective-permute-start.8 = (bf16[144,128]{1,0:T(8,128)(2,1)S(1)}, bf16[144,128]{1,0:T(8,128)(2,1)S(1)}, u32[]{:S(2)}, u32[]{:S(2)}) collective-permute-start(bf16[144,128]{1,0:T(8,128)(2,1)S(1)} %add_convert_fusion.3), channel_id=1, source_target_pairs={{0,2},{1,3},{2,0},{3,1},{4,6},{5,7},{6,4},{7,5},{8,10},{9,11},{10,... | collective-permute-start | bytes 110600 | tf_op jit(solution)/shard_map/ppermute | solution.py:402
  39.5 4.9 %collective-permute-start.9 = (bf16[144,128]{1,0:T(8,128)(2,1)S(1)}, bf16[144,128]{1,0:T(8,128)(2,1)S(1)}, u32[]{:S(2)}, u32[]{:S(2)}) collective-permute-start(bf16[144,128]{1,0:T(8,128)(2,1)S(1)} %add_convert_fusion.3), channel_id=1, source_target_pairs={{0,3},{1,2},{2,1},{3,0},{4,7},{5,6},{6,5},{7,4},{8,11},{9,10},{10,... | collective-permute-start | bytes 110600 | tf_op jit(solution)/shard_map/ppermute | solution.py:402
  44.4 5.2 %copy-start.8 = (f32[2,256]{1,0:T(2,128)S(1)}, f32[2,256]{1,0:T(2,128)}, u32[]{:S(2)}) copy-start(f32[2,256]{1,0:T(2,128)} %out_bias.3) | copy-start | bytes 6148
  44.4 5.2 %collective-permute-start.10 = (bf16[144,128]{1,0:T(8,128)(2,1)S(1)}, bf16[144,128]{1,0:T(8,128)(2,1)S(1)}, u32[]{:S(2)}, u32[]{:S(2)}) collective-permute-start(bf16[144,128]{1,0:T(8,128)(2,1)S(1)} %add_convert_fusion.2.payload), channel_id=1, source_target_pairs={{0,4},{1,5},{2,6},{3,7},{4,0},{5,1},{6,2},{7,3},{8,12},{9,13},{10,... | collective-permute-start | bytes 110600 | tf_op jit(solution)/shard_map/ppermute | solution.py:402
  62.4 1.9 %collective-permute-start.11 = (bf16[144,128]{1,0:T(8,128)(2,1)S(1)}, bf16[144,128]{1,0:T(8,128)(2,1)S(1)}, u32[]{:S(2)}, u32[]{:S(2)}) collective-permute-start(bf16[144,128]{1,0:T(8,128)(2,1)S(1)} %get-tuple-element.20), channel_id=1, source_target_pairs={{0,8},{8,0},{16,24},{24,16},{1,9},{9,1},{17,25},{25,17},{2,10},{10... | collective-permute-start | bytes 110600 | tf_op jit(solution)/shard_map/ppermute | solution.py:402
  62.4 4.2 %collective-permute-start.12 = (bf16[144,128]{1,0:T(8,128)(2,1)S(1)}, bf16[144,128]{1,0:T(8,128)(2,1)S(1)}, u32[]{:S(2)}, u32[]{:S(2)}) collective-permute-start(bf16[144,128]{1,0:T(8,128)(2,1)S(1)} %get-tuple-element.20), channel_id=1, source_target_pairs={{0,16},{8,24},{16,0},{24,8},{1,17},{9,25},{17,1},{25,9},{2,18},{10... | collective-permute-start | bytes 110600 | tf_op jit(solution)/shard_map/ppermute | solution.py:402
  63.2 3.8 %collective-permute-start.13 = (bf16[144,128]{1,0:T(8,128)(2,1)S(1)}, bf16[144,128]{1,0:T(8,128)(2,1)S(1)}, u32[]{:S(2)}, u32[]{:S(2)}) collective-permute-start(bf16[144,128]{1,0:T(8,128)(2,1)S(1)} %get-tuple-element.20), channel_id=1, source_target_pairs={{0,24},{8,16},{16,8},{24,0},{1,25},{9,17},{17,9},{25,1},{2,26},{10... | collective-permute-start | bytes 110600 | tf_op jit(solution)/shard_map/ppermute | solution.py:402
  67.0 4.0 %collective-permute-start.14 = (bf16[144,128]{1,0:T(8,128)(2,1)S(1)}, bf16[144,128]{1,0:T(8,128)(2,1)S(1)}, u32[]{:S(2)}, u32[]{:S(2)}) collective-permute-start(bf16[144,128]{1,0:T(8,128)(2,1)S(1)} %add_convert_fusion.1), channel_id=1, source_target_pairs={{0,1},{1,0},{2,3},{3,2},{4,5},{5,4},{6,7},{7,6},{8,9},{9,8},{10,11... | collective-permute-start | bytes 110600 | tf_op jit(solution)/shard_map/ppermute | solution.py:402
  68.3 4.0 %collective-permute-start.15 = (bf16[144,128]{1,0:T(8,128)(2,1)S(1)}, bf16[144,128]{1,0:T(8,128)(2,1)S(1)}, u32[]{:S(2)}, u32[]{:S(2)}) collective-permute-start(bf16[144,128]{1,0:T(8,128)(2,1)S(1)} %add_convert_fusion.1), channel_id=1, source_target_pairs={{0,2},{1,3},{2,0},{3,1},{4,6},{5,7},{6,4},{7,5},{8,10},{9,11},{10,... | collective-permute-start | bytes 110600 | tf_op jit(solution)/shard_map/ppermute | solution.py:402
  68.4 4.9 %collective-permute-start.16 = (bf16[144,128]{1,0:T(8,128)(2,1)S(1)}, bf16[144,128]{1,0:T(8,128)(2,1)S(1)}, u32[]{:S(2)}, u32[]{:S(2)}) collective-permute-start(bf16[144,128]{1,0:T(8,128)(2,1)S(1)} %add_convert_fusion.1), channel_id=1, source_target_pairs={{0,3},{1,2},{2,1},{3,0},{4,7},{5,6},{6,5},{7,4},{8,11},{9,10},{10,... | collective-permute-start | bytes 110600 | tf_op jit(solution)/shard_map/ppermute | solution.py:402
  73.3 5.0 %collective-permute-start.17 = (bf16[144,128]{1,0:T(8,128)(2,1)S(1)}, bf16[144,128]{1,0:T(8,128)(2,1)S(1)}, u32[]{:S(2)}, u32[]{:S(2)}) collective-permute-start(bf16[144,128]{1,0:T(8,128)(2,1)S(1)} %add_convert_fusion.payload), channel_id=1, source_target_pairs={{0,4},{1,5},{2,6},{3,7},{4,0},{5,1},{6,2},{7,3},{8,12},{9,13},{10,... | collective-permute-start | bytes 110600 | tf_op jit(solution)/shard_map/ppermute | solution.py:402
  (8 other events, 14.6 us)

commit v6 on v5

--- a/solution.py
+++ b/solution.py
@@ -12,12 +12,19 @@
 SIDE = 8
 REACH = 7
 KEY_ROWS = 16
+TILE = 16
+PARTS = 4
 F32 = jnp.float32
 BF16 = jnp.bfloat16
 
 
-def hard_swish(value):
-    return value * jnp.minimum(jnp.maximum(value * (1.0 / 6.0) + 0.5, 0.0), 1.0)
+def six_hard_swish(value):
+    return value * jnp.minimum(jnp.maximum(value + 3.0, 0.0), 6.0)
+
+
+def parted(count, parts):
+    cuts = [count * k // parts for k in range(parts + 1)]
+    return [(a, b - a) for a, b in zip(cuts, cuts[1:]) if b > a]
 
 
 def clear_outside(ref, halo, cols):
@@ -39,17 +46,6 @@
     @pl.when(col == lax.axis_size("col") - 1)
     def _():
         ref[:, cols : cols + SIDE, :] = jnp.zeros((rows, SIDE, ref.shape[2]), ref.dtype)
-
-
-def grouped_loop(count, most, body):
-    size = next(n for n in range(min(most, count), 0, -1) if count % n == 0)
-
-    def group(index, carry):
-        for r in range(size):
-            body(index * size + r)
-        return carry
-
-    lax.fori_loop(0, count // size, group, 0)
 
 
 def flat(value):
@@ -62,10 +58,28 @@
     return across == along
 
 
+def depthwise_row(rows, taps, size, width):
+    rows = [row.reshape(width // TILE, TILE, LANES) for row in rows]
+    total = None
+    for b in range(size):
+        part = None
+        for a in range(size):
+            term = rows[a] * taps(a, b)[None]
+            part = term if part is None else part + term
+        part = part.reshape(width, LANES).astype(F32)
+        if b != size // 2:
+            part = pltpu.roll(part, (size // 2 - b) % width, 0)
+        total = part if total is None else total + part
+    return total
+
+
 def front(x_ref, weights, outs, scratch, halo, tile, head_dim, section):
     expand, expand_bias, depth, depth_bias, project, project_bias = weights[:6]
     mixed_out, query_out, payload_out = outs
-    hidden, spread, total, mixed, qkv, scaled, query, qkv_weight, agg, group, sems = scratch
+    (
+        hidden_0, hidden_1, total, mixed, qkv, query, wide_depth, wide_agg,
+        qkv_weight, agg, group, sems,
+    ) = scratch
     loads = [
         pltpu.make_async_copy(weights[6].at[section], qkv_weight, sems.at[0]),
         pltpu.make_async_copy(weights[7].at[section], agg, sems.at[1]),
@@ -76,48 +90,59 @@
     rows, width, channels = x_ref.shape
     tile_rows, tile_cols = tile
     inner = rows - 2
-    chunk = hidden.shape[2]
-    x = flat(x_ref[...])
-
-    def expanded(step, carry):
-        at = pl.multiple_of(step * chunk, chunk)
-        value = jnp.dot(x, expand[section, :, pl.ds(at, chunk)], preferred_element_type=F32)
-        value = hard_swish(value + expand_bias[section : section + 1, pl.ds(at, chunk)])
-        hidden[...] = value.reshape(rows, width, chunk)
-        clear_outside(hidden, halo, tile_cols)
-
-        def one_row(r):
+    chunk = hidden_0.shape[2]
+    chunks = expand.shape[2] // chunk
+    for index in range(9):
+        taps = depth[index // 3, index % 3, section : section + 1, :] * (1.0 / 6.0)
+        wide_depth[index] = jnp.broadcast_to(taps, (TILE, taps.shape[1])).astype(BF16)
+    total[...] = 6.0 * (flat(x_ref[1 : rows - 1]).astype(F32) + project_bias[section : section + 1, :])
+
+    def expand_rows(out, at, first, size):
+        value = jnp.dot(
+            flat(x_ref[first : first + size]), expand[section, :, pl.ds(at, chunk)],
+            preferred_element_type=F32,
+        )
+        value = (value + expand_bias[section : section + 1, pl.ds(at, chunk)]).astype(BF16)
+        out[first : first + size] = six_hard_swish(value).reshape(size, width, chunk)
+
+    def spread_rows(hidden, at, first, size):
+        spread = []
+        for r in range(first, first + size):
+            lanes = []
             for lane in range(0, chunk, LANES):
                 here = pl.ds(pl.multiple_of(at + lane, LANES), LANES)
-                above, level, below = (hidden[r + a, :, lane : lane + LANES] for a in range(3))
-                parts = [
-                    above * depth[0, b, section : section + 1, here]
-                    + level * depth[1, b, section : section + 1, here]
-                    + below * depth[2, b, section : section + 1, here]
-                    for b in range(3)
-                ]
-                value = parts[1] + pltpu.roll(parts[0], 1, 0) + pltpu.roll(parts[2], width - 1, 0)
-                value = hard_swish(value + depth_bias[section : section + 1, here])
-                spread[r, :, lane : lane + LANES] = value.astype(BF16)
-
-        grouped_loop(inner, 7, one_row)
-        product = jnp.dot(
-            flat(spread[...]), project[section, pl.ds(at, chunk), :], preferred_element_type=F32
-        )
-
-        @pl.when(step == 0)
-        def _():
-            total[...] = product
-
-        @pl.when(step > 0)
-        def _():
-            total[...] += product
-
+                value = depthwise_row(
+                    [hidden[r + a, :, lane : lane + LANES] for a in range(3)],
+                    lambda a, b: wide_depth[3 * a + b, :, here], 3, width,
+                )
+                value = (value + depth_bias[section : section + 1, here]).astype(BF16)
+                lanes.append(six_hard_swish(value))
+            spread.append(jnp.concatenate(lanes, axis=1))
+        pixels = slice(first * width, (first + size) * width)
+        total[pixels] += jnp.dot(
+            jnp.concatenate(spread, axis=0), project[section, pl.ds(at, chunk), :],
+            preferred_element_type=F32,
+        )
+
+    def stage(index, current, following):
+        at = pl.multiple_of(index * chunk, chunk)
+        ahead = pl.multiple_of(jnp.minimum(index + 1, chunks - 1) * chunk, chunk)
+        for (first, size), (from_row, count) in zip(parted(inner, PARTS), parted(rows, PARTS)):
+            expand_rows(following, ahead, from_row, count)
+            spread_rows(current, at, first, size)
+        clear_outside(following, halo, tile_cols)
+
+    for first, size in parted(rows, PARTS):
+        expand_rows(hidden_0, 0, first, size)
+    clear_outside(hidden_0, halo, tile_cols)
+
+    def two_stages(index, carry):
+        stage(2 * index, hidden_0, hidden_1)
+        stage(2 * index + 1, hidden_1, hidden_0)
         return carry
 
-    lax.fori_loop(0, expand.shape[2] // chunk, expanded, 0)
-    value = total[...] + project_bias[section : section + 1, :] + flat(x_ref[1 : rows - 1]).astype(F32)
-    mixed[...] = value.astype(BF16).reshape(inner, width, channels)
+    lax.fori_loop(0, chunks // 2, two_stages, 0)
+    mixed[...] = (total[...] * (1.0 / 6.0)).astype(BF16).reshape(inner, width, channels)
     outer = inner - 4
     stores = [
         pltpu.make_async_copy(mixed.at[pl.ds(2, outer)], mixed_out, sems.at[3]),
@@ -126,111 +151,154 @@
     stores[0].start()
     for load in loads:
         load.wait()
-    value = jnp.dot(flat(mixed[...]), qkv_weight[...], preferred_element_type=F32)
-    qkv[...] = value.reshape(inner, width, 3 * channels)
+    for index in range(25):
+        taps = agg[index : index + 1, :]
+        wide_agg[index] = jnp.broadcast_to(taps, (TILE, taps.shape[1])).astype(BF16)
+    for first, size in parted(inner, PARTS):
+        value = jnp.dot(
+            flat(mixed[first : first + size]), qkv_weight[...], preferred_element_type=F32
+        )
+        qkv[first : first + size] = value.astype(BF16).reshape(size, width, 3 * channels)
     around = halo - 1
     clear_outside(qkv, around, tile_cols)
 
-    def aggregated(kind, first, count):
-        def one_row(r):
-            for lane in range(0, channels, LANES):
-                here = slice(kind * channels + lane, kind * channels + lane + LANES)
-                value = None
-                for b in range(5):
-                    part = None
-                    for a in range(5):
-                        term = qkv[first + r + a, :, here] * agg[5 * a + b : 5 * a + b + 1, here]
-                        part = term if part is None else part + term
-                    if b != 2:
-                        part = pltpu.roll(part, (2 - b) % width, 0)
-                    value = part if value is None else value + part
-                scaled[r, :, lane : lane + LANES] = value.astype(BF16)
-
-        grouped_loop(count, 5, one_row)
-        value = jnp.dot(flat(scaled[0:count]), group[kind], preferred_element_type=F32)
-        return value.reshape(count, width, channels)
-
-    query[:, :, 0:channels] = jnp.maximum(qkv[2 : inner - 2, :, 0:channels], 0.0).astype(BF16)
-    query[:, :, channels : 2 * channels] = jnp.maximum(
-        aggregated(0, 0, outer), 0.0
-    ).astype(BF16)
-
+    def aggregated(kind, first, size):
+        scaled = []
+        for r in range(size):
+            lanes = []
+            for lane in range(kind * channels, (kind + 1) * channels, LANES):
+                here = slice(lane, lane + LANES)
+                value = depthwise_row(
+                    [qkv[first + r + a, :, here] for a in range(5)],
+                    lambda a, b: wide_agg[5 * a + b, :, here], 5, width,
+                )
+                lanes.append(value.astype(BF16))
+            scaled.append(jnp.concatenate(lanes, axis=1))
+        value = jnp.dot(
+            jnp.concatenate(scaled, axis=0), group[kind], preferred_element_type=F32
+        )
+        return value.astype(BF16).reshape(size, width, channels)
+
+    query[:, :, 0:channels] = jnp.maximum(qkv[2 : inner - 2, :, 0:channels], 0.0)
+    size = next(n for n in range(5, 0, -1) if outer % n == 0)
+
+    def query_rows(index, carry):
+        at = index * size
+        query[pl.ds(at, size), :, channels : 2 * channels] = jnp.maximum(
+            aggregated(0, at, size), 0.0
+        )
+        return carry
+
+    lax.fori_loop(0, outer // size, query_rows, 0)
     stores[1].start()
-
-    def own(value):
-        return flat(value[:, 0:tile_cols, :])
+    size = next(n for n in range(4, 0, -1) if tile_rows % n == 0)
+
+    def summed(key, value):
+        key = jnp.maximum(flat(key[:, 0:tile_cols]), 0.0)
+        value = flat(value[:, 0:tile_cols])
+        products = [
+            lax.dot_general(
+                key[:, lane : lane + LANES], value[:, lane : lane + LANES],
+                (((0,), (0,)), ((), ())), preferred_element_type=F32,
+            )
+            for lane in range(0, channels, LANES)
+        ]
+        return products, jnp.sum(key.astype(F32), axis=0, keepdims=True)
 
     mine = slice(around, around + tile_rows)
-    keys = [own(qkv[mine, :, channels : 2 * channels]), own(aggregated(1, around - 2, tile_rows))]
-    values = [
-        own(qkv[mine, :, 2 * channels : 3 * channels]),
-        own(aggregated(2, around - 2, tile_rows)),
-    ]
+    products, sums = summed(
+        qkv[mine, :, channels : 2 * channels], qkv[mine, :, 2 * channels : 3 * channels]
+    )
+
+    def grouped_rows(index, carry):
+        at = around - 2 + index * size
+        more, sums = summed(aggregated(1, at, size), aggregated(2, at, size))
+        return [a + b for a, b in zip(carry[0], more)], carry[1] + sums
+
+    more, more_sums = lax.fori_loop(
+        0, tile_rows // size, grouped_rows,
+        ([jnp.zeros((LANES, LANES), F32) for _ in products], jnp.zeros_like(sums)),
+    )
+    products = products + more
+    sums = jnp.concatenate([sums, more_sums], axis=1)
     same = same_head(head_dim)
     summary = jnp.zeros((LANES, LANES), F32)
     key_sums = []
-    index = 0
-    for key, value in zip(keys, values):
-        key = jnp.maximum(key, 0.0)
-        sums = jnp.sum(key, axis=0, keepdims=True)
-        key, value = key.astype(BF16), value.astype(BF16)
-        for lane in range(0, channels, LANES):
-            here = slice(lane, lane + LANES)
-            product = lax.dot_general(
-                key[:, here], value[:, here], (((0,), (0,)), ((), ())), preferred_element_type=F32
-            )
-            product = jnp.where(same, product, 0.0)
-            if index:
-                product = pltpu.roll(product, index * head_dim, 1)
-            summary = summary + product
-            key_sums.append(sums[:, here])
-            index += 1
-    key_sums = jnp.concatenate(
-        key_sums + [jnp.zeros((KEY_ROWS - index, LANES), F32)], axis=0
-    )
+    for index, product in enumerate(products):
+        product = jnp.where(same, product, 0.0)
+        if index:
+            product = pltpu.roll(product, index * head_dim, 1)
+        summary = summary + product
+        key_sums.append(sums[:, index * LANES : (index + 1) * LANES])
+    key_sums.append(jnp.zeros((KEY_ROWS - len(products), LANES), F32))
     payload_out[0:LANES, :] = summary.astype(BF16)
-    payload_out[LANES : LANES + KEY_ROWS, :] = key_sums.astype(BF16)
+    payload_out[LANES : LANES + KEY_ROWS, :] = jnp.concatenate(key_sums, axis=0).astype(BF16)
     for store in stores:
         store.wait()
 
 
 def attend(
-    mixed_in, query_in, payloads, weight, bias, mixed_ref, query_ref, sems, head_dim, section
+    mixed_in, query_in, payloads, weight, bias, mixed_ref, query_ref, sems, head_dim, section, x_ref
 ):
-    loads = [
-        pltpu.make_async_copy(query_in, query_ref, sems.at[0]),
-        pltpu.make_async_copy(mixed_in, mixed_ref, sems.at[1]),
-    ]
-    for load in loads:
-        load.start()
+    rows, width, channels = x_ref.shape
+    groups = parted(rows, PARTS)
+    loads = []
+    for index, (first, size) in enumerate(groups):
+        here = pl.ds(first, size)
+        for at, (source, target) in enumerate(((query_in, query_ref), (mixed_in, mixed_ref))):
+            load = pltpu.make_async_copy(source.at[here], target.at[here], sems.at[at, index])
+            load.start()
+            loads.append(load)
     same = same_head(head_dim)
     square = (LANES, LANES)
     diagonal = lax.broadcasted_iota(jnp.int32, square, 0) == lax.broadcasted_iota(
         jnp.int32, square, 1
     )
     ones = jnp.where(same, 1.0, 0.0).astype(BF16)
+    nothing = jnp.zeros(square, BF16)
     payload = payloads[0][...].astype(F32)
     for part in payloads[1:]:
         payload = payload + part[...].astype(F32)
     packed = payload[0:LANES]
-    for load in loads:
-        load.wait()
-    query = flat(query_ref[...])
-    total = flat(mixed_ref[...]).astype(F32) + bias[section : section + 1, :]
-    for index in range(query.shape[1] // LANES):
+    count = 2 * channels // LANES
+    summaries, sums = [], []
+    for index in range(count):
         summary = packed if index == 0 else pltpu.roll(packed, LANES - index * head_dim, 1)
-        summary = jnp.where(same, summary, 0.0).astype(BF16)
-        sums = payload[LANES + index : LANES + index + 1]
-        sums = jnp.where(diagonal, sums, 0.0).astype(BF16)
-        sums = jnp.dot(sums, ones, preferred_element_type=F32).astype(BF16)
-        part = query[:, index * LANES : (index + 1) * LANES]
-        numer = jnp.dot(part, summary, preferred_element_type=F32)
-        denom = jnp.dot(part, sums, preferred_element_type=F32)
-        attended = (numer / (denom + 1e-6)).astype(BF16)
-        total = total + jnp.dot(
-            attended, weight[section, index * LANES : (index + 1) * LANES, :], preferred_element_type=F32
-        )
-    return total
+        summaries.append(jnp.where(same, summary, 0.0).astype(BF16))
+        keys = payload[LANES + index : LANES + index + 1]
+        keys = jnp.where(diagonal, keys, 0.0).astype(BF16)
+        sums.append(jnp.dot(keys, ones, preferred_element_type=F32).astype(BF16))
+
+    def paired(blocks, index):
+        return jnp.concatenate(
+            [
+                jnp.concatenate([blocks[index], nothing], axis=1),
+                jnp.concatenate([nothing, blocks[index + 1]], axis=1),
+            ],
+            axis=0,
+        )
+
+    summaries = [paired(summaries, index) for index in range(0, count, 2)]
+    sums = [paired(sums, index) for index in range(0, count, 2)]
+    step = 2 * LANES
+    for index, (first, size) in enumerate(groups):
+        for load in loads[2 * index : 2 * index + 2]:
+            load.wait()
+        query = flat(query_ref[first : first + size])
+        parts = []
+        for branch in range(count // 2):
+            part = query[:, branch * step : (branch + 1) * step]
+            numer = jnp.dot(part, summaries[branch], preferred_element_type=F32)
+            denom = jnp.dot(part, sums[branch], preferred_element_type=F32) + 1e-6
+            inverse = pl.reciprocal(denom, approx=True)
+            inverse = inverse * (2.0 - denom * inverse)
+            parts.append((numer * inverse).astype(BF16))
+        value = jnp.dot(
+            jnp.concatenate(parts, axis=1), weight[section], preferred_element_type=F32
+        )
+        value = value + bias[section : section + 1, :]
+        value = value + flat(mixed_ref[first : first + size]).astype(F32)
+        x_ref[first : first + size] = value.astype(BF16).reshape(size, width, channels)
 
 
 def tap(section, a, b):
@@ -317,10 +385,10 @@
 def second_kernel(tile, head_dim, mixed, query, payload, other, out_weight, out_bias, *refs):
     weights, outs, scratch = refs[:9], refs[9:12], refs[12:]
     x_ref, mixed_ref, query_ref, sems = scratch[:4]
-    value = attend(
-        mixed, query, (payload, other), out_weight, out_bias, mixed_ref, query_ref, sems, head_dim, 0
-    )
-    x_ref[...] = value.astype(BF16).reshape(x_ref.shape)
+    attend(
+        mixed, query, (payload, other), out_weight, out_bias, mixed_ref, query_ref, sems, head_dim,
+        0, x_ref,
+    )
     front(x_ref, weights, outs, scratch[4:], REACH - 3, tile, head_dim, 1)
 
 
@@ -330,10 +398,10 @@
 ):
     rows, cols = tile
     width = cols + 2 * SIDE
-    value = attend(
-        mixed, query, (payload, other), out_weight, out_bias, mixed_ref, query_ref, sems, head_dim, 1
-    )
-    x_ref[...] = value.astype(BF16).reshape(x_ref.shape)
+    attend(
+        mixed, query, (payload, other), out_weight, out_bias, mixed_ref, query_ref, sems, head_dim,
+        1, x_ref,
+    )
     clear_outside(x_ref, 1, cols)
     map_out[...] = x_ref[1 : 1 + rows, 0:cols, :]
     total = None
@@ -506,13 +574,14 @@
 
     def front_scratch(count):
         return [
-            pltpu.VMEM((count, width, 256), F32),
-            pltpu.VMEM((count - 2, width, 256), BF16),
+            pltpu.VMEM((count, width, 256), BF16),
+            pltpu.VMEM((count, width, 256), BF16),
             pltpu.VMEM(((count - 2) * width, channels), F32),
             pltpu.VMEM((count - 2, width, channels), BF16),
-            pltpu.VMEM((count - 2, width, 3 * channels), F32),
-            pltpu.VMEM((count - 6, width, channels), BF16),
+            pltpu.VMEM((count - 2, width, 3 * channels), BF16),
             pltpu.VMEM((count - 6, width, 2 * channels), BF16),
+            pltpu.VMEM((9, TILE, expand_weight.shape[2]), BF16),
+            pltpu.VMEM((25, TILE, 3 * channels), BF16),
             pltpu.VMEM(qkv_weight.shape[1:], BF16),
             pltpu.VMEM(taps.shape[1:], F32),
             pltpu.VMEM(group.shape[1:], BF16),
@@ -524,7 +593,7 @@
             pltpu.VMEM((count, width, channels), BF16),
             pltpu.VMEM((count, width, channels), BF16),
             pltpu.VMEM((count, width, 2 * channels), BF16),
-            pltpu.SemaphoreType.DMA((2,)),
+            pltpu.SemaphoreType.DMA((2, PARTS)),
         ]
 
     first_rows = rows + 2 * REACH

time: 82 us -> 82.4 us (level)
    pallas_call x1, Pallas kernels: 13.4 us -> 11.7 us  [local(): pl.pallas_call(functools.partial(first_kernel, tile, head_dim), out_shape...]
    pallas_call x1, Pallas kernels: 3.33 us -> 4.32 us  [local(): pl.pallas_call(functools.partial(last_kernel, tile, head_dim), out_shape=...]
    pallas_call x1, Pallas kernels: 12.7 us -> 13.6 us  [local(): pl.pallas_call(functools.partial(second_kernel, tile, head_dim), out_shap...]
where the time goes in v6:
time: 82.4 us; the launch traced here: 82.2 us
  Pallas kernels  31.6 us (38%)
  starting transfers between devices  29.1 us (35%)
  waiting for transfers between devices  17.8 us (22%)
  local copies, waits for them, and re-layouts  2.42 us (3%)
  between operations  1.1 us (1%)
    ppermute x14, starting transfers between devices, sum_by_permutes(): lax.ppermute(value, axis, [(i, partner(i, stride, radix, k)) for i in ran...  24.6 us
    ppermute x14, waiting for transfers between devices, sum_by_permutes(): lax.ppermute(value, axis, [(i, partner(i, stride, radix, k)) for i in ran...  17.6 us
    pallas_call x1, Pallas kernels, local(): pl.pallas_call(functools.partial(second_kernel, tile, head_dim), out_shap...  13.6 us
    pallas_call x1, Pallas kernels, local(): pl.pallas_call(functools.partial(first_kernel, tile, head_dim), out_shape...  11.7 us
    ppermute x4, starting transfers between devices, pair_exchange(): return lax.ppermute(value, axis, pairs)  4.43 us
    pallas_call x1, Pallas kernels, local(): pl.pallas_call(functools.partial(last_kernel, tile, head_dim), out_shape=...  4.32 us
    pallas_call x1, Pallas kernels, local(): pl.pallas_call(functools.partial(prepare_kernel, head_dim), out_shape=mad...  1.89 us
  transfers between devices with their start and end apart: 18, of which 12 were waited for; matrix products, arithmetic and copies ran while one was open for 0% of the time, Pallas kernels for 2%

profile of v6, /device:TPU:0, one launch (start us, length us, event | category | flops | bytes accessed | tf_op | source)
XLA Modules:
  0.0 82.2 jit_solution(2012556866357580911)
XLA Ops:
  0.6 1.0 %constant_dynamic-slice_fusion.2 = (bf16[7,32,256]{2,1,0:T(8,128)(2,1)S(1)}, bf16[7,32,256]{2,1,0:T(8,128)(2,1)S(1)}) fusion(bf16[8,32,256]{2,1,0:T(8,128)(2,1)} %own.1, s32[]{:T(128)S(6)} %select_n.42, s32[]{:T(128)S(6)} %select_n.41), kind=kLoop, calls=%fused_computation.9 | loop fusion | bytes 458760 | tf_op jit(solution)/shard_map/dynamic_slice | solution.py:525
  3.9 2.6 %collective-permute-start.2 = (bf16[22,8,256]{2,1,0:T(8,128)(2,1)S(1)}, bf16[22,8,256]{2,1,0:T(8,128)(2,1)S(1)}, u32[]{:S(2)}, u32[]{:S(2)}) collective-permute-start(bf16[22,8,256]{2,1,0:T(8,128)(2,1)S(1)} %get-tuple-element.23), channel_id=1, source_target_pairs={{0,1},{1,0},{2,3},{3,2},{4,5},{5,4},{6,7},{7,6},{8,9},{9,8},{10,11... | collective-permute-start | bytes 270344 | tf_op jit(solution)/shard_map/ppermute | solution.py:496
  7.2 1.9 %prepare.1 = (bf16[2,256,768]{2,1,0:T(8,128)(2,1)S(1)}, f32[2,32,768]{2,1,0:T(8,128)S(1)}, bf16[2,3,256,256]{3,2,1,0:T(8,128)(2,1)S(1)}, bf16[3,128,256]{2,1,0:T(8,128)(2,1)S(1)}) custom-call(bf16[2,256,768]{2,1,0:T(8,128)(2,1)S(1)} %copy-done.9, f32[5,5,2,768]{3,2,1,0:T(2,128)S(1)} %bitcast.5, bf16[2,24,32,32]{3,2,1,0:T(8,128)(2,1)S(1)} %copy-done.10, ...), custom_call_target="tpu_custom_call" | custom-call | flops 2000000000 | bytes 4000000 | tf_op jit(solution)/shard_map/prepare/pallas_call | solution.py:547
  9.8 11.7 %first.1 = (bf16[16,48,256]{2,1,0:T(8,128)(2,1)S(1)}, bf16[16,48,512]{2,1,0:T(8,128)(2,1)S(1)}, bf16[144,128]{1,0:T(8,128)(2,1)S(1)}) custom-call(bf16[8,32,256]{2,1,0:T(8,128)(2,1)S(1)} %copy-done.3, bf16[7,32,256]{2,1,0:T(8,128)(2,1)S(1)} %collective-permute-done.row_0, bf16[7,32,256]{2,1,0:T(8,128)(2,1)S(1)} %collective-permute-done.1.row_1, ...), custom_call_target="tpu_custom_call" | custom-call | tf_op jit(solution)/shard_map/first/pallas_call | solution.py:600
  21.6 4.8 %collective-permute-start.4 = (bf16[144,128]{1,0:T(8,128)(2,1)S(1)}, bf16[144,128]{1,0:T(8,128)(2,1)S(1)}, u32[]{:S(2)}, u32[]{:S(2)}) collective-permute-start(bf16[144,128]{1,0:T(8,128)(2,1)S(1)} %get-tuple-element.17), channel_id=1, source_target_pairs={{0,8},{8,0},{16,24},{24,16},{1,9},{9,1},{17,25},{25,17},{2,10},{10... | collective-permute-start | bytes 110600 | tf_op jit(solution)/shard_map/ppermute | solution.py:470
  26.4 1.7 %collective-permute-start.5 = (bf16[144,128]{1,0:T(8,128)(2,1)S(1)}, bf16[144,128]{1,0:T(8,128)(2,1)S(1)}, u32[]{:S(2)}, u32[]{:S(2)}) collective-permute-start(bf16[144,128]{1,0:T(8,128)(2,1)S(1)} %get-tuple-element.17), channel_id=1, source_target_pairs={{0,16},{8,24},{16,0},{24,8},{1,17},{9,25},{17,1},{25,9},{2,18},{10... | collective-permute-start | bytes 110600 | tf_op jit(solution)/shard_map/ppermute | solution.py:470
  28.1 2.2 %collective-permute-done.5 = bf16[144,128]{1,0:T(8,128)(2,1)S(1)} collective-permute-done((bf16[144,128]{1,0:T(8,128)(2,1)S(1)}, bf16[144,128]{1,0:T(8,128)(2,1)S(1)}, u32[]{:S(2)}, u32[]{:S(2)}) %collective-permute-start.5) | collective-permute-done | bytes 36896 | tf_op jit(solution)/shard_map/ppermute | solution.py:470
  30.3 1.2 %collective-permute-done.6 = bf16[144,128]{1,0:T(8,128)(2,1)S(1)} collective-permute-done((bf16[144,128]{1,0:T(8,128)(2,1)S(1)}, bf16[144,128]{1,0:T(8,128)(2,1)S(1)}, u32[]{:S(2)}, u32[]{:S(2)}) %collective-permute-start.6) | collective-permute-done | bytes 36896 | tf_op jit(solution)/shard_map/ppermute | solution.py:470
  31.5 4.8 %collective-permute-start.7 = (bf16[144,128]{1,0:T(8,128)(2,1)S(1)}, bf16[144,128]{1,0:T(8,128)(2,1)S(1)}, u32[]{:S(2)}, u32[]{:S(2)}) collective-permute-start(bf16[144,128]{1,0:T(8,128)(2,1)S(1)} %add_convert_fusion.3), channel_id=1, source_target_pairs={{0,1},{1,0},{2,3},{3,2},{4,5},{5,4},{6,7},{7,6},{8,9},{9,8},{10,11... | collective-permute-start | bytes 110600 | tf_op jit(solution)/shard_map/ppermute | solution.py:470
  36.4 1.6 %collective-permute-start.8 = (bf16[144,128]{1,0:T(8,128)(2,1)S(1)}, bf16[144,128]{1,0:T(8,128)(2,1)S(1)}, u32[]{:S(2)}, u32[]{:S(2)}) collective-permute-start(bf16[144,128]{1,0:T(8,128)(2,1)S(1)} %add_convert_fusion.3), channel_id=1, source_target_pairs={{0,2},{1,3},{2,0},{3,1},{4,6},{5,7},{6,4},{7,5},{8,10},{9,11},{10,... | collective-permute-start | bytes 110600 | tf_op jit(solution)/shard_map/ppermute | solution.py:470
  38.9 1.4 %collective-permute-done.8 = bf16[144,128]{1,0:T(8,128)(2,1)S(1)} collective-permute-done((bf16[144,128]{1,0:T(8,128)(2,1)S(1)}, bf16[144,128]{1,0:T(8,128)(2,1)S(1)}, u32[]{:S(2)}, u32[]{:S(2)}) %collective-permute-start.8) | collective-permute-done | bytes 36896 | tf_op jit(solution)/shard_map/ppermute | solution.py:470
  40.3 2.5 %collective-permute-done.9 = bf16[144,128]{1,0:T(8,128)(2,1)S(1)} collective-permute-done((bf16[144,128]{1,0:T(8,128)(2,1)S(1)}, bf16[144,128]{1,0:T(8,128)(2,1)S(1)}, u32[]{:S(2)}, u32[]{:S(2)}) %collective-permute-start.9) | collective-permute-done | bytes 36896 | tf_op jit(solution)/shard_map/ppermute | solution.py:470
  42.8 2.2 %collective-permute-start.10 = (bf16[144,128]{1,0:T(8,128)(2,1)S(1)}, bf16[144,128]{1,0:T(8,128)(2,1)S(1)}, u32[]{:S(2)}, u32[]{:S(2)}) collective-permute-start(bf16[144,128]{1,0:T(8,128)(2,1)S(1)} %add_convert_fusion.2.payload), channel_id=1, source_target_pairs={{0,4},{1,5},{2,6},{3,7},{4,0},{5,1},{6,2},{7,3},{8,12},{9,13},{10,... | collective-permute-start | bytes 110600 | tf_op jit(solution)/shard_map/ppermute | solution.py:470
  45.1 3.0 %collective-permute-done.10.other = bf16[144,128]{1,0:T(8,128)(2,1)S(1)} collective-permute-done((bf16[144,128]{1,0:T(8,128)(2,1)S(1)}, bf16[144,128]{1,0:T(8,128)(2,1)S(1)}, u32[]{:S(2)}, u32[]{:S(2)}) %collective-permute-start.10) | collective-permute-done | bytes 36896 | tf_op jit(solution)/shard_map/ppermute | solution.py:470
  48.1 13.6 %second.1 = (bf16[10,48,256]{2,1,0:T(8,128)(2,1)S(1)}, bf16[10,48,512]{2,1,0:T(8,128)(2,1)S(1)}, bf16[144,128]{1,0:T(8,128)(2,1)S(1)}) custom-call(bf16[16,48,256]{2,1,0:T(8,128)(2,1)S(1)} %get-tuple-element.15.mixed, bf16[16,48,512]{2,1,0:T(8,128)(2,1)S(1)} %get-tuple-element.16.query, bf16[144,128]{1,0:T(8,128)(2,1)S(1)} %add_convert_fusion.2.payload, ...), custom_call_target="tpu_custom_call" | custom-call | tf_op jit(solution)/shard_map/second/pallas_call | solution.py:614
  62.6 1.0 %collective-permute-start.13 = (bf16[144,128]{1,0:T(8,128)(2,1)S(1)}, bf16[144,128]{1,0:T(8,128)(2,1)S(1)}, u32[]{:S(2)}, u32[]{:S(2)}) collective-permute-start(bf16[144,128]{1,0:T(8,128)(2,1)S(1)} %get-tuple-element.20), channel_id=1, source_target_pairs={{0,24},{8,16},{16,8},{24,0},{1,25},{9,17},{17,9},{25,1},{2,26},{10... | collective-permute-start | bytes 110600 | tf_op jit(solution)/shard_map/ppermute | solution.py:470
  63.7 2.3 %collective-permute-done.12 = bf16[144,128]{1,0:T(8,128)(2,1)S(1)} collective-permute-done((bf16[144,128]{1,0:T(8,128)(2,1)S(1)}, bf16[144,128]{1,0:T(8,128)(2,1)S(1)}, u32[]{:S(2)}, u32[]{:S(2)}) %collective-permute-start.12) | collective-permute-done | bytes 36896 | tf_op jit(solution)/shard_map/ppermute | solution.py:470
  66.4 1.3 %collective-permute-start.14 = (bf16[144,128]{1,0:T(8,128)(2,1)S(1)}, bf16[144,128]{1,0:T(8,128)(2,1)S(1)}, u32[]{:S(2)}, u32[]{:S(2)}) collective-permute-start(bf16[144,128]{1,0:T(8,128)(2,1)S(1)} %add_convert_fusion.1), channel_id=1, source_target_pairs={{0,1},{1,0},{2,3},{3,2},{4,5},{5,4},{6,7},{7,6},{8,9},{9,8},{10,11... | collective-permute-start | bytes 110600 | tf_op jit(solution)/shard_map/ppermute | solution.py:470
  67.8 2.2 %collective-permute-start.16 = (bf16[144,128]{1,0:T(8,128)(2,1)S(1)}, bf16[144,128]{1,0:T(8,128)(2,1)S(1)}, u32[]{:S(2)}, u32[]{:S(2)}) collective-permute-start(bf16[144,128]{1,0:T(8,128)(2,1)S(1)} %add_convert_fusion.1), channel_id=1, source_target_pairs={{0,3},{1,2},{2,1},{3,0},{4,7},{5,6},{6,5},{7,4},{8,11},{9,10},{10,... | collective-permute-start | bytes 110600 | tf_op jit(solution)/shard_map/ppermute | solution.py:470
  70.5 1.2 %collective-permute-done.15 = bf16[144,128]{1,0:T(8,128)(2,1)S(1)} collective-permute-done((bf16[144,128]{1,0:T(8,128)(2,1)S(1)}, bf16[144,128]{1,0:T(8,128)(2,1)S(1)}, u32[]{:S(2)}, u32[]{:S(2)}) %collective-permute-start.15) | collective-permute-done | bytes 36896 | tf_op jit(solution)/shard_map/ppermute | solution.py:470
  71.7 1.0 %collective-permute-done.16 = bf16[144,128]{1,0:T(8,128)(2,1)S(1)} collective-permute-done((bf16[144,128]{1,0:T(8,128)(2,1)S(1)}, bf16[144,128]{1,0:T(8,128)(2,1)S(1)}, u32[]{:S(2)}, u32[]{:S(2)}) %collective-permute-start.16) | collective-permute-done | bytes 36896 | tf_op jit(solution)/shard_map/ppermute | solution.py:470
  72.7 3.0 %collective-permute-start.17 = (bf16[144,128]{1,0:T(8,128)(2,1)S(1)}, bf16[144,128]{1,0:T(8,128)(2,1)S(1)}, u32[]{:S(2)}, u32[]{:S(2)}) collective-permute-start(bf16[144,128]{1,0:T(8,128)(2,1)S(1)} %add_convert_fusion.payload), channel_id=1, source_target_pairs={{0,4},{1,5},{2,6},{3,7},{4,0},{5,1},{6,2},{7,3},{8,12},{9,13},{10,... | collective-permute-start | bytes 110600 | tf_op jit(solution)/shard_map/ppermute | solution.py:470
  75.8 1.8 %collective-permute-done.17.other = bf16[144,128]{1,0:T(8,128)(2,1)S(1)} collective-permute-done((bf16[144,128]{1,0:T(8,128)(2,1)S(1)}, bf16[144,128]{1,0:T(8,128)(2,1)S(1)}, u32[]{:S(2)}, u32[]{:S(2)}) %collective-permute-start.17) | collective-permute-done | bytes 36896 | tf_op jit(solution)/shard_map/ppermute | solution.py:470
  77.7 4.3 %last.1 = (bf16[8,32,256]{2,1,0:T(8,128)(2,1)}, f32[4,8,32]{2,1,0:T(8,128)}) custom-call(bf16[10,48,256]{2,1,0:T(8,128)(2,1)S(1)} %get-tuple-element.18.mixed, bf16[10,48,512]{2,1,0:T(8,128)(2,1)S(1)} %get-tuple-element.19.query, bf16[144,128]{1,0:T(8,128)(2,1)S(1)} %add_convert_fusion.payload, bf16[144,128]{1,0:T(8,128)(2,1)S(1)} %collective-permute-done.17.other, ...), custom_call_target="tpu_custom_call" | custom-call | tf_op jit(solution)/shard_map/last/pallas_call | solution.py:626
  (53 shorter events, 6.7 us)
Async XLA Ops:
  1.6 1.5 %collective-permute-start = (bf16[7,32,256]{2,1,0:T(8,128)(2,1)S(1)}, bf16[7,32,256]{2,1,0:T(8,128)(2,1)S(1)}, u32[]{:S(2)}, u32[]{:S(2)}) collective-permute-start(bf16[7,32,256]{2,1,0:T(8,128)(2,1)S(1)} %get-tuple-element.27), channel_id=1, source_target_pairs={{0,8},{8,0},{16,24},{24,16},{1,9},{9,1},{17,25},{25,17},{2,10},{10... | collective-permute-start | bytes 344072 | tf_op jit(solution)/shard_map/ppermute | solution.py:496
  2.2 1.0 %collective-permute-start.1 = (bf16[7,32,256]{2,1,0:T(8,128)(2,1)S(1)}, bf16[7,32,256]{2,1,0:T(8,128)(2,1)S(1)}, u32[]{:S(2)}, u32[]{:S(2)}) collective-permute-start(bf16[7,32,256]{2,1,0:T(8,128)(2,1)S(1)} %get-tuple-element.26), channel_id=1, source_target_pairs={{8,16},{16,8},{9,17},{17,9},{10,18},{18,10},{11,19},{19,11},{12,20... | collective-permute-start | bytes 344072 | tf_op jit(solution)/shard_map/ppermute | solution.py:496
  2.9 4.3 %copy-start.9 = (bf16[2,256,768]{2,1,0:T(8,128)(2,1)S(1)}, bf16[2,256,768]{2,1,0:T(8,128)(2,1)}, u32[]{:S(2)}) copy-start(bf16[2,256,768]{2,1,0:T(8,128)(2,1)} %qkv.1) | copy-start | bytes 2359300
  3.8 3.4 %copy-start.10 = (bf16[2,24,32,32]{3,2,1,0:T(8,128)(2,1)S(1)}, bf16[2,24,32,32]{3,2,1,0:T(8,128)(2,1)}, u32[]{:S(2)}) copy-start(bf16[2,24,32,32]{3,2,1,0:T(8,128)(2,1)} %group.1) | copy-start | bytes 294916
  3.8 3.4 %copy-start.11 = (f32[2,5,5,768]{3,0,2,1:T(2,128)S(1)}, f32[2,5,5,768]{3,0,2,1:T(2,128)}, u32[]{:S(2)}) copy-start(f32[2,5,5,768]{3,0,2,1:T(2,128)} %param.22) | copy-start | bytes 460804
  3.8 3.4 %copy-start.12 = (bf16[3,3,4,256]{3,2,1,0:T(4,128)(2,1)S(1)}, bf16[3,3,4,256]{3,2,1,0:T(4,128)(2,1)}, u32[]{:S(2)}) copy-start(bf16[3,3,4,256]{3,2,1,0:T(4,128)(2,1)} %head.1) | copy-start | bytes 55300
  3.9 5.3 %collective-permute-start.2 = (bf16[22,8,256]{2,1,0:T(8,128)(2,1)S(1)}, bf16[22,8,256]{2,1,0:T(8,128)(2,1)S(1)}, u32[]{:S(2)}, u32[]{:S(2)}) collective-permute-start(bf16[22,8,256]{2,1,0:T(8,128)(2,1)S(1)} %get-tuple-element.23), channel_id=1, source_target_pairs={{0,1},{1,0},{2,3},{3,2},{4,5},{5,4},{6,7},{7,6},{8,9},{9,8},{10,11... | collective-permute-start | bytes 270344 | tf_op jit(solution)/shard_map/ppermute | solution.py:496
  6.5 2.7 %collective-permute-start.3 = (bf16[22,8,256]{2,1,0:T(8,128)(2,1)S(1)}, bf16[22,8,256]{2,1,0:T(8,128)(2,1)S(1)}, u32[]{:S(2)}, u32[]{:S(2)}) collective-permute-start(bf16[22,8,256]{2,1,0:T(8,128)(2,1)S(1)} %get-tuple-element.22), channel_id=1, source_target_pairs={{1,2},{2,1},{3,4},{4,3},{5,6},{6,5},{9,10},{10,9},{11,12},{12,11},... | collective-permute-start | bytes 270344 | tf_op jit(solution)/shard_map/ppermute | solution.py:496
  9.8 38.2 %copy-start.2 = (bf16[2,512,256]{2,1,0:T(8,128)(2,1)S(1)}, bf16[2,512,256]{2,1,0:T(8,128)(2,1)}, u32[]{:S(2)}) copy-start(bf16[2,512,256]{2,1,0:T(8,128)(2,1)} %out_weight.3) | copy-start | bytes 1572868
  21.6 6.6 %collective-permute-start.4 = (bf16[144,128]{1,0:T(8,128)(2,1)S(1)}, bf16[144,128]{1,0:T(8,128)(2,1)S(1)}, u32[]{:S(2)}, u32[]{:S(2)}) collective-permute-start(bf16[144,128]{1,0:T(8,128)(2,1)S(1)} %get-tuple-element.17), channel_id=1, source_target_pairs={{0,8},{8,0},{16,24},{24,16},{1,9},{9,1},{17,25},{25,17},{2,10},{10... | collective-permute-start | bytes 110600 | tf_op jit(solution)/shard_map/ppermute | solution.py:470
  26.4 4.0 %collective-permute-start.5 = (bf16[144,128]{1,0:T(8,128)(2,1)S(1)}, bf16[144,128]{1,0:T(8,128)(2,1)S(1)}, u32[]{:S(2)}, u32[]{:S(2)}) collective-permute-start(bf16[144,128]{1,0:T(8,128)(2,1)S(1)} %get-tuple-element.17), channel_id=1, source_target_pairs={{0,16},{8,24},{16,0},{24,8},{1,17},{9,25},{17,1},{25,9},{2,18},{10... | collective-permute-start | bytes 110600 | tf_op jit(solution)/shard_map/ppermute | solution.py:470
  28.1 3.4 %collective-permute-start.6 = (bf16[144,128]{1,0:T(8,128)(2,1)S(1)}, bf16[144,128]{1,0:T(8,128)(2,1)S(1)}, u32[]{:S(2)}, u32[]{:S(2)}) collective-permute-start(bf16[144,128]{1,0:T(8,128)(2,1)S(1)} %get-tuple-element.17), channel_id=1, source_target_pairs={{0,24},{8,16},{16,8},{24,0},{1,25},{9,17},{17,9},{25,1},{2,26},{10... | collective-permute-start | bytes 110600 | tf_op jit(solution)/shard_map/ppermute | solution.py:470
  31.5 7.4 %collective-permute-start.7 = (bf16[144,128]{1,0:T(8,128)(2,1)S(1)}, bf16[144,128]{1,0:T(8,128)(2,1)S(1)}, u32[]{:S(2)}, u32[]{:S(2)}) collective-permute-start(bf16[144,128]{1,0:T(8,128)(2,1)S(1)} %add_convert_fusion.3), channel_id=1, source_target_pairs={{0,1},{1,0},{2,3},{3,2},{4,5},{5,4},{6,7},{7,6},{8,9},{9,8},{10,11... | collective-permute-start | bytes 110600 | tf_op jit(solution)/shard_map/ppermute | solution.py:470
  36.4 4.0 %collective-permute-start.8 = (bf16[144,128]{1,0:T(8,128)(2,1)S(1)}, bf16[144,128]{1,0:T(8,128)(2,1)S(1)}, u32[]{:S(2)}, u32[]{:S(2)}) collective-permute-start(bf16[144,128]{1,0:T(8,128)(2,1)S(1)} %add_convert_fusion.3), channel_id=1, source_target_pairs={{0,2},{1,3},{2,0},{3,1},{4,6},{5,7},{6,4},{7,5},{8,10},{9,11},{10,... | collective-permute-start | bytes 110600 | tf_op jit(solution)/shard_map/ppermute | solution.py:470
  37.9 4.9 %collective-permute-start.9 = (bf16[144,128]{1,0:T(8,128)(2,1)S(1)}, bf16[144,128]{1,0:T(8,128)(2,1)S(1)}, u32[]{:S(2)}, u32[]{:S(2)}) collective-permute-start(bf16[144,128]{1,0:T(8,128)(2,1)S(1)} %add_convert_fusion.3), channel_id=1, source_target_pairs={{0,3},{1,2},{2,1},{3,0},{4,7},{5,6},{6,5},{7,4},{8,11},{9,10},{10,... | collective-permute-start | bytes 110600 | tf_op jit(solution)/shard_map/ppermute | solution.py:470
  42.8 5.2 %copy-start.8 = (f32[2,256]{1,0:T(2,128)S(1)}, f32[2,256]{1,0:T(2,128)}, u32[]{:S(2)}) copy-start(f32[2,256]{1,0:T(2,128)} %out_bias.3) | copy-start | bytes 6148
  42.8 5.2 %collective-permute-start.10 = (bf16[144,128]{1,0:T(8,128)(2,1)S(1)}, bf16[144,128]{1,0:T(8,128)(2,1)S(1)}, u32[]{:S(2)}, u32[]{:S(2)}) collective-permute-start(bf16[144,128]{1,0:T(8,128)(2,1)S(1)} %add_convert_fusion.2.payload), channel_id=1, source_target_pairs={{0,4},{1,5},{2,6},{3,7},{4,0},{5,1},{6,2},{7,3},{8,12},{9,13},{10,... | collective-permute-start | bytes 110600 | tf_op jit(solution)/shard_map/ppermute | solution.py:470
  61.7 1.9 %collective-permute-start.11 = (bf16[144,128]{1,0:T(8,128)(2,1)S(1)}, bf16[144,128]{1,0:T(8,128)(2,1)S(1)}, u32[]{:S(2)}, u32[]{:S(2)}) collective-permute-start(bf16[144,128]{1,0:T(8,128)(2,1)S(1)} %get-tuple-element.20), channel_id=1, source_target_pairs={{0,8},{8,0},{16,24},{24,16},{1,9},{9,1},{17,25},{25,17},{2,10},{10... | collective-permute-start | bytes 110600 | tf_op jit(solution)/shard_map/ppermute | solution.py:470
  61.8 4.2 %collective-permute-start.12 = (bf16[144,128]{1,0:T(8,128)(2,1)S(1)}, bf16[144,128]{1,0:T(8,128)(2,1)S(1)}, u32[]{:S(2)}, u32[]{:S(2)}) collective-permute-start(bf16[144,128]{1,0:T(8,128)(2,1)S(1)} %get-tuple-element.20), channel_id=1, source_target_pairs={{0,16},{8,24},{16,0},{24,8},{1,17},{9,25},{17,1},{25,9},{2,18},{10... | collective-permute-start | bytes 110600 | tf_op jit(solution)/shard_map/ppermute | solution.py:470
  62.6 3.8 %collective-permute-start.13 = (bf16[144,128]{1,0:T(8,128)(2,1)S(1)}, bf16[144,128]{1,0:T(8,128)(2,1)S(1)}, u32[]{:S(2)}, u32[]{:S(2)}) collective-permute-start(bf16[144,128]{1,0:T(8,128)(2,1)S(1)} %get-tuple-element.20), channel_id=1, source_target_pairs={{0,24},{8,16},{16,8},{24,0},{1,25},{9,17},{17,9},{25,1},{2,26},{10... | collective-permute-start | bytes 110600 | tf_op jit(solution)/shard_map/ppermute | solution.py:470
  66.4 4.0 %collective-permute-start.14 = (bf16[144,128]{1,0:T(8,128)(2,1)S(1)}, bf16[144,128]{1,0:T(8,128)(2,1)S(1)}, u32[]{:S(2)}, u32[]{:S(2)}) collective-permute-start(bf16[144,128]{1,0:T(8,128)(2,1)S(1)} %add_convert_fusion.1), channel_id=1, source_target_pairs={{0,1},{1,0},{2,3},{3,2},{4,5},{5,4},{6,7},{7,6},{8,9},{9,8},{10,11... | collective-permute-start | bytes 110600 | tf_op jit(solution)/shard_map/ppermute | solution.py:470
  67.7 4.0 %collective-permute-start.15 = (bf16[144,128]{1,0:T(8,128)(2,1)S(1)}, bf16[144,128]{1,0:T(8,128)(2,1)S(1)}, u32[]{:S(2)}, u32[]{:S(2)}) collective-permute-start(bf16[144,128]{1,0:T(8,128)(2,1)S(1)} %add_convert_fusion.1), channel_id=1, source_target_pairs={{0,2},{1,3},{2,0},{3,1},{4,6},{5,7},{6,4},{7,5},{8,10},{9,11},{10,... | collective-permute-start | bytes 110600 | tf_op jit(solution)/shard_map/ppermute | solution.py:470
  67.8 4.9 %collective-permute-start.16 = (bf16[144,128]{1,0:T(8,128)(2,1)S(1)}, bf16[144,128]{1,0:T(8,128)(2,1)S(1)}, u32[]{:S(2)}, u32[]{:S(2)}) collective-permute-start(bf16[144,128]{1,0:T(8,128)(2,1)S(1)} %add_convert_fusion.1), channel_id=1, source_target_pairs={{0,3},{1,2},{2,1},{3,0},{4,7},{5,6},{6,5},{7,4},{8,11},{9,10},{10,... | collective-permute-start | bytes 110600 | tf_op jit(solution)/shard_map/ppermute | solution.py:470
  72.7 4.9 %collective-permute-start.17 = (bf16[144,128]{1,0:T(8,128)(2,1)S(1)}, bf16[144,128]{1,0:T(8,128)(2,1)S(1)}, u32[]{:S(2)}, u32[]{:S(2)}) collective-permute-start(bf16[144,128]{1,0:T(8,128)(2,1)S(1)} %add_convert_fusion.payload), channel_id=1, source_target_pairs={{0,4},{1,5},{2,6},{3,7},{4,0},{5,1},{6,2},{7,3},{8,12},{9,13},{10,... | collective-permute-start | bytes 110600 | tf_op jit(solution)/shard_map/ppermute | solution.py:470
  (8 other events, 14.6 us)

commit v7 on v6

--- a/solution.py
+++ b/solution.py
@@ -13,7 +13,6 @@
 REACH = 7
 KEY_ROWS = 16
 TILE = 16
-PARTS = 4
 F32 = jnp.float32
 BF16 = jnp.bfloat16
 
@@ -22,9 +21,18 @@
     return value * jnp.minimum(jnp.maximum(value + 3.0, 0.0), 6.0)
 
 
-def parted(count, parts):
-    cuts = [count * k // parts for k in range(parts + 1)]
-    return [(a, b - a) for a, b in zip(cuts, cuts[1:]) if b > a]
+def group_size(count, most):
+    return next(n for n in range(min(most, count), 0, -1) if count % n == 0)
+
+
+def by_groups(count, most, body):
+    size = group_size(count, most)
+
+    def group(index, carry):
+        body(index * size, size)
+        return carry
+
+    lax.fori_loop(0, count // size, group, 0)
 
 
 def clear_outside(ref, halo, cols):
@@ -77,7 +85,7 @@
     expand, expand_bias, depth, depth_bias, project, project_bias = weights[:6]
     mixed_out, query_out, payload_out = outs
     (
-        hidden_0, hidden_1, total, mixed, qkv, query, wide_depth, wide_agg,
+        hidden, total, mixed, qkv, query, wide_depth, wide_agg,
         qkv_weight, agg, group, sems,
     ) = scratch
     loads = [
@@ -90,59 +98,79 @@
     rows, width, channels = x_ref.shape
     tile_rows, tile_cols = tile
     inner = rows - 2
-    chunk = hidden_0.shape[2]
+    chunk = hidden.shape[3]
     chunks = expand.shape[2] // chunk
     for index in range(9):
         taps = depth[index // 3, index % 3, section : section + 1, :] * (1.0 / 6.0)
         wide_depth[index] = jnp.broadcast_to(taps, (TILE, taps.shape[1])).astype(BF16)
-    total[...] = 6.0 * (flat(x_ref[1 : rows - 1]).astype(F32) + project_bias[section : section + 1, :])
-
-    def expand_rows(out, at, first, size):
+
+    def start_rows(first, size):
+        value = x_ref[pl.ds(first + 1, size)].astype(F32) + project_bias[section : section + 1, :]
+        total[pl.ds(first, size)] = 6.0 * value
+
+    by_groups(inner, 2, start_rows)
+
+    def expand_rows(slot, at, first, size):
         value = jnp.dot(
-            flat(x_ref[first : first + size]), expand[section, :, pl.ds(at, chunk)],
+            flat(x_ref[pl.ds(first, size)]), expand[section, :, pl.ds(at, chunk)],
             preferred_element_type=F32,
         )
         value = (value + expand_bias[section : section + 1, pl.ds(at, chunk)]).astype(BF16)
-        out[first : first + size] = six_hard_swish(value).reshape(size, width, chunk)
-
-    def spread_rows(hidden, at, first, size):
+        hidden[slot, pl.ds(first, size)] = six_hard_swish(value).reshape(size, width, chunk)
+
+    def spread_rows(slot, at, first, size):
         spread = []
-        for r in range(first, first + size):
+        for r in range(size):
             lanes = []
             for lane in range(0, chunk, LANES):
                 here = pl.ds(pl.multiple_of(at + lane, LANES), LANES)
                 value = depthwise_row(
-                    [hidden[r + a, :, lane : lane + LANES] for a in range(3)],
+                    [hidden[slot, first + r + a, :, lane : lane + LANES] for a in range(3)],
                     lambda a, b: wide_depth[3 * a + b, :, here], 3, width,
                 )
                 value = (value + depth_bias[section : section + 1, here]).astype(BF16)
                 lanes.append(six_hard_swish(value))
             spread.append(jnp.concatenate(lanes, axis=1))
-        pixels = slice(first * width, (first + size) * width)
-        total[pixels] += jnp.dot(
+        value = jnp.dot(
             jnp.concatenate(spread, axis=0), project[section, pl.ds(at, chunk), :],
             preferred_element_type=F32,
         )
-
-    def stage(index, current, following):
+        total[pl.ds(first, size)] += value.reshape(size, width, channels)
+
+    size = group_size(inner, 7)
+    groups = inner // size
+    ahead = -(-rows // groups)
+
+    def ahead_rows(slot, at, group):
+        expand_rows(slot, at, jnp.minimum(group * ahead, rows - ahead), ahead)
+
+    def first_rows(group, carry):
+        ahead_rows(0, 0, group)
+        return carry
+
+    lax.fori_loop(0, groups, first_rows, 0)
+    clear_outside(hidden.at[0], halo, tile_cols)
+
+    def stage(index, carry):
+        slot = index % 2
         at = pl.multiple_of(index * chunk, chunk)
-        ahead = pl.multiple_of(jnp.minimum(index + 1, chunks - 1) * chunk, chunk)
-        for (first, size), (from_row, count) in zip(parted(inner, PARTS), parted(rows, PARTS)):
-            expand_rows(following, ahead, from_row, count)
-            spread_rows(current, at, first, size)
-        clear_outside(following, halo, tile_cols)
-
-    for first, size in parted(rows, PARTS):
-        expand_rows(hidden_0, 0, first, size)
-    clear_outside(hidden_0, halo, tile_cols)
-
-    def two_stages(index, carry):
-        stage(2 * index, hidden_0, hidden_1)
-        stage(2 * index + 1, hidden_1, hidden_0)
+        following = pl.multiple_of(jnp.minimum(index + 1, chunks - 1) * chunk, chunk)
+
+        def group_rows(group, carry):
+            spread_rows(slot, at, group * size, size)
+            ahead_rows(1 - slot, following, group)
+            return carry
+
+        lax.fori_loop(0, groups, group_rows, 0)
+        clear_outside(hidden.at[1 - slot], halo, tile_cols)
         return carry
 
-    lax.fori_loop(0, chunks // 2, two_stages, 0)
-    mixed[...] = (total[...] * (1.0 / 6.0)).astype(BF16).reshape(inner, width, channels)
+    lax.fori_loop(0, chunks, stage, 0)
+
+    def mixed_rows(first, size):
+        mixed[pl.ds(first, size)] = (total[pl.ds(first, size)] * (1.0 / 6.0)).astype(BF16)
+
+    by_groups(inner, 2, mixed_rows)
     outer = inner - 4
     stores = [
         pltpu.make_async_copy(mixed.at[pl.ds(2, outer)], mixed_out, sems.at[3]),
@@ -154,11 +182,14 @@
     for index in range(25):
         taps = agg[index : index + 1, :]
         wide_agg[index] = jnp.broadcast_to(taps, (TILE, taps.shape[1])).astype(BF16)
-    for first, size in parted(inner, PARTS):
+
+    def qkv_rows(first, size):
         value = jnp.dot(
-            flat(mixed[first : first + size]), qkv_weight[...], preferred_element_type=F32
-        )
-        qkv[first : first + size] = value.astype(BF16).reshape(size, width, 3 * channels)
+            flat(mixed[pl.ds(first, size)]), qkv_weight[...], preferred_element_type=F32
+        )
+        qkv[pl.ds(first, size)] = value.astype(BF16).reshape(size, width, 3 * channels)
+
+    by_groups(inner, 7, qkv_rows)
     around = halo - 1
     clear_outside(qkv, around, tile_cols)
 
@@ -179,19 +210,14 @@
         )
         return value.astype(BF16).reshape(size, width, channels)
 
-    query[:, :, 0:channels] = jnp.maximum(qkv[2 : inner - 2, :, 0:channels], 0.0)
-    size = next(n for n in range(5, 0, -1) if outer % n == 0)
-
-    def query_rows(index, carry):
-        at = index * size
-        query[pl.ds(at, size), :, channels : 2 * channels] = jnp.maximum(
-            aggregated(0, at, size), 0.0
-        )
-        return carry
-
-    lax.fori_loop(0, outer // size, query_rows, 0)
+    def query_rows(first, size):
+        here = pl.ds(first, size)
+        query[here, :, 0:channels] = jnp.maximum(qkv[pl.ds(first + 2, size), :, 0:channels], 0.0)
+        query[here, :, channels : 2 * channels] = jnp.maximum(aggregated(0, first, size), 0.0)
+
+    by_groups(outer, 5, query_rows)
     stores[1].start()
-    size = next(n for n in range(4, 0, -1) if tile_rows % n == 0)
+    size = group_size(tile_rows, 4)
 
     def summed(key, value):
         key = jnp.maximum(flat(key[:, 0:tile_cols]), 0.0)
@@ -241,14 +267,10 @@
     mixed_in, query_in, payloads, weight, bias, mixed_ref, query_ref, sems, head_dim, section, x_ref
 ):
     rows, width, channels = x_ref.shape
-    groups = parted(rows, PARTS)
-    loads = []
-    for index, (first, size) in enumerate(groups):
-        here = pl.ds(first, size)
-        for at, (source, target) in enumerate(((query_in, query_ref), (mixed_in, mixed_ref))):
-            load = pltpu.make_async_copy(source.at[here], target.at[here], sems.at[at, index])
-            load.start()
-            loads.append(load)
+    halves = [(query_in, query_ref), (mixed_in, mixed_ref)]
+    loads = [pltpu.make_async_copy(a, b, sems.at[k]) for k, (a, b) in enumerate(halves)]
+    for load in loads:
+        load.start()
     same = same_head(head_dim)
     square = (LANES, LANES)
     diagonal = lax.broadcasted_iota(jnp.int32, square, 0) == lax.broadcasted_iota(
@@ -281,10 +303,11 @@
     summaries = [paired(summaries, index) for index in range(0, count, 2)]
     sums = [paired(sums, index) for index in range(0, count, 2)]
     step = 2 * LANES
-    for index, (first, size) in enumerate(groups):
-        for load in loads[2 * index : 2 * index + 2]:
-            load.wait()
-        query = flat(query_ref[first : first + size])
+    for load in loads:
+        load.wait()
+
+    def attend_rows(first, size):
+        query = flat(query_ref[pl.ds(first, size)])
         parts = []
         for branch in range(count // 2):
             part = query[:, branch * step : (branch + 1) * step]
@@ -297,8 +320,10 @@
             jnp.concatenate(parts, axis=1), weight[section], preferred_element_type=F32
         )
         value = value + bias[section : section + 1, :]
-        value = value + flat(mixed_ref[first : first + size]).astype(F32)
-        x_ref[first : first + size] = value.astype(BF16).reshape(size, width, channels)
+        value = value + flat(mixed_ref[pl.ds(first, size)]).astype(F32)
+        x_ref[pl.ds(first, size)] = value.astype(BF16).reshape(size, width, channels)
+
+    by_groups(rows, 5, attend_rows)
 
 
 def tap(section, a, b):
@@ -574,9 +599,8 @@
 
     def front_scratch(count):
         return [
-            pltpu.VMEM((count, width, 256), BF16),
-            pltpu.VMEM((count, width, 256), BF16),
-            pltpu.VMEM(((count - 2) * width, channels), F32),
+            pltpu.VMEM((2, count, width, 256), BF16),
+            pltpu.VMEM((count - 2, width, channels), F32),
             pltpu.VMEM((count - 2, width, channels), BF16),
             pltpu.VMEM((count - 2, width, 3 * channels), BF16),
             pltpu.VMEM((count - 6, width, 2 * channels), BF16),
@@ -593,7 +617,7 @@
             pltpu.VMEM((count, width, channels), BF16),
             pltpu.VMEM((count, width, channels), BF16),
             pltpu.VMEM((count, width, 2 * channels), BF16),
-            pltpu.SemaphoreType.DMA((2, PARTS)),
+            pltpu.SemaphoreType.DMA((2,)),
         ]
 
     first_rows = rows + 2 * REACH

time: 82.4 us -> 82.7 us (level)
    pallas_call x1, Pallas kernels: 11.7 us -> 14.3 us  [local(): pl.pallas_call(functools.partial(first_kernel, tile, head_dim), out_shape...]
    pallas_call x1, Pallas kernels: 13.6 us -> 12.6 us  [local(): pl.pallas_call(functools.partial(second_kernel, tile, head_dim), out_shap...]
    pallas_call x1, Pallas kernels: 4.32 us -> 3.33 us  [local(): pl.pallas_call(functools.partial(last_kernel, tile, head_dim), out_shape=...]
where the time goes in v7:
time: 82.7 us; the launch traced here: 82.5 us
  Pallas kernels  32.1 us (39%)
  starting transfers between devices  29 us (35%)
  waiting for transfers between devices  17.8 us (22%)
  local copies, waits for them, and re-layouts  2.42 us (3%)
  between operations  0.94 us (1%)
    ppermute x14, starting transfers between devices, sum_by_permutes(): lax.ppermute(value, axis, [(i, partner(i, stride, radix, k)) for i in ran...  24.6 us
    ppermute x14, waiting for transfers between devices, sum_by_permutes(): lax.ppermute(value, axis, [(i, partner(i, stride, radix, k)) for i in ran...  17.5 us
    pallas_call x1, Pallas kernels, local(): pl.pallas_call(functools.partial(first_kernel, tile, head_dim), out_shape...  14.3 us
    pallas_call x1, Pallas kernels, local(): pl.pallas_call(functools.partial(second_kernel, tile, head_dim), out_shap...  12.6 us
    ppermute x4, starting transfers between devices, pair_exchange(): return lax.ppermute(value, axis, pairs)  4.43 us
    pallas_call x1, Pallas kernels, local(): pl.pallas_call(functools.partial(last_kernel, tile, head_dim), out_shape=...  3.33 us
    pallas_call x1, Pallas kernels, local(): pl.pallas_call(functools.partial(prepare_kernel, head_dim), out_shape=mad...  1.9 us
  transfers between devices with their start and end apart: 18, of which 12 were waited for; matrix products, arithmetic and copies ran while one was open for 0% of the time, Pallas kernels for 2%

profile of v7, /device:TPU:0, one launch (start us, length us, event | category | flops | bytes accessed | tf_op | source)
XLA Modules:
  0.0 82.5 jit_solution(9768802258775601049)
XLA Ops:
  0.6 1.0 %constant_dynamic-slice_fusion.2 = (bf16[7,32,256]{2,1,0:T(8,128)(2,1)S(1)}, bf16[7,32,256]{2,1,0:T(8,128)(2,1)S(1)}) fusion(bf16[8,32,256]{2,1,0:T(8,128)(2,1)} %own.1, s32[]{:T(128)S(6)} %select_n.42, s32[]{:T(128)S(6)} %select_n.41), kind=kLoop, calls=%fused_computation.9 | loop fusion | bytes 458760 | tf_op jit(solution)/shard_map/dynamic_slice | solution.py:550
  3.9 2.6 %collective-permute-start.2 = (bf16[22,8,256]{2,1,0:T(8,128)(2,1)S(1)}, bf16[22,8,256]{2,1,0:T(8,128)(2,1)S(1)}, u32[]{:S(2)}, u32[]{:S(2)}) collective-permute-start(bf16[22,8,256]{2,1,0:T(8,128)(2,1)S(1)} %get-tuple-element.23), channel_id=1, source_target_pairs={{0,1},{1,0},{2,3},{3,2},{4,5},{5,4},{6,7},{7,6},{8,9},{9,8},{10,11... | collective-permute-start | bytes 270344 | tf_op jit(solution)/shard_map/ppermute | solution.py:521
  7.2 1.9 %prepare.1 = (bf16[2,256,768]{2,1,0:T(8,128)(2,1)S(1)}, f32[2,32,768]{2,1,0:T(8,128)S(1)}, bf16[2,3,256,256]{3,2,1,0:T(8,128)(2,1)S(1)}, bf16[3,128,256]{2,1,0:T(8,128)(2,1)S(1)}) custom-call(bf16[2,256,768]{2,1,0:T(8,128)(2,1)S(1)} %copy-done.9, f32[5,5,2,768]{3,2,1,0:T(2,128)S(1)} %bitcast.5, bf16[2,24,32,32]{3,2,1,0:T(8,128)(2,1)S(1)} %copy-done.10, ...), custom_call_target="tpu_custom_call" | custom-call | flops 2000000000 | bytes 4000000 | tf_op jit(solution)/shard_map/prepare/pallas_call | solution.py:572
  9.9 14.3 %first.1 = (bf16[16,48,256]{2,1,0:T(8,128)(2,1)S(1)}, bf16[16,48,512]{2,1,0:T(8,128)(2,1)S(1)}, bf16[144,128]{1,0:T(8,128)(2,1)S(1)}) custom-call(bf16[8,32,256]{2,1,0:T(8,128)(2,1)S(1)} %copy-done.3, bf16[7,32,256]{2,1,0:T(8,128)(2,1)S(1)} %collective-permute-done.row_0, bf16[7,32,256]{2,1,0:T(8,128)(2,1)S(1)} %collective-permute-done.1.row_1, ...), custom_call_target="tpu_custom_call" | custom-call | tf_op jit(solution)/shard_map/first/pallas_call | solution.py:624
  24.2 4.8 %collective-permute-start.4 = (bf16[144,128]{1,0:T(8,128)(2,1)S(1)}, bf16[144,128]{1,0:T(8,128)(2,1)S(1)}, u32[]{:S(2)}, u32[]{:S(2)}) collective-permute-start(bf16[144,128]{1,0:T(8,128)(2,1)S(1)} %get-tuple-element.17), channel_id=1, source_target_pairs={{0,8},{8,0},{16,24},{24,16},{1,9},{9,1},{17,25},{25,17},{2,10},{10... | collective-permute-start | bytes 110600 | tf_op jit(solution)/shard_map/ppermute | solution.py:495
  28.9 1.7 %collective-permute-start.5 = (bf16[144,128]{1,0:T(8,128)(2,1)S(1)}, bf16[144,128]{1,0:T(8,128)(2,1)S(1)}, u32[]{:S(2)}, u32[]{:S(2)}) collective-permute-start(bf16[144,128]{1,0:T(8,128)(2,1)S(1)} %get-tuple-element.17), channel_id=1, source_target_pairs={{0,16},{8,24},{16,0},{24,8},{1,17},{9,25},{17,1},{25,9},{2,18},{10... | collective-permute-start | bytes 110600 | tf_op jit(solution)/shard_map/ppermute | solution.py:495
  30.7 2.2 %collective-permute-done.5 = bf16[144,128]{1,0:T(8,128)(2,1)S(1)} collective-permute-done((bf16[144,128]{1,0:T(8,128)(2,1)S(1)}, bf16[144,128]{1,0:T(8,128)(2,1)S(1)}, u32[]{:S(2)}, u32[]{:S(2)}) %collective-permute-start.5) | collective-permute-done | bytes 36896 | tf_op jit(solution)/shard_map/ppermute | solution.py:495
  32.9 1.2 %collective-permute-done.6 = bf16[144,128]{1,0:T(8,128)(2,1)S(1)} collective-permute-done((bf16[144,128]{1,0:T(8,128)(2,1)S(1)}, bf16[144,128]{1,0:T(8,128)(2,1)S(1)}, u32[]{:S(2)}, u32[]{:S(2)}) %collective-permute-start.6) | collective-permute-done | bytes 36896 | tf_op jit(solution)/shard_map/ppermute | solution.py:495
  34.1 4.8 %collective-permute-start.7 = (bf16[144,128]{1,0:T(8,128)(2,1)S(1)}, bf16[144,128]{1,0:T(8,128)(2,1)S(1)}, u32[]{:S(2)}, u32[]{:S(2)}) collective-permute-start(bf16[144,128]{1,0:T(8,128)(2,1)S(1)} %add_convert_fusion.3), channel_id=1, source_target_pairs={{0,1},{1,0},{2,3},{3,2},{4,5},{5,4},{6,7},{7,6},{8,9},{9,8},{10,11... | collective-permute-start | bytes 110600 | tf_op jit(solution)/shard_map/ppermute | solution.py:495
  38.9 1.6 %collective-permute-start.8 = (bf16[144,128]{1,0:T(8,128)(2,1)S(1)}, bf16[144,128]{1,0:T(8,128)(2,1)S(1)}, u32[]{:S(2)}, u32[]{:S(2)}) collective-permute-start(bf16[144,128]{1,0:T(8,128)(2,1)S(1)} %add_convert_fusion.3), channel_id=1, source_target_pairs={{0,2},{1,3},{2,0},{3,1},{4,6},{5,7},{6,4},{7,5},{8,10},{9,11},{10,... | collective-permute-start | bytes 110600 | tf_op jit(solution)/shard_map/ppermute | solution.py:495
  41.5 1.4 %collective-permute-done.8 = bf16[144,128]{1,0:T(8,128)(2,1)S(1)} collective-permute-done((bf16[144,128]{1,0:T(8,128)(2,1)S(1)}, bf16[144,128]{1,0:T(8,128)(2,1)S(1)}, u32[]{:S(2)}, u32[]{:S(2)}) %collective-permute-start.8) | collective-permute-done | bytes 36896 | tf_op jit(solution)/shard_map/ppermute | solution.py:495
  42.9 2.5 %collective-permute-done.9 = bf16[144,128]{1,0:T(8,128)(2,1)S(1)} collective-permute-done((bf16[144,128]{1,0:T(8,128)(2,1)S(1)}, bf16[144,128]{1,0:T(8,128)(2,1)S(1)}, u32[]{:S(2)}, u32[]{:S(2)}) %collective-permute-start.9) | collective-permute-done | bytes 36896 | tf_op jit(solution)/shard_map/ppermute | solution.py:495
  45.4 2.2 %collective-permute-start.10 = (bf16[144,128]{1,0:T(8,128)(2,1)S(1)}, bf16[144,128]{1,0:T(8,128)(2,1)S(1)}, u32[]{:S(2)}, u32[]{:S(2)}) collective-permute-start(bf16[144,128]{1,0:T(8,128)(2,1)S(1)} %add_convert_fusion.2.payload), channel_id=1, source_target_pairs={{0,4},{1,5},{2,6},{3,7},{4,0},{5,1},{6,2},{7,3},{8,12},{9,13},{10,... | collective-permute-start | bytes 110600 | tf_op jit(solution)/shard_map/ppermute | solution.py:495
  47.6 3.0 %collective-permute-done.10.other = bf16[144,128]{1,0:T(8,128)(2,1)S(1)} collective-permute-done((bf16[144,128]{1,0:T(8,128)(2,1)S(1)}, bf16[144,128]{1,0:T(8,128)(2,1)S(1)}, u32[]{:S(2)}, u32[]{:S(2)}) %collective-permute-start.10) | collective-permute-done | bytes 36896 | tf_op jit(solution)/shard_map/ppermute | solution.py:495
  50.6 12.6 %second.1 = (bf16[10,48,256]{2,1,0:T(8,128)(2,1)S(1)}, bf16[10,48,512]{2,1,0:T(8,128)(2,1)S(1)}, bf16[144,128]{1,0:T(8,128)(2,1)S(1)}) custom-call(bf16[16,48,256]{2,1,0:T(8,128)(2,1)S(1)} %get-tuple-element.15.mixed, bf16[16,48,512]{2,1,0:T(8,128)(2,1)S(1)} %get-tuple-element.16.query, bf16[144,128]{1,0:T(8,128)(2,1)S(1)} %add_convert_fusion.2.payload, ...), custom_call_target="tpu_custom_call" | custom-call | tf_op jit(solution)/shard_map/second/pallas_call | solution.py:638
  64.1 1.0 %collective-permute-start.13 = (bf16[144,128]{1,0:T(8,128)(2,1)S(1)}, bf16[144,128]{1,0:T(8,128)(2,1)S(1)}, u32[]{:S(2)}, u32[]{:S(2)}) collective-permute-start(bf16[144,128]{1,0:T(8,128)(2,1)S(1)} %get-tuple-element.20), channel_id=1, source_target_pairs={{0,24},{8,16},{16,8},{24,0},{1,25},{9,17},{17,9},{25,1},{2,26},{10... | collective-permute-start | bytes 110600 | tf_op jit(solution)/shard_map/ppermute | solution.py:495
  65.1 2.4 %collective-permute-done.12 = bf16[144,128]{1,0:T(8,128)(2,1)S(1)} collective-permute-done((bf16[144,128]{1,0:T(8,128)(2,1)S(1)}, bf16[144,128]{1,0:T(8,128)(2,1)S(1)}, u32[]{:S(2)}, u32[]{:S(2)}) %collective-permute-start.12) | collective-permute-done | bytes 36896 | tf_op jit(solution)/shard_map/ppermute | solution.py:495
  67.9 1.3 %collective-permute-start.14 = (bf16[144,128]{1,0:T(8,128)(2,1)S(1)}, bf16[144,128]{1,0:T(8,128)(2,1)S(1)}, u32[]{:S(2)}, u32[]{:S(2)}) collective-permute-start(bf16[144,128]{1,0:T(8,128)(2,1)S(1)} %add_convert_fusion.1), channel_id=1, source_target_pairs={{0,1},{1,0},{2,3},{3,2},{4,5},{5,4},{6,7},{7,6},{8,9},{9,8},{10,11... | collective-permute-start | bytes 110600 | tf_op jit(solution)/shard_map/ppermute | solution.py:495
  69.3 2.2 %collective-permute-start.16 = (bf16[144,128]{1,0:T(8,128)(2,1)S(1)}, bf16[144,128]{1,0:T(8,128)(2,1)S(1)}, u32[]{:S(2)}, u32[]{:S(2)}) collective-permute-start(bf16[144,128]{1,0:T(8,128)(2,1)S(1)} %add_convert_fusion.1), channel_id=1, source_target_pairs={{0,3},{1,2},{2,1},{3,0},{4,7},{5,6},{6,5},{7,4},{8,11},{9,10},{10,... | collective-permute-start | bytes 110600 | tf_op jit(solution)/shard_map/ppermute | solution.py:495
  71.9 1.2 %collective-permute-done.15 = bf16[144,128]{1,0:T(8,128)(2,1)S(1)} collective-permute-done((bf16[144,128]{1,0:T(8,128)(2,1)S(1)}, bf16[144,128]{1,0:T(8,128)(2,1)S(1)}, u32[]{:S(2)}, u32[]{:S(2)}) %collective-permute-start.15) | collective-permute-done | bytes 36896 | tf_op jit(solution)/shard_map/ppermute | solution.py:495
  73.1 1.0 %collective-permute-done.16 = bf16[144,128]{1,0:T(8,128)(2,1)S(1)} collective-permute-done((bf16[144,128]{1,0:T(8,128)(2,1)S(1)}, bf16[144,128]{1,0:T(8,128)(2,1)S(1)}, u32[]{:S(2)}, u32[]{:S(2)}) %collective-permute-start.16) | collective-permute-done | bytes 36896 | tf_op jit(solution)/shard_map/ppermute | solution.py:495
  74.2 3.0 %collective-permute-start.17 = (bf16[144,128]{1,0:T(8,128)(2,1)S(1)}, bf16[144,128]{1,0:T(8,128)(2,1)S(1)}, u32[]{:S(2)}, u32[]{:S(2)}) collective-permute-start(bf16[144,128]{1,0:T(8,128)(2,1)S(1)} %add_convert_fusion.payload), channel_id=1, source_target_pairs={{0,4},{1,5},{2,6},{3,7},{4,0},{5,1},{6,2},{7,3},{8,12},{9,13},{10,... | collective-permute-start | bytes 110600 | tf_op jit(solution)/shard_map/ppermute | solution.py:495
  77.3 1.8 %collective-permute-done.17.other = bf16[144,128]{1,0:T(8,128)(2,1)S(1)} collective-permute-done((bf16[144,128]{1,0:T(8,128)(2,1)S(1)}, bf16[144,128]{1,0:T(8,128)(2,1)S(1)}, u32[]{:S(2)}, u32[]{:S(2)}) %collective-permute-start.17) | collective-permute-done | bytes 36896 | tf_op jit(solution)/shard_map/ppermute | solution.py:495
  79.1 3.3 %last.1 = (bf16[8,32,256]{2,1,0:T(8,128)(2,1)}, f32[4,8,32]{2,1,0:T(8,128)}) custom-call(bf16[10,48,256]{2,1,0:T(8,128)(2,1)S(1)} %get-tuple-element.18.mixed, bf16[10,48,512]{2,1,0:T(8,128)(2,1)S(1)} %get-tuple-element.19.query, bf16[144,128]{1,0:T(8,128)(2,1)S(1)} %add_convert_fusion.payload, bf16[144,128]{1,0:T(8,128)(2,1)S(1)} %collective-permute-done.17.other, ...), custom_call_target="tpu_custom_call" | custom-call | tf_op jit(solution)/shard_map/last/pallas_call | solution.py:650
  (53 shorter events, 6.6 us)
Async XLA Ops:
  1.6 1.5 %collective-permute-start = (bf16[7,32,256]{2,1,0:T(8,128)(2,1)S(1)}, bf16[7,32,256]{2,1,0:T(8,128)(2,1)S(1)}, u32[]{:S(2)}, u32[]{:S(2)}) collective-permute-start(bf16[7,32,256]{2,1,0:T(8,128)(2,1)S(1)} %get-tuple-element.27), channel_id=1, source_target_pairs={{0,8},{8,0},{16,24},{24,16},{1,9},{9,1},{17,25},{25,17},{2,10},{10... | collective-permute-start | bytes 344072 | tf_op jit(solution)/shard_map/ppermute | solution.py:521
  2.2 1.0 %collective-permute-start.1 = (bf16[7,32,256]{2,1,0:T(8,128)(2,1)S(1)}, bf16[7,32,256]{2,1,0:T(8,128)(2,1)S(1)}, u32[]{:S(2)}, u32[]{:S(2)}) collective-permute-start(bf16[7,32,256]{2,1,0:T(8,128)(2,1)S(1)} %get-tuple-element.26), channel_id=1, source_target_pairs={{8,16},{16,8},{9,17},{17,9},{10,18},{18,10},{11,19},{19,11},{12,20... | collective-permute-start | bytes 344072 | tf_op jit(solution)/shard_map/ppermute | solution.py:521
  2.9 4.3 %copy-start.9 = (bf16[2,256,768]{2,1,0:T(8,128)(2,1)S(1)}, bf16[2,256,768]{2,1,0:T(8,128)(2,1)}, u32[]{:S(2)}) copy-start(bf16[2,256,768]{2,1,0:T(8,128)(2,1)} %qkv.1) | copy-start | bytes 2359300
  3.8 3.4 %copy-start.10 = (bf16[2,24,32,32]{3,2,1,0:T(8,128)(2,1)S(1)}, bf16[2,24,32,32]{3,2,1,0:T(8,128)(2,1)}, u32[]{:S(2)}) copy-start(bf16[2,24,32,32]{3,2,1,0:T(8,128)(2,1)} %group.1) | copy-start | bytes 294916
  3.8 3.4 %copy-start.11 = (f32[2,5,5,768]{3,0,2,1:T(2,128)S(1)}, f32[2,5,5,768]{3,0,2,1:T(2,128)}, u32[]{:S(2)}) copy-start(f32[2,5,5,768]{3,0,2,1:T(2,128)} %param.22) | copy-start | bytes 460804
  3.8 3.4 %copy-start.12 = (bf16[3,3,4,256]{3,2,1,0:T(4,128)(2,1)S(1)}, bf16[3,3,4,256]{3,2,1,0:T(4,128)(2,1)}, u32[]{:S(2)}) copy-start(bf16[3,3,4,256]{3,2,1,0:T(4,128)(2,1)} %head.1) | copy-start | bytes 55300
  3.9 5.3 %collective-permute-start.2 = (bf16[22,8,256]{2,1,0:T(8,128)(2,1)S(1)}, bf16[22,8,256]{2,1,0:T(8,128)(2,1)S(1)}, u32[]{:S(2)}, u32[]{:S(2)}) collective-permute-start(bf16[22,8,256]{2,1,0:T(8,128)(2,1)S(1)} %get-tuple-element.23), channel_id=1, source_target_pairs={{0,1},{1,0},{2,3},{3,2},{4,5},{5,4},{6,7},{7,6},{8,9},{9,8},{10,11... | collective-permute-start | bytes 270344 | tf_op jit(solution)/shard_map/ppermute | solution.py:521
  6.5 2.7 %collective-permute-start.3 = (bf16[22,8,256]{2,1,0:T(8,128)(2,1)S(1)}, bf16[22,8,256]{2,1,0:T(8,128)(2,1)S(1)}, u32[]{:S(2)}, u32[]{:S(2)}) collective-permute-start(bf16[22,8,256]{2,1,0:T(8,128)(2,1)S(1)} %get-tuple-element.22), channel_id=1, source_target_pairs={{1,2},{2,1},{3,4},{4,3},{5,6},{6,5},{9,10},{10,9},{11,12},{12,11},... | collective-permute-start | bytes 270344 | tf_op jit(solution)/shard_map/ppermute | solution.py:521
  9.8 40.8 %copy-start.2 = (bf16[2,512,256]{2,1,0:T(8,128)(2,1)S(1)}, bf16[2,512,256]{2,1,0:T(8,128)(2,1)}, u32[]{:S(2)}) copy-start(bf16[2,512,256]{2,1,0:T(8,128)(2,1)} %out_weight.3) | copy-start | bytes 1572868
  24.2 6.5 %collective-permute-start.4 = (bf16[144,128]{1,0:T(8,128)(2,1)S(1)}, bf16[144,128]{1,0:T(8,128)(2,1)S(1)}, u32[]{:S(2)}, u32[]{:S(2)}) collective-permute-start(bf16[144,128]{1,0:T(8,128)(2,1)S(1)} %get-tuple-element.17), channel_id=1, source_target_pairs={{0,8},{8,0},{16,24},{24,16},{1,9},{9,1},{17,25},{25,17},{2,10},{10... | collective-permute-start | bytes 110600 | tf_op jit(solution)/shard_map/ppermute | solution.py:495
  28.9 4.0 %collective-permute-start.5 = (bf16[144,128]{1,0:T(8,128)(2,1)S(1)}, bf16[144,128]{1,0:T(8,128)(2,1)S(1)}, u32[]{:S(2)}, u32[]{:S(2)}) collective-permute-start(bf16[144,128]{1,0:T(8,128)(2,1)S(1)} %get-tuple-element.17), channel_id=1, source_target_pairs={{0,16},{8,24},{16,0},{24,8},{1,17},{9,25},{17,1},{25,9},{2,18},{10... | collective-permute-start | bytes 110600 | tf_op jit(solution)/shard_map/ppermute | solution.py:495
  30.6 3.4 %collective-permute-start.6 = (bf16[144,128]{1,0:T(8,128)(2,1)S(1)}, bf16[144,128]{1,0:T(8,128)(2,1)S(1)}, u32[]{:S(2)}, u32[]{:S(2)}) collective-permute-start(bf16[144,128]{1,0:T(8,128)(2,1)S(1)} %get-tuple-element.17), channel_id=1, source_target_pairs={{0,24},{8,16},{16,8},{24,0},{1,25},{9,17},{17,9},{25,1},{2,26},{10... | collective-permute-start | bytes 110600 | tf_op jit(solution)/shard_map/ppermute | solution.py:495
  34.1 7.4 %collective-permute-start.7 = (bf16[144,128]{1,0:T(8,128)(2,1)S(1)}, bf16[144,128]{1,0:T(8,128)(2,1)S(1)}, u32[]{:S(2)}, u32[]{:S(2)}) collective-permute-start(bf16[144,128]{1,0:T(8,128)(2,1)S(1)} %add_convert_fusion.3), channel_id=1, source_target_pairs={{0,1},{1,0},{2,3},{3,2},{4,5},{5,4},{6,7},{7,6},{8,9},{9,8},{10,11... | collective-permute-start | bytes 110600 | tf_op jit(solution)/shard_map/ppermute | solution.py:495
  38.9 4.0 %collective-permute-start.8 = (bf16[144,128]{1,0:T(8,128)(2,1)S(1)}, bf16[144,128]{1,0:T(8,128)(2,1)S(1)}, u32[]{:S(2)}, u32[]{:S(2)}) collective-permute-start(bf16[144,128]{1,0:T(8,128)(2,1)S(1)} %add_convert_fusion.3), channel_id=1, source_target_pairs={{0,2},{1,3},{2,0},{3,1},{4,6},{5,7},{6,4},{7,5},{8,10},{9,11},{10,... | collective-permute-start | bytes 110600 | tf_op jit(solution)/shard_map/ppermute | solution.py:495
  40.5 4.9 %collective-permute-start.9 = (bf16[144,128]{1,0:T(8,128)(2,1)S(1)}, bf16[144,128]{1,0:T(8,128)(2,1)S(1)}, u32[]{:S(2)}, u32[]{:S(2)}) collective-permute-start(bf16[144,128]{1,0:T(8,128)(2,1)S(1)} %add_convert_fusion.3), channel_id=1, source_target_pairs={{0,3},{1,2},{2,1},{3,0},{4,7},{5,6},{6,5},{7,4},{8,11},{9,10},{10,... | collective-permute-start | bytes 110600 | tf_op jit(solution)/shard_map/ppermute | solution.py:495
  45.4 5.2 %copy-start.8 = (f32[2,256]{1,0:T(2,128)S(1)}, f32[2,256]{1,0:T(2,128)}, u32[]{:S(2)}) copy-start(f32[2,256]{1,0:T(2,128)} %out_bias.3) | copy-start | bytes 6148
  45.4 5.2 %collective-permute-start.10 = (bf16[144,128]{1,0:T(8,128)(2,1)S(1)}, bf16[144,128]{1,0:T(8,128)(2,1)S(1)}, u32[]{:S(2)}, u32[]{:S(2)}) collective-permute-start(bf16[144,128]{1,0:T(8,128)(2,1)S(1)} %add_convert_fusion.2.payload), channel_id=1, source_target_pairs={{0,4},{1,5},{2,6},{3,7},{4,0},{5,1},{6,2},{7,3},{8,12},{9,13},{10,... | collective-permute-start | bytes 110600 | tf_op jit(solution)/shard_map/ppermute | solution.py:495
  63.2 1.9 %collective-permute-start.11 = (bf16[144,128]{1,0:T(8,128)(2,1)S(1)}, bf16[144,128]{1,0:T(8,128)(2,1)S(1)}, u32[]{:S(2)}, u32[]{:S(2)}) collective-permute-start(bf16[144,128]{1,0:T(8,128)(2,1)S(1)} %get-tuple-element.20), channel_id=1, source_target_pairs={{0,8},{8,0},{16,24},{24,16},{1,9},{9,1},{17,25},{25,17},{2,10},{10... | collective-permute-start | bytes 110600 | tf_op jit(solution)/shard_map/ppermute | solution.py:495
  63.3 4.2 %collective-permute-start.12 = (bf16[144,128]{1,0:T(8,128)(2,1)S(1)}, bf16[144,128]{1,0:T(8,128)(2,1)S(1)}, u32[]{:S(2)}, u32[]{:S(2)}) collective-permute-start(bf16[144,128]{1,0:T(8,128)(2,1)S(1)} %get-tuple-element.20), channel_id=1, source_target_pairs={{0,16},{8,24},{16,0},{24,8},{1,17},{9,25},{17,1},{25,9},{2,18},{10... | collective-permute-start | bytes 110600 | tf_op jit(solution)/shard_map/ppermute | solution.py:495
  64.1 3.8 %collective-permute-start.13 = (bf16[144,128]{1,0:T(8,128)(2,1)S(1)}, bf16[144,128]{1,0:T(8,128)(2,1)S(1)}, u32[]{:S(2)}, u32[]{:S(2)}) collective-permute-start(bf16[144,128]{1,0:T(8,128)(2,1)S(1)} %get-tuple-element.20), channel_id=1, source_target_pairs={{0,24},{8,16},{16,8},{24,0},{1,25},{9,17},{17,9},{25,1},{2,26},{10... | collective-permute-start | bytes 110600 | tf_op jit(solution)/shard_map/ppermute | solution.py:495
  67.9 4.0 %collective-permute-start.14 = (bf16[144,128]{1,0:T(8,128)(2,1)S(1)}, bf16[144,128]{1,0:T(8,128)(2,1)S(1)}, u32[]{:S(2)}, u32[]{:S(2)}) collective-permute-start(bf16[144,128]{1,0:T(8,128)(2,1)S(1)} %add_convert_fusion.1), channel_id=1, source_target_pairs={{0,1},{1,0},{2,3},{3,2},{4,5},{5,4},{6,7},{7,6},{8,9},{9,8},{10,11... | collective-permute-start | bytes 110600 | tf_op jit(solution)/shard_map/ppermute | solution.py:495
  69.2 4.0 %collective-permute-start.15 = (bf16[144,128]{1,0:T(8,128)(2,1)S(1)}, bf16[144,128]{1,0:T(8,128)(2,1)S(1)}, u32[]{:S(2)}, u32[]{:S(2)}) collective-permute-start(bf16[144,128]{1,0:T(8,128)(2,1)S(1)} %add_convert_fusion.1), channel_id=1, source_target_pairs={{0,2},{1,3},{2,0},{3,1},{4,6},{5,7},{6,4},{7,5},{8,10},{9,11},{10,... | collective-permute-start | bytes 110600 | tf_op jit(solution)/shard_map/ppermute | solution.py:495
  69.3 4.9 %collective-permute-start.16 = (bf16[144,128]{1,0:T(8,128)(2,1)S(1)}, bf16[144,128]{1,0:T(8,128)(2,1)S(1)}, u32[]{:S(2)}, u32[]{:S(2)}) collective-permute-start(bf16[144,128]{1,0:T(8,128)(2,1)S(1)} %add_convert_fusion.1), channel_id=1, source_target_pairs={{0,3},{1,2},{2,1},{3,0},{4,7},{5,6},{6,5},{7,4},{8,11},{9,10},{10,... | collective-permute-start | bytes 110600 | tf_op jit(solution)/shard_map/ppermute | solution.py:495
  74.2 4.9 %collective-permute-start.17 = (bf16[144,128]{1,0:T(8,128)(2,1)S(1)}, bf16[144,128]{1,0:T(8,128)(2,1)S(1)}, u32[]{:S(2)}, u32[]{:S(2)}) collective-permute-start(bf16[144,128]{1,0:T(8,128)(2,1)S(1)} %add_convert_fusion.payload), channel_id=1, source_target_pairs={{0,4},{1,5},{2,6},{3,7},{4,0},{5,1},{6,2},{7,3},{8,12},{9,13},{10,... | collective-permute-start | bytes 110600 | tf_op jit(solution)/shard_map/ppermute | solution.py:495
  (8 other events, 14.6 us)

commit v8 on v6

--- a/solution.py
+++ b/solution.py
@@ -25,6 +25,20 @@
 def parted(count, parts):
     cuts = [count * k // parts for k in range(parts + 1)]
     return [(a, b - a) for a, b in zip(cuts, cuts[1:]) if b > a]
+
+
+def group_size(count, most):
+    return next(n for n in range(min(most, count), 0, -1) if count % n == 0)
+
+
+def by_groups(count, most, body):
+    size = group_size(count, most)
+
+    def group(index, carry):
+        body(index * size, size)
+        return carry
+
+    lax.fori_loop(0, count // size, group, 0)
 
 
 def clear_outside(ref, halo, cols):
@@ -241,14 +255,10 @@
     mixed_in, query_in, payloads, weight, bias, mixed_ref, query_ref, sems, head_dim, section, x_ref
 ):
     rows, width, channels = x_ref.shape
-    groups = parted(rows, PARTS)
-    loads = []
-    for index, (first, size) in enumerate(groups):
-        here = pl.ds(first, size)
-        for at, (source, target) in enumerate(((query_in, query_ref), (mixed_in, mixed_ref))):
-            load = pltpu.make_async_copy(source.at[here], target.at[here], sems.at[at, index])
-            load.start()
-            loads.append(load)
+    halves = [(query_in, query_ref), (mixed_in, mixed_ref)]
+    loads = [pltpu.make_async_copy(a, b, sems.at[k]) for k, (a, b) in enumerate(halves)]
+    for load in loads:
+        load.start()
     same = same_head(head_dim)
     square = (LANES, LANES)
     diagonal = lax.broadcasted_iota(jnp.int32, square, 0) == lax.broadcasted_iota(
@@ -281,10 +291,11 @@
     summaries = [paired(summaries, index) for index in range(0, count, 2)]
     sums = [paired(sums, index) for index in range(0, count, 2)]
     step = 2 * LANES
-    for index, (first, size) in enumerate(groups):
-        for load in loads[2 * index : 2 * index + 2]:
-            load.wait()
-        query = flat(query_ref[first : first + size])
+    for load in loads:
+        load.wait()
+
+    def attend_rows(first, size):
+        query = flat(query_ref[pl.ds(first, size)])
         parts = []
         for branch in range(count // 2):
             part = query[:, branch * step : (branch + 1) * step]
@@ -297,8 +308,10 @@
             jnp.concatenate(parts, axis=1), weight[section], preferred_element_type=F32
         )
         value = value + bias[section : section + 1, :]
-        value = value + flat(mixed_ref[first : first + size]).astype(F32)
-        x_ref[first : first + size] = value.astype(BF16).reshape(size, width, channels)
+        value = value + flat(mixed_ref[pl.ds(first, size)]).astype(F32)
+        x_ref[pl.ds(first, size)] = value.astype(BF16).reshape(size, width, channels)
+
+    by_groups(rows, 5, attend_rows)
 
 
 def tap(section, a, b):
@@ -360,25 +373,15 @@
         store.wait()
 
 
-def first_kernel(tile, head_dim, own, row_0, row_1, col_0, col_1, *refs):
+def first_kernel(tile, head_dim, own, row_0, row_1, *refs):
     weights, outs, scratch = refs[:9], refs[9:12], refs[12:]
     x_ref = scratch[0]
     rows, cols = tile
-    x_ref[REACH : REACH + rows, 0:cols, :] = own[...]
     below = REACH + rows
-    even = lax.axis_index("row") % 2 == 0
-    x_ref[pl.ds(jnp.where(even, below, 0), REACH), 0:cols, :] = row_0[...]
-    x_ref[pl.ds(jnp.where(even, 0, below), REACH), 0:cols, :] = row_1[...]
-    even = lax.axis_index("col") % 2 == 0
-
-    @pl.when(even)
-    def _():
-        x_ref[:, cols : cols + 2 * SIDE, :] = jnp.concatenate([col_0[...], col_1[...]], axis=1)
-
-    @pl.when(jnp.logical_not(even))
-    def _():
-        x_ref[:, cols : cols + 2 * SIDE, :] = jnp.concatenate([col_1[...], col_0[...]], axis=1)
-
+    even = lax.axis_index("row") & 1 == 0
+    x_ref[REACH:below] = own[...]
+    x_ref[pl.ds(jnp.where(even, below, 0), REACH)] = row_0[...]
+    x_ref[pl.ds(jnp.where(even, 0, below), REACH)] = row_1[...]
     front(x_ref, weights, outs, scratch[1:], REACH, tile, head_dim, 0)
 
 
@@ -525,15 +528,17 @@
             lax.dynamic_slice_in_dim(value, jnp.where(odd == at, far, 0), size, dim) for at in (0, 1)
         ]
 
-    odd_row = lax.axis_index("row") % 2
-    odd_col = lax.axis_index("col") % 2
-    low, high = edges(features, 0, REACH, odd_row)
-    row_halos = [pair_exchange(low, "row", 0), pair_exchange(high, "row", 1)]
-    below = jnp.where(odd_row == 0, row_halos[0], row_halos[1])
-    above = jnp.where(odd_row == 0, row_halos[1], row_halos[0])
-    tall = jnp.concatenate([above, features, below], axis=0)
-    low, high = edges(tall, 1, SIDE, odd_col)
-    col_halos = [pair_exchange(low, "col", 0), pair_exchange(high, "col", 1)]
+    odd_row = lax.axis_index("row") & 1
+    odd_col = lax.axis_index("col") & 1
+    low, high = edges(features, 1, SIDE, odd_col)
+    col_1 = pair_exchange(high, "col", 1)
+    col_0 = pair_exchange(low, "col", 0)
+    right = jnp.where(odd_col == 0, col_0, col_1)
+    left = jnp.where(odd_col == 0, col_1, col_0)
+    wide_rows = jnp.concatenate([features, right, left], axis=1)
+    low, high = edges(wide_rows, 0, REACH, odd_row)
+    row_1 = pair_exchange(high, "row", 1)
+    row_0 = pair_exchange(low, "row", 0)
 
     aggregate_depth = aggregate_depth.transpose(1, 2, 0, 3)
     depth_weight = depth_weight.transpose(1, 2, 0, 3)
@@ -593,7 +598,7 @@
             pltpu.VMEM((count, width, channels), BF16),
             pltpu.VMEM((count, width, channels), BF16),
             pltpu.VMEM((count, width, 2 * channels), BF16),
-            pltpu.SemaphoreType.DMA((2, PARTS)),
+            pltpu.SemaphoreType.DMA((2,)),
         ]
 
     first_rows = rows + 2 * REACH
@@ -601,13 +606,13 @@
         functools.partial(first_kernel, tile, head_dim),
         out_shape=outs_of(first_rows - 6),
         grid=(1,),
-        in_specs=[near()] * 5 + weight_specs,
+        in_specs=[near()] * 3 + weight_specs,
         out_specs=[far(), far(), near()],
         scratch_shapes=[pltpu.VMEM((first_rows, width, channels), BF16)]
         + front_scratch(first_rows),
         compiler_params=params,
         name="first",
-    )(features, *row_halos, *col_halos, *weights)
+    )(wide_rows, row_0, row_1, *weights)
     payload, other = sum_by_permutes(payload)
 
     second_rows = first_rows - 6

time: 82.4 us -> 80.5 us (0.977)
  Pallas kernels: 31.6 us -> 29 us
  waiting for transfers between devices: 17.8 us -> 18.8 us
  other arithmetic: 0.16 us -> 1.03 us
    pallas_call x1, Pallas kernels: 13.6 us -> 12 us  [local(): pl.pallas_call(functools.partial(second_kernel, tile, head_dim), out_shap...]
    pallas_call x1, Pallas kernels: 4.32 us -> 3.33 us  [local(): pl.pallas_call(functools.partial(last_kernel, tile, head_dim), out_shape=...]
    ppermute x4, waiting for transfers between devices: 0.27 us -> 1.23 us  [pair_exchange(): return lax.ppermute(value, axis, pairs)]
    concatenate x1, other arithmetic: 0.04 us -> 0.92 us  [local(): wide_rows = jnp.concatenate([features, right, left], axis=1)]
where the time goes in v8:
time: 80.5 us; the launch traced here: 80.3 us
  Pallas kernels  29 us (36%)
  starting transfers between devices  28.8 us (36%)
  waiting for transfers between devices  18.8 us (23%)
  local copies, waits for them, and re-layouts  1.73 us (2%)
  between operations  1.05 us (1%)
  other arithmetic  1.03 us (1%)
    ppermute x14, starting transfers between devices, sum_by_permutes(): lax.ppermute(value, axis, [(i, partner(i, stride, radix, k)) for i in ran...  24.3 us
    ppermute x14, waiting for transfers between devices, sum_by_permutes(): lax.ppermute(value, axis, [(i, partner(i, stride, radix, k)) for i in ran...  17.6 us
    pallas_call x1, Pallas kernels, local(): pl.pallas_call(functools.partial(second_kernel, tile, head_dim), out_shap...  12 us
    pallas_call x1, Pallas kernels, local(): pl.pallas_call(functools.partial(first_kernel, tile, head_dim), out_shape...  11.7 us
    ppermute x4, starting transfers between devices, pair_exchange(): return lax.ppermute(value, axis, pairs)  4.49 us
    pallas_call x1, Pallas kernels, local(): pl.pallas_call(functools.partial(last_kernel, tile, head_dim), out_shape=...  3.33 us
    pallas_call x1, Pallas kernels, local(): pl.pallas_call(functools.partial(prepare_kernel, head_dim), out_shape=mad...  1.9 us
  transfers between devices with their start and end apart: 18, of which 12 were waited for; matrix products, arithmetic and copies ran while one was open for 0% of the time, Pallas kernels for 2%

profile of v8, /device:TPU:0, one launch (start us, length us, event | category | flops | bytes accessed | tf_op | source)
XLA Modules:
  0.0 80.3 jit_solution(3901416188435450668)
XLA Ops:
  1.5 3.0 %collective-permute-start = (bf16[8,8,256]{2,1,0:T(8,128)(2,1)S(1)}, bf16[8,8,256]{2,1,0:T(8,128)(2,1)S(1)}, u32[]{:S(2)}, u32[]{:S(2)}) collective-permute-start(bf16[8,8,256]{2,1,0:T(8,128)(2,1)S(1)} %get-tuple-element.24), channel_id=1, source_target_pairs={{0,1},{1,0},{2,3},{3,2},{4,5},{5,4},{6,7},{7,6},{8,9},{9,8},{10,11... | collective-permute-start | bytes 98312 | tf_op jit(solution)/shard_map/ppermute | solution.py:499
  5.1 1.2 %collective-permute-done = bf16[8,8,256]{2,1,0:T(8,128)(2,1)S(1)} collective-permute-done((bf16[8,8,256]{2,1,0:T(8,128)(2,1)S(1)}, bf16[8,8,256]{2,1,0:T(8,128)(2,1)S(1)}, u32[]{:S(2)}, u32[]{:S(2)}) %collective-permute-start) | collective-permute-done | bytes 32800 | tf_op jit(solution)/shard_map/ppermute | solution.py:499
  8.4 1.9 %prepare.1 = (bf16[2,256,768]{2,1,0:T(8,128)(2,1)S(1)}, f32[2,32,768]{2,1,0:T(8,128)S(1)}, bf16[2,3,256,256]{3,2,1,0:T(8,128)(2,1)S(1)}, bf16[3,128,256]{2,1,0:T(8,128)(2,1)S(1)}) custom-call(bf16[2,256,768]{2,1,0:T(8,128)(2,1)S(1)} %copy-done.8, f32[5,5,2,768]{3,2,1,0:T(2,128)S(1)} %bitcast.5, bf16[2,24,32,32]{3,2,1,0:T(8,128)(2,1)S(1)} %copy-done.9, ...), custom_call_target="tpu_custom_call" | custom-call | flops 2000000000 | bytes 4000000 | tf_op jit(solution)/shard_map/prepare/pallas_call | solution.py:552
  11.0 11.7 %first.1 = (bf16[16,48,256]{2,1,0:T(8,128)(2,1)S(1)}, bf16[16,48,512]{2,1,0:T(8,128)(2,1)S(1)}, bf16[144,128]{1,0:T(8,128)(2,1)S(1)}) custom-call(bf16[8,48,256]{2,1,0:T(8,128)(2,1)S(1)} %pad_maximum_fusion.own, bf16[7,48,256]{2,1,0:T(8,128)(2,1)S(1)} %collective-permute-done.2.row_0, bf16[7,48,256]{2,1,0:T(8,128)(2,1)S(1)} %collective-permute-done.3.row_1, ...), custom_call_target="tpu_custom_call" | custom-call | tf_op jit(solution)/shard_map/first/pallas_call | solution.py:605
  22.7 4.4 %collective-permute-start.4 = (bf16[144,128]{1,0:T(8,128)(2,1)S(1)}, bf16[144,128]{1,0:T(8,128)(2,1)S(1)}, u32[]{:S(2)}, u32[]{:S(2)}) collective-permute-start(bf16[144,128]{1,0:T(8,128)(2,1)S(1)} %get-tuple-element.17), channel_id=1, source_target_pairs={{0,8},{8,0},{16,24},{24,16},{1,9},{9,1},{17,25},{25,17},{2,10},{10... | collective-permute-start | bytes 110600 | tf_op jit(solution)/shard_map/ppermute | solution.py:473
  27.1 1.7 %collective-permute-start.5 = (bf16[144,128]{1,0:T(8,128)(2,1)S(1)}, bf16[144,128]{1,0:T(8,128)(2,1)S(1)}, u32[]{:S(2)}, u32[]{:S(2)}) collective-permute-start(bf16[144,128]{1,0:T(8,128)(2,1)S(1)} %get-tuple-element.17), channel_id=1, source_target_pairs={{0,16},{8,24},{16,0},{24,8},{1,17},{9,25},{17,1},{25,9},{2,18},{10... | collective-permute-start | bytes 110600 | tf_op jit(solution)/shard_map/ppermute | solution.py:473
  28.9 2.2 %collective-permute-done.5 = bf16[144,128]{1,0:T(8,128)(2,1)S(1)} collective-permute-done((bf16[144,128]{1,0:T(8,128)(2,1)S(1)}, bf16[144,128]{1,0:T(8,128)(2,1)S(1)}, u32[]{:S(2)}, u32[]{:S(2)}) %collective-permute-start.5) | collective-permute-done | bytes 36896 | tf_op jit(solution)/shard_map/ppermute | solution.py:473
  31.1 1.2 %collective-permute-done.6 = bf16[144,128]{1,0:T(8,128)(2,1)S(1)} collective-permute-done((bf16[144,128]{1,0:T(8,128)(2,1)S(1)}, bf16[144,128]{1,0:T(8,128)(2,1)S(1)}, u32[]{:S(2)}, u32[]{:S(2)}) %collective-permute-start.6) | collective-permute-done | bytes 36896 | tf_op jit(solution)/shard_map/ppermute | solution.py:473
  32.3 4.8 %collective-permute-start.7 = (bf16[144,128]{1,0:T(8,128)(2,1)S(1)}, bf16[144,128]{1,0:T(8,128)(2,1)S(1)}, u32[]{:S(2)}, u32[]{:S(2)}) collective-permute-start(bf16[144,128]{1,0:T(8,128)(2,1)S(1)} %add_convert_fusion.3), channel_id=1, source_target_pairs={{0,1},{1,0},{2,3},{3,2},{4,5},{5,4},{6,7},{7,6},{8,9},{9,8},{10,11... | collective-permute-start | bytes 110600 | tf_op jit(solution)/shard_map/ppermute | solution.py:473
  37.1 1.6 %collective-permute-start.8 = (bf16[144,128]{1,0:T(8,128)(2,1)S(1)}, bf16[144,128]{1,0:T(8,128)(2,1)S(1)}, u32[]{:S(2)}, u32[]{:S(2)}) collective-permute-start(bf16[144,128]{1,0:T(8,128)(2,1)S(1)} %add_convert_fusion.3), channel_id=1, source_target_pairs={{0,2},{1,3},{2,0},{3,1},{4,6},{5,7},{6,4},{7,5},{8,10},{9,11},{10,... | collective-permute-start | bytes 110600 | tf_op jit(solution)/shard_map/ppermute | solution.py:473
  39.7 1.4 %collective-permute-done.8 = bf16[144,128]{1,0:T(8,128)(2,1)S(1)} collective-permute-done((bf16[144,128]{1,0:T(8,128)(2,1)S(1)}, bf16[144,128]{1,0:T(8,128)(2,1)S(1)}, u32[]{:S(2)}, u32[]{:S(2)}) %collective-permute-start.8) | collective-permute-done | bytes 36896 | tf_op jit(solution)/shard_map/ppermute | solution.py:473
  41.1 2.5 %collective-permute-done.9 = bf16[144,128]{1,0:T(8,128)(2,1)S(1)} collective-permute-done((bf16[144,128]{1,0:T(8,128)(2,1)S(1)}, bf16[144,128]{1,0:T(8,128)(2,1)S(1)}, u32[]{:S(2)}, u32[]{:S(2)}) %collective-permute-start.9) | collective-permute-done | bytes 36896 | tf_op jit(solution)/shard_map/ppermute | solution.py:473
  43.6 2.2 %collective-permute-start.10 = (bf16[144,128]{1,0:T(8,128)(2,1)S(1)}, bf16[144,128]{1,0:T(8,128)(2,1)S(1)}, u32[]{:S(2)}, u32[]{:S(2)}) collective-permute-start(bf16[144,128]{1,0:T(8,128)(2,1)S(1)} %add_convert_fusion.2.payload), channel_id=1, source_target_pairs={{0,4},{1,5},{2,6},{3,7},{4,0},{5,1},{6,2},{7,3},{8,12},{9,13},{10,... | collective-permute-start | bytes 110600 | tf_op jit(solution)/shard_map/ppermute | solution.py:473
  45.8 3.0 %collective-permute-done.10.other = bf16[144,128]{1,0:T(8,128)(2,1)S(1)} collective-permute-done((bf16[144,128]{1,0:T(8,128)(2,1)S(1)}, bf16[144,128]{1,0:T(8,128)(2,1)S(1)}, u32[]{:S(2)}, u32[]{:S(2)}) %collective-permute-start.10) | collective-permute-done | bytes 36896 | tf_op jit(solution)/shard_map/ppermute | solution.py:473
  48.8 12.0 %second.1 = (bf16[10,48,256]{2,1,0:T(8,128)(2,1)S(1)}, bf16[10,48,512]{2,1,0:T(8,128)(2,1)S(1)}, bf16[144,128]{1,0:T(8,128)(2,1)S(1)}) custom-call(bf16[16,48,256]{2,1,0:T(8,128)(2,1)S(1)} %get-tuple-element.15.mixed, bf16[16,48,512]{2,1,0:T(8,128)(2,1)S(1)} %get-tuple-element.16.query, bf16[144,128]{1,0:T(8,128)(2,1)S(1)} %add_convert_fusion.2.payload, ...), custom_call_target="tpu_custom_call" | custom-call | tf_op jit(solution)/shard_map/second/pallas_call | solution.py:619
  60.9 1.2 %collective-permute-start.12 = (bf16[144,128]{1,0:T(8,128)(2,1)S(1)}, bf16[144,128]{1,0:T(8,128)(2,1)S(1)}, u32[]{:S(2)}, u32[]{:S(2)}) collective-permute-start(bf16[144,128]{1,0:T(8,128)(2,1)S(1)} %get-tuple-element.20), channel_id=1, source_target_pairs={{0,16},{8,24},{16,0},{24,8},{1,17},{9,25},{17,1},{25,9},{2,18},{10... | collective-permute-start | bytes 110600 | tf_op jit(solution)/shard_map/ppermute | solution.py:473
  62.8 2.2 %collective-permute-done.12 = bf16[144,128]{1,0:T(8,128)(2,1)S(1)} collective-permute-done((bf16[144,128]{1,0:T(8,128)(2,1)S(1)}, bf16[144,128]{1,0:T(8,128)(2,1)S(1)}, u32[]{:S(2)}, u32[]{:S(2)}) %collective-permute-start.12) | collective-permute-done | bytes 36896 | tf_op jit(solution)/shard_map/ppermute | solution.py:473
  65.6 1.3 %collective-permute-start.14 = (bf16[144,128]{1,0:T(8,128)(2,1)S(1)}, bf16[144,128]{1,0:T(8,128)(2,1)S(1)}, u32[]{:S(2)}, u32[]{:S(2)}) collective-permute-start(bf16[144,128]{1,0:T(8,128)(2,1)S(1)} %add_convert_fusion.1), channel_id=1, source_target_pairs={{0,1},{1,0},{2,3},{3,2},{4,5},{5,4},{6,7},{7,6},{8,9},{9,8},{10,11... | collective-permute-start | bytes 110600 | tf_op jit(solution)/shard_map/ppermute | solution.py:473
  67.0 2.1 %collective-permute-start.16 = (bf16[144,128]{1,0:T(8,128)(2,1)S(1)}, bf16[144,128]{1,0:T(8,128)(2,1)S(1)}, u32[]{:S(2)}, u32[]{:S(2)}) collective-permute-start(bf16[144,128]{1,0:T(8,128)(2,1)S(1)} %add_convert_fusion.1), channel_id=1, source_target_pairs={{0,3},{1,2},{2,1},{3,0},{4,7},{5,6},{6,5},{7,4},{8,11},{9,10},{10,... | collective-permute-start | bytes 110600 | tf_op jit(solution)/shard_map/ppermute | solution.py:473
  69.6 1.2 %collective-permute-done.15 = bf16[144,128]{1,0:T(8,128)(2,1)S(1)} collective-permute-done((bf16[144,128]{1,0:T(8,128)(2,1)S(1)}, bf16[144,128]{1,0:T(8,128)(2,1)S(1)}, u32[]{:S(2)}, u32[]{:S(2)}) %collective-permute-start.15) | collective-permute-done | bytes 36896 | tf_op jit(solution)/shard_map/ppermute | solution.py:473
  70.8 1.0 %collective-permute-done.16 = bf16[144,128]{1,0:T(8,128)(2,1)S(1)} collective-permute-done((bf16[144,128]{1,0:T(8,128)(2,1)S(1)}, bf16[144,128]{1,0:T(8,128)(2,1)S(1)}, u32[]{:S(2)}, u32[]{:S(2)}) %collective-permute-start.16) | collective-permute-done | bytes 36896 | tf_op jit(solution)/shard_map/ppermute | solution.py:473
  71.9 3.0 %collective-permute-start.17 = (bf16[144,128]{1,0:T(8,128)(2,1)S(1)}, bf16[144,128]{1,0:T(8,128)(2,1)S(1)}, u32[]{:S(2)}, u32[]{:S(2)}) collective-permute-start(bf16[144,128]{1,0:T(8,128)(2,1)S(1)} %add_convert_fusion.payload), channel_id=1, source_target_pairs={{0,4},{1,5},{2,6},{3,7},{4,0},{5,1},{6,2},{7,3},{8,12},{9,13},{10,... | collective-permute-start | bytes 110600 | tf_op jit(solution)/shard_map/ppermute | solution.py:473
  75.0 1.8 %collective-permute-done.17.other = bf16[144,128]{1,0:T(8,128)(2,1)S(1)} collective-permute-done((bf16[144,128]{1,0:T(8,128)(2,1)S(1)}, bf16[144,128]{1,0:T(8,128)(2,1)S(1)}, u32[]{:S(2)}, u32[]{:S(2)}) %collective-permute-start.17) | collective-permute-done | bytes 36896 | tf_op jit(solution)/shard_map/ppermute | solution.py:473
  76.8 3.3 %last.1 = (bf16[8,32,256]{2,1,0:T(8,128)(2,1)}, f32[4,8,32]{2,1,0:T(8,128)}) custom-call(bf16[10,48,256]{2,1,0:T(8,128)(2,1)S(1)} %get-tuple-element.18.mixed, bf16[10,48,512]{2,1,0:T(8,128)(2,1)S(1)} %get-tuple-element.19.query, bf16[144,128]{1,0:T(8,128)(2,1)S(1)} %add_convert_fusion.payload, bf16[144,128]{1,0:T(8,128)(2,1)S(1)} %collective-permute-done.17.other, ...), custom_call_target="tpu_custom_call" | custom-call | tf_op jit(solution)/shard_map/last/pallas_call | solution.py:631
  (51 shorter events, 7.3 us)
Async XLA Ops:
  0.6 7.7 %copy-start.8 = (bf16[2,256,768]{2,1,0:T(8,128)(2,1)S(1)}, bf16[2,256,768]{2,1,0:T(8,128)(2,1)}, u32[]{:S(2)}) copy-start(bf16[2,256,768]{2,1,0:T(8,128)(2,1)} %qkv.1) | copy-start | bytes 2359300
  1.5 4.9 %collective-permute-start = (bf16[8,8,256]{2,1,0:T(8,128)(2,1)S(1)}, bf16[8,8,256]{2,1,0:T(8,128)(2,1)S(1)}, u32[]{:S(2)}, u32[]{:S(2)}) collective-permute-start(bf16[8,8,256]{2,1,0:T(8,128)(2,1)S(1)} %get-tuple-element.24), channel_id=1, source_target_pairs={{0,1},{1,0},{2,3},{3,2},{4,5},{5,4},{6,7},{7,6},{8,9},{9,8},{10,11... | collective-permute-start | bytes 98312 | tf_op jit(solution)/shard_map/ppermute | solution.py:499
  4.5 1.9 %collective-permute-start.1 = (bf16[8,8,256]{2,1,0:T(8,128)(2,1)S(1)}, bf16[8,8,256]{2,1,0:T(8,128)(2,1)S(1)}, u32[]{:S(2)}, u32[]{:S(2)}) collective-permute-start(bf16[8,8,256]{2,1,0:T(8,128)(2,1)S(1)} %get-tuple-element.25), channel_id=1, source_target_pairs={{1,2},{2,1},{3,4},{4,3},{5,6},{6,5},{9,10},{10,9},{11,12},{12,11},... | collective-permute-start | bytes 98312 | tf_op jit(solution)/shard_map/ppermute | solution.py:499
  7.4 2.9 %collective-permute-start.2 = (bf16[7,48,256]{2,1,0:T(8,128)(2,1)S(1)}, bf16[7,48,256]{2,1,0:T(8,128)(2,1)S(1)}, u32[]{:S(2)}, u32[]{:S(2)}) collective-permute-start(bf16[7,48,256]{2,1,0:T(8,128)(2,1)S(1)} %get-tuple-element.23), channel_id=1, source_target_pairs={{0,8},{8,0},{16,24},{24,16},{1,9},{9,1},{17,25},{25,17},{2,10},{10... | collective-permute-start | bytes 516104 | tf_op jit(solution)/shard_map/ppermute | solution.py:499
  7.5 2.8 %collective-permute-start.3 = (bf16[7,48,256]{2,1,0:T(8,128)(2,1)S(1)}, bf16[7,48,256]{2,1,0:T(8,128)(2,1)S(1)}, u32[]{:S(2)}, u32[]{:S(2)}) collective-permute-start(bf16[7,48,256]{2,1,0:T(8,128)(2,1)S(1)} %get-tuple-element.22), channel_id=1, source_target_pairs={{8,16},{16,8},{9,17},{17,9},{10,18},{18,10},{11,19},{19,11},{12,20... | collective-permute-start | bytes 516104 | tf_op jit(solution)/shard_map/ppermute | solution.py:499
  8.4 2.0 %copy-start.4 = (f32[2,1024]{1,0:T(2,128)S(1)}, f32[2,1024]{1,0:T(2,128)}, u32[]{:S(2)}) copy-start(f32[2,1024]{1,0:T(2,128)} %refs_1_.3) | copy-start | bytes 24580
  8.4 2.0 %copy-start.5 = (f32[2,1024]{1,0:T(2,128)S(1)}, f32[2,1024]{1,0:T(2,128)}, u32[]{:S(2)}) copy-start(f32[2,1024]{1,0:T(2,128)} %refs_3_.3) | copy-start | bytes 24580
  11.0 37.8 %copy-start.2 = (bf16[2,512,256]{2,1,0:T(8,128)(2,1)S(1)}, bf16[2,512,256]{2,1,0:T(8,128)(2,1)}, u32[]{:S(2)}) copy-start(bf16[2,512,256]{2,1,0:T(8,128)(2,1)} %out_weight.3) | copy-start | bytes 1572868
  22.7 6.2 %collective-permute-start.4 = (bf16[144,128]{1,0:T(8,128)(2,1)S(1)}, bf16[144,128]{1,0:T(8,128)(2,1)S(1)}, u32[]{:S(2)}, u32[]{:S(2)}) collective-permute-start(bf16[144,128]{1,0:T(8,128)(2,1)S(1)} %get-tuple-element.17), channel_id=1, source_target_pairs={{0,8},{8,0},{16,24},{24,16},{1,9},{9,1},{17,25},{25,17},{2,10},{10... | collective-permute-start | bytes 110600 | tf_op jit(solution)/shard_map/ppermute | solution.py:473
  27.1 4.0 %collective-permute-start.5 = (bf16[144,128]{1,0:T(8,128)(2,1)S(1)}, bf16[144,128]{1,0:T(8,128)(2,1)S(1)}, u32[]{:S(2)}, u32[]{:S(2)}) collective-permute-start(bf16[144,128]{1,0:T(8,128)(2,1)S(1)} %get-tuple-element.17), channel_id=1, source_target_pairs={{0,16},{8,24},{16,0},{24,8},{1,17},{9,25},{17,1},{25,9},{2,18},{10... | collective-permute-start | bytes 110600 | tf_op jit(solution)/shard_map/ppermute | solution.py:473
  28.8 3.4 %collective-permute-start.6 = (bf16[144,128]{1,0:T(8,128)(2,1)S(1)}, bf16[144,128]{1,0:T(8,128)(2,1)S(1)}, u32[]{:S(2)}, u32[]{:S(2)}) collective-permute-start(bf16[144,128]{1,0:T(8,128)(2,1)S(1)} %get-tuple-element.17), channel_id=1, source_target_pairs={{0,24},{8,16},{16,8},{24,0},{1,25},{9,17},{17,9},{25,1},{2,26},{10... | collective-permute-start | bytes 110600 | tf_op jit(solution)/shard_map/ppermute | solution.py:473
  32.3 7.4 %collective-permute-start.7 = (bf16[144,128]{1,0:T(8,128)(2,1)S(1)}, bf16[144,128]{1,0:T(8,128)(2,1)S(1)}, u32[]{:S(2)}, u32[]{:S(2)}) collective-permute-start(bf16[144,128]{1,0:T(8,128)(2,1)S(1)} %add_convert_fusion.3), channel_id=1, source_target_pairs={{0,1},{1,0},{2,3},{3,2},{4,5},{5,4},{6,7},{7,6},{8,9},{9,8},{10,11... | collective-permute-start | bytes 110600 | tf_op jit(solution)/shard_map/ppermute | solution.py:473
  37.1 4.0 %collective-permute-start.8 = (bf16[144,128]{1,0:T(8,128)(2,1)S(1)}, bf16[144,128]{1,0:T(8,128)(2,1)S(1)}, u32[]{:S(2)}, u32[]{:S(2)}) collective-permute-start(bf16[144,128]{1,0:T(8,128)(2,1)S(1)} %add_convert_fusion.3), channel_id=1, source_target_pairs={{0,2},{1,3},{2,0},{3,1},{4,6},{5,7},{6,4},{7,5},{8,10},{9,11},{10,... | collective-permute-start | bytes 110600 | tf_op jit(solution)/shard_map/ppermute | solution.py:473
  38.7 4.9 %collective-permute-start.9 = (bf16[144,128]{1,0:T(8,128)(2,1)S(1)}, bf16[144,128]{1,0:T(8,128)(2,1)S(1)}, u32[]{:S(2)}, u32[]{:S(2)}) collective-permute-start(bf16[144,128]{1,0:T(8,128)(2,1)S(1)} %add_convert_fusion.3), channel_id=1, source_target_pairs={{0,3},{1,2},{2,1},{3,0},{4,7},{5,6},{6,5},{7,4},{8,11},{9,10},{10,... | collective-permute-start | bytes 110600 | tf_op jit(solution)/shard_map/ppermute | solution.py:473
  43.6 5.2 %copy-start.7 = (f32[2,256]{1,0:T(2,128)S(1)}, f32[2,256]{1,0:T(2,128)}, u32[]{:S(2)}) copy-start(f32[2,256]{1,0:T(2,128)} %out_bias.3) | copy-start | bytes 6148
  43.6 5.2 %collective-permute-start.10 = (bf16[144,128]{1,0:T(8,128)(2,1)S(1)}, bf16[144,128]{1,0:T(8,128)(2,1)S(1)}, u32[]{:S(2)}, u32[]{:S(2)}) collective-permute-start(bf16[144,128]{1,0:T(8,128)(2,1)S(1)} %add_convert_fusion.2.payload), channel_id=1, source_target_pairs={{0,4},{1,5},{2,6},{3,7},{4,0},{5,1},{6,2},{7,3},{8,12},{9,13},{10,... | collective-permute-start | bytes 110600 | tf_op jit(solution)/shard_map/ppermute | solution.py:473
  60.8 1.9 %collective-permute-start.11 = (bf16[144,128]{1,0:T(8,128)(2,1)S(1)}, bf16[144,128]{1,0:T(8,128)(2,1)S(1)}, u32[]{:S(2)}, u32[]{:S(2)}) collective-permute-start(bf16[144,128]{1,0:T(8,128)(2,1)S(1)} %get-tuple-element.20), channel_id=1, source_target_pairs={{0,8},{8,0},{16,24},{24,16},{1,9},{9,1},{17,25},{25,17},{2,10},{10... | collective-permute-start | bytes 110600 | tf_op jit(solution)/shard_map/ppermute | solution.py:473
  60.9 4.0 %collective-permute-start.12 = (bf16[144,128]{1,0:T(8,128)(2,1)S(1)}, bf16[144,128]{1,0:T(8,128)(2,1)S(1)}, u32[]{:S(2)}, u32[]{:S(2)}) collective-permute-start(bf16[144,128]{1,0:T(8,128)(2,1)S(1)} %get-tuple-element.20), channel_id=1, source_target_pairs={{0,16},{8,24},{16,0},{24,8},{1,17},{9,25},{17,1},{25,9},{2,18},{10... | collective-permute-start | bytes 110600 | tf_op jit(solution)/shard_map/ppermute | solution.py:473
  62.1 3.4 %collective-permute-start.13 = (bf16[144,128]{1,0:T(8,128)(2,1)S(1)}, bf16[144,128]{1,0:T(8,128)(2,1)S(1)}, u32[]{:S(2)}, u32[]{:S(2)}) collective-permute-start(bf16[144,128]{1,0:T(8,128)(2,1)S(1)} %get-tuple-element.20), channel_id=1, source_target_pairs={{0,24},{8,16},{16,8},{24,0},{1,25},{9,17},{17,9},{25,1},{2,26},{10... | collective-permute-start | bytes 110600 | tf_op jit(solution)/shard_map/ppermute | solution.py:473
  65.6 4.0 %collective-permute-start.14 = (bf16[144,128]{1,0:T(8,128)(2,1)S(1)}, bf16[144,128]{1,0:T(8,128)(2,1)S(1)}, u32[]{:S(2)}, u32[]{:S(2)}) collective-permute-start(bf16[144,128]{1,0:T(8,128)(2,1)S(1)} %add_convert_fusion.1), channel_id=1, source_target_pairs={{0,1},{1,0},{2,3},{3,2},{4,5},{5,4},{6,7},{7,6},{8,9},{9,8},{10,11... | collective-permute-start | bytes 110600 | tf_op jit(solution)/shard_map/ppermute | solution.py:473
  66.9 4.0 %collective-permute-start.15 = (bf16[144,128]{1,0:T(8,128)(2,1)S(1)}, bf16[144,128]{1,0:T(8,128)(2,1)S(1)}, u32[]{:S(2)}, u32[]{:S(2)}) collective-permute-start(bf16[144,128]{1,0:T(8,128)(2,1)S(1)} %add_convert_fusion.1), channel_id=1, source_target_pairs={{0,2},{1,3},{2,0},{3,1},{4,6},{5,7},{6,4},{7,5},{8,10},{9,11},{10,... | collective-permute-start | bytes 110600 | tf_op jit(solution)/shard_map/ppermute | solution.py:473
  67.0 4.9 %collective-permute-start.16 = (bf16[144,128]{1,0:T(8,128)(2,1)S(1)}, bf16[144,128]{1,0:T(8,128)(2,1)S(1)}, u32[]{:S(2)}, u32[]{:S(2)}) collective-permute-start(bf16[144,128]{1,0:T(8,128)(2,1)S(1)} %add_convert_fusion.1), channel_id=1, source_target_pairs={{0,3},{1,2},{2,1},{3,0},{4,7},{5,6},{6,5},{7,4},{8,11},{9,10},{10,... | collective-permute-start | bytes 110600 | tf_op jit(solution)/shard_map/ppermute | solution.py:473
  71.9 3.0 %copy-start.12 = (f32[4]{0:T(128)S(1)}, f32[4]{0:T(128)}, u32[]{:S(2)}) copy-start(f32[4]{0:T(128)} %param.27) | copy-start | bytes 52
  71.9 4.9 %collective-permute-start.17 = (bf16[144,128]{1,0:T(8,128)(2,1)S(1)}, bf16[144,128]{1,0:T(8,128)(2,1)S(1)}, u32[]{:S(2)}, u32[]{:S(2)}) collective-permute-start(bf16[144,128]{1,0:T(8,128)(2,1)S(1)} %add_convert_fusion.payload), channel_id=1, source_target_pairs={{0,4},{1,5},{2,6},{3,7},{4,0},{5,1},{6,2},{7,3},{8,12},{9,13},{10,... | collective-permute-start | bytes 110600 | tf_op jit(solution)/shard_map/ppermute | solution.py:473
  (7 other events, 9.7 us)

commit v9 on v8

--- a/solution.py
+++ b/solution.py
@@ -10,16 +10,16 @@
 SECTIONS = 2
 LANES = 128
 SIDE = 8
+TILE = 16
 REACH = 7
 KEY_ROWS = 16
-TILE = 16
 PARTS = 4
 F32 = jnp.float32
 BF16 = jnp.bfloat16
 
 
-def six_hard_swish(value):
-    return value * jnp.minimum(jnp.maximum(value + 3.0, 0.0), 6.0)
+def six_hard_swish(value, bound=6.0):
+    return value * jnp.minimum(jnp.maximum(value + 3.0, 0.0), bound)
 
 
 def parted(count, parts):
@@ -41,9 +41,9 @@
     lax.fori_loop(0, count // size, group, 0)
 
 
-def clear_outside(ref, halo, cols):
+def clear_rows(ref, halo):
     rows = ref.shape[0]
-    row, col = lax.axis_index("row"), lax.axis_index("col")
+    row = lax.axis_index("row")
 
     @pl.when(row == 0)
     def _():
@@ -53,17 +53,37 @@
     def _():
         ref[rows - halo : rows] = jnp.zeros((halo,) + ref.shape[1:], ref.dtype)
 
-    @pl.when(col == 0)
-    def _():
-        ref[:, cols + SIDE : cols + 2 * SIDE, :] = jnp.zeros((rows, SIDE, ref.shape[2]), ref.dtype)
-
-    @pl.when(col == lax.axis_size("col") - 1)
-    def _():
-        ref[:, cols : cols + SIDE, :] = jnp.zeros((rows, SIDE, ref.shape[2]), ref.dtype)
+
+def column_of(low, count, total, lanes):
+    shape = (count, TILE, lanes)
+    number = lax.broadcasted_iota(jnp.int32, shape, 0) + low
+    column = lax.broadcasted_iota(jnp.int32, shape, 1) * total + number
+    width = total * TILE
+    return jnp.where(column < 0, column + width, jnp.where(column >= width, column - width, column))
+
+
+def inside(low, count, total, cols, lanes):
+    column = column_of(low, count, total, lanes)
+    col = lax.axis_index("col")
+    last = col == lax.axis_size("col") - 1
+    start = jnp.where(last, cols, cols + SIDE)
+    stop = jnp.where(col == 0, total * TILE, cols + SIDE)
+    return jnp.where((column >= start) & (column < stop), 0.0, 1.0)
+
+
+def class_of(value, number):
+    total = value.shape[0]
+    steps = number // total
+    part = value[number - steps * total]
+    return pltpu.roll(part, -steps % TILE, 0) if steps else part
 
 
 def flat(value):
     return value.reshape(-1, value.shape[-1])
+
+
+def wide(value):
+    return jnp.broadcast_to(value, (TILE, value.shape[1])).astype(BF16)
 
 
 def same_head(head_dim):
@@ -72,52 +92,59 @@
     return across == along
 
 
-def depthwise_row(rows, taps, size, width):
-    rows = [row.reshape(width // TILE, TILE, LANES) for row in rows]
-    total = None
+def depthwise_row(rows, taps, size, total):
+    value = None
     for b in range(size):
         part = None
         for a in range(size):
-            term = rows[a] * taps(a, b)[None]
+            term = rows[a][b : b + total] * taps(a, b)[None]
             part = term if part is None else part + term
-        part = part.reshape(width, LANES).astype(F32)
-        if b != size // 2:
-            part = pltpu.roll(part, (size // 2 - b) % width, 0)
-        total = part if total is None else total + part
-    return total
+        value = part if value is None else value + part
+    return value
 
 
 def front(x_ref, weights, outs, scratch, halo, tile, head_dim, section):
-    expand, expand_bias, depth, depth_bias, project, project_bias = weights[:6]
+    expand, expand_bias, depth, depth_bias, project = weights[:5]
     mixed_out, query_out, payload_out = outs
     (
-        hidden_0, hidden_1, total, mixed, qkv, query, wide_depth, wide_agg,
-        qkv_weight, agg, group, sems,
+        hidden_0, hidden_1, total, mixed, around_mixed, qkv, query, wide_depth, wide_agg, bound,
+        project_bias, qkv_weight, agg, group, sems,
     ) = scratch
     loads = [
-        pltpu.make_async_copy(weights[6].at[section], qkv_weight, sems.at[0]),
-        pltpu.make_async_copy(weights[7].at[section], agg, sems.at[1]),
-        pltpu.make_async_copy(weights[8].at[section], group, sems.at[2]),
+        pltpu.make_async_copy(weights[5], project_bias, sems.at[0]),
+        pltpu.make_async_copy(weights[6].at[section], qkv_weight, sems.at[1]),
+        pltpu.make_async_copy(weights[7].at[section], agg, sems.at[2]),
+        pltpu.make_async_copy(weights[8].at[section], group, sems.at[3]),
     ]
     for load in loads:
         load.start()
-    rows, width, channels = x_ref.shape
+    rows, channels = x_ref.shape[0], x_ref.shape[3]
+    classes = x_ref.shape[1] - 2
+    width = classes * TILE
     tile_rows, tile_cols = tile
     inner = rows - 2
-    chunk = hidden_0.shape[2]
+    chunk = hidden_0.shape[3]
     chunks = expand.shape[2] // chunk
+    this = slice(section, section + 1)
     for index in range(9):
-        taps = depth[index // 3, index % 3, section : section + 1, :] * (1.0 / 6.0)
-        wide_depth[index] = jnp.broadcast_to(taps, (TILE, taps.shape[1])).astype(BF16)
-    total[...] = 6.0 * (flat(x_ref[1 : rows - 1]).astype(F32) + project_bias[section : section + 1, :])
+        wide_depth[index] = wide(depth[index // 3, index % 3, this, :] * (1.0 / 6.0))
+    wide_depth[9] = wide(depth_bias[this, :])
+    bound[...] = (6.0 * inside(-1, classes + 2, classes, tile_cols, chunk)).astype(BF16)
+
+    def start_rows(first, size):
+        value = x_ref[pl.ds(first + 1, size), 1 : 1 + classes].astype(F32)
+        total[pl.ds(first, size)] = 6.0 * value
+
+    by_groups(inner, 2, start_rows)
 
     def expand_rows(out, at, first, size):
         value = jnp.dot(
             flat(x_ref[first : first + size]), expand[section, :, pl.ds(at, chunk)],
             preferred_element_type=F32,
         )
-        value = (value + expand_bias[section : section + 1, pl.ds(at, chunk)]).astype(BF16)
-        out[first : first + size] = six_hard_swish(value).reshape(size, width, chunk)
+        value = (value + expand_bias[this, pl.ds(at, chunk)]).astype(BF16)
+        value = value.reshape(size, classes + 2, TILE, chunk)
+        out[first : first + size] = six_hard_swish(value, bound[...][None])
 
     def spread_rows(hidden, at, first, size):
         spread = []
@@ -126,17 +153,16 @@
             for lane in range(0, chunk, LANES):
                 here = pl.ds(pl.multiple_of(at + lane, LANES), LANES)
                 value = depthwise_row(
-                    [hidden[r + a, :, lane : lane + LANES] for a in range(3)],
-                    lambda a, b: wide_depth[3 * a + b, :, here], 3, width,
+                    [hidden[r + a, :, :, lane : lane + LANES] for a in range(3)],
+                    lambda a, b: wide_depth[3 * a + b, :, here], 3, classes,
                 )
-                value = (value + depth_bias[section : section + 1, here]).astype(BF16)
-                lanes.append(six_hard_swish(value))
-            spread.append(jnp.concatenate(lanes, axis=1))
-        pixels = slice(first * width, (first + size) * width)
-        total[pixels] += jnp.dot(
-            jnp.concatenate(spread, axis=0), project[section, pl.ds(at, chunk), :],
+                lanes.append(six_hard_swish(value + wide_depth[9, :, here][None]))
+            spread.append(jnp.concatenate(lanes, axis=2))
+        value = jnp.dot(
+            flat(jnp.concatenate(spread, axis=0)), project[section, pl.ds(at, chunk), :],
             preferred_element_type=F32,
         )
+        total[first : first + size] += value.reshape(size, classes, TILE, channels)
 
     def stage(index, current, following):
         at = pl.multiple_of(index * chunk, chunk)
@@ -144,11 +170,11 @@
         for (first, size), (from_row, count) in zip(parted(inner, PARTS), parted(rows, PARTS)):
             expand_rows(following, ahead, from_row, count)
             spread_rows(current, at, first, size)
-        clear_outside(following, halo, tile_cols)
+        clear_rows(following, halo)
 
     for first, size in parted(rows, PARTS):
         expand_rows(hidden_0, 0, first, size)
-    clear_outside(hidden_0, halo, tile_cols)
+    clear_rows(hidden_0, halo)
 
     def two_stages(index, carry):
         stage(2 * index, hidden_0, hidden_1)
@@ -156,25 +182,44 @@
         return carry
 
     lax.fori_loop(0, chunks // 2, two_stages, 0)
-    mixed[...] = (total[...] * (1.0 / 6.0)).astype(BF16).reshape(inner, width, channels)
+    loads[0].wait()
+
+    def mixed_rows(index, carry):
+        value = total[index] * (1.0 / 6.0) + project_bias[this, :]
+        mixed[index] = value.astype(BF16)
+        for number in range(-2, classes + 2):
+            around_mixed[index, number + 2] = class_of(value, number).astype(BF16)
+        return carry
+
+    lax.fori_loop(0, inner, mixed_rows, 0)
     outer = inner - 4
     stores = [
-        pltpu.make_async_copy(mixed.at[pl.ds(2, outer)], mixed_out, sems.at[3]),
-        pltpu.make_async_copy(query, query_out, sems.at[4]),
+        pltpu.make_async_copy(mixed.at[pl.ds(2, outer)], mixed_out, sems.at[4]),
+        pltpu.make_async_copy(query, query_out, sems.at[5]),
     ]
     stores[0].start()
-    for load in loads:
+    for load in loads[1:]:
         load.wait()
     for index in range(25):
-        taps = agg[index : index + 1, :]
-        wide_agg[index] = jnp.broadcast_to(taps, (TILE, taps.shape[1])).astype(BF16)
+        wide_agg[index] = wide(agg[index : index + 1, :])
+    around = halo - 1
+    in_map = inside(-2, classes + 4, classes, tile_cols, channels).astype(BF16)
+
+    def qkv_rows(first, size, low, high):
+        value = jnp.dot(
+            flat(around_mixed[first : first + size]), qkv_weight[:, low:high],
+            preferred_element_type=F32,
+        )
+        value = value.astype(BF16).reshape(size, classes + 4, TILE, high - low)
+        for lane in range(low, high, channels):
+            part = value[..., lane - low : lane - low + channels]
+            qkv[first : first + size, :, :, lane : lane + channels] = part * in_map[None]
+
     for first, size in parted(inner, PARTS):
-        value = jnp.dot(
-            flat(mixed[first : first + size]), qkv_weight[...], preferred_element_type=F32
-        )
-        qkv[first : first + size] = value.astype(BF16).reshape(size, width, 3 * channels)
-    around = halo - 1
-    clear_outside(qkv, around, tile_cols)
+        qkv_rows(first, size, 0, channels)
+    for first, size in parted(tile_rows + 4, PARTS - 1):
+        qkv_rows(around - 2 + first, size, channels, 3 * channels)
+    clear_rows(qkv, around)
 
     def aggregated(kind, first, size):
         scaled = []
@@ -183,33 +228,30 @@
             for lane in range(kind * channels, (kind + 1) * channels, LANES):
                 here = slice(lane, lane + LANES)
                 value = depthwise_row(
-                    [qkv[first + r + a, :, here] for a in range(5)],
-                    lambda a, b: wide_agg[5 * a + b, :, here], 5, width,
+                    [qkv[first + r + a, :, :, here] for a in range(5)],
+                    lambda a, b: wide_agg[5 * a + b, :, here], 5, classes,
                 )
-                lanes.append(value.astype(BF16))
-            scaled.append(jnp.concatenate(lanes, axis=1))
+                lanes.append(value)
+            scaled.append(jnp.concatenate(lanes, axis=2))
         value = jnp.dot(
-            jnp.concatenate(scaled, axis=0), group[kind], preferred_element_type=F32
+            flat(jnp.concatenate(scaled, axis=0)), group[kind], preferred_element_type=F32
         )
-        return value.astype(BF16).reshape(size, width, channels)
-
-    query[:, :, 0:channels] = jnp.maximum(qkv[2 : inner - 2, :, 0:channels], 0.0)
-    size = next(n for n in range(5, 0, -1) if outer % n == 0)
-
-    def query_rows(index, carry):
-        at = index * size
-        query[pl.ds(at, size), :, channels : 2 * channels] = jnp.maximum(
-            aggregated(0, at, size), 0.0
-        )
-        return carry
-
-    lax.fori_loop(0, outer // size, query_rows, 0)
+        return value.astype(BF16).reshape(size, classes, TILE, channels)
+
+    def query_rows(first, size):
+        here = pl.ds(first, size)
+        centre = qkv[pl.ds(first + 2, size), 2 : 2 + classes, :, 0:channels]
+        query[here, :, :, 0:channels] = jnp.maximum(centre, 0.0)
+        query[here, :, :, channels : 2 * channels] = jnp.maximum(aggregated(0, first, size), 0.0)
+
+    by_groups(outer, 5, query_rows)
     stores[1].start()
-    size = next(n for n in range(4, 0, -1) if tile_rows % n == 0)
+    size = group_size(tile_rows, 4)
+    own = jnp.where(column_of(0, classes, classes, channels) < tile_cols, 1.0, 0.0).astype(BF16)
 
     def summed(key, value):
-        key = jnp.maximum(flat(key[:, 0:tile_cols]), 0.0)
-        value = flat(value[:, 0:tile_cols])
+        key = flat(jnp.maximum(key, 0.0) * own[None])
+        value = flat(value)
         products = [
             lax.dot_general(
                 key[:, lane : lane + LANES], value[:, lane : lane + LANES],
@@ -219,10 +261,8 @@
         ]
         return products, jnp.sum(key.astype(F32), axis=0, keepdims=True)
 
-    mine = slice(around, around + tile_rows)
-    products, sums = summed(
-        qkv[mine, :, channels : 2 * channels], qkv[mine, :, 2 * channels : 3 * channels]
-    )
+    mine = qkv[around : around + tile_rows, 2 : 2 + classes, :, channels : 3 * channels]
+    products, sums = summed(mine[..., 0:channels], mine[..., channels : 2 * channels])
 
     def grouped_rows(index, carry):
         at = around - 2 + index * size
@@ -252,10 +292,12 @@
 
 
 def attend(
-    mixed_in, query_in, payloads, weight, bias, mixed_ref, query_ref, sems, head_dim, section, x_ref
+    mixed_in, query_in, payloads, weight, bias_in, held, head_dim, section, x_ref, beyond
 ):
-    rows, width, channels = x_ref.shape
-    halves = [(query_in, query_ref), (mixed_in, mixed_ref)]
+    mixed_ref, query_ref, bias, sems = held
+    rows, channels = x_ref.shape[0], x_ref.shape[3]
+    classes = x_ref.shape[1] - 2 * beyond
+    halves = [(query_in, query_ref), (mixed_in, mixed_ref), (bias_in, bias)]
     loads = [pltpu.make_async_copy(a, b, sems.at[k]) for k, (a, b) in enumerate(halves)]
     for load in loads:
         load.start()
@@ -309,7 +351,11 @@
         )
         value = value + bias[section : section + 1, :]
         value = value + flat(mixed_ref[pl.ds(first, size)]).astype(F32)
-        x_ref[pl.ds(first, size)] = value.astype(BF16).reshape(size, width, channels)
+        value = value.reshape(size, classes, TILE, channels)
+        x_ref[pl.ds(first, size), beyond : beyond + classes] = value.astype(BF16)
+        for number in [*range(-beyond, 0), *range(classes, classes + beyond)]:
+            for r in range(size):
+                x_ref[first + r, number + beyond] = class_of(value[r], number).astype(BF16)
 
     by_groups(rows, 5, attend_rows)
 
@@ -375,38 +421,67 @@
 
 def first_kernel(tile, head_dim, own, row_0, row_1, *refs):
     weights, outs, scratch = refs[:9], refs[9:12], refs[12:]
-    x_ref = scratch[0]
-    rows, cols = tile
+    natural, x_ref = scratch[:2]
+    rows, width = own.shape[:2]
+    classes = x_ref.shape[1] - 2
+    even = lax.axis_index("row") & 1 == 0
     below = REACH + rows
-    even = lax.axis_index("row") & 1 == 0
-    x_ref[REACH:below] = own[...]
-    x_ref[pl.ds(jnp.where(even, below, 0), REACH)] = row_0[...]
-    x_ref[pl.ds(jnp.where(even, 0, below), REACH)] = row_1[...]
-    front(x_ref, weights, outs, scratch[1:], REACH, tile, head_dim, 0)
+    pieces = [
+        (own, REACH, rows),
+        (row_0, jnp.where(even, below, 0), REACH),
+        (row_1, jnp.where(even, 0, below), REACH),
+    ]
+    for piece, start, count in pieces:
+
+        def one_row(index, carry, piece=piece, start=start):
+            value = piece[index].astype(F32)
+            for lane in range(0, value.shape[1], LANES):
+                half = lane // LANES
+                part = value[:, lane : lane + LANES]
+                natural[half, 8 : 8 + width, :] = part
+                natural[half, 7:8, :] = part[width - 1 : width]
+                natural[half, 8 + width : 9 + width, :] = part[0:1]
+                for number in range(-1, classes + 1):
+                    part = natural[half, pl.ds(8 + number, TILE, stride=classes), :]
+                    x_ref[start + index, number + 1, :, lane : lane + LANES] = part.astype(BF16)
+            return carry
+
+        lax.fori_loop(0, count, one_row, 0)
+    front(x_ref, weights, outs, scratch[2:], REACH, tile, head_dim, 0)
 
 
 def second_kernel(tile, head_dim, mixed, query, payload, other, out_weight, out_bias, *refs):
     weights, outs, scratch = refs[:9], refs[9:12], refs[12:]
-    x_ref, mixed_ref, query_ref, sems = scratch[:4]
+    x_ref = scratch[0]
     attend(
-        mixed, query, (payload, other), out_weight, out_bias, mixed_ref, query_ref, sems, head_dim,
-        0, x_ref,
+        mixed, query, (payload, other), out_weight, out_bias, scratch[1:5], head_dim, 0, x_ref, 1
     )
-    front(x_ref, weights, outs, scratch[4:], REACH - 3, tile, head_dim, 1)
+    front(x_ref, weights, outs, scratch[5:], REACH - 3, tile, head_dim, 1)
 
 
 def last_kernel(
     tile, head_dim, mixed, query, payload, other, out_weight, out_bias, head_weight, head_bias,
-    map_out, boxes_out, x_ref, mixed_ref, query_ref, sems,
+    map_out, boxes_out, x_ref, mixed_ref, query_ref, bias, natural, sems,
 ):
     rows, cols = tile
-    width = cols + 2 * SIDE
+    classes, channels = x_ref.shape[1], x_ref.shape[3]
+    width = classes * TILE
     attend(
-        mixed, query, (payload, other), out_weight, out_bias, mixed_ref, query_ref, sems, head_dim,
-        1, x_ref,
+        mixed, query, (payload, other), out_weight, out_bias, (mixed_ref, query_ref, bias, sems),
+        head_dim, 1, x_ref, 0,
     )
-    clear_outside(x_ref, 1, cols)
-    map_out[...] = x_ref[1 : 1 + rows, 0:cols, :]
+    in_map = inside(0, classes, classes, cols, channels).astype(BF16)
+    x_ref[...] = x_ref[...] * in_map[None]
+    clear_rows(x_ref, 1)
+
+    def natural_row(value, r):
+        for number in range(classes):
+            natural[r, pl.ds(number, TILE, stride=classes), :] = value[number]
+
+    for lane in range(0, channels, LANES):
+        for r in range(rows):
+            natural_row(x_ref[1 + r, :, :, lane : lane + LANES].astype(F32), r)
+        map_out[:, :, lane : lane + LANES] = natural[:, 0:cols, :].astype(BF16)
     total = None
     for a in range(3):
         part = lax.dot_general(
@@ -414,22 +489,22 @@
             preferred_element_type=F32,
         )
         total = part if total is None else total + part
-    total = total.reshape(rows, width, LANES)
-    lane = lax.broadcasted_iota(jnp.int32, (width, LANES), 1) // 4
-    shifted = [
-        jnp.where(
-            lane == 0,
-            pltpu.roll(total[r], 1, 0),
-            jnp.where(lane == 2, pltpu.roll(total[r], width - 1, 0), total[r]),
+    total = total.reshape(rows, classes, TILE, LANES)
+    tap = lax.broadcasted_iota(jnp.int32, (TILE, LANES), 1) // 4
+    for r in range(rows):
+        numbers = [class_of(total[r], number) for number in range(-1, classes + 1)]
+        natural_row(
+            [
+                jnp.where(tap == 0, numbers[k], jnp.where(tap == 2, numbers[k + 2], numbers[k + 1]))
+                for k in range(classes)
+            ],
+            r,
         )
-        for r in range(rows)
-    ]
-    shifted = jnp.concatenate(shifted, axis=0)
     across = lax.broadcasted_iota(jnp.int32, (8, LANES), 0)
     along = lax.broadcasted_iota(jnp.int32, (8, LANES), 1)
     fold = jnp.where((along % 4 == across) & (along < 12), 1.0, 0.0)
     boxes = lax.dot_general(
-        fold, shifted, (((1,), (1,)), ((), ())), precision=lax.Precision.HIGHEST,
+        fold, flat(natural[...]), (((1,), (1,)), ((), ())), precision=lax.Precision.HIGHEST,
         preferred_element_type=F32,
     )
     boxes = boxes[0:4] + head_bias[...]
@@ -519,8 +594,9 @@
     head_dim = aggregate_group.shape[2]
     heads = channels // head_dim
     width = cols + 2 * SIDE
+    classes = width // TILE
     tile = (rows, cols)
-    wide = expand_weight.shape[2]
+    hidden = expand_weight.shape[2]
 
     def edges(value, dim, size, odd):
         far = value.shape[dim] - size
@@ -533,8 +609,8 @@
     low, high = edges(features, 1, SIDE, odd_col)
     col_1 = pair_exchange(high, "col", 1)
     col_0 = pair_exchange(low, "col", 0)
-    right = jnp.where(odd_col == 0, col_0, col_1)
-    left = jnp.where(odd_col == 0, col_1, col_0)
+    right = jnp.where(odd_col == 1, col_1, col_0)
+    left = jnp.where(odd_col == 1, col_0, col_1)
     wide_rows = jnp.concatenate([features, right, left], axis=1)
     low, high = edges(wide_rows, 0, REACH, odd_row)
     row_1 = pair_exchange(high, "row", 1)
@@ -568,37 +644,43 @@
         expand_weight, expand_bias, depth_weight, depth_bias, project_weight, project_bias,
         qkv_weight, taps, group,
     ]
-    weight_specs = [near()] * 6 + [far()] * 3
+    weight_specs = [near()] * 5 + [far()] * 4
+
+    def held(count, beyond, kinds=1):
+        return pltpu.VMEM((count, classes + 2 * beyond, TILE, kinds * channels), BF16)
 
     def outs_of(count):
         return [
-            jax.ShapeDtypeStruct((count, width, channels), BF16),
-            jax.ShapeDtypeStruct((count, width, 2 * channels), BF16),
+            jax.ShapeDtypeStruct((count, classes, TILE, channels), BF16),
+            jax.ShapeDtypeStruct((count, classes, TILE, 2 * channels), BF16),
             jax.ShapeDtypeStruct((LANES + KEY_ROWS, LANES), BF16),
         ]
 
     def front_scratch(count):
         return [
-            pltpu.VMEM((count, width, 256), BF16),
-            pltpu.VMEM((count, width, 256), BF16),
-            pltpu.VMEM(((count - 2) * width, channels), F32),
-            pltpu.VMEM((count - 2, width, channels), BF16),
-            pltpu.VMEM((count - 2, width, 3 * channels), BF16),
-            pltpu.VMEM((count - 6, width, 2 * channels), BF16),
-            pltpu.VMEM((9, TILE, expand_weight.shape[2]), BF16),
+            held(count, 1),
+            held(count, 1),
+            pltpu.VMEM((count - 2, classes, TILE, channels), F32),
+            held(count - 2, 0),
+            held(count - 2, 2),
+            held(count - 2, 2, 3),
+            held(count - 6, 0, 2),
+            pltpu.VMEM((10, TILE, hidden), BF16),
             pltpu.VMEM((25, TILE, 3 * channels), BF16),
+            pltpu.VMEM((classes + 2, TILE, channels), BF16),
+            pltpu.VMEM(project_bias.shape, F32),
             pltpu.VMEM(qkv_weight.shape[1:], BF16),
             pltpu.VMEM(taps.shape[1:], F32),
             pltpu.VMEM(group.shape[1:], BF16),
-            pltpu.SemaphoreType.DMA((5,)),
+            pltpu.SemaphoreType.DMA((6,)),
         ]
 
-    def attend_scratch(count):
+    def attend_scratch(count, beyond):
         return [
-            pltpu.VMEM((count, width, channels), BF16),
-            pltpu.VMEM((count, width, channels), BF16),
-            pltpu.VMEM((count, width, 2 * channels), BF16),
-            pltpu.SemaphoreType.DMA((2,)),
+            held(count, beyond),
+            held(count, 0),
+            held(count, 0, 2),
+            pltpu.VMEM(output_bias.shape, F32),
         ]
 
     first_rows = rows + 2 * REACH
@@ -608,7 +690,7 @@
         grid=(1,),
         in_specs=[near()] * 3 + weight_specs,
         out_specs=[far(), far(), near()],
-        scratch_shapes=[pltpu.VMEM((first_rows, width, channels), BF16)]
+        scratch_shapes=[pltpu.VMEM((channels // LANES, width + 16, LANES), F32), held(first_rows, 1)]
         + front_scratch(first_rows),
         compiler_params=params,
         name="first",
@@ -620,9 +702,11 @@
         functools.partial(second_kernel, tile, head_dim),
         out_shape=outs_of(second_rows - 6),
         grid=(1,),
-        in_specs=[far()] * 2 + [near()] * 4 + weight_specs,
+        in_specs=[far()] * 2 + [near()] * 3 + [far()] + weight_specs,
         out_specs=[far(), far(), near()],
-        scratch_shapes=attend_scratch(second_rows) + front_scratch(second_rows),
+        scratch_shapes=attend_scratch(second_rows, 1)
+        + [pltpu.SemaphoreType.DMA((3,))]
+        + front_scratch(second_rows),
         compiler_params=params,
         name="second",
     )(mixed, query, payload, other, output_weight, output_bias, *weights)
@@ -635,9 +719,10 @@
             jax.ShapeDtypeStruct((4, rows, cols), F32),
         ],
         grid=(1,),
-        in_specs=[far()] * 2 + [near()] * 6,
+        in_specs=[far()] * 2 + [near()] * 3 + [far()] + [near()] * 2,
         out_specs=[near()] * 2,
-        scratch_shapes=attend_scratch(rows + 2),
+        scratch_shapes=attend_scratch(rows + 2, 0)
+        + [pltpu.VMEM((rows, width, LANES), F32), pltpu.SemaphoreType.DMA((3,))],
         compiler_params=params,
         name="last",
     )(

time: 80.5 us -> 83.2 us (1.034)
  starting transfers between devices: 28.8 us -> 25.6 us
  waiting for transfers between devices: 18.8 us -> 21.7 us
  Pallas kernels: 29 us -> 31.8 us
    ppermute x14, starting transfers between devices: 24.3 us -> 18.3 us  [sum_by_permutes(): lax.ppermute(value, axis, [(i, partner(i, stride, radix, k)) for i in ran...]
    ppermute x4, starting transfers between devices: 4.49 us -> 7.32 us  [pair_exchange(): return lax.ppermute(value, axis, pairs)]
    ppermute x14, waiting for transfers between devices: 17.6 us -> 19.8 us  [sum_by_permutes(): lax.ppermute(value, axis, [(i, partner(i, stride, radix, k)) for i in ran...]
    pallas_call x1, Pallas kernels: 12 us -> 13.6 us  [local(): pl.pallas_call(functools.partial(second_kernel, tile, head_dim), out_shap...]
    pallas_call x1, Pallas kernels: 11.7 us -> 12.9 us  [local(): pl.pallas_call(functools.partial(first_kernel, tile, head_dim), out_shape...]
  transfers between devices with their start and end apart: 18 -> 18, of which waited for: 12 -> 13; matrix products, arithmetic and copies ran while one was open for 0% -> 0% of each run, Pallas kernels for 2% -> 2%
where the time goes in v9:
time: 83.2 us; the launch traced here: 83 us
  Pallas kernels  31.8 us (38%)
  starting transfers between devices  25.6 us (31%)
  waiting for transfers between devices  21.7 us (26%)
  local copies, waits for them, and re-layouts  1.73 us (2%)
  other arithmetic  1.03 us (1%)
  between operations  1.03 us (1%)
    ppermute x14, waiting for transfers between devices, sum_by_permutes(): lax.ppermute(value, axis, [(i, partner(i, stride, radix, k)) for i in ran...  19.8 us
    ppermute x14, starting transfers between devices, sum_by_permutes(): lax.ppermute(value, axis, [(i, partner(i, stride, radix, k)) for i in ran...  18.3 us
    pallas_call x1, Pallas kernels, local(): pl.pallas_call(functools.partial(second_kernel, tile, head_dim), out_shap...  13.6 us
    pallas_call x1, Pallas kernels, local(): pl.pallas_call(functools.partial(first_kernel, tile, head_dim), out_shape...  12.9 us
    ppermute x4, starting transfers between devices, pair_exchange(): return lax.ppermute(value, axis, pairs)  7.32 us
    pallas_call x1, Pallas kernels, local(): pl.pallas_call(functools.partial(last_kernel, tile, head_dim), out_shape=...  3.38 us
    ppermute x4, waiting for transfers between devices, pair_exchange(): return lax.ppermute(value, axis, pairs)  1.9 us
    pallas_call x1, Pallas kernels, local(): pl.pallas_call(functools.partial(prepare_kernel, head_dim), out_shape=mad...  1.9 us
  transfers between devices with their start and end apart: 18, of which 13 were waited for; matrix products, arithmetic and copies ran while one was open for 0% of the time, Pallas kernels for 2%

profile of v9, /device:TPU:0, one launch (start us, length us, event | category | flops | bytes accessed | tf_op | source)
XLA Modules:
  0.0 83.0 jit_solution(16237254152585111211)
XLA Ops:
  0.7 0.9 %constant_dynamic-slice_fusion.3 = (bf16[8,8,256]{2,1,0:T(8,128)(2,1)S(1)}, bf16[8,8,256]{2,1,0:T(8,128)(2,1)S(1)}) fusion(bf16[8,32,256]{2,1,0:T(8,128)(2,1)} %param.14, s32[]{:T(128)S(6)} %select_n.30, s32[]{:T(128)S(6)} %select_n.31), kind=kLoop, calls=%fused_computation.10 | loop fusion | bytes 131080 | tf_op jit(solution)/shard_map/dynamic_slice | solution.py:604
  2.2 5.8 %collective-permute-start.1 = (bf16[8,8,256]{2,1,0:T(8,128)(2,1)S(1)}, bf16[8,8,256]{2,1,0:T(8,128)(2,1)S(1)}, u32[]{:S(2)}, u32[]{:S(2)}) collective-permute-start(bf16[8,8,256]{2,1,0:T(8,128)(2,1)S(1)} %get-tuple-element.25), channel_id=1, source_target_pairs={{0,1},{1,0},{2,3},{3,2},{4,5},{5,4},{6,7},{7,6},{8,9},{9,8},{10,11... | collective-permute-start | bytes 98312 | tf_op jit(solution)/shard_map/ppermute | solution.py:574
  8.0 1.9 %collective-permute-done.1 = bf16[8,8,256]{2,1,0:T(8,128)(2,1)S(1)} collective-permute-done((bf16[8,8,256]{2,1,0:T(8,128)(2,1)S(1)}, bf16[8,8,256]{2,1,0:T(8,128)(2,1)S(1)}, u32[]{:S(2)}, u32[]{:S(2)}) %collective-permute-start.1) | collective-permute-done | bytes 32800 | tf_op jit(solution)/shard_map/ppermute | solution.py:574
  9.9 0.9 %pad_maximum_fusion.own = bf16[8,48,256]{2,1,0:T(8,128)(2,1)S(1)} fusion(bf16[8,8,256]{2,1,0:T(8,128)(2,1)S(1)} %get-tuple-element.27, bf16[8,8,256]{2,1,0:T(8,128)(2,1)S(1)} %get-tuple-element.26, bf16[8,32,256]{2,1,0:T(8,128)(2,1)} %param.14), kind=kLoop, calls=%fused_computation | loop fusion | flops 589824 | bytes 393216 | tf_op jit(solution)/shard_map/concatenate | solution.py:614
  11.0 0.8 collective-permute-start.3
  11.9 1.9 %prepare.1 = (bf16[2,256,768]{2,1,0:T(8,128)(2,1)S(1)}, f32[2,32,768]{2,1,0:T(8,128)S(1)}, bf16[2,3,256,256]{3,2,1,0:T(8,128)(2,1)S(1)}, bf16[3,128,256]{2,1,0:T(8,128)(2,1)S(1)}) custom-call(bf16[2,256,768]{2,1,0:T(8,128)(2,1)S(1)} %copy-done.8, f32[5,5,2,768]{3,2,1,0:T(2,128)S(1)} %bitcast.5, bf16[2,24,32,32]{3,2,1,0:T(8,128)(2,1)S(1)} %copy-done.9, ...), custom_call_target="tpu_custom_call" | custom-call | flops 2000000000 | bytes 4000000 | tf_op jit(solution)/shard_map/prepare/pallas_call | solution.py:628
  14.5 12.9 %first.1 = (bf16[16,3,16,256]{3,2,1,0:T(8,128)(2,1)S(1)}, bf16[16,3,16,512]{3,2,1,0:T(8,128)(2,1)S(1)}, bf16[144,128]{1,0:T(8,128)(2,1)S(1)}) custom-call(bf16[8,48,256]{2,1,0:T(8,128)(2,1)S(1)} %pad_maximum_fusion.own, bf16[7,48,256]{2,1,0:T(8,128)(2,1)S(1)} %collective-permute-done.2.row_0, bf16[7,48,256]{2,1,0:T(8,128)(2,1)S(1)} %collective-permute-done.3.row_1, ...), custom_call_target="tpu_custom_call" | custom-call | tf_op jit(solution)/shard_map/first/pallas_call | solution.py:687
  27.4 4.4 %collective-permute-start.4 = (bf16[144,128]{1,0:T(8,128)(2,1)S(1)}, bf16[144,128]{1,0:T(8,128)(2,1)S(1)}, u32[]{:S(2)}, u32[]{:S(2)}) collective-permute-start(bf16[144,128]{1,0:T(8,128)(2,1)S(1)} %get-tuple-element.17), channel_id=1, source_target_pairs={{0,8},{8,0},{16,24},{24,16},{1,9},{9,1},{17,25},{25,17},{2,10},{10... | collective-permute-start | bytes 110600 | tf_op jit(solution)/shard_map/ppermute | solution.py:548
  31.8 1.2 %collective-permute-start.5 = (bf16[144,128]{1,0:T(8,128)(2,1)S(1)}, bf16[144,128]{1,0:T(8,128)(2,1)S(1)}, u32[]{:S(2)}, u32[]{:S(2)}) collective-permute-start(bf16[144,128]{1,0:T(8,128)(2,1)S(1)} %get-tuple-element.17), channel_id=1, source_target_pairs={{0,16},{8,24},{16,0},{24,8},{1,17},{9,25},{17,1},{25,9},{2,18},{10... | collective-permute-start | bytes 110600 | tf_op jit(solution)/shard_map/ppermute | solution.py:548
  33.2 2.5 %collective-permute-done.5 = bf16[144,128]{1,0:T(8,128)(2,1)S(1)} collective-permute-done((bf16[144,128]{1,0:T(8,128)(2,1)S(1)}, bf16[144,128]{1,0:T(8,128)(2,1)S(1)}, u32[]{:S(2)}, u32[]{:S(2)}) %collective-permute-start.5) | collective-permute-done | bytes 36896 | tf_op jit(solution)/shard_map/ppermute | solution.py:548
  36.5 2.1 %collective-permute-start.7 = (bf16[144,128]{1,0:T(8,128)(2,1)S(1)}, bf16[144,128]{1,0:T(8,128)(2,1)S(1)}, u32[]{:S(2)}, u32[]{:S(2)}) collective-permute-start(bf16[144,128]{1,0:T(8,128)(2,1)S(1)} %add_convert_fusion.3), channel_id=1, source_target_pairs={{0,1},{1,0},{2,3},{3,2},{4,5},{5,4},{6,7},{7,6},{8,9},{9,8},{10,11... | collective-permute-start | bytes 110600 | tf_op jit(solution)/shard_map/ppermute | solution.py:548
  38.6 1.6 %collective-permute-start.8 = (bf16[144,128]{1,0:T(8,128)(2,1)S(1)}, bf16[144,128]{1,0:T(8,128)(2,1)S(1)}, u32[]{:S(2)}, u32[]{:S(2)}) collective-permute-start(bf16[144,128]{1,0:T(8,128)(2,1)S(1)} %add_convert_fusion.3), channel_id=1, source_target_pairs={{0,2},{1,3},{2,0},{3,1},{4,6},{5,7},{6,4},{7,5},{8,10},{9,11},{10,... | collective-permute-start | bytes 110600 | tf_op jit(solution)/shard_map/ppermute | solution.py:548
  40.5 2.4 %collective-permute-done.8 = bf16[144,128]{1,0:T(8,128)(2,1)S(1)} collective-permute-done((bf16[144,128]{1,0:T(8,128)(2,1)S(1)}, bf16[144,128]{1,0:T(8,128)(2,1)S(1)}, u32[]{:S(2)}, u32[]{:S(2)}) %collective-permute-start.8) | collective-permute-done | bytes 36896 | tf_op jit(solution)/shard_map/ppermute | solution.py:548
  42.9 2.1 %collective-permute-done.9 = bf16[144,128]{1,0:T(8,128)(2,1)S(1)} collective-permute-done((bf16[144,128]{1,0:T(8,128)(2,1)S(1)}, bf16[144,128]{1,0:T(8,128)(2,1)S(1)}, u32[]{:S(2)}, u32[]{:S(2)}) %collective-permute-start.9) | collective-permute-done | bytes 36896 | tf_op jit(solution)/shard_map/ppermute | solution.py:548
  45.0 1.1 %collective-permute-start.10 = (bf16[144,128]{1,0:T(8,128)(2,1)S(1)}, bf16[144,128]{1,0:T(8,128)(2,1)S(1)}, u32[]{:S(2)}, u32[]{:S(2)}) collective-permute-start(bf16[144,128]{1,0:T(8,128)(2,1)S(1)} %add_convert_fusion.2.payload), channel_id=1, source_target_pairs={{0,4},{1,5},{2,6},{3,7},{4,0},{5,1},{6,2},{7,3},{8,12},{9,13},{10,... | collective-permute-start | bytes 110600 | tf_op jit(solution)/shard_map/ppermute | solution.py:548
  46.1 4.1 %collective-permute-done.10.other = bf16[144,128]{1,0:T(8,128)(2,1)S(1)} collective-permute-done((bf16[144,128]{1,0:T(8,128)(2,1)S(1)}, bf16[144,128]{1,0:T(8,128)(2,1)S(1)}, u32[]{:S(2)}, u32[]{:S(2)}) %collective-permute-start.10) | collective-permute-done | bytes 36896 | tf_op jit(solution)/shard_map/ppermute | solution.py:548
  50.2 13.6 %second.1 = (bf16[10,3,16,256]{3,2,1,0:T(8,128)(2,1)S(1)}, bf16[10,3,16,512]{3,2,1,0:T(8,128)(2,1)S(1)}, bf16[144,128]{1,0:T(8,128)(2,1)S(1)}) custom-call(bf16[16,3,16,256]{3,2,1,0:T(8,128)(2,1)S(1)} %get-tuple-element.15.mixed, bf16[16,3,16,512]{3,2,1,0:T(8,128)(2,1)S(1)} %get-tuple-element.16.query, bf16[144,128]{1,0:T(8,128)(2,1)S(1)} %add_convert_fusion.2.payload, ...), custom_call_target="tpu_custom_call" | custom-call | tf_op jit(solution)/shard_map/second/pallas_call | solution.py:701
  63.9 1.2 %collective-permute-start.12 = (bf16[144,128]{1,0:T(8,128)(2,1)S(1)}, bf16[144,128]{1,0:T(8,128)(2,1)S(1)}, u32[]{:S(2)}, u32[]{:S(2)}) collective-permute-start(bf16[144,128]{1,0:T(8,128)(2,1)S(1)} %get-tuple-element.20), channel_id=1, source_target_pairs={{0,16},{8,24},{16,0},{24,8},{1,17},{9,25},{17,1},{25,9},{2,18},{10... | collective-permute-start | bytes 110600 | tf_op jit(solution)/shard_map/ppermute | solution.py:548
  65.8 2.2 %collective-permute-done.12 = bf16[144,128]{1,0:T(8,128)(2,1)S(1)} collective-permute-done((bf16[144,128]{1,0:T(8,128)(2,1)S(1)}, bf16[144,128]{1,0:T(8,128)(2,1)S(1)}, u32[]{:S(2)}, u32[]{:S(2)}) %collective-permute-start.12) | collective-permute-done | bytes 36896 | tf_op jit(solution)/shard_map/ppermute | solution.py:548
  69.4 2.8 %collective-permute-start.16 = (bf16[144,128]{1,0:T(8,128)(2,1)S(1)}, bf16[144,128]{1,0:T(8,128)(2,1)S(1)}, u32[]{:S(2)}, u32[]{:S(2)}) collective-permute-start(bf16[144,128]{1,0:T(8,128)(2,1)S(1)} %add_convert_fusion.1), channel_id=1, source_target_pairs={{0,3},{1,2},{2,1},{3,0},{4,7},{5,6},{6,5},{7,4},{8,11},{9,10},{10,... | collective-permute-start | bytes 110600 | tf_op jit(solution)/shard_map/ppermute | solution.py:548
  73.4 1.1 %collective-permute-done.16 = bf16[144,128]{1,0:T(8,128)(2,1)S(1)} collective-permute-done((bf16[144,128]{1,0:T(8,128)(2,1)S(1)}, bf16[144,128]{1,0:T(8,128)(2,1)S(1)}, u32[]{:S(2)}, u32[]{:S(2)}) %collective-permute-start.16) | collective-permute-done | bytes 36896 | tf_op jit(solution)/shard_map/ppermute | solution.py:548
  74.5 2.3 %collective-permute-start.17 = (bf16[144,128]{1,0:T(8,128)(2,1)S(1)}, bf16[144,128]{1,0:T(8,128)(2,1)S(1)}, u32[]{:S(2)}, u32[]{:S(2)}) collective-permute-start(bf16[144,128]{1,0:T(8,128)(2,1)S(1)} %add_convert_fusion.payload), channel_id=1, source_target_pairs={{0,4},{1,5},{2,6},{3,7},{4,0},{5,1},{6,2},{7,3},{8,12},{9,13},{10,... | collective-permute-start | bytes 110600 | tf_op jit(solution)/shard_map/ppermute | solution.py:548
  76.9 2.6 %collective-permute-done.17.other = bf16[144,128]{1,0:T(8,128)(2,1)S(1)} collective-permute-done((bf16[144,128]{1,0:T(8,128)(2,1)S(1)}, bf16[144,128]{1,0:T(8,128)(2,1)S(1)}, u32[]{:S(2)}, u32[]{:S(2)}) %collective-permute-start.17) | collective-permute-done | bytes 36896 | tf_op jit(solution)/shard_map/ppermute | solution.py:548
  79.4 3.4 %last.1 = (bf16[8,32,256]{2,1,0:T(8,128)(2,1)}, f32[4,8,32]{2,1,0:T(8,128)}) custom-call(bf16[10,3,16,256]{3,2,1,0:T(8,128)(2,1)S(1)} %get-tuple-element.18.mixed, bf16[10,3,16,512]{3,2,1,0:T(8,128)(2,1)S(1)} %get-tuple-element.19.query, bf16[144,128]{1,0:T(8,128)(2,1)S(1)} %add_convert_fusion.payload, bf16[144,128]{1,0:T(8,128)(2,1)S(1)} %collective-permute-done.17.other, ...), custom_call_target="tpu_custom_call" | custom-call | tf_op jit(solution)/shard_map/last/pallas_call | solution.py:715
  (51 shorter events, 6.3 us)
Async XLA Ops:
  0.6 11.1 %copy-start.8 = (bf16[2,256,768]{2,1,0:T(8,128)(2,1)S(1)}, bf16[2,256,768]{2,1,0:T(8,128)(2,1)}, u32[]{:S(2)}) copy-start(bf16[2,256,768]{2,1,0:T(8,128)(2,1)} %qkv.1) | copy-start | bytes 2359300
  1.5 6.5 %collective-permute-start = (bf16[8,8,256]{2,1,0:T(8,128)(2,1)S(1)}, bf16[8,8,256]{2,1,0:T(8,128)(2,1)S(1)}, u32[]{:S(2)}, u32[]{:S(2)}) collective-permute-start(bf16[8,8,256]{2,1,0:T(8,128)(2,1)S(1)} %get-tuple-element.24), channel_id=1, source_target_pairs={{1,2},{2,1},{3,4},{4,3},{5,6},{6,5},{9,10},{10,9},{11,12},{12,11},... | collective-permute-start | bytes 98312 | tf_op jit(solution)/shard_map/ppermute | solution.py:574
  2.2 7.7 %collective-permute-start.1 = (bf16[8,8,256]{2,1,0:T(8,128)(2,1)S(1)}, bf16[8,8,256]{2,1,0:T(8,128)(2,1)S(1)}, u32[]{:S(2)}, u32[]{:S(2)}) collective-permute-start(bf16[8,8,256]{2,1,0:T(8,128)(2,1)S(1)} %get-tuple-element.25), channel_id=1, source_target_pairs={{0,1},{1,0},{2,3},{3,2},{4,5},{5,4},{6,7},{7,6},{8,9},{9,8},{10,11... | collective-permute-start | bytes 98312 | tf_op jit(solution)/shard_map/ppermute | solution.py:574
  10.9 2.9 %collective-permute-start.2 = (bf16[7,48,256]{2,1,0:T(8,128)(2,1)S(1)}, bf16[7,48,256]{2,1,0:T(8,128)(2,1)S(1)}, u32[]{:S(2)}, u32[]{:S(2)}) collective-permute-start(bf16[7,48,256]{2,1,0:T(8,128)(2,1)S(1)} %get-tuple-element.23), channel_id=1, source_target_pairs={{0,8},{8,0},{16,24},{24,16},{1,9},{9,1},{17,25},{25,17},{2,10},{10... | collective-permute-start | bytes 516104 | tf_op jit(solution)/shard_map/ppermute | solution.py:574
  11.0 2.8 %collective-permute-start.3 = (bf16[7,48,256]{2,1,0:T(8,128)(2,1)S(1)}, bf16[7,48,256]{2,1,0:T(8,128)(2,1)S(1)}, u32[]{:S(2)}, u32[]{:S(2)}) collective-permute-start(bf16[7,48,256]{2,1,0:T(8,128)(2,1)S(1)} %get-tuple-element.22), channel_id=1, source_target_pairs={{8,16},{16,8},{9,17},{17,9},{10,18},{18,10},{11,19},{19,11},{12,20... | collective-permute-start | bytes 516104 | tf_op jit(solution)/shard_map/ppermute | solution.py:574
  11.8 2.0 %copy-start.4 = (f32[2,1024]{1,0:T(2,128)S(1)}, f32[2,1024]{1,0:T(2,128)}, u32[]{:S(2)}) copy-start(f32[2,1024]{1,0:T(2,128)} %refs_1_.3) | copy-start | bytes 24580
  11.9 2.0 %copy-start.5 = (f32[2,1024]{1,0:T(2,128)S(1)}, f32[2,1024]{1,0:T(2,128)}, u32[]{:S(2)}) copy-start(f32[2,1024]{1,0:T(2,128)} %refs_3_.3) | copy-start | bytes 24580
  14.5 35.8 %copy-start.2 = (bf16[2,512,256]{2,1,0:T(8,128)(2,1)S(1)}, bf16[2,512,256]{2,1,0:T(8,128)(2,1)}, u32[]{:S(2)}) copy-start(bf16[2,512,256]{2,1,0:T(8,128)(2,1)} %out_weight.3) | copy-start | bytes 1572868
  27.4 5.8 %collective-permute-start.4 = (bf16[144,128]{1,0:T(8,128)(2,1)S(1)}, bf16[144,128]{1,0:T(8,128)(2,1)S(1)}, u32[]{:S(2)}, u32[]{:S(2)}) collective-permute-start(bf16[144,128]{1,0:T(8,128)(2,1)S(1)} %get-tuple-element.17), channel_id=1, source_target_pairs={{0,8},{8,0},{16,24},{24,16},{1,9},{9,1},{17,25},{25,17},{2,10},{10... | collective-permute-start | bytes 110600 | tf_op jit(solution)/shard_map/ppermute | solution.py:548
  31.8 4.0 %collective-permute-start.5 = (bf16[144,128]{1,0:T(8,128)(2,1)S(1)}, bf16[144,128]{1,0:T(8,128)(2,1)S(1)}, u32[]{:S(2)}, u32[]{:S(2)}) collective-permute-start(bf16[144,128]{1,0:T(8,128)(2,1)S(1)} %get-tuple-element.17), channel_id=1, source_target_pairs={{0,16},{8,24},{16,0},{24,8},{1,17},{9,25},{17,1},{25,9},{2,18},{10... | collective-permute-start | bytes 110600 | tf_op jit(solution)/shard_map/ppermute | solution.py:548
  33.0 3.4 %collective-permute-start.6 = (bf16[144,128]{1,0:T(8,128)(2,1)S(1)}, bf16[144,128]{1,0:T(8,128)(2,1)S(1)}, u32[]{:S(2)}, u32[]{:S(2)}) collective-permute-start(bf16[144,128]{1,0:T(8,128)(2,1)S(1)} %get-tuple-element.17), channel_id=1, source_target_pairs={{0,24},{8,16},{16,8},{24,0},{1,25},{9,17},{17,9},{25,1},{2,26},{10... | collective-permute-start | bytes 110600 | tf_op jit(solution)/shard_map/ppermute | solution.py:548
  36.5 4.0 %collective-permute-start.7 = (bf16[144,128]{1,0:T(8,128)(2,1)S(1)}, bf16[144,128]{1,0:T(8,128)(2,1)S(1)}, u32[]{:S(2)}, u32[]{:S(2)}) collective-permute-start(bf16[144,128]{1,0:T(8,128)(2,1)S(1)} %add_convert_fusion.3), channel_id=1, source_target_pairs={{0,1},{1,0},{2,3},{3,2},{4,5},{5,4},{6,7},{7,6},{8,9},{9,8},{10,11... | collective-permute-start | bytes 110600 | tf_op jit(solution)/shard_map/ppermute | solution.py:548
  38.6 4.3 %collective-permute-start.8 = (bf16[144,128]{1,0:T(8,128)(2,1)S(1)}, bf16[144,128]{1,0:T(8,128)(2,1)S(1)}, u32[]{:S(2)}, u32[]{:S(2)}) collective-permute-start(bf16[144,128]{1,0:T(8,128)(2,1)S(1)} %add_convert_fusion.3), channel_id=1, source_target_pairs={{0,2},{1,3},{2,0},{3,1},{4,6},{5,7},{6,4},{7,5},{8,10},{9,11},{10,... | collective-permute-start | bytes 110600 | tf_op jit(solution)/shard_map/ppermute | solution.py:548
  40.1 4.9 %collective-permute-start.9 = (bf16[144,128]{1,0:T(8,128)(2,1)S(1)}, bf16[144,128]{1,0:T(8,128)(2,1)S(1)}, u32[]{:S(2)}, u32[]{:S(2)}) collective-permute-start(bf16[144,128]{1,0:T(8,128)(2,1)S(1)} %add_convert_fusion.3), channel_id=1, source_target_pairs={{0,3},{1,2},{2,1},{3,0},{4,7},{5,6},{6,5},{7,4},{8,11},{9,10},{10,... | collective-permute-start | bytes 110600 | tf_op jit(solution)/shard_map/ppermute | solution.py:548
  45.0 5.2 %copy-start.7 = (f32[2,256]{1,0:T(2,128)S(1)}, f32[2,256]{1,0:T(2,128)}, u32[]{:S(2)}) copy-start(f32[2,256]{1,0:T(2,128)} %out_bias.3) | copy-start | bytes 6148
  45.0 5.2 %collective-permute-start.10 = (bf16[144,128]{1,0:T(8,128)(2,1)S(1)}, bf16[144,128]{1,0:T(8,128)(2,1)S(1)}, u32[]{:S(2)}, u32[]{:S(2)}) collective-permute-start(bf16[144,128]{1,0:T(8,128)(2,1)S(1)} %add_convert_fusion.2.payload), channel_id=1, source_target_pairs={{0,4},{1,5},{2,6},{3,7},{4,0},{5,1},{6,2},{7,3},{8,12},{9,13},{10,... | collective-permute-start | bytes 110600 | tf_op jit(solution)/shard_map/ppermute | solution.py:548
  63.8 1.9 %collective-permute-start.11 = (bf16[144,128]{1,0:T(8,128)(2,1)S(1)}, bf16[144,128]{1,0:T(8,128)(2,1)S(1)}, u32[]{:S(2)}, u32[]{:S(2)}) collective-permute-start(bf16[144,128]{1,0:T(8,128)(2,1)S(1)} %get-tuple-element.20), channel_id=1, source_target_pairs={{0,8},{8,0},{16,24},{24,16},{1,9},{9,1},{17,25},{25,17},{2,10},{10... | collective-permute-start | bytes 110600 | tf_op jit(solution)/shard_map/ppermute | solution.py:548
  63.9 4.0 %collective-permute-start.12 = (bf16[144,128]{1,0:T(8,128)(2,1)S(1)}, bf16[144,128]{1,0:T(8,128)(2,1)S(1)}, u32[]{:S(2)}, u32[]{:S(2)}) collective-permute-start(bf16[144,128]{1,0:T(8,128)(2,1)S(1)} %get-tuple-element.20), channel_id=1, source_target_pairs={{0,16},{8,24},{16,0},{24,8},{1,17},{9,25},{17,1},{25,9},{2,18},{10... | collective-permute-start | bytes 110600 | tf_op jit(solution)/shard_map/ppermute | solution.py:548
  65.1 3.4 %collective-permute-start.13 = (bf16[144,128]{1,0:T(8,128)(2,1)S(1)}, bf16[144,128]{1,0:T(8,128)(2,1)S(1)}, u32[]{:S(2)}, u32[]{:S(2)}) collective-permute-start(bf16[144,128]{1,0:T(8,128)(2,1)S(1)} %get-tuple-element.20), channel_id=1, source_target_pairs={{0,24},{8,16},{16,8},{24,0},{1,25},{9,17},{17,9},{25,1},{2,26},{10... | collective-permute-start | bytes 110600 | tf_op jit(solution)/shard_map/ppermute | solution.py:548
  68.6 4.0 %collective-permute-start.14 = (bf16[144,128]{1,0:T(8,128)(2,1)S(1)}, bf16[144,128]{1,0:T(8,128)(2,1)S(1)}, u32[]{:S(2)}, u32[]{:S(2)}) collective-permute-start(bf16[144,128]{1,0:T(8,128)(2,1)S(1)} %add_convert_fusion.1), channel_id=1, source_target_pairs={{0,1},{1,0},{2,3},{3,2},{4,5},{5,4},{6,7},{7,6},{8,9},{9,8},{10,11... | collective-permute-start | bytes 110600 | tf_op jit(solution)/shard_map/ppermute | solution.py:548
  69.1 4.2 %collective-permute-start.15 = (bf16[144,128]{1,0:T(8,128)(2,1)S(1)}, bf16[144,128]{1,0:T(8,128)(2,1)S(1)}, u32[]{:S(2)}, u32[]{:S(2)}) collective-permute-start(bf16[144,128]{1,0:T(8,128)(2,1)S(1)} %add_convert_fusion.1), channel_id=1, source_target_pairs={{0,2},{1,3},{2,0},{3,1},{4,6},{5,7},{6,4},{7,5},{8,10},{9,11},{10,... | collective-permute-start | bytes 110600 | tf_op jit(solution)/shard_map/ppermute | solution.py:548
  69.4 5.1 %collective-permute-start.16 = (bf16[144,128]{1,0:T(8,128)(2,1)S(1)}, bf16[144,128]{1,0:T(8,128)(2,1)S(1)}, u32[]{:S(2)}, u32[]{:S(2)}) collective-permute-start(bf16[144,128]{1,0:T(8,128)(2,1)S(1)} %add_convert_fusion.1), channel_id=1, source_target_pairs={{0,3},{1,2},{2,1},{3,0},{4,7},{5,6},{6,5},{7,4},{8,11},{9,10},{10,... | collective-permute-start | bytes 110600 | tf_op jit(solution)/shard_map/ppermute | solution.py:548
  74.5 2.3 %copy-start.12 = (f32[4]{0:T(128)S(1)}, f32[4]{0:T(128)}, u32[]{:S(2)}) copy-start(f32[4]{0:T(128)} %param.27) | copy-start | bytes 52
  74.5 4.9 %collective-permute-start.17 = (bf16[144,128]{1,0:T(8,128)(2,1)S(1)}, bf16[144,128]{1,0:T(8,128)(2,1)S(1)}, u32[]{:S(2)}, u32[]{:S(2)}) collective-permute-start(bf16[144,128]{1,0:T(8,128)(2,1)S(1)} %add_convert_fusion.payload), channel_id=1, source_target_pairs={{0,4},{1,5},{2,6},{3,7},{4,0},{5,1},{6,2},{7,3},{8,12},{9,13},{10,... | collective-permute-start | bytes 110600 | tf_op jit(solution)/shard_map/ppermute | solution.py:548
  (7 other events, 9.7 us)

commit v10 on v8

--- a/solution.py
+++ b/solution.py
@@ -87,17 +87,43 @@
     return total
 
 
+def spread_taps(agg, wide_agg):
+    for index in range(25):
+        taps = agg[index : index + 1, :]
+        wide_agg[index] = jnp.broadcast_to(taps, (TILE, taps.shape[1])).astype(BF16)
+
+
+def aggregated(source, wide_agg, group, low, first, size, channels):
+    width = source.shape[1]
+    scaled = []
+    for r in range(size):
+        lanes = []
+        for lane in range(low, low + channels, LANES):
+            here = slice(lane, lane + LANES)
+            value = depthwise_row(
+                [source[first + r + a, :, here] for a in range(5)],
+                lambda a, b: wide_agg[5 * a + b, :, here], 5, width,
+            )
+            lanes.append(value.astype(BF16))
+        scaled.append(jnp.concatenate(lanes, axis=1))
+    value = jnp.dot(jnp.concatenate(scaled, axis=0), group, preferred_element_type=F32)
+    return value.astype(BF16).reshape(size, width, channels)
+
+
 def front(x_ref, weights, outs, scratch, halo, tile, head_dim, section):
-    expand, expand_bias, depth, depth_bias, project, project_bias = weights[:6]
-    mixed_out, query_out, payload_out = outs
+    expand, expand_bias, depth, depth_bias, project = weights[:5]
+    mixed_out, payload_out = outs
     (
-        hidden_0, hidden_1, total, mixed, qkv, query, wide_depth, wide_agg,
-        qkv_weight, agg, group, sems,
+        hidden_0, hidden_1, total, mixed, pairs, wide_depth, wide_agg,
+        project_bias, pair_weight, agg, group, sems,
     ) = scratch
+    channels = x_ref.shape[2]
+    tail = pl.ds(channels, 2 * channels)
     loads = [
-        pltpu.make_async_copy(weights[6].at[section], qkv_weight, sems.at[0]),
-        pltpu.make_async_copy(weights[7].at[section], agg, sems.at[1]),
-        pltpu.make_async_copy(weights[8].at[section], group, sems.at[2]),
+        pltpu.make_async_copy(weights[5], project_bias, sems.at[0]),
+        pltpu.make_async_copy(weights[6].at[section, :, tail], pair_weight, sems.at[1]),
+        pltpu.make_async_copy(weights[7].at[section, :, tail], agg, sems.at[2]),
+        pltpu.make_async_copy(weights[8].at[section, pl.ds(1, 2)], group, sems.at[3]),
     ]
     for load in loads:
         load.start()
@@ -109,7 +135,7 @@
     for index in range(9):
         taps = depth[index // 3, index % 3, section : section + 1, :] * (1.0 / 6.0)
         wide_depth[index] = jnp.broadcast_to(taps, (TILE, taps.shape[1])).astype(BF16)
-    total[...] = 6.0 * (flat(x_ref[1 : rows - 1]).astype(F32) + project_bias[section : section + 1, :])
+    total[...] = 6.0 * flat(x_ref[1 : rows - 1]).astype(F32)
 
     def expand_rows(out, at, first, size):
         value = jnp.dot(
@@ -156,56 +182,25 @@
         return carry
 
     lax.fori_loop(0, chunks // 2, two_stages, 0)
-    mixed[...] = (total[...] * (1.0 / 6.0)).astype(BF16).reshape(inner, width, channels)
-    outer = inner - 4
-    stores = [
-        pltpu.make_async_copy(mixed.at[pl.ds(2, outer)], mixed_out, sems.at[3]),
-        pltpu.make_async_copy(query, query_out, sems.at[4]),
-    ]
-    stores[0].start()
-    for load in loads:
+    loads[0].wait()
+    value = total[...] * (1.0 / 6.0) + project_bias[section : section + 1, :]
+    mixed[...] = value.astype(BF16).reshape(inner, width, channels)
+    store = pltpu.make_async_copy(mixed, mixed_out, sems.at[4])
+    store.start()
+    for load in loads[1:]:
         load.wait()
-    for index in range(25):
-        taps = agg[index : index + 1, :]
-        wide_agg[index] = jnp.broadcast_to(taps, (TILE, taps.shape[1])).astype(BF16)
-    for first, size in parted(inner, PARTS):
+    spread_taps(agg, wide_agg)
+    around = halo - 1
+    first_pair = around - 2
+    count = tile_rows + 4
+    for first, size in parted(count, PARTS - 1):
+        at = first_pair + first
         value = jnp.dot(
-            flat(mixed[first : first + size]), qkv_weight[...], preferred_element_type=F32
-        )
-        qkv[first : first + size] = value.astype(BF16).reshape(size, width, 3 * channels)
-    around = halo - 1
-    clear_outside(qkv, around, tile_cols)
-
-    def aggregated(kind, first, size):
-        scaled = []
-        for r in range(size):
-            lanes = []
-            for lane in range(kind * channels, (kind + 1) * channels, LANES):
-                here = slice(lane, lane + LANES)
-                value = depthwise_row(
-                    [qkv[first + r + a, :, here] for a in range(5)],
-                    lambda a, b: wide_agg[5 * a + b, :, here], 5, width,
-                )
-                lanes.append(value.astype(BF16))
-            scaled.append(jnp.concatenate(lanes, axis=1))
-        value = jnp.dot(
-            jnp.concatenate(scaled, axis=0), group[kind], preferred_element_type=F32
-        )
-        return value.astype(BF16).reshape(size, width, channels)
-
-    query[:, :, 0:channels] = jnp.maximum(qkv[2 : inner - 2, :, 0:channels], 0.0)
-    size = next(n for n in range(5, 0, -1) if outer % n == 0)
-
-    def query_rows(index, carry):
-        at = index * size
-        query[pl.ds(at, size), :, channels : 2 * channels] = jnp.maximum(
-            aggregated(0, at, size), 0.0
-        )
-        return carry
-
-    lax.fori_loop(0, outer // size, query_rows, 0)
-    stores[1].start()
-    size = next(n for n in range(4, 0, -1) if tile_rows % n == 0)
+            flat(mixed[at : at + size]), pair_weight[...], preferred_element_type=F32
+        )
+        pairs[first : first + size] = value.astype(BF16).reshape(size, width, 2 * channels)
+    clear_outside(pairs, 2, tile_cols)
+    size = group_size(tile_rows, 4)
 
     def summed(key, value):
         key = jnp.maximum(flat(key[:, 0:tile_cols]), 0.0)
@@ -219,14 +214,17 @@
         ]
         return products, jnp.sum(key.astype(F32), axis=0, keepdims=True)
 
-    mine = slice(around, around + tile_rows)
+    mine = slice(2, 2 + tile_rows)
     products, sums = summed(
-        qkv[mine, :, channels : 2 * channels], qkv[mine, :, 2 * channels : 3 * channels]
+        pairs[mine, :, 0:channels], pairs[mine, :, channels : 2 * channels]
     )
 
     def grouped_rows(index, carry):
-        at = around - 2 + index * size
-        more, sums = summed(aggregated(1, at, size), aggregated(2, at, size))
+        at = index * size
+        more, sums = summed(
+            aggregated(pairs, wide_agg, group[0], 0, at, size, channels),
+            aggregated(pairs, wide_agg, group[1], channels, at, size, channels),
+        )
         return [a + b for a, b in zip(carry[0], more)], carry[1] + sums
 
     more, more_sums = lax.fori_loop(
@@ -247,15 +245,52 @@
     key_sums.append(jnp.zeros((KEY_ROWS - len(products), LANES), F32))
     payload_out[0:LANES, :] = summary.astype(BF16)
     payload_out[LANES : LANES + KEY_ROWS, :] = jnp.concatenate(key_sums, axis=0).astype(BF16)
-    for store in stores:
-        store.wait()
+    store.wait()
+
+
+def query_kernel(
+    tile, section, mixed_in, qkv_weight, taps, groups, query_out,
+    mixed, centre, query, weight, agg, group, wide_agg, sems,
+):
+    rows, width, channels = mixed.shape
+    head = pl.ds(0, channels)
+    loads = [
+        pltpu.make_async_copy(mixed_in, mixed, sems.at[0]),
+        pltpu.make_async_copy(qkv_weight.at[section, :, head], weight, sems.at[1]),
+        pltpu.make_async_copy(taps.at[section, :, head], agg, sems.at[2]),
+        pltpu.make_async_copy(groups.at[section, 0], group, sems.at[3]),
+    ]
+    for load in loads:
+        load.start()
+    for load in loads:
+        load.wait()
+    spread_taps(agg, wide_agg)
+    for first, size in parted(rows, PARTS):
+        value = jnp.dot(
+            flat(mixed[first : first + size]), weight[...], preferred_element_type=F32
+        )
+        centre[first : first + size] = value.astype(BF16).reshape(size, width, channels)
+    clear_outside(centre, (rows - tile[0]) // 2, tile[1])
+
+    def query_rows(first, size):
+        here = pl.ds(first, size)
+        query[here, :, 0:channels] = jnp.maximum(centre[pl.ds(first + 2, size)], 0.0)
+        grouped = aggregated(centre, wide_agg, group[...], 0, first, size, channels)
+        query[here, :, channels : 2 * channels] = jnp.maximum(grouped, 0.0)
+
+    by_groups(rows - 4, 5, query_rows)
+    store = pltpu.make_async_copy(query, query_out, sems.at[4])
+    store.start()
+    store.wait()
 
 
 def attend(
-    mixed_in, query_in, payloads, weight, bias, mixed_ref, query_ref, sems, head_dim, section, x_ref
+    mixed_in, query_in, payloads, weight, bias_in, held, head_dim, section, x_ref
 ):
     rows, width, channels = x_ref.shape
-    halves = [(query_in, query_ref), (mixed_in, mixed_ref)]
+    mixed_ref, query_ref, bias, sems = held
+    inner = mixed_in.at[pl.ds(2, rows)]
+    halves = [(query_in, query_ref), (inner, mixed_ref), (bias_in, bias)]
     loads = [pltpu.make_async_copy(a, b, sems.at[k]) for k, (a, b) in enumerate(halves)]
     for load in loads:
         load.start()
@@ -374,7 +409,7 @@
 
 
 def first_kernel(tile, head_dim, own, row_0, row_1, *refs):
-    weights, outs, scratch = refs[:9], refs[9:12], refs[12:]
+    weights, outs, scratch = refs[:9], refs[9:11], refs[11:]
     x_ref = scratch[0]
     rows, cols = tile
     below = REACH + rows
@@ -386,24 +421,22 @@
 
 
 def second_kernel(tile, head_dim, mixed, query, payload, other, out_weight, out_bias, *refs):
-    weights, outs, scratch = refs[:9], refs[9:12], refs[12:]
-    x_ref, mixed_ref, query_ref, sems = scratch[:4]
+    weights, outs, scratch = refs[:9], refs[9:11], refs[11:]
+    x_ref = scratch[0]
     attend(
-        mixed, query, (payload, other), out_weight, out_bias, mixed_ref, query_ref, sems, head_dim,
-        0, x_ref,
+        mixed, query, (payload, other), out_weight, out_bias, scratch[1:5], head_dim, 0, x_ref
     )
-    front(x_ref, weights, outs, scratch[4:], REACH - 3, tile, head_dim, 1)
+    front(x_ref, weights, outs, scratch[5:], REACH - 3, tile, head_dim, 1)
 
 
 def last_kernel(
     tile, head_dim, mixed, query, payload, other, out_weight, out_bias, head_weight, head_bias,
-    map_out, boxes_out, x_ref, mixed_ref, query_ref, sems,
+    map_out, boxes_out, x_ref, *held,
 ):
     rows, cols = tile
     width = cols + 2 * SIDE
     attend(
-        mixed, query, (payload, other), out_weight, out_bias, mixed_ref, query_ref, sems, head_dim,
-        1, x_ref,
+        mixed, query, (payload, other), out_weight, out_bias, held, head_dim, 1, x_ref
     )
     clear_outside(x_ref, 1, cols)
     map_out[...] = x_ref[1 : 1 + rows, 0:cols, :]
@@ -533,8 +566,8 @@
     low, high = edges(features, 1, SIDE, odd_col)
     col_1 = pair_exchange(high, "col", 1)
     col_0 = pair_exchange(low, "col", 0)
-    right = jnp.where(odd_col == 0, col_0, col_1)
-    left = jnp.where(odd_col == 0, col_1, col_0)
+    right = jnp.where(odd_col == 1, col_1, col_0)
+    left = jnp.where(odd_col == 1, col_0, col_1)
     wide_rows = jnp.concatenate([features, right, left], axis=1)
     low, high = edges(wide_rows, 0, REACH, odd_row)
     row_1 = pair_exchange(high, "row", 1)
@@ -568,12 +601,11 @@
         expand_weight, expand_bias, depth_weight, depth_bias, project_weight, project_bias,
         qkv_weight, taps, group,
     ]
-    weight_specs = [near()] * 6 + [far()] * 3
+    weight_specs = [near()] * 5 + [far()] * 4
 
     def outs_of(count):
         return [
             jax.ShapeDtypeStruct((count, width, channels), BF16),
-            jax.ShapeDtypeStruct((count, width, 2 * channels), BF16),
             jax.ShapeDtypeStruct((LANES + KEY_ROWS, LANES), BF16),
         ]
 
@@ -583,13 +615,13 @@
             pltpu.VMEM((count, width, 256), BF16),
             pltpu.VMEM(((count - 2) * width, channels), F32),
             pltpu.VMEM((count - 2, width, channels), BF16),
-            pltpu.VMEM((count - 2, width, 3 * channels), BF16),
-            pltpu.VMEM((count - 6, width, 2 * channels), BF16),
+            pltpu.VMEM((rows + 4, width, 2 * channels), BF16),
             pltpu.VMEM((9, TILE, expand_weight.shape[2]), BF16),
-            pltpu.VMEM((25, TILE, 3 * channels), BF16),
-            pltpu.VMEM(qkv_weight.shape[1:], BF16),
-            pltpu.VMEM(taps.shape[1:], F32),
-            pltpu.VMEM(group.shape[1:], BF16),
+            pltpu.VMEM((25, TILE, 2 * channels), BF16),
+            pltpu.VMEM(project_bias.shape, F32),
+            pltpu.VMEM((channels, 2 * channels), BF16),
+            pltpu.VMEM((32, 2 * channels), F32),
+            pltpu.VMEM((2, channels, channels), BF16),
             pltpu.SemaphoreType.DMA((5,)),
         ]
 
@@ -598,34 +630,63 @@
             pltpu.VMEM((count, width, channels), BF16),
             pltpu.VMEM((count, width, channels), BF16),
             pltpu.VMEM((count, width, 2 * channels), BF16),
-            pltpu.SemaphoreType.DMA((2,)),
+            pltpu.VMEM(output_bias.shape, F32),
+            pltpu.SemaphoreType.DMA((3,)),
         ]
 
+    def queries(mixed, section):
+        count = mixed.shape[0]
+        units = (count - 4) * width * channels
+        return pl.pallas_call(
+            functools.partial(query_kernel, tile, section),
+            out_shape=jax.ShapeDtypeStruct((count - 4, width, 2 * channels), BF16),
+            grid=(1,),
+            in_specs=[far()] * 4,
+            out_specs=far(),
+            scratch_shapes=[
+                pltpu.VMEM((count, width, channels), BF16),
+                pltpu.VMEM((count, width, channels), BF16),
+                pltpu.VMEM((count - 4, width, 2 * channels), BF16),
+                pltpu.VMEM((channels, channels), BF16),
+                pltpu.VMEM((32, channels), F32),
+                pltpu.VMEM((channels, channels), BF16),
+                pltpu.VMEM((25, TILE, channels), BF16),
+                pltpu.SemaphoreType.DMA((5,)),
+            ],
+            compiler_params=params,
+            cost_estimate=pl.CostEstimate(
+                flops=8 * units * channels, bytes_accessed=8 * units, transcendentals=0
+            ),
+            name="queries",
+        )(mixed, qkv_weight, taps, group)
+
     first_rows = rows + 2 * REACH
-    mixed, query, payload = pl.pallas_call(
+    mixed, payload = pl.pallas_call(
         functools.partial(first_kernel, tile, head_dim),
-        out_shape=outs_of(first_rows - 6),
+        out_shape=outs_of(first_rows - 2),
         grid=(1,),
         in_specs=[near()] * 3 + weight_specs,
-        out_specs=[far(), far(), near()],
+        out_specs=[far(), near()],
         scratch_shapes=[pltpu.VMEM((first_rows, width, channels), BF16)]
         + front_scratch(first_rows),
         compiler_params=params,
         name="first",
     )(wide_rows, row_0, row_1, *weights)
+    query = queries(mixed, 0)
     payload, other = sum_by_permutes(payload)
 
     second_rows = first_rows - 6
-    mixed, query, payload = pl.pallas_call(
+    mixed, payload = pl.pallas_call(
         functools.partial(second_kernel, tile, head_dim),
-        out_shape=outs_of(second_rows - 6),
+        out_shape=outs_of(second_rows - 2),
         grid=(1,),
-        in_specs=[far()] * 2 + [near()] * 4 + weight_specs,
-        out_specs=[far(), far(), near()],
+        in_specs=[far()] * 2 + [near()] * 3 + [far()] + weight_specs,
+        out_specs=[far(), near()],
         scratch_shapes=attend_scratch(second_rows) + front_scratch(second_rows),
         compiler_params=params,
         name="second",
     )(mixed, query, payload, other, output_weight, output_bias, *weights)
+    query = queries(mixed, 1)
     payload, other = sum_by_permutes(payload)
 
     return pl.pallas_call(
@@ -635,7 +696,7 @@
             jax.ShapeDtypeStruct((4, rows, cols), F32),
         ],
         grid=(1,),
-        in_specs=[far()] * 2 + [near()] * 6,
+        in_specs=[far()] * 2 + [near()] * 3 + [far()] + [near()] * 2,
         out_specs=[near()] * 2,
         scratch_shapes=attend_scratch(rows + 2),
         compiler_params=params,

time: 80.5 us -> 75.7 us (0.940)
  starting transfers between devices: 28.8 us -> 25.2 us
  waiting for transfers between devices: 18.8 us -> 17.3 us
    ppermute x14, starting transfers between devices: 24.3 us -> 17.9 us  [sum_by_permutes(): lax.ppermute(value, axis, [(i, partner(i, stride, radix, k)) for i in ran...]
    pallas_call x0 -> x2, Pallas kernels: none -> 5.4 us  [queries(): pl.pallas_call(functools.partial(query_kernel, tile, section), out_shape=...]
    pallas_call x1, Pallas kernels: 11.7 us -> 8.84 us  [local(): pl.pallas_call(functools.partial(first_kernel, tile, head_dim), out_shape...]
    ppermute x4, starting transfers between devices: 4.49 us -> 7.32 us  [pair_exchange(): return lax.ppermute(value, axis, pairs)]
    ppermute x14, waiting for transfers between devices: 17.6 us -> 15.4 us  [sum_by_permutes(): lax.ppermute(value, axis, [(i, partner(i, stride, radix, k)) for i in ran...]
    pallas_call x1, Pallas kernels: 12 us -> 9.81 us  [local(): pl.pallas_call(functools.partial(second_kernel, tile, head_dim), out_shap...]
  transfers between devices with their start and end apart: 18 -> 18, of which waited for: 12 -> 13; matrix products, arithmetic and copies ran while one was open for 0% -> 0% of each run, Pallas kernels for 2% -> 10%
where the time goes in v10:
time: 75.7 us; the launch traced here: 75.5 us
  Pallas kernels  29.3 us (39%)
  starting transfers between devices  25.2 us (33%)
  waiting for transfers between devices  17.3 us (23%)
  local copies, waits for them, and re-layouts  1.73 us (2%)
  between operations  1.04 us (1%)
  other arithmetic  1.03 us (1%)
    ppermute x14, starting transfers between devices, sum_by_permutes(): lax.ppermute(value, axis, [(i, partner(i, stride, radix, k)) for i in ran...  17.9 us
    ppermute x14, waiting for transfers between devices, sum_by_permutes(): lax.ppermute(value, axis, [(i, partner(i, stride, radix, k)) for i in ran...  15.4 us
    pallas_call x1, Pallas kernels, local(): pl.pallas_call(functools.partial(second_kernel, tile, head_dim), out_shap...  9.81 us
    pallas_call x1, Pallas kernels, local(): pl.pallas_call(functools.partial(first_kernel, tile, head_dim), out_shape...  8.84 us
    ppermute x4, starting transfers between devices, pair_exchange(): return lax.ppermute(value, axis, pairs)  7.32 us
    pallas_call x2, Pallas kernels, queries(): pl.pallas_call(functools.partial(query_kernel, tile, section), out_shape=...  5.4 us
    pallas_call x1, Pallas kernels, local(): pl.pallas_call(functools.partial(last_kernel, tile, head_dim), out_shape=...  3.34 us
    ppermute x4, waiting for transfers between devices, pair_exchange(): return lax.ppermute(value, axis, pairs)  1.9 us
  transfers between devices with their start and end apart: 18, of which 13 were waited for; matrix products, arithmetic and copies ran while one was open for 0% of the time, Pallas kernels for 10%

profile of v10, /device:TPU:0, one launch (start us, length us, event | category | flops | bytes accessed | tf_op | source)
XLA Modules:
  0.0 75.5 jit_solution(3267947672670842997)
XLA Ops:
  2.2 5.8 %collective-permute-start.1 = (bf16[8,8,256]{2,1,0:T(8,128)(2,1)S(1)}, bf16[8,8,256]{2,1,0:T(8,128)(2,1)S(1)}, u32[]{:S(2)}, u32[]{:S(2)}) collective-permute-start(bf16[8,8,256]{2,1,0:T(8,128)(2,1)S(1)} %get-tuple-element.21), channel_id=1, source_target_pairs={{0,1},{1,0},{2,3},{3,2},{4,5},{5,4},{6,7},{7,6},{8,9},{9,8},{10,11... | collective-permute-start | bytes 98312 | tf_op jit(solution)/shard_map/ppermute | solution.py:532
  8.0 1.9 %collective-permute-done.1 = bf16[8,8,256]{2,1,0:T(8,128)(2,1)S(1)} collective-permute-done((bf16[8,8,256]{2,1,0:T(8,128)(2,1)S(1)}, bf16[8,8,256]{2,1,0:T(8,128)(2,1)S(1)}, u32[]{:S(2)}, u32[]{:S(2)}) %collective-permute-start.1) | collective-permute-done | bytes 32800 | tf_op jit(solution)/shard_map/ppermute | solution.py:532
  11.9 1.9 %prepare.1 = (bf16[2,256,768]{2,1,0:T(8,128)(2,1)S(1)}, f32[2,32,768]{2,1,0:T(8,128)S(1)}, bf16[2,3,256,256]{3,2,1,0:T(8,128)(2,1)S(1)}, bf16[3,128,256]{2,1,0:T(8,128)(2,1)S(1)}) custom-call(bf16[2,256,768]{2,1,0:T(8,128)(2,1)S(1)} %copy-done.8, f32[5,5,2,768]{3,2,1,0:T(2,128)S(1)} %bitcast.5, bf16[2,24,32,32]{3,2,1,0:T(8,128)(2,1)S(1)} %copy-done.9, ...), custom_call_target="tpu_custom_call" | custom-call | flops 2000000000 | bytes 4000000 | tf_op jit(solution)/shard_map/prepare/pallas_call | solution.py:585
  14.5 8.8 %first.1 = (bf16[20,48,256]{2,1,0:T(8,128)(2,1)S(1)}, bf16[144,128]{1,0:T(8,128)(2,1)S(1)}) custom-call(bf16[8,48,256]{2,1,0:T(8,128)(2,1)S(1)} %pad_maximum_fusion.own, bf16[7,48,256]{2,1,0:T(8,128)(2,1)S(1)} %collective-permute-done.2.row_0, bf16[7,48,256]{2,1,0:T(8,128)(2,1)S(1)} %collective-permute-done.3.row_1, bf16[2,256,1024]{2,1,0:T(8,128)(2,1)S(1)} %copy-done, ...), custom_call_target="tpu_custom_call" | custom-call | tf_op jit(solution)/shard_map/first/pallas_call | solution.py:664
  23.3 4.4 %collective-permute-start.4 = (bf16[144,128]{1,0:T(8,128)(2,1)S(1)}, bf16[144,128]{1,0:T(8,128)(2,1)S(1)}, u32[]{:S(2)}, u32[]{:S(2)}) collective-permute-start(bf16[144,128]{1,0:T(8,128)(2,1)S(1)} %get-tuple-element.14), channel_id=1, source_target_pairs={{0,8},{8,0},{16,24},{24,16},{1,9},{9,1},{17,25},{25,17},{2,10},{10... | collective-permute-start | bytes 110600 | tf_op jit(solution)/shard_map/ppermute | solution.py:506
  27.7 1.2 %collective-permute-start.5 = (bf16[144,128]{1,0:T(8,128)(2,1)S(1)}, bf16[144,128]{1,0:T(8,128)(2,1)S(1)}, u32[]{:S(2)}, u32[]{:S(2)}) collective-permute-start(bf16[144,128]{1,0:T(8,128)(2,1)S(1)} %get-tuple-element.14), channel_id=1, source_target_pairs={{0,16},{8,24},{16,0},{24,8},{1,17},{9,25},{17,1},{25,9},{2,18},{10... | collective-permute-start | bytes 110600 | tf_op jit(solution)/shard_map/ppermute | solution.py:506
  29.2 2.5 %collective-permute-done.5 = bf16[144,128]{1,0:T(8,128)(2,1)S(1)} collective-permute-done((bf16[144,128]{1,0:T(8,128)(2,1)S(1)}, bf16[144,128]{1,0:T(8,128)(2,1)S(1)}, u32[]{:S(2)}, u32[]{:S(2)}) %collective-permute-start.5) | collective-permute-done | bytes 36896 | tf_op jit(solution)/shard_map/ppermute | solution.py:506
  32.4 2.1 %collective-permute-start.7 = (bf16[144,128]{1,0:T(8,128)(2,1)S(1)}, bf16[144,128]{1,0:T(8,128)(2,1)S(1)}, u32[]{:S(2)}, u32[]{:S(2)}) collective-permute-start(bf16[144,128]{1,0:T(8,128)(2,1)S(1)} %add_convert_fusion.3), channel_id=1, source_target_pairs={{0,1},{1,0},{2,3},{3,2},{4,5},{5,4},{6,7},{7,6},{8,9},{9,8},{10,11... | collective-permute-start | bytes 110600 | tf_op jit(solution)/shard_map/ppermute | solution.py:506
  34.5 1.6 %collective-permute-start.8 = (bf16[144,128]{1,0:T(8,128)(2,1)S(1)}, bf16[144,128]{1,0:T(8,128)(2,1)S(1)}, u32[]{:S(2)}, u32[]{:S(2)}) collective-permute-start(bf16[144,128]{1,0:T(8,128)(2,1)S(1)} %add_convert_fusion.3), channel_id=1, source_target_pairs={{0,2},{1,3},{2,0},{3,1},{4,6},{5,7},{6,4},{7,5},{8,10},{9,11},{10,... | collective-permute-start | bytes 110600 | tf_op jit(solution)/shard_map/ppermute | solution.py:506
  36.4 2.3 %collective-permute-done.8 = bf16[144,128]{1,0:T(8,128)(2,1)S(1)} collective-permute-done((bf16[144,128]{1,0:T(8,128)(2,1)S(1)}, bf16[144,128]{1,0:T(8,128)(2,1)S(1)}, u32[]{:S(2)}, u32[]{:S(2)}) %collective-permute-start.8) | collective-permute-done | bytes 36896 | tf_op jit(solution)/shard_map/ppermute | solution.py:506
  38.8 2.1 %collective-permute-done.9 = bf16[144,128]{1,0:T(8,128)(2,1)S(1)} collective-permute-done((bf16[144,128]{1,0:T(8,128)(2,1)S(1)}, bf16[144,128]{1,0:T(8,128)(2,1)S(1)}, u32[]{:S(2)}, u32[]{:S(2)}) %collective-permute-start.9) | collective-permute-done | bytes 36896 | tf_op jit(solution)/shard_map/ppermute | solution.py:506
  40.9 1.1 %collective-permute-start.10 = (bf16[144,128]{1,0:T(8,128)(2,1)S(1)}, bf16[144,128]{1,0:T(8,128)(2,1)S(1)}, u32[]{:S(2)}, u32[]{:S(2)}) collective-permute-start(bf16[144,128]{1,0:T(8,128)(2,1)S(1)} %add_convert_fusion.2.payload), channel_id=1, source_target_pairs={{0,4},{1,5},{2,6},{3,7},{4,0},{5,1},{6,2},{7,3},{8,12},{9,13},{10,... | collective-permute-start | bytes 110600 | tf_op jit(solution)/shard_map/ppermute | solution.py:506
  42.1 3.1 %queries.2.query = bf16[16,48,512]{2,1,0:T(8,128)(2,1)S(1)} custom-call(bf16[20,48,256]{2,1,0:T(8,128)(2,1)S(1)} %get-tuple-element.13.mixed_in.mixed, bf16[2,256,768]{2,1,0:T(8,128)(2,1)S(1)} %get-tuple-element.10.refs_6_.qkv_weight, f32[2,32,768]{2,1,0:T(8,128)S(1)} %get-tuple-element.11.refs_7_.taps, ...), custom_call_target="tpu_custom_call" | custom-call | flops 402653184 | bytes 1572864 | tf_op jit(solution)/shard_map/queries/pallas_call | solution.py:640
  45.2 1.0 %collective-permute-done.10.other = bf16[144,128]{1,0:T(8,128)(2,1)S(1)} collective-permute-done((bf16[144,128]{1,0:T(8,128)(2,1)S(1)}, bf16[144,128]{1,0:T(8,128)(2,1)S(1)}, u32[]{:S(2)}, u32[]{:S(2)}) %collective-permute-start.10) | collective-permute-done | bytes 36896 | tf_op jit(solution)/shard_map/ppermute | solution.py:506
  46.2 9.8 %second.1 = (bf16[14,48,256]{2,1,0:T(8,128)(2,1)S(1)}, bf16[144,128]{1,0:T(8,128)(2,1)S(1)}) custom-call(bf16[20,48,256]{2,1,0:T(8,128)(2,1)S(1)} %get-tuple-element.13.mixed_in.mixed, bf16[16,48,512]{2,1,0:T(8,128)(2,1)S(1)} %queries.2.query, bf16[144,128]{1,0:T(8,128)(2,1)S(1)} %add_convert_fusion.2.payload, ...), custom_call_target="tpu_custom_call" | custom-call | tf_op jit(solution)/shard_map/second/pallas_call | solution.py:679
  56.1 1.2 %collective-permute-start.12 = (bf16[144,128]{1,0:T(8,128)(2,1)S(1)}, bf16[144,128]{1,0:T(8,128)(2,1)S(1)}, u32[]{:S(2)}, u32[]{:S(2)}) collective-permute-start(bf16[144,128]{1,0:T(8,128)(2,1)S(1)} %get-tuple-element.16), channel_id=1, source_target_pairs={{0,16},{8,24},{16,0},{24,8},{1,17},{9,25},{17,1},{25,9},{2,18},{10... | collective-permute-start | bytes 110600 | tf_op jit(solution)/shard_map/ppermute | solution.py:506
  57.9 2.2 %collective-permute-done.12 = bf16[144,128]{1,0:T(8,128)(2,1)S(1)} collective-permute-done((bf16[144,128]{1,0:T(8,128)(2,1)S(1)}, bf16[144,128]{1,0:T(8,128)(2,1)S(1)}, u32[]{:S(2)}, u32[]{:S(2)}) %collective-permute-start.12) | collective-permute-done | bytes 36896 | tf_op jit(solution)/shard_map/ppermute | solution.py:506
  60.7 1.0 %collective-permute-start.14 = (bf16[144,128]{1,0:T(8,128)(2,1)S(1)}, bf16[144,128]{1,0:T(8,128)(2,1)S(1)}, u32[]{:S(2)}, u32[]{:S(2)}) collective-permute-start(bf16[144,128]{1,0:T(8,128)(2,1)S(1)} %add_convert_fusion.1), channel_id=1, source_target_pairs={{0,1},{1,0},{2,3},{3,2},{4,5},{5,4},{6,7},{7,6},{8,9},{9,8},{10,11... | collective-permute-start | bytes 110600 | tf_op jit(solution)/shard_map/ppermute | solution.py:506
  62.2 2.1 %collective-permute-start.16 = (bf16[144,128]{1,0:T(8,128)(2,1)S(1)}, bf16[144,128]{1,0:T(8,128)(2,1)S(1)}, u32[]{:S(2)}, u32[]{:S(2)}) collective-permute-start(bf16[144,128]{1,0:T(8,128)(2,1)S(1)} %add_convert_fusion.1), channel_id=1, source_target_pairs={{0,3},{1,2},{2,1},{3,0},{4,7},{5,6},{6,5},{7,4},{8,11},{9,10},{10,... | collective-permute-start | bytes 110600 | tf_op jit(solution)/shard_map/ppermute | solution.py:506
  64.8 1.2 %collective-permute-done.15 = bf16[144,128]{1,0:T(8,128)(2,1)S(1)} collective-permute-done((bf16[144,128]{1,0:T(8,128)(2,1)S(1)}, bf16[144,128]{1,0:T(8,128)(2,1)S(1)}, u32[]{:S(2)}, u32[]{:S(2)}) %collective-permute-start.15) | collective-permute-done | bytes 36896 | tf_op jit(solution)/shard_map/ppermute | solution.py:506
  66.0 1.1 %collective-permute-done.16 = bf16[144,128]{1,0:T(8,128)(2,1)S(1)} collective-permute-done((bf16[144,128]{1,0:T(8,128)(2,1)S(1)}, bf16[144,128]{1,0:T(8,128)(2,1)S(1)}, u32[]{:S(2)}, u32[]{:S(2)}) %collective-permute-start.16) | collective-permute-done | bytes 36896 | tf_op jit(solution)/shard_map/ppermute | solution.py:506
  67.1 1.8 %collective-permute-start.17 = (bf16[144,128]{1,0:T(8,128)(2,1)S(1)}, bf16[144,128]{1,0:T(8,128)(2,1)S(1)}, u32[]{:S(2)}, u32[]{:S(2)}) collective-permute-start(bf16[144,128]{1,0:T(8,128)(2,1)S(1)} %add_convert_fusion.payload), channel_id=1, source_target_pairs={{0,4},{1,5},{2,6},{3,7},{4,0},{5,1},{6,2},{7,3},{8,12},{9,13},{10,... | collective-permute-start | bytes 110600 | tf_op jit(solution)/shard_map/ppermute | solution.py:506
  69.0 2.3 %queries.3.query = bf16[10,48,512]{2,1,0:T(8,128)(2,1)S(1)} custom-call(bf16[14,48,256]{2,1,0:T(8,128)(2,1)S(1)} %get-tuple-element.15.mixed_in.mixed, bf16[2,256,768]{2,1,0:T(8,128)(2,1)S(1)} %get-tuple-element.10.refs_6_.qkv_weight, f32[2,32,768]{2,1,0:T(8,128)S(1)} %get-tuple-element.11.refs_7_.taps, ...), custom_call_target="tpu_custom_call" | custom-call | flops 251658240 | bytes 983040 | tf_op jit(solution)/shard_map/queries/pallas_call | solution.py:640
  72.0 3.3 %last.1 = (bf16[8,32,256]{2,1,0:T(8,128)(2,1)}, f32[4,8,32]{2,1,0:T(8,128)}) custom-call(bf16[14,48,256]{2,1,0:T(8,128)(2,1)S(1)} %get-tuple-element.15.mixed_in.mixed, bf16[10,48,512]{2,1,0:T(8,128)(2,1)S(1)} %queries.3.query, bf16[144,128]{1,0:T(8,128)(2,1)S(1)} %add_convert_fusion.payload, bf16[144,128]{1,0:T(8,128)(2,1)S(1)} %collective-permute-done.17.other, ...), custom_call_target="tpu_custom_call" | custom-call | tf_op jit(solution)/shard_map/last/pallas_call | solution.py:692
  (53 shorter events, 8.6 us)
Async XLA Ops:
  0.6 11.1 %copy-start.8 = (bf16[2,256,768]{2,1,0:T(8,128)(2,1)S(1)}, bf16[2,256,768]{2,1,0:T(8,128)(2,1)}, u32[]{:S(2)}) copy-start(bf16[2,256,768]{2,1,0:T(8,128)(2,1)} %qkv.1) | copy-start | bytes 2359300
  1.5 6.5 %collective-permute-start = (bf16[8,8,256]{2,1,0:T(8,128)(2,1)S(1)}, bf16[8,8,256]{2,1,0:T(8,128)(2,1)S(1)}, u32[]{:S(2)}, u32[]{:S(2)}) collective-permute-start(bf16[8,8,256]{2,1,0:T(8,128)(2,1)S(1)} %get-tuple-element.20), channel_id=1, source_target_pairs={{1,2},{2,1},{3,4},{4,3},{5,6},{6,5},{9,10},{10,9},{11,12},{12,11},... | collective-permute-start | bytes 98312 | tf_op jit(solution)/shard_map/ppermute | solution.py:532
  2.2 7.7 %collective-permute-start.1 = (bf16[8,8,256]{2,1,0:T(8,128)(2,1)S(1)}, bf16[8,8,256]{2,1,0:T(8,128)(2,1)S(1)}, u32[]{:S(2)}, u32[]{:S(2)}) collective-permute-start(bf16[8,8,256]{2,1,0:T(8,128)(2,1)S(1)} %get-tuple-element.21), channel_id=1, source_target_pairs={{0,1},{1,0},{2,3},{3,2},{4,5},{5,4},{6,7},{7,6},{8,9},{9,8},{10,11... | collective-permute-start | bytes 98312 | tf_op jit(solution)/shard_map/ppermute | solution.py:532
  10.9 2.9 %collective-permute-start.2 = (bf16[7,48,256]{2,1,0:T(8,128)(2,1)S(1)}, bf16[7,48,256]{2,1,0:T(8,128)(2,1)S(1)}, u32[]{:S(2)}, u32[]{:S(2)}) collective-permute-start(bf16[7,48,256]{2,1,0:T(8,128)(2,1)S(1)} %get-tuple-element.19), channel_id=1, source_target_pairs={{0,8},{8,0},{16,24},{24,16},{1,9},{9,1},{17,25},{25,17},{2,10},{10... | collective-permute-start | bytes 516104 | tf_op jit(solution)/shard_map/ppermute | solution.py:532
  11.0 2.8 %collective-permute-start.3 = (bf16[7,48,256]{2,1,0:T(8,128)(2,1)S(1)}, bf16[7,48,256]{2,1,0:T(8,128)(2,1)S(1)}, u32[]{:S(2)}, u32[]{:S(2)}) collective-permute-start(bf16[7,48,256]{2,1,0:T(8,128)(2,1)S(1)} %get-tuple-element.18), channel_id=1, source_target_pairs={{8,16},{16,8},{9,17},{17,9},{10,18},{18,10},{11,19},{19,11},{12,20... | collective-permute-start | bytes 516104 | tf_op jit(solution)/shard_map/ppermute | solution.py:532
  11.8 2.0 %copy-start.3 = (f32[2,3,3,1024]{3,0,2,1:T(2,128)S(1)}, f32[2,3,3,1024]{3,0,2,1:T(2,128)}, u32[]{:S(2)}) copy-start(f32[2,3,3,1024]{3,0,2,1:T(2,128)} %param.17) | copy-start | bytes 221188
  11.8 2.0 %copy-start.4 = (f32[2,1024]{1,0:T(2,128)S(1)}, f32[2,1024]{1,0:T(2,128)}, u32[]{:S(2)}) copy-start(f32[2,1024]{1,0:T(2,128)} %refs_1_.3) | copy-start | bytes 24580
  11.9 2.0 %copy-start.5 = (f32[2,1024]{1,0:T(2,128)S(1)}, f32[2,1024]{1,0:T(2,128)}, u32[]{:S(2)}) copy-start(f32[2,1024]{1,0:T(2,128)} %refs_3_.3) | copy-start | bytes 24580
  23.3 5.8 %collective-permute-start.4 = (bf16[144,128]{1,0:T(8,128)(2,1)S(1)}, bf16[144,128]{1,0:T(8,128)(2,1)S(1)}, u32[]{:S(2)}, u32[]{:S(2)}) collective-permute-start(bf16[144,128]{1,0:T(8,128)(2,1)S(1)} %get-tuple-element.14), channel_id=1, source_target_pairs={{0,8},{8,0},{16,24},{24,16},{1,9},{9,1},{17,25},{25,17},{2,10},{10... | collective-permute-start | bytes 110600 | tf_op jit(solution)/shard_map/ppermute | solution.py:506
  27.7 4.0 %collective-permute-start.5 = (bf16[144,128]{1,0:T(8,128)(2,1)S(1)}, bf16[144,128]{1,0:T(8,128)(2,1)S(1)}, u32[]{:S(2)}, u32[]{:S(2)}) collective-permute-start(bf16[144,128]{1,0:T(8,128)(2,1)S(1)} %get-tuple-element.14), channel_id=1, source_target_pairs={{0,16},{8,24},{16,0},{24,8},{1,17},{9,25},{17,1},{25,9},{2,18},{10... | collective-permute-start | bytes 110600 | tf_op jit(solution)/shard_map/ppermute | solution.py:506
  29.0 3.4 %collective-permute-start.6 = (bf16[144,128]{1,0:T(8,128)(2,1)S(1)}, bf16[144,128]{1,0:T(8,128)(2,1)S(1)}, u32[]{:S(2)}, u32[]{:S(2)}) collective-permute-start(bf16[144,128]{1,0:T(8,128)(2,1)S(1)} %get-tuple-element.14), channel_id=1, source_target_pairs={{0,24},{8,16},{16,8},{24,0},{1,25},{9,17},{17,9},{25,1},{2,26},{10... | collective-permute-start | bytes 110600 | tf_op jit(solution)/shard_map/ppermute | solution.py:506
  32.4 4.0 %collective-permute-start.7 = (bf16[144,128]{1,0:T(8,128)(2,1)S(1)}, bf16[144,128]{1,0:T(8,128)(2,1)S(1)}, u32[]{:S(2)}, u32[]{:S(2)}) collective-permute-start(bf16[144,128]{1,0:T(8,128)(2,1)S(1)} %add_convert_fusion.3), channel_id=1, source_target_pairs={{0,1},{1,0},{2,3},{3,2},{4,5},{5,4},{6,7},{7,6},{8,9},{9,8},{10,11... | collective-permute-start | bytes 110600 | tf_op jit(solution)/shard_map/ppermute | solution.py:506
  34.5 4.3 %collective-permute-start.8 = (bf16[144,128]{1,0:T(8,128)(2,1)S(1)}, bf16[144,128]{1,0:T(8,128)(2,1)S(1)}, u32[]{:S(2)}, u32[]{:S(2)}) collective-permute-start(bf16[144,128]{1,0:T(8,128)(2,1)S(1)} %add_convert_fusion.3), channel_id=1, source_target_pairs={{0,2},{1,3},{2,0},{3,1},{4,6},{5,7},{6,4},{7,5},{8,10},{9,11},{10,... | collective-permute-start | bytes 110600 | tf_op jit(solution)/shard_map/ppermute | solution.py:506
  36.1 4.9 %collective-permute-start.9 = (bf16[144,128]{1,0:T(8,128)(2,1)S(1)}, bf16[144,128]{1,0:T(8,128)(2,1)S(1)}, u32[]{:S(2)}, u32[]{:S(2)}) collective-permute-start(bf16[144,128]{1,0:T(8,128)(2,1)S(1)} %add_convert_fusion.3), channel_id=1, source_target_pairs={{0,3},{1,2},{2,1},{3,0},{4,7},{5,6},{6,5},{7,4},{8,11},{9,10},{10,... | collective-permute-start | bytes 110600 | tf_op jit(solution)/shard_map/ppermute | solution.py:506
  40.9 5.2 %collective-permute-start.10 = (bf16[144,128]{1,0:T(8,128)(2,1)S(1)}, bf16[144,128]{1,0:T(8,128)(2,1)S(1)}, u32[]{:S(2)}, u32[]{:S(2)}) collective-permute-start(bf16[144,128]{1,0:T(8,128)(2,1)S(1)} %add_convert_fusion.2.payload), channel_id=1, source_target_pairs={{0,4},{1,5},{2,6},{3,7},{4,0},{5,1},{6,2},{7,3},{8,12},{9,13},{10,... | collective-permute-start | bytes 110600 | tf_op jit(solution)/shard_map/ppermute | solution.py:506
  42.0 4.1 %copy-start.2 = (bf16[2,512,256]{2,1,0:T(8,128)(2,1)S(1)}, bf16[2,512,256]{2,1,0:T(8,128)(2,1)}, u32[]{:S(2)}) copy-start(bf16[2,512,256]{2,1,0:T(8,128)(2,1)} %out_weight.3) | copy-start | bytes 1572868
  42.1 4.1 %copy-start.7 = (f32[2,256]{1,0:T(2,128)S(1)}, f32[2,256]{1,0:T(2,128)}, u32[]{:S(2)}) copy-start(f32[2,256]{1,0:T(2,128)} %out_bias.3) | copy-start | bytes 6148
  56.0 1.9 %collective-permute-start.11 = (bf16[144,128]{1,0:T(8,128)(2,1)S(1)}, bf16[144,128]{1,0:T(8,128)(2,1)S(1)}, u32[]{:S(2)}, u32[]{:S(2)}) collective-permute-start(bf16[144,128]{1,0:T(8,128)(2,1)S(1)} %get-tuple-element.16), channel_id=1, source_target_pairs={{0,8},{8,0},{16,24},{24,16},{1,9},{9,1},{17,25},{25,17},{2,10},{10... | collective-permute-start | bytes 110600 | tf_op jit(solution)/shard_map/ppermute | solution.py:506
  56.1 4.0 %collective-permute-start.12 = (bf16[144,128]{1,0:T(8,128)(2,1)S(1)}, bf16[144,128]{1,0:T(8,128)(2,1)S(1)}, u32[]{:S(2)}, u32[]{:S(2)}) collective-permute-start(bf16[144,128]{1,0:T(8,128)(2,1)S(1)} %get-tuple-element.16), channel_id=1, source_target_pairs={{0,16},{8,24},{16,0},{24,8},{1,17},{9,25},{17,1},{25,9},{2,18},{10... | collective-permute-start | bytes 110600 | tf_op jit(solution)/shard_map/ppermute | solution.py:506
  57.3 3.4 %collective-permute-start.13 = (bf16[144,128]{1,0:T(8,128)(2,1)S(1)}, bf16[144,128]{1,0:T(8,128)(2,1)S(1)}, u32[]{:S(2)}, u32[]{:S(2)}) collective-permute-start(bf16[144,128]{1,0:T(8,128)(2,1)S(1)} %get-tuple-element.16), channel_id=1, source_target_pairs={{0,24},{8,16},{16,8},{24,0},{1,25},{9,17},{17,9},{25,1},{2,26},{10... | collective-permute-start | bytes 110600 | tf_op jit(solution)/shard_map/ppermute | solution.py:506
  60.7 4.0 %collective-permute-start.14 = (bf16[144,128]{1,0:T(8,128)(2,1)S(1)}, bf16[144,128]{1,0:T(8,128)(2,1)S(1)}, u32[]{:S(2)}, u32[]{:S(2)}) collective-permute-start(bf16[144,128]{1,0:T(8,128)(2,1)S(1)} %add_convert_fusion.1), channel_id=1, source_target_pairs={{0,1},{1,0},{2,3},{3,2},{4,5},{5,4},{6,7},{7,6},{8,9},{9,8},{10,11... | collective-permute-start | bytes 110600 | tf_op jit(solution)/shard_map/ppermute | solution.py:506
  61.8 4.2 %collective-permute-start.15 = (bf16[144,128]{1,0:T(8,128)(2,1)S(1)}, bf16[144,128]{1,0:T(8,128)(2,1)S(1)}, u32[]{:S(2)}, u32[]{:S(2)}) collective-permute-start(bf16[144,128]{1,0:T(8,128)(2,1)S(1)} %add_convert_fusion.1), channel_id=1, source_target_pairs={{0,2},{1,3},{2,0},{3,1},{4,6},{5,7},{6,4},{7,5},{8,10},{9,11},{10,... | collective-permute-start | bytes 110600 | tf_op jit(solution)/shard_map/ppermute | solution.py:506
  62.2 4.9 %collective-permute-start.16 = (bf16[144,128]{1,0:T(8,128)(2,1)S(1)}, bf16[144,128]{1,0:T(8,128)(2,1)S(1)}, u32[]{:S(2)}, u32[]{:S(2)}) collective-permute-start(bf16[144,128]{1,0:T(8,128)(2,1)S(1)} %add_convert_fusion.1), channel_id=1, source_target_pairs={{0,3},{1,2},{2,1},{3,0},{4,7},{5,6},{6,5},{7,4},{8,11},{9,10},{10,... | collective-permute-start | bytes 110600 | tf_op jit(solution)/shard_map/ppermute | solution.py:506
  67.1 4.9 %collective-permute-start.17 = (bf16[144,128]{1,0:T(8,128)(2,1)S(1)}, bf16[144,128]{1,0:T(8,128)(2,1)S(1)}, u32[]{:S(2)}, u32[]{:S(2)}) collective-permute-start(bf16[144,128]{1,0:T(8,128)(2,1)S(1)} %add_convert_fusion.payload), channel_id=1, source_target_pairs={{0,4},{1,5},{2,6},{3,7},{4,0},{5,1},{6,2},{7,3},{8,12},{9,13},{10,... | collective-permute-start | bytes 110600 | tf_op jit(solution)/shard_map/ppermute | solution.py:506
  (7 other events, 9.5 us)

commit v11 on v10

--- a/solution.py
+++ b/solution.py
@@ -13,7 +13,7 @@
 REACH = 7
 KEY_ROWS = 16
 TILE = 16
-PARTS = 4
+PARTS = 2
 F32 = jnp.float32
 BF16 = jnp.bfloat16
 
@@ -249,8 +249,8 @@
 
 
 def query_kernel(
-    tile, section, mixed_in, qkv_weight, taps, groups, query_out,
-    mixed, centre, query, weight, agg, group, wide_agg, sems,
+    tile, section, mixed_in, qkv_weight, taps, groups, query, mixed_out,
+    mixed, centre, weight, agg, group, wide_agg, sems,
 ):
     rows, width, channels = mixed.shape
     head = pl.ds(0, channels)
@@ -264,6 +264,7 @@
         load.start()
     for load in loads:
         load.wait()
+    mixed_out[...] = mixed[2 : rows - 2]
     spread_taps(agg, wide_agg)
     for first, size in parted(rows, PARTS):
         value = jnp.dot(
@@ -279,21 +280,15 @@
         query[here, :, channels : 2 * channels] = jnp.maximum(grouped, 0.0)
 
     by_groups(rows - 4, 5, query_rows)
-    store = pltpu.make_async_copy(query, query_out, sems.at[4])
-    store.start()
-    store.wait()
 
 
 def attend(
-    mixed_in, query_in, payloads, weight, bias_in, held, head_dim, section, x_ref
+    mixed_ref, query_ref, payloads, weight, bias_in, held, head_dim, section, x_ref
 ):
     rows, width, channels = x_ref.shape
-    mixed_ref, query_ref, bias, sems = held
-    inner = mixed_in.at[pl.ds(2, rows)]
-    halves = [(query_in, query_ref), (inner, mixed_ref), (bias_in, bias)]
-    loads = [pltpu.make_async_copy(a, b, sems.at[k]) for k, (a, b) in enumerate(halves)]
-    for load in loads:
-        load.start()
+    bias, sem = held
+    load = pltpu.make_async_copy(bias_in, bias, sem)
+    load.start()
     same = same_head(head_dim)
     square = (LANES, LANES)
     diagonal = lax.broadcasted_iota(jnp.int32, square, 0) == lax.broadcasted_iota(
@@ -326,8 +321,7 @@
     summaries = [paired(summaries, index) for index in range(0, count, 2)]
     sums = [paired(sums, index) for index in range(0, count, 2)]
     step = 2 * LANES
-    for load in loads:
-        load.wait()
+    load.wait()
 
     def attend_rows(first, size):
         query = flat(query_ref[pl.ds(first, size)])
@@ -354,9 +348,10 @@
     return slice(at, at + 1)
 
 
-def prepare_kernel(head_dim, qkv, agg, group, head, *refs):
-    outs, made, taps, sems = refs[:4], refs[4:8], refs[8], refs[9]
+def prepare_kernel(head_dim, qkv, agg, group, head, project_bias, output_bias, *refs):
+    outs, made, taps, sems = refs[:6], refs[6:10], refs[10], refs[11]
     qkv_out, agg_out, group_out, head_out = made
+    made = [*made, project_bias, output_bias]
     sections, channels, wide = qkv.shape
     half = 3 * LANES
     heads = LANES // head_dim
@@ -401,7 +396,7 @@
     for a in range(3):
         rows = [head[a, b] for b in range(3)] + [jnp.zeros((4, channels), BF16)]
         head_out[a, 0:16, :] = jnp.concatenate(rows, axis=0)
-    stores = [pltpu.make_async_copy(made[i], outs[i], sems.at[i]) for i in range(4)]
+    stores = [pltpu.make_async_copy(made[i], outs[i], sems.at[i]) for i in range(6)]
     for store in stores:
         store.start()
     for store in stores:
@@ -424,9 +419,9 @@
     weights, outs, scratch = refs[:9], refs[9:11], refs[11:]
     x_ref = scratch[0]
     attend(
-        mixed, query, (payload, other), out_weight, out_bias, scratch[1:5], head_dim, 0, x_ref
+        mixed, query, (payload, other), out_weight, out_bias, scratch[1:3], head_dim, 0, x_ref
     )
-    front(x_ref, weights, outs, scratch[5:], REACH - 3, tile, head_dim, 1)
+    front(x_ref, weights, outs, scratch[3:], REACH - 3, tile, head_dim, 1)
 
 
 def last_kernel(
@@ -493,11 +488,11 @@
     return i + (other - digit) * stride
 
 
-def sum_by_permutes(value):
+def sum_by_permutes(value, most):
     rounds = []
     for axis in ("row", "col"):
         stride = 1
-        for radix in digits(lax.axis_size(axis), 4):
+        for radix in digits(lax.axis_size(axis), most[axis]):
             rounds.append((axis, stride, radix))
             stride *= radix
     for axis, stride, radix in rounds:
@@ -582,20 +577,21 @@
         jax.ShapeDtypeStruct((SECTIONS, 3, channels, channels), BF16),
         jax.ShapeDtypeStruct((3, LANES, channels), BF16),
     ]
-    qkv_weight, taps, group, head_weight = pl.pallas_call(
+    biases = [jax.ShapeDtypeStruct(array.shape, F32) for array in (project_bias, output_bias)]
+    qkv_weight, taps, group, head_weight, project_bias, output_bias = pl.pallas_call(
         functools.partial(prepare_kernel, head_dim),
-        out_shape=made,
+        out_shape=made + biases,
         grid=(1,),
-        in_specs=[near()] * 4,
-        out_specs=[far()] * 4,
+        in_specs=[near()] * 6,
+        out_specs=[far()] * 6,
         scratch_shapes=[pltpu.VMEM(array.shape, array.dtype) for array in made]
-        + [pltpu.VMEM((32 * SECTIONS, 3 * channels), F32), pltpu.SemaphoreType.DMA((4,))],
+        + [pltpu.VMEM((32 * SECTIONS, 3 * channels), F32), pltpu.SemaphoreType.DMA((6,))],
         compiler_params=params,
         cost_estimate=pl.CostEstimate(
             flops=2 * 10**9, bytes_accessed=4 * 10**6, transcendentals=0
         ),
         name="prepare",
-    )(qkv_weight, aggregate_depth, aggregate_group, head_weight)
+    )(qkv_weight, aggregate_depth, aggregate_group, head_weight, project_bias, output_bias)
 
     weights = [
         expand_weight, expand_bias, depth_weight, depth_bias, project_weight, project_bias,
@@ -628,10 +624,8 @@
     def attend_scratch(count):
         return [
             pltpu.VMEM((count, width, channels), BF16),
-            pltpu.VMEM((count, width, channels), BF16),
-            pltpu.VMEM((count, width, 2 * channels), BF16),
             pltpu.VMEM(output_bias.shape, F32),
-            pltpu.SemaphoreType.DMA((3,)),
+            pltpu.SemaphoreType.DMA,
         ]
 
     def queries(mixed, section):
@@ -639,19 +633,21 @@
         units = (count - 4) * width * channels
         return pl.pallas_call(
             functools.partial(query_kernel, tile, section),
-            out_shape=jax.ShapeDtypeStruct((count - 4, width, 2 * channels), BF16),
+            out_shape=[
+                jax.ShapeDtypeStruct((count - 4, width, 2 * channels), BF16),
+                jax.ShapeDtypeStruct((count - 4, width, channels), BF16),
+            ],
             grid=(1,),
             in_specs=[far()] * 4,
-            out_specs=far(),
+            out_specs=[near()] * 2,
             scratch_shapes=[
                 pltpu.VMEM((count, width, channels), BF16),
                 pltpu.VMEM((count, width, channels), BF16),
-                pltpu.VMEM((count - 4, width, 2 * channels), BF16),
                 pltpu.VMEM((channels, channels), BF16),
                 pltpu.VMEM((32, channels), F32),
                 pltpu.VMEM((channels, channels), BF16),
                 pltpu.VMEM((25, TILE, channels), BF16),
-                pltpu.SemaphoreType.DMA((5,)),
+                pltpu.SemaphoreType.DMA((4,)),
             ],
             compiler_params=params,
             cost_estimate=pl.CostEstimate(
@@ -672,22 +668,22 @@
         compiler_params=params,
         name="first",
     )(wide_rows, row_0, row_1, *weights)
-    query = queries(mixed, 0)
-    payload, other = sum_by_permutes(payload)
+    query, mixed = queries(mixed, 0)
+    payload, other = sum_by_permutes(payload, {"row": 4, "col": 2})
 
     second_rows = first_rows - 6
     mixed, payload = pl.pallas_call(
         functools.partial(second_kernel, tile, head_dim),
         out_shape=outs_of(second_rows - 2),
         grid=(1,),
-        in_specs=[far()] * 2 + [near()] * 3 + [far()] + weight_specs,
+        in_specs=[near()] * 5 + [far()] + weight_specs,
         out_specs=[far(), near()],
         scratch_shapes=attend_scratch(second_rows) + front_scratch(second_rows),
         compiler_params=params,
         name="second",
     )(mixed, query, payload, other, output_weight, output_bias, *weights)
-    query = queries(mixed, 1)
-    payload, other = sum_by_permutes(payload)
+    query, mixed = queries(mixed, 1)
+    payload, other = sum_by_permutes(payload, {"row": 2, "col": 2})
 
     return pl.pallas_call(
         functools.partial(last_kernel, tile, head_dim),
@@ -696,7 +692,7 @@
             jax.ShapeDtypeStruct((4, rows, cols), F32),
         ],
         grid=(1,),
-        in_specs=[far()] * 2 + [near()] * 3 + [far()] + [near()] * 2,
+        in_specs=[near()] * 5 + [far()] + [near()] * 2,
         out_specs=[near()] * 2,
         scratch_shapes=attend_scratch(rows + 2),
         compiler_params=params,

time: 75.7 us -> 76.1 us (level)
  Pallas kernels: 29.3 us -> 27.7 us
  starting transfers between devices: 25.2 us -> 26.8 us
    ppermute x14 -> x11, starting transfers between devices: 17.9 us -> 19.4 us  [sum_by_permutes(): lax.ppermute(value, axis, [(i, partner(i, stride, radix, k)) for i in ran...]
    ppermute x14 -> x11, waiting for transfers between devices: 15.4 us -> 15.7 us  [sum_by_permutes(): lax.ppermute(value, axis, [(i, partner(i, stride, radix, k)) for i in ran...]
  transfers between devices with their start and end apart: 18 -> 15, of which waited for: 13 -> 9; matrix products, arithmetic and copies ran while one was open for 0% -> 0% of each run, Pallas kernels for 10% -> 9%
where the time goes in v11:
time: 76.1 us; the launch traced here: 75.9 us
  Pallas kernels  27.7 us (36%)
  starting transfers between devices  26.8 us (35%)
  waiting for transfers between devices  17.6 us (23%)
  local copies, waits for them, and re-layouts  1.71 us (2%)
  between operations  1.11 us (1%)
  other arithmetic  1.04 us (1%)
    ppermute x11, starting transfers between devices, sum_by_permutes(): lax.ppermute(value, axis, [(i, partner(i, stride, radix, k)) for i in ran...  19.4 us
    ppermute x11, waiting for transfers between devices, sum_by_permutes(): lax.ppermute(value, axis, [(i, partner(i, stride, radix, k)) for i in ran...  15.7 us
    pallas_call x1, Pallas kernels, local(): pl.pallas_call(functools.partial(second_kernel, tile, head_dim), out_shap...  9.38 us
    pallas_call x1, Pallas kernels, local(): pl.pallas_call(functools.partial(first_kernel, tile, head_dim), out_shape...  8.69 us
    ppermute x4, starting transfers between devices, pair_exchange(): return lax.ppermute(value, axis, pairs)  7.32 us
    pallas_call x2, Pallas kernels, queries(): pl.pallas_call(functools.partial(query_kernel, tile, section), out_shape=...  5.03 us
    pallas_call x1, Pallas kernels, local(): pl.pallas_call(functools.partial(last_kernel, tile, head_dim), out_shape=...  2.7 us
    pallas_call x1, Pallas kernels, local(): pl.pallas_call(functools.partial(prepare_kernel, head_dim), out_shape=mad...  1.92 us
  transfers between devices with their start and end apart: 15, of which 9 were waited for; matrix products, arithmetic and copies ran while one was open for 0% of the time, Pallas kernels for 9%

profile of v11, /device:TPU:0, one launch (start us, length us, event | category | flops | bytes accessed | tf_op | source)
XLA Modules:
  0.0 75.9 jit_solution(15673617286039112794)
XLA Ops:
  2.2 5.8 %collective-permute-start.1 = (bf16[8,8,256]{2,1,0:T(8,128)(2,1)S(1)}, bf16[8,8,256]{2,1,0:T(8,128)(2,1)S(1)}, u32[]{:S(2)}, u32[]{:S(2)}) collective-permute-start(bf16[8,8,256]{2,1,0:T(8,128)(2,1)S(1)} %get-tuple-element.33), channel_id=1, source_target_pairs={{0,1},{1,0},{2,3},{3,2},{4,5},{5,4},{6,7},{7,6},{8,9},{9,8},{10,11... | collective-permute-start | bytes 98312 | tf_op jit(solution)/shard_map/ppermute | solution.py:527
  8.0 1.9 %collective-permute-done.1 = bf16[8,8,256]{2,1,0:T(8,128)(2,1)S(1)} collective-permute-done((bf16[8,8,256]{2,1,0:T(8,128)(2,1)S(1)}, bf16[8,8,256]{2,1,0:T(8,128)(2,1)S(1)}, u32[]{:S(2)}, u32[]{:S(2)}) %collective-permute-start.1) | collective-permute-done | bytes 32800 | tf_op jit(solution)/shard_map/ppermute | solution.py:527
  11.9 1.9 %prepare.1 = (bf16[2,256,768]{2,1,0:T(8,128)(2,1)S(1)}, f32[2,32,768]{2,1,0:T(8,128)S(1)}, bf16[2,3,256,256]{3,2,1,0:T(8,128)(2,1)S(1)}, bf16[3,128,256]{2,1,0:T...) custom-call(bf16[2,256,768]{2,1,0:T(8,128)(2,1)S(1)} %copy-done.6, f32[5,5,2,768]{3,2,1,0:T(2,128)S(1)} %bitcast.5, ...), custom_call_target="tpu_custom_call" | custom-call | flops 2000000000 | bytes 4000000 | tf_op jit(solution)/shard_map/prepare/pallas_call | solution.py:581
  14.5 8.7 %first.1 = (bf16[20,48,256]{2,1,0:T(8,128)(2,1)S(1)}, bf16[144,128]{1,0:T(8,128)(2,1)S(1)}) custom-call(bf16[8,48,256]{2,1,0:T(8,128)(2,1)S(1)} %pad_maximum_fusion.own, bf16[7,48,256]{2,1,0:T(8,128)(2,1)S(1)} %collective-permute-done.2.row_0, bf16[7,48,256]{2,1,0:T(8,128)(2,1)S(1)} %collective-permute-done.3.row_1, bf16[2,256,1024]{2,1,0:T(8,128)(2,1)S(1)} %copy-done, ...), custom_call_target="tpu_custom_call" | custom-call | tf_op jit(solution)/shard_map/first/pallas_call | solution.py:660
  23.2 1.6 %collective-permute-start.6 = (bf16[144,128]{1,0:T(8,128)(2,1)S(1)}, bf16[144,128]{1,0:T(8,128)(2,1)S(1)}, u32[]{:S(2)}, u32[]{:S(2)}) collective-permute-start(bf16[144,128]{1,0:T(8,128)(2,1)S(1)} %get-tuple-element.23), channel_id=1, source_target_pairs={{0,24},{8,16},{16,8},{24,0},{1,25},{9,17},{17,9},{25,1},{2,26},{10... | collective-permute-start | bytes 110600 | tf_op jit(solution)/shard_map/ppermute | solution.py:501
  24.8 3.8 %collective-permute-start.5 = (bf16[144,128]{1,0:T(8,128)(2,1)S(1)}, bf16[144,128]{1,0:T(8,128)(2,1)S(1)}, u32[]{:S(2)}, u32[]{:S(2)}) collective-permute-start(bf16[144,128]{1,0:T(8,128)(2,1)S(1)} %get-tuple-element.23), channel_id=1, source_target_pairs={{0,16},{8,24},{16,0},{24,8},{1,17},{9,25},{17,1},{25,9},{2,18},{10... | collective-permute-start | bytes 110600 | tf_op jit(solution)/shard_map/ppermute | solution.py:501
  28.6 2.5 %collective-permute-done.5 = bf16[144,128]{1,0:T(8,128)(2,1)S(1)} collective-permute-done((bf16[144,128]{1,0:T(8,128)(2,1)S(1)}, bf16[144,128]{1,0:T(8,128)(2,1)S(1)}, u32[]{:S(2)}, u32[]{:S(2)}) %collective-permute-start.5) | collective-permute-done | bytes 36896 | tf_op jit(solution)/shard_map/ppermute | solution.py:501
  31.1 2.1 %collective-permute-start.7 = (bf16[144,128]{1,0:T(8,128)(2,1)S(1)}, bf16[144,128]{1,0:T(8,128)(2,1)S(1)}, u32[]{:S(2)}, u32[]{:S(2)}) collective-permute-start(bf16[144,128]{1,0:T(8,128)(2,1)S(1)} %add_convert_fusion.6), channel_id=1, source_target_pairs={{0,1},{1,0},{2,3},{3,2},{4,5},{5,4},{6,7},{7,6},{8,9},{9,8},{10,11... | collective-permute-start | bytes 110600 | tf_op jit(solution)/shard_map/ppermute | solution.py:501
  33.2 2.0 %collective-permute-done.7 = bf16[144,128]{1,0:T(8,128)(2,1)S(1)} collective-permute-done((bf16[144,128]{1,0:T(8,128)(2,1)S(1)}, bf16[144,128]{1,0:T(8,128)(2,1)S(1)}, u32[]{:S(2)}, u32[]{:S(2)}) %collective-permute-start.7) | collective-permute-done | bytes 36896 | tf_op jit(solution)/shard_map/ppermute | solution.py:501
  35.2 2.0 %collective-permute-start.8 = (bf16[144,128]{1,0:T(8,128)(2,1)S(1)}, bf16[144,128]{1,0:T(8,128)(2,1)S(1)}, u32[]{:S(2)}, u32[]{:S(2)}) collective-permute-start(bf16[144,128]{1,0:T(8,128)(2,1)S(1)} %add_convert_fusion.5), channel_id=1, source_target_pairs={{0,2},{1,3},{2,0},{3,1},{4,6},{5,7},{6,4},{7,5},{8,10},{9,11},{10,... | collective-permute-start | bytes 110600 | tf_op jit(solution)/shard_map/ppermute | solution.py:501
  37.2 2.0 %collective-permute-done.8 = bf16[144,128]{1,0:T(8,128)(2,1)S(1)} collective-permute-done((bf16[144,128]{1,0:T(8,128)(2,1)S(1)}, bf16[144,128]{1,0:T(8,128)(2,1)S(1)}, u32[]{:S(2)}, u32[]{:S(2)}) %collective-permute-start.8) | collective-permute-done | bytes 36896 | tf_op jit(solution)/shard_map/ppermute | solution.py:501
  39.2 3.0 %collective-permute-start.9 = (bf16[144,128]{1,0:T(8,128)(2,1)S(1)}, bf16[144,128]{1,0:T(8,128)(2,1)S(1)}, u32[]{:S(2)}, u32[]{:S(2)}) collective-permute-start(bf16[144,128]{1,0:T(8,128)(2,1)S(1)} %add_convert_fusion.4.payload), channel_id=1, source_target_pairs={{0,4},{1,5},{2,6},{3,7},{4,0},{5,1},{6,2},{7,3},{8,12},{9,13},{10,... | collective-permute-start | bytes 110600 | tf_op jit(solution)/shard_map/ppermute | solution.py:501
  42.2 3.0 %queries.2 = (bf16[16,48,512]{2,1,0:T(8,128)(2,1)S(1)}, bf16[16,48,256]{2,1,0:T(8,128)(2,1)S(1)}) custom-call(bf16[20,48,256]{2,1,0:T(8,128)(2,1)S(1)} %get-tuple-element.20.mixed_in, bf16[2,256,768]{2,1,0:T(8,128)(2,1)S(1)} %get-tuple-element.17.refs_6_.qkv_weight, f32[2,32,768]{2,1,0:T(8,128)S(1)} %get-tuple-element.18.refs_7_.taps, ...), custom_call_target="tpu_custom_call" | custom-call | flops 402653184 | bytes 1572864 | tf_op jit(solution)/shard_map/queries/pallas_call | solution.py:634
  45.3 9.4 %second.1 = (bf16[14,48,256]{2,1,0:T(8,128)(2,1)S(1)}, bf16[144,128]{1,0:T(8,128)(2,1)S(1)}) custom-call(bf16[16,48,256]{2,1,0:T(8,128)(2,1)S(1)} %get-tuple-element.21.mixed, bf16[16,48,512]{2,1,0:T(8,128)(2,1)S(1)} %get-tuple-element.22.query, bf16[144,128]{1,0:T(8,128)(2,1)S(1)} %add_convert_fusion.4.payload, ...), custom_call_target="tpu_custom_call" | custom-call | tf_op jit(solution)/shard_map/second/pallas_call | solution.py:675
  54.8 1.2 %collective-permute-done.10 = bf16[144,128]{1,0:T(8,128)(2,1)S(1)} collective-permute-done((bf16[144,128]{1,0:T(8,128)(2,1)S(1)}, bf16[144,128]{1,0:T(8,128)(2,1)S(1)}, u32[]{:S(2)}, u32[]{:S(2)}) %collective-permute-start.10) | collective-permute-done | bytes 36896 | tf_op jit(solution)/shard_map/ppermute | solution.py:501
  56.0 1.8 %collective-permute-start.11 = (bf16[144,128]{1,0:T(8,128)(2,1)S(1)}, bf16[144,128]{1,0:T(8,128)(2,1)S(1)}, u32[]{:S(2)}, u32[]{:S(2)}) collective-permute-start(bf16[144,128]{1,0:T(8,128)(2,1)S(1)} %add_convert_fusion.3), channel_id=1, source_target_pairs={{0,16},{8,24},{16,0},{24,8},{1,17},{9,25},{17,1},{25,9},{2,18},{10... | collective-permute-start | bytes 110600 | tf_op jit(solution)/shard_map/ppermute | solution.py:501
  57.7 2.3 %collective-permute-done.11 = bf16[144,128]{1,0:T(8,128)(2,1)S(1)} collective-permute-done((bf16[144,128]{1,0:T(8,128)(2,1)S(1)}, bf16[144,128]{1,0:T(8,128)(2,1)S(1)}, u32[]{:S(2)}, u32[]{:S(2)}) %collective-permute-start.11) | collective-permute-done | bytes 36896 | tf_op jit(solution)/shard_map/ppermute | solution.py:501
  60.0 1.7 %collective-permute-start.12 = (bf16[144,128]{1,0:T(8,128)(2,1)S(1)}, bf16[144,128]{1,0:T(8,128)(2,1)S(1)}, u32[]{:S(2)}, u32[]{:S(2)}) collective-permute-start(bf16[144,128]{1,0:T(8,128)(2,1)S(1)} %add_convert_fusion.2), channel_id=1, source_target_pairs={{0,1},{1,0},{2,3},{3,2},{4,5},{5,4},{6,7},{7,6},{8,9},{9,8},{10,11... | collective-permute-start | bytes 110600 | tf_op jit(solution)/shard_map/ppermute | solution.py:501
  61.7 2.4 %collective-permute-done.12 = bf16[144,128]{1,0:T(8,128)(2,1)S(1)} collective-permute-done((bf16[144,128]{1,0:T(8,128)(2,1)S(1)}, bf16[144,128]{1,0:T(8,128)(2,1)S(1)}, u32[]{:S(2)}, u32[]{:S(2)}) %collective-permute-start.12) | collective-permute-done | bytes 36896 | tf_op jit(solution)/shard_map/ppermute | solution.py:501
  64.1 1.6 %collective-permute-start.13 = (bf16[144,128]{1,0:T(8,128)(2,1)S(1)}, bf16[144,128]{1,0:T(8,128)(2,1)S(1)}, u32[]{:S(2)}, u32[]{:S(2)}) collective-permute-start(bf16[144,128]{1,0:T(8,128)(2,1)S(1)} %add_convert_fusion.1), channel_id=1, source_target_pairs={{0,2},{1,3},{2,0},{3,1},{4,6},{5,7},{6,4},{7,5},{8,10},{9,11},{10,... | collective-permute-start | bytes 110600 | tf_op jit(solution)/shard_map/ppermute | solution.py:501
  65.7 2.4 %collective-permute-done.13 = bf16[144,128]{1,0:T(8,128)(2,1)S(1)} collective-permute-done((bf16[144,128]{1,0:T(8,128)(2,1)S(1)}, bf16[144,128]{1,0:T(8,128)(2,1)S(1)}, u32[]{:S(2)}, u32[]{:S(2)}) %collective-permute-start.13) | collective-permute-done | bytes 36896 | tf_op jit(solution)/shard_map/ppermute | solution.py:501
  68.1 1.9 %collective-permute-start.14 = (bf16[144,128]{1,0:T(8,128)(2,1)S(1)}, bf16[144,128]{1,0:T(8,128)(2,1)S(1)}, u32[]{:S(2)}, u32[]{:S(2)}) collective-permute-start(bf16[144,128]{1,0:T(8,128)(2,1)S(1)} %add_convert_fusion.payload), channel_id=1, source_target_pairs={{0,4},{1,5},{2,6},{3,7},{4,0},{5,1},{6,2},{7,3},{8,12},{9,13},{10,... | collective-permute-start | bytes 110600 | tf_op jit(solution)/shard_map/ppermute | solution.py:501
  70.1 2.0 %queries.3 = (bf16[10,48,512]{2,1,0:T(8,128)(2,1)S(1)}, bf16[10,48,256]{2,1,0:T(8,128)(2,1)S(1)}) custom-call(bf16[14,48,256]{2,1,0:T(8,128)(2,1)S(1)} %get-tuple-element.25.mixed_in, bf16[2,256,768]{2,1,0:T(8,128)(2,1)S(1)} %get-tuple-element.17.refs_6_.qkv_weight, f32[2,32,768]{2,1,0:T(8,128)S(1)} %get-tuple-element.18.refs_7_.taps, ...), custom_call_target="tpu_custom_call" | custom-call | flops 251658240 | bytes 983040 | tf_op jit(solution)/shard_map/queries/pallas_call | solution.py:634
  73.0 2.7 %last.1 = (bf16[8,32,256]{2,1,0:T(8,128)(2,1)}, f32[4,8,32]{2,1,0:T(8,128)}) custom-call(bf16[10,48,256]{2,1,0:T(8,128)(2,1)S(1)} %get-tuple-element.26.mixed, bf16[10,48,512]{2,1,0:T(8,128)(2,1)S(1)} %get-tuple-element.27.query, bf16[144,128]{1,0:T(8,128)(2,1)S(1)} %add_convert_fusion.payload, bf16[144,128]{1,0:T(8,128)(2,1)S(1)} %collective-permute-done.14.other, ...), custom_call_target="tpu_custom_call" | custom-call | tf_op jit(solution)/shard_map/last/pallas_call | solution.py:688
  (50 shorter events, 5.3 us)
Async XLA Ops:
  0.6 11.2 %copy-start.6 = (bf16[2,256,768]{2,1,0:T(8,128)(2,1)S(1)}, bf16[2,256,768]{2,1,0:T(8,128)(2,1)}, u32[]{:S(2)}) copy-start(bf16[2,256,768]{2,1,0:T(8,128)(2,1)} %qkv.1) | copy-start | bytes 2359300
  1.5 6.5 %collective-permute-start = (bf16[8,8,256]{2,1,0:T(8,128)(2,1)S(1)}, bf16[8,8,256]{2,1,0:T(8,128)(2,1)S(1)}, u32[]{:S(2)}, u32[]{:S(2)}) collective-permute-start(bf16[8,8,256]{2,1,0:T(8,128)(2,1)S(1)} %get-tuple-element.32), channel_id=1, source_target_pairs={{1,2},{2,1},{3,4},{4,3},{5,6},{6,5},{9,10},{10,9},{11,12},{12,11},... | collective-permute-start | bytes 98312 | tf_op jit(solution)/shard_map/ppermute | solution.py:527
  2.2 7.7 %collective-permute-start.1 = (bf16[8,8,256]{2,1,0:T(8,128)(2,1)S(1)}, bf16[8,8,256]{2,1,0:T(8,128)(2,1)S(1)}, u32[]{:S(2)}, u32[]{:S(2)}) collective-permute-start(bf16[8,8,256]{2,1,0:T(8,128)(2,1)S(1)} %get-tuple-element.33), channel_id=1, source_target_pairs={{0,1},{1,0},{2,3},{3,2},{4,5},{5,4},{6,7},{7,6},{8,9},{9,8},{10,11... | collective-permute-start | bytes 98312 | tf_op jit(solution)/shard_map/ppermute | solution.py:527
  10.8 1.0 %copy-start.8 = (f32[2,5,5,768]{3,0,2,1:T(2,128)S(1)}, f32[2,5,5,768]{3,0,2,1:T(2,128)}, u32[]{:S(2)}) copy-start(f32[2,5,5,768]{3,0,2,1:T(2,128)} %param.22) | copy-start | bytes 460804
  10.8 1.0 %copy-start.9 = (bf16[3,3,4,256]{3,2,1,0:T(4,128)(2,1)S(1)}, bf16[3,3,4,256]{3,2,1,0:T(4,128)(2,1)}, u32[]{:S(2)}) copy-start(bf16[3,3,4,256]{3,2,1,0:T(4,128)(2,1)} %head.1) | copy-start | bytes 55300
  10.9 2.9 %collective-permute-start.2 = (bf16[7,48,256]{2,1,0:T(8,128)(2,1)S(1)}, bf16[7,48,256]{2,1,0:T(8,128)(2,1)S(1)}, u32[]{:S(2)}, u32[]{:S(2)}) collective-permute-start(bf16[7,48,256]{2,1,0:T(8,128)(2,1)S(1)} %get-tuple-element.31), channel_id=1, source_target_pairs={{0,8},{8,0},{16,24},{24,16},{1,9},{9,1},{17,25},{25,17},{2,10},{10... | collective-permute-start | bytes 516104 | tf_op jit(solution)/shard_map/ppermute | solution.py:527
  11.0 2.9 %collective-permute-start.3 = (bf16[7,48,256]{2,1,0:T(8,128)(2,1)S(1)}, bf16[7,48,256]{2,1,0:T(8,128)(2,1)S(1)}, u32[]{:S(2)}, u32[]{:S(2)}) collective-permute-start(bf16[7,48,256]{2,1,0:T(8,128)(2,1)S(1)} %get-tuple-element.30), channel_id=1, source_target_pairs={{8,16},{16,8},{9,17},{17,9},{10,18},{18,10},{11,19},{19,11},{12,20... | collective-permute-start | bytes 516104 | tf_op jit(solution)/shard_map/ppermute | solution.py:527
  11.8 2.0 %copy-start = (bf16[2,256,1024]{2,1,0:T(8,128)(2,1)S(1)}, bf16[2,256,1024]{2,1,0:T(8,128)(2,1)}, u32[]{:S(2)}) copy-start(bf16[2,256,1024]{2,1,0:T(8,128)(2,1)} %refs_0_.3) | copy-start | bytes 3145732
  11.9 2.0 %copy-start.1 = (bf16[2,1024,256]{2,1,0:T(8,128)(2,1)S(1)}, bf16[2,1024,256]{2,1,0:T(8,128)(2,1)}, u32[]{:S(2)}) copy-start(bf16[2,1024,256]{2,1,0:T(8,128)(2,1)} %refs_4_.3) | copy-start | bytes 3145732
  11.9 2.0 %copy-start.3 = (f32[2,3,3,1024]{3,0,2,1:T(2,128)S(1)}, f32[2,3,3,1024]{3,0,2,1:T(2,128)}, u32[]{:S(2)}) copy-start(f32[2,3,3,1024]{3,0,2,1:T(2,128)} %param.17) | copy-start | bytes 221188
  11.9 2.0 %copy-start.5 = (f32[2,1024]{1,0:T(2,128)S(1)}, f32[2,1024]{1,0:T(2,128)}, u32[]{:S(2)}) copy-start(f32[2,1024]{1,0:T(2,128)} %refs_3_.3) | copy-start | bytes 24580
  23.2 5.4 %collective-permute-start.6 = (bf16[144,128]{1,0:T(8,128)(2,1)S(1)}, bf16[144,128]{1,0:T(8,128)(2,1)S(1)}, u32[]{:S(2)}, u32[]{:S(2)}) collective-permute-start(bf16[144,128]{1,0:T(8,128)(2,1)S(1)} %get-tuple-element.23), channel_id=1, source_target_pairs={{0,24},{8,16},{16,8},{24,0},{1,25},{9,17},{17,9},{25,1},{2,26},{10... | collective-permute-start | bytes 110600 | tf_op jit(solution)/shard_map/ppermute | solution.py:501
  24.8 6.3 %collective-permute-start.5 = (bf16[144,128]{1,0:T(8,128)(2,1)S(1)}, bf16[144,128]{1,0:T(8,128)(2,1)S(1)}, u32[]{:S(2)}, u32[]{:S(2)}) collective-permute-start(bf16[144,128]{1,0:T(8,128)(2,1)S(1)} %get-tuple-element.23), channel_id=1, source_target_pairs={{0,16},{8,24},{16,0},{24,8},{1,17},{9,25},{17,1},{25,9},{2,18},{10... | collective-permute-start | bytes 110600 | tf_op jit(solution)/shard_map/ppermute | solution.py:501
  28.6 2.5 %collective-permute-start.4 = (bf16[144,128]{1,0:T(8,128)(2,1)S(1)}, bf16[144,128]{1,0:T(8,128)(2,1)S(1)}, u32[]{:S(2)}, u32[]{:S(2)}) collective-permute-start(bf16[144,128]{1,0:T(8,128)(2,1)S(1)} %get-tuple-element.23), channel_id=1, source_target_pairs={{0,8},{8,0},{16,24},{24,16},{1,9},{9,1},{17,25},{25,17},{2,10},{10... | collective-permute-start | bytes 110600 | tf_op jit(solution)/shard_map/ppermute | solution.py:501
  31.1 4.0 %collective-permute-start.7 = (bf16[144,128]{1,0:T(8,128)(2,1)S(1)}, bf16[144,128]{1,0:T(8,128)(2,1)S(1)}, u32[]{:S(2)}, u32[]{:S(2)}) collective-permute-start(bf16[144,128]{1,0:T(8,128)(2,1)S(1)} %add_convert_fusion.6), channel_id=1, source_target_pairs={{0,1},{1,0},{2,3},{3,2},{4,5},{5,4},{6,7},{7,6},{8,9},{9,8},{10,11... | collective-permute-start | bytes 110600 | tf_op jit(solution)/shard_map/ppermute | solution.py:501
  35.2 4.0 %collective-permute-start.8 = (bf16[144,128]{1,0:T(8,128)(2,1)S(1)}, bf16[144,128]{1,0:T(8,128)(2,1)S(1)}, u32[]{:S(2)}, u32[]{:S(2)}) collective-permute-start(bf16[144,128]{1,0:T(8,128)(2,1)S(1)} %add_convert_fusion.5), channel_id=1, source_target_pairs={{0,2},{1,3},{2,0},{3,1},{4,6},{5,7},{6,4},{7,5},{8,10},{9,11},{10,... | collective-permute-start | bytes 110600 | tf_op jit(solution)/shard_map/ppermute | solution.py:501
  39.2 6.1 %collective-permute-start.9 = (bf16[144,128]{1,0:T(8,128)(2,1)S(1)}, bf16[144,128]{1,0:T(8,128)(2,1)S(1)}, u32[]{:S(2)}, u32[]{:S(2)}) collective-permute-start(bf16[144,128]{1,0:T(8,128)(2,1)S(1)} %add_convert_fusion.4.payload), channel_id=1, source_target_pairs={{0,4},{1,5},{2,6},{3,7},{4,0},{5,1},{6,2},{7,3},{8,12},{9,13},{10,... | collective-permute-start | bytes 110600 | tf_op jit(solution)/shard_map/ppermute | solution.py:501
  42.2 3.1 %copy-start.2 = (bf16[2,512,256]{2,1,0:T(8,128)(2,1)S(1)}, bf16[2,512,256]{2,1,0:T(8,128)(2,1)}, u32[]{:S(2)}) copy-start(bf16[2,512,256]{2,1,0:T(8,128)(2,1)} %out_weight.3) | copy-start | bytes 1572868
  54.7 1.3 %collective-permute-start.10 = (bf16[144,128]{1,0:T(8,128)(2,1)S(1)}, bf16[144,128]{1,0:T(8,128)(2,1)S(1)}, u32[]{:S(2)}, u32[]{:S(2)}) collective-permute-start(bf16[144,128]{1,0:T(8,128)(2,1)S(1)} %get-tuple-element.28), channel_id=1, source_target_pairs={{0,8},{8,0},{16,24},{24,16},{1,9},{9,1},{17,25},{25,17},{2,10},{10... | collective-permute-start | bytes 110600 | tf_op jit(solution)/shard_map/ppermute | solution.py:501
  56.0 4.0 %collective-permute-start.11 = (bf16[144,128]{1,0:T(8,128)(2,1)S(1)}, bf16[144,128]{1,0:T(8,128)(2,1)S(1)}, u32[]{:S(2)}, u32[]{:S(2)}) collective-permute-start(bf16[144,128]{1,0:T(8,128)(2,1)S(1)} %add_convert_fusion.3), channel_id=1, source_target_pairs={{0,16},{8,24},{16,0},{24,8},{1,17},{9,25},{17,1},{25,9},{2,18},{10... | collective-permute-start | bytes 110600 | tf_op jit(solution)/shard_map/ppermute | solution.py:501
  60.0 4.0 %collective-permute-start.12 = (bf16[144,128]{1,0:T(8,128)(2,1)S(1)}, bf16[144,128]{1,0:T(8,128)(2,1)S(1)}, u32[]{:S(2)}, u32[]{:S(2)}) collective-permute-start(bf16[144,128]{1,0:T(8,128)(2,1)S(1)} %add_convert_fusion.2), channel_id=1, source_target_pairs={{0,1},{1,0},{2,3},{3,2},{4,5},{5,4},{6,7},{7,6},{8,9},{9,8},{10,11... | collective-permute-start | bytes 110600 | tf_op jit(solution)/shard_map/ppermute | solution.py:501
  64.1 4.0 %collective-permute-start.13 = (bf16[144,128]{1,0:T(8,128)(2,1)S(1)}, bf16[144,128]{1,0:T(8,128)(2,1)S(1)}, u32[]{:S(2)}, u32[]{:S(2)}) collective-permute-start(bf16[144,128]{1,0:T(8,128)(2,1)S(1)} %add_convert_fusion.1), channel_id=1, source_target_pairs={{0,2},{1,3},{2,0},{3,1},{4,6},{5,7},{6,4},{7,5},{8,10},{9,11},{10,... | collective-permute-start | bytes 110600 | tf_op jit(solution)/shard_map/ppermute | solution.py:501
  68.1 1.9 %copy-start.12 = (f32[4]{0:T(128)S(1)}, f32[4]{0:T(128)}, u32[]{:S(2)}) copy-start(f32[4]{0:T(128)} %param.27) | copy-start | bytes 52
  68.1 4.9 %collective-permute-start.14 = (bf16[144,128]{1,0:T(8,128)(2,1)S(1)}, bf16[144,128]{1,0:T(8,128)(2,1)S(1)}, u32[]{:S(2)}, u32[]{:S(2)}) collective-permute-start(bf16[144,128]{1,0:T(8,128)(2,1)S(1)} %add_convert_fusion.payload), channel_id=1, source_target_pairs={{0,4},{1,5},{2,6},{3,7},{4,0},{5,1},{6,2},{7,3},{8,12},{9,13},{10,... | collective-permute-start | bytes 110600 | tf_op jit(solution)/shard_map/ppermute | solution.py:501
  (4 other events, 3.6 us)

commit v12 on v11

--- a/solution.py
+++ b/solution.py
@@ -1,4 +1,5 @@
 import functools
+import itertools
 
 import jax
 import jax.numpy as jnp
@@ -473,50 +474,56 @@
     return pl.BlockSpec(memory_space=pltpu.HBM)
 
 
-def digits(size, most):
-    radices = []
+def factors(size):
+    found = []
     while size > 1:
-        radix = next((r for r in range(min(most, size), 1, -1) if size % r == 0), size)
-        radices.append(radix)
-        size //= radix
-    return radices
-
-
-def partner(i, stride, radix, step):
-    digit = (i // stride) % radix
-    other = digit ^ step if radix & (radix - 1) == 0 else (digit + step) % radix
-    return i + (other - digit) * stride
-
-
-def sum_by_permutes(value, most):
-    rounds = []
-    for axis in ("row", "col"):
-        stride = 1
-        for radix in digits(lax.axis_size(axis), most[axis]):
-            rounds.append((axis, stride, radix))
+        found.append(next(p for p in range(2, size + 1) if size % p == 0))
+        size //= found[-1]
+    return found
+
+
+def rounds_of(rows, cols, most):
+    rounds, places = [], most + 1
+    for axis, stride, size in (("row", 2, rows // 2), ("col", 1, cols)):
+        for radix in factors(size):
+            if places * radix > most:
+                rounds.append([])
+                places = 1
+            rounds[-1].append((axis, stride, radix))
+            places *= radix
             stride *= radix
-    for axis, stride, radix in rounds:
-        count = lax.axis_size(axis)
-        others = [
-            lax.ppermute(value, axis, [(i, partner(i, stride, radix, k)) for i in range(count)])
-            for k in range(1, radix)
-        ]
-        if (axis, stride, radix) == rounds[-1] and radix == 2:
-            return value, others[0]
-        total = value.astype(F32)
-        for other in others:
-            total = total + other.astype(F32)
-        value = total.astype(BF16)
-    return value, jnp.zeros_like(value)
-
-
-def digits(size, most):
-    radices = []
-    while size > 1:
-        radix = next((r for r in range(min(most, size), 1, -1) if size % r == 0), size)
-        radices.append(radix)
-        size //= radix
-    return radices
+    return rounds
+
+
+def moved(place, digits, steps):
+    place = dict(place)
+    for (axis, stride, radix), step in zip(digits, steps):
+        digit = (place[axis] // stride) % radix
+        other = digit ^ step if radix == 2 else (digit + step) % radix
+        place[axis] += (other - digit) * stride
+    return place
+
+
+def sum_by_permutes(value):
+    rows, cols = lax.axis_size("row"), lax.axis_size("col")
+    odd = lax.axis_index("row") & 1 == 1
+    value = value.astype(F32) + lax.ppermute(
+        value, "row", [(r, r + 1) for r in range(0, rows, 2)]
+    ).astype(F32)
+    for digits in rounds_of(rows, cols, 4):
+        sent = value.astype(BF16)
+        value = sent.astype(F32)
+        for steps in itertools.product(*(range(radix) for _, _, radix in digits)):
+            if not any(steps):
+                continue
+            pairs = []
+            for r in range(1, rows, 2):
+                for c in range(cols):
+                    to = moved({"row": r, "col": c}, digits, steps)
+                    pairs.append((r * cols + c, to["row"] * cols + to["col"]))
+            value = value + lax.ppermute(sent, ("row", "col"), pairs).astype(F32)
+    value = jnp.where(odd, value, 0.0).astype(BF16)
+    return value, lax.ppermute(value, "row", [(r + 1, r) for r in range(0, rows, 2)])
 
 
 def pair_exchange(value, axis, first):
@@ -669,7 +676,7 @@
         name="first",
     )(wide_rows, row_0, row_1, *weights)
     query, mixed = queries(mixed, 0)
-    payload, other = sum_by_permutes(payload, {"row": 4, "col": 2})
+    payload, other = sum_by_permutes(payload)
 
     second_rows = first_rows - 6
     mixed, payload = pl.pallas_call(
@@ -683,7 +690,7 @@
         name="second",
     )(mixed, query, payload, other, output_weight, output_bias, *weights)
     query, mixed = queries(mixed, 1)
-    payload, other = sum_by_permutes(payload, {"row": 2, "col": 2})
+    payload, other = sum_by_permutes(payload)
 
     return pl.pallas_call(
         functools.partial(last_kernel, tile, head_dim),

time: 76.1 us -> 98.2 us (1.29); the launches traced: 75.9 us -> 96.6 us
  waiting for transfers between devices: 17.6 us -> 37.4 us
  starting transfers between devices: 26.8 us -> 27.8 us
    ppermute x11 -> x16, waiting for transfers between devices: 15.7 us -> 35.5 us  [the longest x2 33.7 us: sum_by_permutes(): lax.ppermute(value, 'row', [(r + 1, r) for r in range(0, rows, 2)])]
    ppermute x11 -> x16, starting transfers between devices: 19.4 us -> 20.5 us  [the longest x2 9.9 us: sum_by_permutes(): lax.ppermute(value, 'row', [(r, r + 1) for r in range(0, rows, 2)])]
  transfers between devices with their start and end apart: 15 -> 20, of which waited for: 9 -> 5; matrix products, arithmetic and copies ran while one was open for 0% -> 0% of each run, Pallas kernels for 9% -> 7%
where the time goes in v12:
time: 98.2 us; the launch traced here: 96.6 us
  waiting for transfers between devices  37.4 us (38%)
  starting transfers between devices  27.8 us (28%)
  Pallas kernels  27.6 us (28%)
  local copies, waits for them, and re-layouts  1.71 us (2%)
  between operations  1.16 us (1%)
  other arithmetic  1.07 us (1%)
    ppermute x2, waiting for transfers between devices, sum_by_permutes(): lax.ppermute(value, 'row', [(r + 1, r) for r in range(0, rows, 2)])  33.7 us
    ppermute x2, starting transfers between devices, sum_by_permutes(): lax.ppermute(value, 'row', [(r, r + 1) for r in range(0, rows, 2)])  9.9 us
    pallas_call x1, Pallas kernels, local(): pl.pallas_call(functools.partial(second_kernel, tile, head_dim), out_shap...  9.21 us
    pallas_call x1, Pallas kernels, local(): pl.pallas_call(functools.partial(first_kernel, tile, head_dim), out_shape...  8.69 us
    ppermute x12, starting transfers between devices, sum_by_permutes(): value = value + lax.ppermute(sent, ('row', 'col'), pairs).astype(F32)  7.96 us
    ppermute x4, starting transfers between devices, pair_exchange(): return lax.ppermute(value, axis, pairs)  7.32 us
    pallas_call x2, Pallas kernels, queries(): pl.pallas_call(functools.partial(query_kernel, tile, section), out_shape=...  5.05 us
    pallas_call x1, Pallas kernels, local(): pl.pallas_call(functools.partial(last_kernel, tile, head_dim), out_shape=...  2.7 us
  transfers between devices with their start and end apart: 20, of which 5 were waited for; matrix products, arithmetic and copies ran while one was open for 0% of the time, Pallas kernels for 7%

profile of v12, /device:TPU:0, one launch (start us, length us, event | category | flops | bytes accessed | tf_op | source)
XLA Modules:
  0.0 96.6 jit_solution(9240027665873509226)
XLA Ops:
  0.7 0.9 constant_dynamic-slice_fusion.3
  2.2 5.8 %collective-permute-start.1 = (bf16[8,8,256]{2,1,0:T(8,128)(2,1)S(1)}, bf16[8,8,256]{2,1,0:T(8,128)(2,1)S(1)}, u32[]{:S(2)}, u32[]{:S(2)}) collective-permute-start(bf16[8,8,256]{2,1,0:T(8,128)(2,1)S(1)} %get-tuple-element.33), channel_id=1, source_target_pairs={{0,1},{1,0},{2,3},{3,2},{4,5},{5,4},{6,7},{7,6},{8,9},{9,8},{10,11... | collective-permute-start | bytes 98312 | tf_op jit(solution)/shard_map/ppermute | solution.py:534
  8.0 1.9 %collective-permute-done.1 = bf16[8,8,256]{2,1,0:T(8,128)(2,1)S(1)} collective-permute-done((bf16[8,8,256]{2,1,0:T(8,128)(2,1)S(1)}, bf16[8,8,256]{2,1,0:T(8,128)(2,1)S(1)}, u32[]{:S(2)}, u32[]{:S(2)}) %collective-permute-start.1) | collective-permute-done | bytes 32800 | tf_op jit(solution)/shard_map/ppermute | solution.py:534
  9.9 0.9 pad_maximum_fusion.own
  11.0 0.8 collective-permute-start.3
  11.9 1.9 %prepare.1 = (bf16[2,256,768]{2,1,0:T(8,128)(2,1)S(1)}, f32[2,32,768]{2,1,0:T(8,128)S(1)}, bf16[2,3,256,256]{3,2,1,0:T(8,128)(2,1)S(1)}, bf16[3,128,256]{2,1,0:T...) custom-call(bf16[2,256,768]{2,1,0:T(8,128)(2,1)S(1)} %copy-done.6, f32[5,5,2,768]{3,2,1,0:T(2,128)S(1)} %bitcast.5, ...), custom_call_target="tpu_custom_call" | custom-call | flops 2000000000 | bytes 4000000 | tf_op jit(solution)/shard_map/prepare/pallas_call | solution.py:588
  14.5 8.7 %first.1 = (bf16[20,48,256]{2,1,0:T(8,128)(2,1)S(1)}, bf16[144,128]{1,0:T(8,128)(2,1)S(1)}) custom-call(bf16[8,48,256]{2,1,0:T(8,128)(2,1)S(1)} %pad_maximum_fusion.own, bf16[7,48,256]{2,1,0:T(8,128)(2,1)S(1)} %collective-permute-done.2.row_0, bf16[7,48,256]{2,1,0:T(8,128)(2,1)S(1)} %collective-permute-done.3.row_1, bf16[2,256,1024]{2,1,0:T(8,128)(2,1)S(1)} %copy-done, ...), custom_call_target="tpu_custom_call" | custom-call | tf_op jit(solution)/shard_map/first/pallas_call | solution.py:667
  23.2 5.6 %collective-permute-start.4 = (bf16[144,128]{1,0:T(8,128)(2,1)S(1)}, bf16[144,128]{1,0:T(8,128)(2,1)S(1)}, u32[]{:S(2)}, u32[]{:S(2)}) collective-permute-start(bf16[144,128]{1,0:T(8,128)(2,1)S(1)} %get-tuple-element.23), channel_id=1, source_target_pairs={{0,8},{16,24},{1,9},{17,25},{2,10},{18,26},{3,11},{19,27},{4,12},{... | collective-permute-start | bytes 110600 | tf_op jit(solution)/shard_map/ppermute | solution.py:510
  28.8 0.8 collective-permute-done.4
  29.7 0.7 collective-permute-start.7
  30.4 0.7 collective-permute-start.6
  31.0 0.7 collective-permute-start.5
  31.8 0.7 collective-permute-start.10
  32.4 0.7 collective-permute-start.9
  33.8 1.3 %collective-permute-start.11 = (bf16[144,128]{1,0:T(8,128)(2,1)S(1)}, bf16[144,128]{1,0:T(8,128)(2,1)S(1)}, u32[]{:S(2)}, u32[]{:S(2)}) collective-permute-start(bf16[144,128]{1,0:T(8,128)(2,1)S(1)} %select_convert_fusion.1.payload), channel_id=1, source_target_pairs={{8,0},{24,16},{9,1},{25,17},{10,2},{26,18},{11,3},{27,19},{12,4},{... | collective-permute-start | bytes 110600 | tf_op jit(solution)/shard_map/ppermute | solution.py:526
  35.2 3.1 %queries.2 = (bf16[16,48,512]{2,1,0:T(8,128)(2,1)S(1)}, bf16[16,48,256]{2,1,0:T(8,128)(2,1)S(1)}) custom-call(bf16[20,48,256]{2,1,0:T(8,128)(2,1)S(1)} %get-tuple-element.20.mixed_in, bf16[2,256,768]{2,1,0:T(8,128)(2,1)S(1)} %get-tuple-element.17.refs_6_.qkv_weight, f32[2,32,768]{2,1,0:T(8,128)S(1)} %get-tuple-element.18.refs_7_.taps, ...), custom_call_target="tpu_custom_call" | custom-call | flops 402653184 | bytes 1572864 | tf_op jit(solution)/shard_map/queries/pallas_call | solution.py:641
  38.2 17.3 %collective-permute-done.11.other = bf16[144,128]{1,0:T(8,128)(2,1)S(1)} collective-permute-done((bf16[144,128]{1,0:T(8,128)(2,1)S(1)}, bf16[144,128]{1,0:T(8,128)(2,1)S(1)}, u32[]{:S(2)}, u32[]{:S(2)}) %collective-permute-start.11) | collective-permute-done | bytes 36896 | tf_op jit(solution)/shard_map/ppermute | solution.py:526
  55.5 9.2 %second.1 = (bf16[14,48,256]{2,1,0:T(8,128)(2,1)S(1)}, bf16[144,128]{1,0:T(8,128)(2,1)S(1)}) custom-call(bf16[16,48,256]{2,1,0:T(8,128)(2,1)S(1)} %get-tuple-element.21.mixed, bf16[16,48,512]{2,1,0:T(8,128)(2,1)S(1)} %get-tuple-element.22.query, bf16[144,128]{1,0:T(8,128)(2,1)S(1)} %select_convert_fusion.1.payload, ...), custom_call_target="tpu_custom_call" | custom-call | tf_op jit(solution)/shard_map/second/pallas_call | solution.py:682
  64.7 4.3 %collective-permute-start.12 = (bf16[144,128]{1,0:T(8,128)(2,1)S(1)}, bf16[144,128]{1,0:T(8,128)(2,1)S(1)}, u32[]{:S(2)}, u32[]{:S(2)}) collective-permute-start(bf16[144,128]{1,0:T(8,128)(2,1)S(1)} %get-tuple-element.28), channel_id=1, source_target_pairs={{0,8},{16,24},{1,9},{17,25},{2,10},{18,26},{3,11},{19,27},{4,12},{... | collective-permute-start | bytes 110600 | tf_op jit(solution)/shard_map/ppermute | solution.py:510
  69.1 0.8 collective-permute-done.12
  74.1 1.3 %collective-permute-start.19 = (bf16[144,128]{1,0:T(8,128)(2,1)S(1)}, bf16[144,128]{1,0:T(8,128)(2,1)S(1)}, u32[]{:S(2)}, u32[]{:S(2)}) collective-permute-start(bf16[144,128]{1,0:T(8,128)(2,1)S(1)} %select_convert_fusion.payload), channel_id=1, source_target_pairs={{8,0},{24,16},{9,1},{25,17},{10,2},{26,18},{11,3},{27,19},{12,4},{... | collective-permute-start | bytes 110600 | tf_op jit(solution)/shard_map/ppermute | solution.py:526
  75.5 2.0 %queries.3 = (bf16[10,48,512]{2,1,0:T(8,128)(2,1)S(1)}, bf16[10,48,256]{2,1,0:T(8,128)(2,1)S(1)}) custom-call(bf16[14,48,256]{2,1,0:T(8,128)(2,1)S(1)} %get-tuple-element.25.mixed_in, bf16[2,256,768]{2,1,0:T(8,128)(2,1)S(1)} %get-tuple-element.17.refs_6_.qkv_weight, f32[2,32,768]{2,1,0:T(8,128)S(1)} %get-tuple-element.18.refs_7_.taps, ...), custom_call_target="tpu_custom_call" | custom-call | flops 251658240 | bytes 983040 | tf_op jit(solution)/shard_map/queries/pallas_call | solution.py:641
  77.5 16.4 %collective-permute-done.19.other = bf16[144,128]{1,0:T(8,128)(2,1)S(1)} collective-permute-done((bf16[144,128]{1,0:T(8,128)(2,1)S(1)}, bf16[144,128]{1,0:T(8,128)(2,1)S(1)}, u32[]{:S(2)}, u32[]{:S(2)}) %collective-permute-start.19) | collective-permute-done | bytes 36896 | tf_op jit(solution)/shard_map/ppermute | solution.py:526
  93.9 2.7 %last.1 = (bf16[8,32,256]{2,1,0:T(8,128)(2,1)}, f32[4,8,32]{2,1,0:T(8,128)}) custom-call(bf16[10,48,256]{2,1,0:T(8,128)(2,1)S(1)} %get-tuple-element.26.mixed, bf16[10,48,512]{2,1,0:T(8,128)(2,1)S(1)} %get-tuple-element.27.query, bf16[144,128]{1,0:T(8,128)(2,1)S(1)} %select_convert_fusion.payload, bf16[144,128]{1,0:T(8,128)(2,1)S(1)} %collective-permute-done.19.other, ...), custom_call_target="tpu_custom_call" | custom-call | tf_op jit(solution)/shard_map/last/pallas_call | solution.py:695
  (59 shorter events, 6.4 us)
Async XLA Ops:
  0.6 11.2 %copy-start.6 = (bf16[2,256,768]{2,1,0:T(8,128)(2,1)S(1)}, bf16[2,256,768]{2,1,0:T(8,128)(2,1)}, u32[]{:S(2)}) copy-start(bf16[2,256,768]{2,1,0:T(8,128)(2,1)} %qkv.1) | copy-start | bytes 2359300
  1.5 6.5 %collective-permute-start = (bf16[8,8,256]{2,1,0:T(8,128)(2,1)S(1)}, bf16[8,8,256]{2,1,0:T(8,128)(2,1)S(1)}, u32[]{:S(2)}, u32[]{:S(2)}) collective-permute-start(bf16[8,8,256]{2,1,0:T(8,128)(2,1)S(1)} %get-tuple-element.32), channel_id=1, source_target_pairs={{1,2},{2,1},{3,4},{4,3},{5,6},{6,5},{9,10},{10,9},{11,12},{12,11},... | collective-permute-start | bytes 98312 | tf_op jit(solution)/shard_map/ppermute | solution.py:534
  2.2 7.7 %collective-permute-start.1 = (bf16[8,8,256]{2,1,0:T(8,128)(2,1)S(1)}, bf16[8,8,256]{2,1,0:T(8,128)(2,1)S(1)}, u32[]{:S(2)}, u32[]{:S(2)}) collective-permute-start(bf16[8,8,256]{2,1,0:T(8,128)(2,1)S(1)} %get-tuple-element.33), channel_id=1, source_target_pairs={{0,1},{1,0},{2,3},{3,2},{4,5},{5,4},{6,7},{7,6},{8,9},{9,8},{10,11... | collective-permute-start | bytes 98312 | tf_op jit(solution)/shard_map/ppermute | solution.py:534
  10.9 2.9 %collective-permute-start.2 = (bf16[7,48,256]{2,1,0:T(8,128)(2,1)S(1)}, bf16[7,48,256]{2,1,0:T(8,128)(2,1)S(1)}, u32[]{:S(2)}, u32[]{:S(2)}) collective-permute-start(bf16[7,48,256]{2,1,0:T(8,128)(2,1)S(1)} %get-tuple-element.31), channel_id=1, source_target_pairs={{0,8},{8,0},{16,24},{24,16},{1,9},{9,1},{17,25},{25,17},{2,10},{10... | collective-permute-start | bytes 516104 | tf_op jit(solution)/shard_map/ppermute | solution.py:534
  11.0 2.9 %collective-permute-start.3 = (bf16[7,48,256]{2,1,0:T(8,128)(2,1)S(1)}, bf16[7,48,256]{2,1,0:T(8,128)(2,1)S(1)}, u32[]{:S(2)}, u32[]{:S(2)}) collective-permute-start(bf16[7,48,256]{2,1,0:T(8,128)(2,1)S(1)} %get-tuple-element.30), channel_id=1, source_target_pairs={{8,16},{16,8},{9,17},{17,9},{10,18},{18,10},{11,19},{19,11},{12,20... | collective-permute-start | bytes 516104 | tf_op jit(solution)/shard_map/ppermute | solution.py:534
  11.9 2.0 %copy-start = (bf16[2,256,1024]{2,1,0:T(8,128)(2,1)S(1)}, bf16[2,256,1024]{2,1,0:T(8,128)(2,1)}, u32[]{:S(2)}) copy-start(bf16[2,256,1024]{2,1,0:T(8,128)(2,1)} %refs_0_.3) | copy-start | bytes 3145732
  11.9 2.0 %copy-start.1 = (bf16[2,1024,256]{2,1,0:T(8,128)(2,1)S(1)}, bf16[2,1024,256]{2,1,0:T(8,128)(2,1)}, u32[]{:S(2)}) copy-start(bf16[2,1024,256]{2,1,0:T(8,128)(2,1)} %refs_4_.3) | copy-start | bytes 3145732
  23.2 6.4 %collective-permute-start.4 = (bf16[144,128]{1,0:T(8,128)(2,1)S(1)}, bf16[144,128]{1,0:T(8,128)(2,1)S(1)}, u32[]{:S(2)}, u32[]{:S(2)}) collective-permute-start(bf16[144,128]{1,0:T(8,128)(2,1)S(1)} %get-tuple-element.23), channel_id=1, source_target_pairs={{0,8},{16,24},{1,9},{17,25},{2,10},{18,26},{3,11},{19,27},{4,12},{... | collective-permute-start | bytes 110600 | tf_op jit(solution)/shard_map/ppermute | solution.py:510
  29.7 2.0 %collective-permute-start.7 = (bf16[144,128]{1,0:T(8,128)(2,1)S(1)}, bf16[144,128]{1,0:T(8,128)(2,1)S(1)}, u32[]{:S(2)}, u32[]{:S(2)}) collective-permute-start(bf16[144,128]{1,0:T(8,128)(2,1)S(1)} %add_convert_fusion.3), channel_id=1, source_target_pairs={{8,25},{9,24},{10,27},{11,26},{12,29},{13,28},{14,31},{15,30},{24,... | collective-permute-start | bytes 110600 | tf_op jit(solution)/shard_map/ppermute | solution.py:524
  30.4 1.4 %collective-permute-start.6 = (bf16[144,128]{1,0:T(8,128)(2,1)S(1)}, bf16[144,128]{1,0:T(8,128)(2,1)S(1)}, u32[]{:S(2)}, u32[]{:S(2)}) collective-permute-start(bf16[144,128]{1,0:T(8,128)(2,1)S(1)} %add_convert_fusion.3), channel_id=1, source_target_pairs={{8,24},{9,25},{10,26},{11,27},{12,28},{13,29},{14,30},{15,31},{24,... | collective-permute-start | bytes 110600 | tf_op jit(solution)/shard_map/ppermute | solution.py:524
  31.0 0.7 collective-permute-start.5
  31.8 2.0 %collective-permute-start.10 = (bf16[144,128]{1,0:T(8,128)(2,1)S(1)}, bf16[144,128]{1,0:T(8,128)(2,1)S(1)}, u32[]{:S(2)}, u32[]{:S(2)}) collective-permute-start(bf16[144,128]{1,0:T(8,128)(2,1)S(1)} %add_convert_fusion.2), channel_id=1, source_target_pairs={{8,14},{9,15},{10,12},{11,13},{12,10},{13,11},{14,8},{15,9},{24,30... | collective-permute-start | bytes 110600 | tf_op jit(solution)/shard_map/ppermute | solution.py:524
  32.4 1.4 %collective-permute-start.9 = (bf16[144,128]{1,0:T(8,128)(2,1)S(1)}, bf16[144,128]{1,0:T(8,128)(2,1)S(1)}, u32[]{:S(2)}, u32[]{:S(2)}) collective-permute-start(bf16[144,128]{1,0:T(8,128)(2,1)S(1)} %add_convert_fusion.2), channel_id=1, source_target_pairs={{8,10},{9,11},{10,8},{11,9},{12,14},{13,15},{14,12},{15,13},{24,26... | collective-permute-start | bytes 110600 | tf_op jit(solution)/shard_map/ppermute | solution.py:524
  33.1 0.7 collective-permute-start.8
  33.8 21.7 %collective-permute-start.11 = (bf16[144,128]{1,0:T(8,128)(2,1)S(1)}, bf16[144,128]{1,0:T(8,128)(2,1)S(1)}, u32[]{:S(2)}, u32[]{:S(2)}) collective-permute-start(bf16[144,128]{1,0:T(8,128)(2,1)S(1)} %select_convert_fusion.1.payload), channel_id=1, source_target_pairs={{8,0},{24,16},{9,1},{25,17},{10,2},{26,18},{11,3},{27,19},{12,4},{... | collective-permute-start | bytes 110600 | tf_op jit(solution)/shard_map/ppermute | solution.py:526
  35.1 20.4 %copy-start.2 = (bf16[2,512,256]{2,1,0:T(8,128)(2,1)S(1)}, bf16[2,512,256]{2,1,0:T(8,128)(2,1)}, u32[]{:S(2)}) copy-start(bf16[2,512,256]{2,1,0:T(8,128)(2,1)} %out_weight.3) | copy-start | bytes 1572868
  64.7 5.2 %collective-permute-start.12 = (bf16[144,128]{1,0:T(8,128)(2,1)S(1)}, bf16[144,128]{1,0:T(8,128)(2,1)S(1)}, u32[]{:S(2)}, u32[]{:S(2)}) collective-permute-start(bf16[144,128]{1,0:T(8,128)(2,1)S(1)} %get-tuple-element.28), channel_id=1, source_target_pairs={{0,8},{16,24},{1,9},{17,25},{2,10},{18,26},{3,11},{19,27},{4,12},{... | collective-permute-start | bytes 110600 | tf_op jit(solution)/shard_map/ppermute | solution.py:510
  69.9 2.0 %collective-permute-start.15 = (bf16[144,128]{1,0:T(8,128)(2,1)S(1)}, bf16[144,128]{1,0:T(8,128)(2,1)S(1)}, u32[]{:S(2)}, u32[]{:S(2)}) collective-permute-start(bf16[144,128]{1,0:T(8,128)(2,1)S(1)} %add_convert_fusion.1), channel_id=1, source_target_pairs={{8,25},{9,24},{10,27},{11,26},{12,29},{13,28},{14,31},{15,30},{24,... | collective-permute-start | bytes 110600 | tf_op jit(solution)/shard_map/ppermute | solution.py:524
  70.6 1.4 %collective-permute-start.14 = (bf16[144,128]{1,0:T(8,128)(2,1)S(1)}, bf16[144,128]{1,0:T(8,128)(2,1)S(1)}, u32[]{:S(2)}, u32[]{:S(2)}) collective-permute-start(bf16[144,128]{1,0:T(8,128)(2,1)S(1)} %add_convert_fusion.1), channel_id=1, source_target_pairs={{8,24},{9,25},{10,26},{11,27},{12,28},{13,29},{14,30},{15,31},{24,... | collective-permute-start | bytes 110600 | tf_op jit(solution)/shard_map/ppermute | solution.py:524
  71.3 0.7 collective-permute-start.13
  72.0 2.0 %collective-permute-start.18 = (bf16[144,128]{1,0:T(8,128)(2,1)S(1)}, bf16[144,128]{1,0:T(8,128)(2,1)S(1)}, u32[]{:S(2)}, u32[]{:S(2)}) collective-permute-start(bf16[144,128]{1,0:T(8,128)(2,1)S(1)} %add_convert_fusion), channel_id=1, source_target_pairs={{8,14},{9,15},{10,12},{11,13},{12,10},{13,11},{14,8},{15,9},{24,30... | collective-permute-start | bytes 110600 | tf_op jit(solution)/shard_map/ppermute | solution.py:524
  72.7 1.4 %collective-permute-start.17 = (bf16[144,128]{1,0:T(8,128)(2,1)S(1)}, bf16[144,128]{1,0:T(8,128)(2,1)S(1)}, u32[]{:S(2)}, u32[]{:S(2)}) collective-permute-start(bf16[144,128]{1,0:T(8,128)(2,1)S(1)} %add_convert_fusion), channel_id=1, source_target_pairs={{8,10},{9,11},{10,8},{11,9},{12,14},{13,15},{14,12},{15,13},{24,26... | collective-permute-start | bytes 110600 | tf_op jit(solution)/shard_map/ppermute | solution.py:524
  73.4 0.7 collective-permute-start.16
  74.1 19.8 %collective-permute-start.19 = (bf16[144,128]{1,0:T(8,128)(2,1)S(1)}, bf16[144,128]{1,0:T(8,128)(2,1)S(1)}, u32[]{:S(2)}, u32[]{:S(2)}) collective-permute-start(bf16[144,128]{1,0:T(8,128)(2,1)S(1)} %select_convert_fusion.payload), channel_id=1, source_target_pairs={{8,0},{24,16},{9,1},{25,17},{10,2},{26,18},{11,3},{27,19},{12,4},{... | collective-permute-start | bytes 110600 | tf_op jit(solution)/shard_map/ppermute | solution.py:526
  (9 other events, 11.0 us)

commit v13 on v11

--- a/solution.py
+++ b/solution.py
@@ -18,8 +18,8 @@
 BF16 = jnp.bfloat16
 
 
-def six_hard_swish(value):
-    return value * jnp.minimum(jnp.maximum(value + 3.0, 0.0), 6.0)
+def six_hard_swish(value, bound=6.0):
+    return value * jnp.minimum(jnp.maximum(value + 3.0, 0.0), bound)
 
 
 def parted(count, parts):
@@ -60,6 +60,18 @@
     @pl.when(col == lax.axis_size("col") - 1)
     def _():
         ref[:, cols : cols + SIDE, :] = jnp.zeros((rows, SIDE, ref.shape[2]), ref.dtype)
+
+
+def set_bounds(bounds, cols):
+    shape = bounds.shape[1:]
+    column = lax.broadcasted_iota(jnp.int32, shape, 0)
+    row, col = lax.axis_index("row"), lax.axis_index("col")
+    start = jnp.where(col == lax.axis_size("col") - 1, cols, cols + SIDE)
+    stop = jnp.where(col == 0, cols + 2 * SIDE, cols + SIDE)
+    level = jnp.where((column >= start) & (column < stop), 0.0, 6.0)
+    bounds[0] = jnp.where(row == 0, 0.0, level).astype(BF16)
+    bounds[1] = level.astype(BF16)
+    bounds[2] = jnp.where(row == lax.axis_size("row") - 1, 0.0, level).astype(BF16)
 
 
 def flat(value):
@@ -114,7 +126,7 @@
     expand, expand_bias, depth, depth_bias, project = weights[:5]
     mixed_out, payload_out = outs
     (
-        hidden_0, hidden_1, total, mixed, pairs, wide_depth, wide_agg,
+        hidden, spread, bounds, mixed, pairs, wide_depth, wide_agg,
         project_bias, pair_weight, agg, group, sems,
     ) = scratch
     channels = x_ref.shape[2]
@@ -130,61 +142,51 @@
     rows, width, channels = x_ref.shape
     tile_rows, tile_cols = tile
     inner = rows - 2
-    chunk = hidden_0.shape[2]
-    chunks = expand.shape[2] // chunk
+    chunk = bounds.shape[2]
+    chunks = hidden.shape[2] // chunk
+    this = slice(section, section + 1)
     for index in range(9):
         taps = depth[index // 3, index % 3, section : section + 1, :] * (1.0 / 6.0)
         wide_depth[index] = jnp.broadcast_to(taps, (TILE, taps.shape[1])).astype(BF16)
-    total[...] = 6.0 * flat(x_ref[1 : rows - 1]).astype(F32)
-
-    def expand_rows(out, at, first, size):
+    set_bounds(bounds, tile_cols)
+
+    def expand_rows(at, first, size):
         value = jnp.dot(
-            flat(x_ref[first : first + size]), expand[section, :, pl.ds(at, chunk)],
+            flat(x_ref[first : first + size]), expand[section, :, at : at + chunk],
             preferred_element_type=F32,
         )
-        value = (value + expand_bias[section : section + 1, pl.ds(at, chunk)]).astype(BF16)
-        out[first : first + size] = six_hard_swish(value).reshape(size, width, chunk)
-
-    def spread_rows(hidden, at, first, size):
-        spread = []
+        value = (value + expand_bias[this, at : at + chunk]).astype(BF16)
+        for r in range(size):
+            which = 0 if first + r < halo else 2 if first + r >= rows - halo else 1
+            row = value[r * width : (r + 1) * width]
+            hidden[first + r, :, at : at + chunk] = six_hard_swish(row, bounds[which])
+
+    def spread_rows(at, first, size):
         for r in range(first, first + size):
-            lanes = []
-            for lane in range(0, chunk, LANES):
-                here = pl.ds(pl.multiple_of(at + lane, LANES), LANES)
+            for lane in range(at, at + chunk, LANES):
+                here = slice(lane, lane + LANES)
                 value = depthwise_row(
-                    [hidden[r + a, :, lane : lane + LANES] for a in range(3)],
+                    [hidden[r + a, :, here] for a in range(3)],
                     lambda a, b: wide_depth[3 * a + b, :, here], 3, width,
                 )
-                value = (value + depth_bias[section : section + 1, here]).astype(BF16)
-                lanes.append(six_hard_swish(value))
-            spread.append(jnp.concatenate(lanes, axis=1))
-        pixels = slice(first * width, (first + size) * width)
-        total[pixels] += jnp.dot(
-            jnp.concatenate(spread, axis=0), project[section, pl.ds(at, chunk), :],
-            preferred_element_type=F32,
-        )
-
-    def stage(index, current, following):
-        at = pl.multiple_of(index * chunk, chunk)
-        ahead = pl.multiple_of(jnp.minimum(index + 1, chunks - 1) * chunk, chunk)
+                value = (value + depth_bias[this, here]).astype(BF16)
+                spread[r, :, here] = six_hard_swish(value)
+
+    for first, size in parted(rows, PARTS):
+        expand_rows(0, first, size)
+    for at in range(0, chunks * chunk, chunk):
         for (first, size), (from_row, count) in zip(parted(inner, PARTS), parted(rows, PARTS)):
-            expand_rows(following, ahead, from_row, count)
-            spread_rows(current, at, first, size)
-        clear_outside(following, halo, tile_cols)
-
-    for first, size in parted(rows, PARTS):
-        expand_rows(hidden_0, 0, first, size)
-    clear_outside(hidden_0, halo, tile_cols)
-
-    def two_stages(index, carry):
-        stage(2 * index, hidden_0, hidden_1)
-        stage(2 * index + 1, hidden_1, hidden_0)
-        return carry
-
-    lax.fori_loop(0, chunks // 2, two_stages, 0)
+            if at + chunk < chunks * chunk:
+                expand_rows(at + chunk, from_row, count)
+            spread_rows(at, first, size)
     loads[0].wait()
-    value = total[...] * (1.0 / 6.0) + project_bias[section : section + 1, :]
-    mixed[...] = value.astype(BF16).reshape(inner, width, channels)
+    for first, size in parted(inner, PARTS):
+        value = jnp.dot(
+            flat(spread[first : first + size]), project[section], preferred_element_type=F32
+        )
+        value = value * (1.0 / 6.0) + project_bias[this, :]
+        value = value + flat(x_ref[first + 1 : first + 1 + size]).astype(F32)
+        mixed[first : first + size] = value.astype(BF16).reshape(size, width, channels)
     store = pltpu.make_async_copy(mixed, mixed_out, sems.at[4])
     store.start()
     for load in loads[1:]:
@@ -488,11 +490,11 @@
     return i + (other - digit) * stride
 
 
-def sum_by_permutes(value, most):
+def sum_by_permutes(value):
     rounds = []
     for axis in ("row", "col"):
         stride = 1
-        for radix in digits(lax.axis_size(axis), most[axis]):
+        for radix in digits(lax.axis_size(axis), 4):
             rounds.append((axis, stride, radix))
             stride *= radix
     for axis, stride, radix in rounds:
@@ -607,9 +609,9 @@
 
     def front_scratch(count):
         return [
-            pltpu.VMEM((count, width, 256), BF16),
-            pltpu.VMEM((count, width, 256), BF16),
-            pltpu.VMEM(((count - 2) * width, channels), F32),
+            pltpu.VMEM((count, width, expand_weight.shape[2]), BF16),
+            pltpu.VMEM((count - 2, width, expand_weight.shape[2]), BF16),
+            pltpu.VMEM((3, width, 256), BF16),
             pltpu.VMEM((count - 2, width, channels), BF16),
             pltpu.VMEM((rows + 4, width, 2 * channels), BF16),
             pltpu.VMEM((9, TILE, expand_weight.shape[2]), BF16),
@@ -669,7 +671,7 @@
         name="first",
     )(wide_rows, row_0, row_1, *weights)
     query, mixed = queries(mixed, 0)
-    payload, other = sum_by_permutes(payload, {"row": 4, "col": 2})
+    payload, other = sum_by_permutes(payload)
 
     second_rows = first_rows - 6
     mixed, payload = pl.pallas_call(
@@ -683,7 +685,7 @@
         name="second",
     )(mixed, query, payload, other, output_weight, output_bias, *weights)
     query, mixed = queries(mixed, 1)
-    payload, other = sum_by_permutes(payload, {"row": 2, "col": 2})
+    payload, other = sum_by_permutes(payload)
 
     return pl.pallas_call(
         functools.partial(last_kernel, tile, head_dim),

time: 76.1 us -> 74 us (0.972)
  waiting for transfers between devices: 17.6 us -> 13.9 us
  Pallas kernels: 27.7 us -> 29.7 us
    ppermute x11 -> x14, waiting for transfers between devices: 15.7 us -> 12 us  [sum_by_permutes(): lax.ppermute(value, axis, [(i, partner(i, stride, radix, k)) for i in ran...]
    pallas_call x1, Pallas kernels: 8.69 us -> 9.91 us  [local(): pl.pallas_call(functools.partial(first_kernel, tile, head_dim), out_shape...]
    ppermute x11 -> x14, starting transfers between devices: 19.4 us -> 18.9 us  [sum_by_permutes(): lax.ppermute(value, axis, [(i, partner(i, stride, radix, k)) for i in ran...]
  transfers between devices with their start and end apart: 15 -> 18, of which waited for: 9 -> 11; matrix products, arithmetic and copies ran while one was open for 0% -> 0% of each run, Pallas kernels for 9% -> 10%
where the time goes in v13:
time: 74 us; the launch traced here: 73.8 us
  Pallas kernels  29.7 us (40%)
  starting transfers between devices  26.3 us (36%)
  waiting for transfers between devices  13.9 us (19%)
  local copies, waits for them, and re-layouts  1.71 us (2%)
  between operations  1.1 us (1%)
  other arithmetic  1.03 us (1%)
    ppermute x14, starting transfers between devices, sum_by_permutes(): lax.ppermute(value, axis, [(i, partner(i, stride, radix, k)) for i in ran...  18.9 us
    ppermute x14, waiting for transfers between devices, sum_by_permutes(): lax.ppermute(value, axis, [(i, partner(i, stride, radix, k)) for i in ran...  12 us
    pallas_call x1, Pallas kernels, local(): pl.pallas_call(functools.partial(second_kernel, tile, head_dim), out_shap...  9.98 us
    pallas_call x1, Pallas kernels, local(): pl.pallas_call(functools.partial(first_kernel, tile, head_dim), out_shape...  9.91 us
    ppermute x4, starting transfers between devices, pair_exchange(): return lax.ppermute(value, axis, pairs)  7.32 us
    pallas_call x2, Pallas kernels, queries(): pl.pallas_call(functools.partial(query_kernel, tile, section), out_shape=...  5.21 us
    pallas_call x1, Pallas kernels, local(): pl.pallas_call(functools.partial(last_kernel, tile, head_dim), out_shape=...  2.7 us
    pallas_call x1, Pallas kernels, local(): pl.pallas_call(functools.partial(prepare_kernel, head_dim), out_shape=mad...  1.92 us
  transfers between devices with their start and end apart: 18, of which 11 were waited for; matrix products, arithmetic and copies ran while one was open for 0% of the time, Pallas kernels for 10%

profile of v13, /device:TPU:0, one launch (start us, length us, event | category | flops | bytes accessed | tf_op | source)
XLA Modules:
  0.0 73.8 jit_solution(6084884161677392974)
XLA Ops:
  0.7 0.9 %constant_dynamic-slice_fusion.3 = (bf16[8,8,256]{2,1,0:T(8,128)(2,1)S(1)}, bf16[8,8,256]{2,1,0:T(8,128)(2,1)S(1)}) fusion(bf16[8,32,256]{2,1,0:T(8,128)(2,1)} %param.14, s32[]{:T(128)S(6)} %select_n.30, s32[]{:T(128)S(6)} %select_n.31), kind=kLoop, calls=%fused_computation.10 | loop fusion | bytes 131080 | tf_op jit(solution)/shard_map/dynamic_slice | solution.py:558
  2.2 5.8 %collective-permute-start.1 = (bf16[8,8,256]{2,1,0:T(8,128)(2,1)S(1)}, bf16[8,8,256]{2,1,0:T(8,128)(2,1)S(1)}, u32[]{:S(2)}, u32[]{:S(2)}) collective-permute-start(bf16[8,8,256]{2,1,0:T(8,128)(2,1)S(1)} %get-tuple-element.33), channel_id=1, source_target_pairs={{0,1},{1,0},{2,3},{3,2},{4,5},{5,4},{6,7},{7,6},{8,9},{9,8},{10,11... | collective-permute-start | bytes 98312 | tf_op jit(solution)/shard_map/ppermute | solution.py:529
  8.0 1.9 %collective-permute-done.1 = bf16[8,8,256]{2,1,0:T(8,128)(2,1)S(1)} collective-permute-done((bf16[8,8,256]{2,1,0:T(8,128)(2,1)S(1)}, bf16[8,8,256]{2,1,0:T(8,128)(2,1)S(1)}, u32[]{:S(2)}, u32[]{:S(2)}) %collective-permute-start.1) | collective-permute-done | bytes 32800 | tf_op jit(solution)/shard_map/ppermute | solution.py:529
  9.9 0.9 %pad_maximum_fusion.own = bf16[8,48,256]{2,1,0:T(8,128)(2,1)S(1)} fusion(bf16[8,8,256]{2,1,0:T(8,128)(2,1)S(1)} %get-tuple-element.35, bf16[8,8,256]{2,1,0:T(8,128)(2,1)S(1)} %get-tuple-element.34, bf16[8,32,256]{2,1,0:T(8,128)(2,1)} %param.14), kind=kLoop, calls=%fused_computation | loop fusion | flops 589824 | bytes 393216 | tf_op jit(solution)/shard_map/concatenate | solution.py:568
  11.9 1.9 %prepare.1 = (bf16[2,256,768]{2,1,0:T(8,128)(2,1)S(1)}, f32[2,32,768]{2,1,0:T(8,128)S(1)}, bf16[2,3,256,256]{3,2,1,0:T(8,128)(2,1)S(1)}, bf16[3,128,256]{2,1,0:T...) custom-call(bf16[2,256,768]{2,1,0:T(8,128)(2,1)S(1)} %copy-done.6, f32[5,5,2,768]{3,2,1,0:T(2,128)S(1)} %bitcast.5, ...), custom_call_target="tpu_custom_call" | custom-call | flops 2000000000 | bytes 4000000 | tf_op jit(solution)/shard_map/prepare/pallas_call | solution.py:583
  14.5 9.9 %first.1 = (bf16[20,48,256]{2,1,0:T(8,128)(2,1)S(1)}, bf16[144,128]{1,0:T(8,128)(2,1)S(1)}) custom-call(bf16[8,48,256]{2,1,0:T(8,128)(2,1)S(1)} %pad_maximum_fusion.own, bf16[7,48,256]{2,1,0:T(8,128)(2,1)S(1)} %collective-permute-done.2.row_0, bf16[7,48,256]{2,1,0:T(8,128)(2,1)S(1)} %collective-permute-done.3.row_1, bf16[2,256,1024]{2,1,0:T(8,128)(2,1)S(1)} %copy-done, ...), custom_call_target="tpu_custom_call" | custom-call | tf_op jit(solution)/shard_map/first/pallas_call | solution.py:662
  24.4 1.5 %collective-permute-start.6 = (bf16[144,128]{1,0:T(8,128)(2,1)S(1)}, bf16[144,128]{1,0:T(8,128)(2,1)S(1)}, u32[]{:S(2)}, u32[]{:S(2)}) collective-permute-start(bf16[144,128]{1,0:T(8,128)(2,1)S(1)} %get-tuple-element.23), channel_id=1, source_target_pairs={{0,24},{8,16},{16,8},{24,0},{1,25},{9,17},{17,9},{25,1},{2,26},{10... | collective-permute-start | bytes 110600 | tf_op jit(solution)/shard_map/ppermute | solution.py:503
  26.0 3.9 %collective-permute-start.5 = (bf16[144,128]{1,0:T(8,128)(2,1)S(1)}, bf16[144,128]{1,0:T(8,128)(2,1)S(1)}, u32[]{:S(2)}, u32[]{:S(2)}) collective-permute-start(bf16[144,128]{1,0:T(8,128)(2,1)S(1)} %get-tuple-element.23), channel_id=1, source_target_pairs={{0,16},{8,24},{16,0},{24,8},{1,17},{9,25},{17,1},{25,9},{2,18},{10... | collective-permute-start | bytes 110600 | tf_op jit(solution)/shard_map/ppermute | solution.py:503
  29.9 2.5 %collective-permute-done.5 = bf16[144,128]{1,0:T(8,128)(2,1)S(1)} collective-permute-done((bf16[144,128]{1,0:T(8,128)(2,1)S(1)}, bf16[144,128]{1,0:T(8,128)(2,1)S(1)}, u32[]{:S(2)}, u32[]{:S(2)}) %collective-permute-start.5) | collective-permute-done | bytes 36896 | tf_op jit(solution)/shard_map/ppermute | solution.py:503
  32.4 3.1 %collective-permute-start.9 = (bf16[144,128]{1,0:T(8,128)(2,1)S(1)}, bf16[144,128]{1,0:T(8,128)(2,1)S(1)}, u32[]{:S(2)}, u32[]{:S(2)}) collective-permute-start(bf16[144,128]{1,0:T(8,128)(2,1)S(1)} %add_convert_fusion.3), channel_id=1, source_target_pairs={{0,3},{1,2},{2,1},{3,0},{4,7},{5,6},{6,5},{7,4},{8,11},{9,10},{10,... | collective-permute-start | bytes 110600 | tf_op jit(solution)/shard_map/ppermute | solution.py:503
  36.1 1.3 %collective-permute-done.9 = bf16[144,128]{1,0:T(8,128)(2,1)S(1)} collective-permute-done((bf16[144,128]{1,0:T(8,128)(2,1)S(1)}, bf16[144,128]{1,0:T(8,128)(2,1)S(1)}, u32[]{:S(2)}, u32[]{:S(2)}) %collective-permute-start.9) | collective-permute-done | bytes 36896 | tf_op jit(solution)/shard_map/ppermute | solution.py:503
  37.4 2.0 %collective-permute-done.8 = bf16[144,128]{1,0:T(8,128)(2,1)S(1)} collective-permute-done((bf16[144,128]{1,0:T(8,128)(2,1)S(1)}, bf16[144,128]{1,0:T(8,128)(2,1)S(1)}, u32[]{:S(2)}, u32[]{:S(2)}) %collective-permute-start.8) | collective-permute-done | bytes 36896 | tf_op jit(solution)/shard_map/ppermute | solution.py:503
  39.9 2.7 %collective-permute-start.10 = (bf16[144,128]{1,0:T(8,128)(2,1)S(1)}, bf16[144,128]{1,0:T(8,128)(2,1)S(1)}, u32[]{:S(2)}, u32[]{:S(2)}) collective-permute-start(bf16[144,128]{1,0:T(8,128)(2,1)S(1)} %add_convert_fusion.2.payload), channel_id=1, source_target_pairs={{0,4},{1,5},{2,6},{3,7},{4,0},{5,1},{6,2},{7,3},{8,12},{9,13},{10,... | collective-permute-start | bytes 110600 | tf_op jit(solution)/shard_map/ppermute | solution.py:503
  42.5 3.2 %queries.2 = (bf16[16,48,512]{2,1,0:T(8,128)(2,1)S(1)}, bf16[16,48,256]{2,1,0:T(8,128)(2,1)S(1)}) custom-call(bf16[20,48,256]{2,1,0:T(8,128)(2,1)S(1)} %get-tuple-element.20.mixed_in, bf16[2,256,768]{2,1,0:T(8,128)(2,1)S(1)} %get-tuple-element.17.refs_6_.qkv_weight, f32[2,32,768]{2,1,0:T(8,128)S(1)} %get-tuple-element.18.refs_7_.taps, ...), custom_call_target="tpu_custom_call" | custom-call | flops 402653184 | bytes 1572864 | tf_op jit(solution)/shard_map/queries/pallas_call | solution.py:636
  45.8 10.0 %second.1 = (bf16[14,48,256]{2,1,0:T(8,128)(2,1)S(1)}, bf16[144,128]{1,0:T(8,128)(2,1)S(1)}) custom-call(bf16[16,48,256]{2,1,0:T(8,128)(2,1)S(1)} %get-tuple-element.21.mixed, bf16[16,48,512]{2,1,0:T(8,128)(2,1)S(1)} %get-tuple-element.22.query, bf16[144,128]{1,0:T(8,128)(2,1)S(1)} %add_convert_fusion.2.payload, ...), custom_call_target="tpu_custom_call" | custom-call | tf_op jit(solution)/shard_map/second/pallas_call | solution.py:677
  55.9 1.5 %collective-permute-start.12 = (bf16[144,128]{1,0:T(8,128)(2,1)S(1)}, bf16[144,128]{1,0:T(8,128)(2,1)S(1)}, u32[]{:S(2)}, u32[]{:S(2)}) collective-permute-start(bf16[144,128]{1,0:T(8,128)(2,1)S(1)} %get-tuple-element.28), channel_id=1, source_target_pairs={{0,16},{8,24},{16,0},{24,8},{1,17},{9,25},{17,1},{25,9},{2,18},{10... | collective-permute-start | bytes 110600 | tf_op jit(solution)/shard_map/ppermute | solution.py:503
  57.7 1.9 %collective-permute-done.13 = bf16[144,128]{1,0:T(8,128)(2,1)S(1)} collective-permute-done((bf16[144,128]{1,0:T(8,128)(2,1)S(1)}, bf16[144,128]{1,0:T(8,128)(2,1)S(1)}, u32[]{:S(2)}, u32[]{:S(2)}) %collective-permute-start.13) | collective-permute-done | bytes 36896 | tf_op jit(solution)/shard_map/ppermute | solution.py:503
  60.1 1.4 %collective-permute-start.16 = (bf16[144,128]{1,0:T(8,128)(2,1)S(1)}, bf16[144,128]{1,0:T(8,128)(2,1)S(1)}, u32[]{:S(2)}, u32[]{:S(2)}) collective-permute-start(bf16[144,128]{1,0:T(8,128)(2,1)S(1)} %add_convert_fusion.1), channel_id=1, source_target_pairs={{0,3},{1,2},{2,1},{3,0},{4,7},{5,6},{6,5},{7,4},{8,11},{9,10},{10,... | collective-permute-start | bytes 110600 | tf_op jit(solution)/shard_map/ppermute | solution.py:503
  62.0 1.6 %collective-permute-start.14 = (bf16[144,128]{1,0:T(8,128)(2,1)S(1)}, bf16[144,128]{1,0:T(8,128)(2,1)S(1)}, u32[]{:S(2)}, u32[]{:S(2)}) collective-permute-start(bf16[144,128]{1,0:T(8,128)(2,1)S(1)} %add_convert_fusion.1), channel_id=1, source_target_pairs={{0,1},{1,0},{2,3},{3,2},{4,5},{5,4},{6,7},{7,6},{8,9},{9,8},{10,11... | collective-permute-start | bytes 110600 | tf_op jit(solution)/shard_map/ppermute | solution.py:503
  63.6 1.4 %collective-permute-done.16 = bf16[144,128]{1,0:T(8,128)(2,1)S(1)} collective-permute-done((bf16[144,128]{1,0:T(8,128)(2,1)S(1)}, bf16[144,128]{1,0:T(8,128)(2,1)S(1)}, u32[]{:S(2)}, u32[]{:S(2)}) %collective-permute-start.16) | collective-permute-done | bytes 36896 | tf_op jit(solution)/shard_map/ppermute | solution.py:503
  66.0 1.7 %collective-permute-start.17 = (bf16[144,128]{1,0:T(8,128)(2,1)S(1)}, bf16[144,128]{1,0:T(8,128)(2,1)S(1)}, u32[]{:S(2)}, u32[]{:S(2)}) collective-permute-start(bf16[144,128]{1,0:T(8,128)(2,1)S(1)} %add_convert_fusion.payload), channel_id=1, source_target_pairs={{0,4},{1,5},{2,6},{3,7},{4,0},{5,1},{6,2},{7,3},{8,12},{9,13},{10,... | collective-permute-start | bytes 110600 | tf_op jit(solution)/shard_map/ppermute | solution.py:503
  67.8 2.0 %queries.3 = (bf16[10,48,512]{2,1,0:T(8,128)(2,1)S(1)}, bf16[10,48,256]{2,1,0:T(8,128)(2,1)S(1)}) custom-call(bf16[14,48,256]{2,1,0:T(8,128)(2,1)S(1)} %get-tuple-element.25.mixed_in, bf16[2,256,768]{2,1,0:T(8,128)(2,1)S(1)} %get-tuple-element.17.refs_6_.qkv_weight, f32[2,32,768]{2,1,0:T(8,128)S(1)} %get-tuple-element.18.refs_7_.taps, ...), custom_call_target="tpu_custom_call" | custom-call | flops 251658240 | bytes 983040 | tf_op jit(solution)/shard_map/queries/pallas_call | solution.py:636
  69.7 1.1 %collective-permute-done.17.other = bf16[144,128]{1,0:T(8,128)(2,1)S(1)} collective-permute-done((bf16[144,128]{1,0:T(8,128)(2,1)S(1)}, bf16[144,128]{1,0:T(8,128)(2,1)S(1)}, u32[]{:S(2)}, u32[]{:S(2)}) %collective-permute-start.17) | collective-permute-done | bytes 36896 | tf_op jit(solution)/shard_map/ppermute | solution.py:503
  70.9 2.7 %last.1 = (bf16[8,32,256]{2,1,0:T(8,128)(2,1)}, f32[4,8,32]{2,1,0:T(8,128)}) custom-call(bf16[10,48,256]{2,1,0:T(8,128)(2,1)S(1)} %get-tuple-element.26.mixed, bf16[10,48,512]{2,1,0:T(8,128)(2,1)S(1)} %get-tuple-element.27.query, bf16[144,128]{1,0:T(8,128)(2,1)S(1)} %add_convert_fusion.payload, bf16[144,128]{1,0:T(8,128)(2,1)S(1)} %collective-permute-done.17.other, ...), custom_call_target="tpu_custom_call" | custom-call | tf_op jit(solution)/shard_map/last/pallas_call | solution.py:690
  (53 shorter events, 5.8 us)
Async XLA Ops:
  0.6 11.2 %copy-start.6 = (bf16[2,256,768]{2,1,0:T(8,128)(2,1)S(1)}, bf16[2,256,768]{2,1,0:T(8,128)(2,1)}, u32[]{:S(2)}) copy-start(bf16[2,256,768]{2,1,0:T(8,128)(2,1)} %qkv.1) | copy-start | bytes 2359300
  1.5 6.5 %collective-permute-start = (bf16[8,8,256]{2,1,0:T(8,128)(2,1)S(1)}, bf16[8,8,256]{2,1,0:T(8,128)(2,1)S(1)}, u32[]{:S(2)}, u32[]{:S(2)}) collective-permute-start(bf16[8,8,256]{2,1,0:T(8,128)(2,1)S(1)} %get-tuple-element.32), channel_id=1, source_target_pairs={{1,2},{2,1},{3,4},{4,3},{5,6},{6,5},{9,10},{10,9},{11,12},{12,11},... | collective-permute-start | bytes 98312 | tf_op jit(solution)/shard_map/ppermute | solution.py:529
  2.2 7.7 %collective-permute-start.1 = (bf16[8,8,256]{2,1,0:T(8,128)(2,1)S(1)}, bf16[8,8,256]{2,1,0:T(8,128)(2,1)S(1)}, u32[]{:S(2)}, u32[]{:S(2)}) collective-permute-start(bf16[8,8,256]{2,1,0:T(8,128)(2,1)S(1)} %get-tuple-element.33), channel_id=1, source_target_pairs={{0,1},{1,0},{2,3},{3,2},{4,5},{5,4},{6,7},{7,6},{8,9},{9,8},{10,11... | collective-permute-start | bytes 98312 | tf_op jit(solution)/shard_map/ppermute | solution.py:529
  10.9 2.9 %collective-permute-start.2 = (bf16[7,48,256]{2,1,0:T(8,128)(2,1)S(1)}, bf16[7,48,256]{2,1,0:T(8,128)(2,1)S(1)}, u32[]{:S(2)}, u32[]{:S(2)}) collective-permute-start(bf16[7,48,256]{2,1,0:T(8,128)(2,1)S(1)} %get-tuple-element.31), channel_id=1, source_target_pairs={{0,8},{8,0},{16,24},{24,16},{1,9},{9,1},{17,25},{25,17},{2,10},{10... | collective-permute-start | bytes 516104 | tf_op jit(solution)/shard_map/ppermute | solution.py:529
  11.0 2.9 %collective-permute-start.3 = (bf16[7,48,256]{2,1,0:T(8,128)(2,1)S(1)}, bf16[7,48,256]{2,1,0:T(8,128)(2,1)S(1)}, u32[]{:S(2)}, u32[]{:S(2)}) collective-permute-start(bf16[7,48,256]{2,1,0:T(8,128)(2,1)S(1)} %get-tuple-element.30), channel_id=1, source_target_pairs={{8,16},{16,8},{9,17},{17,9},{10,18},{18,10},{11,19},{19,11},{12,20... | collective-permute-start | bytes 516104 | tf_op jit(solution)/shard_map/ppermute | solution.py:529
  11.8 2.0 %copy-start = (bf16[2,256,1024]{2,1,0:T(8,128)(2,1)S(1)}, bf16[2,256,1024]{2,1,0:T(8,128)(2,1)}, u32[]{:S(2)}) copy-start(bf16[2,256,1024]{2,1,0:T(8,128)(2,1)} %refs_0_.3) | copy-start | bytes 3145732
  11.9 2.0 %copy-start.1 = (bf16[2,1024,256]{2,1,0:T(8,128)(2,1)S(1)}, bf16[2,1024,256]{2,1,0:T(8,128)(2,1)}, u32[]{:S(2)}) copy-start(bf16[2,1024,256]{2,1,0:T(8,128)(2,1)} %refs_4_.3) | copy-start | bytes 3145732
  11.9 2.0 %copy-start.3 = (f32[2,3,3,1024]{3,0,2,1:T(2,128)S(1)}, f32[2,3,3,1024]{3,0,2,1:T(2,128)}, u32[]{:S(2)}) copy-start(f32[2,3,3,1024]{3,0,2,1:T(2,128)} %param.17) | copy-start | bytes 221188
  11.9 2.0 %copy-start.5 = (f32[2,1024]{1,0:T(2,128)S(1)}, f32[2,1024]{1,0:T(2,128)}, u32[]{:S(2)}) copy-start(f32[2,1024]{1,0:T(2,128)} %refs_3_.3) | copy-start | bytes 24580
  24.4 5.4 %collective-permute-start.6 = (bf16[144,128]{1,0:T(8,128)(2,1)S(1)}, bf16[144,128]{1,0:T(8,128)(2,1)S(1)}, u32[]{:S(2)}, u32[]{:S(2)}) collective-permute-start(bf16[144,128]{1,0:T(8,128)(2,1)S(1)} %get-tuple-element.23), channel_id=1, source_target_pairs={{0,24},{8,16},{16,8},{24,0},{1,25},{9,17},{17,9},{25,1},{2,26},{10... | collective-permute-start | bytes 110600 | tf_op jit(solution)/shard_map/ppermute | solution.py:503
  26.0 6.4 %collective-permute-start.5 = (bf16[144,128]{1,0:T(8,128)(2,1)S(1)}, bf16[144,128]{1,0:T(8,128)(2,1)S(1)}, u32[]{:S(2)}, u32[]{:S(2)}) collective-permute-start(bf16[144,128]{1,0:T(8,128)(2,1)S(1)} %get-tuple-element.23), channel_id=1, source_target_pairs={{0,16},{8,24},{16,0},{24,8},{1,17},{9,25},{17,1},{25,9},{2,18},{10... | collective-permute-start | bytes 110600 | tf_op jit(solution)/shard_map/ppermute | solution.py:503
  29.9 2.5 %collective-permute-start.4 = (bf16[144,128]{1,0:T(8,128)(2,1)S(1)}, bf16[144,128]{1,0:T(8,128)(2,1)S(1)}, u32[]{:S(2)}, u32[]{:S(2)}) collective-permute-start(bf16[144,128]{1,0:T(8,128)(2,1)S(1)} %get-tuple-element.23), channel_id=1, source_target_pairs={{0,8},{8,0},{16,24},{24,16},{1,9},{9,1},{17,25},{25,17},{2,10},{10... | collective-permute-start | bytes 110600 | tf_op jit(solution)/shard_map/ppermute | solution.py:503
  32.4 5.0 %collective-permute-start.9 = (bf16[144,128]{1,0:T(8,128)(2,1)S(1)}, bf16[144,128]{1,0:T(8,128)(2,1)S(1)}, u32[]{:S(2)}, u32[]{:S(2)}) collective-permute-start(bf16[144,128]{1,0:T(8,128)(2,1)S(1)} %add_convert_fusion.3), channel_id=1, source_target_pairs={{0,3},{1,2},{2,1},{3,0},{4,7},{5,6},{6,5},{7,4},{8,11},{9,10},{10,... | collective-permute-start | bytes 110600 | tf_op jit(solution)/shard_map/ppermute | solution.py:503
  35.5 4.0 %collective-permute-start.8 = (bf16[144,128]{1,0:T(8,128)(2,1)S(1)}, bf16[144,128]{1,0:T(8,128)(2,1)S(1)}, u32[]{:S(2)}, u32[]{:S(2)}) collective-permute-start(bf16[144,128]{1,0:T(8,128)(2,1)S(1)} %add_convert_fusion.3), channel_id=1, source_target_pairs={{0,2},{1,3},{2,0},{3,1},{4,6},{5,7},{6,4},{7,5},{8,10},{9,11},{10,... | collective-permute-start | bytes 110600 | tf_op jit(solution)/shard_map/ppermute | solution.py:503
  35.9 4.0 %collective-permute-start.7 = (bf16[144,128]{1,0:T(8,128)(2,1)S(1)}, bf16[144,128]{1,0:T(8,128)(2,1)S(1)}, u32[]{:S(2)}, u32[]{:S(2)}) collective-permute-start(bf16[144,128]{1,0:T(8,128)(2,1)S(1)} %add_convert_fusion.3), channel_id=1, source_target_pairs={{0,1},{1,0},{2,3},{3,2},{4,5},{5,4},{6,7},{7,6},{8,9},{9,8},{10,11... | collective-permute-start | bytes 110600 | tf_op jit(solution)/shard_map/ppermute | solution.py:503
  39.9 5.9 %collective-permute-start.10 = (bf16[144,128]{1,0:T(8,128)(2,1)S(1)}, bf16[144,128]{1,0:T(8,128)(2,1)S(1)}, u32[]{:S(2)}, u32[]{:S(2)}) collective-permute-start(bf16[144,128]{1,0:T(8,128)(2,1)S(1)} %add_convert_fusion.2.payload), channel_id=1, source_target_pairs={{0,4},{1,5},{2,6},{3,7},{4,0},{5,1},{6,2},{7,3},{8,12},{9,13},{10,... | collective-permute-start | bytes 110600 | tf_op jit(solution)/shard_map/ppermute | solution.py:503
  42.5 3.3 %copy-start.2 = (bf16[2,512,256]{2,1,0:T(8,128)(2,1)S(1)}, bf16[2,512,256]{2,1,0:T(8,128)(2,1)}, u32[]{:S(2)}) copy-start(bf16[2,512,256]{2,1,0:T(8,128)(2,1)} %out_weight.3) | copy-start | bytes 1572868
  55.8 3.8 %collective-permute-start.13 = (bf16[144,128]{1,0:T(8,128)(2,1)S(1)}, bf16[144,128]{1,0:T(8,128)(2,1)S(1)}, u32[]{:S(2)}, u32[]{:S(2)}) collective-permute-start(bf16[144,128]{1,0:T(8,128)(2,1)S(1)} %get-tuple-element.28), channel_id=1, source_target_pairs={{0,24},{8,16},{16,8},{24,0},{1,25},{9,17},{17,9},{25,1},{2,26},{10... | collective-permute-start | bytes 110600 | tf_op jit(solution)/shard_map/ppermute | solution.py:503
  55.9 4.2 %collective-permute-start.12 = (bf16[144,128]{1,0:T(8,128)(2,1)S(1)}, bf16[144,128]{1,0:T(8,128)(2,1)S(1)}, u32[]{:S(2)}, u32[]{:S(2)}) collective-permute-start(bf16[144,128]{1,0:T(8,128)(2,1)S(1)} %get-tuple-element.28), channel_id=1, source_target_pairs={{0,16},{8,24},{16,0},{24,8},{1,17},{9,25},{17,1},{25,9},{2,18},{10... | collective-permute-start | bytes 110600 | tf_op jit(solution)/shard_map/ppermute | solution.py:503
  57.4 2.6 %collective-permute-start.11 = (bf16[144,128]{1,0:T(8,128)(2,1)S(1)}, bf16[144,128]{1,0:T(8,128)(2,1)S(1)}, u32[]{:S(2)}, u32[]{:S(2)}) collective-permute-start(bf16[144,128]{1,0:T(8,128)(2,1)S(1)} %get-tuple-element.28), channel_id=1, source_target_pairs={{0,8},{8,0},{16,24},{24,16},{1,9},{9,1},{17,25},{25,17},{2,10},{10... | collective-permute-start | bytes 110600 | tf_op jit(solution)/shard_map/ppermute | solution.py:503
  60.1 5.0 %collective-permute-start.16 = (bf16[144,128]{1,0:T(8,128)(2,1)S(1)}, bf16[144,128]{1,0:T(8,128)(2,1)S(1)}, u32[]{:S(2)}, u32[]{:S(2)}) collective-permute-start(bf16[144,128]{1,0:T(8,128)(2,1)S(1)} %add_convert_fusion.1), channel_id=1, source_target_pairs={{0,3},{1,2},{2,1},{3,0},{4,7},{5,6},{6,5},{7,4},{8,11},{9,10},{10,... | collective-permute-start | bytes 110600 | tf_op jit(solution)/shard_map/ppermute | solution.py:503
  61.5 4.0 %collective-permute-start.15 = (bf16[144,128]{1,0:T(8,128)(2,1)S(1)}, bf16[144,128]{1,0:T(8,128)(2,1)S(1)}, u32[]{:S(2)}, u32[]{:S(2)}) collective-permute-start(bf16[144,128]{1,0:T(8,128)(2,1)S(1)} %add_convert_fusion.1), channel_id=1, source_target_pairs={{0,2},{1,3},{2,0},{3,1},{4,6},{5,7},{6,4},{7,5},{8,10},{9,11},{10,... | collective-permute-start | bytes 110600 | tf_op jit(solution)/shard_map/ppermute | solution.py:503
  62.0 4.0 %collective-permute-start.14 = (bf16[144,128]{1,0:T(8,128)(2,1)S(1)}, bf16[144,128]{1,0:T(8,128)(2,1)S(1)}, u32[]{:S(2)}, u32[]{:S(2)}) collective-permute-start(bf16[144,128]{1,0:T(8,128)(2,1)S(1)} %add_convert_fusion.1), channel_id=1, source_target_pairs={{0,1},{1,0},{2,3},{3,2},{4,5},{5,4},{6,7},{7,6},{8,9},{9,8},{10,11... | collective-permute-start | bytes 110600 | tf_op jit(solution)/shard_map/ppermute | solution.py:503
  66.0 4.9 %collective-permute-start.17 = (bf16[144,128]{1,0:T(8,128)(2,1)S(1)}, bf16[144,128]{1,0:T(8,128)(2,1)S(1)}, u32[]{:S(2)}, u32[]{:S(2)}) collective-permute-start(bf16[144,128]{1,0:T(8,128)(2,1)S(1)} %add_convert_fusion.payload), channel_id=1, source_target_pairs={{0,4},{1,5},{2,6},{3,7},{4,0},{5,1},{6,2},{7,3},{8,12},{9,13},{10,... | collective-permute-start | bytes 110600 | tf_op jit(solution)/shard_map/ppermute | solution.py:503
  (7 other events, 7.4 us)

commit v14 on v13

--- a/solution.py
+++ b/solution.py
@@ -20,11 +20,6 @@
 
 def six_hard_swish(value, bound=6.0):
     return value * jnp.minimum(jnp.maximum(value + 3.0, 0.0), bound)
-
-
-def parted(count, parts):
-    cuts = [count * k // parts for k in range(parts + 1)]
-    return [(a, b - a) for a, b in zip(cuts, cuts[1:]) if b > a]
 
 
 def group_size(count, most):
@@ -99,18 +94,19 @@
     return total
 
 
-def spread_taps(agg, wide_agg):
+def spread_taps(agg, wide_agg, kind):
+    channels = wide_agg.shape[3]
     for index in range(25):
-        taps = agg[index : index + 1, :]
-        wide_agg[index] = jnp.broadcast_to(taps, (TILE, taps.shape[1])).astype(BF16)
-
-
-def aggregated(source, wide_agg, group, low, first, size, channels):
-    width = source.shape[1]
+        taps = agg[index : index + 1, kind * channels : (kind + 1) * channels]
+        wide_agg[kind, index] = jnp.broadcast_to(taps, (TILE, channels)).astype(BF16)
+
+
+def aggregated(source, wide_agg, group, first, size):
+    width, channels = source.shape[1:]
     scaled = []
     for r in range(size):
         lanes = []
-        for lane in range(low, low + channels, LANES):
+        for lane in range(0, channels, LANES):
             here = slice(lane, lane + LANES)
             value = depthwise_row(
                 [source[first + r + a, :, here] for a in range(5)],
@@ -126,7 +122,7 @@
     expand, expand_bias, depth, depth_bias, project = weights[:5]
     mixed_out, payload_out = outs
     (
-        hidden, spread, bounds, mixed, pairs, wide_depth, wide_agg,
+        hidden_0, hidden_1, spread, bounds, mixed, pairs, grouped, wide_depth, wide_agg,
         project_bias, pair_weight, agg, group, sems,
     ) = scratch
     channels = x_ref.shape[2]
@@ -143,66 +139,107 @@
     tile_rows, tile_cols = tile
     inner = rows - 2
     chunk = bounds.shape[2]
-    chunks = hidden.shape[2] // chunk
+    chunks = spread.shape[0]
     this = slice(section, section + 1)
     for index in range(9):
         taps = depth[index // 3, index % 3, section : section + 1, :] * (1.0 / 6.0)
         wide_depth[index] = jnp.broadcast_to(taps, (TILE, taps.shape[1])).astype(BF16)
     set_bounds(bounds, tile_cols)
 
-    def expand_rows(at, first, size):
+    def expand_rows(hidden, index, first, size):
+        at = pl.ds(pl.multiple_of(index * chunk, chunk), chunk)
         value = jnp.dot(
-            flat(x_ref[first : first + size]), expand[section, :, at : at + chunk],
-            preferred_element_type=F32,
+            flat(x_ref[pl.ds(first, size)]), expand[section, :, at], preferred_element_type=F32
         )
-        value = (value + expand_bias[this, at : at + chunk]).astype(BF16)
+        value = (value + expand_bias[this, at]).astype(BF16)
         for r in range(size):
-            which = 0 if first + r < halo else 2 if first + r >= rows - halo else 1
-            row = value[r * width : (r + 1) * width]
-            hidden[first + r, :, at : at + chunk] = six_hard_swish(row, bounds[which])
-
-    def spread_rows(at, first, size):
-        for r in range(first, first + size):
-            for lane in range(at, at + chunk, LANES):
-                here = slice(lane, lane + LANES)
+            row = first + r
+            which = jnp.where(row < halo, 0, jnp.where(row >= rows - halo, 2, 1))
+            part = value[r * width : (r + 1) * width]
+            hidden[row] = six_hard_swish(part, bounds[which])
+
+    def spread_rows(hidden, index, first, size):
+        for r in range(size):
+            for lane in range(0, chunk, LANES):
+                here = pl.ds(pl.multiple_of(index * chunk + lane, LANES), LANES)
                 value = depthwise_row(
-                    [hidden[r + a, :, here] for a in range(3)],
+                    [hidden[first + r + a, :, lane : lane + LANES] for a in range(3)],
                     lambda a, b: wide_depth[3 * a + b, :, here], 3, width,
                 )
                 value = (value + depth_bias[this, here]).astype(BF16)
-                spread[r, :, here] = six_hard_swish(value)
-
-    for first, size in parted(rows, PARTS):
-        expand_rows(0, first, size)
-    for at in range(0, chunks * chunk, chunk):
-        for (first, size), (from_row, count) in zip(parted(inner, PARTS), parted(rows, PARTS)):
-            if at + chunk < chunks * chunk:
-                expand_rows(at + chunk, from_row, count)
-            spread_rows(at, first, size)
+                spread[index, first + r, :, lane : lane + LANES] = six_hard_swish(value)
+
+    size = inner // PARTS
+    ahead = -(-rows // PARTS)
+
+    def loop(count, body):
+        lax.fori_loop(0, count, lambda index, carry: (body(index), carry)[1], 0)
+
+    def ahead_rows(hidden, index, part):
+        expand_rows(hidden, index, jnp.minimum(part * ahead, rows - ahead), ahead)
+
+    loop(PARTS, lambda part: ahead_rows(hidden_0, 0, part))
+
+    def two_chunks(pair):
+        def even_rows(part):
+            spread_rows(hidden_0, 2 * pair, part * size, size)
+            ahead_rows(hidden_1, 2 * pair + 1, part)
+
+        def odd_rows(part):
+            spread_rows(hidden_1, 2 * pair + 1, part * size, size)
+            ahead_rows(hidden_0, jnp.minimum(2 * pair + 2, chunks - 1), part)
+
+        loop(PARTS, even_rows)
+        loop(PARTS, odd_rows)
+
+    loop(chunks // 2, two_chunks)
     loads[0].wait()
-    for first, size in parted(inner, PARTS):
-        value = jnp.dot(
-            flat(spread[first : first + size]), project[section], preferred_element_type=F32
+    weight = project[section]
+
+    def project_rows(part):
+        here = pl.ds(part * size, size)
+        value = project_bias[this, :] + flat(x_ref[pl.ds(part * size + 1, size)]).astype(F32)
+        lanes = [flat(spread[index, here]) for index in range(chunks)]
+        product = jnp.dot(
+            jnp.concatenate(lanes, axis=1), weight, preferred_element_type=F32
         )
-        value = value * (1.0 / 6.0) + project_bias[this, :]
-        value = value + flat(x_ref[first + 1 : first + 1 + size]).astype(F32)
-        mixed[first : first + size] = value.astype(BF16).reshape(size, width, channels)
+        value = product * (1.0 / 6.0) + value
+        mixed[here] = value.astype(BF16).reshape(size, width, channels)
+
+    loop(PARTS, project_rows)
     store = pltpu.make_async_copy(mixed, mixed_out, sems.at[4])
     store.start()
     for load in loads[1:]:
         load.wait()
-    spread_taps(agg, wide_agg)
+    for kind in range(2):
+        spread_taps(agg, wide_agg, kind)
     around = halo - 1
-    first_pair = around - 2
     count = tile_rows + 4
-    for first, size in parted(count, PARTS - 1):
-        at = first_pair + first
+    size = group_size(count, 6)
+
+    def pair_rows(part):
+        first = part * size
         value = jnp.dot(
-            flat(mixed[at : at + size]), pair_weight[...], preferred_element_type=F32
+            flat(mixed[pl.ds(around - 2 + first, size)]), pair_weight[...],
+            preferred_element_type=F32,
         )
-        pairs[first : first + size] = value.astype(BF16).reshape(size, width, 2 * channels)
-    clear_outside(pairs, 2, tile_cols)
-    size = group_size(tile_rows, 4)
+        value = value.astype(BF16).reshape(size, width, 2 * channels)
+        for kind in range(2):
+            here = slice(kind * channels, (kind + 1) * channels)
+            pairs[kind, pl.ds(first, size)] = value[:, :, here]
+
+    loop(count // size, pair_rows)
+    for kind in range(2):
+        clear_outside(pairs.at[kind], 2, tile_cols)
+    step = group_size(tile_rows, 4)
+    turns = tile_rows // step
+
+    def grouped_rows(index):
+        kind, first = index // turns, index % turns * step
+        value = aggregated(pairs.at[kind], wide_agg.at[kind], group[kind], first, step)
+        grouped[kind, pl.ds(first, step)] = value
+
+    loop(2 * turns, grouped_rows)
 
     def summed(key, value):
         key = jnp.maximum(flat(key[:, 0:tile_cols]), 0.0)
@@ -217,22 +254,8 @@
         return products, jnp.sum(key.astype(F32), axis=0, keepdims=True)
 
     mine = slice(2, 2 + tile_rows)
-    products, sums = summed(
-        pairs[mine, :, 0:channels], pairs[mine, :, channels : 2 * channels]
-    )
-
-    def grouped_rows(index, carry):
-        at = index * size
-        more, sums = summed(
-            aggregated(pairs, wide_agg, group[0], 0, at, size, channels),
-            aggregated(pairs, wide_agg, group[1], channels, at, size, channels),
-        )
-        return [a + b for a, b in zip(carry[0], more)], carry[1] + sums
-
-    more, more_sums = lax.fori_loop(
-        0, tile_rows // size, grouped_rows,
-        ([jnp.zeros((LANES, LANES), F32) for _ in products], jnp.zeros_like(sums)),
-    )
+    products, sums = summed(pairs[0, mine], pairs[1, mine])
+    more, more_sums = summed(grouped[0], grouped[1])
     products = products + more
     sums = jnp.concatenate([sums, more_sums], axis=1)
     same = same_head(head_dim)
@@ -267,18 +290,20 @@
     for load in loads:
         load.wait()
     mixed_out[...] = mixed[2 : rows - 2]
-    spread_taps(agg, wide_agg)
-    for first, size in parted(rows, PARTS):
-        value = jnp.dot(
-            flat(mixed[first : first + size]), weight[...], preferred_element_type=F32
-        )
-        centre[first : first + size] = value.astype(BF16).reshape(size, width, channels)
+    spread_taps(agg, wide_agg, 0)
+
+    def centre_rows(first, size):
+        here = pl.ds(first, size)
+        value = jnp.dot(flat(mixed[here]), weight[...], preferred_element_type=F32)
+        centre[here] = value.astype(BF16).reshape(size, width, channels)
+
+    by_groups(rows, 10, centre_rows)
     clear_outside(centre, (rows - tile[0]) // 2, tile[1])
 
     def query_rows(first, size):
         here = pl.ds(first, size)
         query[here, :, 0:channels] = jnp.maximum(centre[pl.ds(first + 2, size)], 0.0)
-        grouped = aggregated(centre, wide_agg, group[...], 0, first, size, channels)
+        grouped = aggregated(centre, wide_agg.at[0], group[...], first, size)
         query[here, :, channels : 2 * channels] = jnp.maximum(grouped, 0.0)
 
     by_groups(rows - 4, 5, query_rows)
@@ -609,13 +634,15 @@
 
     def front_scratch(count):
         return [
-            pltpu.VMEM((count, width, expand_weight.shape[2]), BF16),
-            pltpu.VMEM((count - 2, width, expand_weight.shape[2]), BF16),
+            pltpu.VMEM((count, width, 256), BF16),
+            pltpu.VMEM((count, width, 256), BF16),
+            pltpu.VMEM((expand_weight.shape[2] // 256, count - 2, width, 256), BF16),
             pltpu.VMEM((3, width, 256), BF16),
             pltpu.VMEM((count - 2, width, channels), BF16),
-            pltpu.VMEM((rows + 4, width, 2 * channels), BF16),
+            pltpu.VMEM((2, rows + 4, width, channels), BF16),
+            pltpu.VMEM((2, rows, width, channels), BF16),
             pltpu.VMEM((9, TILE, expand_weight.shape[2]), BF16),
-            pltpu.VMEM((25, TILE, 2 * channels), BF16),
+            pltpu.VMEM((2, 25, TILE, channels), BF16),
             pltpu.VMEM(project_bias.shape, F32),
             pltpu.VMEM((channels, 2 * channels), BF16),
             pltpu.VMEM((32, 2 * channels), F32),
@@ -648,7 +675,7 @@
                 pltpu.VMEM((channels, channels), BF16),
                 pltpu.VMEM((32, channels), F32),
                 pltpu.VMEM((channels, channels), BF16),
-                pltpu.VMEM((25, TILE, channels), BF16),
+                pltpu.VMEM((1, 25, TILE, channels), BF16),
                 pltpu.SemaphoreType.DMA((4,)),
             ],
             compiler_params=params,

time: 74 us -> 74.4 us (level)
  Pallas kernels: 29.7 us -> 30.5 us
where the time goes in v14:
time: 74.4 us; the launch traced here: 74.2 us
  Pallas kernels  30.5 us (41%)
  starting transfers between devices  26.3 us (35%)
  waiting for transfers between devices  13.8 us (19%)
  local copies, waits for them, and re-layouts  1.71 us (2%)
  other arithmetic  1.03 us (1%)
  between operations  0.94 us (1%)
    ppermute x14, starting transfers between devices, sum_by_permutes(): lax.ppermute(value, axis, [(i, partner(i, stride, radix, k)) for i in ran...  19 us
    ppermute x14, waiting for transfers between devices, sum_by_permutes(): lax.ppermute(value, axis, [(i, partner(i, stride, radix, k)) for i in ran...  11.9 us
    pallas_call x1, Pallas kernels, local(): pl.pallas_call(functools.partial(second_kernel, tile, head_dim), out_shap...  10.4 us
    pallas_call x1, Pallas kernels, local(): pl.pallas_call(functools.partial(first_kernel, tile, head_dim), out_shape...  10 us
    ppermute x4, starting transfers between devices, pair_exchange(): return lax.ppermute(value, axis, pairs)  7.32 us
    pallas_call x2, Pallas kernels, queries(): pl.pallas_call(functools.partial(query_kernel, tile, section), out_shape=...  5.37 us
    pallas_call x1, Pallas kernels, local(): pl.pallas_call(functools.partial(last_kernel, tile, head_dim), out_shape=...  2.7 us
    pallas_call x1, Pallas kernels, local(): pl.pallas_call(functools.partial(prepare_kernel, head_dim), out_shape=mad...  1.92 us
  transfers between devices with their start and end apart: 18, of which 11 were waited for; matrix products, arithmetic and copies ran while one was open for 0% of the time, Pallas kernels for 10%

profile of v14, /device:TPU:0, one launch (start us, length us, event | category | flops | bytes accessed | tf_op | source)
XLA Modules:
  0.0 74.2 jit_solution(11685734082613336882)
XLA Ops:
  0.7 0.9 %constant_dynamic-slice_fusion.3 = (bf16[8,8,256]{2,1,0:T(8,128)(2,1)S(1)}, bf16[8,8,256]{2,1,0:T(8,128)(2,1)S(1)}) fusion(bf16[8,32,256]{2,1,0:T(8,128)(2,1)} %param.14, s32[]{:T(128)S(6)} %select_n.30, s32[]{:T(128)S(6)} %select_n.31), kind=kLoop, calls=%fused_computation.10 | loop fusion | bytes 131080 | tf_op jit(solution)/shard_map/dynamic_slice | solution.py:583
  2.2 5.8 %collective-permute-start.1 = (bf16[8,8,256]{2,1,0:T(8,128)(2,1)S(1)}, bf16[8,8,256]{2,1,0:T(8,128)(2,1)S(1)}, u32[]{:S(2)}, u32[]{:S(2)}) collective-permute-start(bf16[8,8,256]{2,1,0:T(8,128)(2,1)S(1)} %get-tuple-element.33), channel_id=1, source_target_pairs={{0,1},{1,0},{2,3},{3,2},{4,5},{5,4},{6,7},{7,6},{8,9},{9,8},{10,11... | collective-permute-start | bytes 98312 | tf_op jit(solution)/shard_map/ppermute | solution.py:554
  8.0 1.9 %collective-permute-done.1 = bf16[8,8,256]{2,1,0:T(8,128)(2,1)S(1)} collective-permute-done((bf16[8,8,256]{2,1,0:T(8,128)(2,1)S(1)}, bf16[8,8,256]{2,1,0:T(8,128)(2,1)S(1)}, u32[]{:S(2)}, u32[]{:S(2)}) %collective-permute-start.1) | collective-permute-done | bytes 32800 | tf_op jit(solution)/shard_map/ppermute | solution.py:554
  9.9 0.9 %pad_maximum_fusion.own = bf16[8,48,256]{2,1,0:T(8,128)(2,1)S(1)} fusion(bf16[8,8,256]{2,1,0:T(8,128)(2,1)S(1)} %get-tuple-element.35, bf16[8,8,256]{2,1,0:T(8,128)(2,1)S(1)} %get-tuple-element.34, bf16[8,32,256]{2,1,0:T(8,128)(2,1)} %param.14), kind=kLoop, calls=%fused_computation | loop fusion | flops 589824 | bytes 393216 | tf_op jit(solution)/shard_map/concatenate | solution.py:593
  11.9 1.9 %prepare.1 = (bf16[2,256,768]{2,1,0:T(8,128)(2,1)S(1)}, f32[2,32,768]{2,1,0:T(8,128)S(1)}, bf16[2,3,256,256]{3,2,1,0:T(8,128)(2,1)S(1)}, bf16[3,128,256]{2,1,0:T...) custom-call(bf16[2,256,768]{2,1,0:T(8,128)(2,1)S(1)} %copy-done.6, f32[5,5,2,768]{3,2,1,0:T(2,128)S(1)} %bitcast.5, ...), custom_call_target="tpu_custom_call" | custom-call | flops 2000000000 | bytes 4000000 | tf_op jit(solution)/shard_map/prepare/pallas_call | solution.py:608
  14.5 10.0 %first.1 = (bf16[20,48,256]{2,1,0:T(8,128)(2,1)S(1)}, bf16[144,128]{1,0:T(8,128)(2,1)S(1)}) custom-call(bf16[8,48,256]{2,1,0:T(8,128)(2,1)S(1)} %pad_maximum_fusion.own, bf16[7,48,256]{2,1,0:T(8,128)(2,1)S(1)} %collective-permute-done.2.row_0, bf16[7,48,256]{2,1,0:T(8,128)(2,1)S(1)} %collective-permute-done.3.row_1, bf16[2,256,1024]{2,1,0:T(8,128)(2,1)S(1)} %copy-done, ...), custom_call_target="tpu_custom_call" | custom-call | tf_op jit(solution)/shard_map/first/pallas_call | solution.py:689
  24.6 1.5 %collective-permute-start.6 = (bf16[144,128]{1,0:T(8,128)(2,1)S(1)}, bf16[144,128]{1,0:T(8,128)(2,1)S(1)}, u32[]{:S(2)}, u32[]{:S(2)}) collective-permute-start(bf16[144,128]{1,0:T(8,128)(2,1)S(1)} %get-tuple-element.23), channel_id=1, source_target_pairs={{0,24},{8,16},{16,8},{24,0},{1,25},{9,17},{17,9},{25,1},{2,26},{10... | collective-permute-start | bytes 110600 | tf_op jit(solution)/shard_map/ppermute | solution.py:528
  26.1 3.9 %collective-permute-start.5 = (bf16[144,128]{1,0:T(8,128)(2,1)S(1)}, bf16[144,128]{1,0:T(8,128)(2,1)S(1)}, u32[]{:S(2)}, u32[]{:S(2)}) collective-permute-start(bf16[144,128]{1,0:T(8,128)(2,1)S(1)} %get-tuple-element.23), channel_id=1, source_target_pairs={{0,16},{8,24},{16,0},{24,8},{1,17},{9,25},{17,1},{25,9},{2,18},{10... | collective-permute-start | bytes 110600 | tf_op jit(solution)/shard_map/ppermute | solution.py:528
  30.0 2.5 %collective-permute-done.5 = bf16[144,128]{1,0:T(8,128)(2,1)S(1)} collective-permute-done((bf16[144,128]{1,0:T(8,128)(2,1)S(1)}, bf16[144,128]{1,0:T(8,128)(2,1)S(1)}, u32[]{:S(2)}, u32[]{:S(2)}) %collective-permute-start.5) | collective-permute-done | bytes 36896 | tf_op jit(solution)/shard_map/ppermute | solution.py:528
  32.5 3.1 %collective-permute-start.9 = (bf16[144,128]{1,0:T(8,128)(2,1)S(1)}, bf16[144,128]{1,0:T(8,128)(2,1)S(1)}, u32[]{:S(2)}, u32[]{:S(2)}) collective-permute-start(bf16[144,128]{1,0:T(8,128)(2,1)S(1)} %add_convert_fusion.3), channel_id=1, source_target_pairs={{0,3},{1,2},{2,1},{3,0},{4,7},{5,6},{6,5},{7,4},{8,11},{9,10},{10,... | collective-permute-start | bytes 110600 | tf_op jit(solution)/shard_map/ppermute | solution.py:528
  36.2 1.3 %collective-permute-done.9 = bf16[144,128]{1,0:T(8,128)(2,1)S(1)} collective-permute-done((bf16[144,128]{1,0:T(8,128)(2,1)S(1)}, bf16[144,128]{1,0:T(8,128)(2,1)S(1)}, u32[]{:S(2)}, u32[]{:S(2)}) %collective-permute-start.9) | collective-permute-done | bytes 36896 | tf_op jit(solution)/shard_map/ppermute | solution.py:528
  37.5 2.0 %collective-permute-done.8 = bf16[144,128]{1,0:T(8,128)(2,1)S(1)} collective-permute-done((bf16[144,128]{1,0:T(8,128)(2,1)S(1)}, bf16[144,128]{1,0:T(8,128)(2,1)S(1)}, u32[]{:S(2)}, u32[]{:S(2)}) %collective-permute-start.8) | collective-permute-done | bytes 36896 | tf_op jit(solution)/shard_map/ppermute | solution.py:528
  40.0 2.6 %collective-permute-start.10 = (bf16[144,128]{1,0:T(8,128)(2,1)S(1)}, bf16[144,128]{1,0:T(8,128)(2,1)S(1)}, u32[]{:S(2)}, u32[]{:S(2)}) collective-permute-start(bf16[144,128]{1,0:T(8,128)(2,1)S(1)} %add_convert_fusion.2.payload), channel_id=1, source_target_pairs={{0,4},{1,5},{2,6},{3,7},{4,0},{5,1},{6,2},{7,3},{8,12},{9,13},{10,... | collective-permute-start | bytes 110600 | tf_op jit(solution)/shard_map/ppermute | solution.py:528
  42.7 3.2 %queries.2 = (bf16[16,48,512]{2,1,0:T(8,128)(2,1)S(1)}, bf16[16,48,256]{2,1,0:T(8,128)(2,1)S(1)}) custom-call(bf16[20,48,256]{2,1,0:T(8,128)(2,1)S(1)} %get-tuple-element.20.mixed_in, bf16[2,256,768]{2,1,0:T(8,128)(2,1)S(1)} %get-tuple-element.17.refs_6_.qkv_weight, f32[2,32,768]{2,1,0:T(8,128)S(1)} %get-tuple-element.18.refs_7_.taps, ...), custom_call_target="tpu_custom_call" | custom-call | flops 402653184 | bytes 1572864 | tf_op jit(solution)/shard_map/queries/pallas_call | solution.py:663
  45.9 10.4 %second.1 = (bf16[14,48,256]{2,1,0:T(8,128)(2,1)S(1)}, bf16[144,128]{1,0:T(8,128)(2,1)S(1)}) custom-call(bf16[16,48,256]{2,1,0:T(8,128)(2,1)S(1)} %get-tuple-element.21.mixed, bf16[16,48,512]{2,1,0:T(8,128)(2,1)S(1)} %get-tuple-element.22.query, bf16[144,128]{1,0:T(8,128)(2,1)S(1)} %add_convert_fusion.2.payload, ...), custom_call_target="tpu_custom_call" | custom-call | tf_op jit(solution)/shard_map/second/pallas_call | solution.py:704
  56.5 1.5 %collective-permute-start.12 = (bf16[144,128]{1,0:T(8,128)(2,1)S(1)}, bf16[144,128]{1,0:T(8,128)(2,1)S(1)}, u32[]{:S(2)}, u32[]{:S(2)}) collective-permute-start(bf16[144,128]{1,0:T(8,128)(2,1)S(1)} %get-tuple-element.28), channel_id=1, source_target_pairs={{0,16},{8,24},{16,0},{24,8},{1,17},{9,25},{17,1},{25,9},{2,18},{10... | collective-permute-start | bytes 110600 | tf_op jit(solution)/shard_map/ppermute | solution.py:528
  58.3 1.9 %collective-permute-done.13 = bf16[144,128]{1,0:T(8,128)(2,1)S(1)} collective-permute-done((bf16[144,128]{1,0:T(8,128)(2,1)S(1)}, bf16[144,128]{1,0:T(8,128)(2,1)S(1)}, u32[]{:S(2)}, u32[]{:S(2)}) %collective-permute-start.13) | collective-permute-done | bytes 36896 | tf_op jit(solution)/shard_map/ppermute | solution.py:528
  60.7 1.5 %collective-permute-start.16 = (bf16[144,128]{1,0:T(8,128)(2,1)S(1)}, bf16[144,128]{1,0:T(8,128)(2,1)S(1)}, u32[]{:S(2)}, u32[]{:S(2)}) collective-permute-start(bf16[144,128]{1,0:T(8,128)(2,1)S(1)} %add_convert_fusion.1), channel_id=1, source_target_pairs={{0,3},{1,2},{2,1},{3,0},{4,7},{5,6},{6,5},{7,4},{8,11},{9,10},{10,... | collective-permute-start | bytes 110600 | tf_op jit(solution)/shard_map/ppermute | solution.py:528
  62.6 1.6 %collective-permute-start.14 = (bf16[144,128]{1,0:T(8,128)(2,1)S(1)}, bf16[144,128]{1,0:T(8,128)(2,1)S(1)}, u32[]{:S(2)}, u32[]{:S(2)}) collective-permute-start(bf16[144,128]{1,0:T(8,128)(2,1)S(1)} %add_convert_fusion.1), channel_id=1, source_target_pairs={{0,1},{1,0},{2,3},{3,2},{4,5},{5,4},{6,7},{7,6},{8,9},{9,8},{10,11... | collective-permute-start | bytes 110600 | tf_op jit(solution)/shard_map/ppermute | solution.py:528
  64.2 1.4 %collective-permute-done.16 = bf16[144,128]{1,0:T(8,128)(2,1)S(1)} collective-permute-done((bf16[144,128]{1,0:T(8,128)(2,1)S(1)}, bf16[144,128]{1,0:T(8,128)(2,1)S(1)}, u32[]{:S(2)}, u32[]{:S(2)}) %collective-permute-start.16) | collective-permute-done | bytes 36896 | tf_op jit(solution)/shard_map/ppermute | solution.py:528
  66.6 1.7 %collective-permute-start.17 = (bf16[144,128]{1,0:T(8,128)(2,1)S(1)}, bf16[144,128]{1,0:T(8,128)(2,1)S(1)}, u32[]{:S(2)}, u32[]{:S(2)}) collective-permute-start(bf16[144,128]{1,0:T(8,128)(2,1)S(1)} %add_convert_fusion.payload), channel_id=1, source_target_pairs={{0,4},{1,5},{2,6},{3,7},{4,0},{5,1},{6,2},{7,3},{8,12},{9,13},{10,... | collective-permute-start | bytes 110600 | tf_op jit(solution)/shard_map/ppermute | solution.py:528
  68.4 2.2 %queries.3 = (bf16[10,48,512]{2,1,0:T(8,128)(2,1)S(1)}, bf16[10,48,256]{2,1,0:T(8,128)(2,1)S(1)}) custom-call(bf16[14,48,256]{2,1,0:T(8,128)(2,1)S(1)} %get-tuple-element.25.mixed_in, bf16[2,256,768]{2,1,0:T(8,128)(2,1)S(1)} %get-tuple-element.17.refs_6_.qkv_weight, f32[2,32,768]{2,1,0:T(8,128)S(1)} %get-tuple-element.18.refs_7_.taps, ...), custom_call_target="tpu_custom_call" | custom-call | flops 251658240 | bytes 983040 | tf_op jit(solution)/shard_map/queries/pallas_call | solution.py:663
  70.5 1.0 %collective-permute-done.17.other = bf16[144,128]{1,0:T(8,128)(2,1)S(1)} collective-permute-done((bf16[144,128]{1,0:T(8,128)(2,1)S(1)}, bf16[144,128]{1,0:T(8,128)(2,1)S(1)}, u32[]{:S(2)}, u32[]{:S(2)}) %collective-permute-start.17) | collective-permute-done | bytes 36896 | tf_op jit(solution)/shard_map/ppermute | solution.py:528
  71.5 2.7 %last.1 = (bf16[8,32,256]{2,1,0:T(8,128)(2,1)}, f32[4,8,32]{2,1,0:T(8,128)}) custom-call(bf16[10,48,256]{2,1,0:T(8,128)(2,1)S(1)} %get-tuple-element.26.mixed, bf16[10,48,512]{2,1,0:T(8,128)(2,1)S(1)} %get-tuple-element.27.query, bf16[144,128]{1,0:T(8,128)(2,1)S(1)} %add_convert_fusion.payload, bf16[144,128]{1,0:T(8,128)(2,1)S(1)} %collective-permute-done.17.other, ...), custom_call_target="tpu_custom_call" | custom-call | tf_op jit(solution)/shard_map/last/pallas_call | solution.py:717
  (53 shorter events, 5.8 us)
Async XLA Ops:
  0.6 11.2 %copy-start.6 = (bf16[2,256,768]{2,1,0:T(8,128)(2,1)S(1)}, bf16[2,256,768]{2,1,0:T(8,128)(2,1)}, u32[]{:S(2)}) copy-start(bf16[2,256,768]{2,1,0:T(8,128)(2,1)} %qkv.1) | copy-start | bytes 2359300
  1.5 6.5 %collective-permute-start = (bf16[8,8,256]{2,1,0:T(8,128)(2,1)S(1)}, bf16[8,8,256]{2,1,0:T(8,128)(2,1)S(1)}, u32[]{:S(2)}, u32[]{:S(2)}) collective-permute-start(bf16[8,8,256]{2,1,0:T(8,128)(2,1)S(1)} %get-tuple-element.32), channel_id=1, source_target_pairs={{1,2},{2,1},{3,4},{4,3},{5,6},{6,5},{9,10},{10,9},{11,12},{12,11},... | collective-permute-start | bytes 98312 | tf_op jit(solution)/shard_map/ppermute | solution.py:554
  2.2 7.7 %collective-permute-start.1 = (bf16[8,8,256]{2,1,0:T(8,128)(2,1)S(1)}, bf16[8,8,256]{2,1,0:T(8,128)(2,1)S(1)}, u32[]{:S(2)}, u32[]{:S(2)}) collective-permute-start(bf16[8,8,256]{2,1,0:T(8,128)(2,1)S(1)} %get-tuple-element.33), channel_id=1, source_target_pairs={{0,1},{1,0},{2,3},{3,2},{4,5},{5,4},{6,7},{7,6},{8,9},{9,8},{10,11... | collective-permute-start | bytes 98312 | tf_op jit(solution)/shard_map/ppermute | solution.py:554
  10.9 2.9 %collective-permute-start.2 = (bf16[7,48,256]{2,1,0:T(8,128)(2,1)S(1)}, bf16[7,48,256]{2,1,0:T(8,128)(2,1)S(1)}, u32[]{:S(2)}, u32[]{:S(2)}) collective-permute-start(bf16[7,48,256]{2,1,0:T(8,128)(2,1)S(1)} %get-tuple-element.31), channel_id=1, source_target_pairs={{0,8},{8,0},{16,24},{24,16},{1,9},{9,1},{17,25},{25,17},{2,10},{10... | collective-permute-start | bytes 516104 | tf_op jit(solution)/shard_map/ppermute | solution.py:554
  11.0 2.9 %collective-permute-start.3 = (bf16[7,48,256]{2,1,0:T(8,128)(2,1)S(1)}, bf16[7,48,256]{2,1,0:T(8,128)(2,1)S(1)}, u32[]{:S(2)}, u32[]{:S(2)}) collective-permute-start(bf16[7,48,256]{2,1,0:T(8,128)(2,1)S(1)} %get-tuple-element.30), channel_id=1, source_target_pairs={{8,16},{16,8},{9,17},{17,9},{10,18},{18,10},{11,19},{19,11},{12,20... | collective-permute-start | bytes 516104 | tf_op jit(solution)/shard_map/ppermute | solution.py:554
  11.8 2.0 %copy-start = (bf16[2,256,1024]{2,1,0:T(8,128)(2,1)S(1)}, bf16[2,256,1024]{2,1,0:T(8,128)(2,1)}, u32[]{:S(2)}) copy-start(bf16[2,256,1024]{2,1,0:T(8,128)(2,1)} %refs_0_.3) | copy-start | bytes 3145732
  11.9 2.0 %copy-start.1 = (bf16[2,1024,256]{2,1,0:T(8,128)(2,1)S(1)}, bf16[2,1024,256]{2,1,0:T(8,128)(2,1)}, u32[]{:S(2)}) copy-start(bf16[2,1024,256]{2,1,0:T(8,128)(2,1)} %refs_4_.3) | copy-start | bytes 3145732
  11.9 2.0 %copy-start.3 = (f32[2,3,3,1024]{3,0,2,1:T(2,128)S(1)}, f32[2,3,3,1024]{3,0,2,1:T(2,128)}, u32[]{:S(2)}) copy-start(f32[2,3,3,1024]{3,0,2,1:T(2,128)} %param.17) | copy-start | bytes 221188
  11.9 2.0 %copy-start.5 = (f32[2,1024]{1,0:T(2,128)S(1)}, f32[2,1024]{1,0:T(2,128)}, u32[]{:S(2)}) copy-start(f32[2,1024]{1,0:T(2,128)} %refs_3_.3) | copy-start | bytes 24580
  24.6 5.4 %collective-permute-start.6 = (bf16[144,128]{1,0:T(8,128)(2,1)S(1)}, bf16[144,128]{1,0:T(8,128)(2,1)S(1)}, u32[]{:S(2)}, u32[]{:S(2)}) collective-permute-start(bf16[144,128]{1,0:T(8,128)(2,1)S(1)} %get-tuple-element.23), channel_id=1, source_target_pairs={{0,24},{8,16},{16,8},{24,0},{1,25},{9,17},{17,9},{25,1},{2,26},{10... | collective-permute-start | bytes 110600 | tf_op jit(solution)/shard_map/ppermute | solution.py:528
  26.1 6.4 %collective-permute-start.5 = (bf16[144,128]{1,0:T(8,128)(2,1)S(1)}, bf16[144,128]{1,0:T(8,128)(2,1)S(1)}, u32[]{:S(2)}, u32[]{:S(2)}) collective-permute-start(bf16[144,128]{1,0:T(8,128)(2,1)S(1)} %get-tuple-element.23), channel_id=1, source_target_pairs={{0,16},{8,24},{16,0},{24,8},{1,17},{9,25},{17,1},{25,9},{2,18},{10... | collective-permute-start | bytes 110600 | tf_op jit(solution)/shard_map/ppermute | solution.py:528
  30.0 2.5 %collective-permute-start.4 = (bf16[144,128]{1,0:T(8,128)(2,1)S(1)}, bf16[144,128]{1,0:T(8,128)(2,1)S(1)}, u32[]{:S(2)}, u32[]{:S(2)}) collective-permute-start(bf16[144,128]{1,0:T(8,128)(2,1)S(1)} %get-tuple-element.23), channel_id=1, source_target_pairs={{0,8},{8,0},{16,24},{24,16},{1,9},{9,1},{17,25},{25,17},{2,10},{10... | collective-permute-start | bytes 110600 | tf_op jit(solution)/shard_map/ppermute | solution.py:528
  32.5 5.0 %collective-permute-start.9 = (bf16[144,128]{1,0:T(8,128)(2,1)S(1)}, bf16[144,128]{1,0:T(8,128)(2,1)S(1)}, u32[]{:S(2)}, u32[]{:S(2)}) collective-permute-start(bf16[144,128]{1,0:T(8,128)(2,1)S(1)} %add_convert_fusion.3), channel_id=1, source_target_pairs={{0,3},{1,2},{2,1},{3,0},{4,7},{5,6},{6,5},{7,4},{8,11},{9,10},{10,... | collective-permute-start | bytes 110600 | tf_op jit(solution)/shard_map/ppermute | solution.py:528
  35.6 4.0 %collective-permute-start.8 = (bf16[144,128]{1,0:T(8,128)(2,1)S(1)}, bf16[144,128]{1,0:T(8,128)(2,1)S(1)}, u32[]{:S(2)}, u32[]{:S(2)}) collective-permute-start(bf16[144,128]{1,0:T(8,128)(2,1)S(1)} %add_convert_fusion.3), channel_id=1, source_target_pairs={{0,2},{1,3},{2,0},{3,1},{4,6},{5,7},{6,4},{7,5},{8,10},{9,11},{10,... | collective-permute-start | bytes 110600 | tf_op jit(solution)/shard_map/ppermute | solution.py:528
  36.1 4.0 %collective-permute-start.7 = (bf16[144,128]{1,0:T(8,128)(2,1)S(1)}, bf16[144,128]{1,0:T(8,128)(2,1)S(1)}, u32[]{:S(2)}, u32[]{:S(2)}) collective-permute-start(bf16[144,128]{1,0:T(8,128)(2,1)S(1)} %add_convert_fusion.3), channel_id=1, source_target_pairs={{0,1},{1,0},{2,3},{3,2},{4,5},{5,4},{6,7},{7,6},{8,9},{9,8},{10,11... | collective-permute-start | bytes 110600 | tf_op jit(solution)/shard_map/ppermute | solution.py:528
  40.0 5.9 %collective-permute-start.10 = (bf16[144,128]{1,0:T(8,128)(2,1)S(1)}, bf16[144,128]{1,0:T(8,128)(2,1)S(1)}, u32[]{:S(2)}, u32[]{:S(2)}) collective-permute-start(bf16[144,128]{1,0:T(8,128)(2,1)S(1)} %add_convert_fusion.2.payload), channel_id=1, source_target_pairs={{0,4},{1,5},{2,6},{3,7},{4,0},{5,1},{6,2},{7,3},{8,12},{9,13},{10,... | collective-permute-start | bytes 110600 | tf_op jit(solution)/shard_map/ppermute | solution.py:528
  42.7 3.2 %copy-start.2 = (bf16[2,512,256]{2,1,0:T(8,128)(2,1)S(1)}, bf16[2,512,256]{2,1,0:T(8,128)(2,1)}, u32[]{:S(2)}) copy-start(bf16[2,512,256]{2,1,0:T(8,128)(2,1)} %out_weight.3) | copy-start | bytes 1572868
  56.4 3.8 %collective-permute-start.13 = (bf16[144,128]{1,0:T(8,128)(2,1)S(1)}, bf16[144,128]{1,0:T(8,128)(2,1)S(1)}, u32[]{:S(2)}, u32[]{:S(2)}) collective-permute-start(bf16[144,128]{1,0:T(8,128)(2,1)S(1)} %get-tuple-element.28), channel_id=1, source_target_pairs={{0,24},{8,16},{16,8},{24,0},{1,25},{9,17},{17,9},{25,1},{2,26},{10... | collective-permute-start | bytes 110600 | tf_op jit(solution)/shard_map/ppermute | solution.py:528
  56.5 4.2 %collective-permute-start.12 = (bf16[144,128]{1,0:T(8,128)(2,1)S(1)}, bf16[144,128]{1,0:T(8,128)(2,1)S(1)}, u32[]{:S(2)}, u32[]{:S(2)}) collective-permute-start(bf16[144,128]{1,0:T(8,128)(2,1)S(1)} %get-tuple-element.28), channel_id=1, source_target_pairs={{0,16},{8,24},{16,0},{24,8},{1,17},{9,25},{17,1},{25,9},{2,18},{10... | collective-permute-start | bytes 110600 | tf_op jit(solution)/shard_map/ppermute | solution.py:528
  58.0 2.6 %collective-permute-start.11 = (bf16[144,128]{1,0:T(8,128)(2,1)S(1)}, bf16[144,128]{1,0:T(8,128)(2,1)S(1)}, u32[]{:S(2)}, u32[]{:S(2)}) collective-permute-start(bf16[144,128]{1,0:T(8,128)(2,1)S(1)} %get-tuple-element.28), channel_id=1, source_target_pairs={{0,8},{8,0},{16,24},{24,16},{1,9},{9,1},{17,25},{25,17},{2,10},{10... | collective-permute-start | bytes 110600 | tf_op jit(solution)/shard_map/ppermute | solution.py:528
  60.7 5.0 %collective-permute-start.16 = (bf16[144,128]{1,0:T(8,128)(2,1)S(1)}, bf16[144,128]{1,0:T(8,128)(2,1)S(1)}, u32[]{:S(2)}, u32[]{:S(2)}) collective-permute-start(bf16[144,128]{1,0:T(8,128)(2,1)S(1)} %add_convert_fusion.1), channel_id=1, source_target_pairs={{0,3},{1,2},{2,1},{3,0},{4,7},{5,6},{6,5},{7,4},{8,11},{9,10},{10,... | collective-permute-start | bytes 110600 | tf_op jit(solution)/shard_map/ppermute | solution.py:528
  62.1 4.0 %collective-permute-start.15 = (bf16[144,128]{1,0:T(8,128)(2,1)S(1)}, bf16[144,128]{1,0:T(8,128)(2,1)S(1)}, u32[]{:S(2)}, u32[]{:S(2)}) collective-permute-start(bf16[144,128]{1,0:T(8,128)(2,1)S(1)} %add_convert_fusion.1), channel_id=1, source_target_pairs={{0,2},{1,3},{2,0},{3,1},{4,6},{5,7},{6,4},{7,5},{8,10},{9,11},{10,... | collective-permute-start | bytes 110600 | tf_op jit(solution)/shard_map/ppermute | solution.py:528
  62.6 4.0 %collective-permute-start.14 = (bf16[144,128]{1,0:T(8,128)(2,1)S(1)}, bf16[144,128]{1,0:T(8,128)(2,1)S(1)}, u32[]{:S(2)}, u32[]{:S(2)}) collective-permute-start(bf16[144,128]{1,0:T(8,128)(2,1)S(1)} %add_convert_fusion.1), channel_id=1, source_target_pairs={{0,1},{1,0},{2,3},{3,2},{4,5},{5,4},{6,7},{7,6},{8,9},{9,8},{10,11... | collective-permute-start | bytes 110600 | tf_op jit(solution)/shard_map/ppermute | solution.py:528
  66.6 4.9 %collective-permute-start.17 = (bf16[144,128]{1,0:T(8,128)(2,1)S(1)}, bf16[144,128]{1,0:T(8,128)(2,1)S(1)}, u32[]{:S(2)}, u32[]{:S(2)}) collective-permute-start(bf16[144,128]{1,0:T(8,128)(2,1)S(1)} %add_convert_fusion.payload), channel_id=1, source_target_pairs={{0,4},{1,5},{2,6},{3,7},{4,0},{5,1},{6,2},{7,3},{8,12},{9,13},{10,... | collective-permute-start | bytes 110600 | tf_op jit(solution)/shard_map/ppermute | solution.py:528
  (7 other events, 7.4 us)

commit v15 on v11

--- a/solution.py
+++ b/solution.py
@@ -403,15 +403,30 @@
         store.wait()
 
 
-def first_kernel(tile, head_dim, own, row_0, row_1, *refs):
+def first_kernel(
+    tile, head_dim, own, row_0, row_1, col_0, col_1, corner_0, corner_1, *refs
+):
     weights, outs, scratch = refs[:9], refs[9:11], refs[11:]
     x_ref = scratch[0]
     rows, cols = tile
     below = REACH + rows
-    even = lax.axis_index("row") & 1 == 0
-    x_ref[REACH:below] = own[...]
-    x_ref[pl.ds(jnp.where(even, below, 0), REACH)] = row_0[...]
-    x_ref[pl.ds(jnp.where(even, 0, below), REACH)] = row_1[...]
+    even_row = lax.axis_index("row") & 1 == 0
+    even_col = lax.axis_index("col") & 1 == 0
+
+    def sides(part_0, part_1):
+        right = jnp.where(even_col, part_0, part_1)
+        left = jnp.where(even_col, part_1, part_0)
+        return jnp.concatenate([right, left], axis=1)
+
+    x_ref[REACH:below, 0:cols, :] = own[...]
+    x_ref[REACH:below, cols : cols + 2 * SIDE, :] = sides(col_0[...], col_1[...])
+    for row, corner, first in (
+        (row_0, corner_0, jnp.where(even_row, below, 0)),
+        (row_1, corner_1, jnp.where(even_row, 0, below)),
+    ):
+        here = pl.ds(first, REACH)
+        x_ref[here, 0:cols, :] = row[...]
+        x_ref[here, cols : cols + 2 * SIDE, :] = sides(corner[0:REACH], corner[REACH:])
     front(x_ref, weights, outs, scratch[1:], REACH, tile, head_dim, 0)
 
 
@@ -488,11 +503,11 @@
     return i + (other - digit) * stride
 
 
-def sum_by_permutes(value, most):
+def sum_by_permutes(value):
     rounds = []
     for axis in ("row", "col"):
         stride = 1
-        for radix in digits(lax.axis_size(axis), most[axis]):
+        for radix in digits(lax.axis_size(axis), 4):
             rounds.append((axis, stride, radix))
             stride *= radix
     for axis, stride, radix in rounds:
@@ -561,12 +576,15 @@
     low, high = edges(features, 1, SIDE, odd_col)
     col_1 = pair_exchange(high, "col", 1)
     col_0 = pair_exchange(low, "col", 0)
-    right = jnp.where(odd_col == 1, col_1, col_0)
-    left = jnp.where(odd_col == 1, col_0, col_1)
-    wide_rows = jnp.concatenate([features, right, left], axis=1)
-    low, high = edges(wide_rows, 0, REACH, odd_row)
+    low, high = edges(features, 0, REACH, odd_row)
     row_1 = pair_exchange(high, "row", 1)
     row_0 = pair_exchange(low, "row", 0)
+    low, high = (
+        jnp.concatenate(pieces, axis=0)
+        for pieces in zip(edges(col_0, 0, REACH, odd_row), edges(col_1, 0, REACH, odd_row))
+    )
+    corner_1 = pair_exchange(high, "row", 1)
+    corner_0 = pair_exchange(low, "row", 0)
 
     aggregate_depth = aggregate_depth.transpose(1, 2, 0, 3)
     depth_weight = depth_weight.transpose(1, 2, 0, 3)
@@ -661,15 +679,15 @@
         functools.partial(first_kernel, tile, head_dim),
         out_shape=outs_of(first_rows - 2),
         grid=(1,),
-        in_specs=[near()] * 3 + weight_specs,
+        in_specs=[near()] * 7 + weight_specs,
         out_specs=[far(), near()],
         scratch_shapes=[pltpu.VMEM((first_rows, width, channels), BF16)]
         + front_scratch(first_rows),
         compiler_params=params,
         name="first",
-    )(wide_rows, row_0, row_1, *weights)
+    )(features, row_0, row_1, col_0, col_1, corner_0, corner_1, *weights)
     query, mixed = queries(mixed, 0)
-    payload, other = sum_by_permutes(payload, {"row": 4, "col": 2})
+    payload, other = sum_by_permutes(payload)
 
     second_rows = first_rows - 6
     mixed, payload = pl.pallas_call(
@@ -683,7 +701,7 @@
         name="second",
     )(mixed, query, payload, other, output_weight, output_bias, *weights)
     query, mixed = queries(mixed, 1)
-    payload, other = sum_by_permutes(payload, {"row": 2, "col": 2})
+    payload, other = sum_by_permutes(payload)
 
     return pl.pallas_call(
         functools.partial(last_kernel, tile, head_dim),

time: 76.1 us -> 73.6 us (0.967)
  waiting for transfers between devices: 17.6 us -> 13.7 us
  starting transfers between devices: 26.8 us -> 27.9 us
  other arithmetic: 1.04 us -> 0.12 us
  local copies, waits for them, and re-layouts: 1.71 us -> 2.61 us
    ppermute x11 -> x14, waiting for transfers between devices: 15.7 us -> 11.8 us  [sum_by_permutes(): lax.ppermute(value, axis, [(i, partner(i, stride, radix, k)) for i in ran...]
    ppermute x4 -> x6, starting transfers between devices: 7.32 us -> 10.2 us  [pair_exchange(): return lax.ppermute(value, axis, pairs)]
    ppermute x11 -> x14, starting transfers between devices: 19.4 us -> 17.8 us  [sum_by_permutes(): lax.ppermute(value, axis, [(i, partner(i, stride, radix, k)) for i in ran...]
    unnamed x26 -> x28, local copies, waits for them, and re-layouts: 0.72 us -> 1.65 us
    concatenate x1 -> x2, other arithmetic: 0.92 us -> 0.02 us  [local(): jnp.concatenate(pieces, axis=0)]
    ppermute x4 -> x6, waiting for transfers between devices: 1.9 us -> 1.9 us  [pair_exchange(): return lax.ppermute(value, axis, pairs)]
  transfers between devices with their start and end apart: 15 -> 20, of which waited for: 9 -> 11; matrix products, arithmetic and copies ran while one was open for 0% -> 0% of each run, Pallas kernels for 9% -> 10%
where the time goes in v15:
time: 73.6 us; the launch traced here: 73.3 us
  starting transfers between devices  27.9 us (38%)
  Pallas kernels  27.8 us (38%)
  waiting for transfers between devices  13.7 us (19%)
  local copies, waits for them, and re-layouts  2.61 us (4%)
  between operations  1.11 us (2%)
    ppermute x14, starting transfers between devices, sum_by_permutes(): lax.ppermute(value, axis, [(i, partner(i, stride, radix, k)) for i in ran...  17.8 us
    ppermute x14, waiting for transfers between devices, sum_by_permutes(): lax.ppermute(value, axis, [(i, partner(i, stride, radix, k)) for i in ran...  11.8 us
    ppermute x6, starting transfers between devices, pair_exchange(): return lax.ppermute(value, axis, pairs)  10.2 us
    pallas_call x1, Pallas kernels, local(): pl.pallas_call(functools.partial(second_kernel, tile, head_dim), out_shap...  9.39 us
    pallas_call x1, Pallas kernels, local(): pl.pallas_call(functools.partial(first_kernel, tile, head_dim), out_shape...  8.75 us
    pallas_call x2, Pallas kernels, queries(): pl.pallas_call(functools.partial(query_kernel, tile, section), out_shape=...  5.05 us
    pallas_call x1, Pallas kernels, local(): pl.pallas_call(functools.partial(last_kernel, tile, head_dim), out_shape=...  2.7 us
    pallas_call x1, Pallas kernels, local(): pl.pallas_call(functools.partial(prepare_kernel, head_dim), out_shape=mad...  1.92 us
  transfers between devices with their start and end apart: 20, of which 11 were waited for; matrix products, arithmetic and copies ran while one was open for 0% of the time, Pallas kernels for 10%

profile of v15, /device:TPU:0, one launch (start us, length us, event | category | flops | bytes accessed | tf_op | source)
XLA Modules:
  0.0 73.3 jit_solution(11174952712472505128)
XLA Ops:
  3.4 5.5 %collective-permute-start.2 = (bf16[8,8,256]{2,1,0:T(8,128)(2,1)S(1)}, bf16[8,8,256]{2,1,0:T(8,128)(2,1)S(1)}, u32[]{:S(2)}, u32[]{:S(2)}) collective-permute-start(bf16[8,8,256]{2,1,0:T(8,128)(2,1)S(1)} %get-tuple-element.31), channel_id=1, source_target_pairs={{0,1},{1,0},{2,3},{3,2},{4,5},{5,4},{6,7},{7,6},{8,9},{9,8},{10,11... | collective-permute-start | bytes 98312 | tf_op jit(solution)/shard_map/ppermute | solution.py:542
  8.9 1.9 %collective-permute-done.2.col_0 = bf16[8,8,256]{2,1,0:T(8,128)(2,1)S(1)} collective-permute-done((bf16[8,8,256]{2,1,0:T(8,128)(2,1)S(1)}, bf16[8,8,256]{2,1,0:T(8,128)(2,1)S(1)}, u32[]{:S(2)}, u32[]{:S(2)}) %collective-permute-start.2) | collective-permute-done | bytes 32800 | tf_op jit(solution)/shard_map/ppermute | solution.py:542
  10.8 2.0 %collective-permute-start.4 = (bf16[14,8,256]{2,1,0:T(8,128)(2,1)S(1)}, bf16[14,8,256]{2,1,0:T(8,128)(2,1)S(1)}, u32[]{:S(2)}, u32[]{:S(2)}) collective-permute-start(bf16[14,8,256]{2,1,0:T(8,128)(2,1)S(1)} %pad_maximum_fusion), channel_id=1, source_target_pairs={{0,8},{8,0},{16,24},{24,16},{1,9},{9,1},{17,25},{25,17},{2,10},{10... | collective-permute-start | bytes 172040 | tf_op jit(solution)/shard_map/ppermute | solution.py:542
  13.7 1.0 %copy-done.8 = bf16[2,24,32,32]{3,2,1,0:T(8,128)(2,1)S(1)} copy-done((bf16[2,24,32,32]{3,2,1,0:T(8,128)(2,1)S(1)}, bf16[2,24,32,32]{3,2,1,0:T(8,128)(2,1)}, u32[]{:S(2)}) %copy-start.8) | copy-done | bytes 98328
  14.7 1.9 %prepare.1 = (bf16[2,256,768]{2,1,0:T(8,128)(2,1)S(1)}, f32[2,32,768]{2,1,0:T(8,128)S(1)}, bf16[2,3,256,256]{3,2,1,0:T(8,128)(2,1)S(1)}, bf16[3,128,256]{2,1,0:T...) custom-call(bf16[2,256,768]{2,1,0:T(8,128)(2,1)S(1)} %copy-done.7, f32[5,5,2,768]{3,2,1,0:T(2,128)S(1)} %bitcast.5, ...), custom_call_target="tpu_custom_call" | custom-call | flops 2000000000 | bytes 4000000 | tf_op jit(solution)/shard_map/prepare/pallas_call | solution.py:599
  17.4 8.7 %first.1 = (bf16[20,48,256]{2,1,0:T(8,128)(2,1)S(1)}, bf16[144,128]{1,0:T(8,128)(2,1)S(1)}) custom-call(bf16[8,32,256]{2,1,0:T(8,128)(2,1)S(1)} %copy-done.3, bf16[7,32,256]{2,1,0:T(8,128)(2,1)S(1)} %collective-permute-done.row_0, bf16[7,32,256]{2,1,0:T(8,128)(2,1)S(1)} %collective-permute-done.1.row_1, bf16[8,8,256]{2,1,0:T(8,128)(2,1)S(1)} %collective-permute-done.2.col_0, ...), custom_call_target="tpu_custom_call" | custom-call | tf_op jit(solution)/shard_map/first/pallas_call | solution.py:678
  26.1 1.5 %collective-permute-start.8 = (bf16[144,128]{1,0:T(8,128)(2,1)S(1)}, bf16[144,128]{1,0:T(8,128)(2,1)S(1)}, u32[]{:S(2)}, u32[]{:S(2)}) collective-permute-start(bf16[144,128]{1,0:T(8,128)(2,1)S(1)} %get-tuple-element.23), channel_id=1, source_target_pairs={{0,24},{8,16},{16,8},{24,0},{1,25},{9,17},{17,9},{25,1},{2,26},{10... | collective-permute-start | bytes 110600 | tf_op jit(solution)/shard_map/ppermute | solution.py:516
  27.6 2.7 %collective-permute-start.7 = (bf16[144,128]{1,0:T(8,128)(2,1)S(1)}, bf16[144,128]{1,0:T(8,128)(2,1)S(1)}, u32[]{:S(2)}, u32[]{:S(2)}) collective-permute-start(bf16[144,128]{1,0:T(8,128)(2,1)S(1)} %get-tuple-element.23), channel_id=1, source_target_pairs={{0,16},{8,24},{16,0},{24,8},{1,17},{9,25},{17,1},{25,9},{2,18},{10... | collective-permute-start | bytes 110600 | tf_op jit(solution)/shard_map/ppermute | solution.py:516
  30.3 2.5 %collective-permute-done.7 = bf16[144,128]{1,0:T(8,128)(2,1)S(1)} collective-permute-done((bf16[144,128]{1,0:T(8,128)(2,1)S(1)}, bf16[144,128]{1,0:T(8,128)(2,1)S(1)}, u32[]{:S(2)}, u32[]{:S(2)}) %collective-permute-start.7) | collective-permute-done | bytes 36896 | tf_op jit(solution)/shard_map/ppermute | solution.py:516
  32.9 2.9 %collective-permute-start.11 = (bf16[144,128]{1,0:T(8,128)(2,1)S(1)}, bf16[144,128]{1,0:T(8,128)(2,1)S(1)}, u32[]{:S(2)}, u32[]{:S(2)}) collective-permute-start(bf16[144,128]{1,0:T(8,128)(2,1)S(1)} %add_convert_fusion.3), channel_id=1, source_target_pairs={{0,3},{1,2},{2,1},{3,0},{4,7},{5,6},{6,5},{7,4},{8,11},{9,10},{10,... | collective-permute-start | bytes 110600 | tf_op jit(solution)/shard_map/ppermute | solution.py:516
  36.4 1.8 %collective-permute-done.11 = bf16[144,128]{1,0:T(8,128)(2,1)S(1)} collective-permute-done((bf16[144,128]{1,0:T(8,128)(2,1)S(1)}, bf16[144,128]{1,0:T(8,128)(2,1)S(1)}, u32[]{:S(2)}, u32[]{:S(2)}) %collective-permute-start.11) | collective-permute-done | bytes 36896 | tf_op jit(solution)/shard_map/ppermute | solution.py:516
  38.2 1.5 %collective-permute-done.10 = bf16[144,128]{1,0:T(8,128)(2,1)S(1)} collective-permute-done((bf16[144,128]{1,0:T(8,128)(2,1)S(1)}, bf16[144,128]{1,0:T(8,128)(2,1)S(1)}, u32[]{:S(2)}, u32[]{:S(2)}) %collective-permute-start.10) | collective-permute-done | bytes 36896 | tf_op jit(solution)/shard_map/ppermute | solution.py:516
  40.2 2.7 %collective-permute-start.12 = (bf16[144,128]{1,0:T(8,128)(2,1)S(1)}, bf16[144,128]{1,0:T(8,128)(2,1)S(1)}, u32[]{:S(2)}, u32[]{:S(2)}) collective-permute-start(bf16[144,128]{1,0:T(8,128)(2,1)S(1)} %add_convert_fusion.2.payload), channel_id=1, source_target_pairs={{0,4},{1,5},{2,6},{3,7},{4,0},{5,1},{6,2},{7,3},{8,12},{9,13},{10,... | collective-permute-start | bytes 110600 | tf_op jit(solution)/shard_map/ppermute | solution.py:516
  42.8 3.1 %queries.2 = (bf16[16,48,512]{2,1,0:T(8,128)(2,1)S(1)}, bf16[16,48,256]{2,1,0:T(8,128)(2,1)S(1)}) custom-call(bf16[20,48,256]{2,1,0:T(8,128)(2,1)S(1)} %get-tuple-element.20.mixed_in, bf16[2,256,768]{2,1,0:T(8,128)(2,1)S(1)} %get-tuple-element.17.refs_6_.qkv_weight, f32[2,32,768]{2,1,0:T(8,128)S(1)} %get-tuple-element.18.refs_7_.taps, ...), custom_call_target="tpu_custom_call" | custom-call | flops 402653184 | bytes 1572864 | tf_op jit(solution)/shard_map/queries/pallas_call | solution.py:652
  45.9 9.4 %second.1 = (bf16[14,48,256]{2,1,0:T(8,128)(2,1)S(1)}, bf16[144,128]{1,0:T(8,128)(2,1)S(1)}) custom-call(bf16[16,48,256]{2,1,0:T(8,128)(2,1)S(1)} %get-tuple-element.21.mixed, bf16[16,48,512]{2,1,0:T(8,128)(2,1)S(1)} %get-tuple-element.22.query, bf16[144,128]{1,0:T(8,128)(2,1)S(1)} %add_convert_fusion.2.payload, ...), custom_call_target="tpu_custom_call" | custom-call | tf_op jit(solution)/shard_map/second/pallas_call | solution.py:693
  55.4 1.7 %collective-permute-start.14 = (bf16[144,128]{1,0:T(8,128)(2,1)S(1)}, bf16[144,128]{1,0:T(8,128)(2,1)S(1)}, u32[]{:S(2)}, u32[]{:S(2)}) collective-permute-start(bf16[144,128]{1,0:T(8,128)(2,1)S(1)} %get-tuple-element.28), channel_id=1, source_target_pairs={{0,16},{8,24},{16,0},{24,8},{1,17},{9,25},{17,1},{25,9},{2,18},{10... | collective-permute-start | bytes 110600 | tf_op jit(solution)/shard_map/ppermute | solution.py:516
  57.3 1.7 %collective-permute-done.15 = bf16[144,128]{1,0:T(8,128)(2,1)S(1)} collective-permute-done((bf16[144,128]{1,0:T(8,128)(2,1)S(1)}, bf16[144,128]{1,0:T(8,128)(2,1)S(1)}, u32[]{:S(2)}, u32[]{:S(2)}) %collective-permute-start.15) | collective-permute-done | bytes 36896 | tf_op jit(solution)/shard_map/ppermute | solution.py:516
  59.6 1.5 %collective-permute-start.18 = (bf16[144,128]{1,0:T(8,128)(2,1)S(1)}, bf16[144,128]{1,0:T(8,128)(2,1)S(1)}, u32[]{:S(2)}, u32[]{:S(2)}) collective-permute-start(bf16[144,128]{1,0:T(8,128)(2,1)S(1)} %add_convert_fusion.1), channel_id=1, source_target_pairs={{0,3},{1,2},{2,1},{3,0},{4,7},{5,6},{6,5},{7,4},{8,11},{9,10},{10,... | collective-permute-start | bytes 110600 | tf_op jit(solution)/shard_map/ppermute | solution.py:516
  61.5 1.7 %collective-permute-start.16 = (bf16[144,128]{1,0:T(8,128)(2,1)S(1)}, bf16[144,128]{1,0:T(8,128)(2,1)S(1)}, u32[]{:S(2)}, u32[]{:S(2)}) collective-permute-start(bf16[144,128]{1,0:T(8,128)(2,1)S(1)} %add_convert_fusion.1), channel_id=1, source_target_pairs={{0,1},{1,0},{2,3},{3,2},{4,5},{5,4},{6,7},{7,6},{8,9},{9,8},{10,11... | collective-permute-start | bytes 110600 | tf_op jit(solution)/shard_map/ppermute | solution.py:516
  63.2 1.6 %collective-permute-done.18 = bf16[144,128]{1,0:T(8,128)(2,1)S(1)} collective-permute-done((bf16[144,128]{1,0:T(8,128)(2,1)S(1)}, bf16[144,128]{1,0:T(8,128)(2,1)S(1)}, u32[]{:S(2)}, u32[]{:S(2)}) %collective-permute-start.18) | collective-permute-done | bytes 36896 | tf_op jit(solution)/shard_map/ppermute | solution.py:516
  65.5 1.9 %collective-permute-start.19 = (bf16[144,128]{1,0:T(8,128)(2,1)S(1)}, bf16[144,128]{1,0:T(8,128)(2,1)S(1)}, u32[]{:S(2)}, u32[]{:S(2)}) collective-permute-start(bf16[144,128]{1,0:T(8,128)(2,1)S(1)} %add_convert_fusion.payload), channel_id=1, source_target_pairs={{0,4},{1,5},{2,6},{3,7},{4,0},{5,1},{6,2},{7,3},{8,12},{9,13},{10,... | collective-permute-start | bytes 110600 | tf_op jit(solution)/shard_map/ppermute | solution.py:516
  67.5 2.0 %queries.3 = (bf16[10,48,512]{2,1,0:T(8,128)(2,1)S(1)}, bf16[10,48,256]{2,1,0:T(8,128)(2,1)S(1)}) custom-call(bf16[14,48,256]{2,1,0:T(8,128)(2,1)S(1)} %get-tuple-element.25.mixed_in, bf16[2,256,768]{2,1,0:T(8,128)(2,1)S(1)} %get-tuple-element.17.refs_6_.qkv_weight, f32[2,32,768]{2,1,0:T(8,128)S(1)} %get-tuple-element.18.refs_7_.taps, ...), custom_call_target="tpu_custom_call" | custom-call | flops 251658240 | bytes 983040 | tf_op jit(solution)/shard_map/queries/pallas_call | solution.py:652
  69.5 1.0 %collective-permute-done.19.other = bf16[144,128]{1,0:T(8,128)(2,1)S(1)} collective-permute-done((bf16[144,128]{1,0:T(8,128)(2,1)S(1)}, bf16[144,128]{1,0:T(8,128)(2,1)S(1)}, u32[]{:S(2)}, u32[]{:S(2)}) %collective-permute-start.19) | collective-permute-done | bytes 36896 | tf_op jit(solution)/shard_map/ppermute | solution.py:516
  70.4 2.7 %last.1 = (bf16[8,32,256]{2,1,0:T(8,128)(2,1)}, f32[4,8,32]{2,1,0:T(8,128)}) custom-call(bf16[10,48,256]{2,1,0:T(8,128)(2,1)S(1)} %get-tuple-element.26.mixed, bf16[10,48,512]{2,1,0:T(8,128)(2,1)S(1)} %get-tuple-element.27.query, bf16[144,128]{1,0:T(8,128)(2,1)S(1)} %add_convert_fusion.payload, bf16[144,128]{1,0:T(8,128)(2,1)S(1)} %collective-permute-done.19.other, ...), custom_call_target="tpu_custom_call" | custom-call | tf_op jit(solution)/shard_map/last/pallas_call | solution.py:706
  (61 shorter events, 7.5 us)
Async XLA Ops:
  0.7 13.0 %copy-start.10 = (bf16[3,3,4,256]{3,2,1,0:T(4,128)(2,1)S(1)}, bf16[3,3,4,256]{3,2,1,0:T(4,128)(2,1)}, u32[]{:S(2)}) copy-start(bf16[3,3,4,256]{3,2,1,0:T(4,128)(2,1)} %head.1) | copy-start | bytes 55300
  1.5 7.4 %collective-permute-start.3 = (bf16[8,8,256]{2,1,0:T(8,128)(2,1)S(1)}, bf16[8,8,256]{2,1,0:T(8,128)(2,1)S(1)}, u32[]{:S(2)}, u32[]{:S(2)}) collective-permute-start(bf16[8,8,256]{2,1,0:T(8,128)(2,1)S(1)} %get-tuple-element.30), channel_id=1, source_target_pairs={{1,2},{2,1},{3,4},{4,3},{5,6},{6,5},{9,10},{10,9},{11,12},{12,11},... | collective-permute-start | bytes 98312 | tf_op jit(solution)/shard_map/ppermute | solution.py:542
  2.2 11.5 %copy-start.9 = (f32[2,5,5,768]{3,0,2,1:T(2,128)S(1)}, f32[2,5,5,768]{3,0,2,1:T(2,128)}, u32[]{:S(2)}) copy-start(f32[2,5,5,768]{3,0,2,1:T(2,128)} %param.22) | copy-start | bytes 460804
  2.2 11.5 %copy-start.7 = (bf16[2,256,768]{2,1,0:T(8,128)(2,1)S(1)}, bf16[2,256,768]{2,1,0:T(8,128)(2,1)}, u32[]{:S(2)}) copy-start(bf16[2,256,768]{2,1,0:T(8,128)(2,1)} %qkv.1) | copy-start | bytes 2359300
  2.2 14.5 %collective-permute-start = (bf16[7,32,256]{2,1,0:T(8,128)(2,1)S(1)}, bf16[7,32,256]{2,1,0:T(8,128)(2,1)S(1)}, u32[]{:S(2)}, u32[]{:S(2)}) collective-permute-start(bf16[7,32,256]{2,1,0:T(8,128)(2,1)S(1)} %get-tuple-element.33), channel_id=1, source_target_pairs={{0,8},{8,0},{16,24},{24,16},{1,9},{9,1},{17,25},{25,17},{2,10},{10... | collective-permute-start | bytes 344072 | tf_op jit(solution)/shard_map/ppermute | solution.py:542
  2.7 14.0 %collective-permute-start.1 = (bf16[7,32,256]{2,1,0:T(8,128)(2,1)S(1)}, bf16[7,32,256]{2,1,0:T(8,128)(2,1)S(1)}, u32[]{:S(2)}, u32[]{:S(2)}) collective-permute-start(bf16[7,32,256]{2,1,0:T(8,128)(2,1)S(1)} %get-tuple-element.32), channel_id=1, source_target_pairs={{8,16},{16,8},{9,17},{17,9},{10,18},{18,10},{11,19},{19,11},{12,20... | collective-permute-start | bytes 344072 | tf_op jit(solution)/shard_map/ppermute | solution.py:542
  3.4 7.4 %collective-permute-start.2 = (bf16[8,8,256]{2,1,0:T(8,128)(2,1)S(1)}, bf16[8,8,256]{2,1,0:T(8,128)(2,1)S(1)}, u32[]{:S(2)}, u32[]{:S(2)}) collective-permute-start(bf16[8,8,256]{2,1,0:T(8,128)(2,1)S(1)} %get-tuple-element.31), channel_id=1, source_target_pairs={{0,1},{1,0},{2,3},{3,2},{4,5},{5,4},{6,7},{7,6},{8,9},{9,8},{10,11... | collective-permute-start | bytes 98312 | tf_op jit(solution)/shard_map/ppermute | solution.py:542
  10.8 5.9 %collective-permute-start.4 = (bf16[14,8,256]{2,1,0:T(8,128)(2,1)S(1)}, bf16[14,8,256]{2,1,0:T(8,128)(2,1)S(1)}, u32[]{:S(2)}, u32[]{:S(2)}) collective-permute-start(bf16[14,8,256]{2,1,0:T(8,128)(2,1)S(1)} %pad_maximum_fusion), channel_id=1, source_target_pairs={{0,8},{8,0},{16,24},{24,16},{1,9},{9,1},{17,25},{25,17},{2,10},{10... | collective-permute-start | bytes 172040 | tf_op jit(solution)/shard_map/ppermute | solution.py:542
  12.9 3.8 %collective-permute-start.5 = (bf16[14,8,256]{2,1,0:T(8,128)(2,1)S(1)}, bf16[14,8,256]{2,1,0:T(8,128)(2,1)S(1)}, u32[]{:S(2)}, u32[]{:S(2)}) collective-permute-start(bf16[14,8,256]{2,1,0:T(8,128)(2,1)S(1)} %pad_maximum_fusion.1), channel_id=1, source_target_pairs={{8,16},{16,8},{9,17},{17,9},{10,18},{18,10},{11,19},{19,11},{12,20... | collective-permute-start | bytes 172040 | tf_op jit(solution)/shard_map/ppermute | solution.py:542
  26.1 4.2 %collective-permute-start.8 = (bf16[144,128]{1,0:T(8,128)(2,1)S(1)}, bf16[144,128]{1,0:T(8,128)(2,1)S(1)}, u32[]{:S(2)}, u32[]{:S(2)}) collective-permute-start(bf16[144,128]{1,0:T(8,128)(2,1)S(1)} %get-tuple-element.23), channel_id=1, source_target_pairs={{0,24},{8,16},{16,8},{24,0},{1,25},{9,17},{17,9},{25,1},{2,26},{10... | collective-permute-start | bytes 110600 | tf_op jit(solution)/shard_map/ppermute | solution.py:516
  27.6 5.3 %collective-permute-start.7 = (bf16[144,128]{1,0:T(8,128)(2,1)S(1)}, bf16[144,128]{1,0:T(8,128)(2,1)S(1)}, u32[]{:S(2)}, u32[]{:S(2)}) collective-permute-start(bf16[144,128]{1,0:T(8,128)(2,1)S(1)} %get-tuple-element.23), channel_id=1, source_target_pairs={{0,16},{8,24},{16,0},{24,8},{1,17},{9,25},{17,1},{25,9},{2,18},{10... | collective-permute-start | bytes 110600 | tf_op jit(solution)/shard_map/ppermute | solution.py:516
  30.3 2.5 %collective-permute-start.6 = (bf16[144,128]{1,0:T(8,128)(2,1)S(1)}, bf16[144,128]{1,0:T(8,128)(2,1)S(1)}, u32[]{:S(2)}, u32[]{:S(2)}) collective-permute-start(bf16[144,128]{1,0:T(8,128)(2,1)S(1)} %get-tuple-element.23), channel_id=1, source_target_pairs={{0,8},{8,0},{16,24},{24,16},{1,9},{9,1},{17,25},{25,17},{2,10},{10... | collective-permute-start | bytes 110600 | tf_op jit(solution)/shard_map/ppermute | solution.py:516
  32.9 5.3 %collective-permute-start.11 = (bf16[144,128]{1,0:T(8,128)(2,1)S(1)}, bf16[144,128]{1,0:T(8,128)(2,1)S(1)}, u32[]{:S(2)}, u32[]{:S(2)}) collective-permute-start(bf16[144,128]{1,0:T(8,128)(2,1)S(1)} %add_convert_fusion.3), channel_id=1, source_target_pairs={{0,3},{1,2},{2,1},{3,0},{4,7},{5,6},{6,5},{7,4},{8,11},{9,10},{10,... | collective-permute-start | bytes 110600 | tf_op jit(solution)/shard_map/ppermute | solution.py:516
  35.8 4.0 %collective-permute-start.10 = (bf16[144,128]{1,0:T(8,128)(2,1)S(1)}, bf16[144,128]{1,0:T(8,128)(2,1)S(1)}, u32[]{:S(2)}, u32[]{:S(2)}) collective-permute-start(bf16[144,128]{1,0:T(8,128)(2,1)S(1)} %add_convert_fusion.3), channel_id=1, source_target_pairs={{0,2},{1,3},{2,0},{3,1},{4,6},{5,7},{6,4},{7,5},{8,10},{9,11},{10,... | collective-permute-start | bytes 110600 | tf_op jit(solution)/shard_map/ppermute | solution.py:516
  36.2 4.0 %collective-permute-start.9 = (bf16[144,128]{1,0:T(8,128)(2,1)S(1)}, bf16[144,128]{1,0:T(8,128)(2,1)S(1)}, u32[]{:S(2)}, u32[]{:S(2)}) collective-permute-start(bf16[144,128]{1,0:T(8,128)(2,1)S(1)} %add_convert_fusion.3), channel_id=1, source_target_pairs={{0,1},{1,0},{2,3},{3,2},{4,5},{5,4},{6,7},{7,6},{8,9},{9,8},{10,11... | collective-permute-start | bytes 110600 | tf_op jit(solution)/shard_map/ppermute | solution.py:516
  40.2 5.7 %collective-permute-start.12 = (bf16[144,128]{1,0:T(8,128)(2,1)S(1)}, bf16[144,128]{1,0:T(8,128)(2,1)S(1)}, u32[]{:S(2)}, u32[]{:S(2)}) collective-permute-start(bf16[144,128]{1,0:T(8,128)(2,1)S(1)} %add_convert_fusion.2.payload), channel_id=1, source_target_pairs={{0,4},{1,5},{2,6},{3,7},{4,0},{5,1},{6,2},{7,3},{8,12},{9,13},{10,... | collective-permute-start | bytes 110600 | tf_op jit(solution)/shard_map/ppermute | solution.py:516
  42.8 3.1 %copy-start.2 = (bf16[2,512,256]{2,1,0:T(8,128)(2,1)S(1)}, bf16[2,512,256]{2,1,0:T(8,128)(2,1)}, u32[]{:S(2)}) copy-start(bf16[2,512,256]{2,1,0:T(8,128)(2,1)} %out_weight.3) | copy-start | bytes 1572868
  55.3 3.7 %collective-permute-start.15 = (bf16[144,128]{1,0:T(8,128)(2,1)S(1)}, bf16[144,128]{1,0:T(8,128)(2,1)S(1)}, u32[]{:S(2)}, u32[]{:S(2)}) collective-permute-start(bf16[144,128]{1,0:T(8,128)(2,1)S(1)} %get-tuple-element.28), channel_id=1, source_target_pairs={{0,24},{8,16},{16,8},{24,0},{1,25},{9,17},{17,9},{25,1},{2,26},{10... | collective-permute-start | bytes 110600 | tf_op jit(solution)/shard_map/ppermute | solution.py:516
  55.4 4.2 %collective-permute-start.14 = (bf16[144,128]{1,0:T(8,128)(2,1)S(1)}, bf16[144,128]{1,0:T(8,128)(2,1)S(1)}, u32[]{:S(2)}, u32[]{:S(2)}) collective-permute-start(bf16[144,128]{1,0:T(8,128)(2,1)S(1)} %get-tuple-element.28), channel_id=1, source_target_pairs={{0,16},{8,24},{16,0},{24,8},{1,17},{9,25},{17,1},{25,9},{2,18},{10... | collective-permute-start | bytes 110600 | tf_op jit(solution)/shard_map/ppermute | solution.py:516
  57.1 2.5 %collective-permute-start.13 = (bf16[144,128]{1,0:T(8,128)(2,1)S(1)}, bf16[144,128]{1,0:T(8,128)(2,1)S(1)}, u32[]{:S(2)}, u32[]{:S(2)}) collective-permute-start(bf16[144,128]{1,0:T(8,128)(2,1)S(1)} %get-tuple-element.28), channel_id=1, source_target_pairs={{0,8},{8,0},{16,24},{24,16},{1,9},{9,1},{17,25},{25,17},{2,10},{10... | collective-permute-start | bytes 110600 | tf_op jit(solution)/shard_map/ppermute | solution.py:516
  59.6 5.2 %collective-permute-start.18 = (bf16[144,128]{1,0:T(8,128)(2,1)S(1)}, bf16[144,128]{1,0:T(8,128)(2,1)S(1)}, u32[]{:S(2)}, u32[]{:S(2)}) collective-permute-start(bf16[144,128]{1,0:T(8,128)(2,1)S(1)} %add_convert_fusion.1), channel_id=1, source_target_pairs={{0,3},{1,2},{2,1},{3,0},{4,7},{5,6},{6,5},{7,4},{8,11},{9,10},{10,... | collective-permute-start | bytes 110600 | tf_op jit(solution)/shard_map/ppermute | solution.py:516
  61.1 4.0 %collective-permute-start.17 = (bf16[144,128]{1,0:T(8,128)(2,1)S(1)}, bf16[144,128]{1,0:T(8,128)(2,1)S(1)}, u32[]{:S(2)}, u32[]{:S(2)}) collective-permute-start(bf16[144,128]{1,0:T(8,128)(2,1)S(1)} %add_convert_fusion.1), channel_id=1, source_target_pairs={{0,2},{1,3},{2,0},{3,1},{4,6},{5,7},{6,4},{7,5},{8,10},{9,11},{10,... | collective-permute-start | bytes 110600 | tf_op jit(solution)/shard_map/ppermute | solution.py:516
  61.5 4.0 %collective-permute-start.16 = (bf16[144,128]{1,0:T(8,128)(2,1)S(1)}, bf16[144,128]{1,0:T(8,128)(2,1)S(1)}, u32[]{:S(2)}, u32[]{:S(2)}) collective-permute-start(bf16[144,128]{1,0:T(8,128)(2,1)S(1)} %add_convert_fusion.1), channel_id=1, source_target_pairs={{0,1},{1,0},{2,3},{3,2},{4,5},{5,4},{6,7},{7,6},{8,9},{9,8},{10,11... | collective-permute-start | bytes 110600 | tf_op jit(solution)/shard_map/ppermute | solution.py:516
  65.5 4.9 %collective-permute-start.19 = (bf16[144,128]{1,0:T(8,128)(2,1)S(1)}, bf16[144,128]{1,0:T(8,128)(2,1)S(1)}, u32[]{:S(2)}, u32[]{:S(2)}) collective-permute-start(bf16[144,128]{1,0:T(8,128)(2,1)S(1)} %add_convert_fusion.payload), channel_id=1, source_target_pairs={{0,4},{1,5},{2,6},{3,7},{4,0},{5,1},{6,2},{7,3},{8,12},{9,13},{10,... | collective-permute-start | bytes 110600 | tf_op jit(solution)/shard_map/ppermute | solution.py:516
  (10 other events, 14.9 us)

commit v16 on v15

--- a/solution.py
+++ b/solution.py
@@ -579,13 +579,6 @@
     low, high = edges(features, 0, REACH, odd_row)
     row_1 = pair_exchange(high, "row", 1)
     row_0 = pair_exchange(low, "row", 0)
-    low, high = (
-        jnp.concatenate(pieces, axis=0)
-        for pieces in zip(edges(col_0, 0, REACH, odd_row), edges(col_1, 0, REACH, odd_row))
-    )
-    corner_1 = pair_exchange(high, "row", 1)
-    corner_0 = pair_exchange(low, "row", 0)
-
     aggregate_depth = aggregate_depth.transpose(1, 2, 0, 3)
     depth_weight = depth_weight.transpose(1, 2, 0, 3)
     params = pltpu.CompilerParams(vmem_limit_bytes=24 * 2**20)
@@ -610,6 +603,14 @@
         ),
         name="prepare",
     )(qkv_weight, aggregate_depth, aggregate_group, head_weight, project_bias, output_bias)
+
+    col_0, col_1, taps = lax.optimization_barrier((col_0, col_1, taps))
+    low, high = (
+        jnp.concatenate(pieces, axis=0)
+        for pieces in zip(edges(col_0, 0, REACH, odd_row), edges(col_1, 0, REACH, odd_row))
+    )
+    corner_1 = pair_exchange(high, "row", 1)
+    corner_0 = pair_exchange(low, "row", 0)
 
     weights = [
         expand_weight, expand_bias, depth_weight, depth_bias, project_weight, project_bias,

time: 73.6 us -> 74.5 us (1.012)
  starting transfers between devices: 27.9 us -> 29.7 us
  waiting for transfers between devices: 13.7 us -> 12.2 us
    ppermute x14, starting transfers between devices: 17.8 us -> 21.8 us  [sum_by_permutes(): lax.ppermute(value, axis, [(i, partner(i, stride, radix, k)) for i in ran...]
    ppermute x6, starting transfers between devices: 10.2 us -> 7.86 us  [pair_exchange(): return lax.ppermute(value, axis, pairs)]
    ppermute x6, waiting for transfers between devices: 1.9 us -> 0.09 us  [pair_exchange(): return lax.ppermute(value, axis, pairs)]
  transfers between devices with their start and end apart: 20 -> 20, of which waited for: 11 -> 10; matrix products, arithmetic and copies ran while one was open for 0% -> 0% of each run, Pallas kernels for 10% -> 9%
where the time goes in v16:
time: 74.5 us; the launch traced here: 74.2 us
  starting transfers between devices  29.7 us (40%)
  Pallas kernels  27.8 us (37%)
  waiting for transfers between devices  12.2 us (16%)
  local copies, waits for them, and re-layouts  3.27 us (4%)
  between operations  1.12 us (2%)
    ppermute x14, starting transfers between devices, sum_by_permutes(): lax.ppermute(value, axis, [(i, partner(i, stride, radix, k)) for i in ran...  21.8 us
    ppermute x14, waiting for transfers between devices, sum_by_permutes(): lax.ppermute(value, axis, [(i, partner(i, stride, radix, k)) for i in ran...  12.1 us
    pallas_call x1, Pallas kernels, local(): pl.pallas_call(functools.partial(second_kernel, tile, head_dim), out_shap...  9.4 us
    pallas_call x1, Pallas kernels, local(): pl.pallas_call(functools.partial(first_kernel, tile, head_dim), out_shape...  8.76 us
    ppermute x6, starting transfers between devices, pair_exchange(): return lax.ppermute(value, axis, pairs)  7.86 us
    pallas_call x2, Pallas kernels, queries(): pl.pallas_call(functools.partial(query_kernel, tile, section), out_shape=...  5.03 us
    pallas_call x1, Pallas kernels, local(): pl.pallas_call(functools.partial(last_kernel, tile, head_dim), out_shape=...  2.7 us
    unnamed x28, local copies, waits for them, and re-layouts  2.1 us
  transfers between devices with their start and end apart: 20, of which 10 were waited for; matrix products, arithmetic and copies ran while one was open for 0% of the time, Pallas kernels for 9%

profile of v16, /device:TPU:0, one launch (start us, length us, event | category | flops | bytes accessed | tf_op | source)
XLA Modules:
  0.0 74.2 jit_solution(3101210048005453448)
XLA Ops:
  0.7 1.0 %constant_dynamic-slice_fusion.6 = (bf16[7,32,256]{2,1,0:T(8,128)(2,1)S(1)}, bf16[7,32,256]{2,1,0:T(8,128)(2,1)S(1)}) fusion(bf16[8,32,256]{2,1,0:T(8,128)(2,1)} %own.1, s32[]{:T(128)S(6)} %select_n.26, s32[]{:T(128)S(6)} %select_n.25), kind=kLoop, calls=%fused_computation.12 | loop fusion | bytes 458760 | tf_op jit(solution)/shard_map/dynamic_slice | solution.py:571
  3.0 2.6 %collective-permute-start.2 = (bf16[8,8,256]{2,1,0:T(8,128)(2,1)S(1)}, bf16[8,8,256]{2,1,0:T(8,128)(2,1)S(1)}, u32[]{:S(2)}, u32[]{:S(2)}) collective-permute-start(bf16[8,8,256]{2,1,0:T(8,128)(2,1)S(1)} %get-tuple-element.37), channel_id=1, source_target_pairs={{0,1},{1,0},{2,3},{3,2},{4,5},{5,4},{6,7},{7,6},{8,9},{9,8},{10,11... | collective-permute-start | bytes 98312 | tf_op jit(solution)/shard_map/ppermute | solution.py:542
  6.3 1.1 %copy-done.7 = bf16[2,256,768]{2,1,0:T(8,128)(2,1)S(1)} copy-done((bf16[2,256,768]{2,1,0:T(8,128)(2,1)S(1)}, bf16[2,256,768]{2,1,0:T(8,128)(2,1)}, u32[]{:S(2)}) %copy-start.7) | copy-done | bytes 786456
  8.3 1.9 %prepare.1 = (bf16[2,256,768]{2,1,0:T(8,128)(2,1)S(1)}, f32[2,32,768]{2,1,0:T(8,128)S(1)}, bf16[2,3,256,256]{3,2,1,0:T(8,128)(2,1)S(1)}, bf16[3,128,256]{2,1,0:T...) custom-call(bf16[2,256,768]{2,1,0:T(8,128)(2,1)S(1)} %copy-done.7, f32[5,5,2,768]{3,2,1,0:T(2,128)S(1)} %bitcast.5, ...), custom_call_target="tpu_custom_call" | custom-call | flops 2000000000 | bytes 4000000 | tf_op jit(solution)/shard_map/prepare/pallas_call | solution.py:592
  10.3 2.6 %collective-permute-start.4 = (bf16[14,8,256]{2,1,0:T(8,128)(2,1)S(1)}, bf16[14,8,256]{2,1,0:T(8,128)(2,1)S(1)}, u32[]{:S(2)}, u32[]{:S(2)}) collective-permute-start(bf16[14,8,256]{2,1,0:T(8,128)(2,1)S(1)} %pad_maximum_fusion), channel_id=1, source_target_pairs={{0,8},{8,0},{16,24},{24,16},{1,9},{9,1},{17,25},{25,17},{2,10},{10... | collective-permute-start | bytes 172040 | tf_op jit(solution)/shard_map/ppermute | solution.py:542
  13.9 8.8 %first.1 = (bf16[20,48,256]{2,1,0:T(8,128)(2,1)S(1)}, bf16[144,128]{1,0:T(8,128)(2,1)S(1)}) custom-call(bf16[8,32,256]{2,1,0:T(8,128)(2,1)S(1)} %copy-done.3, bf16[7,32,256]{2,1,0:T(8,128)(2,1)S(1)} %collective-permute-done.row_0, bf16[7,32,256]{2,1,0:T(8,128)(2,1)S(1)} %collective-permute-done.1.row_1, bf16[8,8,256]{2,1,0:T(8,128)(2,1)S(1)} %collective-permute-done.2.col_0, ...), custom_call_target="tpu_custom_call" | custom-call | tf_op jit(solution)/shard_map/first/pallas_call | solution.py:679
  22.7 1.0 %collective-permute-start.8 = (bf16[144,128]{1,0:T(8,128)(2,1)S(1)}, bf16[144,128]{1,0:T(8,128)(2,1)S(1)}, u32[]{:S(2)}, u32[]{:S(2)}) collective-permute-start(bf16[144,128]{1,0:T(8,128)(2,1)S(1)} %get-tuple-element.29), channel_id=1, source_target_pairs={{0,24},{8,16},{16,8},{24,0},{1,25},{9,17},{17,9},{25,1},{2,26},{10... | collective-permute-start | bytes 110600 | tf_op jit(solution)/shard_map/ppermute | solution.py:516
  23.7 5.3 %collective-permute-start.7 = (bf16[144,128]{1,0:T(8,128)(2,1)S(1)}, bf16[144,128]{1,0:T(8,128)(2,1)S(1)}, u32[]{:S(2)}, u32[]{:S(2)}) collective-permute-start(bf16[144,128]{1,0:T(8,128)(2,1)S(1)} %get-tuple-element.29), channel_id=1, source_target_pairs={{0,16},{8,24},{16,0},{24,8},{1,17},{9,25},{17,1},{25,9},{2,18},{10... | collective-permute-start | bytes 110600 | tf_op jit(solution)/shard_map/ppermute | solution.py:516
  29.0 2.7 %collective-permute-done.7 = bf16[144,128]{1,0:T(8,128)(2,1)S(1)} collective-permute-done((bf16[144,128]{1,0:T(8,128)(2,1)S(1)}, bf16[144,128]{1,0:T(8,128)(2,1)S(1)}, u32[]{:S(2)}, u32[]{:S(2)}) %collective-permute-start.7) | collective-permute-done | bytes 36896 | tf_op jit(solution)/shard_map/ppermute | solution.py:516
  31.8 4.9 %collective-permute-start.11 = (bf16[144,128]{1,0:T(8,128)(2,1)S(1)}, bf16[144,128]{1,0:T(8,128)(2,1)S(1)}, u32[]{:S(2)}, u32[]{:S(2)}) collective-permute-start(bf16[144,128]{1,0:T(8,128)(2,1)S(1)} %add_convert_fusion.3), channel_id=1, source_target_pairs={{0,3},{1,2},{2,1},{3,0},{4,7},{5,6},{6,5},{7,4},{8,11},{9,10},{10,... | collective-permute-start | bytes 110600 | tf_op jit(solution)/shard_map/ppermute | solution.py:516
  37.3 1.5 %collective-permute-done.11 = bf16[144,128]{1,0:T(8,128)(2,1)S(1)} collective-permute-done((bf16[144,128]{1,0:T(8,128)(2,1)S(1)}, bf16[144,128]{1,0:T(8,128)(2,1)S(1)}, u32[]{:S(2)}, u32[]{:S(2)}) %collective-permute-start.11) | collective-permute-done | bytes 36896 | tf_op jit(solution)/shard_map/ppermute | solution.py:516
  38.8 1.8 %collective-permute-done.10 = bf16[144,128]{1,0:T(8,128)(2,1)S(1)} collective-permute-done((bf16[144,128]{1,0:T(8,128)(2,1)S(1)}, bf16[144,128]{1,0:T(8,128)(2,1)S(1)}, u32[]{:S(2)}, u32[]{:S(2)}) %collective-permute-start.10) | collective-permute-done | bytes 36896 | tf_op jit(solution)/shard_map/ppermute | solution.py:516
  41.1 2.7 %collective-permute-start.12 = (bf16[144,128]{1,0:T(8,128)(2,1)S(1)}, bf16[144,128]{1,0:T(8,128)(2,1)S(1)}, u32[]{:S(2)}, u32[]{:S(2)}) collective-permute-start(bf16[144,128]{1,0:T(8,128)(2,1)S(1)} %add_convert_fusion.2.payload), channel_id=1, source_target_pairs={{0,4},{1,5},{2,6},{3,7},{4,0},{5,1},{6,2},{7,3},{8,12},{9,13},{10,... | collective-permute-start | bytes 110600 | tf_op jit(solution)/shard_map/ppermute | solution.py:516
  43.8 3.0 %queries.2 = (bf16[16,48,512]{2,1,0:T(8,128)(2,1)S(1)}, bf16[16,48,256]{2,1,0:T(8,128)(2,1)S(1)}) custom-call(bf16[20,48,256]{2,1,0:T(8,128)(2,1)S(1)} %get-tuple-element.26.mixed_in, bf16[2,256,768]{2,1,0:T(8,128)(2,1)S(1)} %get-tuple-element.23.refs_6_.qkv_weight, f32[2,32,768]{2,1,0:T(8,128)S(1)} %get-tuple-element.24.refs_7_.taps, ...), custom_call_target="tpu_custom_call" | custom-call | flops 402653184 | bytes 1572864 | tf_op jit(solution)/shard_map/queries/pallas_call | solution.py:653
  46.8 9.4 %second.1 = (bf16[14,48,256]{2,1,0:T(8,128)(2,1)S(1)}, bf16[144,128]{1,0:T(8,128)(2,1)S(1)}) custom-call(bf16[16,48,256]{2,1,0:T(8,128)(2,1)S(1)} %get-tuple-element.27.mixed, bf16[16,48,512]{2,1,0:T(8,128)(2,1)S(1)} %get-tuple-element.28.query, bf16[144,128]{1,0:T(8,128)(2,1)S(1)} %add_convert_fusion.2.payload, ...), custom_call_target="tpu_custom_call" | custom-call | tf_op jit(solution)/shard_map/second/pallas_call | solution.py:694
  56.3 1.5 %collective-permute-start.14 = (bf16[144,128]{1,0:T(8,128)(2,1)S(1)}, bf16[144,128]{1,0:T(8,128)(2,1)S(1)}, u32[]{:S(2)}, u32[]{:S(2)}) collective-permute-start(bf16[144,128]{1,0:T(8,128)(2,1)S(1)} %get-tuple-element.34), channel_id=1, source_target_pairs={{0,16},{8,24},{16,0},{24,8},{1,17},{9,25},{17,1},{25,9},{2,18},{10... | collective-permute-start | bytes 110600 | tf_op jit(solution)/shard_map/ppermute | solution.py:516
  58.2 1.9 %collective-permute-done.15 = bf16[144,128]{1,0:T(8,128)(2,1)S(1)} collective-permute-done((bf16[144,128]{1,0:T(8,128)(2,1)S(1)}, bf16[144,128]{1,0:T(8,128)(2,1)S(1)}, u32[]{:S(2)}, u32[]{:S(2)}) %collective-permute-start.15) | collective-permute-done | bytes 36896 | tf_op jit(solution)/shard_map/ppermute | solution.py:516
  60.7 1.2 %collective-permute-start.17 = (bf16[144,128]{1,0:T(8,128)(2,1)S(1)}, bf16[144,128]{1,0:T(8,128)(2,1)S(1)}, u32[]{:S(2)}, u32[]{:S(2)}) collective-permute-start(bf16[144,128]{1,0:T(8,128)(2,1)S(1)} %add_convert_fusion.1), channel_id=1, source_target_pairs={{0,2},{1,3},{2,0},{3,1},{4,6},{5,7},{6,4},{7,5},{8,10},{9,11},{10,... | collective-permute-start | bytes 110600 | tf_op jit(solution)/shard_map/ppermute | solution.py:516
  62.0 2.0 %collective-permute-start.16 = (bf16[144,128]{1,0:T(8,128)(2,1)S(1)}, bf16[144,128]{1,0:T(8,128)(2,1)S(1)}, u32[]{:S(2)}, u32[]{:S(2)}) collective-permute-start(bf16[144,128]{1,0:T(8,128)(2,1)S(1)} %add_convert_fusion.1), channel_id=1, source_target_pairs={{0,1},{1,0},{2,3},{3,2},{4,5},{5,4},{6,7},{7,6},{8,9},{9,8},{10,11... | collective-permute-start | bytes 110600 | tf_op jit(solution)/shard_map/ppermute | solution.py:516
  64.0 1.5 %collective-permute-done.18 = bf16[144,128]{1,0:T(8,128)(2,1)S(1)} collective-permute-done((bf16[144,128]{1,0:T(8,128)(2,1)S(1)}, bf16[144,128]{1,0:T(8,128)(2,1)S(1)}, u32[]{:S(2)}, u32[]{:S(2)}) %collective-permute-start.18) | collective-permute-done | bytes 36896 | tf_op jit(solution)/shard_map/ppermute | solution.py:516
  66.0 1.8 %collective-permute-start.19 = (bf16[144,128]{1,0:T(8,128)(2,1)S(1)}, bf16[144,128]{1,0:T(8,128)(2,1)S(1)}, u32[]{:S(2)}, u32[]{:S(2)}) collective-permute-start(bf16[144,128]{1,0:T(8,128)(2,1)S(1)} %add_convert_fusion.payload), channel_id=1, source_target_pairs={{0,4},{1,5},{2,6},{3,7},{4,0},{5,1},{6,2},{7,3},{8,12},{9,13},{10,... | collective-permute-start | bytes 110600 | tf_op jit(solution)/shard_map/ppermute | solution.py:516
  67.9 2.0 %queries.3 = (bf16[10,48,512]{2,1,0:T(8,128)(2,1)S(1)}, bf16[10,48,256]{2,1,0:T(8,128)(2,1)S(1)}) custom-call(bf16[14,48,256]{2,1,0:T(8,128)(2,1)S(1)} %get-tuple-element.31.mixed_in, bf16[2,256,768]{2,1,0:T(8,128)(2,1)S(1)} %get-tuple-element.23.refs_6_.qkv_weight, f32[2,32,768]{2,1,0:T(8,128)S(1)} %get-tuple-element.24.refs_7_.taps, ...), custom_call_target="tpu_custom_call" | custom-call | flops 251658240 | bytes 983040 | tf_op jit(solution)/shard_map/queries/pallas_call | solution.py:653
  69.9 1.4 %collective-permute-done.19.other = bf16[144,128]{1,0:T(8,128)(2,1)S(1)} collective-permute-done((bf16[144,128]{1,0:T(8,128)(2,1)S(1)}, bf16[144,128]{1,0:T(8,128)(2,1)S(1)}, u32[]{:S(2)}, u32[]{:S(2)}) %collective-permute-start.19) | collective-permute-done | bytes 36896 | tf_op jit(solution)/shard_map/ppermute | solution.py:516
  71.3 2.7 %last.1 = (bf16[8,32,256]{2,1,0:T(8,128)(2,1)}, f32[4,8,32]{2,1,0:T(8,128)}) custom-call(bf16[10,48,256]{2,1,0:T(8,128)(2,1)S(1)} %get-tuple-element.32.mixed, bf16[10,48,512]{2,1,0:T(8,128)(2,1)S(1)} %get-tuple-element.33.query, bf16[144,128]{1,0:T(8,128)(2,1)S(1)} %add_convert_fusion.payload, bf16[144,128]{1,0:T(8,128)(2,1)S(1)} %collective-permute-done.19.other, ...), custom_call_target="tpu_custom_call" | custom-call | tf_op jit(solution)/shard_map/last/pallas_call | solution.py:707
  (60 shorter events, 6.6 us)
Async XLA Ops:
  0.7 5.6 %copy-start.8 = (bf16[2,24,32,32]{3,2,1,0:T(8,128)(2,1)S(1)}, bf16[2,24,32,32]{3,2,1,0:T(8,128)(2,1)}, u32[]{:S(2)}) copy-start(bf16[2,24,32,32]{3,2,1,0:T(8,128)(2,1)} %group.1) | copy-start | bytes 294916
  1.7 12.2 %collective-permute-start = (bf16[7,32,256]{2,1,0:T(8,128)(2,1)S(1)}, bf16[7,32,256]{2,1,0:T(8,128)(2,1)S(1)}, u32[]{:S(2)}, u32[]{:S(2)}) collective-permute-start(bf16[7,32,256]{2,1,0:T(8,128)(2,1)S(1)} %get-tuple-element.39), channel_id=1, source_target_pairs={{0,8},{8,0},{16,24},{24,16},{1,9},{9,1},{17,25},{25,17},{2,10},{10... | collective-permute-start | bytes 344072 | tf_op jit(solution)/shard_map/ppermute | solution.py:542
  2.2 11.6 %collective-permute-start.1 = (bf16[7,32,256]{2,1,0:T(8,128)(2,1)S(1)}, bf16[7,32,256]{2,1,0:T(8,128)(2,1)S(1)}, u32[]{:S(2)}, u32[]{:S(2)}) collective-permute-start(bf16[7,32,256]{2,1,0:T(8,128)(2,1)S(1)} %get-tuple-element.38), channel_id=1, source_target_pairs={{8,16},{16,8},{9,17},{17,9},{10,18},{18,10},{11,19},{19,11},{12,20... | collective-permute-start | bytes 344072 | tf_op jit(solution)/shard_map/ppermute | solution.py:542
  3.0 7.3 %collective-permute-start.2 = (bf16[8,8,256]{2,1,0:T(8,128)(2,1)S(1)}, bf16[8,8,256]{2,1,0:T(8,128)(2,1)S(1)}, u32[]{:S(2)}, u32[]{:S(2)}) collective-permute-start(bf16[8,8,256]{2,1,0:T(8,128)(2,1)S(1)} %get-tuple-element.37), channel_id=1, source_target_pairs={{0,1},{1,0},{2,3},{3,2},{4,5},{5,4},{6,7},{7,6},{8,9},{9,8},{10,11... | collective-permute-start | bytes 98312 | tf_op jit(solution)/shard_map/ppermute | solution.py:542
  5.6 4.7 %collective-permute-start.3 = (bf16[8,8,256]{2,1,0:T(8,128)(2,1)S(1)}, bf16[8,8,256]{2,1,0:T(8,128)(2,1)S(1)}, u32[]{:S(2)}, u32[]{:S(2)}) collective-permute-start(bf16[8,8,256]{2,1,0:T(8,128)(2,1)S(1)} %get-tuple-element.36), channel_id=1, source_target_pairs={{1,2},{2,1},{3,4},{4,3},{5,6},{6,5},{9,10},{10,9},{11,12},{12,11},... | collective-permute-start | bytes 98312 | tf_op jit(solution)/shard_map/ppermute | solution.py:542
  8.3 5.5 %copy-start = (bf16[2,256,1024]{2,1,0:T(8,128)(2,1)S(1)}, bf16[2,256,1024]{2,1,0:T(8,128)(2,1)}, u32[]{:S(2)}) copy-start(bf16[2,256,1024]{2,1,0:T(8,128)(2,1)} %refs_0_.3) | copy-start | bytes 3145732
  8.3 5.5 %copy-start.1 = (bf16[2,1024,256]{2,1,0:T(8,128)(2,1)S(1)}, bf16[2,1024,256]{2,1,0:T(8,128)(2,1)}, u32[]{:S(2)}) copy-start(bf16[2,1024,256]{2,1,0:T(8,128)(2,1)} %refs_4_.3) | copy-start | bytes 3145732
  10.3 3.6 %copy-start.4 = (f32[2,3,3,1024]{3,0,2,1:T(2,128)S(1)}, f32[2,3,3,1024]{3,0,2,1:T(2,128)}, u32[]{:S(2)}) copy-start(f32[2,3,3,1024]{3,0,2,1:T(2,128)} %param.17) | copy-start | bytes 221188
  10.3 3.5 %collective-permute-start.4 = (bf16[14,8,256]{2,1,0:T(8,128)(2,1)S(1)}, bf16[14,8,256]{2,1,0:T(8,128)(2,1)S(1)}, u32[]{:S(2)}, u32[]{:S(2)}) collective-permute-start(bf16[14,8,256]{2,1,0:T(8,128)(2,1)S(1)} %pad_maximum_fusion), channel_id=1, source_target_pairs={{0,8},{8,0},{16,24},{24,16},{1,9},{9,1},{17,25},{25,17},{2,10},{10... | collective-permute-start | bytes 172040 | tf_op jit(solution)/shard_map/ppermute | solution.py:542
  13.0 0.9 %collective-permute-start.5 = (bf16[14,8,256]{2,1,0:T(8,128)(2,1)S(1)}, bf16[14,8,256]{2,1,0:T(8,128)(2,1)S(1)}, u32[]{:S(2)}, u32[]{:S(2)}) collective-permute-start(bf16[14,8,256]{2,1,0:T(8,128)(2,1)S(1)} %pad_maximum_fusion.1), channel_id=1, source_target_pairs={{8,16},{16,8},{9,17},{17,9},{10,18},{18,10},{11,19},{19,11},{12,20... | collective-permute-start | bytes 172040 | tf_op jit(solution)/shard_map/ppermute | solution.py:542
  22.7 6.3 %collective-permute-start.8 = (bf16[144,128]{1,0:T(8,128)(2,1)S(1)}, bf16[144,128]{1,0:T(8,128)(2,1)S(1)}, u32[]{:S(2)}, u32[]{:S(2)}) collective-permute-start(bf16[144,128]{1,0:T(8,128)(2,1)S(1)} %get-tuple-element.29), channel_id=1, source_target_pairs={{0,24},{8,16},{16,8},{24,0},{1,25},{9,17},{17,9},{25,1},{2,26},{10... | collective-permute-start | bytes 110600 | tf_op jit(solution)/shard_map/ppermute | solution.py:516
  23.7 8.0 %collective-permute-start.7 = (bf16[144,128]{1,0:T(8,128)(2,1)S(1)}, bf16[144,128]{1,0:T(8,128)(2,1)S(1)}, u32[]{:S(2)}, u32[]{:S(2)}) collective-permute-start(bf16[144,128]{1,0:T(8,128)(2,1)S(1)} %get-tuple-element.29), channel_id=1, source_target_pairs={{0,16},{8,24},{16,0},{24,8},{1,17},{9,25},{17,1},{25,9},{2,18},{10... | collective-permute-start | bytes 110600 | tf_op jit(solution)/shard_map/ppermute | solution.py:516
  29.0 2.7 %collective-permute-start.6 = (bf16[144,128]{1,0:T(8,128)(2,1)S(1)}, bf16[144,128]{1,0:T(8,128)(2,1)S(1)}, u32[]{:S(2)}, u32[]{:S(2)}) collective-permute-start(bf16[144,128]{1,0:T(8,128)(2,1)S(1)} %get-tuple-element.29), channel_id=1, source_target_pairs={{0,8},{8,0},{16,24},{24,16},{1,9},{9,1},{17,25},{25,17},{2,10},{10... | collective-permute-start | bytes 110600 | tf_op jit(solution)/shard_map/ppermute | solution.py:516
  31.8 7.0 %collective-permute-start.11 = (bf16[144,128]{1,0:T(8,128)(2,1)S(1)}, bf16[144,128]{1,0:T(8,128)(2,1)S(1)}, u32[]{:S(2)}, u32[]{:S(2)}) collective-permute-start(bf16[144,128]{1,0:T(8,128)(2,1)S(1)} %add_convert_fusion.3), channel_id=1, source_target_pairs={{0,3},{1,2},{2,1},{3,0},{4,7},{5,6},{6,5},{7,4},{8,11},{9,10},{10,... | collective-permute-start | bytes 110600 | tf_op jit(solution)/shard_map/ppermute | solution.py:516
  36.7 4.0 %collective-permute-start.10 = (bf16[144,128]{1,0:T(8,128)(2,1)S(1)}, bf16[144,128]{1,0:T(8,128)(2,1)S(1)}, u32[]{:S(2)}, u32[]{:S(2)}) collective-permute-start(bf16[144,128]{1,0:T(8,128)(2,1)S(1)} %add_convert_fusion.3), channel_id=1, source_target_pairs={{0,2},{1,3},{2,0},{3,1},{4,6},{5,7},{6,4},{7,5},{8,10},{9,11},{10,... | collective-permute-start | bytes 110600 | tf_op jit(solution)/shard_map/ppermute | solution.py:516
  37.1 4.0 %collective-permute-start.9 = (bf16[144,128]{1,0:T(8,128)(2,1)S(1)}, bf16[144,128]{1,0:T(8,128)(2,1)S(1)}, u32[]{:S(2)}, u32[]{:S(2)}) collective-permute-start(bf16[144,128]{1,0:T(8,128)(2,1)S(1)} %add_convert_fusion.3), channel_id=1, source_target_pairs={{0,1},{1,0},{2,3},{3,2},{4,5},{5,4},{6,7},{7,6},{8,9},{9,8},{10,11... | collective-permute-start | bytes 110600 | tf_op jit(solution)/shard_map/ppermute | solution.py:516
  41.1 5.7 %collective-permute-start.12 = (bf16[144,128]{1,0:T(8,128)(2,1)S(1)}, bf16[144,128]{1,0:T(8,128)(2,1)S(1)}, u32[]{:S(2)}, u32[]{:S(2)}) collective-permute-start(bf16[144,128]{1,0:T(8,128)(2,1)S(1)} %add_convert_fusion.2.payload), channel_id=1, source_target_pairs={{0,4},{1,5},{2,6},{3,7},{4,0},{5,1},{6,2},{7,3},{8,12},{9,13},{10,... | collective-permute-start | bytes 110600 | tf_op jit(solution)/shard_map/ppermute | solution.py:516
  56.2 3.8 %collective-permute-start.15 = (bf16[144,128]{1,0:T(8,128)(2,1)S(1)}, bf16[144,128]{1,0:T(8,128)(2,1)S(1)}, u32[]{:S(2)}, u32[]{:S(2)}) collective-permute-start(bf16[144,128]{1,0:T(8,128)(2,1)S(1)} %get-tuple-element.34), channel_id=1, source_target_pairs={{0,24},{8,16},{16,8},{24,0},{1,25},{9,17},{17,9},{25,1},{2,26},{10... | collective-permute-start | bytes 110600 | tf_op jit(solution)/shard_map/ppermute | solution.py:516
  56.3 4.1 %collective-permute-start.14 = (bf16[144,128]{1,0:T(8,128)(2,1)S(1)}, bf16[144,128]{1,0:T(8,128)(2,1)S(1)}, u32[]{:S(2)}, u32[]{:S(2)}) collective-permute-start(bf16[144,128]{1,0:T(8,128)(2,1)S(1)} %get-tuple-element.34), channel_id=1, source_target_pairs={{0,16},{8,24},{16,0},{24,8},{1,17},{9,25},{17,1},{25,9},{2,18},{10... | collective-permute-start | bytes 110600 | tf_op jit(solution)/shard_map/ppermute | solution.py:516
  57.8 2.7 %collective-permute-start.13 = (bf16[144,128]{1,0:T(8,128)(2,1)S(1)}, bf16[144,128]{1,0:T(8,128)(2,1)S(1)}, u32[]{:S(2)}, u32[]{:S(2)}) collective-permute-start(bf16[144,128]{1,0:T(8,128)(2,1)S(1)} %get-tuple-element.34), channel_id=1, source_target_pairs={{0,8},{8,0},{16,24},{24,16},{1,9},{9,1},{17,25},{25,17},{2,10},{10... | collective-permute-start | bytes 110600 | tf_op jit(solution)/shard_map/ppermute | solution.py:516
  60.5 5.0 %collective-permute-start.18 = (bf16[144,128]{1,0:T(8,128)(2,1)S(1)}, bf16[144,128]{1,0:T(8,128)(2,1)S(1)}, u32[]{:S(2)}, u32[]{:S(2)}) collective-permute-start(bf16[144,128]{1,0:T(8,128)(2,1)S(1)} %add_convert_fusion.1), channel_id=1, source_target_pairs={{0,3},{1,2},{2,1},{3,0},{4,7},{5,6},{6,5},{7,4},{8,11},{9,10},{10,... | collective-permute-start | bytes 110600 | tf_op jit(solution)/shard_map/ppermute | solution.py:516
  60.7 4.7 %collective-permute-start.17 = (bf16[144,128]{1,0:T(8,128)(2,1)S(1)}, bf16[144,128]{1,0:T(8,128)(2,1)S(1)}, u32[]{:S(2)}, u32[]{:S(2)}) collective-permute-start(bf16[144,128]{1,0:T(8,128)(2,1)S(1)} %add_convert_fusion.1), channel_id=1, source_target_pairs={{0,2},{1,3},{2,0},{3,1},{4,6},{5,7},{6,4},{7,5},{8,10},{9,11},{10,... | collective-permute-start | bytes 110600 | tf_op jit(solution)/shard_map/ppermute | solution.py:516
  62.0 4.0 %collective-permute-start.16 = (bf16[144,128]{1,0:T(8,128)(2,1)S(1)}, bf16[144,128]{1,0:T(8,128)(2,1)S(1)}, u32[]{:S(2)}, u32[]{:S(2)}) collective-permute-start(bf16[144,128]{1,0:T(8,128)(2,1)S(1)} %add_convert_fusion.1), channel_id=1, source_target_pairs={{0,1},{1,0},{2,3},{3,2},{4,5},{5,4},{6,7},{7,6},{8,9},{9,8},{10,11... | collective-permute-start | bytes 110600 | tf_op jit(solution)/shard_map/ppermute | solution.py:516
  66.0 5.3 %collective-permute-start.19 = (bf16[144,128]{1,0:T(8,128)(2,1)S(1)}, bf16[144,128]{1,0:T(8,128)(2,1)S(1)}, u32[]{:S(2)}, u32[]{:S(2)}) collective-permute-start(bf16[144,128]{1,0:T(8,128)(2,1)S(1)} %add_convert_fusion.payload), channel_id=1, source_target_pairs={{0,4},{1,5},{2,6},{3,7},{4,0},{5,1},{6,2},{7,3},{8,12},{9,13},{10,... | collective-permute-start | bytes 110600 | tf_op jit(solution)/shard_map/ppermute | solution.py:516
  (10 other events, 21.0 us)

commit v17 on v15

--- a/solution.py
+++ b/solution.py
@@ -404,7 +404,7 @@
 
 
 def first_kernel(
-    tile, head_dim, own, row_0, row_1, col_0, col_1, corner_0, corner_1, *refs
+    tile, head_dim, own, col_1, col_0, row_1, row_0, corner_1, corner_0, *refs
 ):
     weights, outs, scratch = refs[:9], refs[9:11], refs[11:]
     x_ref = scratch[0]
@@ -685,7 +685,7 @@
         + front_scratch(first_rows),
         compiler_params=params,
         name="first",
-    )(features, row_0, row_1, col_0, col_1, corner_0, corner_1, *weights)
+    )(features, col_1, col_0, row_1, row_0, corner_1, corner_0, *weights)
     query, mixed = queries(mixed, 0)
     payload, other = sum_by_permutes(payload)
 

time: 73.6 us -> 73.1 us (level)
  waiting for transfers between devices: 13.7 us -> 12.9 us
    ppermute x6, starting transfers between devices: 10.2 us -> 12.2 us  [pair_exchange(): return lax.ppermute(value, axis, pairs)]
    ppermute x6, waiting for transfers between devices: 1.9 us -> 0.02 us  [pair_exchange(): return lax.ppermute(value, axis, pairs)]
    ppermute x14, starting transfers between devices: 17.8 us -> 16.1 us  [sum_by_permutes(): lax.ppermute(value, axis, [(i, partner(i, stride, radix, k)) for i in ran...]
    ppermute x14, waiting for transfers between devices: 11.8 us -> 12.9 us  [sum_by_permutes(): lax.ppermute(value, axis, [(i, partner(i, stride, radix, k)) for i in ran...]
where the time goes in v17:
time: 73.1 us; the launch traced here: 72.8 us
  starting transfers between devices  28.3 us (39%)
  Pallas kernels  27.8 us (38%)
  waiting for transfers between devices  12.9 us (18%)
  local copies, waits for them, and re-layouts  2.61 us (4%)
  between operations  1.09 us (1%)
    ppermute x14, starting transfers between devices, sum_by_permutes(): lax.ppermute(value, axis, [(i, partner(i, stride, radix, k)) for i in ran...  16.1 us
    ppermute x14, waiting for transfers between devices, sum_by_permutes(): lax.ppermute(value, axis, [(i, partner(i, stride, radix, k)) for i in ran...  12.9 us
    ppermute x6, starting transfers between devices, pair_exchange(): return lax.ppermute(value, axis, pairs)  12.2 us
    pallas_call x1, Pallas kernels, local(): pl.pallas_call(functools.partial(second_kernel, tile, head_dim), out_shap...  9.4 us
    pallas_call x1, Pallas kernels, local(): pl.pallas_call(functools.partial(first_kernel, tile, head_dim), out_shape...  8.76 us
    pallas_call x2, Pallas kernels, queries(): pl.pallas_call(functools.partial(query_kernel, tile, section), out_shape=...  5.03 us
    pallas_call x1, Pallas kernels, local(): pl.pallas_call(functools.partial(last_kernel, tile, head_dim), out_shape=...  2.7 us
    pallas_call x1, Pallas kernels, local(): pl.pallas_call(functools.partial(prepare_kernel, head_dim), out_shape=mad...  1.92 us
  transfers between devices with their start and end apart: 20, of which 11 were waited for; matrix products, arithmetic and copies ran while one was open for 0% of the time, Pallas kernels for 10%

profile of v17, /device:TPU:0, one launch (start us, length us, event | category | flops | bytes accessed | tf_op | source)
XLA Modules:
  0.0 72.8 jit_solution(4124921779389520584)
XLA Ops:
  2.1 5.8 %collective-permute-start.1 = (bf16[8,8,256]{2,1,0:T(8,128)(2,1)S(1)}, bf16[8,8,256]{2,1,0:T(8,128)(2,1)S(1)}, u32[]{:S(2)}, u32[]{:S(2)}) collective-permute-start(bf16[8,8,256]{2,1,0:T(8,128)(2,1)S(1)} %get-tuple-element.32), channel_id=1, source_target_pairs={{0,1},{1,0},{2,3},{3,2},{4,5},{5,4},{6,7},{7,6},{8,9},{9,8},{10,11... | collective-permute-start | bytes 98312 | tf_op jit(solution)/shard_map/ppermute | solution.py:542
  8.8 2.9 %collective-permute-start.3 = (bf16[7,32,256]{2,1,0:T(8,128)(2,1)S(1)}, bf16[7,32,256]{2,1,0:T(8,128)(2,1)S(1)}, u32[]{:S(2)}, u32[]{:S(2)}) collective-permute-start(bf16[7,32,256]{2,1,0:T(8,128)(2,1)S(1)} %get-tuple-element.30), channel_id=1, source_target_pairs={{0,8},{8,0},{16,24},{24,16},{1,9},{9,1},{17,25},{25,17},{2,10},{10... | collective-permute-start | bytes 344072 | tf_op jit(solution)/shard_map/ppermute | solution.py:542
  12.5 1.4 %collective-permute-start.5 = (bf16[14,8,256]{2,1,0:T(8,128)(2,1)S(1)}, bf16[14,8,256]{2,1,0:T(8,128)(2,1)S(1)}, u32[]{:S(2)}, u32[]{:S(2)}) collective-permute-start(bf16[14,8,256]{2,1,0:T(8,128)(2,1)S(1)} %pad_maximum_fusion.1), channel_id=1, source_target_pairs={{0,8},{8,0},{16,24},{24,16},{1,9},{9,1},{17,25},{25,17},{2,10},{10... | collective-permute-start | bytes 172040 | tf_op jit(solution)/shard_map/ppermute | solution.py:542
  14.9 1.9 %prepare.1 = (bf16[2,256,768]{2,1,0:T(8,128)(2,1)S(1)}, f32[2,32,768]{2,1,0:T(8,128)S(1)}, bf16[2,3,256,256]{3,2,1,0:T(8,128)(2,1)S(1)}, bf16[3,128,256]{2,1,0:T...) custom-call(bf16[2,256,768]{2,1,0:T(8,128)(2,1)S(1)} %copy-done.7, f32[5,5,2,768]{3,2,1,0:T(2,128)S(1)} %bitcast.5, ...), custom_call_target="tpu_custom_call" | custom-call | flops 2000000000 | bytes 4000000 | tf_op jit(solution)/shard_map/prepare/pallas_call | solution.py:599
  17.5 8.8 %first.1 = (bf16[20,48,256]{2,1,0:T(8,128)(2,1)S(1)}, bf16[144,128]{1,0:T(8,128)(2,1)S(1)}) custom-call(bf16[8,32,256]{2,1,0:T(8,128)(2,1)S(1)} %copy-done.3, bf16[8,8,256]{2,1,0:T(8,128)(2,1)S(1)} %collective-permute-done.col_1, bf16[8,8,256]{2,1,0:T(8,128)(2,1)S(1)} %collective-permute-done.1.col_0, bf16[7,32,256]{2,1,0:T(8,128)(2,1)S(1)} %collective-permute-done.2.row_1, ...), custom_call_target="tpu_custom_call" | custom-call | tf_op jit(solution)/shard_map/first/pallas_call | solution.py:678
  26.2 1.8 %collective-permute-start.8 = (bf16[144,128]{1,0:T(8,128)(2,1)S(1)}, bf16[144,128]{1,0:T(8,128)(2,1)S(1)}, u32[]{:S(2)}, u32[]{:S(2)}) collective-permute-start(bf16[144,128]{1,0:T(8,128)(2,1)S(1)} %get-tuple-element.23), channel_id=1, source_target_pairs={{0,24},{8,16},{16,8},{24,0},{1,25},{9,17},{17,9},{25,1},{2,26},{10... | collective-permute-start | bytes 110600 | tf_op jit(solution)/shard_map/ppermute | solution.py:516
  28.6 1.3 %collective-permute-done.8 = bf16[144,128]{1,0:T(8,128)(2,1)S(1)} collective-permute-done((bf16[144,128]{1,0:T(8,128)(2,1)S(1)}, bf16[144,128]{1,0:T(8,128)(2,1)S(1)}, u32[]{:S(2)}, u32[]{:S(2)}) %collective-permute-start.8) | collective-permute-done | bytes 36896 | tf_op jit(solution)/shard_map/ppermute | solution.py:516
  29.9 2.1 %collective-permute-done.7 = bf16[144,128]{1,0:T(8,128)(2,1)S(1)} collective-permute-done((bf16[144,128]{1,0:T(8,128)(2,1)S(1)}, bf16[144,128]{1,0:T(8,128)(2,1)S(1)}, u32[]{:S(2)}, u32[]{:S(2)}) %collective-permute-start.7) | collective-permute-done | bytes 36896 | tf_op jit(solution)/shard_map/ppermute | solution.py:516
  32.1 1.8 %collective-permute-start.11 = (bf16[144,128]{1,0:T(8,128)(2,1)S(1)}, bf16[144,128]{1,0:T(8,128)(2,1)S(1)}, u32[]{:S(2)}, u32[]{:S(2)}) collective-permute-start(bf16[144,128]{1,0:T(8,128)(2,1)S(1)} %add_convert_fusion.3), channel_id=1, source_target_pairs={{0,3},{1,2},{2,1},{3,0},{4,7},{5,6},{6,5},{7,4},{8,11},{9,10},{10,... | collective-permute-start | bytes 110600 | tf_op jit(solution)/shard_map/ppermute | solution.py:516
  34.1 1.5 %collective-permute-start.9 = (bf16[144,128]{1,0:T(8,128)(2,1)S(1)}, bf16[144,128]{1,0:T(8,128)(2,1)S(1)}, u32[]{:S(2)}, u32[]{:S(2)}) collective-permute-start(bf16[144,128]{1,0:T(8,128)(2,1)S(1)} %add_convert_fusion.3), channel_id=1, source_target_pairs={{0,1},{1,0},{2,3},{3,2},{4,5},{5,4},{6,7},{7,6},{8,9},{9,8},{10,11... | collective-permute-start | bytes 110600 | tf_op jit(solution)/shard_map/ppermute | solution.py:516
  35.6 1.4 %collective-permute-done.11 = bf16[144,128]{1,0:T(8,128)(2,1)S(1)} collective-permute-done((bf16[144,128]{1,0:T(8,128)(2,1)S(1)}, bf16[144,128]{1,0:T(8,128)(2,1)S(1)}, u32[]{:S(2)}, u32[]{:S(2)}) %collective-permute-start.11) | collective-permute-done | bytes 36896 | tf_op jit(solution)/shard_map/ppermute | solution.py:516
  38.1 2.9 %collective-permute-start.12 = (bf16[144,128]{1,0:T(8,128)(2,1)S(1)}, bf16[144,128]{1,0:T(8,128)(2,1)S(1)}, u32[]{:S(2)}, u32[]{:S(2)}) collective-permute-start(bf16[144,128]{1,0:T(8,128)(2,1)S(1)} %add_convert_fusion.2.payload), channel_id=1, source_target_pairs={{0,4},{1,5},{2,6},{3,7},{4,0},{5,1},{6,2},{7,3},{8,12},{9,13},{10,... | collective-permute-start | bytes 110600 | tf_op jit(solution)/shard_map/ppermute | solution.py:516
  40.9 3.0 %queries.2 = (bf16[16,48,512]{2,1,0:T(8,128)(2,1)S(1)}, bf16[16,48,256]{2,1,0:T(8,128)(2,1)S(1)}) custom-call(bf16[20,48,256]{2,1,0:T(8,128)(2,1)S(1)} %get-tuple-element.20.mixed_in, bf16[2,256,768]{2,1,0:T(8,128)(2,1)S(1)} %get-tuple-element.17.refs_6_.qkv_weight, f32[2,32,768]{2,1,0:T(8,128)S(1)} %get-tuple-element.18.refs_7_.taps, ...), custom_call_target="tpu_custom_call" | custom-call | flops 402653184 | bytes 1572864 | tf_op jit(solution)/shard_map/queries/pallas_call | solution.py:652
  44.0 9.4 %second.1 = (bf16[14,48,256]{2,1,0:T(8,128)(2,1)S(1)}, bf16[144,128]{1,0:T(8,128)(2,1)S(1)}) custom-call(bf16[16,48,256]{2,1,0:T(8,128)(2,1)S(1)} %get-tuple-element.21.mixed, bf16[16,48,512]{2,1,0:T(8,128)(2,1)S(1)} %get-tuple-element.22.query, bf16[144,128]{1,0:T(8,128)(2,1)S(1)} %add_convert_fusion.2.payload, ...), custom_call_target="tpu_custom_call" | custom-call | tf_op jit(solution)/shard_map/second/pallas_call | solution.py:693
  53.5 1.4 %collective-permute-start.14 = (bf16[144,128]{1,0:T(8,128)(2,1)S(1)}, bf16[144,128]{1,0:T(8,128)(2,1)S(1)}, u32[]{:S(2)}, u32[]{:S(2)}) collective-permute-start(bf16[144,128]{1,0:T(8,128)(2,1)S(1)} %get-tuple-element.28), channel_id=1, source_target_pairs={{0,16},{8,24},{16,0},{24,8},{1,17},{9,25},{17,1},{25,9},{2,18},{10... | collective-permute-start | bytes 110600 | tf_op jit(solution)/shard_map/ppermute | solution.py:516
  55.3 1.9 %collective-permute-done.15 = bf16[144,128]{1,0:T(8,128)(2,1)S(1)} collective-permute-done((bf16[144,128]{1,0:T(8,128)(2,1)S(1)}, bf16[144,128]{1,0:T(8,128)(2,1)S(1)}, u32[]{:S(2)}, u32[]{:S(2)}) %collective-permute-start.15) | collective-permute-done | bytes 36896 | tf_op jit(solution)/shard_map/ppermute | solution.py:516
  57.7 1.5 %collective-permute-start.18 = (bf16[144,128]{1,0:T(8,128)(2,1)S(1)}, bf16[144,128]{1,0:T(8,128)(2,1)S(1)}, u32[]{:S(2)}, u32[]{:S(2)}) collective-permute-start(bf16[144,128]{1,0:T(8,128)(2,1)S(1)} %add_convert_fusion.1), channel_id=1, source_target_pairs={{0,3},{1,2},{2,1},{3,0},{4,7},{5,6},{6,5},{7,4},{8,11},{9,10},{10,... | collective-permute-start | bytes 110600 | tf_op jit(solution)/shard_map/ppermute | solution.py:516
  59.2 1.5 %collective-permute-start.17 = (bf16[144,128]{1,0:T(8,128)(2,1)S(1)}, bf16[144,128]{1,0:T(8,128)(2,1)S(1)}, u32[]{:S(2)}, u32[]{:S(2)}) collective-permute-start(bf16[144,128]{1,0:T(8,128)(2,1)S(1)} %add_convert_fusion.1), channel_id=1, source_target_pairs={{0,2},{1,3},{2,0},{3,1},{4,6},{5,7},{6,4},{7,5},{8,10},{9,11},{10,... | collective-permute-start | bytes 110600 | tf_op jit(solution)/shard_map/ppermute | solution.py:516
  61.3 1.5 %collective-permute-done.18 = bf16[144,128]{1,0:T(8,128)(2,1)S(1)} collective-permute-done((bf16[144,128]{1,0:T(8,128)(2,1)S(1)}, bf16[144,128]{1,0:T(8,128)(2,1)S(1)}, u32[]{:S(2)}, u32[]{:S(2)}) %collective-permute-start.18) | collective-permute-done | bytes 36896 | tf_op jit(solution)/shard_map/ppermute | solution.py:516
  63.1 1.5 %collective-permute-done.16 = bf16[144,128]{1,0:T(8,128)(2,1)S(1)} collective-permute-done((bf16[144,128]{1,0:T(8,128)(2,1)S(1)}, bf16[144,128]{1,0:T(8,128)(2,1)S(1)}, u32[]{:S(2)}, u32[]{:S(2)}) %collective-permute-start.16) | collective-permute-done | bytes 36896 | tf_op jit(solution)/shard_map/ppermute | solution.py:516
  64.7 1.8 %collective-permute-start.19 = (bf16[144,128]{1,0:T(8,128)(2,1)S(1)}, bf16[144,128]{1,0:T(8,128)(2,1)S(1)}, u32[]{:S(2)}, u32[]{:S(2)}) collective-permute-start(bf16[144,128]{1,0:T(8,128)(2,1)S(1)} %add_convert_fusion.payload), channel_id=1, source_target_pairs={{0,4},{1,5},{2,6},{3,7},{4,0},{5,1},{6,2},{7,3},{8,12},{9,13},{10,... | collective-permute-start | bytes 110600 | tf_op jit(solution)/shard_map/ppermute | solution.py:516
  66.6 2.0 %queries.3 = (bf16[10,48,512]{2,1,0:T(8,128)(2,1)S(1)}, bf16[10,48,256]{2,1,0:T(8,128)(2,1)S(1)}) custom-call(bf16[14,48,256]{2,1,0:T(8,128)(2,1)S(1)} %get-tuple-element.25.mixed_in, bf16[2,256,768]{2,1,0:T(8,128)(2,1)S(1)} %get-tuple-element.17.refs_6_.qkv_weight, f32[2,32,768]{2,1,0:T(8,128)S(1)} %get-tuple-element.18.refs_7_.taps, ...), custom_call_target="tpu_custom_call" | custom-call | flops 251658240 | bytes 983040 | tf_op jit(solution)/shard_map/queries/pallas_call | solution.py:652
  68.6 1.3 %collective-permute-done.19.other = bf16[144,128]{1,0:T(8,128)(2,1)S(1)} collective-permute-done((bf16[144,128]{1,0:T(8,128)(2,1)S(1)}, bf16[144,128]{1,0:T(8,128)(2,1)S(1)}, u32[]{:S(2)}, u32[]{:S(2)}) %collective-permute-start.19) | collective-permute-done | bytes 36896 | tf_op jit(solution)/shard_map/ppermute | solution.py:516
  70.0 2.7 %last.1 = (bf16[8,32,256]{2,1,0:T(8,128)(2,1)}, f32[4,8,32]{2,1,0:T(8,128)}) custom-call(bf16[10,48,256]{2,1,0:T(8,128)(2,1)S(1)} %get-tuple-element.26.mixed, bf16[10,48,512]{2,1,0:T(8,128)(2,1)S(1)} %get-tuple-element.27.query, bf16[144,128]{1,0:T(8,128)(2,1)S(1)} %add_convert_fusion.payload, bf16[144,128]{1,0:T(8,128)(2,1)S(1)} %collective-permute-done.19.other, ...), custom_call_target="tpu_custom_call" | custom-call | tf_op jit(solution)/shard_map/last/pallas_call | solution.py:706
  (61 shorter events, 8.5 us)
Async XLA Ops:
  0.6 7.3 %copy-start.3 = (bf16[8,32,256]{2,1,0:T(8,128)(2,1)S(1)}, bf16[8,32,256]{2,1,0:T(8,128)(2,1)}, u32[]{:S(2)}) copy-start(bf16[8,32,256]{2,1,0:T(8,128)(2,1)} %own.1) | copy-start | bytes 393220
  0.7 13.2 %copy-start.10 = (bf16[3,3,4,256]{3,2,1,0:T(4,128)(2,1)S(1)}, bf16[3,3,4,256]{3,2,1,0:T(4,128)(2,1)}, u32[]{:S(2)}) copy-start(bf16[3,3,4,256]{3,2,1,0:T(4,128)(2,1)} %head.1) | copy-start | bytes 55300
  1.5 10.2 %collective-permute-start = (bf16[8,8,256]{2,1,0:T(8,128)(2,1)S(1)}, bf16[8,8,256]{2,1,0:T(8,128)(2,1)S(1)}, u32[]{:S(2)}, u32[]{:S(2)}) collective-permute-start(bf16[8,8,256]{2,1,0:T(8,128)(2,1)S(1)} %get-tuple-element.33), channel_id=1, source_target_pairs={{1,2},{2,1},{3,4},{4,3},{5,6},{6,5},{9,10},{10,9},{11,12},{12,11},... | collective-permute-start | bytes 98312 | tf_op jit(solution)/shard_map/ppermute | solution.py:542
  2.1 9.6 %collective-permute-start.1 = (bf16[8,8,256]{2,1,0:T(8,128)(2,1)S(1)}, bf16[8,8,256]{2,1,0:T(8,128)(2,1)S(1)}, u32[]{:S(2)}, u32[]{:S(2)}) collective-permute-start(bf16[8,8,256]{2,1,0:T(8,128)(2,1)S(1)} %get-tuple-element.32), channel_id=1, source_target_pairs={{0,1},{1,0},{2,3},{3,2},{4,5},{5,4},{6,7},{7,6},{8,9},{9,8},{10,11... | collective-permute-start | bytes 98312 | tf_op jit(solution)/shard_map/ppermute | solution.py:542
  7.9 5.9 %copy-start.9 = (f32[2,5,5,768]{3,0,2,1:T(2,128)S(1)}, f32[2,5,5,768]{3,0,2,1:T(2,128)}, u32[]{:S(2)}) copy-start(f32[2,5,5,768]{3,0,2,1:T(2,128)} %param.22) | copy-start | bytes 460804
  7.9 5.9 %copy-start.7 = (bf16[2,256,768]{2,1,0:T(8,128)(2,1)S(1)}, bf16[2,256,768]{2,1,0:T(8,128)(2,1)}, u32[]{:S(2)}) copy-start(bf16[2,256,768]{2,1,0:T(8,128)(2,1)} %qkv.1) | copy-start | bytes 2359300
  8.0 8.8 %collective-permute-start.2 = (bf16[7,32,256]{2,1,0:T(8,128)(2,1)S(1)}, bf16[7,32,256]{2,1,0:T(8,128)(2,1)S(1)}, u32[]{:S(2)}, u32[]{:S(2)}) collective-permute-start(bf16[7,32,256]{2,1,0:T(8,128)(2,1)S(1)} %get-tuple-element.31), channel_id=1, source_target_pairs={{8,16},{16,8},{9,17},{17,9},{10,18},{18,10},{11,19},{19,11},{12,20... | collective-permute-start | bytes 344072 | tf_op jit(solution)/shard_map/ppermute | solution.py:542
  8.8 8.0 %collective-permute-start.3 = (bf16[7,32,256]{2,1,0:T(8,128)(2,1)S(1)}, bf16[7,32,256]{2,1,0:T(8,128)(2,1)S(1)}, u32[]{:S(2)}, u32[]{:S(2)}) collective-permute-start(bf16[7,32,256]{2,1,0:T(8,128)(2,1)S(1)} %get-tuple-element.30), channel_id=1, source_target_pairs={{0,8},{8,0},{16,24},{24,16},{1,9},{9,1},{17,25},{25,17},{2,10},{10... | collective-permute-start | bytes 344072 | tf_op jit(solution)/shard_map/ppermute | solution.py:542
  11.7 5.0 %collective-permute-start.4 = (bf16[14,8,256]{2,1,0:T(8,128)(2,1)S(1)}, bf16[14,8,256]{2,1,0:T(8,128)(2,1)S(1)}, u32[]{:S(2)}, u32[]{:S(2)}) collective-permute-start(bf16[14,8,256]{2,1,0:T(8,128)(2,1)S(1)} %pad_maximum_fusion), channel_id=1, source_target_pairs={{8,16},{16,8},{9,17},{17,9},{10,18},{18,10},{11,19},{19,11},{12,20... | collective-permute-start | bytes 172040 | tf_op jit(solution)/shard_map/ppermute | solution.py:542
  12.5 4.3 %collective-permute-start.5 = (bf16[14,8,256]{2,1,0:T(8,128)(2,1)S(1)}, bf16[14,8,256]{2,1,0:T(8,128)(2,1)S(1)}, u32[]{:S(2)}, u32[]{:S(2)}) collective-permute-start(bf16[14,8,256]{2,1,0:T(8,128)(2,1)S(1)} %pad_maximum_fusion.1), channel_id=1, source_target_pairs={{0,8},{8,0},{16,24},{24,16},{1,9},{9,1},{17,25},{25,17},{2,10},{10... | collective-permute-start | bytes 172040 | tf_op jit(solution)/shard_map/ppermute | solution.py:542
  26.2 3.7 %collective-permute-start.8 = (bf16[144,128]{1,0:T(8,128)(2,1)S(1)}, bf16[144,128]{1,0:T(8,128)(2,1)S(1)}, u32[]{:S(2)}, u32[]{:S(2)}) collective-permute-start(bf16[144,128]{1,0:T(8,128)(2,1)S(1)} %get-tuple-element.23), channel_id=1, source_target_pairs={{0,24},{8,16},{16,8},{24,0},{1,25},{9,17},{17,9},{25,1},{2,26},{10... | collective-permute-start | bytes 110600 | tf_op jit(solution)/shard_map/ppermute | solution.py:516
  28.1 4.0 %collective-permute-start.7 = (bf16[144,128]{1,0:T(8,128)(2,1)S(1)}, bf16[144,128]{1,0:T(8,128)(2,1)S(1)}, u32[]{:S(2)}, u32[]{:S(2)}) collective-permute-start(bf16[144,128]{1,0:T(8,128)(2,1)S(1)} %get-tuple-element.23), channel_id=1, source_target_pairs={{0,16},{8,24},{16,0},{24,8},{1,17},{9,25},{17,1},{25,9},{2,18},{10... | collective-permute-start | bytes 110600 | tf_op jit(solution)/shard_map/ppermute | solution.py:516
  28.6 3.5 %collective-permute-start.6 = (bf16[144,128]{1,0:T(8,128)(2,1)S(1)}, bf16[144,128]{1,0:T(8,128)(2,1)S(1)}, u32[]{:S(2)}, u32[]{:S(2)}) collective-permute-start(bf16[144,128]{1,0:T(8,128)(2,1)S(1)} %get-tuple-element.23), channel_id=1, source_target_pairs={{0,8},{8,0},{16,24},{24,16},{1,9},{9,1},{17,25},{25,17},{2,10},{10... | collective-permute-start | bytes 110600 | tf_op jit(solution)/shard_map/ppermute | solution.py:516
  32.1 5.0 %collective-permute-start.11 = (bf16[144,128]{1,0:T(8,128)(2,1)S(1)}, bf16[144,128]{1,0:T(8,128)(2,1)S(1)}, u32[]{:S(2)}, u32[]{:S(2)}) collective-permute-start(bf16[144,128]{1,0:T(8,128)(2,1)S(1)} %add_convert_fusion.3), channel_id=1, source_target_pairs={{0,3},{1,2},{2,1},{3,0},{4,7},{5,6},{6,5},{7,4},{8,11},{9,10},{10,... | collective-permute-start | bytes 110600 | tf_op jit(solution)/shard_map/ppermute | solution.py:516
  33.8 4.0 %collective-permute-start.10 = (bf16[144,128]{1,0:T(8,128)(2,1)S(1)}, bf16[144,128]{1,0:T(8,128)(2,1)S(1)}, u32[]{:S(2)}, u32[]{:S(2)}) collective-permute-start(bf16[144,128]{1,0:T(8,128)(2,1)S(1)} %add_convert_fusion.3), channel_id=1, source_target_pairs={{0,2},{1,3},{2,0},{3,1},{4,6},{5,7},{6,4},{7,5},{8,10},{9,11},{10,... | collective-permute-start | bytes 110600 | tf_op jit(solution)/shard_map/ppermute | solution.py:516
  34.1 4.0 %collective-permute-start.9 = (bf16[144,128]{1,0:T(8,128)(2,1)S(1)}, bf16[144,128]{1,0:T(8,128)(2,1)S(1)}, u32[]{:S(2)}, u32[]{:S(2)}) collective-permute-start(bf16[144,128]{1,0:T(8,128)(2,1)S(1)} %add_convert_fusion.3), channel_id=1, source_target_pairs={{0,1},{1,0},{2,3},{3,2},{4,5},{5,4},{6,7},{7,6},{8,9},{9,8},{10,11... | collective-permute-start | bytes 110600 | tf_op jit(solution)/shard_map/ppermute | solution.py:516
  38.1 5.9 %collective-permute-start.12 = (bf16[144,128]{1,0:T(8,128)(2,1)S(1)}, bf16[144,128]{1,0:T(8,128)(2,1)S(1)}, u32[]{:S(2)}, u32[]{:S(2)}) collective-permute-start(bf16[144,128]{1,0:T(8,128)(2,1)S(1)} %add_convert_fusion.2.payload), channel_id=1, source_target_pairs={{0,4},{1,5},{2,6},{3,7},{4,0},{5,1},{6,2},{7,3},{8,12},{9,13},{10,... | collective-permute-start | bytes 110600 | tf_op jit(solution)/shard_map/ppermute | solution.py:516
  53.4 3.8 %collective-permute-start.15 = (bf16[144,128]{1,0:T(8,128)(2,1)S(1)}, bf16[144,128]{1,0:T(8,128)(2,1)S(1)}, u32[]{:S(2)}, u32[]{:S(2)}) collective-permute-start(bf16[144,128]{1,0:T(8,128)(2,1)S(1)} %get-tuple-element.28), channel_id=1, source_target_pairs={{0,24},{8,16},{16,8},{24,0},{1,25},{9,17},{17,9},{25,1},{2,26},{10... | collective-permute-start | bytes 110600 | tf_op jit(solution)/shard_map/ppermute | solution.py:516
  53.5 4.2 %collective-permute-start.14 = (bf16[144,128]{1,0:T(8,128)(2,1)S(1)}, bf16[144,128]{1,0:T(8,128)(2,1)S(1)}, u32[]{:S(2)}, u32[]{:S(2)}) collective-permute-start(bf16[144,128]{1,0:T(8,128)(2,1)S(1)} %get-tuple-element.28), channel_id=1, source_target_pairs={{0,16},{8,24},{16,0},{24,8},{1,17},{9,25},{17,1},{25,9},{2,18},{10... | collective-permute-start | bytes 110600 | tf_op jit(solution)/shard_map/ppermute | solution.py:516
  54.9 2.8 %collective-permute-start.13 = (bf16[144,128]{1,0:T(8,128)(2,1)S(1)}, bf16[144,128]{1,0:T(8,128)(2,1)S(1)}, u32[]{:S(2)}, u32[]{:S(2)}) collective-permute-start(bf16[144,128]{1,0:T(8,128)(2,1)S(1)} %get-tuple-element.28), channel_id=1, source_target_pairs={{0,8},{8,0},{16,24},{24,16},{1,9},{9,1},{17,25},{25,17},{2,10},{10... | collective-permute-start | bytes 110600 | tf_op jit(solution)/shard_map/ppermute | solution.py:516
  57.7 5.0 %collective-permute-start.18 = (bf16[144,128]{1,0:T(8,128)(2,1)S(1)}, bf16[144,128]{1,0:T(8,128)(2,1)S(1)}, u32[]{:S(2)}, u32[]{:S(2)}) collective-permute-start(bf16[144,128]{1,0:T(8,128)(2,1)S(1)} %add_convert_fusion.1), channel_id=1, source_target_pairs={{0,3},{1,2},{2,1},{3,0},{4,7},{5,6},{6,5},{7,4},{8,11},{9,10},{10,... | collective-permute-start | bytes 110600 | tf_op jit(solution)/shard_map/ppermute | solution.py:516
  59.2 4.0 %collective-permute-start.17 = (bf16[144,128]{1,0:T(8,128)(2,1)S(1)}, bf16[144,128]{1,0:T(8,128)(2,1)S(1)}, u32[]{:S(2)}, u32[]{:S(2)}) collective-permute-start(bf16[144,128]{1,0:T(8,128)(2,1)S(1)} %add_convert_fusion.1), channel_id=1, source_target_pairs={{0,2},{1,3},{2,0},{3,1},{4,6},{5,7},{6,4},{7,5},{8,10},{9,11},{10,... | collective-permute-start | bytes 110600 | tf_op jit(solution)/shard_map/ppermute | solution.py:516
  60.7 4.0 %collective-permute-start.16 = (bf16[144,128]{1,0:T(8,128)(2,1)S(1)}, bf16[144,128]{1,0:T(8,128)(2,1)S(1)}, u32[]{:S(2)}, u32[]{:S(2)}) collective-permute-start(bf16[144,128]{1,0:T(8,128)(2,1)S(1)} %add_convert_fusion.1), channel_id=1, source_target_pairs={{0,1},{1,0},{2,3},{3,2},{4,5},{5,4},{6,7},{7,6},{8,9},{9,8},{10,11... | collective-permute-start | bytes 110600 | tf_op jit(solution)/shard_map/ppermute | solution.py:516
  64.7 5.3 %collective-permute-start.19 = (bf16[144,128]{1,0:T(8,128)(2,1)S(1)}, bf16[144,128]{1,0:T(8,128)(2,1)S(1)}, u32[]{:S(2)}, u32[]{:S(2)}) collective-permute-start(bf16[144,128]{1,0:T(8,128)(2,1)S(1)} %add_convert_fusion.payload), channel_id=1, source_target_pairs={{0,4},{1,5},{2,6},{3,7},{4,0},{5,1},{6,2},{7,3},{8,12},{9,13},{10,... | collective-permute-start | bytes 110600 | tf_op jit(solution)/shard_map/ppermute | solution.py:516
  (10 other events, 17.4 us)

commit v18 on v17

--- a/solution.py
+++ b/solution.py
@@ -18,8 +18,8 @@
 BF16 = jnp.bfloat16
 
 
-def six_hard_swish(value):
-    return value * jnp.minimum(jnp.maximum(value + 3.0, 0.0), 6.0)
+def six_hard_swish(value, bound=6.0):
+    return value * jnp.minimum(jnp.maximum(value + 3.0, 0.0), bound)
 
 
 def parted(count, parts):
@@ -60,6 +60,18 @@
     @pl.when(col == lax.axis_size("col") - 1)
     def _():
         ref[:, cols : cols + SIDE, :] = jnp.zeros((rows, SIDE, ref.shape[2]), ref.dtype)
+
+
+def set_bounds(bounds, cols):
+    shape = bounds.shape[1:]
+    column = lax.broadcasted_iota(jnp.int32, shape, 0)
+    row, col = lax.axis_index("row"), lax.axis_index("col")
+    start = jnp.where(col == lax.axis_size("col") - 1, cols, cols + SIDE)
+    stop = jnp.where(col == 0, cols + 2 * SIDE, cols + SIDE)
+    level = jnp.where((column >= start) & (column < stop), 0.0, 6.0)
+    bounds[0] = jnp.where(row == 0, 0.0, level).astype(BF16)
+    bounds[1] = level.astype(BF16)
+    bounds[2] = jnp.where(row == lax.axis_size("row") - 1, 0.0, level).astype(BF16)
 
 
 def flat(value):
@@ -114,7 +126,7 @@
     expand, expand_bias, depth, depth_bias, project = weights[:5]
     mixed_out, payload_out = outs
     (
-        hidden_0, hidden_1, total, mixed, pairs, wide_depth, wide_agg,
+        hidden_0, hidden_1, total, bounds, mixed, pairs, wide_depth, wide_agg,
         project_bias, pair_weight, agg, group, sems,
     ) = scratch
     channels = x_ref.shape[2]
@@ -135,6 +147,7 @@
     for index in range(9):
         taps = depth[index // 3, index % 3, section : section + 1, :] * (1.0 / 6.0)
         wide_depth[index] = jnp.broadcast_to(taps, (TILE, taps.shape[1])).astype(BF16)
+    set_bounds(bounds, tile_cols)
     total[...] = 6.0 * flat(x_ref[1 : rows - 1]).astype(F32)
 
     def expand_rows(out, at, first, size):
@@ -143,7 +156,10 @@
             preferred_element_type=F32,
         )
         value = (value + expand_bias[section : section + 1, pl.ds(at, chunk)]).astype(BF16)
-        out[first : first + size] = six_hard_swish(value).reshape(size, width, chunk)
+        for r in range(size):
+            which = 0 if first + r < halo else 2 if first + r >= rows - halo else 1
+            part = value[r * width : (r + 1) * width]
+            out[first + r] = six_hard_swish(part, bounds[which])
 
     def spread_rows(hidden, at, first, size):
         spread = []
@@ -168,20 +184,24 @@
         at = pl.multiple_of(index * chunk, chunk)
         ahead = pl.multiple_of(jnp.minimum(index + 1, chunks - 1) * chunk, chunk)
         for (first, size), (from_row, count) in zip(parted(inner, PARTS), parted(rows, PARTS)):
-            expand_rows(following, ahead, from_row, count)
+            if following is not None:
+                expand_rows(following, ahead, from_row, count)
             spread_rows(current, at, first, size)
-        clear_outside(following, halo, tile_cols)
 
     for first, size in parted(rows, PARTS):
         expand_rows(hidden_0, 0, first, size)
-    clear_outside(hidden_0, halo, tile_cols)
 
     def two_stages(index, carry):
         stage(2 * index, hidden_0, hidden_1)
         stage(2 * index + 1, hidden_1, hidden_0)
         return carry
 
-    lax.fori_loop(0, chunks // 2, two_stages, 0)
+    if section == 0:
+        for index in range(0, chunks, 2):
+            stage(index, hidden_0, hidden_1)
+            stage(index + 1, hidden_1, hidden_0 if index + 2 < chunks else None)
+    else:
+        lax.fori_loop(0, chunks // 2, two_stages, 0)
     loads[0].wait()
     value = total[...] * (1.0 / 6.0) + project_bias[section : section + 1, :]
     mixed[...] = value.astype(BF16).reshape(inner, width, channels)
@@ -628,6 +648,7 @@
             pltpu.VMEM((count, width, 256), BF16),
             pltpu.VMEM((count, width, 256), BF16),
             pltpu.VMEM(((count - 2) * width, channels), F32),
+            pltpu.VMEM((3, width, 256), BF16),
             pltpu.VMEM((count - 2, width, channels), BF16),
             pltpu.VMEM((rows + 4, width, 2 * channels), BF16),
             pltpu.VMEM((9, TILE, expand_weight.shape[2]), BF16),

time: 73.1 us -> 72.4 us (level)
  no operation moved by 1% of the time
where the time goes in v18:
time: 72.4 us; the launch traced here: 72.1 us
  starting transfers between devices  28.1 us (39%)
  Pallas kernels  27.2 us (38%)
  waiting for transfers between devices  13 us (18%)
  local copies, waits for them, and re-layouts  2.61 us (4%)
  between operations  1.09 us (2%)
    ppermute x14, starting transfers between devices, sum_by_permutes(): lax.ppermute(value, axis, [(i, partner(i, stride, radix, k)) for i in ran...  15.9 us
    ppermute x14, waiting for transfers between devices, sum_by_permutes(): lax.ppermute(value, axis, [(i, partner(i, stride, radix, k)) for i in ran...  13 us
    ppermute x6, starting transfers between devices, pair_exchange(): return lax.ppermute(value, axis, pairs)  12.2 us
    pallas_call x1, Pallas kernels, local(): pl.pallas_call(functools.partial(second_kernel, tile, head_dim), out_shap...  9.07 us
    pallas_call x1, Pallas kernels, local(): pl.pallas_call(functools.partial(first_kernel, tile, head_dim), out_shape...  8.29 us
    pallas_call x2, Pallas kernels, queries(): pl.pallas_call(functools.partial(query_kernel, tile, section), out_shape=...  5.21 us
    pallas_call x1, Pallas kernels, local(): pl.pallas_call(functools.partial(last_kernel, tile, head_dim), out_shape=...  2.7 us
    pallas_call x1, Pallas kernels, local(): pl.pallas_call(functools.partial(prepare_kernel, head_dim), out_shape=mad...  1.92 us
  transfers between devices with their start and end apart: 20, of which 11 were waited for; matrix products, arithmetic and copies ran while one was open for 0% of the time, Pallas kernels for 10%

profile of v18, /device:TPU:0, one launch (start us, length us, event | category | flops | bytes accessed | tf_op | source)
XLA Modules:
  0.0 72.1 jit_solution(18357557886301886834)
XLA Ops:
  2.1 5.8 %collective-permute-start.1 = (bf16[8,8,256]{2,1,0:T(8,128)(2,1)S(1)}, bf16[8,8,256]{2,1,0:T(8,128)(2,1)S(1)}, u32[]{:S(2)}, u32[]{:S(2)}) collective-permute-start(bf16[8,8,256]{2,1,0:T(8,128)(2,1)S(1)} %get-tuple-element.32), channel_id=1, source_target_pairs={{0,1},{1,0},{2,3},{3,2},{4,5},{5,4},{6,7},{7,6},{8,9},{9,8},{10,11... | collective-permute-start | bytes 98312 | tf_op jit(solution)/shard_map/ppermute | solution.py:562
  8.8 2.9 %collective-permute-start.3 = (bf16[7,32,256]{2,1,0:T(8,128)(2,1)S(1)}, bf16[7,32,256]{2,1,0:T(8,128)(2,1)S(1)}, u32[]{:S(2)}, u32[]{:S(2)}) collective-permute-start(bf16[7,32,256]{2,1,0:T(8,128)(2,1)S(1)} %get-tuple-element.30), channel_id=1, source_target_pairs={{0,8},{8,0},{16,24},{24,16},{1,9},{9,1},{17,25},{25,17},{2,10},{10... | collective-permute-start | bytes 344072 | tf_op jit(solution)/shard_map/ppermute | solution.py:562
  12.5 1.4 %collective-permute-start.5 = (bf16[14,8,256]{2,1,0:T(8,128)(2,1)S(1)}, bf16[14,8,256]{2,1,0:T(8,128)(2,1)S(1)}, u32[]{:S(2)}, u32[]{:S(2)}) collective-permute-start(bf16[14,8,256]{2,1,0:T(8,128)(2,1)S(1)} %pad_maximum_fusion.1), channel_id=1, source_target_pairs={{0,8},{8,0},{16,24},{24,16},{1,9},{9,1},{17,25},{25,17},{2,10},{10... | collective-permute-start | bytes 172040 | tf_op jit(solution)/shard_map/ppermute | solution.py:562
  14.9 1.9 %prepare.1 = (bf16[2,256,768]{2,1,0:T(8,128)(2,1)S(1)}, f32[2,32,768]{2,1,0:T(8,128)S(1)}, bf16[2,3,256,256]{3,2,1,0:T(8,128)(2,1)S(1)}, bf16[3,128,256]{2,1,0:T...) custom-call(bf16[2,256,768]{2,1,0:T(8,128)(2,1)S(1)} %copy-done.7, f32[5,5,2,768]{3,2,1,0:T(2,128)S(1)} %bitcast.5, ...), custom_call_target="tpu_custom_call" | custom-call | flops 2000000000 | bytes 4000000 | tf_op jit(solution)/shard_map/prepare/pallas_call | solution.py:619
  17.5 8.3 %first.1 = (bf16[20,48,256]{2,1,0:T(8,128)(2,1)S(1)}, bf16[144,128]{1,0:T(8,128)(2,1)S(1)}) custom-call(bf16[8,32,256]{2,1,0:T(8,128)(2,1)S(1)} %copy-done.3, bf16[8,8,256]{2,1,0:T(8,128)(2,1)S(1)} %collective-permute-done.col_1, bf16[8,8,256]{2,1,0:T(8,128)(2,1)S(1)} %collective-permute-done.1.col_0, bf16[7,32,256]{2,1,0:T(8,128)(2,1)S(1)} %collective-permute-done.2.row_1, ...), custom_call_target="tpu_custom_call" | custom-call | tf_op jit(solution)/shard_map/first/pallas_call | solution.py:699
  25.8 1.8 %collective-permute-start.8 = (bf16[144,128]{1,0:T(8,128)(2,1)S(1)}, bf16[144,128]{1,0:T(8,128)(2,1)S(1)}, u32[]{:S(2)}, u32[]{:S(2)}) collective-permute-start(bf16[144,128]{1,0:T(8,128)(2,1)S(1)} %get-tuple-element.23), channel_id=1, source_target_pairs={{0,24},{8,16},{16,8},{24,0},{1,25},{9,17},{17,9},{25,1},{2,26},{10... | collective-permute-start | bytes 110600 | tf_op jit(solution)/shard_map/ppermute | solution.py:536
  28.1 1.3 %collective-permute-done.8 = bf16[144,128]{1,0:T(8,128)(2,1)S(1)} collective-permute-done((bf16[144,128]{1,0:T(8,128)(2,1)S(1)}, bf16[144,128]{1,0:T(8,128)(2,1)S(1)}, u32[]{:S(2)}, u32[]{:S(2)}) %collective-permute-start.8) | collective-permute-done | bytes 36896 | tf_op jit(solution)/shard_map/ppermute | solution.py:536
  29.4 2.1 %collective-permute-done.7 = bf16[144,128]{1,0:T(8,128)(2,1)S(1)} collective-permute-done((bf16[144,128]{1,0:T(8,128)(2,1)S(1)}, bf16[144,128]{1,0:T(8,128)(2,1)S(1)}, u32[]{:S(2)}, u32[]{:S(2)}) %collective-permute-start.7) | collective-permute-done | bytes 36896 | tf_op jit(solution)/shard_map/ppermute | solution.py:536
  31.6 1.9 %collective-permute-start.11 = (bf16[144,128]{1,0:T(8,128)(2,1)S(1)}, bf16[144,128]{1,0:T(8,128)(2,1)S(1)}, u32[]{:S(2)}, u32[]{:S(2)}) collective-permute-start(bf16[144,128]{1,0:T(8,128)(2,1)S(1)} %add_convert_fusion.3), channel_id=1, source_target_pairs={{0,3},{1,2},{2,1},{3,0},{4,7},{5,6},{6,5},{7,4},{8,11},{9,10},{10,... | collective-permute-start | bytes 110600 | tf_op jit(solution)/shard_map/ppermute | solution.py:536
  33.7 1.5 %collective-permute-start.9 = (bf16[144,128]{1,0:T(8,128)(2,1)S(1)}, bf16[144,128]{1,0:T(8,128)(2,1)S(1)}, u32[]{:S(2)}, u32[]{:S(2)}) collective-permute-start(bf16[144,128]{1,0:T(8,128)(2,1)S(1)} %add_convert_fusion.3), channel_id=1, source_target_pairs={{0,1},{1,0},{2,3},{3,2},{4,5},{5,4},{6,7},{7,6},{8,9},{9,8},{10,11... | collective-permute-start | bytes 110600 | tf_op jit(solution)/shard_map/ppermute | solution.py:536
  35.1 1.5 %collective-permute-done.11 = bf16[144,128]{1,0:T(8,128)(2,1)S(1)} collective-permute-done((bf16[144,128]{1,0:T(8,128)(2,1)S(1)}, bf16[144,128]{1,0:T(8,128)(2,1)S(1)}, u32[]{:S(2)}, u32[]{:S(2)}) %collective-permute-start.11) | collective-permute-done | bytes 36896 | tf_op jit(solution)/shard_map/ppermute | solution.py:536
  37.6 2.9 %collective-permute-start.12 = (bf16[144,128]{1,0:T(8,128)(2,1)S(1)}, bf16[144,128]{1,0:T(8,128)(2,1)S(1)}, u32[]{:S(2)}, u32[]{:S(2)}) collective-permute-start(bf16[144,128]{1,0:T(8,128)(2,1)S(1)} %add_convert_fusion.2.payload), channel_id=1, source_target_pairs={{0,4},{1,5},{2,6},{3,7},{4,0},{5,1},{6,2},{7,3},{8,12},{9,13},{10,... | collective-permute-start | bytes 110600 | tf_op jit(solution)/shard_map/ppermute | solution.py:536
  40.5 3.2 %queries.2 = (bf16[16,48,512]{2,1,0:T(8,128)(2,1)S(1)}, bf16[16,48,256]{2,1,0:T(8,128)(2,1)S(1)}) custom-call(bf16[20,48,256]{2,1,0:T(8,128)(2,1)S(1)} %get-tuple-element.20.mixed_in, bf16[2,256,768]{2,1,0:T(8,128)(2,1)S(1)} %get-tuple-element.17.refs_6_.qkv_weight, f32[2,32,768]{2,1,0:T(8,128)S(1)} %get-tuple-element.18.refs_7_.taps, ...), custom_call_target="tpu_custom_call" | custom-call | flops 402653184 | bytes 1572864 | tf_op jit(solution)/shard_map/queries/pallas_call | solution.py:673
  43.8 9.1 %second.1 = (bf16[14,48,256]{2,1,0:T(8,128)(2,1)S(1)}, bf16[144,128]{1,0:T(8,128)(2,1)S(1)}) custom-call(bf16[16,48,256]{2,1,0:T(8,128)(2,1)S(1)} %get-tuple-element.21.mixed, bf16[16,48,512]{2,1,0:T(8,128)(2,1)S(1)} %get-tuple-element.22.query, bf16[144,128]{1,0:T(8,128)(2,1)S(1)} %add_convert_fusion.2.payload, ...), custom_call_target="tpu_custom_call" | custom-call | tf_op jit(solution)/shard_map/second/pallas_call | solution.py:714
  52.9 1.4 %collective-permute-start.14 = (bf16[144,128]{1,0:T(8,128)(2,1)S(1)}, bf16[144,128]{1,0:T(8,128)(2,1)S(1)}, u32[]{:S(2)}, u32[]{:S(2)}) collective-permute-start(bf16[144,128]{1,0:T(8,128)(2,1)S(1)} %get-tuple-element.28), channel_id=1, source_target_pairs={{0,16},{8,24},{16,0},{24,8},{1,17},{9,25},{17,1},{25,9},{2,18},{10... | collective-permute-start | bytes 110600 | tf_op jit(solution)/shard_map/ppermute | solution.py:536
  54.8 1.9 %collective-permute-done.15 = bf16[144,128]{1,0:T(8,128)(2,1)S(1)} collective-permute-done((bf16[144,128]{1,0:T(8,128)(2,1)S(1)}, bf16[144,128]{1,0:T(8,128)(2,1)S(1)}, u32[]{:S(2)}, u32[]{:S(2)}) %collective-permute-start.15) | collective-permute-done | bytes 36896 | tf_op jit(solution)/shard_map/ppermute | solution.py:536
  57.0 1.4 %collective-permute-start.18 = (bf16[144,128]{1,0:T(8,128)(2,1)S(1)}, bf16[144,128]{1,0:T(8,128)(2,1)S(1)}, u32[]{:S(2)}, u32[]{:S(2)}) collective-permute-start(bf16[144,128]{1,0:T(8,128)(2,1)S(1)} %add_convert_fusion.1), channel_id=1, source_target_pairs={{0,3},{1,2},{2,1},{3,0},{4,7},{5,6},{6,5},{7,4},{8,11},{9,10},{10,... | collective-permute-start | bytes 110600 | tf_op jit(solution)/shard_map/ppermute | solution.py:536
  58.5 1.6 %collective-permute-start.17 = (bf16[144,128]{1,0:T(8,128)(2,1)S(1)}, bf16[144,128]{1,0:T(8,128)(2,1)S(1)}, u32[]{:S(2)}, u32[]{:S(2)}) collective-permute-start(bf16[144,128]{1,0:T(8,128)(2,1)S(1)} %add_convert_fusion.1), channel_id=1, source_target_pairs={{0,2},{1,3},{2,0},{3,1},{4,6},{5,7},{6,4},{7,5},{8,10},{9,11},{10,... | collective-permute-start | bytes 110600 | tf_op jit(solution)/shard_map/ppermute | solution.py:536
  60.6 1.5 %collective-permute-done.18 = bf16[144,128]{1,0:T(8,128)(2,1)S(1)} collective-permute-done((bf16[144,128]{1,0:T(8,128)(2,1)S(1)}, bf16[144,128]{1,0:T(8,128)(2,1)S(1)}, u32[]{:S(2)}, u32[]{:S(2)}) %collective-permute-start.18) | collective-permute-done | bytes 36896 | tf_op jit(solution)/shard_map/ppermute | solution.py:536
  62.4 1.6 %collective-permute-done.16 = bf16[144,128]{1,0:T(8,128)(2,1)S(1)} collective-permute-done((bf16[144,128]{1,0:T(8,128)(2,1)S(1)}, bf16[144,128]{1,0:T(8,128)(2,1)S(1)}, u32[]{:S(2)}, u32[]{:S(2)}) %collective-permute-start.16) | collective-permute-done | bytes 36896 | tf_op jit(solution)/shard_map/ppermute | solution.py:536
  64.0 1.7 %collective-permute-start.19 = (bf16[144,128]{1,0:T(8,128)(2,1)S(1)}, bf16[144,128]{1,0:T(8,128)(2,1)S(1)}, u32[]{:S(2)}, u32[]{:S(2)}) collective-permute-start(bf16[144,128]{1,0:T(8,128)(2,1)S(1)} %add_convert_fusion.payload), channel_id=1, source_target_pairs={{0,4},{1,5},{2,6},{3,7},{4,0},{5,1},{6,2},{7,3},{8,12},{9,13},{10,... | collective-permute-start | bytes 110600 | tf_op jit(solution)/shard_map/ppermute | solution.py:536
  65.8 2.0 %queries.3 = (bf16[10,48,512]{2,1,0:T(8,128)(2,1)S(1)}, bf16[10,48,256]{2,1,0:T(8,128)(2,1)S(1)}) custom-call(bf16[14,48,256]{2,1,0:T(8,128)(2,1)S(1)} %get-tuple-element.25.mixed_in, bf16[2,256,768]{2,1,0:T(8,128)(2,1)S(1)} %get-tuple-element.17.refs_6_.qkv_weight, f32[2,32,768]{2,1,0:T(8,128)S(1)} %get-tuple-element.18.refs_7_.taps, ...), custom_call_target="tpu_custom_call" | custom-call | flops 251658240 | bytes 983040 | tf_op jit(solution)/shard_map/queries/pallas_call | solution.py:673
  67.8 1.4 %collective-permute-done.19.other = bf16[144,128]{1,0:T(8,128)(2,1)S(1)} collective-permute-done((bf16[144,128]{1,0:T(8,128)(2,1)S(1)}, bf16[144,128]{1,0:T(8,128)(2,1)S(1)}, u32[]{:S(2)}, u32[]{:S(2)}) %collective-permute-start.19) | collective-permute-done | bytes 36896 | tf_op jit(solution)/shard_map/ppermute | solution.py:536
  69.2 2.7 %last.1 = (bf16[8,32,256]{2,1,0:T(8,128)(2,1)}, f32[4,8,32]{2,1,0:T(8,128)}) custom-call(bf16[10,48,256]{2,1,0:T(8,128)(2,1)S(1)} %get-tuple-element.26.mixed, bf16[10,48,512]{2,1,0:T(8,128)(2,1)S(1)} %get-tuple-element.27.query, bf16[144,128]{1,0:T(8,128)(2,1)S(1)} %add_convert_fusion.payload, bf16[144,128]{1,0:T(8,128)(2,1)S(1)} %collective-permute-done.19.other, ...), custom_call_target="tpu_custom_call" | custom-call | tf_op jit(solution)/shard_map/last/pallas_call | solution.py:727
  (61 shorter events, 8.3 us)
Async XLA Ops:
  0.6 7.3 %copy-start.3 = (bf16[8,32,256]{2,1,0:T(8,128)(2,1)S(1)}, bf16[8,32,256]{2,1,0:T(8,128)(2,1)}, u32[]{:S(2)}) copy-start(bf16[8,32,256]{2,1,0:T(8,128)(2,1)} %own.1) | copy-start | bytes 393220
  0.7 13.2 %copy-start.10 = (bf16[3,3,4,256]{3,2,1,0:T(4,128)(2,1)S(1)}, bf16[3,3,4,256]{3,2,1,0:T(4,128)(2,1)}, u32[]{:S(2)}) copy-start(bf16[3,3,4,256]{3,2,1,0:T(4,128)(2,1)} %head.1) | copy-start | bytes 55300
  1.5 10.2 %collective-permute-start = (bf16[8,8,256]{2,1,0:T(8,128)(2,1)S(1)}, bf16[8,8,256]{2,1,0:T(8,128)(2,1)S(1)}, u32[]{:S(2)}, u32[]{:S(2)}) collective-permute-start(bf16[8,8,256]{2,1,0:T(8,128)(2,1)S(1)} %get-tuple-element.33), channel_id=1, source_target_pairs={{1,2},{2,1},{3,4},{4,3},{5,6},{6,5},{9,10},{10,9},{11,12},{12,11},... | collective-permute-start | bytes 98312 | tf_op jit(solution)/shard_map/ppermute | solution.py:562
  2.1 9.6 %collective-permute-start.1 = (bf16[8,8,256]{2,1,0:T(8,128)(2,1)S(1)}, bf16[8,8,256]{2,1,0:T(8,128)(2,1)S(1)}, u32[]{:S(2)}, u32[]{:S(2)}) collective-permute-start(bf16[8,8,256]{2,1,0:T(8,128)(2,1)S(1)} %get-tuple-element.32), channel_id=1, source_target_pairs={{0,1},{1,0},{2,3},{3,2},{4,5},{5,4},{6,7},{7,6},{8,9},{9,8},{10,11... | collective-permute-start | bytes 98312 | tf_op jit(solution)/shard_map/ppermute | solution.py:562
  7.9 5.9 %copy-start.9 = (f32[2,5,5,768]{3,0,2,1:T(2,128)S(1)}, f32[2,5,5,768]{3,0,2,1:T(2,128)}, u32[]{:S(2)}) copy-start(f32[2,5,5,768]{3,0,2,1:T(2,128)} %param.22) | copy-start | bytes 460804
  7.9 5.9 %copy-start.7 = (bf16[2,256,768]{2,1,0:T(8,128)(2,1)S(1)}, bf16[2,256,768]{2,1,0:T(8,128)(2,1)}, u32[]{:S(2)}) copy-start(bf16[2,256,768]{2,1,0:T(8,128)(2,1)} %qkv.1) | copy-start | bytes 2359300
  8.0 8.8 %collective-permute-start.2 = (bf16[7,32,256]{2,1,0:T(8,128)(2,1)S(1)}, bf16[7,32,256]{2,1,0:T(8,128)(2,1)S(1)}, u32[]{:S(2)}, u32[]{:S(2)}) collective-permute-start(bf16[7,32,256]{2,1,0:T(8,128)(2,1)S(1)} %get-tuple-element.31), channel_id=1, source_target_pairs={{8,16},{16,8},{9,17},{17,9},{10,18},{18,10},{11,19},{19,11},{12,20... | collective-permute-start | bytes 344072 | tf_op jit(solution)/shard_map/ppermute | solution.py:562
  8.8 8.0 %collective-permute-start.3 = (bf16[7,32,256]{2,1,0:T(8,128)(2,1)S(1)}, bf16[7,32,256]{2,1,0:T(8,128)(2,1)S(1)}, u32[]{:S(2)}, u32[]{:S(2)}) collective-permute-start(bf16[7,32,256]{2,1,0:T(8,128)(2,1)S(1)} %get-tuple-element.30), channel_id=1, source_target_pairs={{0,8},{8,0},{16,24},{24,16},{1,9},{9,1},{17,25},{25,17},{2,10},{10... | collective-permute-start | bytes 344072 | tf_op jit(solution)/shard_map/ppermute | solution.py:562
  11.7 5.0 %collective-permute-start.4 = (bf16[14,8,256]{2,1,0:T(8,128)(2,1)S(1)}, bf16[14,8,256]{2,1,0:T(8,128)(2,1)S(1)}, u32[]{:S(2)}, u32[]{:S(2)}) collective-permute-start(bf16[14,8,256]{2,1,0:T(8,128)(2,1)S(1)} %pad_maximum_fusion), channel_id=1, source_target_pairs={{8,16},{16,8},{9,17},{17,9},{10,18},{18,10},{11,19},{19,11},{12,20... | collective-permute-start | bytes 172040 | tf_op jit(solution)/shard_map/ppermute | solution.py:562
  12.5 4.3 %collective-permute-start.5 = (bf16[14,8,256]{2,1,0:T(8,128)(2,1)S(1)}, bf16[14,8,256]{2,1,0:T(8,128)(2,1)S(1)}, u32[]{:S(2)}, u32[]{:S(2)}) collective-permute-start(bf16[14,8,256]{2,1,0:T(8,128)(2,1)S(1)} %pad_maximum_fusion.1), channel_id=1, source_target_pairs={{0,8},{8,0},{16,24},{24,16},{1,9},{9,1},{17,25},{25,17},{2,10},{10... | collective-permute-start | bytes 172040 | tf_op jit(solution)/shard_map/ppermute | solution.py:562
  25.8 3.7 %collective-permute-start.8 = (bf16[144,128]{1,0:T(8,128)(2,1)S(1)}, bf16[144,128]{1,0:T(8,128)(2,1)S(1)}, u32[]{:S(2)}, u32[]{:S(2)}) collective-permute-start(bf16[144,128]{1,0:T(8,128)(2,1)S(1)} %get-tuple-element.23), channel_id=1, source_target_pairs={{0,24},{8,16},{16,8},{24,0},{1,25},{9,17},{17,9},{25,1},{2,26},{10... | collective-permute-start | bytes 110600 | tf_op jit(solution)/shard_map/ppermute | solution.py:536
  27.6 4.0 %collective-permute-start.7 = (bf16[144,128]{1,0:T(8,128)(2,1)S(1)}, bf16[144,128]{1,0:T(8,128)(2,1)S(1)}, u32[]{:S(2)}, u32[]{:S(2)}) collective-permute-start(bf16[144,128]{1,0:T(8,128)(2,1)S(1)} %get-tuple-element.23), channel_id=1, source_target_pairs={{0,16},{8,24},{16,0},{24,8},{1,17},{9,25},{17,1},{25,9},{2,18},{10... | collective-permute-start | bytes 110600 | tf_op jit(solution)/shard_map/ppermute | solution.py:536
  28.1 3.4 %collective-permute-start.6 = (bf16[144,128]{1,0:T(8,128)(2,1)S(1)}, bf16[144,128]{1,0:T(8,128)(2,1)S(1)}, u32[]{:S(2)}, u32[]{:S(2)}) collective-permute-start(bf16[144,128]{1,0:T(8,128)(2,1)S(1)} %get-tuple-element.23), channel_id=1, source_target_pairs={{0,8},{8,0},{16,24},{24,16},{1,9},{9,1},{17,25},{25,17},{2,10},{10... | collective-permute-start | bytes 110600 | tf_op jit(solution)/shard_map/ppermute | solution.py:536
  31.6 5.1 %collective-permute-start.11 = (bf16[144,128]{1,0:T(8,128)(2,1)S(1)}, bf16[144,128]{1,0:T(8,128)(2,1)S(1)}, u32[]{:S(2)}, u32[]{:S(2)}) collective-permute-start(bf16[144,128]{1,0:T(8,128)(2,1)S(1)} %add_convert_fusion.3), channel_id=1, source_target_pairs={{0,3},{1,2},{2,1},{3,0},{4,7},{5,6},{6,5},{7,4},{8,11},{9,10},{10,... | collective-permute-start | bytes 110600 | tf_op jit(solution)/shard_map/ppermute | solution.py:536
  33.4 4.0 %collective-permute-start.10 = (bf16[144,128]{1,0:T(8,128)(2,1)S(1)}, bf16[144,128]{1,0:T(8,128)(2,1)S(1)}, u32[]{:S(2)}, u32[]{:S(2)}) collective-permute-start(bf16[144,128]{1,0:T(8,128)(2,1)S(1)} %add_convert_fusion.3), channel_id=1, source_target_pairs={{0,2},{1,3},{2,0},{3,1},{4,6},{5,7},{6,4},{7,5},{8,10},{9,11},{10,... | collective-permute-start | bytes 110600 | tf_op jit(solution)/shard_map/ppermute | solution.py:536
  33.7 4.0 %collective-permute-start.9 = (bf16[144,128]{1,0:T(8,128)(2,1)S(1)}, bf16[144,128]{1,0:T(8,128)(2,1)S(1)}, u32[]{:S(2)}, u32[]{:S(2)}) collective-permute-start(bf16[144,128]{1,0:T(8,128)(2,1)S(1)} %add_convert_fusion.3), channel_id=1, source_target_pairs={{0,1},{1,0},{2,3},{3,2},{4,5},{5,4},{6,7},{7,6},{8,9},{9,8},{10,11... | collective-permute-start | bytes 110600 | tf_op jit(solution)/shard_map/ppermute | solution.py:536
  37.6 6.1 %collective-permute-start.12 = (bf16[144,128]{1,0:T(8,128)(2,1)S(1)}, bf16[144,128]{1,0:T(8,128)(2,1)S(1)}, u32[]{:S(2)}, u32[]{:S(2)}) collective-permute-start(bf16[144,128]{1,0:T(8,128)(2,1)S(1)} %add_convert_fusion.2.payload), channel_id=1, source_target_pairs={{0,4},{1,5},{2,6},{3,7},{4,0},{5,1},{6,2},{7,3},{8,12},{9,13},{10,... | collective-permute-start | bytes 110600 | tf_op jit(solution)/shard_map/ppermute | solution.py:536
  52.8 3.8 %collective-permute-start.15 = (bf16[144,128]{1,0:T(8,128)(2,1)S(1)}, bf16[144,128]{1,0:T(8,128)(2,1)S(1)}, u32[]{:S(2)}, u32[]{:S(2)}) collective-permute-start(bf16[144,128]{1,0:T(8,128)(2,1)S(1)} %get-tuple-element.28), channel_id=1, source_target_pairs={{0,24},{8,16},{16,8},{24,0},{1,25},{9,17},{17,9},{25,1},{2,26},{10... | collective-permute-start | bytes 110600 | tf_op jit(solution)/shard_map/ppermute | solution.py:536
  52.9 4.1 %collective-permute-start.14 = (bf16[144,128]{1,0:T(8,128)(2,1)S(1)}, bf16[144,128]{1,0:T(8,128)(2,1)S(1)}, u32[]{:S(2)}, u32[]{:S(2)}) collective-permute-start(bf16[144,128]{1,0:T(8,128)(2,1)S(1)} %get-tuple-element.28), channel_id=1, source_target_pairs={{0,16},{8,24},{16,0},{24,8},{1,17},{9,25},{17,1},{25,9},{2,18},{10... | collective-permute-start | bytes 110600 | tf_op jit(solution)/shard_map/ppermute | solution.py:536
  54.4 2.7 %collective-permute-start.13 = (bf16[144,128]{1,0:T(8,128)(2,1)S(1)}, bf16[144,128]{1,0:T(8,128)(2,1)S(1)}, u32[]{:S(2)}, u32[]{:S(2)}) collective-permute-start(bf16[144,128]{1,0:T(8,128)(2,1)S(1)} %get-tuple-element.28), channel_id=1, source_target_pairs={{0,8},{8,0},{16,24},{24,16},{1,9},{9,1},{17,25},{25,17},{2,10},{10... | collective-permute-start | bytes 110600 | tf_op jit(solution)/shard_map/ppermute | solution.py:536
  57.0 5.0 %collective-permute-start.18 = (bf16[144,128]{1,0:T(8,128)(2,1)S(1)}, bf16[144,128]{1,0:T(8,128)(2,1)S(1)}, u32[]{:S(2)}, u32[]{:S(2)}) collective-permute-start(bf16[144,128]{1,0:T(8,128)(2,1)S(1)} %add_convert_fusion.1), channel_id=1, source_target_pairs={{0,3},{1,2},{2,1},{3,0},{4,7},{5,6},{6,5},{7,4},{8,11},{9,10},{10,... | collective-permute-start | bytes 110600 | tf_op jit(solution)/shard_map/ppermute | solution.py:536
  58.5 4.0 %collective-permute-start.17 = (bf16[144,128]{1,0:T(8,128)(2,1)S(1)}, bf16[144,128]{1,0:T(8,128)(2,1)S(1)}, u32[]{:S(2)}, u32[]{:S(2)}) collective-permute-start(bf16[144,128]{1,0:T(8,128)(2,1)S(1)} %add_convert_fusion.1), channel_id=1, source_target_pairs={{0,2},{1,3},{2,0},{3,1},{4,6},{5,7},{6,4},{7,5},{8,10},{9,11},{10,... | collective-permute-start | bytes 110600 | tf_op jit(solution)/shard_map/ppermute | solution.py:536
  60.1 4.0 %collective-permute-start.16 = (bf16[144,128]{1,0:T(8,128)(2,1)S(1)}, bf16[144,128]{1,0:T(8,128)(2,1)S(1)}, u32[]{:S(2)}, u32[]{:S(2)}) collective-permute-start(bf16[144,128]{1,0:T(8,128)(2,1)S(1)} %add_convert_fusion.1), channel_id=1, source_target_pairs={{0,1},{1,0},{2,3},{3,2},{4,5},{5,4},{6,7},{7,6},{8,9},{9,8},{10,11... | collective-permute-start | bytes 110600 | tf_op jit(solution)/shard_map/ppermute | solution.py:536
  64.0 5.2 %collective-permute-start.19 = (bf16[144,128]{1,0:T(8,128)(2,1)S(1)}, bf16[144,128]{1,0:T(8,128)(2,1)S(1)}, u32[]{:S(2)}, u32[]{:S(2)}) collective-permute-start(bf16[144,128]{1,0:T(8,128)(2,1)S(1)} %add_convert_fusion.payload), channel_id=1, source_target_pairs={{0,4},{1,5},{2,6},{3,7},{4,0},{5,1},{6,2},{7,3},{8,12},{9,13},{10,... | collective-permute-start | bytes 110600 | tf_op jit(solution)/shard_map/ppermute | solution.py:536
  (10 other events, 17.5 us)

commit v19 on v18

--- a/solution.py
+++ b/solution.py
@@ -166,7 +166,7 @@
         for r in range(first, first + size):
             lanes = []
             for lane in range(0, chunk, LANES):
-                here = pl.ds(pl.multiple_of(at + lane, LANES), LANES)
+                here = pl.ds(at + lane, LANES)
                 value = depthwise_row(
                     [hidden[r + a, :, lane : lane + LANES] for a in range(3)],
                     lambda a, b: wide_depth[3 * a + b, :, here], 3, width,
@@ -181,8 +181,8 @@
         )
 
     def stage(index, current, following):
-        at = pl.multiple_of(index * chunk, chunk)
-        ahead = pl.multiple_of(jnp.minimum(index + 1, chunks - 1) * chunk, chunk)
+        at = index * chunk
+        ahead = at + chunk
         for (first, size), (from_row, count) in zip(parted(inner, PARTS), parted(rows, PARTS)):
             if following is not None:
                 expand_rows(following, ahead, from_row, count)
@@ -191,17 +191,9 @@
     for first, size in parted(rows, PARTS):
         expand_rows(hidden_0, 0, first, size)
 
-    def two_stages(index, carry):
-        stage(2 * index, hidden_0, hidden_1)
-        stage(2 * index + 1, hidden_1, hidden_0)
-        return carry
-
-    if section == 0:
-        for index in range(0, chunks, 2):
-            stage(index, hidden_0, hidden_1)
-            stage(index + 1, hidden_1, hidden_0 if index + 2 < chunks else None)
-    else:
-        lax.fori_loop(0, chunks // 2, two_stages, 0)
+    for index in range(0, chunks, 2):
+        stage(index, hidden_0, hidden_1)
+        stage(index + 1, hidden_1, hidden_0 if index + 2 < chunks else None)
     loads[0].wait()
     value = total[...] * (1.0 / 6.0) + project_bias[section : section + 1, :]
     mixed[...] = value.astype(BF16).reshape(inner, width, channels)
@@ -239,18 +231,15 @@
         pairs[mine, :, 0:channels], pairs[mine, :, channels : 2 * channels]
     )
 
-    def grouped_rows(index, carry):
-        at = index * size
-        more, sums = summed(
+    for at in range(0, tile_rows, size):
+        more, more_sums = summed(
             aggregated(pairs, wide_agg, group[0], 0, at, size, channels),
             aggregated(pairs, wide_agg, group[1], channels, at, size, channels),
         )
-        return [a + b for a, b in zip(carry[0], more)], carry[1] + sums
-
-    more, more_sums = lax.fori_loop(
-        0, tile_rows // size, grouped_rows,
-        ([jnp.zeros((LANES, LANES), F32) for _ in products], jnp.zeros_like(sums)),
-    )
+        if at:
+            more = [a + b for a, b in zip(more, more_before)]
+            more_sums = more_sums + sums_before
+        more_before, sums_before = more, more_sums
     products = products + more
     sums = jnp.concatenate([sums, more_sums], axis=1)
     same = same_head(head_dim)
@@ -299,7 +288,7 @@
         grouped = aggregated(centre, wide_agg, group[...], 0, first, size, channels)
         query[here, :, channels : 2 * channels] = jnp.maximum(grouped, 0.0)
 
-    by_groups(rows - 4, 5, query_rows)
+    by_groups(rows - 4, 8, query_rows)
 
 
 def attend(
@@ -360,7 +349,7 @@
         value = value + flat(mixed_ref[pl.ds(first, size)]).astype(F32)
         x_ref[pl.ds(first, size)] = value.astype(BF16).reshape(size, width, channels)
 
-    by_groups(rows, 5, attend_rows)
+    by_groups(rows, 10, attend_rows)
 
 
 def tap(section, a, b):

time: 72.4 us -> 70.3 us (0.971)
  Pallas kernels: 27.2 us -> 25.1 us
    pallas_call x1, Pallas kernels: 9.07 us -> 7.78 us  [local(): pl.pallas_call(functools.partial(second_kernel, tile, head_dim), out_shap...]
where the time goes in v19:
time: 70.3 us; the launch traced here: 70.1 us
  starting transfers between devices  28.3 us (40%)
  Pallas kernels  25.1 us (36%)
  waiting for transfers between devices  12.8 us (18%)
  local copies, waits for them, and re-layouts  2.61 us (4%)
  between operations  1.09 us (2%)
    ppermute x14, starting transfers between devices, sum_by_permutes(): lax.ppermute(value, axis, [(i, partner(i, stride, radix, k)) for i in ran...  16.2 us
    ppermute x14, waiting for transfers between devices, sum_by_permutes(): lax.ppermute(value, axis, [(i, partner(i, stride, radix, k)) for i in ran...  12.8 us
    ppermute x6, starting transfers between devices, pair_exchange(): return lax.ppermute(value, axis, pairs)  12.2 us
    pallas_call x1, Pallas kernels, local(): pl.pallas_call(functools.partial(first_kernel, tile, head_dim), out_shape...  8.04 us
    pallas_call x1, Pallas kernels, local(): pl.pallas_call(functools.partial(second_kernel, tile, head_dim), out_shap...  7.78 us
    pallas_call x2, Pallas kernels, queries(): pl.pallas_call(functools.partial(query_kernel, tile, section), out_shape=...  4.98 us
    pallas_call x1, Pallas kernels, local(): pl.pallas_call(functools.partial(last_kernel, tile, head_dim), out_shape=...  2.33 us
    pallas_call x1, Pallas kernels, local(): pl.pallas_call(functools.partial(prepare_kernel, head_dim), out_shape=mad...  1.92 us
  transfers between devices with their start and end apart: 20, of which 11 were waited for; matrix products, arithmetic and copies ran while one was open for 0% of the time, Pallas kernels for 10%

profile of v19, /device:TPU:0, one launch (start us, length us, event | category | flops | bytes accessed | tf_op | source)
XLA Modules:
  0.0 70.1 jit_solution(7498276358256419997)
XLA Ops:
  2.1 5.8 %collective-permute-start.1 = (bf16[8,8,256]{2,1,0:T(8,128)(2,1)S(1)}, bf16[8,8,256]{2,1,0:T(8,128)(2,1)S(1)}, u32[]{:S(2)}, u32[]{:S(2)}) collective-permute-start(bf16[8,8,256]{2,1,0:T(8,128)(2,1)S(1)} %get-tuple-element.32), channel_id=1, source_target_pairs={{0,1},{1,0},{2,3},{3,2},{4,5},{5,4},{6,7},{7,6},{8,9},{9,8},{10,11... | collective-permute-start | bytes 98312 | tf_op jit(solution)/shard_map/ppermute | solution.py:551
  8.8 2.9 %collective-permute-start.3 = (bf16[7,32,256]{2,1,0:T(8,128)(2,1)S(1)}, bf16[7,32,256]{2,1,0:T(8,128)(2,1)S(1)}, u32[]{:S(2)}, u32[]{:S(2)}) collective-permute-start(bf16[7,32,256]{2,1,0:T(8,128)(2,1)S(1)} %get-tuple-element.30), channel_id=1, source_target_pairs={{0,8},{8,0},{16,24},{24,16},{1,9},{9,1},{17,25},{25,17},{2,10},{10... | collective-permute-start | bytes 344072 | tf_op jit(solution)/shard_map/ppermute | solution.py:551
  12.5 1.4 %collective-permute-start.5 = (bf16[14,8,256]{2,1,0:T(8,128)(2,1)S(1)}, bf16[14,8,256]{2,1,0:T(8,128)(2,1)S(1)}, u32[]{:S(2)}, u32[]{:S(2)}) collective-permute-start(bf16[14,8,256]{2,1,0:T(8,128)(2,1)S(1)} %pad_maximum_fusion.1), channel_id=1, source_target_pairs={{0,8},{8,0},{16,24},{24,16},{1,9},{9,1},{17,25},{25,17},{2,10},{10... | collective-permute-start | bytes 172040 | tf_op jit(solution)/shard_map/ppermute | solution.py:551
  14.9 1.9 %prepare.1 = (bf16[2,256,768]{2,1,0:T(8,128)(2,1)S(1)}, f32[2,32,768]{2,1,0:T(8,128)S(1)}, bf16[2,3,256,256]{3,2,1,0:T(8,128)(2,1)S(1)}, bf16[3,128,256]{2,1,0:T...) custom-call(bf16[2,256,768]{2,1,0:T(8,128)(2,1)S(1)} %copy-done.7, f32[5,5,2,768]{3,2,1,0:T(2,128)S(1)} %bitcast.5, ...), custom_call_target="tpu_custom_call" | custom-call | flops 2000000000 | bytes 4000000 | tf_op jit(solution)/shard_map/prepare/pallas_call | solution.py:608
  17.5 8.0 %first.1 = (bf16[20,48,256]{2,1,0:T(8,128)(2,1)S(1)}, bf16[144,128]{1,0:T(8,128)(2,1)S(1)}) custom-call(bf16[8,32,256]{2,1,0:T(8,128)(2,1)S(1)} %copy-done.3, bf16[8,8,256]{2,1,0:T(8,128)(2,1)S(1)} %collective-permute-done.col_1, bf16[8,8,256]{2,1,0:T(8,128)(2,1)S(1)} %collective-permute-done.1.col_0, bf16[7,32,256]{2,1,0:T(8,128)(2,1)S(1)} %collective-permute-done.2.row_1, ...), custom_call_target="tpu_custom_call" | custom-call | tf_op jit(solution)/shard_map/first/pallas_call | solution.py:688
  25.5 1.8 %collective-permute-start.8 = (bf16[144,128]{1,0:T(8,128)(2,1)S(1)}, bf16[144,128]{1,0:T(8,128)(2,1)S(1)}, u32[]{:S(2)}, u32[]{:S(2)}) collective-permute-start(bf16[144,128]{1,0:T(8,128)(2,1)S(1)} %get-tuple-element.23), channel_id=1, source_target_pairs={{0,24},{8,16},{16,8},{24,0},{1,25},{9,17},{17,9},{25,1},{2,26},{10... | collective-permute-start | bytes 110600 | tf_op jit(solution)/shard_map/ppermute | solution.py:525
  27.9 1.3 %collective-permute-done.8 = bf16[144,128]{1,0:T(8,128)(2,1)S(1)} collective-permute-done((bf16[144,128]{1,0:T(8,128)(2,1)S(1)}, bf16[144,128]{1,0:T(8,128)(2,1)S(1)}, u32[]{:S(2)}, u32[]{:S(2)}) %collective-permute-start.8) | collective-permute-done | bytes 36896 | tf_op jit(solution)/shard_map/ppermute | solution.py:525
  29.2 2.1 %collective-permute-done.7 = bf16[144,128]{1,0:T(8,128)(2,1)S(1)} collective-permute-done((bf16[144,128]{1,0:T(8,128)(2,1)S(1)}, bf16[144,128]{1,0:T(8,128)(2,1)S(1)}, u32[]{:S(2)}, u32[]{:S(2)}) %collective-permute-start.7) | collective-permute-done | bytes 36896 | tf_op jit(solution)/shard_map/ppermute | solution.py:525
  31.3 1.9 %collective-permute-start.11 = (bf16[144,128]{1,0:T(8,128)(2,1)S(1)}, bf16[144,128]{1,0:T(8,128)(2,1)S(1)}, u32[]{:S(2)}, u32[]{:S(2)}) collective-permute-start(bf16[144,128]{1,0:T(8,128)(2,1)S(1)} %add_convert_fusion.3), channel_id=1, source_target_pairs={{0,3},{1,2},{2,1},{3,0},{4,7},{5,6},{6,5},{7,4},{8,11},{9,10},{10,... | collective-permute-start | bytes 110600 | tf_op jit(solution)/shard_map/ppermute | solution.py:525
  33.4 1.5 %collective-permute-start.9 = (bf16[144,128]{1,0:T(8,128)(2,1)S(1)}, bf16[144,128]{1,0:T(8,128)(2,1)S(1)}, u32[]{:S(2)}, u32[]{:S(2)}) collective-permute-start(bf16[144,128]{1,0:T(8,128)(2,1)S(1)} %add_convert_fusion.3), channel_id=1, source_target_pairs={{0,1},{1,0},{2,3},{3,2},{4,5},{5,4},{6,7},{7,6},{8,9},{9,8},{10,11... | collective-permute-start | bytes 110600 | tf_op jit(solution)/shard_map/ppermute | solution.py:525
  34.9 1.5 %collective-permute-done.11 = bf16[144,128]{1,0:T(8,128)(2,1)S(1)} collective-permute-done((bf16[144,128]{1,0:T(8,128)(2,1)S(1)}, bf16[144,128]{1,0:T(8,128)(2,1)S(1)}, u32[]{:S(2)}, u32[]{:S(2)}) %collective-permute-start.11) | collective-permute-done | bytes 36896 | tf_op jit(solution)/shard_map/ppermute | solution.py:525
  37.4 2.9 %collective-permute-start.12 = (bf16[144,128]{1,0:T(8,128)(2,1)S(1)}, bf16[144,128]{1,0:T(8,128)(2,1)S(1)}, u32[]{:S(2)}, u32[]{:S(2)}) collective-permute-start(bf16[144,128]{1,0:T(8,128)(2,1)S(1)} %add_convert_fusion.2.payload), channel_id=1, source_target_pairs={{0,4},{1,5},{2,6},{3,7},{4,0},{5,1},{6,2},{7,3},{8,12},{9,13},{10,... | collective-permute-start | bytes 110600 | tf_op jit(solution)/shard_map/ppermute | solution.py:525
  40.3 3.0 %queries.2 = (bf16[16,48,512]{2,1,0:T(8,128)(2,1)S(1)}, bf16[16,48,256]{2,1,0:T(8,128)(2,1)S(1)}) custom-call(bf16[20,48,256]{2,1,0:T(8,128)(2,1)S(1)} %get-tuple-element.20.mixed_in, bf16[2,256,768]{2,1,0:T(8,128)(2,1)S(1)} %get-tuple-element.17.refs_6_.qkv_weight, f32[2,32,768]{2,1,0:T(8,128)S(1)} %get-tuple-element.18.refs_7_.taps, ...), custom_call_target="tpu_custom_call" | custom-call | flops 402653184 | bytes 1572864 | tf_op jit(solution)/shard_map/queries/pallas_call | solution.py:662
  43.3 7.8 %second.1 = (bf16[14,48,256]{2,1,0:T(8,128)(2,1)S(1)}, bf16[144,128]{1,0:T(8,128)(2,1)S(1)}) custom-call(bf16[16,48,256]{2,1,0:T(8,128)(2,1)S(1)} %get-tuple-element.21.mixed, bf16[16,48,512]{2,1,0:T(8,128)(2,1)S(1)} %get-tuple-element.22.query, bf16[144,128]{1,0:T(8,128)(2,1)S(1)} %add_convert_fusion.2.payload, ...), custom_call_target="tpu_custom_call" | custom-call | tf_op jit(solution)/shard_map/second/pallas_call | solution.py:703
  51.1 1.4 %collective-permute-start.14 = (bf16[144,128]{1,0:T(8,128)(2,1)S(1)}, bf16[144,128]{1,0:T(8,128)(2,1)S(1)}, u32[]{:S(2)}, u32[]{:S(2)}) collective-permute-start(bf16[144,128]{1,0:T(8,128)(2,1)S(1)} %get-tuple-element.28), channel_id=1, source_target_pairs={{0,16},{8,24},{16,0},{24,8},{1,17},{9,25},{17,1},{25,9},{2,18},{10... | collective-permute-start | bytes 110600 | tf_op jit(solution)/shard_map/ppermute | solution.py:525
  53.0 1.9 %collective-permute-done.15 = bf16[144,128]{1,0:T(8,128)(2,1)S(1)} collective-permute-done((bf16[144,128]{1,0:T(8,128)(2,1)S(1)}, bf16[144,128]{1,0:T(8,128)(2,1)S(1)}, u32[]{:S(2)}, u32[]{:S(2)}) %collective-permute-start.15) | collective-permute-done | bytes 36896 | tf_op jit(solution)/shard_map/ppermute | solution.py:525
  55.3 1.5 %collective-permute-start.18 = (bf16[144,128]{1,0:T(8,128)(2,1)S(1)}, bf16[144,128]{1,0:T(8,128)(2,1)S(1)}, u32[]{:S(2)}, u32[]{:S(2)}) collective-permute-start(bf16[144,128]{1,0:T(8,128)(2,1)S(1)} %add_convert_fusion.1), channel_id=1, source_target_pairs={{0,3},{1,2},{2,1},{3,0},{4,7},{5,6},{6,5},{7,4},{8,11},{9,10},{10,... | collective-permute-start | bytes 110600 | tf_op jit(solution)/shard_map/ppermute | solution.py:525
  56.8 1.4 %collective-permute-start.17 = (bf16[144,128]{1,0:T(8,128)(2,1)S(1)}, bf16[144,128]{1,0:T(8,128)(2,1)S(1)}, u32[]{:S(2)}, u32[]{:S(2)}) collective-permute-start(bf16[144,128]{1,0:T(8,128)(2,1)S(1)} %add_convert_fusion.1), channel_id=1, source_target_pairs={{0,2},{1,3},{2,0},{3,1},{4,6},{5,7},{6,4},{7,5},{8,10},{9,11},{10,... | collective-permute-start | bytes 110600 | tf_op jit(solution)/shard_map/ppermute | solution.py:525
  58.8 1.5 %collective-permute-done.18 = bf16[144,128]{1,0:T(8,128)(2,1)S(1)} collective-permute-done((bf16[144,128]{1,0:T(8,128)(2,1)S(1)}, bf16[144,128]{1,0:T(8,128)(2,1)S(1)}, u32[]{:S(2)}, u32[]{:S(2)}) %collective-permute-start.18) | collective-permute-done | bytes 36896 | tf_op jit(solution)/shard_map/ppermute | solution.py:525
  60.8 1.4 %collective-permute-done.16 = bf16[144,128]{1,0:T(8,128)(2,1)S(1)} collective-permute-done((bf16[144,128]{1,0:T(8,128)(2,1)S(1)}, bf16[144,128]{1,0:T(8,128)(2,1)S(1)}, u32[]{:S(2)}, u32[]{:S(2)}) %collective-permute-start.16) | collective-permute-done | bytes 36896 | tf_op jit(solution)/shard_map/ppermute | solution.py:525
  62.2 1.9 %collective-permute-start.19 = (bf16[144,128]{1,0:T(8,128)(2,1)S(1)}, bf16[144,128]{1,0:T(8,128)(2,1)S(1)}, u32[]{:S(2)}, u32[]{:S(2)}) collective-permute-start(bf16[144,128]{1,0:T(8,128)(2,1)S(1)} %add_convert_fusion.payload), channel_id=1, source_target_pairs={{0,4},{1,5},{2,6},{3,7},{4,0},{5,1},{6,2},{7,3},{8,12},{9,13},{10,... | collective-permute-start | bytes 110600 | tf_op jit(solution)/shard_map/ppermute | solution.py:525
  64.3 2.0 %queries.3 = (bf16[10,48,512]{2,1,0:T(8,128)(2,1)S(1)}, bf16[10,48,256]{2,1,0:T(8,128)(2,1)S(1)}) custom-call(bf16[14,48,256]{2,1,0:T(8,128)(2,1)S(1)} %get-tuple-element.25.mixed_in, bf16[2,256,768]{2,1,0:T(8,128)(2,1)S(1)} %get-tuple-element.17.refs_6_.qkv_weight, f32[2,32,768]{2,1,0:T(8,128)S(1)} %get-tuple-element.18.refs_7_.taps, ...), custom_call_target="tpu_custom_call" | custom-call | flops 251658240 | bytes 983040 | tf_op jit(solution)/shard_map/queries/pallas_call | solution.py:662
  66.2 1.3 %collective-permute-done.19.other = bf16[144,128]{1,0:T(8,128)(2,1)S(1)} collective-permute-done((bf16[144,128]{1,0:T(8,128)(2,1)S(1)}, bf16[144,128]{1,0:T(8,128)(2,1)S(1)}, u32[]{:S(2)}, u32[]{:S(2)}) %collective-permute-start.19) | collective-permute-done | bytes 36896 | tf_op jit(solution)/shard_map/ppermute | solution.py:525
  67.6 2.3 %last.1 = (bf16[8,32,256]{2,1,0:T(8,128)(2,1)}, f32[4,8,32]{2,1,0:T(8,128)}) custom-call(bf16[10,48,256]{2,1,0:T(8,128)(2,1)S(1)} %get-tuple-element.26.mixed, bf16[10,48,512]{2,1,0:T(8,128)(2,1)S(1)} %get-tuple-element.27.query, bf16[144,128]{1,0:T(8,128)(2,1)S(1)} %add_convert_fusion.payload, bf16[144,128]{1,0:T(8,128)(2,1)S(1)} %collective-permute-done.19.other, ...), custom_call_target="tpu_custom_call" | custom-call | tf_op jit(solution)/shard_map/last/pallas_call | solution.py:716
  (61 shorter events, 8.4 us)
Async XLA Ops:
  0.6 7.3 %copy-start.3 = (bf16[8,32,256]{2,1,0:T(8,128)(2,1)S(1)}, bf16[8,32,256]{2,1,0:T(8,128)(2,1)}, u32[]{:S(2)}) copy-start(bf16[8,32,256]{2,1,0:T(8,128)(2,1)} %own.1) | copy-start | bytes 393220
  0.7 13.2 %copy-start.10 = (bf16[3,3,4,256]{3,2,1,0:T(4,128)(2,1)S(1)}, bf16[3,3,4,256]{3,2,1,0:T(4,128)(2,1)}, u32[]{:S(2)}) copy-start(bf16[3,3,4,256]{3,2,1,0:T(4,128)(2,1)} %head.1) | copy-start | bytes 55300
  1.5 10.2 %collective-permute-start = (bf16[8,8,256]{2,1,0:T(8,128)(2,1)S(1)}, bf16[8,8,256]{2,1,0:T(8,128)(2,1)S(1)}, u32[]{:S(2)}, u32[]{:S(2)}) collective-permute-start(bf16[8,8,256]{2,1,0:T(8,128)(2,1)S(1)} %get-tuple-element.33), channel_id=1, source_target_pairs={{1,2},{2,1},{3,4},{4,3},{5,6},{6,5},{9,10},{10,9},{11,12},{12,11},... | collective-permute-start | bytes 98312 | tf_op jit(solution)/shard_map/ppermute | solution.py:551
  2.1 9.6 %collective-permute-start.1 = (bf16[8,8,256]{2,1,0:T(8,128)(2,1)S(1)}, bf16[8,8,256]{2,1,0:T(8,128)(2,1)S(1)}, u32[]{:S(2)}, u32[]{:S(2)}) collective-permute-start(bf16[8,8,256]{2,1,0:T(8,128)(2,1)S(1)} %get-tuple-element.32), channel_id=1, source_target_pairs={{0,1},{1,0},{2,3},{3,2},{4,5},{5,4},{6,7},{7,6},{8,9},{9,8},{10,11... | collective-permute-start | bytes 98312 | tf_op jit(solution)/shard_map/ppermute | solution.py:551
  7.9 5.9 %copy-start.9 = (f32[2,5,5,768]{3,0,2,1:T(2,128)S(1)}, f32[2,5,5,768]{3,0,2,1:T(2,128)}, u32[]{:S(2)}) copy-start(f32[2,5,5,768]{3,0,2,1:T(2,128)} %param.22) | copy-start | bytes 460804
  7.9 5.9 %copy-start.7 = (bf16[2,256,768]{2,1,0:T(8,128)(2,1)S(1)}, bf16[2,256,768]{2,1,0:T(8,128)(2,1)}, u32[]{:S(2)}) copy-start(bf16[2,256,768]{2,1,0:T(8,128)(2,1)} %qkv.1) | copy-start | bytes 2359300
  8.0 8.8 %collective-permute-start.2 = (bf16[7,32,256]{2,1,0:T(8,128)(2,1)S(1)}, bf16[7,32,256]{2,1,0:T(8,128)(2,1)S(1)}, u32[]{:S(2)}, u32[]{:S(2)}) collective-permute-start(bf16[7,32,256]{2,1,0:T(8,128)(2,1)S(1)} %get-tuple-element.31), channel_id=1, source_target_pairs={{8,16},{16,8},{9,17},{17,9},{10,18},{18,10},{11,19},{19,11},{12,20... | collective-permute-start | bytes 344072 | tf_op jit(solution)/shard_map/ppermute | solution.py:551
  8.8 8.0 %collective-permute-start.3 = (bf16[7,32,256]{2,1,0:T(8,128)(2,1)S(1)}, bf16[7,32,256]{2,1,0:T(8,128)(2,1)S(1)}, u32[]{:S(2)}, u32[]{:S(2)}) collective-permute-start(bf16[7,32,256]{2,1,0:T(8,128)(2,1)S(1)} %get-tuple-element.30), channel_id=1, source_target_pairs={{0,8},{8,0},{16,24},{24,16},{1,9},{9,1},{17,25},{25,17},{2,10},{10... | collective-permute-start | bytes 344072 | tf_op jit(solution)/shard_map/ppermute | solution.py:551
  11.7 5.0 %collective-permute-start.4 = (bf16[14,8,256]{2,1,0:T(8,128)(2,1)S(1)}, bf16[14,8,256]{2,1,0:T(8,128)(2,1)S(1)}, u32[]{:S(2)}, u32[]{:S(2)}) collective-permute-start(bf16[14,8,256]{2,1,0:T(8,128)(2,1)S(1)} %pad_maximum_fusion), channel_id=1, source_target_pairs={{8,16},{16,8},{9,17},{17,9},{10,18},{18,10},{11,19},{19,11},{12,20... | collective-permute-start | bytes 172040 | tf_op jit(solution)/shard_map/ppermute | solution.py:551
  12.5 4.3 %collective-permute-start.5 = (bf16[14,8,256]{2,1,0:T(8,128)(2,1)S(1)}, bf16[14,8,256]{2,1,0:T(8,128)(2,1)S(1)}, u32[]{:S(2)}, u32[]{:S(2)}) collective-permute-start(bf16[14,8,256]{2,1,0:T(8,128)(2,1)S(1)} %pad_maximum_fusion.1), channel_id=1, source_target_pairs={{0,8},{8,0},{16,24},{24,16},{1,9},{9,1},{17,25},{25,17},{2,10},{10... | collective-permute-start | bytes 172040 | tf_op jit(solution)/shard_map/ppermute | solution.py:551
  25.5 3.7 %collective-permute-start.8 = (bf16[144,128]{1,0:T(8,128)(2,1)S(1)}, bf16[144,128]{1,0:T(8,128)(2,1)S(1)}, u32[]{:S(2)}, u32[]{:S(2)}) collective-permute-start(bf16[144,128]{1,0:T(8,128)(2,1)S(1)} %get-tuple-element.23), channel_id=1, source_target_pairs={{0,24},{8,16},{16,8},{24,0},{1,25},{9,17},{17,9},{25,1},{2,26},{10... | collective-permute-start | bytes 110600 | tf_op jit(solution)/shard_map/ppermute | solution.py:525
  27.3 4.0 %collective-permute-start.7 = (bf16[144,128]{1,0:T(8,128)(2,1)S(1)}, bf16[144,128]{1,0:T(8,128)(2,1)S(1)}, u32[]{:S(2)}, u32[]{:S(2)}) collective-permute-start(bf16[144,128]{1,0:T(8,128)(2,1)S(1)} %get-tuple-element.23), channel_id=1, source_target_pairs={{0,16},{8,24},{16,0},{24,8},{1,17},{9,25},{17,1},{25,9},{2,18},{10... | collective-permute-start | bytes 110600 | tf_op jit(solution)/shard_map/ppermute | solution.py:525
  27.9 3.4 %collective-permute-start.6 = (bf16[144,128]{1,0:T(8,128)(2,1)S(1)}, bf16[144,128]{1,0:T(8,128)(2,1)S(1)}, u32[]{:S(2)}, u32[]{:S(2)}) collective-permute-start(bf16[144,128]{1,0:T(8,128)(2,1)S(1)} %get-tuple-element.23), channel_id=1, source_target_pairs={{0,8},{8,0},{16,24},{24,16},{1,9},{9,1},{17,25},{25,17},{2,10},{10... | collective-permute-start | bytes 110600 | tf_op jit(solution)/shard_map/ppermute | solution.py:525
  31.3 5.1 %collective-permute-start.11 = (bf16[144,128]{1,0:T(8,128)(2,1)S(1)}, bf16[144,128]{1,0:T(8,128)(2,1)S(1)}, u32[]{:S(2)}, u32[]{:S(2)}) collective-permute-start(bf16[144,128]{1,0:T(8,128)(2,1)S(1)} %add_convert_fusion.3), channel_id=1, source_target_pairs={{0,3},{1,2},{2,1},{3,0},{4,7},{5,6},{6,5},{7,4},{8,11},{9,10},{10,... | collective-permute-start | bytes 110600 | tf_op jit(solution)/shard_map/ppermute | solution.py:525
  33.2 4.0 %collective-permute-start.10 = (bf16[144,128]{1,0:T(8,128)(2,1)S(1)}, bf16[144,128]{1,0:T(8,128)(2,1)S(1)}, u32[]{:S(2)}, u32[]{:S(2)}) collective-permute-start(bf16[144,128]{1,0:T(8,128)(2,1)S(1)} %add_convert_fusion.3), channel_id=1, source_target_pairs={{0,2},{1,3},{2,0},{3,1},{4,6},{5,7},{6,4},{7,5},{8,10},{9,11},{10,... | collective-permute-start | bytes 110600 | tf_op jit(solution)/shard_map/ppermute | solution.py:525
  33.4 4.0 %collective-permute-start.9 = (bf16[144,128]{1,0:T(8,128)(2,1)S(1)}, bf16[144,128]{1,0:T(8,128)(2,1)S(1)}, u32[]{:S(2)}, u32[]{:S(2)}) collective-permute-start(bf16[144,128]{1,0:T(8,128)(2,1)S(1)} %add_convert_fusion.3), channel_id=1, source_target_pairs={{0,1},{1,0},{2,3},{3,2},{4,5},{5,4},{6,7},{7,6},{8,9},{9,8},{10,11... | collective-permute-start | bytes 110600 | tf_op jit(solution)/shard_map/ppermute | solution.py:525
  37.4 5.9 %collective-permute-start.12 = (bf16[144,128]{1,0:T(8,128)(2,1)S(1)}, bf16[144,128]{1,0:T(8,128)(2,1)S(1)}, u32[]{:S(2)}, u32[]{:S(2)}) collective-permute-start(bf16[144,128]{1,0:T(8,128)(2,1)S(1)} %add_convert_fusion.2.payload), channel_id=1, source_target_pairs={{0,4},{1,5},{2,6},{3,7},{4,0},{5,1},{6,2},{7,3},{8,12},{9,13},{10,... | collective-permute-start | bytes 110600 | tf_op jit(solution)/shard_map/ppermute | solution.py:525
  51.1 3.8 %collective-permute-start.15 = (bf16[144,128]{1,0:T(8,128)(2,1)S(1)}, bf16[144,128]{1,0:T(8,128)(2,1)S(1)}, u32[]{:S(2)}, u32[]{:S(2)}) collective-permute-start(bf16[144,128]{1,0:T(8,128)(2,1)S(1)} %get-tuple-element.28), channel_id=1, source_target_pairs={{0,24},{8,16},{16,8},{24,0},{1,25},{9,17},{17,9},{25,1},{2,26},{10... | collective-permute-start | bytes 110600 | tf_op jit(solution)/shard_map/ppermute | solution.py:525
  51.1 4.1 %collective-permute-start.14 = (bf16[144,128]{1,0:T(8,128)(2,1)S(1)}, bf16[144,128]{1,0:T(8,128)(2,1)S(1)}, u32[]{:S(2)}, u32[]{:S(2)}) collective-permute-start(bf16[144,128]{1,0:T(8,128)(2,1)S(1)} %get-tuple-element.28), channel_id=1, source_target_pairs={{0,16},{8,24},{16,0},{24,8},{1,17},{9,25},{17,1},{25,9},{2,18},{10... | collective-permute-start | bytes 110600 | tf_op jit(solution)/shard_map/ppermute | solution.py:525
  52.6 2.7 %collective-permute-start.13 = (bf16[144,128]{1,0:T(8,128)(2,1)S(1)}, bf16[144,128]{1,0:T(8,128)(2,1)S(1)}, u32[]{:S(2)}, u32[]{:S(2)}) collective-permute-start(bf16[144,128]{1,0:T(8,128)(2,1)S(1)} %get-tuple-element.28), channel_id=1, source_target_pairs={{0,8},{8,0},{16,24},{24,16},{1,9},{9,1},{17,25},{25,17},{2,10},{10... | collective-permute-start | bytes 110600 | tf_op jit(solution)/shard_map/ppermute | solution.py:525
  55.3 5.1 %collective-permute-start.18 = (bf16[144,128]{1,0:T(8,128)(2,1)S(1)}, bf16[144,128]{1,0:T(8,128)(2,1)S(1)}, u32[]{:S(2)}, u32[]{:S(2)}) collective-permute-start(bf16[144,128]{1,0:T(8,128)(2,1)S(1)} %add_convert_fusion.1), channel_id=1, source_target_pairs={{0,3},{1,2},{2,1},{3,0},{4,7},{5,6},{6,5},{7,4},{8,11},{9,10},{10,... | collective-permute-start | bytes 110600 | tf_op jit(solution)/shard_map/ppermute | solution.py:525
  56.8 4.0 %collective-permute-start.17 = (bf16[144,128]{1,0:T(8,128)(2,1)S(1)}, bf16[144,128]{1,0:T(8,128)(2,1)S(1)}, u32[]{:S(2)}, u32[]{:S(2)}) collective-permute-start(bf16[144,128]{1,0:T(8,128)(2,1)S(1)} %add_convert_fusion.1), channel_id=1, source_target_pairs={{0,2},{1,3},{2,0},{3,1},{4,6},{5,7},{6,4},{7,5},{8,10},{9,11},{10,... | collective-permute-start | bytes 110600 | tf_op jit(solution)/shard_map/ppermute | solution.py:525
  58.3 4.0 %collective-permute-start.16 = (bf16[144,128]{1,0:T(8,128)(2,1)S(1)}, bf16[144,128]{1,0:T(8,128)(2,1)S(1)}, u32[]{:S(2)}, u32[]{:S(2)}) collective-permute-start(bf16[144,128]{1,0:T(8,128)(2,1)S(1)} %add_convert_fusion.1), channel_id=1, source_target_pairs={{0,1},{1,0},{2,3},{3,2},{4,5},{5,4},{6,7},{7,6},{8,9},{9,8},{10,11... | collective-permute-start | bytes 110600 | tf_op jit(solution)/shard_map/ppermute | solution.py:525
  62.2 5.3 %collective-permute-start.19 = (bf16[144,128]{1,0:T(8,128)(2,1)S(1)}, bf16[144,128]{1,0:T(8,128)(2,1)S(1)}, u32[]{:S(2)}, u32[]{:S(2)}) collective-permute-start(bf16[144,128]{1,0:T(8,128)(2,1)S(1)} %add_convert_fusion.payload), channel_id=1, source_target_pairs={{0,4},{1,5},{2,6},{3,7},{4,0},{5,1},{6,2},{7,3},{8,12},{9,13},{10,... | collective-permute-start | bytes 110600 | tf_op jit(solution)/shard_map/ppermute | solution.py:525
  (10 other events, 17.5 us)

commit v20 on v19

--- a/solution.py
+++ b/solution.py
@@ -123,19 +123,18 @@
 
 
 def front(x_ref, weights, outs, scratch, halo, tile, head_dim, section):
-    expand, expand_bias, depth, depth_bias, project = weights[:5]
+    expand, biases, depth, project = weights[:4]
     mixed_out, payload_out = outs
     (
         hidden_0, hidden_1, total, bounds, mixed, pairs, wide_depth, wide_agg,
-        project_bias, pair_weight, agg, group, sems,
+        pair_weight, agg, group, sems,
     ) = scratch
     channels = x_ref.shape[2]
     tail = pl.ds(channels, 2 * channels)
     loads = [
-        pltpu.make_async_copy(weights[5], project_bias, sems.at[0]),
-        pltpu.make_async_copy(weights[6].at[section, :, tail], pair_weight, sems.at[1]),
-        pltpu.make_async_copy(weights[7].at[section, :, tail], agg, sems.at[2]),
-        pltpu.make_async_copy(weights[8].at[section, pl.ds(1, 2)], group, sems.at[3]),
+        pltpu.make_async_copy(weights[4].at[section, :, tail], pair_weight, sems.at[0]),
+        pltpu.make_async_copy(weights[5].at[section, :, tail], agg, sems.at[1]),
+        pltpu.make_async_copy(weights[6].at[section, pl.ds(1, 2)], group, sems.at[2]),
     ]
     for load in loads:
         load.start()
@@ -143,7 +142,8 @@
     tile_rows, tile_cols = tile
     inner = rows - 2
     chunk = hidden_0.shape[2]
-    chunks = expand.shape[2] // chunk
+    hidden_channels = expand.shape[2]
+    chunks = hidden_channels // chunk
     for index in range(9):
         taps = depth[index // 3, index % 3, section : section + 1, :] * (1.0 / 6.0)
         wide_depth[index] = jnp.broadcast_to(taps, (TILE, taps.shape[1])).astype(BF16)
@@ -155,7 +155,7 @@
             flat(x_ref[first : first + size]), expand[section, :, pl.ds(at, chunk)],
             preferred_element_type=F32,
         )
-        value = (value + expand_bias[section : section + 1, pl.ds(at, chunk)]).astype(BF16)
+        value = (value + biases[section : section + 1, pl.ds(at, chunk)]).astype(BF16)
         for r in range(size):
             which = 0 if first + r < halo else 2 if first + r >= rows - halo else 1
             part = value[r * width : (r + 1) * width]
@@ -171,7 +171,7 @@
                     [hidden[r + a, :, lane : lane + LANES] for a in range(3)],
                     lambda a, b: wide_depth[3 * a + b, :, here], 3, width,
                 )
-                value = (value + depth_bias[section : section + 1, here]).astype(BF16)
+                value = (value + biases[section : section + 1, pl.ds(hidden_channels + at + lane, LANES)]).astype(BF16)
                 lanes.append(six_hard_swish(value))
             spread.append(jnp.concatenate(lanes, axis=1))
         pixels = slice(first * width, (first + size) * width)
@@ -194,12 +194,12 @@
     for index in range(0, chunks, 2):
         stage(index, hidden_0, hidden_1)
         stage(index + 1, hidden_1, hidden_0 if index + 2 < chunks else None)
-    loads[0].wait()
-    value = total[...] * (1.0 / 6.0) + project_bias[section : section + 1, :]
+    last = slice(2 * hidden_channels, 2 * hidden_channels + channels)
+    value = total[...] * (1.0 / 6.0) + biases[section : section + 1, last]
     mixed[...] = value.astype(BF16).reshape(inner, width, channels)
-    store = pltpu.make_async_copy(mixed, mixed_out, sems.at[4])
+    store = pltpu.make_async_copy(mixed, mixed_out, sems.at[3])
     store.start()
-    for load in loads[1:]:
+    for load in loads:
         load.wait()
     spread_taps(agg, wide_agg)
     around = halo - 1
@@ -288,16 +288,16 @@
         grouped = aggregated(centre, wide_agg, group[...], 0, first, size, channels)
         query[here, :, channels : 2 * channels] = jnp.maximum(grouped, 0.0)
 
-    by_groups(rows - 4, 8, query_rows)
+    size = group_size(rows - 4, 8)
+    for first in range(0, rows - 4, size):
+        query_rows(first, size)
 
 
 def attend(
-    mixed_ref, query_ref, payloads, weight, bias_in, held, head_dim, section, x_ref
+    mixed_ref, query_ref, payloads, weight, biases, head_dim, section, x_ref
 ):
     rows, width, channels = x_ref.shape
-    bias, sem = held
-    load = pltpu.make_async_copy(bias_in, bias, sem)
-    load.start()
+    bias = biases[section : section + 1, biases.shape[1] - channels :]
     same = same_head(head_dim)
     square = (LANES, LANES)
     diagonal = lax.broadcasted_iota(jnp.int32, square, 0) == lax.broadcasted_iota(
@@ -330,7 +330,6 @@
     summaries = [paired(summaries, index) for index in range(0, count, 2)]
     sums = [paired(sums, index) for index in range(0, count, 2)]
     step = 2 * LANES
-    load.wait()
 
     def attend_rows(first, size):
         query = flat(query_ref[pl.ds(first, size)])
@@ -345,11 +344,13 @@
         value = jnp.dot(
             jnp.concatenate(parts, axis=1), weight[section], preferred_element_type=F32
         )
-        value = value + bias[section : section + 1, :]
+        value = value + bias
         value = value + flat(mixed_ref[pl.ds(first, size)]).astype(F32)
         x_ref[pl.ds(first, size)] = value.astype(BF16).reshape(size, width, channels)
 
-    by_groups(rows, 10, attend_rows)
+    size = group_size(rows, 10)
+    for first in range(0, rows, size):
+        attend_rows(first, size)
 
 
 def tap(section, a, b):
@@ -357,10 +358,9 @@
     return slice(at, at + 1)
 
 
-def prepare_kernel(head_dim, qkv, agg, group, head, project_bias, output_bias, *refs):
-    outs, made, taps, sems = refs[:6], refs[6:10], refs[10], refs[11]
+def prepare_kernel(head_dim, qkv, agg, group, head, *refs):
+    outs, made, taps, sems = refs[:4], refs[4:8], refs[8], refs[9]
     qkv_out, agg_out, group_out, head_out = made
-    made = [*made, project_bias, output_bias]
     sections, channels, wide = qkv.shape
     half = 3 * LANES
     heads = LANES // head_dim
@@ -405,7 +405,7 @@
     for a in range(3):
         rows = [head[a, b] for b in range(3)] + [jnp.zeros((4, channels), BF16)]
         head_out[a, 0:16, :] = jnp.concatenate(rows, axis=0)
-    stores = [pltpu.make_async_copy(made[i], outs[i], sems.at[i]) for i in range(6)]
+    stores = [pltpu.make_async_copy(made[i], outs[i], sems.at[i]) for i in range(4)]
     for store in stores:
         store.start()
     for store in stores:
@@ -415,7 +415,7 @@
 def first_kernel(
     tile, head_dim, own, col_1, col_0, row_1, row_0, corner_1, corner_0, *refs
 ):
-    weights, outs, scratch = refs[:9], refs[9:11], refs[11:]
+    weights, outs, scratch = refs[:7], refs[7:9], refs[9:]
     x_ref = scratch[0]
     rows, cols = tile
     below = REACH + rows
@@ -439,23 +439,23 @@
     front(x_ref, weights, outs, scratch[1:], REACH, tile, head_dim, 0)
 
 
-def second_kernel(tile, head_dim, mixed, query, payload, other, out_weight, out_bias, *refs):
-    weights, outs, scratch = refs[:9], refs[9:11], refs[11:]
+def second_kernel(tile, head_dim, mixed, query, payload, other, out_weight, biases, *refs):
+    weights, outs, scratch = refs[:7], refs[7:9], refs[9:]
     x_ref = scratch[0]
     attend(
-        mixed, query, (payload, other), out_weight, out_bias, scratch[1:3], head_dim, 0, x_ref
+        mixed, query, (payload, other), out_weight, biases, head_dim, 0, x_ref
     )
-    front(x_ref, weights, outs, scratch[3:], REACH - 3, tile, head_dim, 1)
+    front(x_ref, weights, outs, scratch[1:], REACH - 3, tile, head_dim, 1)
 
 
 def last_kernel(
-    tile, head_dim, mixed, query, payload, other, out_weight, out_bias, head_weight, head_bias,
-    map_out, boxes_out, x_ref, *held,
+    tile, head_dim, mixed, query, payload, other, out_weight, biases, head_weight, head_bias,
+    map_out, boxes_out, x_ref,
 ):
     rows, cols = tile
     width = cols + 2 * SIDE
     attend(
-        mixed, query, (payload, other), out_weight, out_bias, held, head_dim, 1, x_ref
+        mixed, query, (payload, other), out_weight, biases, head_dim, 1, x_ref
     )
     clear_outside(x_ref, 1, cols)
     map_out[...] = x_ref[1 : 1 + rows, 0:cols, :]
@@ -595,6 +595,7 @@
     corner_1 = pair_exchange(high, "row", 1)
     corner_0 = pair_exchange(low, "row", 0)
 
+    biases = jnp.concatenate([expand_bias, depth_bias, project_bias, output_bias], axis=1)
     aggregate_depth = aggregate_depth.transpose(1, 2, 0, 3)
     depth_weight = depth_weight.transpose(1, 2, 0, 3)
     params = pltpu.CompilerParams(vmem_limit_bytes=24 * 2**20)
@@ -604,27 +605,25 @@
         jax.ShapeDtypeStruct((SECTIONS, 3, channels, channels), BF16),
         jax.ShapeDtypeStruct((3, LANES, channels), BF16),
     ]
-    biases = [jax.ShapeDtypeStruct(array.shape, F32) for array in (project_bias, output_bias)]
-    qkv_weight, taps, group, head_weight, project_bias, output_bias = pl.pallas_call(
+    qkv_weight, taps, group, head_weight = pl.pallas_call(
         functools.partial(prepare_kernel, head_dim),
-        out_shape=made + biases,
+        out_shape=made,
         grid=(1,),
-        in_specs=[near()] * 6,
-        out_specs=[far()] * 6,
+        in_specs=[near()] * 4,
+        out_specs=[far()] * 4,
         scratch_shapes=[pltpu.VMEM(array.shape, array.dtype) for array in made]
-        + [pltpu.VMEM((32 * SECTIONS, 3 * channels), F32), pltpu.SemaphoreType.DMA((6,))],
+        + [pltpu.VMEM((32 * SECTIONS, 3 * channels), F32), pltpu.SemaphoreType.DMA((4,))],
         compiler_params=params,
         cost_estimate=pl.CostEstimate(
             flops=2 * 10**9, bytes_accessed=4 * 10**6, transcendentals=0
         ),
         name="prepare",
-    )(qkv_weight, aggregate_depth, aggregate_group, head_weight, project_bias, output_bias)
+    )(qkv_weight, aggregate_depth, aggregate_group, head_weight)
 
     weights = [
-        expand_weight, expand_bias, depth_weight, depth_bias, project_weight, project_bias,
-        qkv_weight, taps, group,
+        expand_weight, biases, depth_weight, project_weight, qkv_weight, taps, group,
     ]
-    weight_specs = [near()] * 5 + [far()] * 4
+    weight_specs = [near()] * 4 + [far()] * 3
 
     def outs_of(count):
         return [
@@ -642,18 +641,15 @@
             pltpu.VMEM((rows + 4, width, 2 * channels), BF16),
             pltpu.VMEM((9, TILE, expand_weight.shape[2]), BF16),
             pltpu.VMEM((25, TILE, 2 * channels), BF16),
-            pltpu.VMEM(project_bias.shape, F32),
             pltpu.VMEM((channels, 2 * channels), BF16),
             pltpu.VMEM((32, 2 * channels), F32),
             pltpu.VMEM((2, channels, channels), BF16),
-            pltpu.SemaphoreType.DMA((5,)),
+            pltpu.SemaphoreType.DMA((4,)),
         ]
 
     def attend_scratch(count):
         return [
             pltpu.VMEM((count, width, channels), BF16),
-            pltpu.VMEM(output_bias.shape, F32),
-            pltpu.SemaphoreType.DMA,
         ]
 
     def queries(mixed, section):
@@ -704,12 +700,12 @@
         functools.partial(second_kernel, tile, head_dim),
         out_shape=outs_of(second_rows - 2),
         grid=(1,),
-        in_specs=[near()] * 5 + [far()] + weight_specs,
+        in_specs=[near()] * 6 + weight_specs,
         out_specs=[far(), near()],
         scratch_shapes=attend_scratch(second_rows) + front_scratch(second_rows),
         compiler_params=params,
         name="second",
-    )(mixed, query, payload, other, output_weight, output_bias, *weights)
+    )(mixed, query, payload, other, output_weight, biases, *weights)
     query, mixed = queries(mixed, 1)
     payload, other = sum_by_permutes(payload)
 
@@ -720,13 +716,13 @@
             jax.ShapeDtypeStruct((4, rows, cols), F32),
         ],
         grid=(1,),
-        in_specs=[near()] * 5 + [far()] + [near()] * 2,
+        in_specs=[near()] * 8,
         out_specs=[near()] * 2,
         scratch_shapes=attend_scratch(rows + 2),
         compiler_params=params,
         name="last",
     )(
-        mixed, query, payload, other, output_weight, output_bias, head_weight,
+        mixed, query, payload, other, output_weight, biases, head_weight,
         head_bias.reshape(4, 1),
     )
 

time: 70.3 us -> 71.1 us (1.011)
  starting transfers between devices: 28.3 us -> 30.4 us
  Pallas kernels: 25.1 us -> 24.1 us
    ppermute x14, starting transfers between devices: 16.2 us -> 18.2 us  [sum_by_permutes(): lax.ppermute(value, axis, [(i, partner(i, stride, radix, k)) for i in ran...]
    ppermute x14, waiting for transfers between devices: 12.8 us -> 11.3 us  [sum_by_permutes(): lax.ppermute(value, axis, [(i, partner(i, stride, radix, k)) for i in ran...]
    ppermute x6, waiting for transfers between devices: 0.02 us -> 0.89 us  [pair_exchange(): return lax.ppermute(value, axis, pairs)]
    unnamed x28 -> x31, local copies, waits for them, and re-layouts: 1.65 us -> 2.11 us
  transfers between devices with their start and end apart: 20 -> 20, of which waited for: 11 -> 11; matrix products, arithmetic and copies ran while one was open for 0% -> 0% of each run, Pallas kernels for 10% -> 9%
where the time goes in v20:
time: 71.1 us; the launch traced here: 70.8 us
  starting transfers between devices  30.4 us (43%)
  Pallas kernels  24.1 us (34%)
  waiting for transfers between devices  12.2 us (17%)
  local copies, waits for them, and re-layouts  3.1 us (4%)
  between operations  0.91 us (1%)
    ppermute x14, starting transfers between devices, sum_by_permutes(): lax.ppermute(value, axis, [(i, partner(i, stride, radix, k)) for i in ran...  18.2 us
    ppermute x6, starting transfers between devices, pair_exchange(): return lax.ppermute(value, axis, pairs)  12.2 us
    ppermute x14, waiting for transfers between devices, sum_by_permutes(): lax.ppermute(value, axis, [(i, partner(i, stride, radix, k)) for i in ran...  11.3 us
    pallas_call x1, Pallas kernels, local(): pl.pallas_call(functools.partial(first_kernel, tile, head_dim), out_shape...  7.96 us
    pallas_call x1, Pallas kernels, local(): pl.pallas_call(functools.partial(second_kernel, tile, head_dim), out_shap...  7.31 us
    pallas_call x2, Pallas kernels, queries(): pl.pallas_call(functools.partial(query_kernel, tile, section), out_shape=...  4.73 us
    pallas_call x1, Pallas kernels, local(): pl.pallas_call(functools.partial(last_kernel, tile, head_dim), out_shape=...  2.2 us
    unnamed x31, local copies, waits for them, and re-layouts  2.11 us
  transfers between devices with their start and end apart: 20, of which 11 were waited for; matrix products, arithmetic and copies ran while one was open for 0% of the time, Pallas kernels for 9%

profile of v20, /device:TPU:0, one launch (start us, length us, event | category | flops | bytes accessed | tf_op | source)
XLA Modules:
  0.0 70.8 jit_solution(3313733855786070972)
XLA Ops:
  2.2 5.8 %collective-permute-start.1 = (bf16[8,8,256]{2,1,0:T(8,128)(2,1)S(1)}, bf16[8,8,256]{2,1,0:T(8,128)(2,1)S(1)}, u32[]{:S(2)}, u32[]{:S(2)}) collective-permute-start(bf16[8,8,256]{2,1,0:T(8,128)(2,1)S(1)} %get-tuple-element.28), channel_id=1, source_target_pairs={{0,1},{1,0},{2,3},{3,2},{4,5},{5,4},{6,7},{7,6},{8,9},{9,8},{10,11... | collective-permute-start | bytes 98312 | tf_op jit(solution)/shard_map/ppermute | solution.py:551
  8.7 2.9 %collective-permute-start.3 = (bf16[7,32,256]{2,1,0:T(8,128)(2,1)S(1)}, bf16[7,32,256]{2,1,0:T(8,128)(2,1)S(1)}, u32[]{:S(2)}, u32[]{:S(2)}) collective-permute-start(bf16[7,32,256]{2,1,0:T(8,128)(2,1)S(1)} %get-tuple-element.26), channel_id=1, source_target_pairs={{0,8},{8,0},{16,24},{24,16},{1,9},{9,1},{17,25},{25,17},{2,10},{10... | collective-permute-start | bytes 344072 | tf_op jit(solution)/shard_map/ppermute | solution.py:551
  11.6 1.1 %copy-done.5 = bf16[2,256,768]{2,1,0:T(8,128)(2,1)S(1)} copy-done((bf16[2,256,768]{2,1,0:T(8,128)(2,1)S(1)}, bf16[2,256,768]{2,1,0:T(8,128)(2,1)}, u32[]{:S(2)}) %copy-start.5) | copy-done | bytes 786456
  13.7 1.9 %prepare.1 = (bf16[2,256,768]{2,1,0:T(8,128)(2,1)S(1)}, f32[2,32,768]{2,1,0:T(8,128)S(1)}, bf16[2,3,256,256]{3,2,1,0:T(8,128)(2,1)S(1)}, bf16[3,128,256]{2,1,0:T(8,128)(2,1)S(1)}) custom-call(bf16[2,256,768]{2,1,0:T(8,128)(2,1)S(1)} %copy-done.5, f32[5,5,2,768]{3,2,1,0:T(2,128)S(1)} %bitcast.5, bf16[2,24,32,32]{3,2,1,0:T(8,128)(2,1)S(1)} %copy-done.6, ...), custom_call_target="tpu_custom_call" | custom-call | flops 2000000000 | bytes 4000000 | tf_op jit(solution)/shard_map/prepare/pallas_call | solution.py:608
  16.5 1.4 %collective-permute-start.5 = (bf16[14,8,256]{2,1,0:T(8,128)(2,1)S(1)}, bf16[14,8,256]{2,1,0:T(8,128)(2,1)S(1)}, u32[]{:S(2)}, u32[]{:S(2)}) collective-permute-start(bf16[14,8,256]{2,1,0:T(8,128)(2,1)S(1)} %pad_maximum_fusion.1), channel_id=1, source_target_pairs={{0,8},{8,0},{16,24},{24,16},{1,9},{9,1},{17,25},{25,17},{2,10},{10... | collective-permute-start | bytes 172040 | tf_op jit(solution)/shard_map/ppermute | solution.py:551
  18.8 8.0 %first.1 = (bf16[20,48,256]{2,1,0:T(8,128)(2,1)S(1)}, bf16[144,128]{1,0:T(8,128)(2,1)S(1)}) custom-call(bf16[8,32,256]{2,1,0:T(8,128)(2,1)S(1)} %copy-done.3, bf16[8,8,256]{2,1,0:T(8,128)(2,1)S(1)} %collective-permute-done.col_1, bf16[8,8,256]{2,1,0:T(8,128)(2,1)S(1)} %collective-permute-done.1.col_0, bf16[7,32,256]{2,1,0:T(8,128)(2,1)S(1)} %collective-permute-done.2.row_1, ...), custom_call_target="tpu_custom_call" | custom-call | tf_op jit(solution)/shard_map/first/pallas_call | solution.py:684
  26.8 1.8 %collective-permute-start.8 = (bf16[144,128]{1,0:T(8,128)(2,1)S(1)}, bf16[144,128]{1,0:T(8,128)(2,1)S(1)}, u32[]{:S(2)}, u32[]{:S(2)}) collective-permute-start(bf16[144,128]{1,0:T(8,128)(2,1)S(1)} %get-tuple-element.20), channel_id=1, source_target_pairs={{0,24},{8,16},{16,8},{24,0},{1,25},{9,17},{17,9},{25,1},{2,26},{10... | collective-permute-start | bytes 110600 | tf_op jit(solution)/shard_map/ppermute | solution.py:525
  28.6 2.5 %collective-permute-start.7 = (bf16[144,128]{1,0:T(8,128)(2,1)S(1)}, bf16[144,128]{1,0:T(8,128)(2,1)S(1)}, u32[]{:S(2)}, u32[]{:S(2)}) collective-permute-start(bf16[144,128]{1,0:T(8,128)(2,1)S(1)} %get-tuple-element.20), channel_id=1, source_target_pairs={{0,16},{8,24},{16,0},{24,8},{1,17},{9,25},{17,1},{25,9},{2,18},{10... | collective-permute-start | bytes 110600 | tf_op jit(solution)/shard_map/ppermute | solution.py:525
  31.1 2.3 %collective-permute-done.7 = bf16[144,128]{1,0:T(8,128)(2,1)S(1)} collective-permute-done((bf16[144,128]{1,0:T(8,128)(2,1)S(1)}, bf16[144,128]{1,0:T(8,128)(2,1)S(1)}, u32[]{:S(2)}, u32[]{:S(2)}) %collective-permute-start.7) | collective-permute-done | bytes 36896 | tf_op jit(solution)/shard_map/ppermute | solution.py:525
  33.4 1.5 %collective-permute-start.11 = (bf16[144,128]{1,0:T(8,128)(2,1)S(1)}, bf16[144,128]{1,0:T(8,128)(2,1)S(1)}, u32[]{:S(2)}, u32[]{:S(2)}) collective-permute-start(bf16[144,128]{1,0:T(8,128)(2,1)S(1)} %add_convert_fusion.3), channel_id=1, source_target_pairs={{0,3},{1,2},{2,1},{3,0},{4,7},{5,6},{6,5},{7,4},{8,11},{9,10},{10,... | collective-permute-start | bytes 110600 | tf_op jit(solution)/shard_map/ppermute | solution.py:525
  35.1 1.8 %collective-permute-start.9 = (bf16[144,128]{1,0:T(8,128)(2,1)S(1)}, bf16[144,128]{1,0:T(8,128)(2,1)S(1)}, u32[]{:S(2)}, u32[]{:S(2)}) collective-permute-start(bf16[144,128]{1,0:T(8,128)(2,1)S(1)} %add_convert_fusion.3), channel_id=1, source_target_pairs={{0,1},{1,0},{2,3},{3,2},{4,5},{5,4},{6,7},{7,6},{8,9},{9,8},{10,11... | collective-permute-start | bytes 110600 | tf_op jit(solution)/shard_map/ppermute | solution.py:525
  37.0 1.5 %collective-permute-done.11 = bf16[144,128]{1,0:T(8,128)(2,1)S(1)} collective-permute-done((bf16[144,128]{1,0:T(8,128)(2,1)S(1)}, bf16[144,128]{1,0:T(8,128)(2,1)S(1)}, u32[]{:S(2)}, u32[]{:S(2)}) %collective-permute-start.11) | collective-permute-done | bytes 36896 | tf_op jit(solution)/shard_map/ppermute | solution.py:525
  39.1 2.9 %collective-permute-start.12 = (bf16[144,128]{1,0:T(8,128)(2,1)S(1)}, bf16[144,128]{1,0:T(8,128)(2,1)S(1)}, u32[]{:S(2)}, u32[]{:S(2)}) collective-permute-start(bf16[144,128]{1,0:T(8,128)(2,1)S(1)} %add_convert_fusion.2.payload), channel_id=1, source_target_pairs={{0,4},{1,5},{2,6},{3,7},{4,0},{5,1},{6,2},{7,3},{8,12},{9,13},{10,... | collective-permute-start | bytes 110600 | tf_op jit(solution)/shard_map/ppermute | solution.py:525
  42.0 2.9 %queries.2 = (bf16[16,48,512]{2,1,0:T(8,128)(2,1)S(1)}, bf16[16,48,256]{2,1,0:T(8,128)(2,1)S(1)}) custom-call(bf16[20,48,256]{2,1,0:T(8,128)(2,1)S(1)} %get-tuple-element.17.mixed_in, bf16[2,256,768]{2,1,0:T(8,128)(2,1)S(1)} %get-tuple-element.14.refs_4_.qkv_weight, f32[2,32,768]{2,1,0:T(8,128)S(1)} %get-tuple-element.15.refs_5_.taps, ...), custom_call_target="tpu_custom_call" | custom-call | flops 402653184 | bytes 1572864 | tf_op jit(solution)/shard_map/queries/pallas_call | solution.py:658
  44.9 7.3 %second.1 = (bf16[14,48,256]{2,1,0:T(8,128)(2,1)S(1)}, bf16[144,128]{1,0:T(8,128)(2,1)S(1)}) custom-call(bf16[16,48,256]{2,1,0:T(8,128)(2,1)S(1)} %get-tuple-element.18.mixed, bf16[16,48,512]{2,1,0:T(8,128)(2,1)S(1)} %get-tuple-element.19.query, bf16[144,128]{1,0:T(8,128)(2,1)S(1)} %add_convert_fusion.2.payload, ...), custom_call_target="tpu_custom_call" | custom-call | tf_op jit(solution)/shard_map/second/pallas_call | solution.py:699
  52.3 1.7 %collective-permute-start.14 = (bf16[144,128]{1,0:T(8,128)(2,1)S(1)}, bf16[144,128]{1,0:T(8,128)(2,1)S(1)}, u32[]{:S(2)}, u32[]{:S(2)}) collective-permute-start(bf16[144,128]{1,0:T(8,128)(2,1)S(1)} %get-tuple-element.24), channel_id=1, source_target_pairs={{0,16},{8,24},{16,0},{24,8},{1,17},{9,25},{17,1},{25,9},{2,18},{10... | collective-permute-start | bytes 110600 | tf_op jit(solution)/shard_map/ppermute | solution.py:525
  54.2 1.7 %collective-permute-done.15 = bf16[144,128]{1,0:T(8,128)(2,1)S(1)} collective-permute-done((bf16[144,128]{1,0:T(8,128)(2,1)S(1)}, bf16[144,128]{1,0:T(8,128)(2,1)S(1)}, u32[]{:S(2)}, u32[]{:S(2)}) %collective-permute-start.15) | collective-permute-done | bytes 36896 | tf_op jit(solution)/shard_map/ppermute | solution.py:525
  56.5 2.1 %collective-permute-start.18 = (bf16[144,128]{1,0:T(8,128)(2,1)S(1)}, bf16[144,128]{1,0:T(8,128)(2,1)S(1)}, u32[]{:S(2)}, u32[]{:S(2)}) collective-permute-start(bf16[144,128]{1,0:T(8,128)(2,1)S(1)} %add_convert_fusion.1), channel_id=1, source_target_pairs={{0,3},{1,2},{2,1},{3,0},{4,7},{5,6},{6,5},{7,4},{8,11},{9,10},{10,... | collective-permute-start | bytes 110600 | tf_op jit(solution)/shard_map/ppermute | solution.py:525
  58.6 1.1 %collective-permute-start.17 = (bf16[144,128]{1,0:T(8,128)(2,1)S(1)}, bf16[144,128]{1,0:T(8,128)(2,1)S(1)}, u32[]{:S(2)}, u32[]{:S(2)}) collective-permute-start(bf16[144,128]{1,0:T(8,128)(2,1)S(1)} %add_convert_fusion.1), channel_id=1, source_target_pairs={{0,2},{1,3},{2,0},{3,1},{4,6},{5,7},{6,4},{7,5},{8,10},{9,11},{10,... | collective-permute-start | bytes 110600 | tf_op jit(solution)/shard_map/ppermute | solution.py:525
  60.1 1.4 %collective-permute-done.18 = bf16[144,128]{1,0:T(8,128)(2,1)S(1)} collective-permute-done((bf16[144,128]{1,0:T(8,128)(2,1)S(1)}, bf16[144,128]{1,0:T(8,128)(2,1)S(1)}, u32[]{:S(2)}, u32[]{:S(2)}) %collective-permute-start.18) | collective-permute-done | bytes 36896 | tf_op jit(solution)/shard_map/ppermute | solution.py:525
  62.5 1.1 %collective-permute-done.16 = bf16[144,128]{1,0:T(8,128)(2,1)S(1)} collective-permute-done((bf16[144,128]{1,0:T(8,128)(2,1)S(1)}, bf16[144,128]{1,0:T(8,128)(2,1)S(1)}, u32[]{:S(2)}, u32[]{:S(2)}) %collective-permute-start.16) | collective-permute-done | bytes 36896 | tf_op jit(solution)/shard_map/ppermute | solution.py:525
  63.6 2.0 %collective-permute-start.19 = (bf16[144,128]{1,0:T(8,128)(2,1)S(1)}, bf16[144,128]{1,0:T(8,128)(2,1)S(1)}, u32[]{:S(2)}, u32[]{:S(2)}) collective-permute-start(bf16[144,128]{1,0:T(8,128)(2,1)S(1)} %add_convert_fusion.payload), channel_id=1, source_target_pairs={{0,4},{1,5},{2,6},{3,7},{4,0},{5,1},{6,2},{7,3},{8,12},{9,13},{10,... | collective-permute-start | bytes 110600 | tf_op jit(solution)/shard_map/ppermute | solution.py:525
  65.8 1.8 %queries.3 = (bf16[10,48,512]{2,1,0:T(8,128)(2,1)S(1)}, bf16[10,48,256]{2,1,0:T(8,128)(2,1)S(1)}) custom-call(bf16[14,48,256]{2,1,0:T(8,128)(2,1)S(1)} %get-tuple-element.21.mixed_in, bf16[2,256,768]{2,1,0:T(8,128)(2,1)S(1)} %get-tuple-element.14.refs_4_.qkv_weight, f32[2,32,768]{2,1,0:T(8,128)S(1)} %get-tuple-element.15.refs_5_.taps, ...), custom_call_target="tpu_custom_call" | custom-call | flops 251658240 | bytes 983040 | tf_op jit(solution)/shard_map/queries/pallas_call | solution.py:658
  68.6 2.2 %last.1 = (bf16[8,32,256]{2,1,0:T(8,128)(2,1)}, f32[4,8,32]{2,1,0:T(8,128)}) custom-call(bf16[10,48,256]{2,1,0:T(8,128)(2,1)S(1)} %get-tuple-element.22.mixed, bf16[10,48,512]{2,1,0:T(8,128)(2,1)S(1)} %get-tuple-element.23.query, bf16[144,128]{1,0:T(8,128)(2,1)S(1)} %add_convert_fusion.payload, bf16[144,128]{1,0:T(8,128)(2,1)S(1)} %collective-permute-done.19.other, ...), custom_call_target="tpu_custom_call" | custom-call | tf_op jit(solution)/shard_map/last/pallas_call | solution.py:712
  (65 shorter events, 9.3 us)
Async XLA Ops:
  0.6 7.3 %copy-start.3 = (bf16[8,32,256]{2,1,0:T(8,128)(2,1)S(1)}, bf16[8,32,256]{2,1,0:T(8,128)(2,1)}, u32[]{:S(2)}) copy-start(bf16[8,32,256]{2,1,0:T(8,128)(2,1)} %own.1) | copy-start | bytes 393220
  0.6 11.0 %copy-start.6 = (bf16[2,24,32,32]{3,2,1,0:T(8,128)(2,1)S(1)}, bf16[2,24,32,32]{3,2,1,0:T(8,128)(2,1)}, u32[]{:S(2)}) copy-start(bf16[2,24,32,32]{3,2,1,0:T(8,128)(2,1)} %group.1) | copy-start | bytes 294916
  1.5 14.1 %collective-permute-start = (bf16[8,8,256]{2,1,0:T(8,128)(2,1)S(1)}, bf16[8,8,256]{2,1,0:T(8,128)(2,1)S(1)}, u32[]{:S(2)}, u32[]{:S(2)}) collective-permute-start(bf16[8,8,256]{2,1,0:T(8,128)(2,1)S(1)} %get-tuple-element.29), channel_id=1, source_target_pairs={{1,2},{2,1},{3,4},{4,3},{5,6},{6,5},{9,10},{10,9},{11,12},{12,11},... | collective-permute-start | bytes 98312 | tf_op jit(solution)/shard_map/ppermute | solution.py:551
  2.2 13.5 %collective-permute-start.1 = (bf16[8,8,256]{2,1,0:T(8,128)(2,1)S(1)}, bf16[8,8,256]{2,1,0:T(8,128)(2,1)S(1)}, u32[]{:S(2)}, u32[]{:S(2)}) collective-permute-start(bf16[8,8,256]{2,1,0:T(8,128)(2,1)S(1)} %get-tuple-element.28), channel_id=1, source_target_pairs={{0,1},{1,0},{2,3},{3,2},{4,5},{5,4},{6,7},{7,6},{8,9},{9,8},{10,11... | collective-permute-start | bytes 98312 | tf_op jit(solution)/shard_map/ppermute | solution.py:551
  8.0 10.8 %collective-permute-start.2 = (bf16[7,32,256]{2,1,0:T(8,128)(2,1)S(1)}, bf16[7,32,256]{2,1,0:T(8,128)(2,1)S(1)}, u32[]{:S(2)}, u32[]{:S(2)}) collective-permute-start(bf16[7,32,256]{2,1,0:T(8,128)(2,1)S(1)} %get-tuple-element.27), channel_id=1, source_target_pairs={{8,16},{16,8},{9,17},{17,9},{10,18},{18,10},{11,19},{19,11},{12,20... | collective-permute-start | bytes 344072 | tf_op jit(solution)/shard_map/ppermute | solution.py:551
  8.7 10.1 %collective-permute-start.3 = (bf16[7,32,256]{2,1,0:T(8,128)(2,1)S(1)}, bf16[7,32,256]{2,1,0:T(8,128)(2,1)S(1)}, u32[]{:S(2)}, u32[]{:S(2)}) collective-permute-start(bf16[7,32,256]{2,1,0:T(8,128)(2,1)S(1)} %get-tuple-element.26), channel_id=1, source_target_pairs={{0,8},{8,0},{16,24},{24,16},{1,9},{9,1},{17,25},{25,17},{2,10},{10... | collective-permute-start | bytes 344072 | tf_op jit(solution)/shard_map/ppermute | solution.py:551
  13.7 5.1 %copy-start = (bf16[2,256,1024]{2,1,0:T(8,128)(2,1)S(1)}, bf16[2,256,1024]{2,1,0:T(8,128)(2,1)}, u32[]{:S(2)}) copy-start(bf16[2,256,1024]{2,1,0:T(8,128)(2,1)} %refs_0_.3) | copy-start | bytes 3145732
  13.7 5.1 %copy-start.1 = (bf16[2,1024,256]{2,1,0:T(8,128)(2,1)S(1)}, bf16[2,1024,256]{2,1,0:T(8,128)(2,1)}, u32[]{:S(2)}) copy-start(bf16[2,1024,256]{2,1,0:T(8,128)(2,1)} %refs_3_.3) | copy-start | bytes 3145732
  15.7 2.2 %collective-permute-start.4 = (bf16[14,8,256]{2,1,0:T(8,128)(2,1)S(1)}, bf16[14,8,256]{2,1,0:T(8,128)(2,1)S(1)}, u32[]{:S(2)}, u32[]{:S(2)}) collective-permute-start(bf16[14,8,256]{2,1,0:T(8,128)(2,1)S(1)} %pad_maximum_fusion), channel_id=1, source_target_pairs={{8,16},{16,8},{9,17},{17,9},{10,18},{18,10},{11,19},{19,11},{12,20... | collective-permute-start | bytes 172040 | tf_op jit(solution)/shard_map/ppermute | solution.py:551
  16.5 2.3 %collective-permute-start.5 = (bf16[14,8,256]{2,1,0:T(8,128)(2,1)S(1)}, bf16[14,8,256]{2,1,0:T(8,128)(2,1)S(1)}, u32[]{:S(2)}, u32[]{:S(2)}) collective-permute-start(bf16[14,8,256]{2,1,0:T(8,128)(2,1)S(1)} %pad_maximum_fusion.1), channel_id=1, source_target_pairs={{0,8},{8,0},{16,24},{24,16},{1,9},{9,1},{17,25},{25,17},{2,10},{10... | collective-permute-start | bytes 172040 | tf_op jit(solution)/shard_map/ppermute | solution.py:551
  26.8 4.3 %collective-permute-start.8 = (bf16[144,128]{1,0:T(8,128)(2,1)S(1)}, bf16[144,128]{1,0:T(8,128)(2,1)S(1)}, u32[]{:S(2)}, u32[]{:S(2)}) collective-permute-start(bf16[144,128]{1,0:T(8,128)(2,1)S(1)} %get-tuple-element.20), channel_id=1, source_target_pairs={{0,24},{8,16},{16,8},{24,0},{1,25},{9,17},{17,9},{25,1},{2,26},{10... | collective-permute-start | bytes 110600 | tf_op jit(solution)/shard_map/ppermute | solution.py:525
  28.6 4.8 %collective-permute-start.7 = (bf16[144,128]{1,0:T(8,128)(2,1)S(1)}, bf16[144,128]{1,0:T(8,128)(2,1)S(1)}, u32[]{:S(2)}, u32[]{:S(2)}) collective-permute-start(bf16[144,128]{1,0:T(8,128)(2,1)S(1)} %get-tuple-element.20), channel_id=1, source_target_pairs={{0,16},{8,24},{16,0},{24,8},{1,17},{9,25},{17,1},{25,9},{2,18},{10... | collective-permute-start | bytes 110600 | tf_op jit(solution)/shard_map/ppermute | solution.py:525
  31.1 2.3 %collective-permute-start.6 = (bf16[144,128]{1,0:T(8,128)(2,1)S(1)}, bf16[144,128]{1,0:T(8,128)(2,1)S(1)}, u32[]{:S(2)}, u32[]{:S(2)}) collective-permute-start(bf16[144,128]{1,0:T(8,128)(2,1)S(1)} %get-tuple-element.20), channel_id=1, source_target_pairs={{0,8},{8,0},{16,24},{24,16},{1,9},{9,1},{17,25},{25,17},{2,10},{10... | collective-permute-start | bytes 110600 | tf_op jit(solution)/shard_map/ppermute | solution.py:525
  33.4 5.1 %collective-permute-start.11 = (bf16[144,128]{1,0:T(8,128)(2,1)S(1)}, bf16[144,128]{1,0:T(8,128)(2,1)S(1)}, u32[]{:S(2)}, u32[]{:S(2)}) collective-permute-start(bf16[144,128]{1,0:T(8,128)(2,1)S(1)} %add_convert_fusion.3), channel_id=1, source_target_pairs={{0,3},{1,2},{2,1},{3,0},{4,7},{5,6},{6,5},{7,4},{8,11},{9,10},{10,... | collective-permute-start | bytes 110600 | tf_op jit(solution)/shard_map/ppermute | solution.py:525
  34.9 4.0 %collective-permute-start.10 = (bf16[144,128]{1,0:T(8,128)(2,1)S(1)}, bf16[144,128]{1,0:T(8,128)(2,1)S(1)}, u32[]{:S(2)}, u32[]{:S(2)}) collective-permute-start(bf16[144,128]{1,0:T(8,128)(2,1)S(1)} %add_convert_fusion.3), channel_id=1, source_target_pairs={{0,2},{1,3},{2,0},{3,1},{4,6},{5,7},{6,4},{7,5},{8,10},{9,11},{10,... | collective-permute-start | bytes 110600 | tf_op jit(solution)/shard_map/ppermute | solution.py:525
  35.1 4.0 %collective-permute-start.9 = (bf16[144,128]{1,0:T(8,128)(2,1)S(1)}, bf16[144,128]{1,0:T(8,128)(2,1)S(1)}, u32[]{:S(2)}, u32[]{:S(2)}) collective-permute-start(bf16[144,128]{1,0:T(8,128)(2,1)S(1)} %add_convert_fusion.3), channel_id=1, source_target_pairs={{0,1},{1,0},{2,3},{3,2},{4,5},{5,4},{6,7},{7,6},{8,9},{9,8},{10,11... | collective-permute-start | bytes 110600 | tf_op jit(solution)/shard_map/ppermute | solution.py:525
  39.1 5.8 %collective-permute-start.12 = (bf16[144,128]{1,0:T(8,128)(2,1)S(1)}, bf16[144,128]{1,0:T(8,128)(2,1)S(1)}, u32[]{:S(2)}, u32[]{:S(2)}) collective-permute-start(bf16[144,128]{1,0:T(8,128)(2,1)S(1)} %add_convert_fusion.2.payload), channel_id=1, source_target_pairs={{0,4},{1,5},{2,6},{3,7},{4,0},{5,1},{6,2},{7,3},{8,12},{9,13},{10,... | collective-permute-start | bytes 110600 | tf_op jit(solution)/shard_map/ppermute | solution.py:525
  52.2 3.7 %collective-permute-start.15 = (bf16[144,128]{1,0:T(8,128)(2,1)S(1)}, bf16[144,128]{1,0:T(8,128)(2,1)S(1)}, u32[]{:S(2)}, u32[]{:S(2)}) collective-permute-start(bf16[144,128]{1,0:T(8,128)(2,1)S(1)} %get-tuple-element.24), channel_id=1, source_target_pairs={{0,24},{8,16},{16,8},{24,0},{1,25},{9,17},{17,9},{25,1},{2,26},{10... | collective-permute-start | bytes 110600 | tf_op jit(solution)/shard_map/ppermute | solution.py:525
  52.3 4.2 %collective-permute-start.14 = (bf16[144,128]{1,0:T(8,128)(2,1)S(1)}, bf16[144,128]{1,0:T(8,128)(2,1)S(1)}, u32[]{:S(2)}, u32[]{:S(2)}) collective-permute-start(bf16[144,128]{1,0:T(8,128)(2,1)S(1)} %get-tuple-element.24), channel_id=1, source_target_pairs={{0,16},{8,24},{16,0},{24,8},{1,17},{9,25},{17,1},{25,9},{2,18},{10... | collective-permute-start | bytes 110600 | tf_op jit(solution)/shard_map/ppermute | solution.py:525
  54.0 2.5 %collective-permute-start.13 = (bf16[144,128]{1,0:T(8,128)(2,1)S(1)}, bf16[144,128]{1,0:T(8,128)(2,1)S(1)}, u32[]{:S(2)}, u32[]{:S(2)}) collective-permute-start(bf16[144,128]{1,0:T(8,128)(2,1)S(1)} %get-tuple-element.24), channel_id=1, source_target_pairs={{0,8},{8,0},{16,24},{24,16},{1,9},{9,1},{17,25},{25,17},{2,10},{10... | collective-permute-start | bytes 110600 | tf_op jit(solution)/shard_map/ppermute | solution.py:525
  56.5 4.9 %collective-permute-start.18 = (bf16[144,128]{1,0:T(8,128)(2,1)S(1)}, bf16[144,128]{1,0:T(8,128)(2,1)S(1)}, u32[]{:S(2)}, u32[]{:S(2)}) collective-permute-start(bf16[144,128]{1,0:T(8,128)(2,1)S(1)} %add_convert_fusion.1), channel_id=1, source_target_pairs={{0,3},{1,2},{2,1},{3,0},{4,7},{5,6},{6,5},{7,4},{8,11},{9,10},{10,... | collective-permute-start | bytes 110600 | tf_op jit(solution)/shard_map/ppermute | solution.py:525
  58.6 4.0 %collective-permute-start.17 = (bf16[144,128]{1,0:T(8,128)(2,1)S(1)}, bf16[144,128]{1,0:T(8,128)(2,1)S(1)}, u32[]{:S(2)}, u32[]{:S(2)}) collective-permute-start(bf16[144,128]{1,0:T(8,128)(2,1)S(1)} %add_convert_fusion.1), channel_id=1, source_target_pairs={{0,2},{1,3},{2,0},{3,1},{4,6},{5,7},{6,4},{7,5},{8,10},{9,11},{10,... | collective-permute-start | bytes 110600 | tf_op jit(solution)/shard_map/ppermute | solution.py:525
  59.6 4.0 %collective-permute-start.16 = (bf16[144,128]{1,0:T(8,128)(2,1)S(1)}, bf16[144,128]{1,0:T(8,128)(2,1)S(1)}, u32[]{:S(2)}, u32[]{:S(2)}) collective-permute-start(bf16[144,128]{1,0:T(8,128)(2,1)S(1)} %add_convert_fusion.1), channel_id=1, source_target_pairs={{0,1},{1,0},{2,3},{3,2},{4,5},{5,4},{6,7},{7,6},{8,9},{9,8},{10,11... | collective-permute-start | bytes 110600 | tf_op jit(solution)/shard_map/ppermute | solution.py:525
  63.6 4.9 %collective-permute-start.19 = (bf16[144,128]{1,0:T(8,128)(2,1)S(1)}, bf16[144,128]{1,0:T(8,128)(2,1)S(1)}, u32[]{:S(2)}, u32[]{:S(2)}) collective-permute-start(bf16[144,128]{1,0:T(8,128)(2,1)S(1)} %add_convert_fusion.payload), channel_id=1, source_target_pairs={{0,4},{1,5},{2,6},{3,7},{4,0},{5,1},{6,2},{7,3},{8,12},{9,13},{10,... | collective-permute-start | bytes 110600 | tf_op jit(solution)/shard_map/ppermute | solution.py:525
  (10 other events, 24.3 us)

commit v21 on v19

--- a/solution.py
+++ b/solution.py
@@ -29,16 +29,6 @@
 
 def group_size(count, most):
     return next(n for n in range(min(most, count), 0, -1) if count % n == 0)
-
-
-def by_groups(count, most, body):
-    size = group_size(count, most)
-
-    def group(index, carry):
-        body(index * size, size)
-        return carry
-
-    lax.fori_loop(0, count // size, group, 0)
 
 
 def clear_outside(ref, halo, cols):
@@ -288,7 +278,9 @@
         grouped = aggregated(centre, wide_agg, group[...], 0, first, size, channels)
         query[here, :, channels : 2 * channels] = jnp.maximum(grouped, 0.0)
 
-    by_groups(rows - 4, 8, query_rows)
+    size = group_size(rows - 4, 8)
+    for first in range(0, rows - 4, size):
+        query_rows(first, size)
 
 
 def attend(
@@ -349,7 +341,9 @@
         value = value + flat(mixed_ref[pl.ds(first, size)]).astype(F32)
         x_ref[pl.ds(first, size)] = value.astype(BF16).reshape(size, width, channels)
 
-    by_groups(rows, 10, attend_rows)
+    size = group_size(rows, 10)
+    for first in range(0, rows, size):
+        attend_rows(first, size)
 
 
 def tap(section, a, b):

time: 70.3 us -> 70 us (level)
  no operation moved by 1% of the time
where the time goes in v21:
time: 70 us; the launch traced here: 69.7 us
  starting transfers between devices  28.4 us (41%)
  Pallas kernels  24.6 us (35%)
  waiting for transfers between devices  12.9 us (18%)
  local copies, waits for them, and re-layouts  2.61 us (4%)
  between operations  1.09 us (2%)
    ppermute x14, starting transfers between devices, sum_by_permutes(): lax.ppermute(value, axis, [(i, partner(i, stride, radix, k)) for i in ran...  16.3 us
    ppermute x14, waiting for transfers between devices, sum_by_permutes(): lax.ppermute(value, axis, [(i, partner(i, stride, radix, k)) for i in ran...  12.9 us
    ppermute x6, starting transfers between devices, pair_exchange(): return lax.ppermute(value, axis, pairs)  12.2 us
    pallas_call x1, Pallas kernels, local(): pl.pallas_call(functools.partial(first_kernel, tile, head_dim), out_shape...  8.04 us
    pallas_call x1, Pallas kernels, local(): pl.pallas_call(functools.partial(second_kernel, tile, head_dim), out_shap...  7.54 us
    pallas_call x2, Pallas kernels, queries(): pl.pallas_call(functools.partial(query_kernel, tile, section), out_shape=...  4.71 us
    pallas_call x1, Pallas kernels, local(): pl.pallas_call(functools.partial(last_kernel, tile, head_dim), out_shape=...  2.33 us
    pallas_call x1, Pallas kernels, local(): pl.pallas_call(functools.partial(prepare_kernel, head_dim), out_shape=mad...  1.92 us
  transfers between devices with their start and end apart: 20, of which 11 were waited for; matrix products, arithmetic and copies ran while one was open for 0% of the time, Pallas kernels for 10%

profile of v21, /device:TPU:0, one launch (start us, length us, event | category | flops | bytes accessed | tf_op | source)
XLA Modules:
  0.0 69.7 jit_solution(16711338693909716731)
XLA Ops:
  2.1 5.8 %collective-permute-start.1 = (bf16[8,8,256]{2,1,0:T(8,128)(2,1)S(1)}, bf16[8,8,256]{2,1,0:T(8,128)(2,1)S(1)}, u32[]{:S(2)}, u32[]{:S(2)}) collective-permute-start(bf16[8,8,256]{2,1,0:T(8,128)(2,1)S(1)} %get-tuple-element.32), channel_id=1, source_target_pairs={{0,1},{1,0},{2,3},{3,2},{4,5},{5,4},{6,7},{7,6},{8,9},{9,8},{10,11... | collective-permute-start | bytes 98312 | tf_op jit(solution)/shard_map/ppermute | solution.py:545
  8.8 2.9 %collective-permute-start.3 = (bf16[7,32,256]{2,1,0:T(8,128)(2,1)S(1)}, bf16[7,32,256]{2,1,0:T(8,128)(2,1)S(1)}, u32[]{:S(2)}, u32[]{:S(2)}) collective-permute-start(bf16[7,32,256]{2,1,0:T(8,128)(2,1)S(1)} %get-tuple-element.30), channel_id=1, source_target_pairs={{0,8},{8,0},{16,24},{24,16},{1,9},{9,1},{17,25},{25,17},{2,10},{10... | collective-permute-start | bytes 344072 | tf_op jit(solution)/shard_map/ppermute | solution.py:545
  12.5 1.4 %collective-permute-start.5 = (bf16[14,8,256]{2,1,0:T(8,128)(2,1)S(1)}, bf16[14,8,256]{2,1,0:T(8,128)(2,1)S(1)}, u32[]{:S(2)}, u32[]{:S(2)}) collective-permute-start(bf16[14,8,256]{2,1,0:T(8,128)(2,1)S(1)} %pad_maximum_fusion.1), channel_id=1, source_target_pairs={{0,8},{8,0},{16,24},{24,16},{1,9},{9,1},{17,25},{25,17},{2,10},{10... | collective-permute-start | bytes 172040 | tf_op jit(solution)/shard_map/ppermute | solution.py:545
  14.9 1.9 %prepare.1 = (bf16[2,256,768]{2,1,0:T(8,128)(2,1)S(1)}, f32[2,32,768]{2,1,0:T(8,128)S(1)}, bf16[2,3,256,256]{3,2,1,0:T(8,128)(2,1)S(1)}, bf16[3,128,256]{2,1,0:T...) custom-call(bf16[2,256,768]{2,1,0:T(8,128)(2,1)S(1)} %copy-done.7, f32[5,5,2,768]{3,2,1,0:T(2,128)S(1)} %bitcast.5, ...), custom_call_target="tpu_custom_call" | custom-call | flops 2000000000 | bytes 4000000 | tf_op jit(solution)/shard_map/prepare/pallas_call | solution.py:602
  17.5 8.0 %first.1 = (bf16[20,48,256]{2,1,0:T(8,128)(2,1)S(1)}, bf16[144,128]{1,0:T(8,128)(2,1)S(1)}) custom-call(bf16[8,32,256]{2,1,0:T(8,128)(2,1)S(1)} %copy-done.3, bf16[8,8,256]{2,1,0:T(8,128)(2,1)S(1)} %collective-permute-done.col_1, bf16[8,8,256]{2,1,0:T(8,128)(2,1)S(1)} %collective-permute-done.1.col_0, bf16[7,32,256]{2,1,0:T(8,128)(2,1)S(1)} %collective-permute-done.2.row_1, ...), custom_call_target="tpu_custom_call" | custom-call | tf_op jit(solution)/shard_map/first/pallas_call | solution.py:682
  25.5 1.8 %collective-permute-start.8 = (bf16[144,128]{1,0:T(8,128)(2,1)S(1)}, bf16[144,128]{1,0:T(8,128)(2,1)S(1)}, u32[]{:S(2)}, u32[]{:S(2)}) collective-permute-start(bf16[144,128]{1,0:T(8,128)(2,1)S(1)} %get-tuple-element.23), channel_id=1, source_target_pairs={{0,24},{8,16},{16,8},{24,0},{1,25},{9,17},{17,9},{25,1},{2,26},{10... | collective-permute-start | bytes 110600 | tf_op jit(solution)/shard_map/ppermute | solution.py:519
  27.9 1.3 %collective-permute-done.8 = bf16[144,128]{1,0:T(8,128)(2,1)S(1)} collective-permute-done((bf16[144,128]{1,0:T(8,128)(2,1)S(1)}, bf16[144,128]{1,0:T(8,128)(2,1)S(1)}, u32[]{:S(2)}, u32[]{:S(2)}) %collective-permute-start.8) | collective-permute-done | bytes 36896 | tf_op jit(solution)/shard_map/ppermute | solution.py:519
  29.2 2.1 %collective-permute-done.7 = bf16[144,128]{1,0:T(8,128)(2,1)S(1)} collective-permute-done((bf16[144,128]{1,0:T(8,128)(2,1)S(1)}, bf16[144,128]{1,0:T(8,128)(2,1)S(1)}, u32[]{:S(2)}, u32[]{:S(2)}) %collective-permute-start.7) | collective-permute-done | bytes 36896 | tf_op jit(solution)/shard_map/ppermute | solution.py:519
  31.3 1.9 %collective-permute-start.11 = (bf16[144,128]{1,0:T(8,128)(2,1)S(1)}, bf16[144,128]{1,0:T(8,128)(2,1)S(1)}, u32[]{:S(2)}, u32[]{:S(2)}) collective-permute-start(bf16[144,128]{1,0:T(8,128)(2,1)S(1)} %add_convert_fusion.3), channel_id=1, source_target_pairs={{0,3},{1,2},{2,1},{3,0},{4,7},{5,6},{6,5},{7,4},{8,11},{9,10},{10,... | collective-permute-start | bytes 110600 | tf_op jit(solution)/shard_map/ppermute | solution.py:519
  33.4 1.5 %collective-permute-start.9 = (bf16[144,128]{1,0:T(8,128)(2,1)S(1)}, bf16[144,128]{1,0:T(8,128)(2,1)S(1)}, u32[]{:S(2)}, u32[]{:S(2)}) collective-permute-start(bf16[144,128]{1,0:T(8,128)(2,1)S(1)} %add_convert_fusion.3), channel_id=1, source_target_pairs={{0,1},{1,0},{2,3},{3,2},{4,5},{5,4},{6,7},{7,6},{8,9},{9,8},{10,11... | collective-permute-start | bytes 110600 | tf_op jit(solution)/shard_map/ppermute | solution.py:519
  34.9 1.5 %collective-permute-done.11 = bf16[144,128]{1,0:T(8,128)(2,1)S(1)} collective-permute-done((bf16[144,128]{1,0:T(8,128)(2,1)S(1)}, bf16[144,128]{1,0:T(8,128)(2,1)S(1)}, u32[]{:S(2)}, u32[]{:S(2)}) %collective-permute-start.11) | collective-permute-done | bytes 36896 | tf_op jit(solution)/shard_map/ppermute | solution.py:519
  37.4 2.9 %collective-permute-start.12 = (bf16[144,128]{1,0:T(8,128)(2,1)S(1)}, bf16[144,128]{1,0:T(8,128)(2,1)S(1)}, u32[]{:S(2)}, u32[]{:S(2)}) collective-permute-start(bf16[144,128]{1,0:T(8,128)(2,1)S(1)} %add_convert_fusion.2.payload), channel_id=1, source_target_pairs={{0,4},{1,5},{2,6},{3,7},{4,0},{5,1},{6,2},{7,3},{8,12},{9,13},{10,... | collective-permute-start | bytes 110600 | tf_op jit(solution)/shard_map/ppermute | solution.py:519
  40.3 2.9 %queries.2 = (bf16[16,48,512]{2,1,0:T(8,128)(2,1)S(1)}, bf16[16,48,256]{2,1,0:T(8,128)(2,1)S(1)}) custom-call(bf16[20,48,256]{2,1,0:T(8,128)(2,1)S(1)} %get-tuple-element.20.mixed_in, bf16[2,256,768]{2,1,0:T(8,128)(2,1)S(1)} %get-tuple-element.17.refs_6_.qkv_weight, f32[2,32,768]{2,1,0:T(8,128)S(1)} %get-tuple-element.18.refs_7_.taps, ...), custom_call_target="tpu_custom_call" | custom-call | flops 402653184 | bytes 1572864 | tf_op jit(solution)/shard_map/queries/pallas_call | solution.py:656
  43.2 7.5 %second.1 = (bf16[14,48,256]{2,1,0:T(8,128)(2,1)S(1)}, bf16[144,128]{1,0:T(8,128)(2,1)S(1)}) custom-call(bf16[16,48,256]{2,1,0:T(8,128)(2,1)S(1)} %get-tuple-element.21.mixed, bf16[16,48,512]{2,1,0:T(8,128)(2,1)S(1)} %get-tuple-element.22.query, bf16[144,128]{1,0:T(8,128)(2,1)S(1)} %add_convert_fusion.2.payload, ...), custom_call_target="tpu_custom_call" | custom-call | tf_op jit(solution)/shard_map/second/pallas_call | solution.py:697
  50.8 1.4 %collective-permute-start.14 = (bf16[144,128]{1,0:T(8,128)(2,1)S(1)}, bf16[144,128]{1,0:T(8,128)(2,1)S(1)}, u32[]{:S(2)}, u32[]{:S(2)}) collective-permute-start(bf16[144,128]{1,0:T(8,128)(2,1)S(1)} %get-tuple-element.28), channel_id=1, source_target_pairs={{0,16},{8,24},{16,0},{24,8},{1,17},{9,25},{17,1},{25,9},{2,18},{10... | collective-permute-start | bytes 110600 | tf_op jit(solution)/shard_map/ppermute | solution.py:519
  52.6 1.9 %collective-permute-done.15 = bf16[144,128]{1,0:T(8,128)(2,1)S(1)} collective-permute-done((bf16[144,128]{1,0:T(8,128)(2,1)S(1)}, bf16[144,128]{1,0:T(8,128)(2,1)S(1)}, u32[]{:S(2)}, u32[]{:S(2)}) %collective-permute-start.15) | collective-permute-done | bytes 36896 | tf_op jit(solution)/shard_map/ppermute | solution.py:519
  55.0 1.7 %collective-permute-start.18 = (bf16[144,128]{1,0:T(8,128)(2,1)S(1)}, bf16[144,128]{1,0:T(8,128)(2,1)S(1)}, u32[]{:S(2)}, u32[]{:S(2)}) collective-permute-start(bf16[144,128]{1,0:T(8,128)(2,1)S(1)} %add_convert_fusion.1), channel_id=1, source_target_pairs={{0,3},{1,2},{2,1},{3,0},{4,7},{5,6},{6,5},{7,4},{8,11},{9,10},{10,... | collective-permute-start | bytes 110600 | tf_op jit(solution)/shard_map/ppermute | solution.py:519
  56.7 1.2 %collective-permute-start.17 = (bf16[144,128]{1,0:T(8,128)(2,1)S(1)}, bf16[144,128]{1,0:T(8,128)(2,1)S(1)}, u32[]{:S(2)}, u32[]{:S(2)}) collective-permute-start(bf16[144,128]{1,0:T(8,128)(2,1)S(1)} %add_convert_fusion.1), channel_id=1, source_target_pairs={{0,2},{1,3},{2,0},{3,1},{4,6},{5,7},{6,4},{7,5},{8,10},{9,11},{10,... | collective-permute-start | bytes 110600 | tf_op jit(solution)/shard_map/ppermute | solution.py:519
  58.6 1.6 %collective-permute-done.18 = bf16[144,128]{1,0:T(8,128)(2,1)S(1)} collective-permute-done((bf16[144,128]{1,0:T(8,128)(2,1)S(1)}, bf16[144,128]{1,0:T(8,128)(2,1)S(1)}, u32[]{:S(2)}, u32[]{:S(2)}) %collective-permute-start.18) | collective-permute-done | bytes 36896 | tf_op jit(solution)/shard_map/ppermute | solution.py:519
  60.7 1.2 %collective-permute-done.16 = bf16[144,128]{1,0:T(8,128)(2,1)S(1)} collective-permute-done((bf16[144,128]{1,0:T(8,128)(2,1)S(1)}, bf16[144,128]{1,0:T(8,128)(2,1)S(1)}, u32[]{:S(2)}, u32[]{:S(2)}) %collective-permute-start.16) | collective-permute-done | bytes 36896 | tf_op jit(solution)/shard_map/ppermute | solution.py:519
  61.9 2.0 %collective-permute-start.19 = (bf16[144,128]{1,0:T(8,128)(2,1)S(1)}, bf16[144,128]{1,0:T(8,128)(2,1)S(1)}, u32[]{:S(2)}, u32[]{:S(2)}) collective-permute-start(bf16[144,128]{1,0:T(8,128)(2,1)S(1)} %add_convert_fusion.payload), channel_id=1, source_target_pairs={{0,4},{1,5},{2,6},{3,7},{4,0},{5,1},{6,2},{7,3},{8,12},{9,13},{10,... | collective-permute-start | bytes 110600 | tf_op jit(solution)/shard_map/ppermute | solution.py:519
  64.0 1.8 %queries.3 = (bf16[10,48,512]{2,1,0:T(8,128)(2,1)S(1)}, bf16[10,48,256]{2,1,0:T(8,128)(2,1)S(1)}) custom-call(bf16[14,48,256]{2,1,0:T(8,128)(2,1)S(1)} %get-tuple-element.25.mixed_in, bf16[2,256,768]{2,1,0:T(8,128)(2,1)S(1)} %get-tuple-element.17.refs_6_.qkv_weight, f32[2,32,768]{2,1,0:T(8,128)S(1)} %get-tuple-element.18.refs_7_.taps, ...), custom_call_target="tpu_custom_call" | custom-call | flops 251658240 | bytes 983040 | tf_op jit(solution)/shard_map/queries/pallas_call | solution.py:656
  65.8 1.4 %collective-permute-done.19.other = bf16[144,128]{1,0:T(8,128)(2,1)S(1)} collective-permute-done((bf16[144,128]{1,0:T(8,128)(2,1)S(1)}, bf16[144,128]{1,0:T(8,128)(2,1)S(1)}, u32[]{:S(2)}, u32[]{:S(2)}) %collective-permute-start.19) | collective-permute-done | bytes 36896 | tf_op jit(solution)/shard_map/ppermute | solution.py:519
  67.2 2.3 %last.1 = (bf16[8,32,256]{2,1,0:T(8,128)(2,1)}, f32[4,8,32]{2,1,0:T(8,128)}) custom-call(bf16[10,48,256]{2,1,0:T(8,128)(2,1)S(1)} %get-tuple-element.26.mixed, bf16[10,48,512]{2,1,0:T(8,128)(2,1)S(1)} %get-tuple-element.27.query, bf16[144,128]{1,0:T(8,128)(2,1)S(1)} %add_convert_fusion.payload, bf16[144,128]{1,0:T(8,128)(2,1)S(1)} %collective-permute-done.19.other, ...), custom_call_target="tpu_custom_call" | custom-call | tf_op jit(solution)/shard_map/last/pallas_call | solution.py:710
  (61 shorter events, 8.7 us)
Async XLA Ops:
  0.6 7.3 %copy-start.3 = (bf16[8,32,256]{2,1,0:T(8,128)(2,1)S(1)}, bf16[8,32,256]{2,1,0:T(8,128)(2,1)}, u32[]{:S(2)}) copy-start(bf16[8,32,256]{2,1,0:T(8,128)(2,1)} %own.1) | copy-start | bytes 393220
  0.7 13.2 %copy-start.10 = (bf16[3,3,4,256]{3,2,1,0:T(4,128)(2,1)S(1)}, bf16[3,3,4,256]{3,2,1,0:T(4,128)(2,1)}, u32[]{:S(2)}) copy-start(bf16[3,3,4,256]{3,2,1,0:T(4,128)(2,1)} %head.1) | copy-start | bytes 55300
  1.5 10.2 %collective-permute-start = (bf16[8,8,256]{2,1,0:T(8,128)(2,1)S(1)}, bf16[8,8,256]{2,1,0:T(8,128)(2,1)S(1)}, u32[]{:S(2)}, u32[]{:S(2)}) collective-permute-start(bf16[8,8,256]{2,1,0:T(8,128)(2,1)S(1)} %get-tuple-element.33), channel_id=1, source_target_pairs={{1,2},{2,1},{3,4},{4,3},{5,6},{6,5},{9,10},{10,9},{11,12},{12,11},... | collective-permute-start | bytes 98312 | tf_op jit(solution)/shard_map/ppermute | solution.py:545
  2.1 9.6 %collective-permute-start.1 = (bf16[8,8,256]{2,1,0:T(8,128)(2,1)S(1)}, bf16[8,8,256]{2,1,0:T(8,128)(2,1)S(1)}, u32[]{:S(2)}, u32[]{:S(2)}) collective-permute-start(bf16[8,8,256]{2,1,0:T(8,128)(2,1)S(1)} %get-tuple-element.32), channel_id=1, source_target_pairs={{0,1},{1,0},{2,3},{3,2},{4,5},{5,4},{6,7},{7,6},{8,9},{9,8},{10,11... | collective-permute-start | bytes 98312 | tf_op jit(solution)/shard_map/ppermute | solution.py:545
  7.9 5.9 %copy-start.9 = (f32[2,5,5,768]{3,0,2,1:T(2,128)S(1)}, f32[2,5,5,768]{3,0,2,1:T(2,128)}, u32[]{:S(2)}) copy-start(f32[2,5,5,768]{3,0,2,1:T(2,128)} %param.22) | copy-start | bytes 460804
  7.9 5.9 %copy-start.7 = (bf16[2,256,768]{2,1,0:T(8,128)(2,1)S(1)}, bf16[2,256,768]{2,1,0:T(8,128)(2,1)}, u32[]{:S(2)}) copy-start(bf16[2,256,768]{2,1,0:T(8,128)(2,1)} %qkv.1) | copy-start | bytes 2359300
  8.0 8.8 %collective-permute-start.2 = (bf16[7,32,256]{2,1,0:T(8,128)(2,1)S(1)}, bf16[7,32,256]{2,1,0:T(8,128)(2,1)S(1)}, u32[]{:S(2)}, u32[]{:S(2)}) collective-permute-start(bf16[7,32,256]{2,1,0:T(8,128)(2,1)S(1)} %get-tuple-element.31), channel_id=1, source_target_pairs={{8,16},{16,8},{9,17},{17,9},{10,18},{18,10},{11,19},{19,11},{12,20... | collective-permute-start | bytes 344072 | tf_op jit(solution)/shard_map/ppermute | solution.py:545
  8.8 8.0 %collective-permute-start.3 = (bf16[7,32,256]{2,1,0:T(8,128)(2,1)S(1)}, bf16[7,32,256]{2,1,0:T(8,128)(2,1)S(1)}, u32[]{:S(2)}, u32[]{:S(2)}) collective-permute-start(bf16[7,32,256]{2,1,0:T(8,128)(2,1)S(1)} %get-tuple-element.30), channel_id=1, source_target_pairs={{0,8},{8,0},{16,24},{24,16},{1,9},{9,1},{17,25},{25,17},{2,10},{10... | collective-permute-start | bytes 344072 | tf_op jit(solution)/shard_map/ppermute | solution.py:545
  11.7 5.0 %collective-permute-start.4 = (bf16[14,8,256]{2,1,0:T(8,128)(2,1)S(1)}, bf16[14,8,256]{2,1,0:T(8,128)(2,1)S(1)}, u32[]{:S(2)}, u32[]{:S(2)}) collective-permute-start(bf16[14,8,256]{2,1,0:T(8,128)(2,1)S(1)} %pad_maximum_fusion), channel_id=1, source_target_pairs={{8,16},{16,8},{9,17},{17,9},{10,18},{18,10},{11,19},{19,11},{12,20... | collective-permute-start | bytes 172040 | tf_op jit(solution)/shard_map/ppermute | solution.py:545
  12.5 4.3 %collective-permute-start.5 = (bf16[14,8,256]{2,1,0:T(8,128)(2,1)S(1)}, bf16[14,8,256]{2,1,0:T(8,128)(2,1)S(1)}, u32[]{:S(2)}, u32[]{:S(2)}) collective-permute-start(bf16[14,8,256]{2,1,0:T(8,128)(2,1)S(1)} %pad_maximum_fusion.1), channel_id=1, source_target_pairs={{0,8},{8,0},{16,24},{24,16},{1,9},{9,1},{17,25},{25,17},{2,10},{10... | collective-permute-start | bytes 172040 | tf_op jit(solution)/shard_map/ppermute | solution.py:545
  25.5 3.7 %collective-permute-start.8 = (bf16[144,128]{1,0:T(8,128)(2,1)S(1)}, bf16[144,128]{1,0:T(8,128)(2,1)S(1)}, u32[]{:S(2)}, u32[]{:S(2)}) collective-permute-start(bf16[144,128]{1,0:T(8,128)(2,1)S(1)} %get-tuple-element.23), channel_id=1, source_target_pairs={{0,24},{8,16},{16,8},{24,0},{1,25},{9,17},{17,9},{25,1},{2,26},{10... | collective-permute-start | bytes 110600 | tf_op jit(solution)/shard_map/ppermute | solution.py:519
  27.3 4.0 %collective-permute-start.7 = (bf16[144,128]{1,0:T(8,128)(2,1)S(1)}, bf16[144,128]{1,0:T(8,128)(2,1)S(1)}, u32[]{:S(2)}, u32[]{:S(2)}) collective-permute-start(bf16[144,128]{1,0:T(8,128)(2,1)S(1)} %get-tuple-element.23), channel_id=1, source_target_pairs={{0,16},{8,24},{16,0},{24,8},{1,17},{9,25},{17,1},{25,9},{2,18},{10... | collective-permute-start | bytes 110600 | tf_op jit(solution)/shard_map/ppermute | solution.py:519
  27.9 3.4 %collective-permute-start.6 = (bf16[144,128]{1,0:T(8,128)(2,1)S(1)}, bf16[144,128]{1,0:T(8,128)(2,1)S(1)}, u32[]{:S(2)}, u32[]{:S(2)}) collective-permute-start(bf16[144,128]{1,0:T(8,128)(2,1)S(1)} %get-tuple-element.23), channel_id=1, source_target_pairs={{0,8},{8,0},{16,24},{24,16},{1,9},{9,1},{17,25},{25,17},{2,10},{10... | collective-permute-start | bytes 110600 | tf_op jit(solution)/shard_map/ppermute | solution.py:519
  31.3 5.1 %collective-permute-start.11 = (bf16[144,128]{1,0:T(8,128)(2,1)S(1)}, bf16[144,128]{1,0:T(8,128)(2,1)S(1)}, u32[]{:S(2)}, u32[]{:S(2)}) collective-permute-start(bf16[144,128]{1,0:T(8,128)(2,1)S(1)} %add_convert_fusion.3), channel_id=1, source_target_pairs={{0,3},{1,2},{2,1},{3,0},{4,7},{5,6},{6,5},{7,4},{8,11},{9,10},{10,... | collective-permute-start | bytes 110600 | tf_op jit(solution)/shard_map/ppermute | solution.py:519
  33.2 4.0 %collective-permute-start.10 = (bf16[144,128]{1,0:T(8,128)(2,1)S(1)}, bf16[144,128]{1,0:T(8,128)(2,1)S(1)}, u32[]{:S(2)}, u32[]{:S(2)}) collective-permute-start(bf16[144,128]{1,0:T(8,128)(2,1)S(1)} %add_convert_fusion.3), channel_id=1, source_target_pairs={{0,2},{1,3},{2,0},{3,1},{4,6},{5,7},{6,4},{7,5},{8,10},{9,11},{10,... | collective-permute-start | bytes 110600 | tf_op jit(solution)/shard_map/ppermute | solution.py:519
  33.4 4.0 %collective-permute-start.9 = (bf16[144,128]{1,0:T(8,128)(2,1)S(1)}, bf16[144,128]{1,0:T(8,128)(2,1)S(1)}, u32[]{:S(2)}, u32[]{:S(2)}) collective-permute-start(bf16[144,128]{1,0:T(8,128)(2,1)S(1)} %add_convert_fusion.3), channel_id=1, source_target_pairs={{0,1},{1,0},{2,3},{3,2},{4,5},{5,4},{6,7},{7,6},{8,9},{9,8},{10,11... | collective-permute-start | bytes 110600 | tf_op jit(solution)/shard_map/ppermute | solution.py:519
  37.4 5.8 %collective-permute-start.12 = (bf16[144,128]{1,0:T(8,128)(2,1)S(1)}, bf16[144,128]{1,0:T(8,128)(2,1)S(1)}, u32[]{:S(2)}, u32[]{:S(2)}) collective-permute-start(bf16[144,128]{1,0:T(8,128)(2,1)S(1)} %add_convert_fusion.2.payload), channel_id=1, source_target_pairs={{0,4},{1,5},{2,6},{3,7},{4,0},{5,1},{6,2},{7,3},{8,12},{9,13},{10,... | collective-permute-start | bytes 110600 | tf_op jit(solution)/shard_map/ppermute | solution.py:519
  50.7 3.8 %collective-permute-start.15 = (bf16[144,128]{1,0:T(8,128)(2,1)S(1)}, bf16[144,128]{1,0:T(8,128)(2,1)S(1)}, u32[]{:S(2)}, u32[]{:S(2)}) collective-permute-start(bf16[144,128]{1,0:T(8,128)(2,1)S(1)} %get-tuple-element.28), channel_id=1, source_target_pairs={{0,24},{8,16},{16,8},{24,0},{1,25},{9,17},{17,9},{25,1},{2,26},{10... | collective-permute-start | bytes 110600 | tf_op jit(solution)/shard_map/ppermute | solution.py:519
  50.8 4.2 %collective-permute-start.14 = (bf16[144,128]{1,0:T(8,128)(2,1)S(1)}, bf16[144,128]{1,0:T(8,128)(2,1)S(1)}, u32[]{:S(2)}, u32[]{:S(2)}) collective-permute-start(bf16[144,128]{1,0:T(8,128)(2,1)S(1)} %get-tuple-element.28), channel_id=1, source_target_pairs={{0,16},{8,24},{16,0},{24,8},{1,17},{9,25},{17,1},{25,9},{2,18},{10... | collective-permute-start | bytes 110600 | tf_op jit(solution)/shard_map/ppermute | solution.py:519
  52.2 2.8 %collective-permute-start.13 = (bf16[144,128]{1,0:T(8,128)(2,1)S(1)}, bf16[144,128]{1,0:T(8,128)(2,1)S(1)}, u32[]{:S(2)}, u32[]{:S(2)}) collective-permute-start(bf16[144,128]{1,0:T(8,128)(2,1)S(1)} %get-tuple-element.28), channel_id=1, source_target_pairs={{0,8},{8,0},{16,24},{24,16},{1,9},{9,1},{17,25},{25,17},{2,10},{10... | collective-permute-start | bytes 110600 | tf_op jit(solution)/shard_map/ppermute | solution.py:519
  55.0 5.2 %collective-permute-start.18 = (bf16[144,128]{1,0:T(8,128)(2,1)S(1)}, bf16[144,128]{1,0:T(8,128)(2,1)S(1)}, u32[]{:S(2)}, u32[]{:S(2)}) collective-permute-start(bf16[144,128]{1,0:T(8,128)(2,1)S(1)} %add_convert_fusion.1), channel_id=1, source_target_pairs={{0,3},{1,2},{2,1},{3,0},{4,7},{5,6},{6,5},{7,4},{8,11},{9,10},{10,... | collective-permute-start | bytes 110600 | tf_op jit(solution)/shard_map/ppermute | solution.py:519
  56.7 4.0 %collective-permute-start.17 = (bf16[144,128]{1,0:T(8,128)(2,1)S(1)}, bf16[144,128]{1,0:T(8,128)(2,1)S(1)}, u32[]{:S(2)}, u32[]{:S(2)}) collective-permute-start(bf16[144,128]{1,0:T(8,128)(2,1)S(1)} %add_convert_fusion.1), channel_id=1, source_target_pairs={{0,2},{1,3},{2,0},{3,1},{4,6},{5,7},{6,4},{7,5},{8,10},{9,11},{10,... | collective-permute-start | bytes 110600 | tf_op jit(solution)/shard_map/ppermute | solution.py:519
  57.9 4.0 %collective-permute-start.16 = (bf16[144,128]{1,0:T(8,128)(2,1)S(1)}, bf16[144,128]{1,0:T(8,128)(2,1)S(1)}, u32[]{:S(2)}, u32[]{:S(2)}) collective-permute-start(bf16[144,128]{1,0:T(8,128)(2,1)S(1)} %add_convert_fusion.1), channel_id=1, source_target_pairs={{0,1},{1,0},{2,3},{3,2},{4,5},{5,4},{6,7},{7,6},{8,9},{9,8},{10,11... | collective-permute-start | bytes 110600 | tf_op jit(solution)/shard_map/ppermute | solution.py:519
  61.9 5.3 %collective-permute-start.19 = (bf16[144,128]{1,0:T(8,128)(2,1)S(1)}, bf16[144,128]{1,0:T(8,128)(2,1)S(1)}, u32[]{:S(2)}, u32[]{:S(2)}) collective-permute-start(bf16[144,128]{1,0:T(8,128)(2,1)S(1)} %add_convert_fusion.payload), channel_id=1, source_target_pairs={{0,4},{1,5},{2,6},{3,7},{4,0},{5,1},{6,2},{7,3},{8,12},{9,13},{10,... | collective-permute-start | bytes 110600 | tf_op jit(solution)/shard_map/ppermute | solution.py:519
  (10 other events, 17.5 us)
